TPU v7x, 32 devices: a whole 2x2x4 slice. The times are simulated.
32 devices in a mesh: row: 8 (over y, x, core), col: 4 (over z).
Axes of the slice: x: 2, y: 2, z: 4, core: 2. Of those that a mesh axis runs over, the one named last changes fastest.
Arguments:
- nodes: bfloat16 [32768, 256], P(('row', 'col')), may hold values from -6 to 6
- tiles: bfloat16 [256, 4, 4, 128, 128], P('row', 'col'), may hold values from -0.12988281 to 0.12988281
- tile_col: int32 [256, 4, 4], P('row', 'col'), may hold values from 0 to 63, as said below
- tile_count: int32 [256, 4], P('row', 'col'), may hold values from 0 to 4, as said below
- w_in: bfloat16 [512, 256], replicated, may hold values from -0.25 to 0.25
- bias_in: float32 [256], replicated, may hold values from -3 to 3
- w_out: bfloat16 [256, 256], replicated, may hold values from -0.375 to 0.375
- ln_gain: float32 [256], replicated, may hold values from 0.1 to 1.9
- ln_shift: float32 [256], replicated, may hold values from -3 to 3
- cotangent: bfloat16 [32768, 256], P(('row', 'col')), may hold values from -6 to 6
Outputs:
- updated: bfloat16 [32768, 256], P(('row', 'col'))
- grad_nodes: bfloat16 [32768, 256], P(('row', 'col'))
- grad_tiles: bfloat16 [256, 4, 4, 128, 128], P('row', 'col')
- grad_w_in: float32 [512, 256], replicated
- grad_w_out: float32 [256, 256], replicated
- grad_vectors: float32 [3, 256], replicated
Inputs may be any that keep to these rules, and one draw needn't show every extreme that they name: `tile_col`: index within the column group; slots at or past the block row's tile_count are ignored. `tile_count`: loads differ between devices; 4 is reached in every draw.
All inputs are finite; a program needn't handle non-finite values.
Results may differ from a plain program's by a relative error of at most 0.02.
Values may be sent and summed in bfloat16 or wider, within the bound.
No kernel may reach another device: no remote copies, remote signals or barrier semaphores. Data moves between devices by JAX's collectives and lax.ppermute only.
A program may use at most 256 MiB of HBM per device.

v0:
```python
import jax
import jax.numpy as jnp
from jax import lax
from jax.sharding import PartitionSpec as P


def pick_blocks(gathered, cols, block, width):
    blocks = gathered.reshape(-1, block, width)
    return blocks[cols]


def body(nodes, tiles, tile_col, tile_count, w_in, bias_in, w_out, ln_gain, ln_shift, cotangent):
    rows, width = nodes.shape
    row_blocks, slots, block = (tiles.shape[0], tiles.shape[2], tiles.shape[3])
    tile_local = tiles[:, 0]
    cols = tile_col[:, 0]
    count = tile_count[:, 0]
    live = lax.broadcasted_iota(jnp.int32, (row_blocks, slots), 1) < count[:, None]
    live_tiles = jnp.where(live[:, :, None, None], tile_local, jnp.zeros((), tile_local.dtype))
    gathered = lax.all_gather(nodes, "row", axis=0, tiled=True)
    picked = pick_blocks(gathered, cols, block, width)
    partial_value = jnp.einsum(
        "rkij,rkjd->rid", live_tiles, picked, preferred_element_type=jnp.float32
    )
    summed = lax.psum_scatter(
        partial_value.reshape(row_blocks * block, width).astype(jnp.bfloat16),
        "col",
        scatter_dimension=0,
        tiled=True,
    )
    pre = (
        jnp.dot(nodes, w_in[:width], preferred_element_type=jnp.float32)
        + jnp.dot(summed, w_in[width:], preferred_element_type=jnp.float32)
        + bias_in
    )
    sig = jax.nn.sigmoid(pre)
    act = (pre * sig).astype(jnp.bfloat16)
    proj = jnp.dot(act, w_out, preferred_element_type=jnp.float32)
    mean = jnp.mean(proj, axis=-1, keepdims=True)
    var = jnp.mean((proj - mean) ** 2, axis=-1, keepdims=True)
    rstd = 1.0 / jnp.sqrt(var + 1e-05)
    normed = (proj - mean) * rstd
    updated = (nodes.astype(jnp.float32) + normed * ln_gain + ln_shift).astype(jnp.bfloat16)
    grad_out = cotangent.astype(jnp.float32)
    gscaled = grad_out * ln_gain
    gproj = (
        (
            gscaled
            - jnp.mean(gscaled, axis=-1, keepdims=True)
            - normed * jnp.mean(gscaled * normed, axis=-1, keepdims=True)
        )
        * rstd
    ).astype(jnp.bfloat16)
    gact = jnp.dot(gproj, w_out.T, preferred_element_type=jnp.float32)
    gpre = gact * sig * (1.0 + pre * (1.0 - sig))
    gpre_b = gpre.astype(jnp.bfloat16)
    gmsg = jnp.dot(gpre_b, w_in[width:].T, preferred_element_type=jnp.float32).astype(jnp.bfloat16)
    direct = grad_out + jnp.dot(gpre_b, w_in[:width].T, preferred_element_type=jnp.float32)
    grad_rows = lax.all_gather(gmsg, "col", axis=0, tiled=True).reshape(row_blocks, block, width)
    back = jnp.einsum("rkij,rid->rkjd", live_tiles, grad_rows, preferred_element_type=jnp.float32)
    col_blocks = gathered.shape[0] // block
    flat_back = back.reshape(row_blocks * slots, block * width)
    flat_cols = cols.reshape(-1)
    column_terms = jax.ops.segment_sum(flat_back, flat_cols, num_segments=col_blocks)
    column_terms = column_terms.astype(jnp.bfloat16)
    agg = lax.psum_scatter(
        column_terms.reshape(col_blocks * block, width), "row", scatter_dimension=0, tiled=True
    ).astype(jnp.float32)
    grad_nodes = (direct + agg).astype(jnp.bfloat16)
    tile_grads = jnp.einsum("rid,rkjd->rkij", grad_rows, picked, preferred_element_type=jnp.float32)
    tile_grads = jnp.where(
        live[:, :, None, None], tile_grads * jnp.float32(width) ** (-0.5), jnp.float32(0.0)
    )
    grad_tiles = tile_grads.astype(jnp.bfloat16)[:, None]
    total_nodes = rows * lax.axis_size("row") * lax.axis_size("col")
    factor = jnp.float32(total_nodes) ** (-0.5)
    local_in = jnp.concatenate(
        [
            jnp.dot(nodes.T, gpre_b, preferred_element_type=jnp.float32),
            jnp.dot(summed.T, gpre_b, preferred_element_type=jnp.float32),
        ],
        axis=0,
    )
    local_out = jnp.dot(act.T, gproj, preferred_element_type=jnp.float32)
    local_vectors = jnp.stack(
        [jnp.sum(gpre, axis=0), jnp.sum(grad_out * normed, axis=0), jnp.sum(grad_out, axis=0)]
    )
    sum_in, sum_out, sum_vectors = lax.psum((local_in, local_out, local_vectors), ("row", "col"))
    return (
        updated,
        grad_nodes,
        grad_tiles,
        sum_in * factor,
        sum_out * factor,
        sum_vectors * factor,
    )


def solution(mesh):
    placed = (
        P(("row", "col"), None),
        P("row", "col", None, None, None),
        P("row", "col", None),
        P("row", "col"),
        P(),
        P(),
        P(),
        P(),
        P(),
        P(("row", "col"), None),
    )
    return jax.shard_map(
        body,
        mesh=mesh,
        in_specs=placed,
        out_specs=(
            P(("row", "col"), None),
            P(("row", "col"), None),
            P("row", "col", None, None, None),
            P(),
            P(),
            P(),
        ),
        check_vma=False,
    )
```

profile of v0, /device:TPU:0, one launch (start us, length us, event | category | flops | bytes accessed | tf_op | source)
XLA Modules:
  0.0 358.3 jit_solution(18256619442268744608)
XLA Ops:
  7.2 0.0 copy-start
  7.2 0.0 all-gather.3.cloned.1.call-start
  7.2 0.7 all-gather.3.cloned.1.call-update
  7.9 0.0 reduce-scatter.3.cloned.1.call-start
  8.0 0.7 compare_select_fusion
  8.7 0.1 copy.26
  8.7 0.1 reshape.104
  8.9 0.7 iota_compare_fusion
  9.6 39.8 %all-gather.3.cloned.1.call-done = bf16[8192,256]{1,0:T(8,128)(2,1)} async-done(((bf16[1024,256]{1,0:T(8,128)(2,1)}), bf16[8192,256]{1,0:T(8,128)(2,1)}) %all-gather.3.cloned.1.call-update) | async-done | bytes 4194320 | tf_op jit(solution)/shard_map/all_gather | solution.py:20
  49.4 8.8 %gather_fusion = bf16[128,128,256]{2,1,0:T(8,128)(2,1)} fusion(bf16[64,128,256]{2,1,0:T(8,128)(2,1)} %bitcast.55, s32[1024]{0:T(1024)S(1)} %pad_clamp_fusion), kind=kCustom, calls=%fused_computation | custom fusion | bytes 16777728 | tf_op jit(solution)/shard_map/gather | solution.py:9
  58.1 7.4 %bitcast_convert_fusion = bf16[32,128,256]{2,1,0:T(8,128)(2,1)} fusion(bf16[32,4,128,256]{3,2,1,0:T(8,128)(2,1)} %bitcast.57, bf16[32,1,4,128,128]{4,3,2,1,0:T(8,128)(2,1)} %param.11, pred[32,4]{1,0:T(8,128)(4,1)S(1)} %iota_compare_fusion), kind=kOutput, calls=%fused_computation.4 | convolution fusion | flops 1076887552 | bytes 14680192 | tf_op jit(solution)/shard_map/rkij,rkjd->rid/dot_general | solution.py:22
  65.5 0.0 reduce-scatter.3.cloned.1.call-update
  65.5 0.0 all-gather.5.cloned.1.call-start
  65.6 0.0 copy-done.2
  65.6 0.2 copy.25
  65.8 0.0 copy-done.5
  65.8 0.2 copy.27
  66.0 0.4 copy-done.4
  66.4 1.3 fusion.22
  67.7 41.8 %reduce-scatter.3.cloned.1.call-done = bf16[1024,256]{1,0:T(8,128)(2,1)} async-done(((bf16[4096,256]{1,0:T(8,128)(2,1)}), bf16[1024,256]{1,0:T(8,128)(2,1)}) %reduce-scatter.3.cloned.1.call-update) | async-done | bytes 524304 | tf_op jit(solution)/shard_map/reduce_scatter | solution.py:25
  109.5 0.0 copy-done.9
  109.5 1.9 multiply_convert_fusion
  111.4 0.0 copy-done
  111.4 0.4 fusion.27
  111.8 0.1 multiply_reduce_fusion
  111.9 0.0 copy-done.7
  111.9 0.5 fusion.18
  112.4 0.0 copy-done.8
  112.5 0.5 fusion.16
  113.0 0.0 copy-start.3
  113.0 0.0 copy-start.6
  113.0 0.8 copy-done.3
  113.8 0.6 fusion.26
  114.4 1.1 convolution_convert_fusion
  115.5 0.0 all-gather.5.cloned.1.call-update
  115.5 0.0 all-reduce.3.cloned.1.call-start
  115.6 0.0 copy-done.6
  115.6 0.1 copy.29
  115.7 0.1 reshape.112
  115.8 0.4 convolution_bitcast_fusion
  116.1 1.4 fusion.28
  117.5 0.8 pad_maximum_fusion
  118.3 2.1 fusion.29
  120.4 0.0 all-reduce.3.cloned.1.call-update
  120.5 0.2 reduce-scatter.5.cloned.1.call-start
  120.7 40.2 %all-gather.5.cloned.1.call-done = bf16[4096,256]{1,0:T(8,128)(2,1)} async-done(((bf16[1024,256]{1,0:T(8,128)(2,1)}), bf16[4096,256]{1,0:T(8,128)(2,1)}) %all-gather.5.cloned.1.call-update) | async-done | bytes 2097168 | tf_op jit(solution)/shard_map/all_gather | solution.py:59
  160.9 6.3 %fusion.3 = f32[32,4,128,256]{3,2,1,0:T(8,128)S(1)} fusion(bf16[32,128,256,1]{2,1,3,0:T(8,128)(2,1)} %bitcast.59, bf16[32,1,4,128,128]{4,3,2,1,0:T(8,128)(2,1)} %param.11, pred[32,4]{1,0:T(8,128)(4,1)S(1)} %iota_compare_fusion), kind=kOutput, calls=%fused_computation.8 | convolution fusion | flops 1075838976 | bytes 23068800 | tf_op jit(solution)/shard_map/rkij,rid->rkjd/dot_general | solution.py:60
  167.2 11.8 %copy.39 = f32[16,8,128,256]{3,1,2,0:T(8,128)} copy(f32[16,8,128,256]{3,2,1,0:T(8,128)S(1)} %bitcast.54) | data formatting | bytes 33554432
  179.0 27.8 %scatter_custom_fusion = f32[64,32768]{1,0:T(8,128)} fusion(s32[128]{0:T(128)S(1)} %reshape.112, f32[128,32768]{1,0:T(8,128)} %bitcast.56, f32[]{:T(128)} %constant.7.clone.1), kind=kCustom, calls=%fused_computation.6 | custom fusion | flops 4194304 | bytes 8389120 | tf_op jit(solution)/shard_map/scatter-add | solution.py:64
  206.8 5.8 %convert_element_type.51 = bf16[64,32768]{1,0:T(8,128)(2,1)} convert(f32[64,32768]{1,0:T(8,128)} %scatter_custom_fusion) | non-fusion elementwise | flops 2097152 | bytes 12582912 | tf_op jit(solution)/shard_map/convert_element_type | solution.py:65
  212.6 7.4 %reshape.101 = bf16[8192,256]{1,0:T(8,128)(2,1)} reshape(bf16[64,32768]{1,0:T(8,128)(2,1)} %convert_element_type.51) | data formatting | bytes 8388608 | tf_op jit(solution)/shard_map/reshape | solution.py:67
  220.0 6.4 %copy.31 = bf16[8192,256]{0,1:T(8,128)(2,1)} copy(bf16[8192,256]{1,0:T(8,128)(2,1)} %reshape.101) | data formatting | bytes 8388608 | tf_op jit(solution)/shard_map/reshape | solution.py:67
  226.4 0.0 reduce-scatter.5.cloned.1.call-update
  226.5 1.0 copy.32
  227.5 38.9 %psum.23 = f32[3,256]{1,0:T(4,128)S(1)} all-reduce(f32[3,256]{1,0:T(4,128)S(1)} %pad_maximum_fusion.1), channel_id=1, replica_groups=mesh['row'=8,'col'=4] {'row','col'}, use_global_device_ids=true, to_apply=%region_12.13 | all-reduce | flops 768 | bytes 6144 | tf_op jit(solution)/shard_map/psum | solution.py:88
  266.4 0.6 broadcast_multiply_fusion.2
  267.0 28.4 %all-reduce.3.cloned.1.call-done = (f32[512,256]{1,0:T(8,128)}, f32[256,256]{1,0:T(8,128)}) async-done(((f32[512,256]{1,0:T(8,128)}, f32[256,256]{1,0:T(8,128)}), (f32[512,256]{1,0:T(8,128)}, f32[256,256]{1,0:T(8,128)})) %all-reduce.3.cloned.1.call-update) | async-done | bytes 786448 | tf_op jit(solution)/shard_map/psum | solution.py:88
  295.4 1.7 broadcast_multiply_fusion.1
  297.1 1.9 broadcast_multiply_fusion
  299.0 8.3 %fusion = bf16[32,1,4,128,128]{3,4,2,0,1:T(8,128)(2,1)} fusion(pred[32,4]{1,0:T(8,128)(4,1)S(1)} %iota_compare_fusion, bf16[32,4,128,256]{3,2,1,0:T(8,128)(2,1)} %bitcast.58, bf16[32,128,256,1]{2,1,3,0:T(8,128)(2,1)} %bitcast.60), kind=kOutput, calls=%fused_computation.3 | convolution fusion | flops 1080033280 | bytes 14680192 | tf_op jit(solution)/shard_map/rid,rkjd->rkij/dot_general | solution.py:70
  307.3 6.6 %copy.34 = bf16[32,1,4,128,128]{4,3,2,1,0:T(8,128)(2,1)} copy(bf16[32,1,4,128,128]{3,4,2,0,1:T(8,128)(2,1)} %fusion) | data formatting | bytes 8388608
  313.8 35.1 %reduce-scatter.5.cloned.1.call-done = bf16[1024,256]{0,1:T(8,128)(2,1)} async-done(((bf16[8192,256]{0,1:T(8,128)(2,1)}), bf16[1024,256]{0,1:T(8,128)(2,1)}) %reduce-scatter.5.cloned.1.call-update) | async-done | bytes 524304 | tf_op jit(solution)/shard_map/reduce_scatter | solution.py:66
  348.9 1.4 fusion.13
  350.3 1.0 copy.33
  (13 shorter events, 0.0 us)
Async XLA Ops:
  7.2 104.2 %copy-start = (bf16[256,256]{1,0:T(8,128)(2,1)S(1)}, bf16[256,256]{1,0:T(8,128)(2,1)}, u32[]{:S(2)}) copy-start(bf16[256,256]{1,0:T(8,128)(2,1)} %param.16) | copy-start | bytes 393220
  7.2 42.2 %all-gather.3.cloned.1.call-start = ((), (), s32[]{:S(2)}) async-start(), calls=%async_computation.2 | async-start | bytes 4718592 | tf_op jit(solution)/shard_map/all_gather | solution.py:20
  7.9 101.6 %reduce-scatter.3.cloned.1.call-start = ((), (), s32[]{:S(2)}) async-start(), calls=%async_computation.3 | async-start | bytes 2621440 | tf_op jit(solution)/shard_map/reduce_scatter | solution.py:25
  58.1 7.5 %copy-start.2 = (bf16[1024,256]{1,0:T(8,128)(2,1)S(1)}, bf16[1024,256]{1,0:T(8,128)(2,1)}, u32[]{:S(2)}) copy-start(bf16[1024,256]{1,0:T(8,128)(2,1)} %param.10) | copy-start | bytes 1572868
  58.1 7.7 %copy-start.5 = (bf16[1024,256]{1,0:T(8,128)(2,1)S(1)}, bf16[1024,256]{1,0:T(8,128)(2,1)}, u32[]{:S(2)}) copy-start(bf16[1024,256]{1,0:T(8,128)(2,1)} %param.19) | copy-start | bytes 1572868
  65.5 0.9 copy-start.4
  65.5 44.0 %copy-start.9 = (f32[256]{0:T(256)S(1)}, f32[256]{0:T(256)}, u32[]{:S(2)}) copy-start(f32[256]{0:T(256)} %param.15) | copy-start | bytes 3076
  65.5 95.4 %all-gather.5.cloned.1.call-start = ((), (), s32[]{:S(2)}) async-start(), calls=%async_computation.4 | async-start | bytes 2621440 | tf_op jit(solution)/shard_map/all_gather | solution.py:59
  67.7 44.2 %copy-start.7 = (f32[256]{0:T(256)S(1)}, f32[256]{0:T(256)}, u32[]{:S(2)}) copy-start(f32[256]{0:T(256)} %param.17) | copy-start | bytes 3076
  67.7 44.7 %copy-start.8 = (f32[256]{0:T(256)S(1)}, f32[256]{0:T(256)}, u32[]{:S(2)}) copy-start(f32[256]{0:T(256)} %param.18) | copy-start | bytes 3076
  113.0 0.8 copy-start.3
  113.0 2.6 copy-start.6
  115.5 179.9 %all-reduce.3.cloned.1.call-start = ((), (), s32[]{:S(2)}) async-start(), calls=%async_computation.6 | async-start | bytes 1572864 | tf_op jit(solution)/shard_map/psum | solution.py:88
  120.5 228.4 %reduce-scatter.5.cloned.1.call-start = ((), (), s32[]{:S(2)}) async-start(), calls=%async_computation.5 | async-start | bytes 4718592 | tf_op jit(solution)/shard_map/reduce_scatter | solution.py:66
  298.9 52.4 %copy-start.1 = (bf16[256,256]{1,0:T(8,128)(2,1)S(1)}, bf16[256,256]{1,0:T(8,128)(2,1)}, u32[]{:S(2)}) copy-start(bf16[256,256]{1,0:T(8,128)(2,1)} %param.16) | copy-start | bytes 393220
Sparse Core Ops, SparseCore 0:
  9.9 39.4 all-gather.2
  65.6 43.8 reduce-scatter.2
  115.6 45.2 all-gather.4
  167.5 127.8 all-reduce.2
  298.6 50.2 reduce-scatter.4
where the time goes:
time: 365 us; the launch traced here: 358 us
  waiting for transfers between devices  186 us (51%)
  local copies, waits for them, and re-layouts  44.9 us (12%)
  other arithmetic  41.2 us (11%)
  blocking collectives  38.9 us (11%)
  matrix products  32.5 us (9%)
  between operations  14.4 us (4%)
    reduce_scatter x1, waiting for transfers between devices, body(): lax.psum_scatter(partial_value.reshape(row_blocks * block, width).astype(...  41.8 us
    all_gather x1, waiting for transfers between devices, body(): lax.all_gather(gmsg, 'col', axis=0, tiled=True)  40.2 us
    all_gather x1, waiting for transfers between devices, body(): gathered = lax.all_gather(nodes, 'row', axis=0, tiled=True)  39.8 us
    psum x1, blocking collectives, body(): lax.psum((local_in, local_out, local_vectors), ('row', 'col'))  38.9 us
    reduce_scatter x1, waiting for transfers between devices, body(): lax.psum_scatter(column_terms.reshape(col_blocks * block, width), 'row',...  35.1 us
    psum x1, waiting for transfers between devices, body(): lax.psum((local_in, local_out, local_vectors), ('row', 'col'))  28.4 us
    scatter-add x1, other arithmetic, body(): jax.ops.segment_sum(flat_back, flat_cols, num_segments=col_blocks)  27.8 us
    unnamed x27, local copies, waits for them, and re-layouts  22.1 us
  transfers between devices with their start and end apart: 5, of which 5 were waited for; matrix products, arithmetic and copies ran while one was open for 26% of the time, Pallas kernels for 0%

commit v1 on v0

v1 whole, which is shorter than its diff:
```python
import functools

import jax
import jax.numpy as jnp
from jax import lax
from jax.experimental import pallas as pl
from jax.experimental.pallas import tpu as pltpu
from jax.sharding import PartitionSpec as P

F32 = jnp.float32
BF16 = jnp.bfloat16
ANY = pl.BlockSpec(memory_space=pl.ANY)
SMEM = pl.BlockSpec(memory_space=pltpu.SMEM)
VMEM = pl.BlockSpec(memory_space=pltpu.VMEM)
MIB = 1 << 20
TN = (((0,), (0,)), ((), ()))
NT = (((1,), (1,)), ((), ()))


def mm(a, b, dims=(((1,), (0,)), ((), ()))):
    return lax.dot_general(a, b, dims, preferred_element_type=F32)


def load_pieces(pieces, dst, sem, first):
    copies = []
    offset = 0
    for index, piece in enumerate(pieces):
        copy = pltpu.make_async_copy(
            piece, dst.at[pl.ds(offset, piece.shape[0])], sem.at[first + index]
        )
        copy.start()
        copies.append(copy)
        offset += piece.shape[0]
    return copies


def masked_tile(tiles, row, slot, count):
    tile = tiles[row, slot]
    return jnp.where(slot < count, tile, jnp.zeros_like(tile))


def forward_kernel(groups, total, n_pieces, cols, counts, off, *refs):
    pieces, tiles = refs[:n_pieces], refs[n_pieces]
    outs = refs[n_pieces + 1 : n_pieces + 1 + len(groups)]
    nodes_v, tiles_v, sem, tile_sem = refs[n_pieces + 1 + len(groups) :]
    rows, width = outs[0].shape
    slots, block = tiles.shape[1], tiles.shape[2]
    blocks = rows // block
    copies = load_pieces(pieces, nodes_v, sem, 0)
    tile_copies = []
    for index, group in enumerate(groups):
        actual = lax.rem(off[0] + group, total)
        copy = pltpu.make_async_copy(
            tiles.at[pl.ds(actual * blocks, blocks)],
            tiles_v.at[pl.ds(index * blocks, blocks)],
            tile_sem.at[index],
        )
        copy.start()
        tile_copies.append(copy)
    for copy in copies:
        copy.wait()
    for index, group in enumerate(groups):
        tile_copies[index].wait()
        first = lax.rem(off[0] + group, total) * blocks
        out = outs[index]

        def step(i, carry, first=first, out=out, index=index):
            row = first + i
            count = counts[row]
            parts = []
            for pair in range(slots // 2):
                left, right = 2 * pair, 2 * pair + 1
                tile = jnp.concatenate(
                    [
                        masked_tile(tiles_v, index * blocks + i, slot, count)
                        for slot in (left, right)
                    ],
                    axis=1,
                )
                node = jnp.concatenate(
                    [
                        nodes_v[pl.ds(pl.multiple_of(cols[row * slots + slot] * block, block), block)]
                        for slot in (left, right)
                    ],
                    axis=0,
                )
                parts.append(mm(tile, node))
            value = parts[0]
            for part in parts[1:]:
                value = value + part
            out[pl.ds(pl.multiple_of(i * block, block), block)] = value.astype(BF16)
            return carry

        lax.fori_loop(0, blocks, step, 0, unroll=4)


def forward_call(cols, counts, off, pieces, tiles, groups, total, rows):
    width = pieces[0].shape[1]
    gathered = sum(piece.shape[0] for piece in pieces)
    slots, block = tiles.shape[1], tiles.shape[2]
    blocks = rows // block
    flops = len(groups) * blocks * slots * 2 * block * block * width
    return pl.pallas_call(
        functools.partial(forward_kernel, groups, total, len(pieces)),
        out_shape=[jax.ShapeDtypeStruct((rows, width), BF16) for _ in groups],
        in_specs=[SMEM, SMEM, SMEM] + [ANY] * (len(pieces) + 1),
        out_specs=[VMEM] * len(groups),
        scratch_shapes=[
            pltpu.VMEM((gathered, width), BF16),
            pltpu.VMEM((len(groups) * blocks,) + tiles.shape[1:], BF16),
            pltpu.SemaphoreType.DMA((len(pieces),)),
            pltpu.SemaphoreType.DMA((len(groups),)),
        ],
        compiler_params=pltpu.CompilerParams(vmem_limit_bytes=40 * MIB),
        cost_estimate=pl.CostEstimate(
            flops=flops, bytes_accessed=2 * gathered * width + 2 * len(groups) * rows * (width + slots * block), transcendentals=0
        ),
        name="partial_messages",
    )(cols, counts, off, *pieces, tiles)


def mlp_kernel(
    n_parts, nodes, cot, *refs
):
    parts = refs[:n_parts]
    w_in, bias, w_out, gain, shift, updated, gmsg, gpre_o, act_o, gproj_o, msg_o, vec = refs[n_parts:]
    width = nodes.shape[1]
    message = parts[0][...].astype(F32)
    for part in parts[1:]:
        message = message + part[...].astype(F32)
    message = message.astype(BF16)
    node = nodes[...]
    pre = mm(node, w_in[:width]) + mm(message, w_in[width:]) + bias[...]
    sig = jax.nn.sigmoid(pre)
    act = (pre * sig).astype(BF16)
    proj = mm(act, w_out[...])
    mean = jnp.mean(proj, axis=-1, keepdims=True)
    var = jnp.mean((proj - mean) ** 2, axis=-1, keepdims=True)
    rstd = 1.0 / jnp.sqrt(var + 1e-05)
    normed = (proj - mean) * rstd
    updated[...] = (node.astype(F32) + normed * gain[...] + shift[...]).astype(BF16)
    grad_out = cot[...].astype(F32)
    gscaled = grad_out * gain[...]
    gproj = (
        (
            gscaled
            - jnp.mean(gscaled, axis=-1, keepdims=True)
            - normed * jnp.mean(gscaled * normed, axis=-1, keepdims=True)
        )
        * rstd
    ).astype(BF16)
    gact = mm(gproj, w_out[...], NT)
    gpre = gact * sig * (1.0 + pre * (1.0 - sig))
    gpre_b = gpre.astype(BF16)
    gmsg[...] = mm(gpre_b, w_in[width:], NT).astype(BF16)
    gpre_o[...] = gpre_b
    act_o[...] = act
    gproj_o[...] = gproj
    msg_o[...] = message

    @pl.when(pl.program_id(0) == 0)
    def _():
        vec[...] = jnp.zeros_like(vec)

    vec[0:1] += jnp.sum(gpre, axis=0, keepdims=True)
    vec[1:2] += jnp.sum(grad_out * normed, axis=0, keepdims=True)
    vec[2:3] += jnp.sum(grad_out, axis=0, keepdims=True)


def mlp_call(nodes, cot, parts, w_in, bias, w_out, gain, shift):
    rows, width = nodes.shape
    step = min(rows, 256)
    blocked = pl.BlockSpec((step, width), lambda i: (i, 0))

    def whole(array):
        return pl.BlockSpec(array.shape, lambda i: (0, 0))

    row_like = jax.ShapeDtypeStruct((rows, width), BF16)
    return pl.pallas_call(
        functools.partial(mlp_kernel, len(parts)),
        grid=(rows // step,),
        out_shape=[row_like] * 6 + [jax.ShapeDtypeStruct((8, width), F32)],
        in_specs=[blocked] * (2 + len(parts)) + [whole(a) for a in (w_in, bias, w_out, gain, shift)],
        out_specs=[blocked] * 6 + [pl.BlockSpec((8, width), lambda i: (0, 0))],
        compiler_params=pltpu.CompilerParams(vmem_limit_bytes=40 * MIB),
        cost_estimate=pl.CostEstimate(
            flops=2 * rows * width * width * 5, bytes_accessed=2 * rows * width * 11, transcendentals=rows * width
        ),
        name="mlp",
    )(nodes, cot, *parts, w_in, bias, w_out, gain, shift)


def weight_kernel(factor, nodes, msg, act, gpre, gproj, cot, w_in, vec, grads, direct):
    width = nodes.shape[1]

    @pl.when(pl.program_id(0) == 0)
    def _():
        grads[: 3 * width] = jnp.zeros((3 * width, width), F32)
        grads[3 * width :] = vec[...] * factor

    gpre_b = gpre[...]
    grads[:width] += mm(nodes[...], gpre_b, TN) * factor
    grads[width : 2 * width] += mm(msg[...], gpre_b, TN) * factor
    grads[2 * width : 3 * width] += mm(act[...], gproj[...], TN) * factor
    direct[...] = cot[...].astype(F32) + mm(gpre_b, w_in[:width], NT)


def weight_call(factor, nodes, msg, act, gpre, gproj, cot, w_in, vec):
    rows, width = nodes.shape
    step = min(rows, 256)
    blocked = pl.BlockSpec((step, width), lambda i: (i, 0))

    def whole(shape):
        return pl.BlockSpec(shape, lambda i: (0, 0))

    grads = (3 * width + 8, width)
    return pl.pallas_call(
        functools.partial(weight_kernel, factor),
        grid=(rows // step,),
        out_shape=[jax.ShapeDtypeStruct(grads, F32), jax.ShapeDtypeStruct((rows, width), F32)],
        in_specs=[blocked] * 6 + [whole(w_in.shape), whole(vec.shape)],
        out_specs=[whole(grads), blocked],
        compiler_params=pltpu.CompilerParams(vmem_limit_bytes=40 * MIB),
        cost_estimate=pl.CostEstimate(
            flops=2 * rows * width * width * 4, bytes_accessed=2 * rows * width * 10, transcendentals=0
        ),
        name="weight_grads",
    )(nodes, msg, act, gpre, gproj, cot, w_in, vec)


def grad_copies(total, rows, refs, dst, sem, off):
    if len(refs) == 1:
        return [(None, pltpu.make_async_copy(refs[0], dst, sem.at[0]))]
    own = off[0]
    jobs = [(None, pltpu.make_async_copy(refs[0], dst.at[pl.ds(own * rows, rows)], sem.at[0]))]
    for distance in range(1, total):
        lower = jnp.maximum(own - distance, 0)
        upper = jnp.minimum(own + distance, total - 1)
        jobs.append(
            (
                own >= distance,
                pltpu.make_async_copy(
                    refs[distance], dst.at[pl.ds(lower * rows, rows)], sem.at[distance]
                ),
            )
        )
        jobs.append(
            (
                own + distance < total,
                pltpu.make_async_copy(
                    refs[total - 1 + distance],
                    dst.at[pl.ds(upper * rows, rows)],
                    sem.at[total - 1 + distance],
                ),
            )
        )
    return jobs


def run_jobs(jobs, verb):
    for condition, copy in jobs:
        if condition is None:
            getattr(copy, verb)()
        else:
            pl.when(condition)(getattr(copy, verb))


def back_kernel(total, rows, n_grads, out_pieces, cols, counts, off, *refs):
    grads, tiles = refs[:n_grads], refs[n_grads]
    outs = refs[n_grads + 1 : n_grads + 1 + len(out_pieces)]
    grad_v, tiles_v, acc, sem, tile_sem = refs[n_grads + 1 + len(out_pieces) :]
    row_blocks, slots, block = tiles.shape[:3]
    jobs = grad_copies(total, rows, grads, grad_v, sem, off)
    run_jobs(jobs, "start")
    tile_copy = pltpu.make_async_copy(tiles, tiles_v, tile_sem.at[0])
    tile_copy.start()
    acc[...] = jnp.zeros_like(acc)
    run_jobs(jobs, "wait")
    tile_copy.wait()

    def step(row, carry):
        count = counts[row]
        grad = grad_v[pl.ds(pl.multiple_of(row * block, block), block)]
        for slot in range(slots):
            part = mm(masked_tile(tiles_v, row, slot, count), grad, TN)
            where = pl.ds(pl.multiple_of(cols[row * slots + slot] * block, block), block)
            acc[where] += part
        return carry

    lax.fori_loop(0, row_blocks, step, 0, unroll=2)
    piece = acc.shape[0] // sum(len(members) for members in out_pieces)
    for out, members in zip(outs, out_pieces):
        for index, member in enumerate(members):
            out[pl.ds(index * piece, piece)] = acc[pl.ds(member * piece, piece)].astype(BF16)


def back_call(cols, counts, off, grads, tiles, total, rows, gathered, out_pieces):
    width = grads[0].shape[1]
    row_blocks, slots, block = tiles.shape[:3]
    n_pieces = sum(len(members) for members in out_pieces)
    piece = gathered // n_pieces
    return pl.pallas_call(
        functools.partial(back_kernel, total, rows, len(grads), out_pieces),
        out_shape=[jax.ShapeDtypeStruct((len(m) * piece, width), BF16) for m in out_pieces],
        in_specs=[SMEM, SMEM, SMEM] + [ANY] * (len(grads) + 1),
        out_specs=[VMEM] * len(out_pieces),
        scratch_shapes=[
            pltpu.VMEM((total * rows, width), BF16),
            pltpu.VMEM(tiles.shape, BF16),
            pltpu.VMEM((gathered, width), F32),
            pltpu.SemaphoreType.DMA((2 * total,)),
            pltpu.SemaphoreType.DMA((1,)),
        ],
        compiler_params=pltpu.CompilerParams(vmem_limit_bytes=56 * MIB),
        cost_estimate=pl.CostEstimate(
            flops=row_blocks * slots * 2 * block * block * width,
            bytes_accessed=2 * width * (gathered + total * rows) + 2 * tiles.size,
            transcendentals=0,
        ),
        name="back_terms",
    )(cols, counts, off, *grads, tiles)


def tile_grad_kernel(total, rows, n_grads, n_pieces, chunk, cols, counts, off, *refs):
    grads = refs[:n_grads]
    pieces = refs[n_grads : n_grads + n_pieces]
    out = refs[n_grads + n_pieces]
    grad_v, nodes_v, sem, piece_sem = refs[n_grads + n_pieces + 1 :]
    slots, block = out.shape[1], out.shape[2]
    width = nodes_v.shape[1]
    scale = float(width) ** -0.5

    @pl.when(pl.program_id(0) == 0)
    def _():
        jobs = grad_copies(total, rows, grads, grad_v, sem, off)
        run_jobs(jobs, "start")
        copies = load_pieces(pieces, nodes_v, piece_sem, 0)
        run_jobs(jobs, "wait")
        for copy in copies:
            copy.wait()

    def step(i, carry):
        row = pl.program_id(0) * chunk + i
        count = counts[row]
        grad = grad_v[pl.ds(pl.multiple_of(row * block, block), block)]
        for slot in range(slots):
            node = nodes_v[pl.ds(pl.multiple_of(cols[row * slots + slot] * block, block), block)]
            value = mm(grad, node, NT) * scale
            out[i, slot] = jnp.where(slot < count, value, 0.0).astype(BF16)
        return carry

    lax.fori_loop(0, chunk, step, 0, unroll=2)


def tile_grad_call(cols, counts, off, grads, pieces, shape, total, rows):
    row_blocks, slots, block = shape[:3]
    width = pieces[0].shape[1]
    gathered = sum(piece.shape[0] for piece in pieces)
    chunk = min(row_blocks, 8)
    return pl.pallas_call(
        functools.partial(tile_grad_kernel, total, rows, len(grads), len(pieces), chunk),
        grid=(row_blocks // chunk,),
        out_shape=jax.ShapeDtypeStruct(shape, BF16),
        in_specs=[SMEM, SMEM, SMEM] + [ANY] * (len(grads) + len(pieces)),
        out_specs=pl.BlockSpec((chunk, slots, block, block), lambda i: (i, 0, 0, 0)),
        scratch_shapes=[
            pltpu.VMEM((total * rows, width), BF16),
            pltpu.VMEM((gathered, width), BF16),
            pltpu.SemaphoreType.DMA((2 * total,)),
            pltpu.SemaphoreType.DMA((len(pieces),)),
        ],
        compiler_params=pltpu.CompilerParams(vmem_limit_bytes=40 * MIB),
        cost_estimate=pl.CostEstimate(
            flops=row_blocks * slots * 2 * block * block * width,
            bytes_accessed=2 * width * (gathered + total * rows) + 2 * row_blocks * slots * block * block,
            transcendentals=0,
        ),
        name="tile_grads",
    )(cols, counts, off, *grads, *pieces)


def add(*terms):
    value = terms[0].astype(F32)
    for term in terms[1:]:
        value = value + term.astype(F32)
    return value.astype(BF16)


def swap(value, bit, size):
    return lax.ppermute(value, "row", [(i, i ^ bit) for i in range(size)])


def shift_line(value, by, size):
    return lax.ppermute(value, "col", [(i, i + by) for i in range(size) if 0 <= i + by < size])


def gather_square(nodes):
    half = nodes.shape[0] // 2
    own = (nodes[:half], nodes[half:])
    y_first = swap(own[0], 4, 8)
    x_second = swap(own[1], 2, 8)
    x_first = swap(own[0], 2, 8)
    y_second = swap(own[1], 4, 8)
    diag = (swap(y_first, 2, 8), swap(x_second, 4, 8))
    even = [own, (x_first, x_second), (y_first, y_second), diag]
    pieces = [nodes, swap(nodes, 1, 8)]
    for pair in even[1:]:
        pieces += list(pair) + [swap(value, 1, 8) for value in pair]
    return pieces


def reduce_square(even, odd, rows):
    half = rows // 2
    other = swap(odd, 1, 8)

    def both(place, part):
        where = slice(place * rows + part * half, place * rows + (part + 1) * half)
        return even[where], other[where]

    diag_first = swap(add(*both(3, 0)), 2, 8)
    diag_second = swap(add(*both(3, 1)), 4, 8)
    x_first = swap(add(*both(1, 0)), 2, 8)
    y_second = swap(add(*both(2, 1)), 4, 8)
    y_first = swap(add(*both(2, 0), diag_first), 4, 8)
    x_second = swap(add(*both(1, 1), diag_second), 2, 8)
    first = sum(term.astype(F32) for term in (*both(0, 0), x_first, y_first))
    second = sum(term.astype(F32) for term in (*both(0, 1), x_second, y_second))
    return jnp.concatenate([first, second], axis=0)


def body(n_row, n_col, nodes, tiles, tile_col, tile_count, w_in, bias_in, w_out, ln_gain, ln_shift, cotangent):
    rows, width = nodes.shape
    row_blocks, _, slots, block = tiles.shape[:4]
    tile_local = tiles.reshape(row_blocks, slots, block, block)
    cols = tile_col.reshape(row_blocks * slots)
    counts = tile_count.reshape(row_blocks)
    blocks = rows // block
    square = n_row == 8
    line = n_col == 4
    if square:
        mine = lax.axis_index("row").astype(jnp.int32)
        cols = ((cols // blocks) ^ mine) * blocks + cols % blocks
        pieces = gather_square(nodes)
    else:
        pieces = [lax.all_gather(nodes, "row", axis=0, tiled=True)]
    gathered = n_row * rows
    zero = jnp.zeros((1,), jnp.int32)
    if line:
        off = lax.axis_index("col").astype(jnp.int32).reshape(1)
        part1, part3 = forward_call(cols, counts, off, pieces, tile_local, (1, 3), n_col, rows)
        part2, part0 = forward_call(cols, counts, off, pieces, tile_local, (2, 0), n_col, rows)
        right = shift_line(part3, 1, n_col)
        left = shift_line(part1, -1, n_col)
        right = shift_line(add(part2, right), 1, n_col)
        left = shift_line(add(part2, left), -1, n_col)
        right = shift_line(add(part1, right), 1, n_col)
        left = shift_line(add(part3, left), -1, n_col)
        parts = [part0, right, left]
    else:
        off = zero
        partial = forward_call(
            cols, counts, off, pieces, tile_local, tuple(range(n_col)), n_col, rows
        )
        parts = [
            lax.psum_scatter(
                jnp.concatenate(partial, axis=0), "col", scatter_dimension=0, tiled=True
            )
        ]
    vectors = [v.reshape(1, width) for v in (bias_in, ln_gain, ln_shift)]
    updated, gmsg, gpre_b, act, gproj, message, vec = mlp_call(
        nodes, cotangent, parts, w_in, vectors[0], w_out, vectors[1], vectors[2]
    )
    if line:
        rights, lefts = [gmsg], [gmsg]
        for _ in range(n_col - 1):
            rights.append(shift_line(rights[-1], 1, n_col))
            lefts.append(shift_line(lefts[-1], -1, n_col))
        grads = rights + lefts[1:]
    else:
        grads = [lax.all_gather(gmsg, "col", axis=0, tiled=True)]
    factor = float(rows * n_row * n_col) ** -0.5
    weight_terms, direct = weight_call(
        factor, nodes, message, act, gpre_b, gproj, cotangent, w_in, vec
    )
    weight_sums = lax.psum(weight_terms, ("row", "col"))
    if square:
        odd, even = back_call(
            cols, counts, off, grads, tile_local, n_col, rows, gathered, ((1, 3, 5, 7), (0, 2, 4, 6))
        )
        back = reduce_square(even, odd, rows)
    else:
        (terms,) = back_call(
            cols, counts, off, grads, tile_local, n_col, rows, gathered, (tuple(range(n_row)),)
        )
        back = lax.psum_scatter(terms, "row", scatter_dimension=0, tiled=True).astype(F32)
    grad_nodes = (direct + back).astype(BF16)
    grad_tiles = tile_grad_call(
        cols, counts, off, grads, pieces, tile_local.shape, n_col, rows
    ).reshape(tiles.shape)
    return (
        updated,
        grad_nodes,
        grad_tiles,
        weight_sums[: 2 * width],
        weight_sums[2 * width : 3 * width],
        weight_sums[3 * width : 3 * width + 3],
    )


def solution(mesh):
    placed = (
        P(("row", "col"), None),
        P("row", "col", None, None, None),
        P("row", "col", None),
        P("row", "col"),
        P(),
        P(),
        P(),
        P(),
        P(),
        P(("row", "col"), None),
    )
    return jax.shard_map(
        functools.partial(body, mesh.shape["row"], mesh.shape["col"]),
        mesh=mesh,
        in_specs=placed,
        out_specs=(
            P(("row", "col"), None),
            P(("row", "col"), None),
            P("row", "col", None, None, None),
            P(),
            P(),
            P(),
        ),
        check_vma=False,
    )
```

time: 365 us -> 341 us (0.934); the launches traced: 358 us -> 339 us
  starting transfers between devices: 0.37 us -> 50.1 us
  blocking collectives: 38.9 us -> 0 us
  matrix products: 32.5 us -> 0 us
  Pallas kernels: 0 us -> 31.9 us
  other arithmetic: 41.2 us -> 9.54 us
  waiting for transfers between devices: 186 us -> 207 us
  local copies, waits for them, and re-layouts: 44.9 us -> 25.9 us
    psum x1, waiting for transfers between devices: 28.4 us -> 122 us  [body(): weight_sums = lax.psum(weight_terms, ('row', 'col'))]
    ppermute x0 -> x32, waiting for transfers between devices: none -> 85.3 us  [the longest x12 47.2 us: shift_line(): lax.ppermute(value, 'col', [(i, i + by) for i in range(size) if 0 <= i +...]
    all_gather x2 -> x0, waiting for transfers between devices: 80 us -> none  [the longest x1 40.2 us: body(): lax.all_gather(gmsg, 'col', axis=0, tiled=True)]
    reduce_scatter x2 -> x0, waiting for transfers between devices: 76.9 us -> none  [the longest x1 41.8 us: body(): lax.psum_scatter(partial_value.reshape(row_blocks * block, width).astype(...]
    ppermute x0 -> x32, starting transfers between devices: none -> 50.1 us  [the longest x12 36.3 us: shift_line(): lax.ppermute(value, 'col', [(i, i + by) for i in range(size) if 0 <= i +...]
    psum x1 -> x0, blocking collectives: 38.9 us -> none  [body(): lax.psum((local_in, local_out, local_vectors), ('row', 'col'))]
    dot_general x12 -> x0, matrix products: 32.5 us -> none  [the longest x1 8.34 us: body(): jnp.einsum('rid,rkjd->rkij', grad_rows, picked, preferred_element_type=jn...]
    pallas_call x0 -> x6, Pallas kernels: none -> 31.9 us  [the longest x1 11.3 us: back_call(): pl.pallas_call(functools.partial(back_kernel, total, rows, len(grads), ou...]
  transfers between devices with their start and end apart: 5 -> 33, of which waited for: 5 -> 22; matrix products, arithmetic and copies ran while one was open for 26% -> 3% of each run, Pallas kernels for 0% -> 4%
where the time goes in v1:
time: 341 us; the launch traced here: 339 us
  waiting for transfers between devices  207 us (61%)
  starting transfers between devices  50.1 us (15%)
  Pallas kernels  31.9 us (9%)
  local copies, waits for them, and re-layouts  25.9 us (8%)
  between operations  14.5 us (4%)
  other arithmetic  9.54 us (3%)
    psum x1, waiting for transfers between devices, body(): weight_sums = lax.psum(weight_terms, ('row', 'col'))  122 us
    ppermute x12, waiting for transfers between devices, shift_line(): lax.ppermute(value, 'col', [(i, i + by) for i in range(size) if 0 <= i +...  47.2 us
    ppermute x20, waiting for transfers between devices, swap(): return lax.ppermute(value, 'row', [(i, i ^ bit) for i in range(size)])  38.1 us
    ppermute x12, starting transfers between devices, shift_line(): lax.ppermute(value, 'col', [(i, i + by) for i in range(size) if 0 <= i +...  36.3 us
    unnamed x89, local copies, waits for them, and re-layouts  19.9 us
    ppermute x20, starting transfers between devices, swap(): return lax.ppermute(value, 'row', [(i, i ^ bit) for i in range(size)])  13.8 us
    pallas_call x1, Pallas kernels, back_call(): pl.pallas_call(functools.partial(back_kernel, total, rows, len(grads), ou...  11.3 us
    pallas_call x1, Pallas kernels, tile_grad_call(): pl.pallas_call(functools.partial(tile_grad_kernel, total, rows, len(grads...  8.1 us
  transfers between devices with their start and end apart: 33, of which 22 were waited for; matrix products, arithmetic and copies ran while one was open for 3% of the time, Pallas kernels for 4%

profile of v1, /device:TPU:0, one launch (start us, length us, event | category | flops | bytes accessed | tf_op | source)
XLA Modules:
  0.0 339.0 jit_solution(9965979175652060624)
XLA Ops:
  7.2 1.1 fusion.4
  8.3 3.0 collective-permute-start.6
  11.3 1.5 collective-permute-start.2
  13.4 5.0 %collective-permute-done.6.refs_7_.refs_14_ = bf16[512,256]{1,0:T(8,128)(2,1)S(1)} collective-permute-done((bf16[512,256]{1,0:T(8,128)(2,1)S(1)}, bf16[512,256]{1,0:T(8,128)(2,1)S(1)}, u32[]{:S(2)}, u32[]{:S(2)}) %collective-permute-start.6) | collective-permute-done | bytes 262176 | tf_op jit(solution)/shard_map/ppermute | solution.py:390
  18.5 2.1 collective-permute-done.2.refs_3_.refs_10_
  20.6 3.5 %collective-permute-done.5.refs_6_.refs_13_ = bf16[512,256]{1,0:T(8,128)(2,1)S(1)} collective-permute-done((bf16[512,256]{1,0:T(8,128)(2,1)S(1)}, bf16[512,256]{1,0:T(8,128)(2,1)S(1)}, u32[]{:S(2)}, u32[]{:S(2)}) %collective-permute-start.5) | collective-permute-done | bytes 262176 | tf_op jit(solution)/shard_map/ppermute | solution.py:390
  24.7 1.5 collective-permute-start.9
  26.3 2.5 collective-permute-done.10.refs_11_.refs_18_
  29.4 3.7 %collective-permute-done.9.refs_10_.refs_17_ = bf16[512,256]{1,0:T(8,128)(2,1)S(1)} collective-permute-done((bf16[512,256]{1,0:T(8,128)(2,1)S(1)}, bf16[512,256]{1,0:T(8,128)(2,1)S(1)}, u32[]{:S(2)}, u32[]{:S(2)}) %collective-permute-start.9) | collective-permute-done | bytes 262176 | tf_op jit(solution)/shard_map/ppermute | solution.py:390
  34.7 2.2 copy-done
  36.9 1.0 copy-done.1
  38.6 3.2 partial_messages.3
  41.8 1.3 collective-permute-start.16
  43.1 4.6 %collective-permute-start.13 = (bf16[1024,256]{1,0:T(8,128)(2,1)S(1)}, bf16[1024,256]{1,0:T(8,128)(2,1)S(1)}, u32[]{:S(2)}, u32[]{:S(2)}) collective-permute-start(bf16[1024,256]{1,0:T(8,128)(2,1)S(1)} %get-tuple-element.24), channel_id=1, source_target_pairs={{0,1},{1,2},{2,3},{4,5},{5,6},{6,7},{8,9},{9,10},{10,11},{12,13},{... | collective-permute-start | bytes 1572872 | tf_op jit(solution)/shard_map/ppermute | solution.py:394
  47.7 3.2 partial_messages.2
  50.9 6.9 %collective-permute-done.16 = bf16[1024,256]{1,0:T(8,128)(2,1)S(1)} collective-permute-done((bf16[1024,256]{1,0:T(8,128)(2,1)S(1)}, bf16[1024,256]{1,0:T(8,128)(2,1)S(1)}, u32[]{:S(2)}, u32[]{:S(2)}) %collective-permute-start.16) | collective-permute-done | bytes 524320 | tf_op jit(solution)/shard_map/ppermute | solution.py:394
  57.8 1.2 collective-permute-done.13
  59.3 1.4 collective-permute-start.17
  60.7 5.0 %collective-permute-start.14 = (bf16[1024,256]{1,0:T(8,128)(2,1)S(1)}, bf16[1024,256]{1,0:T(8,128)(2,1)S(1)}, u32[]{:S(2)}, u32[]{:S(2)}) collective-permute-start(bf16[1024,256]{1,0:T(8,128)(2,1)S(1)} %get-tuple-element.54), channel_id=1, source_target_pairs={{0,1},{1,2},{2,3},{4,5},{5,6},{6,7},{8,9},{9,10},{10,11},{12,13},{... | collective-permute-start | bytes 1572872 | tf_op jit(solution)/shard_map/ppermute | solution.py:394
  65.8 9.2 %collective-permute-done.17 = bf16[1024,256]{1,0:T(8,128)(2,1)S(1)} collective-permute-done((bf16[1024,256]{1,0:T(8,128)(2,1)S(1)}, bf16[1024,256]{1,0:T(8,128)(2,1)S(1)}, u32[]{:S(2)}, u32[]{:S(2)}) %collective-permute-start.17) | collective-permute-done | bytes 524320 | tf_op jit(solution)/shard_map/ppermute | solution.py:394
  75.1 1.3 collective-permute-start.18
  76.6 4.6 %collective-permute-start.15 = (bf16[1024,256]{1,0:T(8,128)(2,1)S(1)}, bf16[1024,256]{1,0:T(8,128)(2,1)S(1)}, u32[]{:S(2)}, u32[]{:S(2)}) collective-permute-start(bf16[1024,256]{1,0:T(8,128)(2,1)S(1)} %add_convert_fusion.1), channel_id=1, source_target_pairs={{0,1},{1,2},{2,3},{4,5},{5,6},{6,7},{8,9},{9,10},{10,11},{12,13},{... | collective-permute-start | bytes 1572872 | tf_op jit(solution)/shard_map/ppermute | solution.py:394
  81.2 8.1 %collective-permute-done.18.refs_2_ = bf16[1024,256]{1,0:T(8,128)(2,1)S(1)} collective-permute-done((bf16[1024,256]{1,0:T(8,128)(2,1)S(1)}, bf16[1024,256]{1,0:T(8,128)(2,1)S(1)}, u32[]{:S(2)}, u32[]{:S(2)}) %collective-permute-start.18) | collective-permute-done | bytes 524320 | tf_op jit(solution)/shard_map/ppermute | solution.py:394
  89.3 1.3 collective-permute-done.15.refs_1_
  90.7 4.7 %mlp.1 = (bf16[1024,256]{1,0:T(8,128)(2,1)}, bf16[1024,256]{1,0:T(8,128)(2,1)S(1)}, bf16[1024,256]{1,0:T(8,128)(2,1)S(1)}, bf16[1024,256]{1,0:T(8,128)(2,1)S(1)}...) custom-call(bf16[1024,256]{1,0:T(8,128)(2,1)S(1)} %copy-done.2, ...), custom_call_target="tpu_custom_call" | custom-call | flops 671088640 | bytes 5767168 | tf_op jit(solution)/shard_map/mlp/pallas_call | solution.py:179
  98.6 1.3 collective-permute-start.22
  99.9 5.1 %collective-permute-start.19 = (bf16[1024,256]{1,0:T(8,128)(2,1)S(1)}, bf16[1024,256]{1,0:T(8,128)(2,1)S(1)}, u32[]{:S(2)}, u32[]{:S(2)}) collective-permute-start(bf16[1024,256]{1,0:T(8,128)(2,1)S(1)} %get-tuple-element.32.refs_0_), channel_id=1, source_target_pairs={{0,1},{1,2},{2,3},{4,5},{5,6},{6,7},{8,9},{9,10},{10,11},{12,13},{... | collective-permute-start | bytes 1572872 | tf_op jit(solution)/shard_map/ppermute | solution.py:394
  105.0 7.4 %collective-permute-done.22.refs_4_ = bf16[1024,256]{1,0:T(8,128)(2,1)S(1)} collective-permute-done((bf16[1024,256]{1,0:T(8,128)(2,1)S(1)}, bf16[1024,256]{1,0:T(8,128)(2,1)S(1)}, u32[]{:S(2)}, u32[]{:S(2)}) %collective-permute-start.22) | collective-permute-done | bytes 524320 | tf_op jit(solution)/shard_map/ppermute | solution.py:394
  112.3 1.3 collective-permute-start.23
  113.6 4.6 %collective-permute-start.20 = (bf16[1024,256]{1,0:T(8,128)(2,1)S(1)}, bf16[1024,256]{1,0:T(8,128)(2,1)S(1)}, u32[]{:S(2)}, u32[]{:S(2)}) collective-permute-start(bf16[1024,256]{1,0:T(8,128)(2,1)S(1)} %collective-permute-done.19.refs_1_), channel_id=1, source_target_pairs={{0,1},{1,2},{2,3},{4,5},{5,6},{6,7},{8,9},{9,10},{10,11},{12,13},{... | collective-permute-start | bytes 1572872 | tf_op jit(solution)/shard_map/ppermute | solution.py:394
  118.2 6.4 %collective-permute-done.23.refs_5_ = bf16[1024,256]{1,0:T(8,128)(2,1)S(1)} collective-permute-done((bf16[1024,256]{1,0:T(8,128)(2,1)S(1)}, bf16[1024,256]{1,0:T(8,128)(2,1)S(1)}, u32[]{:S(2)}, u32[]{:S(2)}) %collective-permute-start.23) | collective-permute-done | bytes 524320 | tf_op jit(solution)/shard_map/ppermute | solution.py:394
  124.6 1.3 collective-permute-start.24
  126.0 4.6 %collective-permute-start.21 = (bf16[1024,256]{1,0:T(8,128)(2,1)S(1)}, bf16[1024,256]{1,0:T(8,128)(2,1)S(1)}, u32[]{:S(2)}, u32[]{:S(2)}) collective-permute-start(bf16[1024,256]{1,0:T(8,128)(2,1)S(1)} %collective-permute-done.20.refs_2_), channel_id=1, source_target_pairs={{0,1},{1,2},{2,3},{4,5},{5,6},{6,7},{8,9},{9,10},{10,11},{12,13},{... | collective-permute-start | bytes 1572872 | tf_op jit(solution)/shard_map/ppermute | solution.py:394
  130.5 5.5 %collective-permute-done.24.refs_6_ = bf16[1024,256]{1,0:T(8,128)(2,1)S(1)} collective-permute-done((bf16[1024,256]{1,0:T(8,128)(2,1)S(1)}, bf16[1024,256]{1,0:T(8,128)(2,1)S(1)}, u32[]{:S(2)}, u32[]{:S(2)}) %collective-permute-start.24) | collective-permute-done | bytes 524320 | tf_op jit(solution)/shard_map/ppermute | solution.py:394
  136.0 1.2 collective-permute-done.21.refs_3_
  138.1 11.3 %back_terms.1 = (bf16[4096,256]{1,0:T(8,128)(2,1)}, bf16[4096,256]{1,0:T(8,128)(2,1)}) custom-call(s32[128]{0:T(128)} %copy-done.37, s32[32]{0:T(128)} %bitcast.14, s32[1]{0:T(128)} %bitcast.1.off, bf16[1024,256]{1,0:T(8,128)(2,1)} %copy-done.7, bf16[1024,256]{1,0:T(8,128)(2,1)} %copy-done.11, bf16[1024,256]{1,0:T(8,128)(2,1)} %copy-done.15, ...), custom_call_target="tpu_custom_call" | custom-call | flops 1073741824 | bytes 10485760 | tf_op jit(solution)/shard_map/back_terms/pallas_call | solution.py:302
  149.5 4.4 %collective-permute-done.25 = bf16[4096,256]{1,0:T(8,128)(2,1)S(1)} collective-permute-done((bf16[4096,256]{1,0:T(8,128)(2,1)}, bf16[4096,256]{1,0:T(8,128)(2,1)S(1)}, u32[]{:S(2)}, u32[]{:S(2)}) %collective-permute-start.25) | collective-permute-done | bytes 2097184 | tf_op jit(solution)/shard_map/ppermute | solution.py:390
  153.8 1.5 add_convert_fusion.7
  155.4 1.2 collective-permute-start.27
  157.5 7.0 %collective-permute-done.27 = bf16[512,256]{1,0:T(8,128)(2,1)S(1)} collective-permute-done((bf16[512,256]{1,0:T(8,128)(2,1)S(1)}, bf16[512,256]{1,0:T(8,128)(2,1)S(1)}, u32[]{:S(2)}, u32[]{:S(2)}) %collective-permute-start.27) | collective-permute-done | bytes 262176 | tf_op jit(solution)/shard_map/ppermute | solution.py:390
  164.6 1.0 add_convert_fusion.5
  165.6 1.3 collective-permute-start.28
  166.9 2.5 collective-permute-done.26
  169.4 3.0 collective-permute-done.28
  172.4 2.2 convert_add_fusion.3
  174.6 1.2 collective-permute-start.29
  175.9 1.5 weight_grads.1
  177.3 1.0 copy-done.22
  180.1 3.0 collective-permute-done.29
  183.1 1.9 add_convert_fusion.3
  185.9 121.7 %all-reduce.2.cloned.1.call-done = f32[776,256]{1,0:T(8,128)} async-done(((f32[776,256]{1,0:T(8,128)}), f32[776,256]{1,0:T(8,128)}) %all-reduce.2.cloned.1.call-update) | async-done | bytes 794640 | tf_op jit(solution)/shard_map/psum | solution.py:485
  307.6 1.3 slice.94
  308.9 1.7 slice.93
  310.6 1.9 slice.92
  312.4 0.9 copy-done.4
  314.4 1.0 copy-done.8
  315.4 1.0 copy-done.10
  316.4 1.0 copy-done.12
  317.5 1.0 copy-done.14
  318.5 1.0 copy-done.16
  319.6 1.0 copy-done.18
  320.6 1.0 copy-done.20
  321.6 8.1 %tile_grads.1 = bf16[32,4,128,128]{3,2,1,0:T(8,128)(2,1)} custom-call(s32[128]{0:T(128)S(1)} %copy-done.38, s32[32]{0:T(128)S(1)} %bitcast.17, s32[1]{0:T(128)} %bitcast.1.off, bf16[1024,256]{1,0:T(8,128)(2,1)S(1)} %copy-done.8, bf16[1024,256]{1,0:T(8,128)(2,1)S(1)} %copy-done.12, bf16[1024,256]{1,0:T(8,128)(2,1)S(1)} %copy-done.16, ...), custom_call_target="tpu_custom_call" | custom-call | flops 1073741824 | bytes 10485760 | tf_op jit(solution)/shard_map/tile_grads/pallas_call | solution.py:360
  329.8 1.4 convert_add_fusion.2
  (113 shorter events, 14.5 us)
Async XLA Ops:
  7.2 300.4 %all-reduce.2.cloned.1.call-start = ((), (), s32[]{:S(2)}) async-start(), calls=%async_computation | async-start | bytes 1589248 | tf_op jit(solution)/shard_map/psum | solution.py:485
  8.3 10.2 %collective-permute-start.6 = (bf16[512,256]{1,0:T(8,128)(2,1)S(1)}, bf16[512,256]{1,0:T(8,128)(2,1)S(1)}, u32[]{:S(2)}, u32[]{:S(2)}) collective-permute-start(bf16[512,256]{1,0:T(8,128)(2,1)S(1)} %get-tuple-element.55), channel_id=1, source_target_pairs={{0,16},{4,20},{8,24},{12,28},{16,0},{20,4},{24,8},{28,12},{1,17},{... | collective-permute-start | bytes 786440 | tf_op jit(solution)/shard_map/ppermute | solution.py:390
  11.3 9.2 %collective-permute-start.2 = (bf16[512,256]{1,0:T(8,128)(2,1)S(1)}, bf16[512,256]{1,0:T(8,128)(2,1)S(1)}, u32[]{:S(2)}, u32[]{:S(2)}) collective-permute-start(bf16[512,256]{1,0:T(8,128)(2,1)S(1)} %get-tuple-element.55), channel_id=1, source_target_pairs={{0,8},{4,12},{8,0},{12,4},{16,24},{20,28},{24,16},{28,20},{1,9},{5... | collective-permute-start | bytes 786440 | tf_op jit(solution)/shard_map/ppermute | solution.py:390
  12.8 11.3 %collective-permute-start.5 = (bf16[512,256]{1,0:T(8,128)(2,1)S(1)}, bf16[512,256]{1,0:T(8,128)(2,1)S(1)}, u32[]{:S(2)}, u32[]{:S(2)}) collective-permute-start(bf16[512,256]{1,0:T(8,128)(2,1)S(1)} %get-tuple-element.56), channel_id=1, source_target_pairs={{0,16},{4,20},{8,24},{12,28},{16,0},{20,4},{24,8},{28,12},{1,17},{... | collective-permute-start | bytes 786440 | tf_op jit(solution)/shard_map/ppermute | solution.py:390
  13.3 11.4 %collective-permute-start.1 = (bf16[512,256]{1,0:T(8,128)(2,1)S(1)}, bf16[512,256]{1,0:T(8,128)(2,1)S(1)}, u32[]{:S(2)}, u32[]{:S(2)}) collective-permute-start(bf16[512,256]{1,0:T(8,128)(2,1)S(1)} %get-tuple-element.56), channel_id=1, source_target_pairs={{0,8},{4,12},{8,0},{12,4},{16,24},{20,28},{24,16},{28,20},{1,9},{5... | collective-permute-start | bytes 786440 | tf_op jit(solution)/shard_map/ppermute | solution.py:390
  13.4 20.6 %collective-permute-start = (bf16[1024,256]{1,0:T(8,128)(2,1)}, bf16[1024,256]{1,0:T(8,128)(2,1)S(1)}, u32[]{:S(2)}, u32[]{:S(2)}) collective-permute-start(bf16[1024,256]{1,0:T(8,128)(2,1)} %refs_7_.1), channel_id=1, source_target_pairs={{0,4},{4,0},{8,12},{12,8},{16,20},{20,16},{24,28},{28,24},{1,5},{5... | collective-permute-start | bytes 1572872 | tf_op jit(solution)/shard_map/ppermute | solution.py:390
  18.4 7.7 %collective-permute-start.8 = (bf16[512,256]{1,0:T(8,128)(2,1)S(1)}, bf16[512,256]{1,0:T(8,128)(2,1)S(1)}, u32[]{:S(2)}, u32[]{:S(2)}) collective-permute-start(bf16[512,256]{1,0:T(8,128)(2,1)S(1)} %collective-permute-done.6.refs_7_.refs_14_), channel_id=1, source_target_pairs={{0,4},{4,0},{8,12},{12,8},{16,20},{20,16},{24,28},{28,24},{1,5},{5... | collective-permute-start | bytes 786440 | tf_op jit(solution)/shard_map/ppermute | solution.py:390
  20.5 8.3 %collective-permute-start.10 = (bf16[512,256]{1,0:T(8,128)(2,1)S(1)}, bf16[512,256]{1,0:T(8,128)(2,1)S(1)}, u32[]{:S(2)}, u32[]{:S(2)}) collective-permute-start(bf16[512,256]{1,0:T(8,128)(2,1)S(1)} %collective-permute-done.2.refs_3_.refs_10_), channel_id=1, source_target_pairs={{0,16},{4,20},{8,24},{12,28},{16,0},{20,4},{24,8},{28,12},{1,17},{... | collective-permute-start | bytes 786440 | tf_op jit(solution)/shard_map/ppermute | solution.py:390
  24.1 4.8 %collective-permute-start.4 = (bf16[512,256]{1,0:T(8,128)(2,1)S(1)}, bf16[512,256]{1,0:T(8,128)(2,1)S(1)}, u32[]{:S(2)}, u32[]{:S(2)}) collective-permute-start(bf16[512,256]{1,0:T(8,128)(2,1)S(1)} %collective-permute-done.2.refs_3_.refs_10_), channel_id=1, source_target_pairs={{0,4},{4,0},{8,12},{12,8},{16,20},{20,16},{24,28},{28,24},{1,5},{5... | collective-permute-start | bytes 786440 | tf_op jit(solution)/shard_map/ppermute | solution.py:390
  24.7 8.4 %collective-permute-start.9 = (bf16[512,256]{1,0:T(8,128)(2,1)S(1)}, bf16[512,256]{1,0:T(8,128)(2,1)S(1)}, u32[]{:S(2)}, u32[]{:S(2)}) collective-permute-start(bf16[512,256]{1,0:T(8,128)(2,1)S(1)} %collective-permute-done.5.refs_6_.refs_13_), channel_id=1, source_target_pairs={{0,8},{4,12},{8,0},{12,4},{16,24},{20,28},{24,16},{28,20},{1,9},{5... | collective-permute-start | bytes 786440 | tf_op jit(solution)/shard_map/ppermute | solution.py:390
  26.2 7.8 %collective-permute-start.7 = (bf16[512,256]{1,0:T(8,128)(2,1)S(1)}, bf16[512,256]{1,0:T(8,128)(2,1)S(1)}, u32[]{:S(2)}, u32[]{:S(2)}) collective-permute-start(bf16[512,256]{1,0:T(8,128)(2,1)S(1)} %collective-permute-done.5.refs_6_.refs_13_), channel_id=1, source_target_pairs={{0,4},{4,0},{8,12},{12,8},{16,20},{20,16},{24,28},{28,24},{1,5},{5... | collective-permute-start | bytes 786440 | tf_op jit(solution)/shard_map/ppermute | solution.py:390
  28.9 5.1 %collective-permute-start.3 = (bf16[512,256]{1,0:T(8,128)(2,1)S(1)}, bf16[512,256]{1,0:T(8,128)(2,1)S(1)}, u32[]{:S(2)}, u32[]{:S(2)}) collective-permute-start(bf16[512,256]{1,0:T(8,128)(2,1)S(1)} %collective-permute-done.1.refs_2_.refs_9_), channel_id=1, source_target_pairs={{0,4},{4,0},{8,12},{12,8},{16,20},{20,16},{24,28},{28,24},{1,5},{5... | collective-permute-start | bytes 786440 | tf_op jit(solution)/shard_map/ppermute | solution.py:390
  28.9 5.2 %collective-permute-start.12 = (bf16[512,256]{1,0:T(8,128)(2,1)S(1)}, bf16[512,256]{1,0:T(8,128)(2,1)S(1)}, u32[]{:S(2)}, u32[]{:S(2)}) collective-permute-start(bf16[512,256]{1,0:T(8,128)(2,1)S(1)} %collective-permute-done.10.refs_11_.refs_18_), channel_id=1, source_target_pairs={{0,4},{4,0},{8,12},{12,8},{16,20},{20,16},{24,28},{28,24},{1,5},{5... | collective-permute-start | bytes 786440 | tf_op jit(solution)/shard_map/ppermute | solution.py:390
  33.1 1.7 collective-permute-start.11
  34.0 13.7 %copy-start.37 = (s32[128]{0:T(128)}, s32[128]{0:T(128)S(1)}, u32[]{:S(2)}) copy-start(s32[128]{0:T(128)S(1)} %fusion.3.cols) | copy-start | bytes 1540
  34.0 13.7 %copy-start.3 = (bf16[512,256]{1,0:T(8,128)(2,1)}, bf16[512,256]{1,0:T(8,128)(2,1)S(1)}, u32[]{:S(2)}) copy-start(bf16[512,256]{1,0:T(8,128)(2,1)S(1)} %collective-permute-done.3.refs_4_.refs_11_) | copy-start | bytes 786436
  34.0 13.7 %copy-start.5 = (bf16[512,256]{1,0:T(8,128)(2,1)}, bf16[512,256]{1,0:T(8,128)(2,1)S(1)}, u32[]{:S(2)}) copy-start(bf16[512,256]{1,0:T(8,128)(2,1)S(1)} %collective-permute-done.12.refs_13_.refs_20_) | copy-start | bytes 786436
  34.7 2.2 copy-start
  36.9 1.0 copy-start.1
  41.8 16.0 %collective-permute-start.16 = (bf16[1024,256]{1,0:T(8,128)(2,1)S(1)}, bf16[1024,256]{1,0:T(8,128)(2,1)S(1)}, u32[]{:S(2)}, u32[]{:S(2)}) collective-permute-start(bf16[1024,256]{1,0:T(8,128)(2,1)S(1)} %get-tuple-element.22), channel_id=1, source_target_pairs={{1,0},{2,1},{3,2},{5,4},{6,5},{7,6},{9,8},{10,9},{11,10},{13,12},{... | collective-permute-start | bytes 1572872 | tf_op jit(solution)/shard_map/ppermute | solution.py:394
  43.1 15.8 %collective-permute-start.13 = (bf16[1024,256]{1,0:T(8,128)(2,1)S(1)}, bf16[1024,256]{1,0:T(8,128)(2,1)S(1)}, u32[]{:S(2)}, u32[]{:S(2)}) collective-permute-start(bf16[1024,256]{1,0:T(8,128)(2,1)S(1)} %get-tuple-element.24), channel_id=1, source_target_pairs={{0,1},{1,2},{2,3},{4,5},{5,6},{6,7},{8,9},{9,10},{10,11},{12,13},{... | collective-permute-start | bytes 1572872 | tf_op jit(solution)/shard_map/ppermute | solution.py:394
  59.2 31.4 %copy-start.2 = (bf16[1024,256]{1,0:T(8,128)(2,1)S(1)}, bf16[1024,256]{1,0:T(8,128)(2,1)}, u32[]{:S(2)}) copy-start(bf16[1024,256]{1,0:T(8,128)(2,1)} %refs_7_.1) | copy-start | bytes 1572868
  59.2 31.4 %copy-start.21 = (bf16[1024,256]{1,0:T(8,128)(2,1)S(1)}, bf16[1024,256]{1,0:T(8,128)(2,1)}, u32[]{:S(2)}) copy-start(bf16[1024,256]{1,0:T(8,128)(2,1)} %cot.3) | copy-start | bytes 1572868
  59.2 31.4 %copy-start.24 = (bf16[512,256]{1,0:T(8,128)(2,1)S(1)}, bf16[512,256]{1,0:T(8,128)(2,1)}, u32[]{:S(2)}) copy-start(bf16[512,256]{1,0:T(8,128)(2,1)} %w_in.1) | copy-start | bytes 786436
  59.2 31.4 %copy-start.34 = (bf16[256,256]{1,0:T(8,128)(2,1)S(1)}, bf16[256,256]{1,0:T(8,128)(2,1)}, u32[]{:S(2)}) copy-start(bf16[256,256]{1,0:T(8,128)(2,1)} %refs_5_.1) | copy-start | bytes 393220
  59.3 31.4 %copy-start.39 = (f32[256]{0:T(256)S(1)}, f32[256]{0:T(256)}, u32[]{:S(2)}) copy-start(f32[256]{0:T(256)} %param.15) | copy-start | bytes 3076
  59.3 31.4 %copy-start.40 = (f32[256]{0:T(256)S(1)}, f32[256]{0:T(256)}, u32[]{:S(2)}) copy-start(f32[256]{0:T(256)} %param.17) | copy-start | bytes 3076
  59.3 31.4 %copy-start.41 = (f32[256]{0:T(256)S(1)}, f32[256]{0:T(256)}, u32[]{:S(2)}) copy-start(f32[256]{0:T(256)} %param.18) | copy-start | bytes 3076
  59.3 15.7 %collective-permute-start.17 = (bf16[1024,256]{1,0:T(8,128)(2,1)S(1)}, bf16[1024,256]{1,0:T(8,128)(2,1)S(1)}, u32[]{:S(2)}, u32[]{:S(2)}) collective-permute-start(bf16[1024,256]{1,0:T(8,128)(2,1)S(1)} %get-tuple-element.53), channel_id=1, source_target_pairs={{1,0},{2,1},{3,2},{5,4},{6,5},{7,6},{9,8},{10,9},{11,10},{13,12},{... | collective-permute-start | bytes 1572872 | tf_op jit(solution)/shard_map/ppermute | solution.py:394
  60.7 15.7 %collective-permute-start.14 = (bf16[1024,256]{1,0:T(8,128)(2,1)S(1)}, bf16[1024,256]{1,0:T(8,128)(2,1)S(1)}, u32[]{:S(2)}, u32[]{:S(2)}) collective-permute-start(bf16[1024,256]{1,0:T(8,128)(2,1)S(1)} %get-tuple-element.54), channel_id=1, source_target_pairs={{0,1},{1,2},{2,3},{4,5},{5,6},{6,7},{8,9},{9,10},{10,11},{12,13},{... | collective-permute-start | bytes 1572872 | tf_op jit(solution)/shard_map/ppermute | solution.py:394
  75.1 14.2 %collective-permute-start.18 = (bf16[1024,256]{1,0:T(8,128)(2,1)S(1)}, bf16[1024,256]{1,0:T(8,128)(2,1)S(1)}, u32[]{:S(2)}, u32[]{:S(2)}) collective-permute-start(bf16[1024,256]{1,0:T(8,128)(2,1)S(1)} %add_convert_fusion), channel_id=1, source_target_pairs={{1,0},{2,1},{3,2},{5,4},{6,5},{7,6},{9,8},{10,9},{11,10},{13,12},{... | collective-permute-start | bytes 1572872 | tf_op jit(solution)/shard_map/ppermute | solution.py:394
  76.6 14.1 %collective-permute-start.15 = (bf16[1024,256]{1,0:T(8,128)(2,1)S(1)}, bf16[1024,256]{1,0:T(8,128)(2,1)S(1)}, u32[]{:S(2)}, u32[]{:S(2)}) collective-permute-start(bf16[1024,256]{1,0:T(8,128)(2,1)S(1)} %add_convert_fusion.1), channel_id=1, source_target_pairs={{0,1},{1,2},{2,3},{4,5},{5,6},{6,7},{8,9},{9,10},{10,11},{12,13},{... | collective-permute-start | bytes 1572872 | tf_op jit(solution)/shard_map/ppermute | solution.py:394
  98.6 38.6 %copy-start.7 = (bf16[1024,256]{1,0:T(8,128)(2,1)}, bf16[1024,256]{1,0:T(8,128)(2,1)S(1)}, u32[]{:S(2)}) copy-start(bf16[1024,256]{1,0:T(8,128)(2,1)S(1)} %get-tuple-element.32.refs_0_) | copy-start | bytes 1572868
  98.6 13.7 %collective-permute-start.22 = (bf16[1024,256]{1,0:T(8,128)(2,1)S(1)}, bf16[1024,256]{1,0:T(8,128)(2,1)S(1)}, u32[]{:S(2)}, u32[]{:S(2)}) collective-permute-start(bf16[1024,256]{1,0:T(8,128)(2,1)S(1)} %get-tuple-element.32.refs_0_), channel_id=1, source_target_pairs={{1,0},{2,1},{3,2},{5,4},{6,5},{7,6},{9,8},{10,9},{11,10},{13,12},{... | collective-permute-start | bytes 1572872 | tf_op jit(solution)/shard_map/ppermute | solution.py:394
  99.9 13.7 %collective-permute-start.19 = (bf16[1024,256]{1,0:T(8,128)(2,1)S(1)}, bf16[1024,256]{1,0:T(8,128)(2,1)S(1)}, u32[]{:S(2)}, u32[]{:S(2)}) collective-permute-start(bf16[1024,256]{1,0:T(8,128)(2,1)S(1)} %get-tuple-element.32.refs_0_), channel_id=1, source_target_pairs={{0,1},{1,2},{2,3},{4,5},{5,6},{6,7},{8,9},{9,10},{10,11},{12,13},{... | collective-permute-start | bytes 1572872 | tf_op jit(solution)/shard_map/ppermute | solution.py:394
  112.3 24.9 %copy-start.9 = (bf16[1024,256]{1,0:T(8,128)(2,1)}, bf16[1024,256]{1,0:T(8,128)(2,1)S(1)}, u32[]{:S(2)}) copy-start(bf16[1024,256]{1,0:T(8,128)(2,1)S(1)} %collective-permute-done.22.refs_4_) | copy-start | bytes 1572868
  112.3 12.3 %collective-permute-start.23 = (bf16[1024,256]{1,0:T(8,128)(2,1)S(1)}, bf16[1024,256]{1,0:T(8,128)(2,1)S(1)}, u32[]{:S(2)}, u32[]{:S(2)}) collective-permute-start(bf16[1024,256]{1,0:T(8,128)(2,1)S(1)} %collective-permute-done.22.refs_4_), channel_id=1, source_target_pairs={{1,0},{2,1},{3,2},{5,4},{6,5},{7,6},{9,8},{10,9},{11,10},{13,12},{... | collective-permute-start | bytes 1572872 | tf_op jit(solution)/shard_map/ppermute | solution.py:394
  113.6 23.6 %copy-start.11 = (bf16[1024,256]{1,0:T(8,128)(2,1)}, bf16[1024,256]{1,0:T(8,128)(2,1)S(1)}, u32[]{:S(2)}) copy-start(bf16[1024,256]{1,0:T(8,128)(2,1)S(1)} %collective-permute-done.19.refs_1_) | copy-start | bytes 1572868
  113.6 12.3 %collective-permute-start.20 = (bf16[1024,256]{1,0:T(8,128)(2,1)S(1)}, bf16[1024,256]{1,0:T(8,128)(2,1)S(1)}, u32[]{:S(2)}, u32[]{:S(2)}) collective-permute-start(bf16[1024,256]{1,0:T(8,128)(2,1)S(1)} %collective-permute-done.19.refs_1_), channel_id=1, source_target_pairs={{0,1},{1,2},{2,3},{4,5},{5,6},{6,7},{8,9},{9,10},{10,11},{12,13},{... | collective-permute-start | bytes 1572872 | tf_op jit(solution)/shard_map/ppermute | solution.py:394
  124.6 12.6 %copy-start.13 = (bf16[1024,256]{1,0:T(8,128)(2,1)}, bf16[1024,256]{1,0:T(8,128)(2,1)S(1)}, u32[]{:S(2)}) copy-start(bf16[1024,256]{1,0:T(8,128)(2,1)S(1)} %collective-permute-done.23.refs_5_) | copy-start | bytes 1572868
  124.6 11.4 %collective-permute-start.24 = (bf16[1024,256]{1,0:T(8,128)(2,1)S(1)}, bf16[1024,256]{1,0:T(8,128)(2,1)S(1)}, u32[]{:S(2)}, u32[]{:S(2)}) collective-permute-start(bf16[1024,256]{1,0:T(8,128)(2,1)S(1)} %collective-permute-done.23.refs_5_), channel_id=1, source_target_pairs={{1,0},{2,1},{3,2},{5,4},{6,5},{7,6},{9,8},{10,9},{11,10},{13,12},{... | collective-permute-start | bytes 1572872 | tf_op jit(solution)/shard_map/ppermute | solution.py:394
  125.9 11.3 %copy-start.15 = (bf16[1024,256]{1,0:T(8,128)(2,1)}, bf16[1024,256]{1,0:T(8,128)(2,1)S(1)}, u32[]{:S(2)}) copy-start(bf16[1024,256]{1,0:T(8,128)(2,1)S(1)} %collective-permute-done.20.refs_2_) | copy-start | bytes 1572868
  126.0 11.3 %collective-permute-start.21 = (bf16[1024,256]{1,0:T(8,128)(2,1)S(1)}, bf16[1024,256]{1,0:T(8,128)(2,1)S(1)}, u32[]{:S(2)}, u32[]{:S(2)}) collective-permute-start(bf16[1024,256]{1,0:T(8,128)(2,1)S(1)} %collective-permute-done.20.refs_2_), channel_id=1, source_target_pairs={{0,1},{1,2},{2,3},{4,5},{5,6},{6,7},{8,9},{9,10},{10,11},{12,13},{... | collective-permute-start | bytes 1572872 | tf_op jit(solution)/shard_map/ppermute | solution.py:394
  136.0 1.2 copy-start.17
  149.4 4.4 %collective-permute-start.25 = (bf16[4096,256]{1,0:T(8,128)(2,1)}, bf16[4096,256]{1,0:T(8,128)(2,1)S(1)}, u32[]{:S(2)}, u32[]{:S(2)}) collective-permute-start(bf16[4096,256]{1,0:T(8,128)(2,1)} %get-tuple-element.34), channel_id=1, source_target_pairs={{0,4},{4,0},{8,12},{12,8},{16,20},{20,16},{24,28},{28,24},{1,5},{5... | collective-permute-start | bytes 6291464 | tf_op jit(solution)/shard_map/ppermute | solution.py:390
  153.8 20.8 %copy-start.42 = (bf16[4096,256]{1,0:T(8,128)(2,1)}, bf16[4096,256]{1,0:T(8,128)(2,1)S(1)}, u32[]{:S(2)}) copy-start(bf16[4096,256]{1,0:T(8,128)(2,1)S(1)} %collective-permute-done.25) | copy-start | bytes 6291460
  155.4 9.2 %collective-permute-start.27 = (bf16[512,256]{1,0:T(8,128)(2,1)S(1)}, bf16[512,256]{1,0:T(8,128)(2,1)S(1)}, u32[]{:S(2)}, u32[]{:S(2)}) collective-permute-start(bf16[512,256]{1,0:T(8,128)(2,1)S(1)} %get-tuple-element.52), channel_id=1, source_target_pairs={{0,8},{4,12},{8,0},{12,4},{16,24},{20,28},{24,16},{28,20},{1,9},{5... | collective-permute-start | bytes 786440 | tf_op jit(solution)/shard_map/ppermute | solution.py:390
  156.6 19.2 %copy-start.27 = (bf16[1024,256]{1,0:T(8,128)(2,1)S(1)}, bf16[1024,256]{1,0:T(8,128)(2,1)}, u32[]{:S(2)}) copy-start(bf16[1024,256]{1,0:T(8,128)(2,1)} %copy-done.26) | copy-start | bytes 1572868
  156.6 19.2 %copy-start.29 = (bf16[1024,256]{1,0:T(8,128)(2,1)S(1)}, bf16[1024,256]{1,0:T(8,128)(2,1)}, u32[]{:S(2)}) copy-start(bf16[1024,256]{1,0:T(8,128)(2,1)} %copy-done.28) | copy-start | bytes 1572868
  156.6 19.2 %copy-start.31 = (bf16[1024,256]{1,0:T(8,128)(2,1)S(1)}, bf16[1024,256]{1,0:T(8,128)(2,1)}, u32[]{:S(2)}) copy-start(bf16[1024,256]{1,0:T(8,128)(2,1)} %copy-done.30) | copy-start | bytes 1572868
  156.6 19.2 %copy-start.33 = (bf16[1024,256]{1,0:T(8,128)(2,1)S(1)}, bf16[1024,256]{1,0:T(8,128)(2,1)}, u32[]{:S(2)}) copy-start(bf16[1024,256]{1,0:T(8,128)(2,1)} %copy-done.32) | copy-start | bytes 1572868
  156.6 12.8 %collective-permute-start.26 = (bf16[512,256]{1,0:T(8,128)(2,1)S(1)}, bf16[512,256]{1,0:T(8,128)(2,1)S(1)}, u32[]{:S(2)}, u32[]{:S(2)}) collective-permute-start(bf16[512,256]{1,0:T(8,128)(2,1)S(1)} %get-tuple-element.51), channel_id=1, source_target_pairs={{0,8},{4,12},{8,0},{12,4},{16,24},{20,28},{24,16},{28,20},{1,9},{5... | collective-permute-start | bytes 786440 | tf_op jit(solution)/shard_map/ppermute | solution.py:390
  165.6 6.8 %collective-permute-start.28 = (bf16[512,256]{1,0:T(8,128)(2,1)S(1)}, bf16[512,256]{1,0:T(8,128)(2,1)S(1)}, u32[]{:S(2)}, u32[]{:S(2)}) collective-permute-start(bf16[512,256]{1,0:T(8,128)(2,1)S(1)} %add_convert_fusion.5), channel_id=1, source_target_pairs={{0,16},{4,20},{8,24},{12,28},{16,0},{20,4},{24,8},{28,12},{1,17},{... | collective-permute-start | bytes 786440 | tf_op jit(solution)/shard_map/ppermute | solution.py:390
  174.6 8.5 %collective-permute-start.29 = (bf16[512,256]{1,0:T(8,128)(2,1)}, bf16[512,256]{1,0:T(8,128)(2,1)}, u32[]{:S(2)}, u32[]{:S(2)}) collective-permute-start(bf16[512,256]{1,0:T(8,128)(2,1)} %get-tuple-element.50), channel_id=1, source_target_pairs={{0,16},{4,20},{8,24},{12,28},{16,0},{20,4},{24,8},{28,12},{1,17},{... | collective-permute-start | bytes 786440 | tf_op jit(solution)/shard_map/ppermute | solution.py:390
  179.2 133.2 %copy-start.36 = (s32[32,1]{0,1:T(1,128)S(1)}, s32[32,1]{0,1:T(1,128)}, u32[]{:S(2)}) copy-start(s32[32,1]{0,1:T(1,128)} %param.13) | copy-start | bytes 388
  179.2 133.2 %copy-start.38 = (s32[128]{0:T(128)S(1)}, s32[128]{0:T(128)}, u32[]{:S(2)}) copy-start(s32[128]{0:T(128)} %copy-done.37) | copy-start | bytes 1540
  179.2 150.5 %collective-permute-start.31 = (bf16[512,256]{1,0:T(8,128)(2,1)}, bf16[512,256]{1,0:T(8,128)(2,1)}, u32[]{:S(2)}, u32[]{:S(2)}) collective-permute-start(bf16[512,256]{1,0:T(8,128)(2,1)} %get-tuple-element.49), channel_id=1, source_target_pairs={{0,16},{4,20},{8,24},{12,28},{16,0},{20,4},{24,8},{28,12},{1,17},{... | collective-permute-start | bytes 786440 | tf_op jit(solution)/shard_map/ppermute | solution.py:390
  185.0 144.8 %collective-permute-start.30 = (bf16[512,256]{1,0:T(8,128)(2,1)}, bf16[512,256]{1,0:T(8,128)(2,1)}, u32[]{:S(2)}, u32[]{:S(2)}) collective-permute-start(bf16[512,256]{1,0:T(8,128)(2,1)} %add_convert_fusion.3), channel_id=1, source_target_pairs={{0,8},{4,12},{8,0},{12,4},{16,24},{20,28},{24,16},{28,20},{1,9},{5... | collective-permute-start | bytes 786440 | tf_op jit(solution)/shard_map/ppermute | solution.py:390
  314.3 1.0 copy-start.8
  315.4 1.0 copy-start.10
  316.4 1.0 copy-start.12
  317.5 1.0 copy-start.14
  321.6 9.5 %copy-start.43 = (f32[512,256]{1,0:T(8,128)S(1)}, f32[512,256]{1,0:T(8,128)}, u32[]{:S(2)}) copy-start(f32[512,256]{1,0:T(8,128)} %get-tuple-element.48) | copy-start | bytes 1572868
  329.8 1.5 copy-start.23
  (13 other events, 11.6 us)
Sparse Core Ops, SparseCore 0:
  179.3 128.2 all-reduce.1

commit v2 on v1

v2 whole, which is shorter than its diff:
```python
import functools

import jax
import jax.numpy as jnp
from jax import lax
from jax.experimental import pallas as pl
from jax.experimental.pallas import tpu as pltpu
from jax.sharding import PartitionSpec as P

F32 = jnp.float32
BF16 = jnp.bfloat16
ANY = pl.BlockSpec(memory_space=pl.ANY)
SMEM = pl.BlockSpec(memory_space=pltpu.SMEM)
VMEM = pl.BlockSpec(memory_space=pltpu.VMEM)
MIB = 1 << 20
TN = (((0,), (0,)), ((), ()))
NT = (((1,), (1,)), ((), ()))
PARAMS = pltpu.CompilerParams(vmem_limit_bytes=60 * MIB)


def mm(a, b, dims=(((1,), (0,)), ((), ()))):
    return lax.dot_general(a, b, dims, preferred_element_type=F32)


def block_at(index, block):
    return pl.ds(pl.multiple_of(index * block, block), block)


def load_pieces(pieces, dst, sem, first):
    copies = []
    offset = 0
    for index, piece in enumerate(pieces):
        copy = pltpu.make_async_copy(
            piece, dst.at[pl.ds(offset, piece.shape[0])], sem.at[first + index]
        )
        copy.start()
        copies.append(copy)
        offset += piece.shape[0]
    return copies


def masked_tile(tiles, row, slot, count):
    tile = tiles[row, slot]
    return jnp.where(slot < count, tile, jnp.zeros_like(tile))


def forward_kernel(picks, n_pieces, cols, counts, order, *refs):
    pieces, tiles = refs[:n_pieces], refs[n_pieces]
    outs = refs[n_pieces + 1 : n_pieces + 1 + len(picks)]
    nodes_v, tiles_v, sem, tile_sem = refs[n_pieces + 1 + len(picks) :]
    rows, width = outs[0].shape
    slots, block = tiles.shape[1], tiles.shape[2]
    blocks = rows // block
    copies = load_pieces(pieces, nodes_v, sem, 0)
    tile_copies = []
    for index, pick in enumerate(picks):
        copy = pltpu.make_async_copy(
            tiles.at[pl.ds(order[pick] * blocks, blocks)],
            tiles_v.at[pl.ds(index * blocks, blocks)],
            tile_sem.at[index],
        )
        copy.start()
        tile_copies.append(copy)
    for copy in copies:
        copy.wait()
    for index, pick in enumerate(picks):
        tile_copies[index].wait()
        first = order[pick] * blocks
        out = outs[index]

        def step(i, carry, first=first, out=out, index=index):
            row = first + i
            count = counts[row]
            parts = []
            for pair in range(slots // 2):
                both = (2 * pair, 2 * pair + 1)
                tile = jnp.concatenate(
                    [masked_tile(tiles_v, index * blocks + i, slot, count) for slot in both], axis=1
                )
                node = jnp.concatenate(
                    [nodes_v[block_at(cols[row * slots + slot], block)] for slot in both], axis=0
                )
                parts.append(mm(tile, node))
            value = parts[0]
            for part in parts[1:]:
                value = value + part
            out[block_at(i, block)] = value.astype(BF16)
            return carry

        lax.fori_loop(0, blocks, step, 0, unroll=4)


def forward_call(cols, counts, order, pieces, tiles, picks, rows, after=()):
    width = pieces[0].shape[1]
    gathered = sum(piece.shape[0] for piece in pieces)
    slots, block = tiles.shape[1], tiles.shape[2]
    blocks = rows // block
    count = len(picks) * blocks * slots
    return pl.pallas_call(
        functools.partial(forward_kernel, picks, len(pieces)),
        out_shape=[jax.ShapeDtypeStruct((rows, width), BF16) for _ in picks],
        in_specs=[SMEM, SMEM, SMEM] + [ANY] * (len(pieces) + 1),
        out_specs=[VMEM] * len(picks),
        scratch_shapes=[
            pltpu.VMEM((gathered, width), BF16),
            pltpu.VMEM((len(picks) * blocks,) + tiles.shape[1:], BF16),
            pltpu.SemaphoreType.DMA((len(pieces),)),
            pltpu.SemaphoreType.DMA((len(picks),)),
        ],
        compiler_params=PARAMS,
        cost_estimate=pl.CostEstimate(
            flops=count * 2 * block * block * width,
            bytes_accessed=2 * (gathered + len(picks) * rows) * width + 2 * count * block * block,
            transcendentals=0,
        ),
        name="partial_messages",
    )(cols, counts, order, *pieces, tiles)


def mlp_kernel(kinds, middle, nodes, cot, *refs):
    n_parts = sum(len(chunk) for chunk in kinds)
    parts = refs[:n_parts]
    w_in, bias, w_out, gain, shift, updated, gpre_o, act_o, gproj_o, msg_o, vec = refs[
        n_parts : n_parts + 11
    ]
    gmsgs = refs[n_parts + 11 :]
    width = nodes.shape[1]
    inner = middle[0] > 0
    messages = []
    place = 0
    for chunk in kinds:
        total = None
        for kind in chunk:
            term = parts[place][...].astype(F32)
            place += 1
            if kind == "inner":
                term = jnp.where(inner, term, 0.0)
            total = term if total is None else total + term
        messages.append(total.astype(BF16))
    message = jnp.concatenate(messages, axis=1) if len(messages) > 1 else messages[0]
    node = nodes[...]
    pre = mm(node, w_in[:width]) + mm(message, w_in[width:]) + bias[...]
    sig = jax.nn.sigmoid(pre)
    act = (pre * sig).astype(BF16)
    proj = mm(act, w_out[...])
    mean = jnp.mean(proj, axis=-1, keepdims=True)
    var = jnp.mean((proj - mean) ** 2, axis=-1, keepdims=True)
    rstd = 1.0 / jnp.sqrt(var + 1e-05)
    normed = (proj - mean) * rstd
    updated[...] = (node.astype(F32) + normed * gain[...] + shift[...]).astype(BF16)
    grad_out = cot[...].astype(F32)
    gscaled = grad_out * gain[...]
    gproj = (
        (
            gscaled
            - jnp.mean(gscaled, axis=-1, keepdims=True)
            - normed * jnp.mean(gscaled * normed, axis=-1, keepdims=True)
        )
        * rstd
    ).astype(BF16)
    gact = mm(gproj, w_out[...], NT)
    gpre = gact * sig * (1.0 + pre * (1.0 - sig))
    gpre_b = gpre.astype(BF16)
    gmsg = mm(gpre_b, w_in[width:], NT).astype(BF16)
    part = width // len(gmsgs)
    for index, out in enumerate(gmsgs):
        out[...] = gmsg[:, index * part : (index + 1) * part]
    gpre_o[...] = gpre_b
    act_o[...] = act
    gproj_o[...] = gproj
    msg_o[...] = message

    @pl.when(pl.program_id(0) == 0)
    def _():
        vec[...] = jnp.zeros_like(vec)

    vec[0:1] += jnp.sum(gpre, axis=0, keepdims=True)
    vec[1:2] += jnp.sum(grad_out * normed, axis=0, keepdims=True)
    vec[2:3] += jnp.sum(grad_out, axis=0, keepdims=True)


def mlp_call(middle, nodes, cot, parts, kinds, w_in, bias, w_out, gain, shift):
    rows, width = nodes.shape
    step = min(rows, 256)

    def blocked(array):
        return pl.BlockSpec((step, array.shape[1]), lambda i: (i, 0))

    def whole(array):
        return pl.BlockSpec(array.shape, lambda i: (0, 0))

    flat = [term for chunk in parts for term in chunk]
    row_like = jax.ShapeDtypeStruct((rows, width), BF16)
    chunk_like = jax.ShapeDtypeStruct((rows, width // len(parts)), BF16)
    outs = [row_like] * 5 + [jax.ShapeDtypeStruct((8, width), F32)] + [chunk_like] * len(parts)
    weights = (w_in, bias, w_out, gain, shift)
    result = pl.pallas_call(
        functools.partial(mlp_kernel, kinds),
        grid=(rows // step,),
        out_shape=outs,
        in_specs=[SMEM] + [blocked(a) for a in (nodes, cot, *flat)] + [whole(a) for a in weights],
        out_specs=[blocked(a) for a in outs[:5]] + [whole(outs[5])] + [blocked(a) for a in outs[6:]],
        compiler_params=PARAMS,
        cost_estimate=pl.CostEstimate(
            flops=2 * rows * width * width * 5, bytes_accessed=2 * rows * width * 11, transcendentals=rows * width
        ),
        name="mlp",
    )(middle, nodes, cot, *flat, *weights)
    return result[:6], result[6:]


def weight_kernel(factor, nodes, msg, act, gpre, gproj, cot, w_in, vec, grads, direct):
    width = nodes.shape[1]

    @pl.when(pl.program_id(0) == 0)
    def _():
        grads[: 3 * width] = jnp.zeros((3 * width, width), F32)
        grads[3 * width :] = vec[...] * factor

    gpre_b = gpre[...]
    grads[:width] += mm(nodes[...], gpre_b, TN) * factor
    grads[width : 2 * width] += mm(msg[...], gpre_b, TN) * factor
    grads[2 * width : 3 * width] += mm(act[...], gproj[...], TN) * factor
    direct[...] = cot[...].astype(F32) + mm(gpre_b, w_in[:width], NT)


def weight_call(factor, nodes, msg, act, gpre, gproj, cot, w_in, vec):
    rows, width = nodes.shape
    step = min(rows, 256)
    blocked = pl.BlockSpec((step, width), lambda i: (i, 0))

    def whole(shape):
        return pl.BlockSpec(shape, lambda i: (0, 0))

    grads = (3 * width + 8, width)
    return pl.pallas_call(
        functools.partial(weight_kernel, factor),
        grid=(rows // step,),
        out_shape=[jax.ShapeDtypeStruct(grads, F32), jax.ShapeDtypeStruct((rows, width), F32)],
        in_specs=[blocked] * 6 + [whole(w_in.shape), whole(vec.shape)],
        out_specs=[whole(grads), blocked],
        compiler_params=PARAMS,
        cost_estimate=pl.CostEstimate(
            flops=2 * rows * width * width * 4, bytes_accessed=2 * rows * width * 10, transcendentals=0
        ),
        name="weight_grads",
    )(nodes, msg, act, gpre, gproj, cot, w_in, vec)


def grad_jobs(rows, refs, dst, sem, order, middle):
    if len(refs) == 1:
        return [(None, pltpu.make_async_copy(refs[0], dst, sem.at[0]))]
    inner = middle[0] > 0
    outer = middle[0] == 0
    plan = ((3, None), (2, None), (1, inner), (1, outer), (0, inner), (0, outer))
    return [
        (
            condition,
            pltpu.make_async_copy(refs[index], dst.at[block_at(order[group], rows)], sem.at[index]),
        )
        for index, (group, condition) in enumerate(plan)
    ]


def run_jobs(jobs, verb):
    for condition, copy in jobs:
        if condition is None:
            getattr(copy, verb)()
        else:
            pl.when(condition)(getattr(copy, verb))


def back_kernel(rows, n_grads, n_after, out_pieces, cols, counts, order, middle, *refs):
    grads, tiles = refs[:n_grads], refs[n_grads]
    refs = refs[n_grads + 1 + n_after :]
    outs = refs[: len(out_pieces)]
    grad_v, tiles_v, acc, sem, tile_sem = refs[len(out_pieces) :]
    row_blocks, slots, block = tiles.shape[:3]
    jobs = grad_jobs(rows, grads, grad_v, sem, order, middle)
    run_jobs(jobs, "start")
    tile_copy = pltpu.make_async_copy(tiles, tiles_v, tile_sem.at[0])
    tile_copy.start()
    acc[...] = jnp.zeros_like(acc)
    run_jobs(jobs, "wait")
    tile_copy.wait()

    def step(row, carry):
        count = counts[row]
        grad = grad_v[block_at(row, block)]
        for slot in range(slots):
            part = mm(masked_tile(tiles_v, row, slot, count), grad, TN)
            acc[block_at(cols[row * slots + slot], block)] += part
        return carry

    lax.fori_loop(0, row_blocks, step, 0, unroll=2)
    piece = acc.shape[0] // sum(len(members) for members in out_pieces)
    for out, members in zip(outs, out_pieces):
        for index, member in enumerate(members):
            out[pl.ds(index * piece, piece)] = acc[pl.ds(member * piece, piece)].astype(BF16)


def back_call(cols, counts, order, middle, grads, tiles, total, gathered, out_pieces, after=()):
    rows, width = grads[0].shape
    rows = total if len(grads) == 1 else rows
    row_blocks, slots, block = tiles.shape[:3]
    piece = gathered // sum(len(members) for members in out_pieces)
    return pl.pallas_call(
        functools.partial(back_kernel, rows, len(grads), len(after), out_pieces),
        out_shape=[jax.ShapeDtypeStruct((len(m) * piece, width), BF16) for m in out_pieces],
        in_specs=[SMEM] * 4 + [ANY] * (len(grads) + 1 + len(after)),
        out_specs=[VMEM] * len(out_pieces),
        scratch_shapes=[
            pltpu.VMEM((total, width), BF16),
            pltpu.VMEM(tiles.shape, BF16),
            pltpu.VMEM((gathered, width), F32),
            pltpu.SemaphoreType.DMA((len(grads),)),
            pltpu.SemaphoreType.DMA((1,)),
        ],
        compiler_params=PARAMS,
        cost_estimate=pl.CostEstimate(
            flops=row_blocks * slots * 2 * block * block * width,
            bytes_accessed=2 * width * (gathered + total) + 2 * tiles.size,
            transcendentals=0,
        ),
        name="back_terms",
    )(cols, counts, order, middle, *grads, tiles, *after)


def tile_grad_kernel(rows, n_grads, n_pieces, n_chunks, n_after, step_rows, cols, counts, order, middle, *refs):
    grads = refs[: n_grads * n_chunks]
    refs = refs[n_grads * n_chunks :]
    pieces = refs[: n_pieces * n_chunks]
    out, grad_v, nodes_v, sem, piece_sem = refs[n_pieces * n_chunks + n_after :]
    slots, block = out.shape[1], out.shape[2]
    width = nodes_v.shape[1]
    part = width // n_chunks
    scale = float(width) ** -0.5

    @pl.when(pl.program_id(0) == 0)
    def _():
        jobs, copies = [], []
        for chunk in range(n_chunks):
            columns = pl.ds(chunk * part, part)
            jobs += grad_jobs(
                rows,
                grads[chunk * n_grads : (chunk + 1) * n_grads],
                grad_v.at[:, columns],
                sem.at[chunk],
                order,
                middle,
            )
            copies += load_pieces(
                pieces[chunk * n_pieces : (chunk + 1) * n_pieces],
                nodes_v.at[:, columns],
                piece_sem.at[chunk],
                0,
            )
        run_jobs(jobs, "start")
        run_jobs(jobs, "wait")
        for copy in copies:
            copy.wait()

    def step(i, carry):
        row = pl.program_id(0) * step_rows + i
        count = counts[row]
        grad = grad_v[block_at(row, block)]
        for slot in range(slots):
            node = nodes_v[block_at(cols[row * slots + slot], block)]
            value = mm(grad, node, NT) * scale
            out[i, slot] = jnp.where(slot < count, value, 0.0).astype(BF16)
        return carry

    lax.fori_loop(0, step_rows, step, 0, unroll=2)


def tile_grad_call(cols, counts, order, middle, grads, pieces, shape, total, after=()):
    row_blocks, slots, block = shape[:3]
    chunks = len(grads)
    rows, width = grads[0][0].shape
    rows = total if len(grads[0]) == 1 else rows
    width = width * chunks
    gathered = sum(piece.shape[0] for piece in pieces[0])
    step_rows = min(row_blocks, 8)
    flat = [a for chunk in grads for a in chunk] + [a for chunk in pieces for a in chunk]
    return pl.pallas_call(
        functools.partial(
            tile_grad_kernel, rows, len(grads[0]), len(pieces[0]), chunks, len(after), step_rows
        ),
        grid=(row_blocks // step_rows,),
        out_shape=jax.ShapeDtypeStruct(shape, BF16),
        in_specs=[SMEM] * 4 + [ANY] * (len(flat) + len(after)),
        out_specs=pl.BlockSpec((step_rows, slots, block, block), lambda i: (i, 0, 0, 0)),
        scratch_shapes=[
            pltpu.VMEM((total, width), BF16),
            pltpu.VMEM((gathered, width), BF16),
            pltpu.SemaphoreType.DMA((chunks, len(grads[0]))),
            pltpu.SemaphoreType.DMA((chunks, len(pieces[0]))),
        ],
        compiler_params=PARAMS,
        cost_estimate=pl.CostEstimate(
            flops=row_blocks * slots * 2 * block * block * width,
            bytes_accessed=2 * width * (gathered + total) + 2 * row_blocks * slots * block * block,
            transcendentals=0,
        ),
        name="tile_grads",
    )(cols, counts, order, middle, *flat, *after)


def add(*terms):
    value = terms[0].astype(F32)
    for term in terms[1:]:
        value = value + term.astype(F32)
    return value.astype(BF16)


def swap(value, bit):
    return lax.ppermute(value, "row", [(i, i ^ bit) for i in range(8)])


def outer_swap(value):
    return lax.ppermute(value, "col", [(0, 1), (1, 0), (2, 3), (3, 2)])


def inner_swap(value):
    return lax.ppermute(value, "col", [(0, 0), (1, 2), (2, 1), (3, 3)])


def gather_square(nodes, by_x):
    x_side, y_side = swap(nodes, 2), swap(nodes, 4)
    diag = swap(y_side, 2) if by_x else swap(x_side, 4)
    pieces = []
    for piece in (nodes, x_side, y_side, diag):
        pieces += [piece, swap(piece, 1)]
    return pieces


def reduce_square(even, odd, rows, by_x):
    other = swap(odd, 1)

    def both(place):
        where = slice(place * rows, (place + 1) * rows)
        return even[where], other[where]

    if by_x:
        diag = swap(add(*both(3)), 2)
        x_side = swap(add(*both(1)), 2)
        y_side = swap(add(*both(2), diag), 4)
    else:
        diag = swap(add(*both(3)), 4)
        y_side = swap(add(*both(2)), 4)
        x_side = swap(add(*both(1), diag), 2)
    return (*both(0), x_side, y_side)


def reduce_line(far, near, pair, own, inner):
    far_in = outer_swap(far)
    near_in = outer_swap(near)
    far_sum = inner_swap(add(far, far_in))
    near_sum = inner_swap(add(near, near_in))
    pair_in = outer_swap(add(pair, jnp.where(inner, far_sum, jnp.zeros_like(far_sum))))
    return own, pair_in, near_sum


def gather_line(own):
    pair = outer_swap(own)
    near_inner = inner_swap(own)
    far_inner = inner_swap(pair)
    near_outer = outer_swap(near_inner)
    far_outer = outer_swap(far_inner)
    return [own, pair, near_inner, near_outer, far_inner, far_outer]


def body(n_row, n_col, nodes, tiles, tile_col, tile_count, w_in, bias_in, w_out, ln_gain, ln_shift, cotangent):
    rows, width = nodes.shape
    row_blocks, _, slots, block = tiles.shape[:4]
    tile_local = tiles.reshape(row_blocks, slots, block, block)
    cols = tile_col.reshape(row_blocks * slots)
    counts = tile_count.reshape(row_blocks)
    blocks = rows // block
    gathered, total = n_row * rows, n_col * rows
    square_line = n_row == 8 and n_col == 4
    if square_line:
        mine = lax.axis_index("row").astype(jnp.int32)
        cols = ((cols // blocks) ^ mine) * blocks + cols % blocks
        level = lax.axis_index("col").astype(jnp.int32)
        low = level < 2
        order = jnp.stack([jnp.where(low, 3, 0), jnp.where(low, 2, 1), level ^ 1, level]).astype(jnp.int32)
        inner = (level == 1) | (level == 2)
        middle = inner.astype(jnp.int32).reshape(1)
        chunks = 2
        part = width // chunks
        pieces, parts, kinds = [], [], []
        for chunk in range(chunks):
            pieces.append(gather_square(nodes[:, chunk * part : (chunk + 1) * part], chunk == 0))
            far, near = forward_call(cols, counts, order, pieces[-1], tile_local, (0, 1), rows)
            pair, own = forward_call(cols, counts, order, pieces[-1], tile_local, (2, 3), rows)
            parts.append(reduce_line(far, near, pair, own, inner))
            kinds.append(("all", "all", "inner"))
    else:
        order = jnp.arange(n_col, dtype=jnp.int32)
        middle = jnp.zeros((1,), jnp.int32)
        pieces = [[lax.all_gather(nodes, "row", axis=0, tiled=True)]]
        partial = forward_call(
            cols, counts, order, pieces[0], tile_local, tuple(range(n_col)), rows
        )
        partial = jnp.concatenate(partial, axis=0)
        parts = [[lax.psum_scatter(partial, "col", scatter_dimension=0, tiled=True)]]
        kinds = [("all",)]
    vectors = [v.reshape(1, width) for v in (bias_in, ln_gain, ln_shift)]
    (updated, gpre_b, act, gproj, message, vec), gmsgs = mlp_call(
        middle, nodes, cotangent, parts, kinds, w_in, vectors[0], w_out, vectors[1], vectors[2]
    )
    if square_line:
        grads = [gather_line(gmsg) for gmsg in gmsgs]
    else:
        grads = [[lax.all_gather(gmsgs[0], "col", axis=0, tiled=True)]]
    factor = float(rows * n_row * n_col) ** -0.5
    weight_terms, direct = weight_call(
        factor, nodes, message, act, gpre_b, gproj, cotangent, w_in, vec
    )
    weight_sums = lax.psum(lax.psum(weight_terms, "row"), "col")
    if square_line:
        sums = []
        for chunk in range(chunks):
            odd, even = back_call(
                cols, counts, order, middle, grads[chunk], tile_local, total, gathered,
                ((1, 3, 5, 7), (0, 2, 4, 6)),
            )
            terms = reduce_square(even, odd, rows, chunk == 0)
            sums.append(sum(term.astype(F32) for term in terms))
        after = (odd,)
        back = jnp.concatenate(sums, axis=1)
    else:
        (terms,) = back_call(
            cols, counts, order, middle, grads[0], tile_local, total, gathered, (tuple(range(n_row)),)
        )
        back = lax.psum_scatter(terms, "row", scatter_dimension=0, tiled=True).astype(F32)
        after = (terms,)
    grad_nodes = (direct + back).astype(BF16)
    grad_tiles = tile_grad_call(
        cols, counts, order, middle, grads, pieces, tile_local.shape, total, after
    ).reshape(tiles.shape)
    return (
        updated,
        grad_nodes,
        grad_tiles,
        weight_sums[: 2 * width],
        weight_sums[2 * width : 3 * width],
        weight_sums[3 * width : 3 * width + 3],
    )


def solution(mesh):
    placed = (
        P(("row", "col"), None),
        P("row", "col", None, None, None),
        P("row", "col", None),
        P("row", "col"),
        P(),
        P(),
        P(),
        P(),
        P(),
        P(("row", "col"), None),
    )
    return jax.shard_map(
        functools.partial(body, mesh.shape["row"], mesh.shape["col"]),
        mesh=mesh,
        in_specs=placed,
        out_specs=(
            P(("row", "col"), None),
            P(("row", "col"), None),
            P("row", "col", None, None, None),
            P(),
            P(),
            P(),
        ),
        check_vma=False,
    )
```

time: 341 us -> 275 us (0.81)
  waiting for transfers between devices: 207 us -> 121 us
  Pallas kernels: 31.9 us -> 57.9 us
  local copies, waits for them, and re-layouts: 25.9 us -> 9.22 us
  starting transfers between devices: 50.1 us -> 62.3 us
    ppermute x32 -> x42, waiting for transfers between devices: 85.3 us -> 38.7 us  [the longest x22 22 us: swap(): return lax.ppermute(value, 'row', [(i, i ^ bit) for i in range(8)])]
    psum x1 -> x2, waiting for transfers between devices: 122 us -> 81.9 us  [body(): weight_sums = lax.psum(lax.psum(weight_terms, 'row'), 'col')]
    pallas_call x5 -> x8, Pallas kernels: 30.5 us -> 52.9 us  [the longest x2 18.3 us: back_call(): pl.pallas_call(functools.partial(back_kernel, rows, len(grads), len(after...]
    unnamed x89 -> x67, local copies, waits for them, and re-layouts: 19.9 us -> 3.14 us
    ppermute x32 -> x42, starting transfers between devices: 50.1 us -> 62.3 us  [the longest x12 38.4 us: outer_swap(): return lax.ppermute(value, 'col', [(0, 1), (1, 0), (2, 3), (3, 2)])]
    pallas_call x1, Pallas kernels: 1.47 us -> 5.07 us  [weight_call(): pl.pallas_call(functools.partial(weight_kernel, factor), grid=(rows // st...]
  transfers between devices with their start and end apart: 33 -> 44, of which waited for: 22 -> 15; matrix products, arithmetic and copies ran while one was open for 3% -> 5% of each run, Pallas kernels for 4% -> 19%
where the time goes in v2:
time: 275 us
  waiting for transfers between devices  121 us (44%)
  starting transfers between devices  62.3 us (23%)
  Pallas kernels  57.9 us (21%)
  between operations  14.6 us (5%)
  other arithmetic  9.91 us (4%)
  local copies, waits for them, and re-layouts  9.22 us (3%)
    psum x2, waiting for transfers between devices, body(): weight_sums = lax.psum(lax.psum(weight_terms, 'row'), 'col')  81.9 us
    ppermute x12, starting transfers between devices, outer_swap(): return lax.ppermute(value, 'col', [(0, 1), (1, 0), (2, 3), (3, 2)])  38.4 us
    ppermute x22, waiting for transfers between devices, swap(): return lax.ppermute(value, 'row', [(i, i ^ bit) for i in range(8)])  22 us
    pallas_call x2, Pallas kernels, back_call(): pl.pallas_call(functools.partial(back_kernel, rows, len(grads), len(after...  18.3 us
    pallas_call x4, Pallas kernels, forward_call(): pl.pallas_call(functools.partial(forward_kernel, picks, len(pieces)), out...  18.3 us
    ppermute x12, waiting for transfers between devices, outer_swap(): return lax.ppermute(value, 'col', [(0, 1), (1, 0), (2, 3), (3, 2)])  16.7 us
    ppermute x22, starting transfers between devices, swap(): return lax.ppermute(value, 'row', [(i, i ^ bit) for i in range(8)])  16.6 us
    pallas_call x1, Pallas kernels, tile_grad_call(): pl.pallas_call(functools.partial(tile_grad_kernel, rows, len(grads[0]), l...  9.69 us
  transfers between devices with their start and end apart: 44, of which 15 were waited for; matrix products, arithmetic and copies ran while one was open for 5% of the time, Pallas kernels for 19%

profile of v2, /device:TPU:0, one launch (start us, length us, event | category | flops | bytes accessed | tf_op | source)
XLA Modules:
  0.0 274.6 jit_solution(14067603520552875050)
XLA Ops:
  7.2 1.1 fusion.2
  8.3 3.0 %collective-permute-start.3 = (bf16[1024,128]{1,0:T(8,128)(2,1)S(1)}, bf16[1024,128]{1,0:T(8,128)(2,1)S(1)}, u32[]{:S(2)}, u32[]{:S(2)}) collective-permute-start(bf16[1024,128]{1,0:T(8,128)(2,1)S(1)} %get-tuple-element.67.refs_0_.refs_12_), channel_id=1, source_target_pairs={{0,16},{4,20},{8,24},{12,28},{16,0},{20,4},{24,8},{28,12},{1,17},{... | collective-permute-start | bytes 786440 | tf_op jit(solution)/shard_map/ppermute | solution.py:417
  11.3 1.5 collective-permute-start.1
  13.4 4.3 %collective-permute-done.3.refs_4_.refs_16_ = bf16[1024,128]{1,0:T(8,128)(2,1)S(1)} collective-permute-done((bf16[1024,128]{1,0:T(8,128)(2,1)S(1)}, bf16[1024,128]{1,0:T(8,128)(2,1)S(1)}, u32[]{:S(2)}, u32[]{:S(2)}) %collective-permute-start.3) | collective-permute-done | bytes 262176 | tf_op jit(solution)/shard_map/ppermute | solution.py:417
  17.6 1.7 collective-permute-start.5
  19.4 1.5 collective-permute-start.15
  21.4 4.8 %collective-permute-done.13.refs_2_.refs_22_ = bf16[1024,128]{1,0:T(8,128)(2,1)S(1)} collective-permute-done((bf16[1024,128]{1,0:T(8,128)(2,1)S(1)}, bf16[1024,128]{1,0:T(8,128)(2,1)S(1)}, u32[]{:S(2)}, u32[]{:S(2)}) %collective-permute-start.13) | collective-permute-done | bytes 262176 | tf_op jit(solution)/shard_map/ppermute | solution.py:417
  26.2 0.8 copy.18
  27.1 3.2 %collective-permute-done.5.refs_6_.refs_18_ = bf16[1024,128]{1,0:T(8,128)(2,1)S(1)} collective-permute-done((bf16[1024,128]{1,0:T(8,128)(2,1)S(1)}, bf16[1024,128]{1,0:T(8,128)(2,1)S(1)}, u32[]{:S(2)}, u32[]{:S(2)}) %collective-permute-start.5) | collective-permute-done | bytes 262176 | tf_op jit(solution)/shard_map/ppermute | solution.py:417
  30.3 0.6 fusion.1.cols
  32.6 0.7 pad_add_fusion.order
  33.3 0.7 copy-done.11
  33.9 4.5 %partial_messages.5 = (bf16[1024,128]{1,0:T(8,128)(2,1)}, bf16[1024,128]{1,0:T(8,128)(2,1)}) custom-call(s32[128]{0:T(128)} %fusion.1.cols, s32[32]{0:T(128)} %bitcast.22, s32[4]{0:T(128)} %pad_add_fusion.order, bf16[1024,128]{1,0:T(8,128)(2,1)} %copy-done.1, bf16[1024,128]{1,0:T(8,128)(2,1)} %copy-done.4, bf16[1024,128]{1,0:T(8,128)(2,1)} %copy-done.3, ...), custom_call_target="tpu_custom_call" | custom-call | flops 268435456 | bytes 4718592 | tf_op jit(solution)/shard_map/partial_messages/pallas_call | solution.py:99
  38.5 1.6 collective-permute-start.7
  40.8 4.5 %partial_messages.7 = (bf16[1024,128]{1,0:T(8,128)(2,1)}, bf16[1024,128]{1,0:T(8,128)(2,1)}) custom-call(s32[128]{0:T(128)} %fusion.1.cols, s32[32]{0:T(128)} %bitcast.23, s32[4]{0:T(128)} %pad_add_fusion.order, bf16[1024,128]{1,0:T(8,128)(2,1)} %copy-done, bf16[1024,128]{1,0:T(8,128)(2,1)} %copy-done.12, bf16[1024,128]{1,0:T(8,128)(2,1)} %copy-done.5, ...), custom_call_target="tpu_custom_call" | custom-call | flops 268435456 | bytes 4718592 | tf_op jit(solution)/shard_map/partial_messages/pallas_call | solution.py:99
  45.3 1.5 collective-permute-start.19
  47.4 4.5 %partial_messages.4 = (bf16[1024,128]{1,0:T(8,128)(2,1)}, bf16[1024,128]{1,0:T(8,128)(2,1)}) custom-call(s32[128]{0:T(128)} %fusion.1.cols, s32[32]{0:T(128)} %bitcast.24, s32[4]{0:T(128)} %pad_add_fusion.order, bf16[1024,128]{1,0:T(8,128)(2,1)} %copy-done.1, bf16[1024,128]{1,0:T(8,128)(2,1)} %copy-done.4, bf16[1024,128]{1,0:T(8,128)(2,1)} %copy-done.3, ...), custom_call_target="tpu_custom_call" | custom-call | flops 268435456 | bytes 4718592 | tf_op jit(solution)/shard_map/partial_messages/pallas_call | solution.py:99
  52.0 4.7 %partial_messages.6 = (bf16[1024,128]{1,0:T(8,128)(2,1)}, bf16[1024,128]{1,0:T(8,128)(2,1)}) custom-call(s32[128]{0:T(128)} %fusion.1.cols, s32[32]{0:T(128)} %bitcast.25, s32[4]{0:T(128)} %pad_add_fusion.order, bf16[1024,128]{1,0:T(8,128)(2,1)} %copy-done, bf16[1024,128]{1,0:T(8,128)(2,1)} %copy-done.12, bf16[1024,128]{1,0:T(8,128)(2,1)} %copy-done.5, ...), custom_call_target="tpu_custom_call" | custom-call | flops 268435456 | bytes 4718592 | tf_op jit(solution)/shard_map/partial_messages/pallas_call | solution.py:99
  56.8 0.7 collective-permute-start.8
  57.6 0.7 collective-permute-start.11
  58.3 0.8 collective-permute-done.19
  59.2 0.7 collective-permute-start.20
  59.9 4.4 %collective-permute-done.22 = bf16[1024,128]{1,0:T(8,128)(2,1)S(1)} collective-permute-done((bf16[1024,128]{1,0:T(8,128)(2,1)}, bf16[1024,128]{1,0:T(8,128)(2,1)S(1)}, u32[]{:S(2)}, u32[]{:S(2)}) %collective-permute-start.22) | collective-permute-done | bytes 262176 | tf_op jit(solution)/shard_map/ppermute | solution.py:421
  64.3 0.7 collective-permute-start.23
  65.1 5.3 %collective-permute-start.9 = (bf16[1024,128]{1,0:T(8,128)(2,1)S(1)}, bf16[1024,128]{1,0:T(8,128)(2,1)S(1)}, u32[]{:S(2)}, u32[]{:S(2)}) collective-permute-start(bf16[1024,128]{1,0:T(8,128)(2,1)S(1)} %add_convert_fusion.10), channel_id=1, source_target_pairs={{0,1},{1,0},{2,3},{3,2},{4,5},{5,4},{6,7},{7,6},{8,9},{9,8},{10,11... | collective-permute-start | bytes 786440 | tf_op jit(solution)/shard_map/ppermute | solution.py:421
  70.4 1.0 add_convert_fusion.7
  71.5 10.2 %collective-permute-start.21 = (bf16[1024,128]{1,0:T(8,128)(2,1)S(1)}, bf16[1024,128]{1,0:T(8,128)(2,1)S(1)}, u32[]{:S(2)}, u32[]{:S(2)}) collective-permute-start(bf16[1024,128]{1,0:T(8,128)(2,1)S(1)} %add_convert_fusion.7), channel_id=1, source_target_pairs={{0,1},{1,0},{2,3},{3,2},{4,5},{5,4},{6,7},{7,6},{8,9},{9,8},{10,11... | collective-permute-start | bytes 786440 | tf_op jit(solution)/shard_map/ppermute | solution.py:421
  81.7 4.3 %collective-permute-done.21.refs_4_ = bf16[1024,128]{1,0:T(8,128)(2,1)S(1)} collective-permute-done((bf16[1024,128]{1,0:T(8,128)(2,1)S(1)}, bf16[1024,128]{1,0:T(8,128)(2,1)S(1)}, u32[]{:S(2)}, u32[]{:S(2)}) %collective-permute-start.21) | collective-permute-done | bytes 262176 | tf_op jit(solution)/shard_map/ppermute | solution.py:421
  86.1 0.7 copy-done.32
  86.7 6.6 %mlp.1 = (bf16[1024,256]{1,0:T(8,128)(2,1)}, bf16[1024,256]{1,0:T(8,128)(2,1)}, bf16[1024,256]{1,0:T(8,128)(2,1)}, bf16[1024,256]{1,0:T(8,128)(2,1)}, bf16[1024,...) custom-call(s32[1]{0:T(128)} %bitcast.middle, ...), custom_call_target="tpu_custom_call" | custom-call | flops 671088640 | bytes 5767168 | tf_op jit(solution)/shard_map/mlp/pallas_call | solution.py:197
  93.4 2.1 collective-permute-start.33
  95.6 1.6 collective-permute-start.34
  97.2 4.3 %collective-permute-done.33.refs_1_.refs_7_ = bf16[1024,128]{1,0:T(8,128)(2,1)S(1)} collective-permute-done((bf16[1024,128]{1,0:T(8,128)(2,1)}, bf16[1024,128]{1,0:T(8,128)(2,1)S(1)}, u32[]{:S(2)}, u32[]{:S(2)}) %collective-permute-start.33) | collective-permute-done | bytes 262176 | tf_op jit(solution)/shard_map/ppermute | solution.py:421
  101.4 0.7 collective-permute-start.36
  102.1 1.6 collective-permute-start.25
  104.2 0.7 collective-permute-start.27
  104.9 7.8 %collective-permute-start.35 = (bf16[1024,128]{1,0:T(8,128)(2,1)S(1)}, bf16[1024,128]{1,0:T(8,128)(2,1)S(1)}, u32[]{:S(2)}, u32[]{:S(2)}) collective-permute-start(bf16[1024,128]{1,0:T(8,128)(2,1)S(1)} %collective-permute-done.34.refs_2_.refs_8_), channel_id=1, source_target_pairs={{0,1},{1,0},{2,3},{3,2},{4,5},{5,4},{6,7},{7,6},{8,9},{9,8},{10,11... | collective-permute-start | bytes 786440 | tf_op jit(solution)/shard_map/ppermute | solution.py:421
  112.8 1.7 collective-permute-start.37
  114.4 4.2 %collective-permute-start.26 = (bf16[1024,128]{1,0:T(8,128)(2,1)S(1)}, bf16[1024,128]{1,0:T(8,128)(2,1)}, u32[]{:S(2)}, u32[]{:S(2)}) collective-permute-start(bf16[1024,128]{1,0:T(8,128)(2,1)S(1)} %collective-permute-done.25.refs_2_), channel_id=1, source_target_pairs={{0,1},{1,0},{2,3},{3,2},{4,5},{5,4},{6,7},{7,6},{8,9},{9,8},{10,11... | collective-permute-start | bytes 786440 | tf_op jit(solution)/shard_map/ppermute | solution.py:421
  118.7 2.8 %collective-permute-start.28 = (bf16[1024,128]{1,0:T(8,128)(2,1)S(1)}, bf16[1024,128]{1,0:T(8,128)(2,1)}, u32[]{:S(2)}, u32[]{:S(2)}) collective-permute-start(bf16[1024,128]{1,0:T(8,128)(2,1)S(1)} %collective-permute-done.27.refs_4_), channel_id=1, source_target_pairs={{0,1},{1,0},{2,3},{3,2},{4,5},{5,4},{6,7},{7,6},{8,9},{9,8},{10,11... | collective-permute-start | bytes 786440 | tf_op jit(solution)/shard_map/ppermute | solution.py:421
  121.5 2.3 collective-permute-done.37.refs_5_.refs_11_
  123.9 0.7 copy-done.23
  124.6 9.1 %back_terms.3 = (bf16[4096,128]{1,0:T(8,128)(2,1)}, bf16[4096,128]{1,0:T(8,128)(2,1)}) custom-call(s32[128]{0:T(128)} %fusion.1.cols, s32[32]{0:T(128)} %bitcast.26, s32[4]{0:T(128)} %pad_add_fusion.order, s32[1]{0:T(128)} %bitcast.middle, bf16[1024,128]{1,0:T(8,128)(2,1)} %get-tuple-element.46.refs_0_.refs_6_, bf16[1024,128]{1,0:T(8,128)(2,1)} %copy-done.16, ...), custom_call_target="tpu_custom_call" | custom-call | flops 536870912 | bytes 7340032 | tf_op jit(solution)/shard_map/back_terms/pallas_call | solution.py:307
  133.8 9.2 %back_terms.2 = (bf16[4096,128]{1,0:T(8,128)(2,1)}, bf16[4096,128]{1,0:T(8,128)(2,1)}) custom-call(s32[128]{0:T(128)} %fusion.1.cols, s32[32]{0:T(128)} %bitcast.27, s32[4]{0:T(128)} %pad_add_fusion.order, s32[1]{0:T(128)} %bitcast.middle, bf16[1024,128]{1,0:T(8,128)(2,1)} %get-tuple-element.43.refs_0_, bf16[1024,128]{1,0:T(8,128)(2,1)} %copy-done.17, ...), custom_call_target="tpu_custom_call" | custom-call | flops 536870912 | bytes 7340032 | tf_op jit(solution)/shard_map/back_terms/pallas_call | solution.py:307
  143.4 5.1 %weight_grads.1 = (f32[776,256]{1,0:T(8,128)}, f32[1024,256]{1,0:T(8,128)}) custom-call(bf16[1024,256]{1,0:T(8,128)(2,1)} %nodes.3, bf16[1024,256]{1,0:T(8,128)(2,1)} %get-tuple-element.37.msg, bf16[1024,256]{1,0:T(8,128)(2,1)} %get-tuple-element.38.act, bf16[1024,256]{1,0:T(8,128)(2,1)} %get-tuple-element.39.gpre, ...), custom_call_target="tpu_custom_call" | custom-call | flops 536870912 | bytes 5242880 | tf_op jit(solution)/shard_map/weight_grads/pallas_call | solution.py:236
  148.6 54.8 %all-reduce.3.cloned.1.call-done = f32[776,256]{1,0:T(8,128)} async-done(((f32[776,256]{1,0:T(8,128)}), f32[776,256]{1,0:T(8,128)}) %all-reduce.3.cloned.1.call-update) | async-done | bytes 794640 | tf_op jit(solution)/shard_map/psum | solution.py:521
  203.5 1.8 collective-permute-start.39
  205.2 2.0 add_convert_fusion.5
  207.6 3.9 %collective-permute-done.39 = bf16[1024,128]{1,0:T(8,128)(2,1)S(1)} collective-permute-done((bf16[1024,128]{1,0:T(8,128)(2,1)S(1)}, bf16[1024,128]{1,0:T(8,128)(2,1)S(1)}, u32[]{:S(2)}, u32[]{:S(2)}) %collective-permute-start.39) | collective-permute-done | bytes 262176 | tf_op jit(solution)/shard_map/ppermute | solution.py:417
  211.6 0.9 add_convert_fusion.1
  212.4 0.6 collective-permute-start.41
  213.6 9.7 %tile_grads.1 = bf16[32,4,128,128]{3,2,1,0:T(8,128)(2,1)} custom-call(s32[128]{0:T(128)} %fusion.1.cols, s32[32]{0:T(128)} %bitcast.28, s32[4]{0:T(128)} %pad_add_fusion.order, s32[1]{0:T(128)} %bitcast.middle, bf16[1024,128]{1,0:T(8,128)(2,1)} %get-tuple-element.43.refs_0_, bf16[1024,128]{1,0:T(8,128)(2,1)} %copy-done.17, bf16[1024,128]{1,0:T(8,128)(2,1)} %copy-done.20, ...), custom_call_target="tpu_custom_call" | custom-call | flops 1073741824 | bytes 10485760 | tf_op jit(solution)/shard_map/tile_grads/pallas_call | solution.py:385
  223.3 27.1 %all-reduce.5.cloned.1.call-done = f32[776,256]{1,0:T(8,128)} async-done(((f32[776,256]{1,0:T(8,128)}), f32[776,256]{1,0:T(8,128)}) %all-reduce.5.cloned.1.call-update) | async-done | bytes 794640 | tf_op jit(solution)/shard_map/psum | solution.py:521
  250.4 2.0 slice.92
  252.3 1.7 slice.93
  254.0 1.3 slice.94
  255.3 1.5 collective-permute-start.30
  256.8 1.1 add_convert_fusion.3
  257.9 1.5 collective-permute-start.32
  259.4 1.2 convert_add_fusion
  260.6 3.0 %collective-permute-done.30 = bf16[1024,128]{1,0:T(8,128)(2,1)S(1)} collective-permute-done((bf16[1024,128]{1,0:T(8,128)(2,1)}, bf16[1024,128]{1,0:T(8,128)(2,1)S(1)}, u32[]{:S(2)}, u32[]{:S(2)}) %collective-permute-start.30) | collective-permute-done | bytes 262176 | tf_op jit(solution)/shard_map/ppermute | solution.py:417
  263.6 2.2 collective-permute-done.32
  265.8 1.1 convert_add_fusion.1
  266.9 0.9 fusion
  (122 shorter events, 6.8 us)
Async XLA Ops:
  7.2 196.2 %all-reduce.3.cloned.1.call-start = ((), (), s32[]{:S(2)}) async-start(), calls=%async_computation | async-start | bytes 1589248 | tf_op jit(solution)/shard_map/psum | solution.py:521
  8.3 24.9 %copy-start.1 = (bf16[1024,128]{1,0:T(8,128)(2,1)}, bf16[1024,128]{1,0:T(8,128)(2,1)S(1)}, u32[]{:S(2)}) copy-start(bf16[1024,128]{1,0:T(8,128)(2,1)S(1)} %get-tuple-element.67.refs_0_.refs_12_) | copy-start | bytes 786436
  8.3 32.3 %copy-start = (bf16[1024,128]{1,0:T(8,128)(2,1)}, bf16[1024,128]{1,0:T(8,128)(2,1)S(1)}, u32[]{:S(2)}) copy-start(bf16[1024,128]{1,0:T(8,128)(2,1)S(1)} %get-tuple-element.66.refs_0_.refs_20_) | copy-start | bytes 786436
  8.3 9.3 %collective-permute-start.3 = (bf16[1024,128]{1,0:T(8,128)(2,1)S(1)}, bf16[1024,128]{1,0:T(8,128)(2,1)S(1)}, u32[]{:S(2)}, u32[]{:S(2)}) collective-permute-start(bf16[1024,128]{1,0:T(8,128)(2,1)S(1)} %get-tuple-element.67.refs_0_.refs_12_), channel_id=1, source_target_pairs={{0,16},{4,20},{8,24},{12,28},{16,0},{20,4},{24,8},{28,12},{1,17},{... | collective-permute-start | bytes 786440 | tf_op jit(solution)/shard_map/ppermute | solution.py:417
  11.3 9.5 %collective-permute-start.1 = (bf16[1024,128]{1,0:T(8,128)(2,1)S(1)}, bf16[1024,128]{1,0:T(8,128)(2,1)S(1)}, u32[]{:S(2)}, u32[]{:S(2)}) collective-permute-start(bf16[1024,128]{1,0:T(8,128)(2,1)S(1)} %get-tuple-element.67.refs_0_.refs_12_), channel_id=1, source_target_pairs={{0,8},{4,12},{8,0},{12,4},{16,24},{20,28},{24,16},{28,20},{1,9},{5... | collective-permute-start | bytes 786440 | tf_op jit(solution)/shard_map/ppermute | solution.py:417
  12.8 8.1 %collective-permute-start = (bf16[1024,128]{1,0:T(8,128)(2,1)S(1)}, bf16[1024,128]{1,0:T(8,128)(2,1)S(1)}, u32[]{:S(2)}, u32[]{:S(2)}) collective-permute-start(bf16[1024,128]{1,0:T(8,128)(2,1)S(1)} %get-tuple-element.67.refs_0_.refs_12_), channel_id=1, source_target_pairs={{0,4},{4,0},{8,12},{12,8},{16,20},{20,16},{24,28},{28,24},{1,5},{5... | collective-permute-start | bytes 786440 | tf_op jit(solution)/shard_map/ppermute | solution.py:417
  12.8 13.4 %collective-permute-start.13 = (bf16[1024,128]{1,0:T(8,128)(2,1)S(1)}, bf16[1024,128]{1,0:T(8,128)(2,1)S(1)}, u32[]{:S(2)}, u32[]{:S(2)}) collective-permute-start(bf16[1024,128]{1,0:T(8,128)(2,1)S(1)} %get-tuple-element.66.refs_0_.refs_20_), channel_id=1, source_target_pairs={{0,8},{4,12},{8,0},{12,4},{16,24},{20,28},{24,16},{28,20},{1,9},{5... | collective-permute-start | bytes 786440 | tf_op jit(solution)/shard_map/ppermute | solution.py:417
  17.6 15.6 %copy-start.2 = (bf16[1024,128]{1,0:T(8,128)(2,1)}, bf16[1024,128]{1,0:T(8,128)(2,1)S(1)}, u32[]{:S(2)}) copy-start(bf16[1024,128]{1,0:T(8,128)(2,1)S(1)} %collective-permute-done.3.refs_4_.refs_16_) | copy-start | bytes 786436
  17.6 12.7 %collective-permute-start.5 = (bf16[1024,128]{1,0:T(8,128)(2,1)S(1)}, bf16[1024,128]{1,0:T(8,128)(2,1)S(1)}, u32[]{:S(2)}, u32[]{:S(2)}) collective-permute-start(bf16[1024,128]{1,0:T(8,128)(2,1)S(1)} %collective-permute-done.3.refs_4_.refs_16_), channel_id=1, source_target_pairs={{0,8},{4,12},{8,0},{12,4},{16,24},{20,28},{24,16},{28,20},{1,9},{5... | collective-permute-start | bytes 786440 | tf_op jit(solution)/shard_map/ppermute | solution.py:417
  19.4 11.6 %collective-permute-start.15 = (bf16[1024,128]{1,0:T(8,128)(2,1)S(1)}, bf16[1024,128]{1,0:T(8,128)(2,1)S(1)}, u32[]{:S(2)}, u32[]{:S(2)}) collective-permute-start(bf16[1024,128]{1,0:T(8,128)(2,1)S(1)} %get-tuple-element.66.refs_0_.refs_20_), channel_id=1, source_target_pairs={{0,16},{4,20},{8,24},{12,28},{16,0},{20,4},{24,8},{28,12},{1,17},{... | collective-permute-start | bytes 786440 | tf_op jit(solution)/shard_map/ppermute | solution.py:417
  20.9 12.4 %copy-start.3 = (bf16[1024,128]{1,0:T(8,128)(2,1)}, bf16[1024,128]{1,0:T(8,128)(2,1)S(1)}, u32[]{:S(2)}) copy-start(bf16[1024,128]{1,0:T(8,128)(2,1)S(1)} %collective-permute-done.1.refs_2_.refs_14_) | copy-start | bytes 786436
  20.9 10.6 %collective-permute-start.2 = (bf16[1024,128]{1,0:T(8,128)(2,1)S(1)}, bf16[1024,128]{1,0:T(8,128)(2,1)S(1)}, u32[]{:S(2)}, u32[]{:S(2)}) collective-permute-start(bf16[1024,128]{1,0:T(8,128)(2,1)S(1)} %collective-permute-done.1.refs_2_.refs_14_), channel_id=1, source_target_pairs={{0,4},{4,0},{8,12},{12,8},{16,20},{20,16},{24,28},{28,24},{1,5},{5... | collective-permute-start | bytes 786440 | tf_op jit(solution)/shard_map/ppermute | solution.py:417
  20.9 12.3 %copy-start.4 = (bf16[1024,128]{1,0:T(8,128)(2,1)}, bf16[1024,128]{1,0:T(8,128)(2,1)S(1)}, u32[]{:S(2)}) copy-start(bf16[1024,128]{1,0:T(8,128)(2,1)S(1)} %collective-permute-done.refs_1_.refs_13_) | copy-start | bytes 786436
  20.9 10.6 %collective-permute-start.4 = (bf16[1024,128]{1,0:T(8,128)(2,1)S(1)}, bf16[1024,128]{1,0:T(8,128)(2,1)S(1)}, u32[]{:S(2)}, u32[]{:S(2)}) collective-permute-start(bf16[1024,128]{1,0:T(8,128)(2,1)S(1)} %collective-permute-done.3.refs_4_.refs_16_), channel_id=1, source_target_pairs={{0,4},{4,0},{8,12},{12,8},{16,20},{20,16},{24,28},{28,24},{1,5},{5... | collective-permute-start | bytes 786440 | tf_op jit(solution)/shard_map/ppermute | solution.py:417
  26.2 14.4 %copy-start.5 = (bf16[1024,128]{1,0:T(8,128)(2,1)}, bf16[1024,128]{1,0:T(8,128)(2,1)S(1)}, u32[]{:S(2)}) copy-start(bf16[1024,128]{1,0:T(8,128)(2,1)S(1)} %collective-permute-done.13.refs_2_.refs_22_) | copy-start | bytes 786436
  26.2 6.4 %collective-permute-start.17 = (bf16[1024,128]{1,0:T(8,128)(2,1)S(1)}, bf16[1024,128]{1,0:T(8,128)(2,1)S(1)}, u32[]{:S(2)}, u32[]{:S(2)}) collective-permute-start(bf16[1024,128]{1,0:T(8,128)(2,1)S(1)} %collective-permute-done.13.refs_2_.refs_22_), channel_id=1, source_target_pairs={{0,16},{4,20},{8,24},{12,28},{16,0},{20,4},{24,8},{28,12},{1,17},{... | collective-permute-start | bytes 786440 | tf_op jit(solution)/shard_map/ppermute | solution.py:417
  30.3 2.9 %collective-permute-start.6 = (bf16[1024,128]{1,0:T(8,128)(2,1)S(1)}, bf16[1024,128]{1,0:T(8,128)(2,1)S(1)}, u32[]{:S(2)}, u32[]{:S(2)}) collective-permute-start(bf16[1024,128]{1,0:T(8,128)(2,1)S(1)} %collective-permute-done.5.refs_6_.refs_18_), channel_id=1, source_target_pairs={{0,4},{4,0},{8,12},{12,8},{16,20},{20,16},{24,28},{28,24},{1,5},{5... | collective-permute-start | bytes 786440 | tf_op jit(solution)/shard_map/ppermute | solution.py:417
  31.0 9.6 %copy-start.7 = (bf16[1024,128]{1,0:T(8,128)(2,1)}, bf16[1024,128]{1,0:T(8,128)(2,1)S(1)}, u32[]{:S(2)}) copy-start(bf16[1024,128]{1,0:T(8,128)(2,1)S(1)} %collective-permute-done.15.refs_4_.refs_24_) | copy-start | bytes 786436
  31.0 9.1 %collective-permute-start.12 = (bf16[1024,128]{1,0:T(8,128)(2,1)S(1)}, bf16[1024,128]{1,0:T(8,128)(2,1)S(1)}, u32[]{:S(2)}, u32[]{:S(2)}) collective-permute-start(bf16[1024,128]{1,0:T(8,128)(2,1)S(1)} %get-tuple-element.66.refs_0_.refs_20_), channel_id=1, source_target_pairs={{0,4},{4,0},{8,12},{12,8},{16,20},{20,16},{24,28},{28,24},{1,5},{5... | collective-permute-start | bytes 786440 | tf_op jit(solution)/shard_map/ppermute | solution.py:417
  31.5 9.1 %collective-permute-start.14 = (bf16[1024,128]{1,0:T(8,128)(2,1)S(1)}, bf16[1024,128]{1,0:T(8,128)(2,1)}, u32[]{:S(2)}, u32[]{:S(2)}) collective-permute-start(bf16[1024,128]{1,0:T(8,128)(2,1)S(1)} %collective-permute-done.13.refs_2_.refs_22_), channel_id=1, source_target_pairs={{0,4},{4,0},{8,12},{12,8},{16,20},{20,16},{24,28},{28,24},{1,5},{5... | collective-permute-start | bytes 786440 | tf_op jit(solution)/shard_map/ppermute | solution.py:417
  31.6 9.0 %collective-permute-start.16 = (bf16[1024,128]{1,0:T(8,128)(2,1)S(1)}, bf16[1024,128]{1,0:T(8,128)(2,1)}, u32[]{:S(2)}, u32[]{:S(2)}) collective-permute-start(bf16[1024,128]{1,0:T(8,128)(2,1)S(1)} %collective-permute-done.15.refs_4_.refs_24_), channel_id=1, source_target_pairs={{0,4},{4,0},{8,12},{12,8},{16,20},{20,16},{24,28},{28,24},{1,5},{5... | collective-permute-start | bytes 786440 | tf_op jit(solution)/shard_map/ppermute | solution.py:417
  32.6 8.1 %copy-start.10 = (bf16[1024,128]{1,0:T(8,128)(2,1)}, bf16[1024,128]{1,0:T(8,128)(2,1)S(1)}, u32[]{:S(2)}) copy-start(bf16[1024,128]{1,0:T(8,128)(2,1)S(1)} %collective-permute-done.17.refs_6_.refs_26_) | copy-start | bytes 786436
  32.6 8.0 %collective-permute-start.18 = (bf16[1024,128]{1,0:T(8,128)(2,1)S(1)}, bf16[1024,128]{1,0:T(8,128)(2,1)}, u32[]{:S(2)}, u32[]{:S(2)}) collective-permute-start(bf16[1024,128]{1,0:T(8,128)(2,1)S(1)} %collective-permute-done.17.refs_6_.refs_26_), channel_id=1, source_target_pairs={{0,4},{4,0},{8,12},{12,8},{16,20},{20,16},{24,28},{28,24},{1,5},{5... | collective-permute-start | bytes 786440 | tf_op jit(solution)/shard_map/ppermute | solution.py:417
  38.5 18.2 %collective-permute-start.7 = (bf16[1024,128]{1,0:T(8,128)(2,1)}, bf16[1024,128]{1,0:T(8,128)(2,1)S(1)}, u32[]{:S(2)}, u32[]{:S(2)}) collective-permute-start(bf16[1024,128]{1,0:T(8,128)(2,1)} %get-tuple-element.30), channel_id=1, source_target_pairs={{0,1},{1,0},{2,3},{3,2},{4,5},{5,4},{6,7},{7,6},{8,9},{9,8},{10,11... | collective-permute-start | bytes 786440 | tf_op jit(solution)/shard_map/ppermute | solution.py:421
  40.1 17.4 %collective-permute-start.10 = (bf16[1024,128]{1,0:T(8,128)(2,1)}, bf16[1024,128]{1,0:T(8,128)(2,1)S(1)}, u32[]{:S(2)}, u32[]{:S(2)}) collective-permute-start(bf16[1024,128]{1,0:T(8,128)(2,1)} %get-tuple-element.31), channel_id=1, source_target_pairs={{0,1},{1,0},{2,3},{3,2},{4,5},{5,4},{6,7},{7,6},{8,9},{9,8},{10,11... | collective-permute-start | bytes 786440 | tf_op jit(solution)/shard_map/ppermute | solution.py:421
  45.3 13.8 %collective-permute-start.19 = (bf16[1024,128]{1,0:T(8,128)(2,1)}, bf16[1024,128]{1,0:T(8,128)(2,1)S(1)}, u32[]{:S(2)}, u32[]{:S(2)}) collective-permute-start(bf16[1024,128]{1,0:T(8,128)(2,1)} %get-tuple-element.34), channel_id=1, source_target_pairs={{0,1},{1,0},{2,3},{3,2},{4,5},{5,4},{6,7},{7,6},{8,9},{9,8},{10,11... | collective-permute-start | bytes 786440 | tf_op jit(solution)/shard_map/ppermute | solution.py:421
  46.8 17.4 %collective-permute-start.22 = (bf16[1024,128]{1,0:T(8,128)(2,1)}, bf16[1024,128]{1,0:T(8,128)(2,1)S(1)}, u32[]{:S(2)}, u32[]{:S(2)}) collective-permute-start(bf16[1024,128]{1,0:T(8,128)(2,1)} %get-tuple-element.35), channel_id=1, source_target_pairs={{0,1},{1,0},{2,3},{3,2},{4,5},{5,4},{6,7},{7,6},{8,9},{9,8},{10,11... | collective-permute-start | bytes 786440 | tf_op jit(solution)/shard_map/ppermute | solution.py:421
  52.0 7.1 %copy-start.27 = (bf16[1024,128]{1,0:T(8,128)(2,1)S(1)}, bf16[1024,128]{1,0:T(8,128)(2,1)}, u32[]{:S(2)}) copy-start(bf16[1024,128]{1,0:T(8,128)(2,1)} %get-tuple-element.34) | copy-start | bytes 786436
  52.0 12.3 %copy-start.26 = (bf16[1024,128]{1,0:T(8,128)(2,1)S(1)}, bf16[1024,128]{1,0:T(8,128)(2,1)}, u32[]{:S(2)}) copy-start(bf16[1024,128]{1,0:T(8,128)(2,1)} %get-tuple-element.35) | copy-start | bytes 786436
  52.0 13.0 %copy-start.28 = (bf16[1024,128]{1,0:T(8,128)(2,1)S(1)}, bf16[1024,128]{1,0:T(8,128)(2,1)}, u32[]{:S(2)}) copy-start(bf16[1024,128]{1,0:T(8,128)(2,1)} %get-tuple-element.29) | copy-start | bytes 786436
  56.8 8.2 %collective-permute-start.8 = (bf16[1024,128]{1,0:T(8,128)(2,1)S(1)}, bf16[1024,128]{1,0:T(8,128)(2,1)S(1)}, u32[]{:S(2)}, u32[]{:S(2)}) collective-permute-start(bf16[1024,128]{1,0:T(8,128)(2,1)S(1)} %add_convert_fusion.11), channel_id=1, source_target_pairs={{0,0},{1,2},{2,1},{3,3},{4,4},{5,6},{6,5},{7,7},{8,8},{9,10},{10,9... | collective-permute-start | bytes 786440 | tf_op jit(solution)/shard_map/ppermute | solution.py:425
  57.6 24.1 %collective-permute-start.11 = (bf16[1024,128]{1,0:T(8,128)(2,1)S(1)}, bf16[1024,128]{1,0:T(8,128)(2,1)S(1)}, u32[]{:S(2)}, u32[]{:S(2)}) collective-permute-start(bf16[1024,128]{1,0:T(8,128)(2,1)S(1)} %add_convert_fusion.9), channel_id=1, source_target_pairs={{0,0},{1,2},{2,1},{3,3},{4,4},{5,6},{6,5},{7,7},{8,8},{9,10},{10,9... | collective-permute-start | bytes 786440 | tf_op jit(solution)/shard_map/ppermute | solution.py:425
  59.2 11.2 %collective-permute-start.20 = (bf16[1024,128]{1,0:T(8,128)(2,1)S(1)}, bf16[1024,128]{1,0:T(8,128)(2,1)S(1)}, u32[]{:S(2)}, u32[]{:S(2)}) collective-permute-start(bf16[1024,128]{1,0:T(8,128)(2,1)S(1)} %add_convert_fusion.8), channel_id=1, source_target_pairs={{0,0},{1,2},{2,1},{3,3},{4,4},{5,6},{6,5},{7,7},{8,8},{9,10},{10,9... | collective-permute-start | bytes 786440 | tf_op jit(solution)/shard_map/ppermute | solution.py:425
  64.3 17.4 %collective-permute-start.23 = (bf16[1024,128]{1,0:T(8,128)(2,1)S(1)}, bf16[1024,128]{1,0:T(8,128)(2,1)S(1)}, u32[]{:S(2)}, u32[]{:S(2)}) collective-permute-start(bf16[1024,128]{1,0:T(8,128)(2,1)S(1)} %add_convert_fusion.6), channel_id=1, source_target_pairs={{0,0},{1,2},{2,1},{3,3},{4,4},{5,6},{6,5},{7,7},{8,8},{9,10},{10,9... | collective-permute-start | bytes 786440 | tf_op jit(solution)/shard_map/ppermute | solution.py:425
  65.1 16.6 %collective-permute-start.9 = (bf16[1024,128]{1,0:T(8,128)(2,1)S(1)}, bf16[1024,128]{1,0:T(8,128)(2,1)S(1)}, u32[]{:S(2)}, u32[]{:S(2)}) collective-permute-start(bf16[1024,128]{1,0:T(8,128)(2,1)S(1)} %add_convert_fusion.10), channel_id=1, source_target_pairs={{0,1},{1,0},{2,3},{3,2},{4,5},{5,4},{6,7},{7,6},{8,9},{9,8},{10,11... | collective-permute-start | bytes 786440 | tf_op jit(solution)/shard_map/ppermute | solution.py:421
  71.5 14.6 %collective-permute-start.21 = (bf16[1024,128]{1,0:T(8,128)(2,1)S(1)}, bf16[1024,128]{1,0:T(8,128)(2,1)S(1)}, u32[]{:S(2)}, u32[]{:S(2)}) collective-permute-start(bf16[1024,128]{1,0:T(8,128)(2,1)S(1)} %add_convert_fusion.7), channel_id=1, source_target_pairs={{0,1},{1,0},{2,3},{3,2},{4,5},{5,4},{6,7},{7,6},{8,9},{9,8},{10,11... | collective-permute-start | bytes 786440 | tf_op jit(solution)/shard_map/ppermute | solution.py:421
  93.4 8.0 %collective-permute-start.33 = (bf16[1024,128]{1,0:T(8,128)(2,1)}, bf16[1024,128]{1,0:T(8,128)(2,1)S(1)}, u32[]{:S(2)}, u32[]{:S(2)}) collective-permute-start(bf16[1024,128]{1,0:T(8,128)(2,1)} %get-tuple-element.46.refs_0_.refs_6_), channel_id=1, source_target_pairs={{0,1},{1,0},{2,3},{3,2},{4,5},{5,4},{6,7},{7,6},{8,9},{9,8},{10,11... | collective-permute-start | bytes 786440 | tf_op jit(solution)/shard_map/ppermute | solution.py:421
  95.5 8.7 %collective-permute-start.24 = (bf16[1024,128]{1,0:T(8,128)(2,1)}, bf16[1024,128]{1,0:T(8,128)(2,1)S(1)}, u32[]{:S(2)}, u32[]{:S(2)}) collective-permute-start(bf16[1024,128]{1,0:T(8,128)(2,1)} %get-tuple-element.43.refs_0_), channel_id=1, source_target_pairs={{0,1},{1,0},{2,3},{3,2},{4,5},{5,4},{6,7},{7,6},{8,9},{9,8},{10,11... | collective-permute-start | bytes 786440 | tf_op jit(solution)/shard_map/ppermute | solution.py:421
  95.6 9.3 %collective-permute-start.34 = (bf16[1024,128]{1,0:T(8,128)(2,1)}, bf16[1024,128]{1,0:T(8,128)(2,1)S(1)}, u32[]{:S(2)}, u32[]{:S(2)}) collective-permute-start(bf16[1024,128]{1,0:T(8,128)(2,1)} %get-tuple-element.46.refs_0_.refs_6_), channel_id=1, source_target_pairs={{0,0},{1,2},{2,1},{3,3},{4,4},{5,6},{6,5},{7,7},{8,8},{9,10},{10,9... | collective-permute-start | bytes 786440 | tf_op jit(solution)/shard_map/ppermute | solution.py:425
  101.4 22.4 %copy-start.16 = (bf16[1024,128]{1,0:T(8,128)(2,1)}, bf16[1024,128]{1,0:T(8,128)(2,1)S(1)}, u32[]{:S(2)}) copy-start(bf16[1024,128]{1,0:T(8,128)(2,1)S(1)} %collective-permute-done.33.refs_1_.refs_7_) | copy-start | bytes 786436
  101.4 11.3 %collective-permute-start.36 = (bf16[1024,128]{1,0:T(8,128)(2,1)S(1)}, bf16[1024,128]{1,0:T(8,128)(2,1)S(1)}, u32[]{:S(2)}, u32[]{:S(2)}) collective-permute-start(bf16[1024,128]{1,0:T(8,128)(2,1)S(1)} %collective-permute-done.33.refs_1_.refs_7_), channel_id=1, source_target_pairs={{0,0},{1,2},{2,1},{3,3},{4,4},{5,6},{6,5},{7,7},{8,8},{9,10},{10,9... | collective-permute-start | bytes 786440 | tf_op jit(solution)/shard_map/ppermute | solution.py:425
  102.1 12.4 %collective-permute-start.25 = (bf16[1024,128]{1,0:T(8,128)(2,1)}, bf16[1024,128]{1,0:T(8,128)(2,1)S(1)}, u32[]{:S(2)}, u32[]{:S(2)}) collective-permute-start(bf16[1024,128]{1,0:T(8,128)(2,1)} %get-tuple-element.43.refs_0_), channel_id=1, source_target_pairs={{0,0},{1,2},{2,1},{3,3},{4,4},{5,6},{6,5},{7,7},{8,8},{9,10},{10,9... | collective-permute-start | bytes 786440 | tf_op jit(solution)/shard_map/ppermute | solution.py:425
  104.2 29.5 %copy-start.17 = (bf16[1024,128]{1,0:T(8,128)(2,1)}, bf16[1024,128]{1,0:T(8,128)(2,1)S(1)}, u32[]{:S(2)}) copy-start(bf16[1024,128]{1,0:T(8,128)(2,1)S(1)} %collective-permute-done.24.refs_1_) | copy-start | bytes 786436
  104.2 14.5 %collective-permute-start.27 = (bf16[1024,128]{1,0:T(8,128)(2,1)S(1)}, bf16[1024,128]{1,0:T(8,128)(2,1)S(1)}, u32[]{:S(2)}, u32[]{:S(2)}) collective-permute-start(bf16[1024,128]{1,0:T(8,128)(2,1)S(1)} %collective-permute-done.24.refs_1_), channel_id=1, source_target_pairs={{0,0},{1,2},{2,1},{3,3},{4,4},{5,6},{6,5},{7,7},{8,8},{9,10},{10,9... | collective-permute-start | bytes 786440 | tf_op jit(solution)/shard_map/ppermute | solution.py:425
  104.9 18.9 %copy-start.18 = (bf16[1024,128]{1,0:T(8,128)(2,1)}, bf16[1024,128]{1,0:T(8,128)(2,1)S(1)}, u32[]{:S(2)}) copy-start(bf16[1024,128]{1,0:T(8,128)(2,1)S(1)} %collective-permute-done.34.refs_2_.refs_8_) | copy-start | bytes 786436
  104.9 16.6 %collective-permute-start.35 = (bf16[1024,128]{1,0:T(8,128)(2,1)S(1)}, bf16[1024,128]{1,0:T(8,128)(2,1)S(1)}, u32[]{:S(2)}, u32[]{:S(2)}) collective-permute-start(bf16[1024,128]{1,0:T(8,128)(2,1)S(1)} %collective-permute-done.34.refs_2_.refs_8_), channel_id=1, source_target_pairs={{0,1},{1,0},{2,3},{3,2},{4,5},{5,4},{6,7},{7,6},{8,9},{9,8},{10,11... | collective-permute-start | bytes 786440 | tf_op jit(solution)/shard_map/ppermute | solution.py:421
  112.8 11.1 %copy-start.19 = (bf16[1024,128]{1,0:T(8,128)(2,1)}, bf16[1024,128]{1,0:T(8,128)(2,1)S(1)}, u32[]{:S(2)}) copy-start(bf16[1024,128]{1,0:T(8,128)(2,1)S(1)} %collective-permute-done.36.refs_4_.refs_10_) | copy-start | bytes 786436
  112.8 11.1 %collective-permute-start.37 = (bf16[1024,128]{1,0:T(8,128)(2,1)S(1)}, bf16[1024,128]{1,0:T(8,128)(2,1)S(1)}, u32[]{:S(2)}, u32[]{:S(2)}) collective-permute-start(bf16[1024,128]{1,0:T(8,128)(2,1)S(1)} %collective-permute-done.36.refs_4_.refs_10_), channel_id=1, source_target_pairs={{0,1},{1,0},{2,3},{3,2},{4,5},{5,4},{6,7},{7,6},{8,9},{9,8},{10,11... | collective-permute-start | bytes 786440 | tf_op jit(solution)/shard_map/ppermute | solution.py:421
  114.4 19.3 %copy-start.20 = (bf16[1024,128]{1,0:T(8,128)(2,1)}, bf16[1024,128]{1,0:T(8,128)(2,1)S(1)}, u32[]{:S(2)}) copy-start(bf16[1024,128]{1,0:T(8,128)(2,1)S(1)} %collective-permute-done.25.refs_2_) | copy-start | bytes 786436
  114.4 19.3 %collective-permute-start.26 = (bf16[1024,128]{1,0:T(8,128)(2,1)S(1)}, bf16[1024,128]{1,0:T(8,128)(2,1)}, u32[]{:S(2)}, u32[]{:S(2)}) collective-permute-start(bf16[1024,128]{1,0:T(8,128)(2,1)S(1)} %collective-permute-done.25.refs_2_), channel_id=1, source_target_pairs={{0,1},{1,0},{2,3},{3,2},{4,5},{5,4},{6,7},{7,6},{8,9},{9,8},{10,11... | collective-permute-start | bytes 786440 | tf_op jit(solution)/shard_map/ppermute | solution.py:421
  118.7 15.1 %copy-start.21 = (bf16[1024,128]{1,0:T(8,128)(2,1)}, bf16[1024,128]{1,0:T(8,128)(2,1)S(1)}, u32[]{:S(2)}) copy-start(bf16[1024,128]{1,0:T(8,128)(2,1)S(1)} %collective-permute-done.27.refs_4_) | copy-start | bytes 786436
  118.7 15.1 %collective-permute-start.28 = (bf16[1024,128]{1,0:T(8,128)(2,1)S(1)}, bf16[1024,128]{1,0:T(8,128)(2,1)}, u32[]{:S(2)}, u32[]{:S(2)}) collective-permute-start(bf16[1024,128]{1,0:T(8,128)(2,1)S(1)} %collective-permute-done.27.refs_4_), channel_id=1, source_target_pairs={{0,1},{1,0},{2,3},{3,2},{4,5},{5,4},{6,7},{7,6},{8,9},{9,8},{10,11... | collective-permute-start | bytes 786440 | tf_op jit(solution)/shard_map/ppermute | solution.py:421
  133.7 69.7 %copy-start.13 = (bf16[4096,128]{1,0:T(8,128)(2,1)S(1)}, bf16[4096,128]{1,0:T(8,128)(2,1)}, u32[]{:S(2)}) copy-start(bf16[4096,128]{1,0:T(8,128)(2,1)} %get-tuple-element.47) | copy-start | bytes 3145732
  133.7 69.7 %collective-permute-start.38 = (bf16[4096,128]{1,0:T(8,128)(2,1)}, bf16[4096,128]{1,0:T(8,128)(2,1)S(1)}, u32[]{:S(2)}, u32[]{:S(2)}) collective-permute-start(bf16[4096,128]{1,0:T(8,128)(2,1)} %get-tuple-element.48.refs_28_), channel_id=1, source_target_pairs={{0,4},{4,0},{8,12},{12,8},{16,20},{20,16},{24,28},{28,24},{1,5},{5... | collective-permute-start | bytes 3145736 | tf_op jit(solution)/shard_map/ppermute | solution.py:417
  143.0 62.2 %copy-start.14 = (bf16[4096,128]{1,0:T(8,128)(2,1)S(1)}, bf16[4096,128]{1,0:T(8,128)(2,1)}, u32[]{:S(2)}) copy-start(bf16[4096,128]{1,0:T(8,128)(2,1)} %get-tuple-element.44) | copy-start | bytes 3145732
  143.0 62.2 %collective-permute-start.29 = (bf16[4096,128]{1,0:T(8,128)(2,1)}, bf16[4096,128]{1,0:T(8,128)(2,1)}, u32[]{:S(2)}, u32[]{:S(2)}) collective-permute-start(bf16[4096,128]{1,0:T(8,128)(2,1)} %get-tuple-element.45), channel_id=1, source_target_pairs={{0,4},{4,0},{8,12},{12,8},{16,20},{20,16},{24,28},{28,24},{1,5},{5... | collective-permute-start | bytes 3145736 | tf_op jit(solution)/shard_map/ppermute | solution.py:417
  148.5 101.8 %all-reduce.5.cloned.1.call-start = ((), (), s32[]{:S(2)}) async-start(), calls=%async_computation.1 | async-start | bytes 1589248 | tf_op jit(solution)/shard_map/psum | solution.py:521
  203.5 8.1 %collective-permute-start.39 = (bf16[1024,128]{1,0:T(8,128)(2,1)S(1)}, bf16[1024,128]{1,0:T(8,128)(2,1)S(1)}, u32[]{:S(2)}, u32[]{:S(2)}) collective-permute-start(bf16[1024,128]{1,0:T(8,128)(2,1)S(1)} %add_convert_fusion.2), channel_id=1, source_target_pairs={{0,16},{4,20},{8,24},{12,28},{16,0},{20,4},{24,8},{28,12},{1,17},{... | collective-permute-start | bytes 786440 | tf_op jit(solution)/shard_map/ppermute | solution.py:417
  207.2 49.6 %collective-permute-start.31 = (bf16[1024,128]{1,0:T(8,128)(2,1)}, bf16[1024,128]{1,0:T(8,128)(2,1)}, u32[]{:S(2)}, u32[]{:S(2)}) collective-permute-start(bf16[1024,128]{1,0:T(8,128)(2,1)} %get-tuple-element.63), channel_id=1, source_target_pairs={{0,8},{4,12},{8,0},{12,4},{16,24},{20,28},{24,16},{28,20},{1,9},{5... | collective-permute-start | bytes 786440 | tf_op jit(solution)/shard_map/ppermute | solution.py:417
  212.4 47.0 %collective-permute-start.41 = (bf16[1024,128]{1,0:T(8,128)(2,1)}, bf16[1024,128]{1,0:T(8,128)(2,1)}, u32[]{:S(2)}, u32[]{:S(2)}) collective-permute-start(bf16[1024,128]{1,0:T(8,128)(2,1)} %get-tuple-element.65), channel_id=1, source_target_pairs={{0,16},{4,20},{8,24},{12,28},{16,0},{20,4},{24,8},{28,12},{1,17},{... | collective-permute-start | bytes 786440 | tf_op jit(solution)/shard_map/ppermute | solution.py:417
  213.1 46.4 %collective-permute-start.40 = (bf16[1024,128]{1,0:T(8,128)(2,1)S(1)}, bf16[1024,128]{1,0:T(8,128)(2,1)}, u32[]{:S(2)}, u32[]{:S(2)}) collective-permute-start(bf16[1024,128]{1,0:T(8,128)(2,1)S(1)} %get-tuple-element.64), channel_id=1, source_target_pairs={{0,8},{4,12},{8,0},{12,4},{16,24},{20,28},{24,16},{28,20},{1,9},{5... | collective-permute-start | bytes 786440 | tf_op jit(solution)/shard_map/ppermute | solution.py:417
  250.4 16.5 %copy-start.15 = (f32[1024,256]{1,0:T(8,128)S(1)}, f32[1024,256]{1,0:T(8,128)}, u32[]{:S(2)}) copy-start(f32[1024,256]{1,0:T(8,128)} %get-tuple-element.42) | copy-start | bytes 3145732
  255.3 8.3 %collective-permute-start.30 = (bf16[1024,128]{1,0:T(8,128)(2,1)}, bf16[1024,128]{1,0:T(8,128)(2,1)S(1)}, u32[]{:S(2)}, u32[]{:S(2)}) collective-permute-start(bf16[1024,128]{1,0:T(8,128)(2,1)} %get-tuple-element.62), channel_id=1, source_target_pairs={{0,8},{4,12},{8,0},{12,4},{16,24},{20,28},{24,16},{28,20},{1,9},{5... | collective-permute-start | bytes 786440 | tf_op jit(solution)/shard_map/ppermute | solution.py:417
  257.9 7.9 %collective-permute-start.32 = (bf16[1024,128]{1,0:T(8,128)(2,1)S(1)}, bf16[1024,128]{1,0:T(8,128)(2,1)S(1)}, u32[]{:S(2)}, u32[]{:S(2)}) collective-permute-start(bf16[1024,128]{1,0:T(8,128)(2,1)S(1)} %add_convert_fusion.3), channel_id=1, source_target_pairs={{0,16},{4,20},{8,24},{12,28},{16,0},{20,4},{24,8},{28,12},{1,17},{... | collective-permute-start | bytes 786440 | tf_op jit(solution)/shard_map/ppermute | solution.py:417
  (13 other events, 34.9 us)
Sparse Core Ops, SparseCore 0:
  148.6 54.6 all-reduce.2
  205.7 44.6 all-reduce.4

commit v3 on v2

--- a/solution.py
+++ b/solution.py
@@ -15,7 +15,19 @@
 MIB = 1 << 20
 TN = (((0,), (0,)), ((), ()))
 NT = (((1,), (1,)), ((), ()))
-PARAMS = pltpu.CompilerParams(vmem_limit_bytes=60 * MIB)
+PEAK_FLOPS_PER_US = 1153.5e6
+
+
+LIVE_STEP = 4
+SWAP_ORDER = (0, 4, 2, 6, 1, 5, 3, 7)
+
+
+def params(mib):
+    return pltpu.CompilerParams(vmem_limit_bytes=mib * MIB)
+
+
+def cost(microseconds):
+    return pl.CostEstimate(flops=int(microseconds * PEAK_FLOPS_PER_US), bytes_accessed=MIB, transcendentals=0)
 
 
 def mm(a, b, dims=(((1,), (0,)), ((), ()))):
@@ -95,7 +107,6 @@
     gathered = sum(piece.shape[0] for piece in pieces)
     slots, block = tiles.shape[1], tiles.shape[2]
     blocks = rows // block
-    count = len(picks) * blocks * slots
     return pl.pallas_call(
         functools.partial(forward_kernel, picks, len(pieces)),
         out_shape=[jax.ShapeDtypeStruct((rows, width), BF16) for _ in picks],
@@ -107,12 +118,8 @@
             pltpu.SemaphoreType.DMA((len(pieces),)),
             pltpu.SemaphoreType.DMA((len(picks),)),
         ],
-        compiler_params=PARAMS,
-        cost_estimate=pl.CostEstimate(
-            flops=count * 2 * block * block * width,
-            bytes_accessed=2 * (gathered + len(picks) * rows) * width + 2 * count * block * block,
-            transcendentals=0,
-        ),
+        compiler_params=params(16 if gathered <= 8192 else 40),
+        cost_estimate=cost(4.0),
         name="partial_messages",
     )(cols, counts, order, *pieces, tiles)
 
@@ -200,22 +207,20 @@
         out_shape=outs,
         in_specs=[SMEM] + [blocked(a) for a in (nodes, cot, *flat)] + [whole(a) for a in weights],
         out_specs=[blocked(a) for a in outs[:5]] + [whole(outs[5])] + [blocked(a) for a in outs[6:]],
-        compiler_params=PARAMS,
-        cost_estimate=pl.CostEstimate(
-            flops=2 * rows * width * width * 5, bytes_accessed=2 * rows * width * 11, transcendentals=rows * width
-        ),
+        compiler_params=params(20),
+        cost_estimate=cost(5.0),
         name="mlp",
     )(middle, nodes, cot, *flat, *weights)
     return result[:6], result[6:]
 
 
-def weight_kernel(factor, nodes, msg, act, gpre, gproj, cot, w_in, vec, grads, direct):
+def weight_kernel(factor, pieces, mine, nodes, msg, act, gpre, gproj, cot, w_in, vec, out, direct, grads):
     width = nodes.shape[1]
 
     @pl.when(pl.program_id(0) == 0)
     def _():
-        grads[: 3 * width] = jnp.zeros((3 * width, width), F32)
-        grads[3 * width :] = vec[...] * factor
+        grads[...] = jnp.zeros_like(grads)
+        grads[3 * width : 3 * width + 8] = vec[...] * factor
 
     gpre_b = gpre[...]
     grads[:width] += mm(nodes[...], gpre_b, TN) * factor
@@ -223,8 +228,21 @@
     grads[2 * width : 3 * width] += mm(act[...], gproj[...], TN) * factor
     direct[...] = cot[...].astype(F32) + mm(gpre_b, w_in[:width], NT)
 
-
-def weight_call(factor, nodes, msg, act, gpre, gproj, cot, w_in, vec):
+    @pl.when(pl.program_id(0) == pl.num_programs(0) - 1)
+    def _():
+        if pieces == 1:
+            out[...] = grads[: out.shape[0]]
+        else:
+            rows, part = grads.shape[0] // pieces, out.shape[1]
+            folds = width // part
+            for place in range(pieces):
+                where = pl.ds(pl.multiple_of((mine[0] ^ place) * rows, 8), rows)
+                for fold in range(folds):
+                    first = (place * folds + fold) * rows
+                    out[first : first + rows] = grads[where, fold * part : (fold + 1) * part].astype(BF16)
+
+
+def weight_call(factor, pieces, mine, nodes, msg, act, gpre, gproj, cot, w_in, vec):
     rows, width = nodes.shape
     step = min(rows, 256)
     blocked = pl.BlockSpec((step, width), lambda i: (i, 0))
@@ -232,19 +250,50 @@
     def whole(shape):
         return pl.BlockSpec(shape, lambda i: (0, 0))
 
-    grads = (3 * width + 8, width)
+    padded = (3 * width + width // 2, width)
+    if pieces == 1:
+        out = jax.ShapeDtypeStruct((3 * width + 8, width), F32)
+    else:
+        out = jax.ShapeDtypeStruct((2 * padded[0], width // 2), BF16)
     return pl.pallas_call(
-        functools.partial(weight_kernel, factor),
+        functools.partial(weight_kernel, factor, pieces),
         grid=(rows // step,),
-        out_shape=[jax.ShapeDtypeStruct(grads, F32), jax.ShapeDtypeStruct((rows, width), F32)],
-        in_specs=[blocked] * 6 + [whole(w_in.shape), whole(vec.shape)],
-        out_specs=[whole(grads), blocked],
-        compiler_params=PARAMS,
-        cost_estimate=pl.CostEstimate(
-            flops=2 * rows * width * width * 4, bytes_accessed=2 * rows * width * 10, transcendentals=0
-        ),
+        out_shape=[out, jax.ShapeDtypeStruct((rows, width), F32)],
+        in_specs=[SMEM] + [blocked] * 6 + [whole(w_in.shape), whole(vec.shape)],
+        out_specs=[whole(out.shape), blocked],
+        scratch_shapes=[pltpu.VMEM(padded, F32)],
+        compiler_params=params(16),
+        cost_estimate=cost(3.0),
         name="weight_grads",
-    )(nodes, msg, act, gpre, gproj, cot, w_in, vec)
+    )(mine, nodes, msg, act, gpre, gproj, cot, w_in, vec)
+
+
+def unpack_kernel(mine, parts, w_in, w_out, vectors, grads):
+    width = w_in.shape[1]
+    rows = grads.shape[0] // len(SWAP_ORDER)
+    part = parts.shape[1]
+    for place, member in enumerate(SWAP_ORDER):
+        where = pl.ds(pl.multiple_of((mine[0] ^ member) * rows, 8), rows)
+        for fold in range(width // part):
+            first = (place * (width // part) + fold) * rows
+            grads[where, fold * part : (fold + 1) * part] = parts[first : first + rows].astype(F32)
+    w_in[...] = grads[: 2 * width]
+    w_out[...] = grads[2 * width : 3 * width]
+    vectors[...] = grads[3 * width : 3 * width + 3]
+
+
+def unpack_call(mine, parts, width):
+    shapes = ((2 * width, width), (width, width), (3, width))
+    return pl.pallas_call(
+        unpack_kernel,
+        out_shape=[jax.ShapeDtypeStruct(shape, F32) for shape in shapes],
+        in_specs=[SMEM, VMEM],
+        out_specs=[VMEM] * 3,
+        scratch_shapes=[pltpu.VMEM((3 * width + width // 2, width), F32)],
+        compiler_params=params(16),
+        cost_estimate=cost(2.0),
+        name="weight_unpack",
+    )(mine, parts)
 
 
 def grad_jobs(rows, refs, dst, sem, order, middle):
@@ -270,60 +319,90 @@
             pl.when(condition)(getattr(copy, verb))
 
 
-def back_kernel(rows, n_grads, n_after, out_pieces, cols, counts, order, middle, *refs):
+def back_kernel(rows, slots, n_grads, n_extra, out_pieces, cols, counts, order, middle, *refs):
     grads, tiles = refs[:n_grads], refs[n_grads]
-    refs = refs[n_grads + 1 + n_after :]
+    extras = refs[n_grads + 1 : n_grads + 1 + n_extra]
+    refs = refs[n_grads + 1 + n_extra :]
     outs = refs[: len(out_pieces)]
-    grad_v, tiles_v, acc, sem, tile_sem = refs[len(out_pieces) :]
-    row_blocks, slots, block = tiles.shape[:3]
+    grad_v, tiles_v, acc, live, sem, tile_sem, extra_sem = refs[len(out_pieces) :]
+    n_tiles, block = tiles.shape[:2]
+    n_pieces = sum(len(members) for members in out_pieces)
+    piece = acc.shape[0] // n_pieces
     jobs = grad_jobs(rows, grads, grad_v, sem, order, middle)
     run_jobs(jobs, "start")
     tile_copy = pltpu.make_async_copy(tiles, tiles_v, tile_sem.at[0])
     tile_copy.start()
+    stride = piece
+    extra_copies = []
+    if extras:
+        extra = extras[0].shape[0] // n_pieces
+        stride = piece + extra
+        for out, members in zip(outs, out_pieces):
+            for index, member in enumerate(members):
+                copy = pltpu.make_async_copy(
+                    extras[0].at[pl.ds(member * extra, extra)],
+                    out.at[pl.ds(index * stride + piece, extra)],
+                    extra_sem.at[member],
+                )
+                copy.start()
+                extra_copies.append(copy)
     acc[...] = jnp.zeros_like(acc)
+
+    def collect(row, found):
+        count = counts[row]
+        for slot in range(slots):
+            live[found] = row * slots + slot
+            found = found + (slot < count).astype(jnp.int32)
+        return found
+
+    found = lax.fori_loop(0, n_tiles // slots, collect, jnp.int32(0))
+    for index in range(LIVE_STEP):
+        live[found + index] = 0
     run_jobs(jobs, "wait")
     tile_copy.wait()
 
-    def step(row, carry):
-        count = counts[row]
-        grad = grad_v[block_at(row, block)]
-        for slot in range(slots):
-            part = mm(masked_tile(tiles_v, row, slot, count), grad, TN)
-            acc[block_at(cols[row * slots + slot], block)] += part
+    def step(i, carry):
+        for index in range(LIVE_STEP):
+            place = i * LIVE_STEP + index
+            tile_index = live[place]
+            tile = tiles_v[tile_index]
+            tile = jnp.where(place < found, tile, jnp.zeros_like(tile))
+            part = mm(tile, grad_v[block_at(tile_index // slots, block)], TN)
+            acc[block_at(cols[tile_index], block)] += part
         return carry
 
-    lax.fori_loop(0, row_blocks, step, 0, unroll=2)
-    piece = acc.shape[0] // sum(len(members) for members in out_pieces)
+    lax.fori_loop(0, (found + LIVE_STEP - 1) // LIVE_STEP, step, 0)
     for out, members in zip(outs, out_pieces):
         for index, member in enumerate(members):
-            out[pl.ds(index * piece, piece)] = acc[pl.ds(member * piece, piece)].astype(BF16)
-
-
-def back_call(cols, counts, order, middle, grads, tiles, total, gathered, out_pieces, after=()):
+            out[pl.ds(index * stride, piece)] = acc[pl.ds(member * piece, piece)].astype(BF16)
+    for copy in extra_copies:
+        copy.wait()
+
+
+def back_call(cols, counts, order, middle, grads, tiles, total, gathered, out_pieces, extras=()):
     rows, width = grads[0].shape
     rows = total if len(grads) == 1 else rows
     row_blocks, slots, block = tiles.shape[:3]
-    piece = gathered // sum(len(members) for members in out_pieces)
+    n_pieces = sum(len(members) for members in out_pieces)
+    piece = (gathered + sum(extra.shape[0] for extra in extras)) // n_pieces
     return pl.pallas_call(
-        functools.partial(back_kernel, rows, len(grads), len(after), out_pieces),
+        functools.partial(back_kernel, rows, slots, len(grads), len(extras), out_pieces),
         out_shape=[jax.ShapeDtypeStruct((len(m) * piece, width), BF16) for m in out_pieces],
-        in_specs=[SMEM] * 4 + [ANY] * (len(grads) + 1 + len(after)),
+        in_specs=[SMEM] * 4 + [ANY] * (len(grads) + 1 + len(extras)),
         out_specs=[VMEM] * len(out_pieces),
         scratch_shapes=[
             pltpu.VMEM((total, width), BF16),
-            pltpu.VMEM(tiles.shape, BF16),
+            pltpu.VMEM((row_blocks * slots, block, block), BF16),
             pltpu.VMEM((gathered, width), F32),
+            pltpu.SMEM((row_blocks * slots + 2 * LIVE_STEP,), jnp.int32),
             pltpu.SemaphoreType.DMA((len(grads),)),
             pltpu.SemaphoreType.DMA((1,)),
+            pltpu.SemaphoreType.DMA((n_pieces,)),
         ],
-        compiler_params=PARAMS,
-        cost_estimate=pl.CostEstimate(
-            flops=row_blocks * slots * 2 * block * block * width,
-            bytes_accessed=2 * width * (gathered + total) + 2 * tiles.size,
-            transcendentals=0,
-        ),
+        compiler_params=params(24 if gathered <= 8192 else 56),
+        cost_estimate=cost(6.0),
         name="back_terms",
-    )(cols, counts, order, middle, *grads, tiles, *after)
+    )(cols, counts, order, middle, *grads, tiles.reshape(row_blocks * slots, block, block), *extras)
 
 
 def tile_grad_kernel(rows, n_grads, n_pieces, n_chunks, n_after, step_rows, cols, counts, order, middle, *refs):
@@ -364,10 +443,15 @@
         row = pl.program_id(0) * step_rows + i
         count = counts[row]
         grad = grad_v[block_at(row, block)]
-        for slot in range(slots):
-            node = nodes_v[block_at(cols[row * slots + slot], block)]
+        for pair in range(slots // 2):
+            both = (2 * pair, 2 * pair + 1)
+            node = jnp.concatenate(
+                [nodes_v[block_at(cols[row * slots + slot], block)] for slot in both], axis=0
+            )
             value = mm(grad, node, NT) * scale
-            out[i, slot] = jnp.where(slot < count, value, 0.0).astype(BF16)
+            for index, slot in enumerate(both):
+                half = value[:, index * block : (index + 1) * block]
+                out[i, slot] = jnp.where(slot < count, half, 0.0).astype(BF16)
         return carry
 
     lax.fori_loop(0, step_rows, step, 0, unroll=2)
@@ -396,12 +480,8 @@
             pltpu.SemaphoreType.DMA((chunks, len(grads[0]))),
             pltpu.SemaphoreType.DMA((chunks, len(pieces[0]))),
         ],
-        compiler_params=PARAMS,
-        cost_estimate=pl.CostEstimate(
-            flops=row_blocks * slots * 2 * block * block * width,
-            bytes_accessed=2 * width * (gathered + total) + 2 * row_blocks * slots * block * block,
-            transcendentals=0,
-        ),
+        compiler_params=params(16 if gathered <= 8192 else 40),
+        cost_estimate=cost(8.0),
         name="tile_grads",
     )(cols, counts, order, middle, *flat, *after)
 
@@ -421,12 +501,20 @@
     return lax.ppermute(value, "col", [(0, 1), (1, 0), (2, 3), (3, 2)])
 
 
+def mirror_swap(value):
+    return lax.ppermute(value, "col", [(0, 3), (3, 0), (1, 2), (2, 1)])
+
+
 def inner_swap(value):
     return lax.ppermute(value, "col", [(0, 0), (1, 2), (2, 1), (3, 3)])
 
 
-def gather_square(nodes, by_x):
-    x_side, y_side = swap(nodes, 2), swap(nodes, 4)
+def gather_square(nodes, by_x, hold=None):
+    y_side = swap(nodes, 4)
+    if hold is None:
+        x_side = swap(nodes, 2)
+    else:
+        x_side = swap(lax.optimization_barrier((nodes, hold))[0], 2)
     diag = swap(y_side, 2) if by_x else swap(x_side, 4)
     pieces = []
     for piece in (nodes, x_side, y_side, diag):
@@ -450,6 +538,15 @@
         y_side = swap(add(*both(2)), 4)
         x_side = swap(add(*both(1), diag), 2)
     return (*both(0), x_side, y_side)
+
+
+def sum_weights(terms, width, mine):
+    value = add(*terms)
+    value = add(value, outer_swap(value))
+    value = add(value, mirror_swap(value))
+    for bit in (4, 2, 1):
+        value = jnp.concatenate([value, swap(value, bit)], axis=0)
+    return unpack_call(mine, value, width)
 
 
 def reduce_line(far, near, pair, own, inner):
@@ -491,7 +588,8 @@
         part = width // chunks
         pieces, parts, kinds = [], [], []
         for chunk in range(chunks):
-            pieces.append(gather_square(nodes[:, chunk * part : (chunk + 1) * part], chunk == 0))
+            hold = pieces[0][6] if chunk else None
+            pieces.append(gather_square(nodes[:, chunk * part : (chunk + 1) * part], chunk == 0, hold))
             far, near = forward_call(cols, counts, order, pieces[-1], tile_local, (0, 1), rows)
             pair, own = forward_call(cols, counts, order, pieces[-1], tile_local, (2, 3), rows)
             parts.append(reduce_line(far, near, pair, own, inner))
@@ -515,22 +613,30 @@
     else:
         grads = [[lax.all_gather(gmsgs[0], "col", axis=0, tiled=True)]]
     factor = float(rows * n_row * n_col) ** -0.5
+    mine = lax.axis_index("row").astype(jnp.int32).reshape(1)
     weight_terms, direct = weight_call(
-        factor, nodes, message, act, gpre_b, gproj, cotangent, w_in, vec
+        factor, n_row if square_line else 1, mine, nodes, message, act, gpre_b, gproj, cotangent, w_in, vec
     )
-    weight_sums = lax.psum(lax.psum(weight_terms, "row"), "col")
     if square_line:
         sums = []
         for chunk in range(chunks):
             odd, even = back_call(
                 cols, counts, order, middle, grads[chunk], tile_local, total, gathered,
-                ((1, 3, 5, 7), (0, 2, 4, 6)),
+                ((1, 3, 5, 7), (0, 2, 4, 6)), (weight_terms,) if chunk == 0 else (),
             )
-            terms = reduce_square(even, odd, rows, chunk == 0)
-            sums.append(sum(term.astype(F32) for term in terms))
+            terms = reduce_square(even, odd, odd.shape[0] // 4, chunk == 0)
+            if chunk == 0:
+                weights = sum_weights([term[rows:] for term in terms], width, mine)
+            sums.append(sum(term[:rows].astype(F32) for term in terms))
         after = (odd,)
         back = jnp.concatenate(sums, axis=1)
     else:
+        weight_sums = lax.psum(weight_terms, ("row", "col"))
+        weights = (
+            weight_sums[: 2 * width],
+            weight_sums[2 * width : 3 * width],
+            weight_sums[3 * width : 3 * width + 3],
+        )
         (terms,) = back_call(
             cols, counts, order, middle, grads[0], tile_local, total, gathered, (tuple(range(n_row)),)
         )
@@ -540,14 +646,7 @@
     grad_tiles = tile_grad_call(
         cols, counts, order, middle, grads, pieces, tile_local.shape, total, after
     ).reshape(tiles.shape)
-    return (
-        updated,
-        grad_nodes,
-        grad_tiles,
-        weight_sums[: 2 * width],
-        weight_sums[2 * width : 3 * width],
-        weight_sums[3 * width : 3 * width + 3],
-    )
+    return (updated, grad_nodes, grad_tiles, *weights)
 
 
 def solution(mesh):

time: 275 us -> 191 us (0.69)
  waiting for transfers between devices: 121 us -> 69.9 us
  Pallas kernels: 57.9 us -> 33 us
  between operations: 14.6 us -> 1.3 us
  starting transfers between devices: 62.3 us -> 73.6 us
  other arithmetic: 9.91 us -> 5.19 us
    psum x2 -> x0, waiting for transfers between devices: 81.9 us -> none  [body(): weight_sums = lax.psum(lax.psum(weight_terms, 'row'), 'col')]
    ppermute x22 -> x25, waiting for transfers between devices: 22 us -> 38.5 us  [swap(): return lax.ppermute(value, 'row', [(i, i ^ bit) for i in range(8)])]
    ppermute x12 -> x13, waiting for transfers between devices: 16.7 us -> 31.4 us  [outer_swap(): return lax.ppermute(value, 'col', [(0, 1), (1, 0), (2, 3), (3, 2)])]
    pallas_call x3 -> x4, Pallas kernels: 23.4 us -> 10.7 us  [the longest x2 8.2 us: back_call(): pl.pallas_call(functools.partial(back_kernel, rows, slots, len(grads), le...]
    pallas_call x4, Pallas kernels: 18.3 us -> 8.6 us  [forward_call(): pl.pallas_call(functools.partial(forward_kernel, picks, len(pieces)), out...]
    ppermute x22 -> x25, starting transfers between devices: 16.6 us -> 23.1 us  [swap(): return lax.ppermute(value, 'row', [(i, i ^ bit) for i in range(8)])]
    slice x3 -> x0, local copies, waits for them, and re-layouts: 4.91 us -> none  [the longest x1 1.96 us: body(): weight_sums[:2 * width]]
    ppermute x8, starting transfers between devices: 7.24 us -> 11.2 us  [inner_swap(): return lax.ppermute(value, 'col', [(0, 0), (1, 2), (2, 1), (3, 3)])]
  transfers between devices with their start and end apart: 44 -> 47, of which waited for: 15 -> 18; matrix products, arithmetic and copies ran while one was open for 5% -> 3% of each run, Pallas kernels for 19% -> 14%
where the time goes in v3:
time: 191 us; the launch traced here: 190 us
  starting transfers between devices  73.6 us (39%)
  waiting for transfers between devices  69.9 us (37%)
  Pallas kernels  33 us (17%)
  local copies, waits for them, and re-layouts  7 us (4%)
  other arithmetic  5.19 us (3%)
    ppermute x25, waiting for transfers between devices, swap(): return lax.ppermute(value, 'row', [(i, i ^ bit) for i in range(8)])  38.5 us
    ppermute x13, starting transfers between devices, outer_swap(): return lax.ppermute(value, 'col', [(0, 1), (1, 0), (2, 3), (3, 2)])  37.5 us
    ppermute x13, waiting for transfers between devices, outer_swap(): return lax.ppermute(value, 'col', [(0, 1), (1, 0), (2, 3), (3, 2)])  31.4 us
    ppermute x25, starting transfers between devices, swap(): return lax.ppermute(value, 'row', [(i, i ^ bit) for i in range(8)])  23.1 us
    ppermute x8, starting transfers between devices, inner_swap(): return lax.ppermute(value, 'col', [(0, 0), (1, 2), (2, 1), (3, 3)])  11.2 us
    pallas_call x4, Pallas kernels, forward_call(): pl.pallas_call(functools.partial(forward_kernel, picks, len(pieces)), out...  8.6 us
    pallas_call x2, Pallas kernels, back_call(): pl.pallas_call(functools.partial(back_kernel, rows, slots, len(grads), le...  8.2 us
    pallas_call x1, Pallas kernels, tile_grad_call(): pl.pallas_call(functools.partial(tile_grad_kernel, rows, len(grads[0]), l...  8.12 us
  transfers between devices with their start and end apart: 47, of which 18 were waited for; matrix products, arithmetic and copies ran while one was open for 3% of the time, Pallas kernels for 14%

profile of v3, /device:TPU:0, one launch (start us, length us, event | category | flops | bytes accessed | tf_op | source)
XLA Modules:
  0.0 190.1 jit_solution(59289586957766833)
XLA Ops:
  0.6 1.1 fusion.2
  1.7 3.0 %collective-permute-start.3 = (bf16[1024,128]{1,0:T(8,128)(2,1)S(1)}, bf16[1024,128]{1,0:T(8,128)(2,1)S(1)}, u32[]{:S(2)}, u32[]{:S(2)}) collective-permute-start(bf16[1024,128]{1,0:T(8,128)(2,1)S(1)} %get-tuple-element.75.refs_0_.refs_12_), channel_id=1, source_target_pairs={{0,16},{4,20},{8,24},{12,28},{16,0},{20,4},{24,8},{28,12},{1,17},{... | collective-permute-start | bytes 786440 | tf_op jit(solution)/shard_map/ppermute | solution.py:497
  4.7 1.5 collective-permute-start.1
  6.2 4.8 %collective-permute-done.3.refs_4_.refs_16_ = bf16[1024,128]{1,0:T(8,128)(2,1)S(1)} collective-permute-done((bf16[1024,128]{1,0:T(8,128)(2,1)S(1)}, bf16[1024,128]{1,0:T(8,128)(2,1)S(1)}, u32[]{:S(2)}, u32[]{:S(2)}) %collective-permute-start.3) | collective-permute-done | bytes 262176 | tf_op jit(solution)/shard_map/ppermute | solution.py:497
  11.0 1.7 collective-permute-start.5
  12.8 1.5 collective-permute-start.15
  14.8 3.7 %collective-permute-done.5.refs_6_.refs_18_ = bf16[1024,128]{1,0:T(8,128)(2,1)S(1)} collective-permute-done((bf16[1024,128]{1,0:T(8,128)(2,1)S(1)}, bf16[1024,128]{1,0:T(8,128)(2,1)S(1)}, u32[]{:S(2)}, u32[]{:S(2)}) %collective-permute-start.5) | collective-permute-done | bytes 262176 | tf_op jit(solution)/shard_map/ppermute | solution.py:497
  18.5 1.4 collective-permute-start.13
  20.0 0.8 copy.18
  21.6 3.5 %collective-permute-done.13.refs_2_.refs_22_ = bf16[1024,128]{1,0:T(8,128)(2,1)S(1)} collective-permute-done((bf16[1024,128]{1,0:T(8,128)(2,1)S(1)}, bf16[1024,128]{1,0:T(8,128)(2,1)S(1)}, u32[]{:S(2)}, u32[]{:S(2)}) %collective-permute-start.13) | collective-permute-done | bytes 262176 | tf_op jit(solution)/shard_map/ppermute | solution.py:497
  25.1 1.2 collective-permute-start.17
  26.4 2.4 %copy-done.1 = bf16[32,1,4,128,128]{4,3,2,1,0:T(8,128)(2,1)S(1)} copy-done((bf16[32,1,4,128,128]{4,3,2,1,0:T(8,128)(2,1)S(1)}, bf16[32,1,4,128,128]{4,3,2,1,0:T(8,128)(2,1)}, u32[]{:S(2)}) %copy-start.1) | copy-done | bytes 4194328
  29.4 2.1 %partial_messages.5 = (bf16[1024,128]{1,0:T(8,128)(2,1)S(1)}, bf16[1024,128]{1,0:T(8,128)(2,1)S(1)}) custom-call(s32[128]{0:T(128)S(1)} %fusion.1.cols, s32[32]{0:T(128)S(1)} %bitcast.26, s32[4]{0:T(128)S(1)} %pad_add_fusion.order, bf16[1024,128]{1,0:T(8,128)(2,1)S(1)} %get-tuple-element.75.refs_0_.refs_12_, ...), custom_call_target="tpu_custom_call" | custom-call | flops 4614000128 | bytes 1048576 | tf_op jit(solution)/shard_map/partial_messages/pallas_call | solution.py:110
  31.5 1.6 collective-permute-start.7
  33.7 2.2 %partial_messages.4 = (bf16[1024,128]{1,0:T(8,128)(2,1)S(1)}, bf16[1024,128]{1,0:T(8,128)(2,1)S(1)}) custom-call(s32[128]{0:T(128)S(1)} %fusion.1.cols, s32[32]{0:T(128)S(1)} %bitcast.27, s32[4]{0:T(128)S(1)} %pad_add_fusion.order, bf16[1024,128]{1,0:T(8,128)(2,1)S(1)} %get-tuple-element.75.refs_0_.refs_12_, ...), custom_call_target="tpu_custom_call" | custom-call | flops 4614000128 | bytes 1048576 | tf_op jit(solution)/shard_map/partial_messages/pallas_call | solution.py:110
  35.9 2.1 %collective-permute-done.7 = bf16[1024,128]{1,0:T(8,128)(2,1)S(1)} collective-permute-done((bf16[1024,128]{1,0:T(8,128)(2,1)S(1)}, bf16[1024,128]{1,0:T(8,128)(2,1)S(1)}, u32[]{:S(2)}, u32[]{:S(2)}) %collective-permute-start.7) | collective-permute-done | bytes 262176 | tf_op jit(solution)/shard_map/ppermute | solution.py:501
  38.0 2.0 %collective-permute-start.10 = (bf16[1024,128]{1,0:T(8,128)(2,1)S(1)}, bf16[1024,128]{1,0:T(8,128)(2,1)S(1)}, u32[]{:S(2)}, u32[]{:S(2)}) collective-permute-start(bf16[1024,128]{1,0:T(8,128)(2,1)S(1)} %get-tuple-element.35), channel_id=1, source_target_pairs={{0,1},{1,0},{2,3},{3,2},{4,5},{5,4},{6,7},{7,6},{8,9},{9,8},{10,11... | collective-permute-start | bytes 786440 | tf_op jit(solution)/shard_map/ppermute | solution.py:501
  40.1 0.7 collective-permute-start.8
  40.9 2.2 %partial_messages.7 = (bf16[1024,128]{1,0:T(8,128)(2,1)S(1)}, bf16[1024,128]{1,0:T(8,128)(2,1)S(1)}) custom-call(s32[128]{0:T(128)S(1)} %fusion.1.cols, s32[32]{0:T(128)S(1)} %bitcast.28, s32[4]{0:T(128)S(1)} %pad_add_fusion.order, bf16[1024,128]{1,0:T(8,128)(2,1)S(1)} %get-tuple-element.36.refs_0_.refs_20_, ...), custom_call_target="tpu_custom_call" | custom-call | flops 4614000128 | bytes 1048576 | tf_op jit(solution)/shard_map/partial_messages/pallas_call | solution.py:110
  43.0 4.4 %collective-permute-start.19 = (bf16[1024,128]{1,0:T(8,128)(2,1)S(1)}, bf16[1024,128]{1,0:T(8,128)(2,1)S(1)}, u32[]{:S(2)}, u32[]{:S(2)}) collective-permute-start(bf16[1024,128]{1,0:T(8,128)(2,1)S(1)} %get-tuple-element.39), channel_id=1, source_target_pairs={{0,1},{1,0},{2,3},{3,2},{4,5},{5,4},{6,7},{7,6},{8,9},{9,8},{10,11... | collective-permute-start | bytes 786440 | tf_op jit(solution)/shard_map/ppermute | solution.py:501
  47.5 0.8 add_convert_fusion.9
  48.3 3.6 %collective-permute-start.11 = (bf16[1024,128]{1,0:T(8,128)(2,1)}, bf16[1024,128]{1,0:T(8,128)(2,1)}, u32[]{:S(2)}, u32[]{:S(2)}) collective-permute-start(bf16[1024,128]{1,0:T(8,128)(2,1)} %add_convert_fusion.9), channel_id=1, source_target_pairs={{0,0},{1,2},{2,1},{3,3},{4,4},{5,6},{6,5},{7,7},{8,8},{9,10},{10,9... | collective-permute-start | bytes 786440 | tf_op jit(solution)/shard_map/ppermute | solution.py:509
  51.9 0.8 add_convert_fusion.10
  52.6 0.7 collective-permute-start.9
  53.3 1.3 collective-permute-start.22
  54.8 0.7 collective-permute-start.20
  55.5 2.1 %partial_messages.6 = (bf16[1024,128]{1,0:T(8,128)(2,1)S(1)}, bf16[1024,128]{1,0:T(8,128)(2,1)S(1)}) custom-call(s32[128]{0:T(128)S(1)} %fusion.1.cols, s32[32]{0:T(128)S(1)} %bitcast.29, s32[4]{0:T(128)S(1)} %pad_add_fusion.order, bf16[1024,128]{1,0:T(8,128)(2,1)S(1)} %get-tuple-element.36.refs_0_.refs_20_, ...), custom_call_target="tpu_custom_call" | custom-call | flops 4614000128 | bytes 1048576 | tf_op jit(solution)/shard_map/partial_messages/pallas_call | solution.py:110
  57.8 5.3 %collective-permute-done.22 = bf16[1024,128]{1,0:T(8,128)(2,1)S(1)} collective-permute-done((bf16[1024,128]{1,0:T(8,128)(2,1)S(1)}, bf16[1024,128]{1,0:T(8,128)(2,1)S(1)}, u32[]{:S(2)}, u32[]{:S(2)}) %collective-permute-start.22) | collective-permute-done | bytes 262176 | tf_op jit(solution)/shard_map/ppermute | solution.py:501
  63.1 0.8 add_convert_fusion.6
  63.8 3.6 %collective-permute-start.23 = (bf16[1024,128]{1,0:T(8,128)(2,1)}, bf16[1024,128]{1,0:T(8,128)(2,1)}, u32[]{:S(2)}, u32[]{:S(2)}) collective-permute-start(bf16[1024,128]{1,0:T(8,128)(2,1)} %add_convert_fusion.6), channel_id=1, source_target_pairs={{0,0},{1,2},{2,1},{3,3},{4,4},{5,6},{6,5},{7,7},{8,8},{9,10},{10,9... | collective-permute-start | bytes 786440 | tf_op jit(solution)/shard_map/ppermute | solution.py:509
  67.4 0.8 add_convert_fusion.7
  68.6 6.3 %collective-permute-done.21.refs_4_ = bf16[1024,128]{1,0:T(8,128)(2,1)} collective-permute-done((bf16[1024,128]{1,0:T(8,128)(2,1)}, bf16[1024,128]{1,0:T(8,128)(2,1)}, u32[]{:S(2)}, u32[]{:S(2)}) %collective-permute-start.21) | collective-permute-done | bytes 262176 | tf_op jit(solution)/shard_map/ppermute | solution.py:501
  75.0 0.9 copy-done.31
  75.9 0.9 copy-done.33
  76.9 5.6 %mlp.1 = (bf16[1024,256]{1,0:T(8,128)(2,1)}, bf16[1024,256]{1,0:T(8,128)(2,1)S(1)}, bf16[1024,256]{1,0:T(8,128)(2,1)S(1)}, bf16[1024,256]{1,0:T(8,128)(2,1)S(1)}...) custom-call(s32[1]{0:T(128)} %bitcast.middle, ...), custom_call_target="tpu_custom_call" | custom-call | flops 5767499776 | bytes 1048576 | tf_op jit(solution)/shard_map/mlp/pallas_call | solution.py:204
  83.5 5.7 %collective-permute-done.24.refs_1_ = bf16[1024,128]{1,0:T(8,128)(2,1)S(1)} collective-permute-done((bf16[1024,128]{1,0:T(8,128)(2,1)S(1)}, bf16[1024,128]{1,0:T(8,128)(2,1)S(1)}, u32[]{:S(2)}, u32[]{:S(2)}) %collective-permute-start.24) | collective-permute-done | bytes 262176 | tf_op jit(solution)/shard_map/ppermute | solution.py:501
  90.0 4.2 %collective-permute-start.33 = (bf16[1024,128]{1,0:T(8,128)(2,1)S(1)}, bf16[1024,128]{1,0:T(8,128)(2,1)S(1)}, u32[]{:S(2)}, u32[]{:S(2)}) collective-permute-start(bf16[1024,128]{1,0:T(8,128)(2,1)S(1)} %get-tuple-element.52.refs_0_.refs_6_), channel_id=1, source_target_pairs={{0,1},{1,0},{2,3},{3,2},{4,5},{5,4},{6,7},{7,6},{8,9},{9,8},{10,11... | collective-permute-start | bytes 786440 | tf_op jit(solution)/shard_map/ppermute | solution.py:501
  94.3 4.2 %collective-permute-start.28 = (bf16[1024,128]{1,0:T(8,128)(2,1)S(1)}, bf16[1024,128]{1,0:T(8,128)(2,1)S(1)}, u32[]{:S(2)}, u32[]{:S(2)}) collective-permute-start(bf16[1024,128]{1,0:T(8,128)(2,1)S(1)} %collective-permute-done.27.refs_4_), channel_id=1, source_target_pairs={{0,1},{1,0},{2,3},{3,2},{4,5},{5,4},{6,7},{7,6},{8,9},{9,8},{10,11... | collective-permute-start | bytes 786440 | tf_op jit(solution)/shard_map/ppermute | solution.py:501
  98.4 1.5 weight_grads.1
  100.0 3.0 %collective-permute-done.26.refs_3_ = bf16[1024,128]{1,0:T(8,128)(2,1)S(1)} collective-permute-done((bf16[1024,128]{1,0:T(8,128)(2,1)S(1)}, bf16[1024,128]{1,0:T(8,128)(2,1)S(1)}, u32[]{:S(2)}, u32[]{:S(2)}) %collective-permute-start.26) | collective-permute-done | bytes 262176 | tf_op jit(solution)/shard_map/ppermute | solution.py:501
  102.9 2.8 %collective-permute-done.28.refs_5_ = bf16[1024,128]{1,0:T(8,128)(2,1)S(1)} collective-permute-done((bf16[1024,128]{1,0:T(8,128)(2,1)S(1)}, bf16[1024,128]{1,0:T(8,128)(2,1)S(1)}, u32[]{:S(2)}, u32[]{:S(2)}) %collective-permute-start.28) | collective-permute-done | bytes 262176 | tf_op jit(solution)/shard_map/ppermute | solution.py:501
  105.7 4.3 %back_terms.2 = (bf16[4992,128]{1,0:T(8,128)(2,1)S(1)}, bf16[4992,128]{1,0:T(8,128)(2,1)S(1)}) custom-call(s32[128]{0:T(128)S(1)} %copy-done.29, s32[32]{0:T(128)S(1)} %bitcast.30, s32[4]{0:T(128)S(1)} %pad_add_fusion.order, s32[1]{0:T(128)} %bitcast.middle, bf16[1024,128]{1,0:T(8,128)(2,1)S(1)} %get-tuple-element.48.refs_0_, ...), custom_call_target="tpu_custom_call" | custom-call | flops 6920999936 | bytes 1048576 | tf_op jit(solution)/shard_map/back_terms/pallas_call | solution.py:388
  110.2 0.7 collective-permute-start.34
  111.5 10.9 %collective-permute-start.35 = (bf16[1024,128]{1,0:T(8,128)(2,1)S(1)}, bf16[1024,128]{1,0:T(8,128)(2,1)S(1)}, u32[]{:S(2)}, u32[]{:S(2)}) collective-permute-start(bf16[1024,128]{1,0:T(8,128)(2,1)S(1)} %collective-permute-done.34.refs_2_.refs_8_), channel_id=1, source_target_pairs={{0,1},{1,0},{2,3},{3,2},{4,5},{5,4},{6,7},{7,6},{8,9},{9,8},{10,11... | collective-permute-start | bytes 786440 | tf_op jit(solution)/shard_map/ppermute | solution.py:501
  122.4 5.2 %collective-permute-start.37 = (bf16[1024,128]{1,0:T(8,128)(2,1)S(1)}, bf16[1024,128]{1,0:T(8,128)(2,1)S(1)}, u32[]{:S(2)}, u32[]{:S(2)}) collective-permute-start(bf16[1024,128]{1,0:T(8,128)(2,1)S(1)} %collective-permute-done.36.refs_4_.refs_10_), channel_id=1, source_target_pairs={{0,1},{1,0},{2,3},{3,2},{4,5},{5,4},{6,7},{7,6},{8,9},{9,8},{10,11... | collective-permute-start | bytes 786440 | tf_op jit(solution)/shard_map/ppermute | solution.py:501
  128.2 5.6 %collective-permute-done.37.refs_5_.refs_11_ = bf16[1024,128]{1,0:T(8,128)(2,1)S(1)} collective-permute-done((bf16[1024,128]{1,0:T(8,128)(2,1)S(1)}, bf16[1024,128]{1,0:T(8,128)(2,1)S(1)}, u32[]{:S(2)}, u32[]{:S(2)}) %collective-permute-start.37) | collective-permute-done | bytes 262176 | tf_op jit(solution)/shard_map/ppermute | solution.py:501
  133.8 3.9 %back_terms.3 = (bf16[4096,128]{1,0:T(8,128)(2,1)S(1)}, bf16[4096,128]{1,0:T(8,128)(2,1)S(1)}) custom-call(s32[128]{0:T(128)S(1)} %copy-done.29, s32[32]{0:T(128)S(1)} %bitcast.31, s32[4]{0:T(128)S(1)} %pad_add_fusion.order, s32[1]{0:T(128)} %bitcast.middle, bf16[1024,128]{1,0:T(8,128)(2,1)S(1)} %get-tuple-element.52.refs_0_.refs_6_, ...), custom_call_target="tpu_custom_call" | custom-call | flops 6920999936 | bytes 1048576 | tf_op jit(solution)/shard_map/back_terms/pallas_call | solution.py:388
  137.7 0.8 collective-permute-start.38
  138.6 4.2 %collective-permute-start.31 = (bf16[1248,128]{1,0:T(8,128)(2,1)S(1)}, bf16[1248,128]{1,0:T(8,128)(2,1)S(1)}, u32[]{:S(2)}, u32[]{:S(2)}) collective-permute-start(bf16[1248,128]{1,0:T(8,128)(2,1)S(1)} %get-tuple-element.71), channel_id=1, source_target_pairs={{0,8},{4,12},{8,0},{12,4},{16,24},{20,28},{24,16},{28,20},{1,9},{5... | collective-permute-start | bytes 958472 | tf_op jit(solution)/shard_map/ppermute | solution.py:497
  143.0 8.3 %collective-permute-done.31 = bf16[1248,128]{1,0:T(8,128)(2,1)S(1)} collective-permute-done((bf16[1248,128]{1,0:T(8,128)(2,1)S(1)}, bf16[1248,128]{1,0:T(8,128)(2,1)S(1)}, u32[]{:S(2)}, u32[]{:S(2)}) %collective-permute-start.31) | collective-permute-done | bytes 319520 | tf_op jit(solution)/shard_map/ppermute | solution.py:497
  151.4 1.0 collective-permute-start.32
  152.6 1.1 collective-permute-start.39
  153.7 4.2 %collective-permute-done.30 = bf16[1248,128]{1,0:T(8,128)(2,1)S(1)} collective-permute-done((bf16[1248,128]{1,0:T(8,128)(2,1)S(1)}, bf16[1248,128]{1,0:T(8,128)(2,1)S(1)}, u32[]{:S(2)}, u32[]{:S(2)}) %collective-permute-start.30) | collective-permute-done | bytes 319520 | tf_op jit(solution)/shard_map/ppermute | solution.py:497
  157.9 4.0 %collective-permute-done.32 = bf16[1248,128]{1,0:T(8,128)(2,1)S(1)} collective-permute-done((bf16[1248,128]{1,0:T(8,128)(2,1)S(1)}, bf16[1248,128]{1,0:T(8,128)(2,1)S(1)}, u32[]{:S(2)}, u32[]{:S(2)}) %collective-permute-start.32) | collective-permute-done | bytes 319520 | tf_op jit(solution)/shard_map/ppermute | solution.py:497
  161.9 2.0 %collective-permute-start.42 = (bf16[224,128]{1,0:T(8,128)(2,1)S(1)}, bf16[224,128]{1,0:T(8,128)(2,1)S(1)}, u32[]{:S(2)}, u32[]{:S(2)}) collective-permute-start(bf16[224,128]{1,0:T(8,128)(2,1)S(1)} %add_convert_fusion.14), channel_id=1, source_target_pairs={{0,1},{1,0},{2,3},{3,2},{4,5},{5,4},{6,7},{7,6},{8,9},{9,8},{10,11... | collective-permute-start | bytes 172040 | tf_op jit(solution)/shard_map/ppermute | solution.py:501
  164.0 2.2 %collective-permute-done.39 = bf16[1024,128]{1,0:T(8,128)(2,1)S(1)} collective-permute-done((bf16[1024,128]{1,0:T(8,128)(2,1)S(1)}, bf16[1024,128]{1,0:T(8,128)(2,1)S(1)}, u32[]{:S(2)}, u32[]{:S(2)}) %collective-permute-start.39) | collective-permute-done | bytes 262176 | tf_op jit(solution)/shard_map/ppermute | solution.py:497
  166.4 1.6 collective-permute-start.40
  168.4 1.8 collective-permute-start.43
  170.2 8.1 %tile_grads.1 = bf16[32,4,128,128]{3,2,1,0:T(8,128)(2,1)} custom-call(s32[128]{0:T(128)S(1)} %copy-done.29, s32[32]{0:T(128)S(1)} %bitcast.32, s32[4]{0:T(128)S(1)} %pad_add_fusion.order, s32[1]{0:T(128)} %bitcast.middle, bf16[1024,128]{1,0:T(8,128)(2,1)S(1)} %get-tuple-element.48.refs_0_, bf16[1024,128]{1,0:T(8,128)(2,1)S(1)} %collective-permute-done.24.refs_1_, ...), custom_call_target="tpu_custom_call" | custom-call | flops 9228000256 | bytes 1048576 | tf_op jit(solution)/shard_map/tile_grads/pallas_call | solution.py:469
  178.4 1.2 collective-permute-start.44
  179.7 2.9 %collective-permute-done.44 = bf16[224,128]{1,0:T(8,128)(2,1)S(1)} collective-permute-done((bf16[224,128]{1,0:T(8,128)(2,1)S(1)}, bf16[224,128]{1,0:T(8,128)(2,1)S(1)}, u32[]{:S(2)}, u32[]{:S(2)}) %collective-permute-start.44) | collective-permute-done | bytes 57376 | tf_op jit(solution)/shard_map/ppermute | solution.py:497
  183.3 4.2 %collective-permute-done.45 = bf16[448,128]{1,0:T(8,128)(2,1)S(1)} collective-permute-done((bf16[448,128]{1,0:T(8,128)(2,1)S(1)}, bf16[448,128]{1,0:T(8,128)(2,1)S(1)}, u32[]{:S(2)}, u32[]{:S(2)}) %collective-permute-start.45) | collective-permute-done | bytes 114720 | tf_op jit(solution)/shard_map/ppermute | solution.py:497
  187.6 0.9 fusion
  189.1 1.0 weight_unpack.1
  (132 shorter events, 8.8 us)
Async XLA Ops:
  1.7 9.3 %collective-permute-start.3 = (bf16[1024,128]{1,0:T(8,128)(2,1)S(1)}, bf16[1024,128]{1,0:T(8,128)(2,1)S(1)}, u32[]{:S(2)}, u32[]{:S(2)}) collective-permute-start(bf16[1024,128]{1,0:T(8,128)(2,1)S(1)} %get-tuple-element.75.refs_0_.refs_12_), channel_id=1, source_target_pairs={{0,16},{4,20},{8,24},{12,28},{16,0},{20,4},{24,8},{28,12},{1,17},{... | collective-permute-start | bytes 786440 | tf_op jit(solution)/shard_map/ppermute | solution.py:497
  4.7 10.1 %collective-permute-start.1 = (bf16[1024,128]{1,0:T(8,128)(2,1)S(1)}, bf16[1024,128]{1,0:T(8,128)(2,1)S(1)}, u32[]{:S(2)}, u32[]{:S(2)}) collective-permute-start(bf16[1024,128]{1,0:T(8,128)(2,1)S(1)} %get-tuple-element.75.refs_0_.refs_12_), channel_id=1, source_target_pairs={{0,8},{4,12},{8,0},{12,4},{16,24},{20,28},{24,16},{28,20},{1,9},{5... | collective-permute-start | bytes 786440 | tf_op jit(solution)/shard_map/ppermute | solution.py:497
  11.0 7.5 %collective-permute-start.5 = (bf16[1024,128]{1,0:T(8,128)(2,1)S(1)}, bf16[1024,128]{1,0:T(8,128)(2,1)S(1)}, u32[]{:S(2)}, u32[]{:S(2)}) collective-permute-start(bf16[1024,128]{1,0:T(8,128)(2,1)S(1)} %collective-permute-done.3.refs_4_.refs_16_), channel_id=1, source_target_pairs={{0,8},{4,12},{8,0},{12,4},{16,24},{20,28},{24,16},{28,20},{1,9},{5... | collective-permute-start | bytes 786440 | tf_op jit(solution)/shard_map/ppermute | solution.py:497
  12.8 7.2 %collective-permute-start.15 = (bf16[1024,128]{1,0:T(8,128)(2,1)S(1)}, bf16[1024,128]{1,0:T(8,128)(2,1)S(1)}, u32[]{:S(2)}, u32[]{:S(2)}) collective-permute-start(bf16[1024,128]{1,0:T(8,128)(2,1)S(1)} %get-tuple-element.36.refs_0_.refs_20_), channel_id=1, source_target_pairs={{0,16},{4,20},{8,24},{12,28},{16,0},{20,4},{24,8},{28,12},{1,17},{... | collective-permute-start | bytes 786440 | tf_op jit(solution)/shard_map/ppermute | solution.py:497
  14.3 6.6 %collective-permute-start = (bf16[1024,128]{1,0:T(8,128)(2,1)S(1)}, bf16[1024,128]{1,0:T(8,128)(2,1)S(1)}, u32[]{:S(2)}, u32[]{:S(2)}) collective-permute-start(bf16[1024,128]{1,0:T(8,128)(2,1)S(1)} %get-tuple-element.75.refs_0_.refs_12_), channel_id=1, source_target_pairs={{0,4},{4,0},{8,12},{12,8},{16,20},{20,16},{24,28},{28,24},{1,5},{5... | collective-permute-start | bytes 786440 | tf_op jit(solution)/shard_map/ppermute | solution.py:497
  14.3 7.2 %collective-permute-start.4 = (bf16[1024,128]{1,0:T(8,128)(2,1)S(1)}, bf16[1024,128]{1,0:T(8,128)(2,1)S(1)}, u32[]{:S(2)}, u32[]{:S(2)}) collective-permute-start(bf16[1024,128]{1,0:T(8,128)(2,1)S(1)} %collective-permute-done.3.refs_4_.refs_16_), channel_id=1, source_target_pairs={{0,4},{4,0},{8,12},{12,8},{16,20},{20,16},{24,28},{28,24},{1,5},{5... | collective-permute-start | bytes 786440 | tf_op jit(solution)/shard_map/ppermute | solution.py:497
  14.8 11.5 %collective-permute-start.2 = (bf16[1024,128]{1,0:T(8,128)(2,1)S(1)}, bf16[1024,128]{1,0:T(8,128)(2,1)S(1)}, u32[]{:S(2)}, u32[]{:S(2)}) collective-permute-start(bf16[1024,128]{1,0:T(8,128)(2,1)S(1)} %collective-permute-done.1.refs_2_.refs_14_), channel_id=1, source_target_pairs={{0,4},{4,0},{8,12},{12,8},{16,20},{20,16},{24,28},{28,24},{1,5},{5... | collective-permute-start | bytes 786440 | tf_op jit(solution)/shard_map/ppermute | solution.py:497
  18.5 6.6 %collective-permute-start.13 = (bf16[1024,128]{1,0:T(8,128)(2,1)S(1)}, bf16[1024,128]{1,0:T(8,128)(2,1)S(1)}, u32[]{:S(2)}, u32[]{:S(2)}) collective-permute-start(bf16[1024,128]{1,0:T(8,128)(2,1)S(1)} %get-tuple-element.36.refs_0_.refs_20_), channel_id=1, source_target_pairs={{0,8},{4,12},{8,0},{12,4},{16,24},{20,28},{24,16},{28,20},{1,9},{5... | collective-permute-start | bytes 786440 | tf_op jit(solution)/shard_map/ppermute | solution.py:497
  19.9 6.4 %collective-permute-start.6 = (bf16[1024,128]{1,0:T(8,128)(2,1)S(1)}, bf16[1024,128]{1,0:T(8,128)(2,1)S(1)}, u32[]{:S(2)}, u32[]{:S(2)}) collective-permute-start(bf16[1024,128]{1,0:T(8,128)(2,1)S(1)} %collective-permute-done.5.refs_6_.refs_18_), channel_id=1, source_target_pairs={{0,4},{4,0},{8,12},{12,8},{16,20},{20,16},{24,28},{28,24},{1,5},{5... | collective-permute-start | bytes 786440 | tf_op jit(solution)/shard_map/ppermute | solution.py:497
  20.9 34.5 %copy-start.28 = (s32[128]{0:T(128)}, s32[128]{0:T(128)S(1)}, u32[]{:S(2)}) copy-start(s32[128]{0:T(128)S(1)} %fusion.1.cols) | copy-start | bytes 1540
  20.9 19.2 %collective-permute-start.12 = (bf16[1024,128]{1,0:T(8,128)(2,1)S(1)}, bf16[1024,128]{1,0:T(8,128)(2,1)S(1)}, u32[]{:S(2)}, u32[]{:S(2)}) collective-permute-start(bf16[1024,128]{1,0:T(8,128)(2,1)S(1)} %get-tuple-element.36.refs_0_.refs_20_), channel_id=1, source_target_pairs={{0,4},{4,0},{8,12},{12,8},{16,20},{20,16},{24,28},{28,24},{1,5},{5... | collective-permute-start | bytes 786440 | tf_op jit(solution)/shard_map/ppermute | solution.py:497
  21.5 19.3 %collective-permute-start.16 = (bf16[1024,128]{1,0:T(8,128)(2,1)S(1)}, bf16[1024,128]{1,0:T(8,128)(2,1)S(1)}, u32[]{:S(2)}, u32[]{:S(2)}) collective-permute-start(bf16[1024,128]{1,0:T(8,128)(2,1)S(1)} %collective-permute-done.15.refs_4_.refs_24_), channel_id=1, source_target_pairs={{0,4},{4,0},{8,12},{12,8},{16,20},{20,16},{24,28},{28,24},{1,5},{5... | collective-permute-start | bytes 786440 | tf_op jit(solution)/shard_map/ppermute | solution.py:497
  25.1 30.3 %copy-start.8 = (bf16[1024,128]{1,0:T(8,128)(2,1)}, bf16[1024,128]{1,0:T(8,128)(2,1)S(1)}, u32[]{:S(2)}) copy-start(bf16[1024,128]{1,0:T(8,128)(2,1)S(1)} %collective-permute-done.13.refs_2_.refs_22_) | copy-start | bytes 786436
  25.1 8.1 %collective-permute-start.17 = (bf16[1024,128]{1,0:T(8,128)(2,1)S(1)}, bf16[1024,128]{1,0:T(8,128)(2,1)S(1)}, u32[]{:S(2)}, u32[]{:S(2)}) collective-permute-start(bf16[1024,128]{1,0:T(8,128)(2,1)S(1)} %collective-permute-done.13.refs_2_.refs_22_), channel_id=1, source_target_pairs={{0,16},{4,20},{8,24},{12,28},{16,0},{20,4},{24,8},{28,12},{1,17},{... | collective-permute-start | bytes 786440 | tf_op jit(solution)/shard_map/ppermute | solution.py:497
  31.5 6.4 %collective-permute-start.7 = (bf16[1024,128]{1,0:T(8,128)(2,1)S(1)}, bf16[1024,128]{1,0:T(8,128)(2,1)S(1)}, u32[]{:S(2)}, u32[]{:S(2)}) collective-permute-start(bf16[1024,128]{1,0:T(8,128)(2,1)S(1)} %get-tuple-element.34), channel_id=1, source_target_pairs={{0,1},{1,0},{2,3},{3,2},{4,5},{5,4},{6,7},{7,6},{8,9},{9,8},{10,11... | collective-permute-start | bytes 786440 | tf_op jit(solution)/shard_map/ppermute | solution.py:501
  33.2 7.6 %collective-permute-start.14 = (bf16[1024,128]{1,0:T(8,128)(2,1)S(1)}, bf16[1024,128]{1,0:T(8,128)(2,1)S(1)}, u32[]{:S(2)}, u32[]{:S(2)}) collective-permute-start(bf16[1024,128]{1,0:T(8,128)(2,1)S(1)} %collective-permute-done.13.refs_2_.refs_22_), channel_id=1, source_target_pairs={{0,4},{4,0},{8,12},{12,8},{16,20},{20,16},{24,28},{28,24},{1,5},{5... | collective-permute-start | bytes 786440 | tf_op jit(solution)/shard_map/ppermute | solution.py:497
  33.2 22.3 %copy-start.16 = (bf16[1024,128]{1,0:T(8,128)(2,1)}, bf16[1024,128]{1,0:T(8,128)(2,1)S(1)}, u32[]{:S(2)}) copy-start(bf16[1024,128]{1,0:T(8,128)(2,1)S(1)} %collective-permute-done.17.refs_6_.refs_26_) | copy-start | bytes 786436
  33.2 7.6 %collective-permute-start.18 = (bf16[1024,128]{1,0:T(8,128)(2,1)S(1)}, bf16[1024,128]{1,0:T(8,128)(2,1)S(1)}, u32[]{:S(2)}, u32[]{:S(2)}) collective-permute-start(bf16[1024,128]{1,0:T(8,128)(2,1)S(1)} %collective-permute-done.17.refs_6_.refs_26_), channel_id=1, source_target_pairs={{0,4},{4,0},{8,12},{12,8},{16,20},{20,16},{24,28},{28,24},{1,5},{5... | collective-permute-start | bytes 786440 | tf_op jit(solution)/shard_map/ppermute | solution.py:497
  38.0 9.5 %collective-permute-start.10 = (bf16[1024,128]{1,0:T(8,128)(2,1)S(1)}, bf16[1024,128]{1,0:T(8,128)(2,1)S(1)}, u32[]{:S(2)}, u32[]{:S(2)}) collective-permute-start(bf16[1024,128]{1,0:T(8,128)(2,1)S(1)} %get-tuple-element.35), channel_id=1, source_target_pairs={{0,1},{1,0},{2,3},{3,2},{4,5},{5,4},{6,7},{7,6},{8,9},{9,8},{10,11... | collective-permute-start | bytes 786440 | tf_op jit(solution)/shard_map/ppermute | solution.py:501
  40.1 11.8 %collective-permute-start.8 = (bf16[1024,128]{1,0:T(8,128)(2,1)S(1)}, bf16[1024,128]{1,0:T(8,128)(2,1)S(1)}, u32[]{:S(2)}, u32[]{:S(2)}) collective-permute-start(bf16[1024,128]{1,0:T(8,128)(2,1)S(1)} %add_convert_fusion.11), channel_id=1, source_target_pairs={{0,0},{1,2},{2,1},{3,3},{4,4},{5,6},{6,5},{7,7},{8,8},{9,10},{10,9... | collective-permute-start | bytes 786440 | tf_op jit(solution)/shard_map/ppermute | solution.py:509
  43.0 11.6 %collective-permute-start.19 = (bf16[1024,128]{1,0:T(8,128)(2,1)S(1)}, bf16[1024,128]{1,0:T(8,128)(2,1)S(1)}, u32[]{:S(2)}, u32[]{:S(2)}) collective-permute-start(bf16[1024,128]{1,0:T(8,128)(2,1)S(1)} %get-tuple-element.39), channel_id=1, source_target_pairs={{0,1},{1,0},{2,3},{3,2},{4,5},{5,4},{6,7},{7,6},{8,9},{9,8},{10,11... | collective-permute-start | bytes 786440 | tf_op jit(solution)/shard_map/ppermute | solution.py:501
  48.3 20.3 %collective-permute-start.11 = (bf16[1024,128]{1,0:T(8,128)(2,1)}, bf16[1024,128]{1,0:T(8,128)(2,1)}, u32[]{:S(2)}, u32[]{:S(2)}) collective-permute-start(bf16[1024,128]{1,0:T(8,128)(2,1)} %add_convert_fusion.9), channel_id=1, source_target_pairs={{0,0},{1,2},{2,1},{3,3},{4,4},{5,6},{6,5},{7,7},{8,8},{9,10},{10,9... | collective-permute-start | bytes 786440 | tf_op jit(solution)/shard_map/ppermute | solution.py:509
  52.6 15.9 %collective-permute-start.9 = (bf16[1024,128]{1,0:T(8,128)(2,1)}, bf16[1024,128]{1,0:T(8,128)(2,1)}, u32[]{:S(2)}, u32[]{:S(2)}) collective-permute-start(bf16[1024,128]{1,0:T(8,128)(2,1)} %add_convert_fusion.10), channel_id=1, source_target_pairs={{0,1},{1,0},{2,3},{3,2},{4,5},{5,4},{6,7},{7,6},{8,9},{9,8},{10,11... | collective-permute-start | bytes 786440 | tf_op jit(solution)/shard_map/ppermute | solution.py:501
  53.3 9.7 %collective-permute-start.22 = (bf16[1024,128]{1,0:T(8,128)(2,1)S(1)}, bf16[1024,128]{1,0:T(8,128)(2,1)S(1)}, u32[]{:S(2)}, u32[]{:S(2)}) collective-permute-start(bf16[1024,128]{1,0:T(8,128)(2,1)S(1)} %get-tuple-element.40), channel_id=1, source_target_pairs={{0,1},{1,0},{2,3},{3,2},{4,5},{5,4},{6,7},{7,6},{8,9},{9,8},{10,11... | collective-permute-start | bytes 786440 | tf_op jit(solution)/shard_map/ppermute | solution.py:501
  54.8 12.7 %collective-permute-start.20 = (bf16[1024,128]{1,0:T(8,128)(2,1)S(1)}, bf16[1024,128]{1,0:T(8,128)(2,1)S(1)}, u32[]{:S(2)}, u32[]{:S(2)}) collective-permute-start(bf16[1024,128]{1,0:T(8,128)(2,1)S(1)} %add_convert_fusion.8), channel_id=1, source_target_pairs={{0,0},{1,2},{2,1},{3,3},{4,4},{5,6},{6,5},{7,7},{8,8},{9,10},{10,9... | collective-permute-start | bytes 786440 | tf_op jit(solution)/shard_map/ppermute | solution.py:509
  57.7 17.2 %copy-start = (bf16[1024,256]{1,0:T(8,128)(2,1)S(1)}, bf16[1024,256]{1,0:T(8,128)(2,1)}, u32[]{:S(2)}) copy-start(bf16[1024,256]{1,0:T(8,128)(2,1)} %nodes.3) | copy-start | bytes 1572868
  57.7 17.2 %copy-start.4 = (bf16[1024,256]{1,0:T(8,128)(2,1)S(1)}, bf16[1024,256]{1,0:T(8,128)(2,1)}, u32[]{:S(2)}) copy-start(bf16[1024,256]{1,0:T(8,128)(2,1)} %cot.3) | copy-start | bytes 1572868
  57.7 17.2 %copy-start.5 = (bf16[512,256]{1,0:T(8,128)(2,1)S(1)}, bf16[512,256]{1,0:T(8,128)(2,1)}, u32[]{:S(2)}) copy-start(bf16[512,256]{1,0:T(8,128)(2,1)} %w_in.1) | copy-start | bytes 786436
  57.7 17.2 %copy-start.22 = (bf16[256,256]{1,0:T(8,128)(2,1)S(1)}, bf16[256,256]{1,0:T(8,128)(2,1)}, u32[]{:S(2)}) copy-start(bf16[256,256]{1,0:T(8,128)(2,1)} %refs_8_.1) | copy-start | bytes 393220
  57.7 17.2 %copy-start.23 = (f32[256]{0:T(256)S(1)}, f32[256]{0:T(256)}, u32[]{:S(2)}) copy-start(f32[256]{0:T(256)} %param.15) | copy-start | bytes 3076
  57.7 17.2 %copy-start.24 = (f32[256]{0:T(256)S(1)}, f32[256]{0:T(256)}, u32[]{:S(2)}) copy-start(f32[256]{0:T(256)} %param.17) | copy-start | bytes 3076
  63.8 4.8 %collective-permute-start.23 = (bf16[1024,128]{1,0:T(8,128)(2,1)}, bf16[1024,128]{1,0:T(8,128)(2,1)}, u32[]{:S(2)}, u32[]{:S(2)}) collective-permute-start(bf16[1024,128]{1,0:T(8,128)(2,1)} %add_convert_fusion.6), channel_id=1, source_target_pairs={{0,0},{1,2},{2,1},{3,3},{4,4},{5,6},{6,5},{7,7},{8,8},{9,10},{10,9... | collective-permute-start | bytes 786440 | tf_op jit(solution)/shard_map/ppermute | solution.py:509
  68.2 6.7 %collective-permute-start.21 = (bf16[1024,128]{1,0:T(8,128)(2,1)}, bf16[1024,128]{1,0:T(8,128)(2,1)}, u32[]{:S(2)}, u32[]{:S(2)}) collective-permute-start(bf16[1024,128]{1,0:T(8,128)(2,1)} %add_convert_fusion.7), channel_id=1, source_target_pairs={{0,1},{1,0},{2,3},{3,2},{4,5},{5,4},{6,7},{7,6},{8,9},{9,8},{10,11... | collective-permute-start | bytes 786440 | tf_op jit(solution)/shard_map/ppermute | solution.py:501
  82.5 6.8 %collective-permute-start.24 = (bf16[1024,128]{1,0:T(8,128)(2,1)S(1)}, bf16[1024,128]{1,0:T(8,128)(2,1)S(1)}, u32[]{:S(2)}, u32[]{:S(2)}) collective-permute-start(bf16[1024,128]{1,0:T(8,128)(2,1)S(1)} %get-tuple-element.48.refs_0_), channel_id=1, source_target_pairs={{0,1},{1,0},{2,3},{3,2},{4,5},{5,4},{6,7},{7,6},{8,9},{9,8},{10,11... | collective-permute-start | bytes 786440 | tf_op jit(solution)/shard_map/ppermute | solution.py:501
  82.9 11.3 %collective-permute-start.25 = (bf16[1024,128]{1,0:T(8,128)(2,1)S(1)}, bf16[1024,128]{1,0:T(8,128)(2,1)S(1)}, u32[]{:S(2)}, u32[]{:S(2)}) collective-permute-start(bf16[1024,128]{1,0:T(8,128)(2,1)S(1)} %get-tuple-element.48.refs_0_), channel_id=1, source_target_pairs={{0,0},{1,2},{2,1},{3,3},{4,4},{5,6},{6,5},{7,7},{8,8},{9,10},{10,9... | collective-permute-start | bytes 786440 | tf_op jit(solution)/shard_map/ppermute | solution.py:509
  89.3 5.0 %collective-permute-start.27 = (bf16[1024,128]{1,0:T(8,128)(2,1)S(1)}, bf16[1024,128]{1,0:T(8,128)(2,1)S(1)}, u32[]{:S(2)}, u32[]{:S(2)}) collective-permute-start(bf16[1024,128]{1,0:T(8,128)(2,1)S(1)} %collective-permute-done.24.refs_1_), channel_id=1, source_target_pairs={{0,0},{1,2},{2,1},{3,3},{4,4},{5,6},{6,5},{7,7},{8,8},{9,10},{10,9... | collective-permute-start | bytes 786440 | tf_op jit(solution)/shard_map/ppermute | solution.py:509
  90.0 20.9 %collective-permute-start.33 = (bf16[1024,128]{1,0:T(8,128)(2,1)S(1)}, bf16[1024,128]{1,0:T(8,128)(2,1)S(1)}, u32[]{:S(2)}, u32[]{:S(2)}) collective-permute-start(bf16[1024,128]{1,0:T(8,128)(2,1)S(1)} %get-tuple-element.52.refs_0_.refs_6_), channel_id=1, source_target_pairs={{0,1},{1,0},{2,3},{3,2},{4,5},{5,4},{6,7},{7,6},{8,9},{9,8},{10,11... | collective-permute-start | bytes 786440 | tf_op jit(solution)/shard_map/ppermute | solution.py:501
  94.2 8.8 %collective-permute-start.26 = (bf16[1024,128]{1,0:T(8,128)(2,1)S(1)}, bf16[1024,128]{1,0:T(8,128)(2,1)S(1)}, u32[]{:S(2)}, u32[]{:S(2)}) collective-permute-start(bf16[1024,128]{1,0:T(8,128)(2,1)S(1)} %collective-permute-done.25.refs_2_), channel_id=1, source_target_pairs={{0,1},{1,0},{2,3},{3,2},{4,5},{5,4},{6,7},{7,6},{8,9},{9,8},{10,11... | collective-permute-start | bytes 786440 | tf_op jit(solution)/shard_map/ppermute | solution.py:501
  94.3 11.5 %collective-permute-start.28 = (bf16[1024,128]{1,0:T(8,128)(2,1)S(1)}, bf16[1024,128]{1,0:T(8,128)(2,1)S(1)}, u32[]{:S(2)}, u32[]{:S(2)}) collective-permute-start(bf16[1024,128]{1,0:T(8,128)(2,1)S(1)} %collective-permute-done.27.refs_4_), channel_id=1, source_target_pairs={{0,1},{1,0},{2,3},{3,2},{4,5},{5,4},{6,7},{7,6},{8,9},{9,8},{10,11... | collective-permute-start | bytes 786440 | tf_op jit(solution)/shard_map/ppermute | solution.py:501
  110.1 28.4 %collective-permute-start.29 = (bf16[4992,128]{1,0:T(8,128)(2,1)S(1)}, bf16[4992,128]{1,0:T(8,128)(2,1)S(1)}, u32[]{:S(2)}, u32[]{:S(2)}) collective-permute-start(bf16[4992,128]{1,0:T(8,128)(2,1)S(1)} %get-tuple-element.51), channel_id=1, source_target_pairs={{0,4},{4,0},{8,12},{12,8},{16,20},{20,16},{24,28},{28,24},{1,5},{5... | collective-permute-start | bytes 3833864 | tf_op jit(solution)/shard_map/ppermute | solution.py:497
  110.2 1.4 collective-permute-start.34
  110.8 11.6 %collective-permute-start.36 = (bf16[1024,128]{1,0:T(8,128)(2,1)S(1)}, bf16[1024,128]{1,0:T(8,128)(2,1)S(1)}, u32[]{:S(2)}, u32[]{:S(2)}) collective-permute-start(bf16[1024,128]{1,0:T(8,128)(2,1)S(1)} %collective-permute-done.33.refs_1_.refs_7_), channel_id=1, source_target_pairs={{0,0},{1,2},{2,1},{3,3},{4,4},{5,6},{6,5},{7,7},{8,8},{9,10},{10,9... | collective-permute-start | bytes 786440 | tf_op jit(solution)/shard_map/ppermute | solution.py:509
  111.5 16.6 %collective-permute-start.35 = (bf16[1024,128]{1,0:T(8,128)(2,1)S(1)}, bf16[1024,128]{1,0:T(8,128)(2,1)S(1)}, u32[]{:S(2)}, u32[]{:S(2)}) collective-permute-start(bf16[1024,128]{1,0:T(8,128)(2,1)S(1)} %collective-permute-done.34.refs_2_.refs_8_), channel_id=1, source_target_pairs={{0,1},{1,0},{2,3},{3,2},{4,5},{5,4},{6,7},{7,6},{8,9},{9,8},{10,11... | collective-permute-start | bytes 786440 | tf_op jit(solution)/shard_map/ppermute | solution.py:501
  122.4 11.4 %collective-permute-start.37 = (bf16[1024,128]{1,0:T(8,128)(2,1)S(1)}, bf16[1024,128]{1,0:T(8,128)(2,1)S(1)}, u32[]{:S(2)}, u32[]{:S(2)}) collective-permute-start(bf16[1024,128]{1,0:T(8,128)(2,1)S(1)} %collective-permute-done.36.refs_4_.refs_10_), channel_id=1, source_target_pairs={{0,1},{1,0},{2,3},{3,2},{4,5},{5,4},{6,7},{7,6},{8,9},{9,8},{10,11... | collective-permute-start | bytes 786440 | tf_op jit(solution)/shard_map/ppermute | solution.py:501
  137.7 14.7 %collective-permute-start.38 = (bf16[4096,128]{1,0:T(8,128)(2,1)S(1)}, bf16[4096,128]{1,0:T(8,128)(2,1)S(1)}, u32[]{:S(2)}, u32[]{:S(2)}) collective-permute-start(bf16[4096,128]{1,0:T(8,128)(2,1)S(1)} %get-tuple-element.54.refs_28_), channel_id=1, source_target_pairs={{0,4},{4,0},{8,12},{12,8},{16,20},{20,16},{24,28},{28,24},{1,5},{5... | collective-permute-start | bytes 3145736 | tf_op jit(solution)/shard_map/ppermute | solution.py:497
  138.6 12.6 %collective-permute-start.31 = (bf16[1248,128]{1,0:T(8,128)(2,1)S(1)}, bf16[1248,128]{1,0:T(8,128)(2,1)S(1)}, u32[]{:S(2)}, u32[]{:S(2)}) collective-permute-start(bf16[1248,128]{1,0:T(8,128)(2,1)S(1)} %get-tuple-element.71), channel_id=1, source_target_pairs={{0,8},{4,12},{8,0},{12,4},{16,24},{20,28},{24,16},{28,20},{1,9},{5... | collective-permute-start | bytes 958472 | tf_op jit(solution)/shard_map/ppermute | solution.py:497
  142.9 15.0 %collective-permute-start.30 = (bf16[1248,128]{1,0:T(8,128)(2,1)S(1)}, bf16[1248,128]{1,0:T(8,128)(2,1)S(1)}, u32[]{:S(2)}, u32[]{:S(2)}) collective-permute-start(bf16[1248,128]{1,0:T(8,128)(2,1)S(1)} %get-tuple-element.70), channel_id=1, source_target_pairs={{0,8},{4,12},{8,0},{12,4},{16,24},{20,28},{24,16},{28,20},{1,9},{5... | collective-permute-start | bytes 958472 | tf_op jit(solution)/shard_map/ppermute | solution.py:497
  151.4 10.5 %collective-permute-start.32 = (bf16[1248,128]{1,0:T(8,128)(2,1)S(1)}, bf16[1248,128]{1,0:T(8,128)(2,1)S(1)}, u32[]{:S(2)}, u32[]{:S(2)}) collective-permute-start(bf16[1248,128]{1,0:T(8,128)(2,1)S(1)} %add_convert_fusion), channel_id=1, source_target_pairs={{0,16},{4,20},{8,24},{12,28},{16,0},{20,4},{24,8},{28,12},{1,17},{... | collective-permute-start | bytes 958472 | tf_op jit(solution)/shard_map/ppermute | solution.py:497
  152.5 17.7 %copy-start.7 = (bf16[1024,128]{1,0:T(8,128)(2,1)S(1)}, bf16[1024,128]{1,0:T(8,128)(2,1)}, u32[]{:S(2)}) copy-start(bf16[1024,128]{1,0:T(8,128)(2,1)} %copy-done.6) | copy-start | bytes 786436
  152.5 17.7 %copy-start.9 = (bf16[1024,128]{1,0:T(8,128)(2,1)S(1)}, bf16[1024,128]{1,0:T(8,128)(2,1)}, u32[]{:S(2)}) copy-start(bf16[1024,128]{1,0:T(8,128)(2,1)} %copy-done.8) | copy-start | bytes 786436
  152.5 17.7 %copy-start.11 = (bf16[1024,128]{1,0:T(8,128)(2,1)S(1)}, bf16[1024,128]{1,0:T(8,128)(2,1)}, u32[]{:S(2)}) copy-start(bf16[1024,128]{1,0:T(8,128)(2,1)} %copy-done.10) | copy-start | bytes 786436
  152.5 17.7 %copy-start.13 = (bf16[1024,128]{1,0:T(8,128)(2,1)S(1)}, bf16[1024,128]{1,0:T(8,128)(2,1)}, u32[]{:S(2)}) copy-start(bf16[1024,128]{1,0:T(8,128)(2,1)} %copy-done.12) | copy-start | bytes 786436
  152.5 17.7 %copy-start.15 = (bf16[1024,128]{1,0:T(8,128)(2,1)S(1)}, bf16[1024,128]{1,0:T(8,128)(2,1)}, u32[]{:S(2)}) copy-start(bf16[1024,128]{1,0:T(8,128)(2,1)} %copy-done.14) | copy-start | bytes 786436
  152.5 17.7 %copy-start.17 = (bf16[1024,128]{1,0:T(8,128)(2,1)S(1)}, bf16[1024,128]{1,0:T(8,128)(2,1)}, u32[]{:S(2)}) copy-start(bf16[1024,128]{1,0:T(8,128)(2,1)} %copy-done.16) | copy-start | bytes 786436
  152.5 17.7 %copy-start.19 = (bf16[1024,128]{1,0:T(8,128)(2,1)S(1)}, bf16[1024,128]{1,0:T(8,128)(2,1)}, u32[]{:S(2)}) copy-start(bf16[1024,128]{1,0:T(8,128)(2,1)} %copy-done.18) | copy-start | bytes 786436
  152.6 17.7 %copy-start.21 = (bf16[1024,128]{1,0:T(8,128)(2,1)S(1)}, bf16[1024,128]{1,0:T(8,128)(2,1)}, u32[]{:S(2)}) copy-start(bf16[1024,128]{1,0:T(8,128)(2,1)} %copy-done.20) | copy-start | bytes 786436
  152.6 13.7 %collective-permute-start.39 = (bf16[1024,128]{1,0:T(8,128)(2,1)S(1)}, bf16[1024,128]{1,0:T(8,128)(2,1)S(1)}, u32[]{:S(2)}, u32[]{:S(2)}) collective-permute-start(bf16[1024,128]{1,0:T(8,128)(2,1)S(1)} %add_convert_fusion.5), channel_id=1, source_target_pairs={{0,16},{4,20},{8,24},{12,28},{16,0},{20,4},{24,8},{28,12},{1,17},{... | collective-permute-start | bytes 786440 | tf_op jit(solution)/shard_map/ppermute | solution.py:497
  161.9 6.4 %collective-permute-start.42 = (bf16[224,128]{1,0:T(8,128)(2,1)S(1)}, bf16[224,128]{1,0:T(8,128)(2,1)S(1)}, u32[]{:S(2)}, u32[]{:S(2)}) collective-permute-start(bf16[224,128]{1,0:T(8,128)(2,1)S(1)} %add_convert_fusion.14), channel_id=1, source_target_pairs={{0,1},{1,0},{2,3},{3,2},{4,5},{5,4},{6,7},{7,6},{8,9},{9,8},{10,11... | collective-permute-start | bytes 172040 | tf_op jit(solution)/shard_map/ppermute | solution.py:501
  166.4 13.2 %collective-permute-start.40 = (bf16[1024,128]{1,0:T(8,128)(2,1)S(1)}, bf16[1024,128]{1,0:T(8,128)(2,1)S(1)}, u32[]{:S(2)}, u32[]{:S(2)}) collective-permute-start(bf16[1024,128]{1,0:T(8,128)(2,1)S(1)} %get-tuple-element.72), channel_id=1, source_target_pairs={{0,8},{4,12},{8,0},{12,4},{16,24},{20,28},{24,16},{28,20},{1,9},{5... | collective-permute-start | bytes 786440 | tf_op jit(solution)/shard_map/ppermute | solution.py:497
  168.0 11.6 %collective-permute-start.41 = (bf16[1024,128]{1,0:T(8,128)(2,1)S(1)}, bf16[1024,128]{1,0:T(8,128)(2,1)S(1)}, u32[]{:S(2)}, u32[]{:S(2)}) collective-permute-start(bf16[1024,128]{1,0:T(8,128)(2,1)S(1)} %get-tuple-element.73), channel_id=1, source_target_pairs={{0,16},{4,20},{8,24},{12,28},{16,0},{20,4},{24,8},{28,12},{1,17},{... | collective-permute-start | bytes 786440 | tf_op jit(solution)/shard_map/ppermute | solution.py:497
  168.4 10.0 %collective-permute-start.43 = (bf16[224,128]{1,0:T(8,128)(2,1)S(1)}, bf16[224,128]{1,0:T(8,128)(2,1)S(1)}, u32[]{:S(2)}, u32[]{:S(2)}) collective-permute-start(bf16[224,128]{1,0:T(8,128)(2,1)S(1)} %add_convert_fusion.13), channel_id=1, source_target_pairs={{0,3},{3,0},{1,2},{2,1},{4,7},{7,4},{5,6},{6,5},{8,11},{11,8},{9,1... | collective-permute-start | bytes 172040 | tf_op jit(solution)/shard_map/ppermute | solution.py:505
  178.4 4.2 %collective-permute-start.44 = (bf16[224,128]{1,0:T(8,128)(2,1)S(1)}, bf16[224,128]{1,0:T(8,128)(2,1)S(1)}, u32[]{:S(2)}, u32[]{:S(2)}) collective-permute-start(bf16[224,128]{1,0:T(8,128)(2,1)S(1)} %add_convert_fusion.12), channel_id=1, source_target_pairs={{0,16},{4,20},{8,24},{12,28},{16,0},{20,4},{24,8},{28,12},{1,17},{... | collective-permute-start | bytes 172040 | tf_op jit(solution)/shard_map/ppermute | solution.py:497
  182.6 4.9 %collective-permute-start.45 = (bf16[448,128]{1,0:T(8,128)(2,1)S(1)}, bf16[448,128]{1,0:T(8,128)(2,1)S(1)}, u32[]{:S(2)}, u32[]{:S(2)}) collective-permute-start(bf16[448,128]{1,0:T(8,128)(2,1)S(1)} %pad_maximum_fusion.2), channel_id=1, source_target_pairs={{0,8},{4,12},{8,0},{12,4},{16,24},{20,28},{24,16},{28,20},{1,9},{5... | collective-permute-start | bytes 344072 | tf_op jit(solution)/shard_map/ppermute | solution.py:497
  187.5 1.6 collective-permute-start.46
  (17 other events, 143.0 us)

commit v4 on v3

v4 whole, which is shorter than its diff:
```python
import functools

import jax
import jax.numpy as jnp
from jax import lax
from jax.experimental import pallas as pl
from jax.experimental.pallas import tpu as pltpu
from jax.sharding import PartitionSpec as P

F32 = jnp.float32
BF16 = jnp.bfloat16
ANY = pl.BlockSpec(memory_space=pl.ANY)
SMEM = pl.BlockSpec(memory_space=pltpu.SMEM)
VMEM = pl.BlockSpec(memory_space=pltpu.VMEM)
MIB = 1 << 20
TN = (((0,), (0,)), ((), ()))
NT = (((1,), (1,)), ((), ()))
PEAK_FLOPS_PER_US = 1153.5e6


LIVE_STEP = 4
GRAD_PLAN = ((3, 0, None), (2, 1, None), (1, 2, "inner"), (1, 3, "outer"), (0, 4, "inner"), (0, 5, "outer"))
SWAP_ORDER = (0, 4, 2, 6, 1, 5, 3, 7)


def params(mib):
    return pltpu.CompilerParams(vmem_limit_bytes=mib * MIB)


def cost(microseconds):
    return pl.CostEstimate(flops=int(microseconds * PEAK_FLOPS_PER_US), bytes_accessed=MIB, transcendentals=0)


def mm(a, b, dims=(((1,), (0,)), ((), ()))):
    return lax.dot_general(a, b, dims, preferred_element_type=F32)


def block_at(index, block):
    return pl.ds(pl.multiple_of(index * block, block), block)


def load_pieces(pieces, dst, sem, first):
    copies = []
    offset = 0
    for index, piece in enumerate(pieces):
        copy = pltpu.make_async_copy(
            piece, dst.at[pl.ds(offset, piece.shape[0])], sem.at[first + index]
        )
        copy.start()
        copies.append(copy)
        offset += piece.shape[0]
    return copies


def forward_kernel(outputs, n_pieces, cols, order, *refs):
    pieces, tiles = refs[:n_pieces], refs[n_pieces]
    outs = refs[n_pieces + 1 : n_pieces + 1 + len(outputs)]
    nodes_v, tiles_v, sem, tile_sem = refs[n_pieces + 1 + len(outputs) :]
    rows = outs[0].shape[0] // len(outputs[0])
    slots, block = tiles.shape[1], tiles.shape[2]
    blocks = rows // block
    copies = load_pieces(pieces, nodes_v, sem, 0)
    places = [(pick, out, index) for out, picks in zip(outs, outputs) for index, pick in enumerate(picks)]
    tile_copies = []
    for place, (pick, _, _) in enumerate(places):
        copy = pltpu.make_async_copy(
            tiles.at[pl.ds(order[pick] * blocks, blocks)],
            tiles_v.at[pl.ds(place * blocks, blocks)],
            tile_sem.at[place],
        )
        copy.start()
        tile_copies.append(copy)
    for copy in copies:
        copy.wait()
    for place, (pick, out, index) in enumerate(places):
        tile_copies[place].wait()
        first = order[pick] * blocks

        def step(i, carry, first=first, out=out, index=index, place=place):
            row = first + i
            parts = []
            for pair in range(slots // 2):
                both = (2 * pair, 2 * pair + 1)
                tile = jnp.concatenate([tiles_v[place * blocks + i, slot] for slot in both], axis=1)
                node = jnp.concatenate(
                    [nodes_v[block_at(cols[row * slots + slot], block)] for slot in both], axis=0
                )
                parts.append(mm(tile, node))
            value = parts[0]
            for part in parts[1:]:
                value = value + part
            out[block_at(index * blocks + i, block)] = value.astype(BF16)
            return carry

        lax.fori_loop(0, blocks, step, 0, unroll=4)


def forward_call(cols, order, pieces, tiles, outputs, rows):
    width = pieces[0].shape[1]
    gathered = sum(piece.shape[0] for piece in pieces)
    slots, block = tiles.shape[1], tiles.shape[2]
    n_picks = sum(len(picks) for picks in outputs)
    return pl.pallas_call(
        functools.partial(forward_kernel, outputs, len(pieces)),
        out_shape=[jax.ShapeDtypeStruct((len(picks) * rows, width), BF16) for picks in outputs],
        in_specs=[SMEM, SMEM] + [ANY] * (len(pieces) + 1),
        out_specs=[VMEM] * len(outputs),
        scratch_shapes=[
            pltpu.VMEM((gathered, width), BF16),
            pltpu.VMEM((n_picks * (rows // block),) + tiles.shape[1:], BF16),
            pltpu.SemaphoreType.DMA((len(pieces),)),
            pltpu.SemaphoreType.DMA((n_picks,)),
        ],
        compiler_params=params(16 if gathered <= 8192 else 40),
        cost_estimate=cost(2.0),
        name="partial_messages",
    )(cols, order, *pieces, tiles)


def mlp_kernel(kinds, middle, nodes, cot, *refs):
    n_parts = sum(len(chunk) for chunk in kinds)
    parts = refs[:n_parts]
    w_in, bias, w_out, gain, shift, updated, gpre_o, act_o, gproj_o, msg_o, vec = refs[
        n_parts : n_parts + 11
    ]
    gmsgs = refs[n_parts + 11 :]
    width = nodes.shape[1]
    inner = middle[0] > 0
    messages = []
    place = 0
    for chunk in kinds:
        total = None
        for kind in chunk:
            term = parts[place][...].astype(F32)
            place += 1
            if kind == "inner":
                term = jnp.where(inner, term, 0.0)
            total = term if total is None else total + term
        messages.append(total.astype(BF16))
    message = jnp.concatenate(messages, axis=1) if len(messages) > 1 else messages[0]
    node = nodes[...]
    pre = mm(node, w_in[:width]) + mm(message, w_in[width:]) + bias[...]
    sig = jax.nn.sigmoid(pre)
    act = (pre * sig).astype(BF16)
    proj = mm(act, w_out[...])
    mean = jnp.mean(proj, axis=-1, keepdims=True)
    var = jnp.mean((proj - mean) ** 2, axis=-1, keepdims=True)
    rstd = 1.0 / jnp.sqrt(var + 1e-05)
    normed = (proj - mean) * rstd
    updated[...] = (node.astype(F32) + normed * gain[...] + shift[...]).astype(BF16)
    grad_out = cot[...].astype(F32)
    gscaled = grad_out * gain[...]
    gproj = (
        (
            gscaled
            - jnp.mean(gscaled, axis=-1, keepdims=True)
            - normed * jnp.mean(gscaled * normed, axis=-1, keepdims=True)
        )
        * rstd
    ).astype(BF16)
    gact = mm(gproj, w_out[...], NT)
    gpre = gact * sig * (1.0 + pre * (1.0 - sig))
    gpre_b = gpre.astype(BF16)
    gmsg = mm(gpre_b, w_in[width:], NT).astype(BF16)
    part = width // len(gmsgs)
    for index, out in enumerate(gmsgs):
        out[...] = gmsg[:, index * part : (index + 1) * part]
    gpre_o[...] = gpre_b
    act_o[...] = act
    gproj_o[...] = gproj
    msg_o[...] = message

    @pl.when(pl.program_id(0) == 0)
    def _():
        vec[...] = jnp.zeros_like(vec)

    vec[0:1] += jnp.sum(gpre, axis=0, keepdims=True)
    vec[1:2] += jnp.sum(grad_out * normed, axis=0, keepdims=True)
    vec[2:3] += jnp.sum(grad_out, axis=0, keepdims=True)


def mlp_call(middle, nodes, cot, parts, kinds, w_in, bias, w_out, gain, shift):
    rows, width = nodes.shape
    step = min(rows, 256)

    def blocked(array):
        return pl.BlockSpec((step, array.shape[1]), lambda i: (i, 0))

    def whole(array):
        return pl.BlockSpec(array.shape, lambda i: (0, 0))

    flat = [term for chunk in parts for term in chunk]
    row_like = jax.ShapeDtypeStruct((rows, width), BF16)
    chunk_like = jax.ShapeDtypeStruct((rows, width // len(parts)), BF16)
    outs = [row_like] * 5 + [jax.ShapeDtypeStruct((8, width), F32)] + [chunk_like] * len(parts)
    weights = (w_in, bias, w_out, gain, shift)
    result = pl.pallas_call(
        functools.partial(mlp_kernel, kinds),
        grid=(rows // step,),
        out_shape=outs,
        in_specs=[SMEM] + [blocked(a) for a in (nodes, cot, *flat)] + [whole(a) for a in weights],
        out_specs=[blocked(a) for a in outs[:5]] + [whole(outs[5])] + [blocked(a) for a in outs[6:]],
        compiler_params=params(20),
        cost_estimate=cost(5.0),
        name="mlp",
    )(middle, nodes, cot, *flat, *weights)
    return result[:6], result[6:]


def weight_kernel(factor, pieces, mine, nodes, msg, act, gpre, gproj, cot, w_in, vec, out, direct, grads):
    width = nodes.shape[1]

    @pl.when(pl.program_id(0) == 0)
    def _():
        grads[...] = jnp.zeros_like(grads)
        grads[3 * width : 3 * width + 8] = vec[...] * factor

    gpre_b = gpre[...]
    grads[:width] += mm(nodes[...], gpre_b, TN) * factor
    grads[width : 2 * width] += mm(msg[...], gpre_b, TN) * factor
    grads[2 * width : 3 * width] += mm(act[...], gproj[...], TN) * factor
    direct[...] = cot[...].astype(F32) + mm(gpre_b, w_in[:width], NT)

    @pl.when(pl.program_id(0) == pl.num_programs(0) - 1)
    def _():
        if pieces == 1:
            out[...] = grads[: out.shape[0]]
        else:
            rows = grads.shape[0] // pieces
            for place, member in enumerate(SWAP_ORDER):
                where = pl.ds(pl.multiple_of((mine[0] ^ member) * rows, 8), rows)
                out[place * rows : (place + 1) * rows] = grads[where]


def weight_call(factor, pieces, mine, nodes, msg, act, gpre, gproj, cot, w_in, vec):
    rows, width = nodes.shape
    step = min(rows, 256)
    blocked = pl.BlockSpec((step, width), lambda i: (i, 0))

    def whole(shape):
        return pl.BlockSpec(shape, lambda i: (0, 0))

    padded = (3 * width + width // 2, width)
    if pieces == 1:
        out = jax.ShapeDtypeStruct((3 * width + 8, width), F32)
    else:
        out = jax.ShapeDtypeStruct(padded, F32)
    return pl.pallas_call(
        functools.partial(weight_kernel, factor, pieces),
        grid=(rows // step,),
        out_shape=[out, jax.ShapeDtypeStruct((rows, width), F32)],
        in_specs=[SMEM] + [blocked] * 6 + [whole(w_in.shape), whole(vec.shape)],
        out_specs=[whole(out.shape), blocked],
        scratch_shapes=[pltpu.VMEM(padded, F32)],
        compiler_params=params(16),
        cost_estimate=cost(3.0),
        name="weight_grads",
    )(mine, nodes, msg, act, gpre, gproj, cot, w_in, vec)


def unpack_kernel(mine, parts, w_in, w_out, vectors, grads):
    width = w_in.shape[1]
    rows = grads.shape[0] // len(SWAP_ORDER)
    for place, member in enumerate(SWAP_ORDER):
        where = pl.ds(pl.multiple_of((mine[0] ^ member) * rows, 8), rows)
        grads[where] = parts[place * rows : (place + 1) * rows].astype(F32)
    w_in[...] = grads[: 2 * width]
    w_out[...] = grads[2 * width : 3 * width]
    vectors[...] = grads[3 * width : 3 * width + 3]


def unpack_call(mine, parts, width):
    shapes = ((2 * width, width), (width, width), (3, width))
    return pl.pallas_call(
        unpack_kernel,
        out_shape=[jax.ShapeDtypeStruct(shape, F32) for shape in shapes],
        in_specs=[SMEM, VMEM],
        out_specs=[VMEM] * 3,
        scratch_shapes=[pltpu.VMEM((3 * width + width // 2, width), F32)],
        compiler_params=params(16),
        cost_estimate=cost(2.0),
        name="weight_unpack",
    )(mine, parts)


def grad_jobs(rows, refs, dst, sem, order, middle, groups=None):
    if len(refs) == 1:
        return [(None, pltpu.make_async_copy(refs[0], dst, sem.at[0]))]
    conditions = {None: None, "inner": middle[0] > 0, "outer": middle[0] == 0}
    jobs = []
    for group, index, kind in GRAD_PLAN:
        if groups is None:
            where = block_at(order[group], rows)
        elif group in groups:
            where = pl.ds(groups.index(group) * rows, rows)
        else:
            continue
        copy = pltpu.make_async_copy(refs[index], dst.at[where], sem.at[index])
        jobs.append((conditions[kind], copy))
    return jobs


def run_jobs(jobs, verb):
    for condition, copy in jobs:
        if condition is None:
            getattr(copy, verb)()
        else:
            pl.when(condition)(getattr(copy, verb))


def for_live(found, entry):
    def several(i, carry):
        for index in range(LIVE_STEP):
            entry(i * LIVE_STEP + index)
        return carry

    def one(i, carry):
        entry(i)
        return carry

    full = found // LIVE_STEP
    lax.fori_loop(0, full, several, 0)
    lax.fori_loop(full * LIVE_STEP, found, one, 0)


def back_kernel(rows, slots, n_grads, n_after, out_pieces, cols, counts, order, middle, *refs):
    grads, tiles = refs[:n_grads], refs[n_grads]
    refs = refs[n_grads + 1 + n_after :]
    outs = refs[: len(out_pieces)]
    grad_v, tiles_v, acc, live, sem, tile_sem = refs[len(out_pieces) :]
    n_tiles, block = tiles.shape[:2]
    jobs = grad_jobs(rows, grads, grad_v, sem, order, middle)
    run_jobs(jobs, "start")
    tile_copy = pltpu.make_async_copy(tiles, tiles_v, tile_sem.at[0])
    tile_copy.start()
    acc[...] = jnp.zeros_like(acc)

    def collect(row, found):
        count = counts[row]
        for slot in range(slots):
            live[found] = row * slots + slot
            found = found + (slot < count).astype(jnp.int32)
        return found

    found = lax.fori_loop(0, n_tiles // slots, collect, jnp.int32(0))
    run_jobs(jobs, "wait")
    tile_copy.wait()

    def entry(place):
        tile_index = live[place]
        part = mm(tiles_v[tile_index], grad_v[block_at(tile_index // slots, block)], TN)
        acc[block_at(cols[tile_index], block)] += part

    for_live(found, entry)
    piece = acc.shape[0] // sum(len(members) for members in out_pieces)
    for out, members in zip(outs, out_pieces):
        for index, member in enumerate(members):
            out[pl.ds(index * piece, piece)] = acc[pl.ds(member * piece, piece)].astype(BF16)


def back_call(cols, counts, order, middle, grads, tiles, total, gathered, out_pieces, after=()):
    rows, width = grads[0].shape
    rows = total if len(grads) == 1 else rows
    row_blocks, slots, block = tiles.shape[:3]
    piece = gathered // sum(len(members) for members in out_pieces)
    return pl.pallas_call(
        functools.partial(back_kernel, rows, slots, len(grads), len(after), out_pieces),
        out_shape=[jax.ShapeDtypeStruct((len(m) * piece, width), BF16) for m in out_pieces],
        in_specs=[SMEM] * 4 + [ANY] * (len(grads) + 1 + len(after)),
        out_specs=[VMEM] * len(out_pieces),
        scratch_shapes=[
            pltpu.VMEM((total, width), BF16),
            pltpu.VMEM((row_blocks * slots, block, block), BF16),
            pltpu.VMEM((gathered, width), F32),
            pltpu.SMEM((row_blocks * slots + 8,), jnp.int32),
            pltpu.SemaphoreType.DMA((len(grads),)),
            pltpu.SemaphoreType.DMA((1,)),
        ],
        compiler_params=params(24 if gathered <= 8192 else 56),
        cost_estimate=cost(5.0),
        name="back_terms",
    )(cols, counts, order, middle, *grads, tiles.reshape(row_blocks * slots, block, block), *after)


def tile_grad_kernel(
    rows, slots, n_grads, n_pieces, n_chunks, n_after, groups, cols, counts, order, middle, *refs
):
    grads = refs[: n_grads * n_chunks]
    refs = refs[n_grads * n_chunks :]
    pieces = refs[: n_pieces * n_chunks]
    out, grad_v, nodes_v, tiles_v, live, source, sem, piece_sem, out_sem = refs[n_pieces * n_chunks + n_after :]
    block = out.shape[1]
    width = nodes_v.shape[1]
    part = width // n_chunks
    scale = float(width) ** -0.5
    blocks = grad_v.shape[0] // (block * len(groups))
    jobs, copies = [], []
    for chunk in range(n_chunks):
        columns = pl.ds(chunk * part, part)
        jobs += grad_jobs(
            rows,
            grads[chunk * n_grads : (chunk + 1) * n_grads],
            grad_v.at[:, columns],
            sem.at[chunk],
            order,
            middle,
            groups,
        )
        copies += load_pieces(
            pieces[chunk * n_pieces : (chunk + 1) * n_pieces],
            nodes_v.at[:, columns],
            piece_sem.at[chunk],
            0,
        )
    run_jobs(jobs, "start")
    tiles_v[...] = jnp.zeros_like(tiles_v)
    found = jnp.int32(0)
    for index, group in enumerate(groups):
        first = order[group] * blocks

        def collect(i, found, first=first, index=index):
            row = first + i
            count = counts[row]
            for slot in range(slots):
                live[found] = (index * blocks + i) * slots + slot
                source[found] = cols[row * slots + slot]
                found = found + (slot < count).astype(jnp.int32)
            return found

        found = lax.fori_loop(0, blocks, collect, found)
    run_jobs(jobs, "wait")
    for copy in copies:
        copy.wait()

    def entry(place):
        tile_index = live[place]
        grad = grad_v[block_at(tile_index // slots, block)]
        node = nodes_v[block_at(source[place], block)]
        tiles_v[tile_index] = (mm(grad, node, NT) * scale).astype(BF16)

    for_live(found, entry)
    size = blocks * slots
    copies = []
    for index, group in enumerate(groups):
        copy = pltpu.make_async_copy(
            tiles_v.at[pl.ds(index * size, size)],
            out.at[pl.ds(order[group] * size, size)],
            out_sem.at[index],
        )
        copy.start()
        copies.append(copy)
    for copy in copies:
        copy.wait()


def tile_grad_call(cols, counts, order, middle, grads, pieces, shape, rows, groups, base=None, after=()):
    row_blocks, slots, block = shape[:3]
    chunks = len(grads)
    width = grads[0][0].shape[1] * chunks
    gathered = sum(piece.shape[0] for piece in pieces[0])
    flat = [a for chunk in grads for a in chunk] + [a for chunk in pieces for a in chunk]
    after = after if base is None else (base,) + tuple(after)
    entries = len(groups) * rows // block * slots
    return pl.pallas_call(
        functools.partial(
            tile_grad_kernel, rows, slots, len(grads[0]), len(pieces[0]), chunks, len(after), groups
        ),
        out_shape=jax.ShapeDtypeStruct((row_blocks * slots, block, block), BF16),
        in_specs=[SMEM] * 4 + [ANY] * (len(flat) + len(after)),
        out_specs=ANY,
        input_output_aliases={} if base is None else {4 + len(flat): 0},
        scratch_shapes=[
            pltpu.VMEM((len(groups) * rows, width), BF16),
            pltpu.VMEM((gathered, width), BF16),
            pltpu.VMEM((entries, block, block), BF16),
            pltpu.SMEM((entries + 8,), jnp.int32),
            pltpu.SMEM((entries + 8,), jnp.int32),
            pltpu.SemaphoreType.DMA((chunks, len(grads[0]))),
            pltpu.SemaphoreType.DMA((chunks, len(pieces[0]))),
            pltpu.SemaphoreType.DMA((len(groups),)),
        ],
        compiler_params=params(16 if gathered <= 8192 else 40),
        cost_estimate=cost(4.0),
        name="tile_grads",
    )(cols, counts, order, middle, *flat, *after)


def add(*terms):
    value = terms[0].astype(F32)
    for term in terms[1:]:
        value = value + term.astype(F32)
    return value.astype(BF16)


def swap(value, bit):
    return lax.ppermute(value, "row", [(i, i ^ bit) for i in range(8)])


def outer_swap(value):
    return lax.ppermute(value, "col", [(0, 1), (1, 0), (2, 3), (3, 2)])


def mirror_swap(value):
    return lax.ppermute(value, "col", [(0, 3), (3, 0), (1, 2), (2, 1)])


def inner_swap(value):
    return lax.ppermute(value, "col", [(0, 0), (1, 2), (2, 1), (3, 3)])


def held(value, *others):
    return lax.optimization_barrier((value, *others))[0]


def gather_square(nodes):
    pieces = []
    for piece in (nodes, swap(nodes, 2), swap(nodes, 4), swap(nodes, 6)):
        pieces += [piece, swap(piece, 1)]
    return pieces


def pair_sums(even, odd, rows):
    other = swap(odd, 1)
    places = [slice(place * rows, (place + 1) * rows) for place in range(4)]
    return (even[places[0]], other[places[0]]), [add(even[p], other[p]) for p in places[1:]]


def reduce_square(sums):
    return [swap(value, bit) for value, bit in zip(sums, (2, 4, 6))]


def scatter_weights(terms):
    for bit in (1, 2, 4):
        half = terms.shape[0] // 2
        terms = terms[:half] + swap(terms[half:], bit)
    return terms


def level_weights(value):
    value = value + outer_swap(value)
    return value + mirror_swap(value)


def gather_weights(value, width, mine):
    value = value.astype(BF16)
    for bit in (4, 2, 1):
        value = jnp.concatenate([value, swap(value, bit)], axis=0)
    return unpack_call(mine, value, width)


def reduce_line(far, near, pair, own, inner):
    far_in = outer_swap(far)
    near_in = outer_swap(held(near, far_in))
    far_sum = inner_swap(add(far, far_in))
    near_sum = inner_swap(add(near, near_in))
    pair_in = outer_swap(add(pair, jnp.where(inner, far_sum, jnp.zeros_like(far_sum))))
    return own, pair_in, near_sum


def reduce_line_joint(both, pair, own, inner):
    rows = own.shape[0]
    both_in = outer_swap(both)
    both_sum = inner_swap(add(both, both_in))
    far_sum = both_sum[:rows]
    pair_in = outer_swap(add(pair, jnp.where(inner, far_sum, jnp.zeros_like(far_sum))))
    return (own, pair_in, both_sum[rows:]), both_in


def gather_line(own):
    pair = outer_swap(own)
    near_inner = inner_swap(own)
    far_inner = inner_swap(pair)
    near_outer = outer_swap(near_inner)
    far_outer = outer_swap(far_inner)
    return [own, pair, near_inner, near_outer, far_inner, far_outer]


def body(n_row, n_col, nodes, tiles, tile_col, tile_count, w_in, bias_in, w_out, ln_gain, ln_shift, cotangent):
    rows, width = nodes.shape
    row_blocks, _, slots, block = tiles.shape[:4]
    tile_local = tiles.reshape(row_blocks, slots, block, block)
    cols = tile_col.reshape(row_blocks * slots)
    counts = tile_count.reshape(row_blocks)
    blocks = rows // block
    gathered, total = n_row * rows, n_col * rows
    square_line = n_row == 8 and n_col == 4
    live = lax.broadcasted_iota(jnp.int32, (row_blocks, slots), 1) < counts[:, None]
    tile_live = jnp.where(live[:, :, None, None], tile_local, jnp.zeros_like(tile_local))
    if square_line:
        mine = lax.axis_index("row").astype(jnp.int32)
        cols = ((cols // blocks) ^ mine) * blocks + cols % blocks
        level = lax.axis_index("col").astype(jnp.int32)
        low = level < 2
        order = jnp.stack([jnp.where(low, 3, 0), jnp.where(low, 2, 1), level ^ 1, level]).astype(jnp.int32)
        inner = (level == 1) | (level == 2)
        middle = inner.astype(jnp.int32).reshape(1)
        part = width // 2
        left = gather_square(nodes[:, :part])
        right = gather_square(held(nodes[:, part:], left[2], left[4], left[6]))
        pieces = [left, right]
        (both,) = forward_call(cols, order, left, tile_live, ((0, 1),), rows)
        pair, own = forward_call(cols, order, left, tile_live, ((2,), (3,)), rows)
        left_parts, both_in = reduce_line_joint(both, pair, own, inner)
        far, near = forward_call(cols, order, right, tile_live, ((0,), (1,)), rows)
        pair, own = forward_call(cols, order, right, tile_live, ((2,), (3,)), rows)
        parts = [left_parts, reduce_line(held(far, both_in), near, pair, own, inner)]
        kinds = [("all", "all", "inner")] * 2
    else:
        order = jnp.arange(n_col, dtype=jnp.int32)
        middle = jnp.zeros((1,), jnp.int32)
        pieces = [[lax.all_gather(nodes, "row", axis=0, tiled=True)]]
        (partial,) = forward_call(cols, order, pieces[0], tile_live, (tuple(range(n_col)),), rows)
        parts = [[lax.psum_scatter(partial, "col", scatter_dimension=0, tiled=True)]]
        kinds = [("all",)]
    vectors = [v.reshape(1, width) for v in (bias_in, ln_gain, ln_shift)]
    (updated, gpre_b, act, gproj, message, vec), gmsgs = mlp_call(
        middle, nodes, cotangent, parts, kinds, w_in, vectors[0], w_out, vectors[1], vectors[2]
    )
    factor = float(rows * n_row * n_col) ** -0.5
    mine = lax.axis_index("row").astype(jnp.int32).reshape(1)
    weight_terms, direct = weight_call(
        factor, n_row if square_line else 1, mine, nodes, message, act, gpre_b, gproj, cotangent, w_in, vec
    )
    if square_line:
        halves = ((1, 3, 5, 7), (0, 2, 4, 6))
        first = gather_line(gmsgs[0])
        second = gather_line(held(gmsgs[1], first[4]))
        grads = [first, second]
        row_weights = scatter_weights(weight_terms)
        odd, even = back_call(
            cols, counts, order, middle, first, tile_live, total, gathered, halves,
            (second[1], second[2], row_weights),
        )
        own_terms, sums = pair_sums(even, odd, rows)
        near_grads = tile_grad_call(
            cols, counts, order, middle, [chunk[:2] for chunk in grads], pieces, tile_local.shape, rows, (3, 2),
            after=(odd,),
        )
        all_weights = level_weights(row_weights)
        odd, even = back_call(
            cols, counts, order, middle, second, tile_live, total, gathered, halves,
            (*sums, all_weights, near_grads),
        )
        left_terms = (*own_terms, *reduce_square(sums))
        own_terms, sums = pair_sums(even, odd, rows)
        right_terms = (*own_terms, *reduce_square(sums))
        weights = gather_weights(all_weights, width, mine)
        back = jnp.concatenate(
            [sum(term.astype(F32) for term in terms) for terms in (left_terms, right_terms)], axis=1
        )
        grad_tiles = tile_grad_call(
            cols, counts, order, middle, grads, pieces, tile_local.shape, rows, (1, 0), near_grads, sums
        )
    else:
        grads = [[lax.all_gather(gmsgs[0], "col", axis=0, tiled=True)]]
        weight_sums = lax.psum(weight_terms, ("row", "col"))
        weights = (
            weight_sums[: 2 * width],
            weight_sums[2 * width : 3 * width],
            weight_sums[3 * width : 3 * width + 3],
        )
        (terms,) = back_call(
            cols, counts, order, middle, grads[0], tile_live, total, gathered, (tuple(range(n_row)),)
        )
        back = lax.psum_scatter(terms, "row", scatter_dimension=0, tiled=True).astype(F32)
        grad_tiles = tile_grad_call(
            cols, counts, order, middle, grads, pieces, tile_local.shape, rows, tuple(range(n_col))
        )
    grad_nodes = (direct + back).astype(BF16)
    grad_tiles = grad_tiles.reshape(tiles.shape)
    return (updated, grad_nodes, grad_tiles, *weights)


def solution(mesh):
    placed = (
        P(("row", "col"), None),
        P("row", "col", None, None, None),
        P("row", "col", None),
        P("row", "col"),
        P(),
        P(),
        P(),
        P(),
        P(),
        P(("row", "col"), None),
    )
    return jax.shard_map(
        functools.partial(body, mesh.shape["row"], mesh.shape["col"]),
        mesh=mesh,
        in_specs=placed,
        out_specs=(
            P(("row", "col"), None),
            P(("row", "col"), None),
            P("row", "col", None, None, None),
            P(),
            P(),
            P(),
        ),
        check_vma=False,
    )
```

time: 191 us -> 193 us (1.010)
  waiting for transfers between devices: 69.9 us -> 58.5 us
  starting transfers between devices: 73.6 us -> 63.4 us
  local copies, waits for them, and re-layouts: 7 us -> 15.8 us
  other arithmetic: 5.19 us -> 12.8 us
  Pallas kernels: 33 us -> 40.2 us
    ppermute x25 -> x28, waiting for transfers between devices: 38.5 us -> 29.2 us  [swap(): return lax.ppermute(value, 'row', [(i, i ^ bit) for i in range(8)])]
    ppermute x13 -> x12, starting transfers between devices: 37.5 us -> 29 us  [outer_swap(): return lax.ppermute(value, 'col', [(0, 1), (1, 0), (2, 3), (3, 2)])]
    unnamed x69 -> x87, local copies, waits for them, and re-layouts: 5.83 us -> 13.5 us
    select_n x0 -> x2, other arithmetic: none -> 7.11 us  [body(): jnp.where(live[:, :, None, None], tile_local, jnp.zeros_like(tile_local))]
    ppermute x13 -> x12, waiting for transfers between devices: 31.4 us -> 24.9 us  [outer_swap(): return lax.ppermute(value, 'col', [(0, 1), (1, 0), (2, 3), (3, 2)])]
    pallas_call x5 -> x6, Pallas kernels: 16.7 us -> 22.1 us  [the longest x2 11.4 us: tile_grad_call(): pl.pallas_call(functools.partial(tile_grad_kernel, rows, slots, len(grads...]
    ppermute x1, waiting for transfers between devices: 0.01 us -> 4.41 us  [mirror_swap(): return lax.ppermute(value, 'col', [(0, 3), (3, 0), (1, 2), (2, 1)])]
    pallas_call x2, Pallas kernels: 8.2 us -> 10.8 us  [back_call(): pl.pallas_call(functools.partial(back_kernel, rows, slots, len(grads), le...]
  transfers between devices with their start and end apart: 47 -> 48, of which waited for: 18 -> 20; matrix products, arithmetic and copies ran while one was open for 3% -> 7% of each run, Pallas kernels for 14% -> 15%
where the time goes in v4:
time: 193 us; the launch traced here: 192 us
  starting transfers between devices  63.4 us (33%)
  waiting for transfers between devices  58.5 us (30%)
  Pallas kernels  40.2 us (21%)
  local copies, waits for them, and re-layouts  15.8 us (8%)
  other arithmetic  12.8 us (7%)
    ppermute x28, waiting for transfers between devices, swap(): return lax.ppermute(value, 'row', [(i, i ^ bit) for i in range(8)])  29.2 us
    ppermute x12, starting transfers between devices, outer_swap(): return lax.ppermute(value, 'col', [(0, 1), (1, 0), (2, 3), (3, 2)])  29 us
    ppermute x12, waiting for transfers between devices, outer_swap(): return lax.ppermute(value, 'col', [(0, 1), (1, 0), (2, 3), (3, 2)])  24.9 us
    ppermute x28, starting transfers between devices, swap(): return lax.ppermute(value, 'row', [(i, i ^ bit) for i in range(8)])  21.4 us
    unnamed x87, local copies, waits for them, and re-layouts  13.5 us
    pallas_call x2, Pallas kernels, tile_grad_call(): pl.pallas_call(functools.partial(tile_grad_kernel, rows, slots, len(grads...  11.4 us
    pallas_call x2, Pallas kernels, back_call(): pl.pallas_call(functools.partial(back_kernel, rows, slots, len(grads), le...  10.8 us
    pallas_call x4, Pallas kernels, forward_call(): pl.pallas_call(functools.partial(forward_kernel, outputs, len(pieces)), o...  10.7 us
  transfers between devices with their start and end apart: 48, of which 20 were waited for; matrix products, arithmetic and copies ran while one was open for 7% of the time, Pallas kernels for 15%

profile of v4, /device:TPU:0, one launch (start us, length us, event | category | flops | bytes accessed | tf_op | source)
XLA Modules:
  0.0 192.0 jit_solution(4762573460431971625)
XLA Ops:
  0.6 1.1 fusion.3
  1.7 4.0 %collective-permute-start.5 = (bf16[1024,128]{1,0:T(8,128)(2,1)S(1)}, bf16[1024,128]{1,0:T(8,128)(2,1)S(1)}, u32[]{:S(2)}, u32[]{:S(2)}) collective-permute-start(bf16[1024,128]{1,0:T(8,128)(2,1)S(1)} %get-tuple-element.81.refs_0_.refs_4_.refs_12_), channel_id=1, source_target_pairs={{0,24},{4,28},{8,16},{12,20},{16,8},{20,12},{24,0},{28,4},{1,25},{... | collective-permute-start | bytes 786440 | tf_op jit(solution)/shard_map/ppermute | solution.py:496
  7.0 4.6 %bitcast_select_fusion.1.refs_8_ = bf16[32,4,128,128]{3,2,1,0:T(8,128)(2,1)} fusion(bf16[32,1,4,128,128]{4,3,2,1,0:T(8,128)(2,1)} %param.11, pred[32,4]{1,0:T(8,128)(4,1)S(1)} %iota_compare_fusion), kind=kLoop, calls=%fused_computation.1 | loop fusion | flops 2097152 | bytes 8388736 | tf_op jit(solution)/shard_map/jit(_where)/select_n | solution.py:588
  11.6 1.2 collective-permute-done.5.refs_6_.refs_10_.refs_18_
  12.8 4.7 %collective-permute-done.3.refs_4_.refs_8_.refs_16_ = bf16[1024,128]{1,0:T(8,128)(2,1)S(1)} collective-permute-done((bf16[1024,128]{1,0:T(8,128)(2,1)S(1)}, bf16[1024,128]{1,0:T(8,128)(2,1)S(1)}, u32[]{:S(2)}, u32[]{:S(2)}) %collective-permute-start.3) | collective-permute-done | bytes 262176 | tf_op jit(solution)/shard_map/ppermute | solution.py:496
  18.4 1.9 collective-permute-start.15
  20.3 1.3 collective-permute-start.13
  22.0 2.3 %copy-done = bf16[32,4,128,128]{3,2,1,0:T(8,128)(2,1)S(1)} copy-done((bf16[32,4,128,128]{3,2,1,0:T(8,128)(2,1)S(1)}, bf16[32,4,128,128]{3,2,1,0:T(8,128)(2,1)}, u32[]{:S(2)}) %copy-start) | copy-done | bytes 4194328
  24.3 2.1 %partial_messages.5 = bf16[2048,128]{1,0:T(8,128)(2,1)S(1)} custom-call(s32[128]{0:T(128)S(1)} %fusion.1.cols, s32[4]{0:T(128)S(1)} %pad_add_fusion.order, bf16[1024,128]{1,0:T(8,128)(2,1)S(1)} %get-tuple-element.81.refs_0_.refs_4_.refs_12_, bf16[1024,128]{1,0:T(8,128)(2,1)S(1)} %collective-permute-done.refs_1_.refs_5_.refs_13_, ...), custom_call_target="tpu_custom_call" | custom-call | flops 2307000064 | bytes 1048576 | tf_op jit(solution)/shard_map/partial_messages/pallas_call | solution.py:103
  26.4 1.8 collective-permute-start.7
  29.5 4.0 %collective-permute-done.13.refs_4_.refs_16_.refs_24_ = bf16[1024,128]{1,0:T(8,128)(2,1)S(1)} collective-permute-done((bf16[1024,128]{1,0:T(8,128)(2,1)S(1)}, bf16[1024,128]{1,0:T(8,128)(2,1)S(1)}, u32[]{:S(2)}, u32[]{:S(2)}) %collective-permute-start.13) | collective-permute-done | bytes 262176 | tf_op jit(solution)/shard_map/ppermute | solution.py:496
  35.2 1.1 collective-permute-done.12.refs_3_.refs_15_.refs_23_
  36.2 2.2 %copy-done.1 = bf16[32,4,128,128]{3,2,1,0:T(8,128)(2,1)S(1)} copy-done((bf16[32,4,128,128]{3,2,1,0:T(8,128)(2,1)S(1)}, bf16[32,4,128,128]{3,2,1,0:T(8,128)(2,1)}, u32[]{:S(2)}) %copy-start.1) | copy-done | bytes 4194328
  38.4 0.9 copy-done.18
  39.4 0.9 copy-done.21
  40.3 3.4 %partial_messages.7 = (bf16[1024,128]{1,0:T(8,128)(2,1)S(1)}, bf16[1024,128]{1,0:T(8,128)(2,1)S(1)}) custom-call(s32[128]{0:T(128)S(1)} %fusion.1.cols, s32[4]{0:T(128)S(1)} %pad_add_fusion.order, bf16[1024,128]{1,0:T(8,128)(2,1)S(1)} %get-tuple-element.35.refs_0_.refs_12_.refs_20_, bf16[1024,128]{1,0:T(8,128)(2,1)} %collective-permute-done.10.refs_1_.refs_13_.refs_21_, ...), custom_call_target="tpu_custom_call" | custom-call | flops 2307000064 | bytes 1048576 | tf_op jit(solution)/shard_map/partial_messages/pallas_call | solution.py:103
  43.7 1.6 collective-permute-start.17
  45.4 1.2 add_convert_fusion
  47.3 2.1 %partial_messages.4 = (bf16[1024,128]{1,0:T(8,128)(2,1)S(1)}, bf16[1024,128]{1,0:T(8,128)(2,1)S(1)}) custom-call(s32[128]{0:T(128)S(1)} %fusion.1.cols, s32[4]{0:T(128)S(1)} %pad_add_fusion.order, bf16[1024,128]{1,0:T(8,128)(2,1)S(1)} %get-tuple-element.81.refs_0_.refs_4_.refs_12_, bf16[1024,128]{1,0:T(8,128)(2,1)S(1)} %collective-permute-done.refs_1_.refs_5_.refs_13_, ...), custom_call_target="tpu_custom_call" | custom-call | flops 2307000064 | bytes 1048576 | tf_op jit(solution)/shard_map/partial_messages/pallas_call | solution.py:103
  50.9 3.1 %partial_messages.6 = (bf16[1024,128]{1,0:T(8,128)(2,1)S(1)}, bf16[1024,128]{1,0:T(8,128)(2,1)S(1)}) custom-call(s32[128]{0:T(128)S(1)} %copy-done.33, s32[4]{0:T(128)S(1)} %pad_add_fusion.order, bf16[1024,128]{1,0:T(8,128)(2,1)S(1)} %get-tuple-element.35.refs_0_.refs_12_.refs_20_, bf16[1024,128]{1,0:T(8,128)(2,1)} %collective-permute-done.10.refs_1_.refs_13_.refs_21_, ...), custom_call_target="tpu_custom_call" | custom-call | flops 2307000064 | bytes 1048576 | tf_op jit(solution)/shard_map/partial_messages/pallas_call | solution.py:103
  54.0 4.4 %collective-permute-start.20 = (bf16[1024,128]{1,0:T(8,128)(2,1)S(1)}, bf16[1024,128]{1,0:T(8,128)(2,1)S(1)}, u32[]{:S(2)}, u32[]{:S(2)}) collective-permute-start(bf16[1024,128]{1,0:T(8,128)(2,1)S(1)} %get-tuple-element.41), channel_id=1, source_target_pairs={{0,1},{1,0},{2,3},{3,2},{4,5},{5,4},{6,7},{7,6},{8,9},{9,8},{10,11... | collective-permute-start | bytes 786440 | tf_op jit(solution)/shard_map/ppermute | solution.py:500
  59.2 0.9 add_convert_fusion.10
  60.1 5.1 %collective-permute-start.9 = (bf16[1024,128]{1,0:T(8,128)(2,1)}, bf16[1024,128]{1,0:T(8,128)(2,1)S(1)}, u32[]{:S(2)}, u32[]{:S(2)}) collective-permute-start(bf16[1024,128]{1,0:T(8,128)(2,1)} %add_convert_fusion.10), channel_id=1, source_target_pairs={{0,1},{1,0},{2,3},{3,2},{4,5},{5,4},{6,7},{7,6},{8,9},{9,8},{10,11... | collective-permute-start | bytes 786440 | tf_op jit(solution)/shard_map/ppermute | solution.py:500
  66.0 1.6 collective-permute-start.21
  67.7 2.4 %collective-permute-start.19 = (bf16[1024,128]{1,0:T(8,128)(2,1)S(1)}, bf16[1024,128]{1,0:T(8,128)(2,1)S(1)}, u32[]{:S(2)}, u32[]{:S(2)}) collective-permute-start(bf16[1024,128]{1,0:T(8,128)(2,1)S(1)} %add_convert_fusion.8), channel_id=1, source_target_pairs={{0,1},{1,0},{2,3},{3,2},{4,5},{5,4},{6,7},{7,6},{8,9},{9,8},{10,11... | collective-permute-start | bytes 786440 | tf_op jit(solution)/shard_map/ppermute | solution.py:500
  70.1 1.0 slice.105.refs_2_
  71.7 4.8 %collective-permute-done.19.refs_4_ = bf16[1024,128]{1,0:T(8,128)(2,1)S(1)} collective-permute-done((bf16[1024,128]{1,0:T(8,128)(2,1)S(1)}, bf16[1024,128]{1,0:T(8,128)(2,1)S(1)}, u32[]{:S(2)}, u32[]{:S(2)}) %collective-permute-start.19) | collective-permute-done | bytes 262176 | tf_op jit(solution)/shard_map/ppermute | solution.py:500
  76.6 0.9 copy-done.36
  77.5 0.9 copy-done.38
  78.5 4.7 %mlp.1 = (bf16[1024,256]{1,0:T(8,128)(2,1)}, bf16[1024,256]{1,0:T(8,128)(2,1)S(1)}, bf16[1024,256]{1,0:T(8,128)(2,1)S(1)}, bf16[1024,256]{1,0:T(8,128)(2,1)S(1)}...) custom-call(s32[1]{0:T(128)} %bitcast.middle, ...), custom_call_target="tpu_custom_call" | custom-call | flops 5767499776 | bytes 1048576 | tf_op jit(solution)/shard_map/mlp/pallas_call | solution.py:197
  83.1 1.5 weight_grads.1
  84.8 1.8 collective-permute-start.22
  86.6 3.6 %collective-permute-start.23 = (bf16[1024,128]{1,0:T(8,128)(2,1)}, bf16[1024,128]{1,0:T(8,128)(2,1)}, u32[]{:S(2)}, u32[]{:S(2)}) collective-permute-start(bf16[1024,128]{1,0:T(8,128)(2,1)} %get-tuple-element.49.refs_0_), channel_id=1, source_target_pairs={{0,0},{1,2},{2,1},{3,3},{4,4},{5,6},{6,5},{7,7},{8,8},{9,10},{10,9... | collective-permute-start | bytes 786440 | tf_op jit(solution)/shard_map/ppermute | solution.py:508
  90.2 3.5 %collective-permute-done.22.refs_1_ = bf16[1024,128]{1,0:T(8,128)(2,1)S(1)} collective-permute-done((bf16[1024,128]{1,0:T(8,128)(2,1)}, bf16[1024,128]{1,0:T(8,128)(2,1)S(1)}, u32[]{:S(2)}, u32[]{:S(2)}) %collective-permute-start.22) | collective-permute-done | bytes 262176 | tf_op jit(solution)/shard_map/ppermute | solution.py:500
  93.7 1.4 collective-permute-start.25
  95.2 1.5 collective-permute-start.30
  96.9 3.8 %collective-permute-start.24 = (bf16[1024,128]{1,0:T(8,128)(2,1)}, bf16[1024,128]{1,0:T(8,128)(2,1)S(1)}, u32[]{:S(2)}, u32[]{:S(2)}) collective-permute-start(bf16[1024,128]{1,0:T(8,128)(2,1)} %collective-permute-done.23.refs_2_), channel_id=1, source_target_pairs={{0,1},{1,0},{2,3},{3,2},{4,5},{5,4},{6,7},{7,6},{8,9},{9,8},{10,11... | collective-permute-start | bytes 786440 | tf_op jit(solution)/shard_map/ppermute | solution.py:500
  100.6 1.6 collective-permute-start.28
  102.2 6.6 %collective-permute-start.27 = (bf16[1024,128]{1,0:T(8,128)(2,1)}, bf16[1024,128]{1,0:T(8,128)(2,1)S(1)}, u32[]{:S(2)}, u32[]{:S(2)}) collective-permute-start(bf16[1024,128]{1,0:T(8,128)(2,1)} %copy-done.23), channel_id=1, source_target_pairs={{0,1},{1,0},{2,3},{3,2},{4,5},{5,4},{6,7},{7,6},{8,9},{9,8},{10,11... | collective-permute-start | bytes 786440 | tf_op jit(solution)/shard_map/ppermute | solution.py:500
  109.0 1.6 collective-permute-start.31
  110.6 2.5 %bitcast_select_fusion.refs_6_ = bf16[128,128,128]{2,1,0:T(8,128)(2,1)S(1)} fusion(bf16[32,1,4,128,128]{4,3,2,1,0:T(8,128)(2,1)} %param.11, pred[128]{0:T(512)(128)(4,1)S(1)} %lt.29), kind=kLoop, calls=%fused_computation | loop fusion | flops 2097152 | bytes 8388736 | tf_op jit(solution)/shard_map/jit(_where)/select_n | solution.py:588
  114.0 2.3 %collective-permute-done.27.refs_7_.refs_3_.refs_1_ = bf16[1024,128]{1,0:T(8,128)(2,1)S(1)} collective-permute-done((bf16[1024,128]{1,0:T(8,128)(2,1)}, bf16[1024,128]{1,0:T(8,128)(2,1)S(1)}, u32[]{:S(2)}, u32[]{:S(2)}) %collective-permute-start.27) | collective-permute-done | bytes 262176 | tf_op jit(solution)/shard_map/ppermute | solution.py:500
  116.3 3.5 %collective-permute-done.26.refs_5_ = bf16[1024,128]{1,0:T(8,128)(2,1)S(1)} collective-permute-done((bf16[1024,128]{1,0:T(8,128)(2,1)}, bf16[1024,128]{1,0:T(8,128)(2,1)S(1)}, u32[]{:S(2)}, u32[]{:S(2)}) %collective-permute-start.26) | collective-permute-done | bytes 262176 | tf_op jit(solution)/shard_map/ppermute | solution.py:500
  119.7 5.3 %back_terms.2 = (bf16[4096,128]{1,0:T(8,128)(2,1)S(1)}, bf16[4096,128]{1,0:T(8,128)(2,1)S(1)}) custom-call(s32[128]{0:T(128)S(1)} %copy-done.34, s32[32]{0:T(128)S(1)} %bitcast.20, s32[4]{0:T(128)S(1)} %pad_add_fusion.order, s32[1]{0:T(128)} %bitcast.middle, bf16[1024,128]{1,0:T(8,128)(2,1)} %get-tuple-element.49.refs_0_, bf16[1024,128]{1,0:T(8,128)(2,1)S(1)} %copy-done.26, ...), custom_call_target="tpu_custom_call" | custom-call | flops 5767499776 | bytes 1048576 | tf_op jit(solution)/shard_map/back_terms/pallas_call | solution.py:366
  125.5 5.2 %collective-permute-done.39 = f32[112,256]{1,0:T(8,128)S(1)} collective-permute-done((f32[112,256]{1,0:T(8,128)S(1)}, f32[112,256]{1,0:T(8,128)S(1)}, u32[]{:S(2)}, u32[]{:S(2)}) %collective-permute-start.39) | collective-permute-done | bytes 114720 | tf_op jit(solution)/shard_map/ppermute | solution.py:500
  130.7 2.8 %collective-permute-start.40 = (f32[112,256]{1,0:T(8,128)S(1)}, f32[112,256]{1,0:T(8,128)S(1)}, u32[]{:S(2)}, u32[]{:S(2)}) collective-permute-start(f32[112,256]{1,0:T(8,128)S(1)} %add.102), channel_id=1, source_target_pairs={{0,3},{3,0},{1,2},{2,1},{4,7},{7,4},{5,6},{6,5},{8,11},{11,8},{9,1... | collective-permute-start | bytes 344072 | tf_op jit(solution)/shard_map/ppermute | solution.py:504
  134.2 4.4 %collective-permute-done.40 = f32[112,256]{1,0:T(8,128)S(1)} collective-permute-done((f32[112,256]{1,0:T(8,128)S(1)}, f32[112,256]{1,0:T(8,128)S(1)}, u32[]{:S(2)}, u32[]{:S(2)}) %collective-permute-start.40) | collective-permute-done | bytes 114720 | tf_op jit(solution)/shard_map/ppermute | solution.py:504
  138.7 1.1 collective-permute-start.45
  139.9 5.8 %tile_grads.2.refs_11_.refs_28_ = bf16[128,128,128]{2,1,0:T(8,128)(2,1)} custom-call(s32[128]{0:T(128)S(1)} %copy-done.34, s32[32]{0:T(128)S(1)} %bitcast.21, s32[4]{0:T(128)S(1)} %pad_add_fusion.order, s32[1]{0:T(128)} %bitcast.middle, bf16[1024,128]{1,0:T(8,128)(2,1)} %get-tuple-element.49.refs_0_, bf16[1024,128]{1,0:T(8,128)(2,1)S(1)} %copy-done.26, ...), custom_call_target="tpu_custom_call" | custom-call | flops 4614000128 | bytes 1048576 | tf_op jit(solution)/shard_map/tile_grads/pallas_call | solution.py:464
  145.7 1.0 collective-permute-start.38
  147.1 5.0 %collective-permute-done.38.refs_5_.refs_11_ = bf16[1024,128]{1,0:T(8,128)(2,1)S(1)} collective-permute-done((bf16[1024,128]{1,0:T(8,128)(2,1)S(1)}, bf16[1024,128]{1,0:T(8,128)(2,1)S(1)}, u32[]{:S(2)}, u32[]{:S(2)}) %collective-permute-start.38) | collective-permute-done | bytes 262176 | tf_op jit(solution)/shard_map/ppermute | solution.py:500
  152.1 2.2 %copy-done.31 = bf16[128,128,128]{2,1,0:T(8,128)(2,1)S(1)} copy-done((bf16[128,128,128]{2,1,0:T(8,128)(2,1)S(1)}, bf16[128,128,128]{2,1,0:T(8,128)(2,1)}, u32[]{:S(2)}) %copy-start.31) | copy-done | bytes 4194328
  154.3 5.5 %back_terms.3 = (bf16[4096,128]{1,0:T(8,128)(2,1)S(1)}, bf16[4096,128]{1,0:T(8,128)(2,1)S(1)}) custom-call(s32[128]{0:T(128)S(1)} %copy-done.34, s32[32]{0:T(128)S(1)} %bitcast.22, s32[4]{0:T(128)S(1)} %pad_add_fusion.order, s32[1]{0:T(128)} %bitcast.middle, bf16[1024,128]{1,0:T(8,128)(2,1)S(1)} %copy-done.24, ...), custom_call_target="tpu_custom_call" | custom-call | flops 5767499776 | bytes 1048576 | tf_op jit(solution)/shard_map/back_terms/pallas_call | solution.py:366
  160.5 1.5 collective-permute-start.35
  162.3 1.7 collective-permute-start.33
  164.0 1.0 weight_unpack.1
  165.0 5.6 %collective-permute-done.35 = bf16[1024,128]{1,0:T(8,128)(2,1)S(1)} collective-permute-done((bf16[1024,128]{1,0:T(8,128)(2,1)S(1)}, bf16[1024,128]{1,0:T(8,128)(2,1)S(1)}, u32[]{:S(2)}, u32[]{:S(2)}) %collective-permute-start.35) | collective-permute-done | bytes 262176 | tf_op jit(solution)/shard_map/ppermute | solution.py:496
  170.6 4.7 %collective-permute-done.34 = bf16[1024,128]{1,0:T(8,128)(2,1)S(1)} collective-permute-done((bf16[1024,128]{1,0:T(8,128)(2,1)S(1)}, bf16[1024,128]{1,0:T(8,128)(2,1)S(1)}, u32[]{:S(2)}, u32[]{:S(2)}) %collective-permute-start.34) | collective-permute-done | bytes 262176 | tf_op jit(solution)/shard_map/ppermute | solution.py:496
  176.4 1.4 collective-permute-start.44
  177.8 1.4 collective-permute-start.43
  179.2 5.6 %tile_grads.3 = bf16[128,128,128]{2,1,0:T(8,128)(2,1)} custom-call(s32[128]{0:T(128)S(1)} %copy-done.34, s32[32]{0:T(128)S(1)} %bitcast.23, s32[4]{0:T(128)S(1)} %pad_add_fusion.order, s32[1]{0:T(128)} %bitcast.middle, bf16[1024,128]{1,0:T(8,128)(2,1)} %get-tuple-element.49.refs_0_, ...), custom_call_target="tpu_custom_call", output_to_operand_aliasing={{}: (32, {})} | custom-call | flops 4614000128 | bytes 1048576 | tf_op jit(solution)/shard_map/tile_grads/pallas_call | solution.py:464
  184.9 4.6 %collective-permute-done.44 = bf16[1024,128]{1,0:T(8,128)(2,1)S(1)} collective-permute-done((bf16[1024,128]{1,0:T(8,128)(2,1)S(1)}, bf16[1024,128]{1,0:T(8,128)(2,1)S(1)}, u32[]{:S(2)}, u32[]{:S(2)}) %collective-permute-start.44) | collective-permute-done | bytes 262176 | tf_op jit(solution)/shard_map/ppermute | solution.py:496
  189.5 1.4 collective-permute-done.43
  191.1 0.9 fusion
  (160 shorter events, 14.9 us)
Async XLA Ops:
  1.7 11.1 %collective-permute-start.5 = (bf16[1024,128]{1,0:T(8,128)(2,1)S(1)}, bf16[1024,128]{1,0:T(8,128)(2,1)S(1)}, u32[]{:S(2)}, u32[]{:S(2)}) collective-permute-start(bf16[1024,128]{1,0:T(8,128)(2,1)S(1)} %get-tuple-element.81.refs_0_.refs_4_.refs_12_), channel_id=1, source_target_pairs={{0,24},{4,28},{8,16},{12,20},{16,8},{20,12},{24,0},{28,4},{1,25},{... | collective-permute-start | bytes 786440 | tf_op jit(solution)/shard_map/ppermute | solution.py:496
  5.7 11.9 %collective-permute-start.3 = (bf16[1024,128]{1,0:T(8,128)(2,1)S(1)}, bf16[1024,128]{1,0:T(8,128)(2,1)S(1)}, u32[]{:S(2)}, u32[]{:S(2)}) collective-permute-start(bf16[1024,128]{1,0:T(8,128)(2,1)S(1)} %get-tuple-element.81.refs_0_.refs_4_.refs_12_), channel_id=1, source_target_pairs={{0,16},{4,20},{8,24},{12,28},{16,0},{20,4},{24,8},{28,12},{1,17},{... | collective-permute-start | bytes 786440 | tf_op jit(solution)/shard_map/ppermute | solution.py:496
  6.2 11.7 %collective-permute-start.1 = (bf16[1024,128]{1,0:T(8,128)(2,1)S(1)}, bf16[1024,128]{1,0:T(8,128)(2,1)S(1)}, u32[]{:S(2)}, u32[]{:S(2)}) collective-permute-start(bf16[1024,128]{1,0:T(8,128)(2,1)S(1)} %get-tuple-element.81.refs_0_.refs_4_.refs_12_), channel_id=1, source_target_pairs={{0,8},{4,12},{8,0},{12,4},{16,24},{20,28},{24,16},{28,20},{1,9},{5... | collective-permute-start | bytes 786440 | tf_op jit(solution)/shard_map/ppermute | solution.py:496
  6.3 14.0 %collective-permute-start = (bf16[1024,128]{1,0:T(8,128)(2,1)S(1)}, bf16[1024,128]{1,0:T(8,128)(2,1)S(1)}, u32[]{:S(2)}, u32[]{:S(2)}) collective-permute-start(bf16[1024,128]{1,0:T(8,128)(2,1)S(1)} %get-tuple-element.81.refs_0_.refs_4_.refs_12_), channel_id=1, source_target_pairs={{0,4},{4,0},{8,12},{12,8},{16,20},{20,16},{24,28},{28,24},{1,5},{5... | collective-permute-start | bytes 786440 | tf_op jit(solution)/shard_map/ppermute | solution.py:496
  12.8 8.8 %collective-permute-start.6 = (bf16[1024,128]{1,0:T(8,128)(2,1)S(1)}, bf16[1024,128]{1,0:T(8,128)(2,1)S(1)}, u32[]{:S(2)}, u32[]{:S(2)}) collective-permute-start(bf16[1024,128]{1,0:T(8,128)(2,1)S(1)} %collective-permute-done.5.refs_6_.refs_10_.refs_18_), channel_id=1, source_target_pairs={{0,4},{4,0},{8,12},{12,8},{16,20},{20,16},{24,28},{28,24},{1,5},{5... | collective-permute-start | bytes 786440 | tf_op jit(solution)/shard_map/ppermute | solution.py:496
  17.6 4.4 %collective-permute-start.4 = (bf16[1024,128]{1,0:T(8,128)(2,1)S(1)}, bf16[1024,128]{1,0:T(8,128)(2,1)S(1)}, u32[]{:S(2)}, u32[]{:S(2)}) collective-permute-start(bf16[1024,128]{1,0:T(8,128)(2,1)S(1)} %collective-permute-done.3.refs_4_.refs_8_.refs_16_), channel_id=1, source_target_pairs={{0,4},{4,0},{8,12},{12,8},{16,20},{20,16},{24,28},{28,24},{1,5},{5... | collective-permute-start | bytes 786440 | tf_op jit(solution)/shard_map/ppermute | solution.py:496
  17.9 29.4 %copy-start.7 = (bf16[1024,128]{1,0:T(8,128)(2,1)}, bf16[1024,128]{1,0:T(8,128)(2,1)S(1)}, u32[]{:S(2)}) copy-start(bf16[1024,128]{1,0:T(8,128)(2,1)S(1)} %collective-permute-done.1.refs_2_.refs_6_.refs_14_) | copy-start | bytes 786436
  17.9 4.1 %collective-permute-start.2 = (bf16[1024,128]{1,0:T(8,128)(2,1)S(1)}, bf16[1024,128]{1,0:T(8,128)(2,1)S(1)}, u32[]{:S(2)}, u32[]{:S(2)}) collective-permute-start(bf16[1024,128]{1,0:T(8,128)(2,1)S(1)} %collective-permute-done.1.refs_2_.refs_6_.refs_14_), channel_id=1, source_target_pairs={{0,4},{4,0},{8,12},{12,8},{16,20},{20,16},{24,28},{28,24},{1,5},{5... | collective-permute-start | bytes 786440 | tf_op jit(solution)/shard_map/ppermute | solution.py:496
  18.4 28.9 %copy-start.32 = (s32[128]{0:T(128)}, s32[128]{0:T(128)S(1)}, u32[]{:S(2)}) copy-start(s32[128]{0:T(128)S(1)} %fusion.1.cols) | copy-start | bytes 1540
  18.4 10.1 %collective-permute-start.15 = (bf16[1024,128]{1,0:T(8,128)(2,1)S(1)}, bf16[1024,128]{1,0:T(8,128)(2,1)S(1)}, u32[]{:S(2)}, u32[]{:S(2)}) collective-permute-start(bf16[1024,128]{1,0:T(8,128)(2,1)S(1)} %get-tuple-element.35.refs_0_.refs_12_.refs_20_), channel_id=1, source_target_pairs={{0,24},{4,28},{8,16},{12,20},{16,8},{20,12},{24,0},{28,4},{1,25},{... | collective-permute-start | bytes 786440 | tf_op jit(solution)/shard_map/ppermute | solution.py:496
  20.3 27.0 %copy-start.9 = (bf16[1024,128]{1,0:T(8,128)(2,1)}, bf16[1024,128]{1,0:T(8,128)(2,1)S(1)}, u32[]{:S(2)}) copy-start(bf16[1024,128]{1,0:T(8,128)(2,1)S(1)} %collective-permute-done.refs_1_.refs_5_.refs_13_) | copy-start | bytes 786436
  20.3 13.2 %collective-permute-start.13 = (bf16[1024,128]{1,0:T(8,128)(2,1)S(1)}, bf16[1024,128]{1,0:T(8,128)(2,1)S(1)}, u32[]{:S(2)}, u32[]{:S(2)}) collective-permute-start(bf16[1024,128]{1,0:T(8,128)(2,1)S(1)} %get-tuple-element.35.refs_0_.refs_12_.refs_20_), channel_id=1, source_target_pairs={{0,16},{4,20},{8,24},{12,28},{16,0},{20,4},{24,8},{28,12},{1,17},{... | collective-permute-start | bytes 786440 | tf_op jit(solution)/shard_map/ppermute | solution.py:496
  21.6 12.7 %collective-permute-start.11 = (bf16[1024,128]{1,0:T(8,128)(2,1)S(1)}, bf16[1024,128]{1,0:T(8,128)(2,1)}, u32[]{:S(2)}, u32[]{:S(2)}) collective-permute-start(bf16[1024,128]{1,0:T(8,128)(2,1)S(1)} %get-tuple-element.35.refs_0_.refs_12_.refs_20_), channel_id=1, source_target_pairs={{0,8},{4,12},{8,0},{12,4},{16,24},{20,28},{24,16},{28,20},{1,9},{5... | collective-permute-start | bytes 786440 | tf_op jit(solution)/shard_map/ppermute | solution.py:496
  26.4 17.3 %collective-permute-start.7 = (bf16[2048,128]{1,0:T(8,128)(2,1)S(1)}, bf16[2048,128]{1,0:T(8,128)(2,1)}, u32[]{:S(2)}, u32[]{:S(2)}) collective-permute-start(bf16[2048,128]{1,0:T(8,128)(2,1)S(1)} %partial_messages.5), channel_id=1, source_target_pairs={{0,1},{1,0},{2,3},{3,2},{4,5},{5,4},{6,7},{7,6},{8,9},{9,8},{10,11... | collective-permute-start | bytes 1572872 | tf_op jit(solution)/shard_map/ppermute | solution.py:500
  28.2 6.5 %collective-permute-start.10 = (bf16[1024,128]{1,0:T(8,128)(2,1)S(1)}, bf16[1024,128]{1,0:T(8,128)(2,1)}, u32[]{:S(2)}, u32[]{:S(2)}) collective-permute-start(bf16[1024,128]{1,0:T(8,128)(2,1)S(1)} %get-tuple-element.35.refs_0_.refs_12_.refs_20_), channel_id=1, source_target_pairs={{0,4},{4,0},{8,12},{12,8},{16,20},{20,16},{24,28},{28,24},{1,5},{5... | collective-permute-start | bytes 786440 | tf_op jit(solution)/shard_map/ppermute | solution.py:496
  28.5 6.2 %collective-permute-start.16 = (bf16[1024,128]{1,0:T(8,128)(2,1)S(1)}, bf16[1024,128]{1,0:T(8,128)(2,1)}, u32[]{:S(2)}, u32[]{:S(2)}) collective-permute-start(bf16[1024,128]{1,0:T(8,128)(2,1)S(1)} %collective-permute-done.15.refs_6_.refs_18_.refs_26_), channel_id=1, source_target_pairs={{0,4},{4,0},{8,12},{12,8},{16,20},{20,16},{24,28},{28,24},{1,5},{5... | collective-permute-start | bytes 786440 | tf_op jit(solution)/shard_map/ppermute | solution.py:496
  33.5 1.7 collective-permute-start.14
  34.3 1.9 collective-permute-start.12
  43.7 10.3 %collective-permute-start.17 = (bf16[1024,128]{1,0:T(8,128)(2,1)S(1)}, bf16[1024,128]{1,0:T(8,128)(2,1)S(1)}, u32[]{:S(2)}, u32[]{:S(2)}) collective-permute-start(bf16[1024,128]{1,0:T(8,128)(2,1)S(1)} %get-tuple-element.39), channel_id=1, source_target_pairs={{0,1},{1,0},{2,3},{3,2},{4,5},{5,4},{6,7},{7,6},{8,9},{9,8},{10,11... | collective-permute-start | bytes 786440 | tf_op jit(solution)/shard_map/ppermute | solution.py:500
  46.5 12.7 %collective-permute-start.8 = (bf16[2048,128]{1,0:T(8,128)(2,1)S(1)}, bf16[2048,128]{1,0:T(8,128)(2,1)S(1)}, u32[]{:S(2)}, u32[]{:S(2)}) collective-permute-start(bf16[2048,128]{1,0:T(8,128)(2,1)S(1)} %add_convert_fusion), channel_id=1, source_target_pairs={{0,0},{1,2},{2,1},{3,3},{4,4},{5,6},{6,5},{7,7},{8,8},{9,10},{10,9... | collective-permute-start | bytes 1572872 | tf_op jit(solution)/shard_map/ppermute | solution.py:508
  50.9 25.7 %copy-start.6 = (bf16[512,256]{1,0:T(8,128)(2,1)S(1)}, bf16[512,256]{1,0:T(8,128)(2,1)}, u32[]{:S(2)}) copy-start(bf16[512,256]{1,0:T(8,128)(2,1)} %w_in.1) | copy-start | bytes 786436
  50.9 25.7 %copy-start.27 = (bf16[256,256]{1,0:T(8,128)(2,1)S(1)}, bf16[256,256]{1,0:T(8,128)(2,1)}, u32[]{:S(2)}) copy-start(bf16[256,256]{1,0:T(8,128)(2,1)} %refs_8_.1) | copy-start | bytes 393220
  50.9 25.7 %copy-start.28 = (f32[256]{0:T(256)S(1)}, f32[256]{0:T(256)}, u32[]{:S(2)}) copy-start(f32[256]{0:T(256)} %param.15) | copy-start | bytes 3076
  50.9 25.7 %copy-start.29 = (f32[256]{0:T(256)S(1)}, f32[256]{0:T(256)}, u32[]{:S(2)}) copy-start(f32[256]{0:T(256)} %param.17) | copy-start | bytes 3076
  50.9 25.7 %copy-start.30 = (f32[256]{0:T(256)S(1)}, f32[256]{0:T(256)}, u32[]{:S(2)}) copy-start(f32[256]{0:T(256)} %param.18) | copy-start | bytes 3076
  54.0 11.2 %collective-permute-start.20 = (bf16[1024,128]{1,0:T(8,128)(2,1)S(1)}, bf16[1024,128]{1,0:T(8,128)(2,1)S(1)}, u32[]{:S(2)}, u32[]{:S(2)}) collective-permute-start(bf16[1024,128]{1,0:T(8,128)(2,1)S(1)} %get-tuple-element.41), channel_id=1, source_target_pairs={{0,1},{1,0},{2,3},{3,2},{4,5},{5,4},{6,7},{7,6},{8,9},{9,8},{10,11... | collective-permute-start | bytes 786440 | tf_op jit(solution)/shard_map/ppermute | solution.py:500
  58.5 9.0 %collective-permute-start.18 = (bf16[1024,128]{1,0:T(8,128)(2,1)S(1)}, bf16[1024,128]{1,0:T(8,128)(2,1)S(1)}, u32[]{:S(2)}, u32[]{:S(2)}) collective-permute-start(bf16[1024,128]{1,0:T(8,128)(2,1)S(1)} %add_convert_fusion.9), channel_id=1, source_target_pairs={{0,0},{1,2},{2,1},{3,3},{4,4},{5,6},{6,5},{7,7},{8,8},{9,10},{10,9... | collective-permute-start | bytes 786440 | tf_op jit(solution)/shard_map/ppermute | solution.py:508
  60.1 11.6 %collective-permute-start.9 = (bf16[1024,128]{1,0:T(8,128)(2,1)}, bf16[1024,128]{1,0:T(8,128)(2,1)S(1)}, u32[]{:S(2)}, u32[]{:S(2)}) collective-permute-start(bf16[1024,128]{1,0:T(8,128)(2,1)} %add_convert_fusion.10), channel_id=1, source_target_pairs={{0,1},{1,0},{2,3},{3,2},{4,5},{5,4},{6,7},{7,6},{8,9},{9,8},{10,11... | collective-permute-start | bytes 786440 | tf_op jit(solution)/shard_map/ppermute | solution.py:500
  66.0 5.7 %collective-permute-start.21 = (bf16[1024,128]{1,0:T(8,128)(2,1)}, bf16[1024,128]{1,0:T(8,128)(2,1)S(1)}, u32[]{:S(2)}, u32[]{:S(2)}) collective-permute-start(bf16[1024,128]{1,0:T(8,128)(2,1)} %add_convert_fusion.7), channel_id=1, source_target_pairs={{0,0},{1,2},{2,1},{3,3},{4,4},{5,6},{6,5},{7,7},{8,8},{9,10},{10,9... | collective-permute-start | bytes 786440 | tf_op jit(solution)/shard_map/ppermute | solution.py:508
  67.7 8.8 %collective-permute-start.19 = (bf16[1024,128]{1,0:T(8,128)(2,1)S(1)}, bf16[1024,128]{1,0:T(8,128)(2,1)S(1)}, u32[]{:S(2)}, u32[]{:S(2)}) collective-permute-start(bf16[1024,128]{1,0:T(8,128)(2,1)S(1)} %add_convert_fusion.8), channel_id=1, source_target_pairs={{0,1},{1,0},{2,3},{3,2},{4,5},{5,4},{6,7},{7,6},{8,9},{9,8},{10,11... | collective-permute-start | bytes 786440 | tf_op jit(solution)/shard_map/ppermute | solution.py:500
  84.7 10.4 %collective-permute-start.29 = (f32[448,256]{1,0:T(8,128)S(1)}, f32[448,256]{1,0:T(8,128)S(1)}, u32[]{:S(2)}, u32[]{:S(2)}) collective-permute-start(f32[448,256]{1,0:T(8,128)S(1)} %slice.83), channel_id=1, source_target_pairs={{0,4},{4,0},{8,12},{12,8},{16,20},{20,16},{24,28},{28,24},{1,5},{5... | collective-permute-start | bytes 1376264 | tf_op jit(solution)/shard_map/ppermute | solution.py:496
  84.8 8.9 %collective-permute-start.22 = (bf16[1024,128]{1,0:T(8,128)(2,1)}, bf16[1024,128]{1,0:T(8,128)(2,1)S(1)}, u32[]{:S(2)}, u32[]{:S(2)}) collective-permute-start(bf16[1024,128]{1,0:T(8,128)(2,1)} %get-tuple-element.49.refs_0_), channel_id=1, source_target_pairs={{0,1},{1,0},{2,3},{3,2},{4,5},{5,4},{6,7},{7,6},{8,9},{9,8},{10,11... | collective-permute-start | bytes 786440 | tf_op jit(solution)/shard_map/ppermute | solution.py:500
  86.6 10.2 %collective-permute-start.23 = (bf16[1024,128]{1,0:T(8,128)(2,1)}, bf16[1024,128]{1,0:T(8,128)(2,1)}, u32[]{:S(2)}, u32[]{:S(2)}) collective-permute-start(bf16[1024,128]{1,0:T(8,128)(2,1)} %get-tuple-element.49.refs_0_), channel_id=1, source_target_pairs={{0,0},{1,2},{2,1},{3,3},{4,4},{5,6},{6,5},{7,7},{8,8},{9,10},{10,9... | collective-permute-start | bytes 786440 | tf_op jit(solution)/shard_map/ppermute | solution.py:508
  93.7 6.9 %collective-permute-start.25 = (bf16[1024,128]{1,0:T(8,128)(2,1)S(1)}, bf16[1024,128]{1,0:T(8,128)(2,1)}, u32[]{:S(2)}, u32[]{:S(2)}) collective-permute-start(bf16[1024,128]{1,0:T(8,128)(2,1)S(1)} %collective-permute-done.22.refs_1_), channel_id=1, source_target_pairs={{0,0},{1,2},{2,1},{3,3},{4,4},{5,6},{6,5},{7,7},{8,8},{9,10},{10,9... | collective-permute-start | bytes 786440 | tf_op jit(solution)/shard_map/ppermute | solution.py:508
  95.2 13.7 %collective-permute-start.30 = (f32[224,256]{1,0:T(8,128)S(1)}, f32[224,256]{1,0:T(8,128)S(1)}, u32[]{:S(2)}, u32[]{:S(2)}) collective-permute-start(f32[224,256]{1,0:T(8,128)S(1)} %slice.107), channel_id=1, source_target_pairs={{0,8},{4,12},{8,0},{12,4},{16,24},{20,28},{24,16},{28,20},{1,9},{5... | collective-permute-start | bytes 688136 | tf_op jit(solution)/shard_map/ppermute | solution.py:496
  96.9 17.1 %collective-permute-start.24 = (bf16[1024,128]{1,0:T(8,128)(2,1)}, bf16[1024,128]{1,0:T(8,128)(2,1)S(1)}, u32[]{:S(2)}, u32[]{:S(2)}) collective-permute-start(bf16[1024,128]{1,0:T(8,128)(2,1)} %collective-permute-done.23.refs_2_), channel_id=1, source_target_pairs={{0,1},{1,0},{2,3},{3,2},{4,5},{5,4},{6,7},{7,6},{8,9},{9,8},{10,11... | collective-permute-start | bytes 786440 | tf_op jit(solution)/shard_map/ppermute | solution.py:500
  100.6 13.3 %collective-permute-start.28 = (bf16[1024,128]{1,0:T(8,128)(2,1)}, bf16[1024,128]{1,0:T(8,128)(2,1)S(1)}, u32[]{:S(2)}, u32[]{:S(2)}) collective-permute-start(bf16[1024,128]{1,0:T(8,128)(2,1)} %copy-done.23), channel_id=1, source_target_pairs={{0,0},{1,2},{2,1},{3,3},{4,4},{5,6},{6,5},{7,7},{8,8},{9,10},{10,9... | collective-permute-start | bytes 786440 | tf_op jit(solution)/shard_map/ppermute | solution.py:508
  102.2 14.0 %collective-permute-start.27 = (bf16[1024,128]{1,0:T(8,128)(2,1)}, bf16[1024,128]{1,0:T(8,128)(2,1)S(1)}, u32[]{:S(2)}, u32[]{:S(2)}) collective-permute-start(bf16[1024,128]{1,0:T(8,128)(2,1)} %copy-done.23), channel_id=1, source_target_pairs={{0,1},{1,0},{2,3},{3,2},{4,5},{5,4},{6,7},{7,6},{8,9},{9,8},{10,11... | collective-permute-start | bytes 786440 | tf_op jit(solution)/shard_map/ppermute | solution.py:500
  108.8 10.9 %collective-permute-start.26 = (bf16[1024,128]{1,0:T(8,128)(2,1)}, bf16[1024,128]{1,0:T(8,128)(2,1)S(1)}, u32[]{:S(2)}, u32[]{:S(2)}) collective-permute-start(bf16[1024,128]{1,0:T(8,128)(2,1)} %collective-permute-done.25.refs_4_), channel_id=1, source_target_pairs={{0,1},{1,0},{2,3},{3,2},{4,5},{5,4},{6,7},{7,6},{8,9},{9,8},{10,11... | collective-permute-start | bytes 786440 | tf_op jit(solution)/shard_map/ppermute | solution.py:500
  109.0 4.9 %collective-permute-start.31 = (f32[112,256]{1,0:T(8,128)S(1)}, f32[112,256]{1,0:T(8,128)S(1)}, u32[]{:S(2)}, u32[]{:S(2)}) collective-permute-start(f32[112,256]{1,0:T(8,128)S(1)} %slice.109), channel_id=1, source_target_pairs={{0,16},{4,20},{8,24},{12,28},{16,0},{20,4},{24,8},{28,12},{1,17},{... | collective-permute-start | bytes 344072 | tf_op jit(solution)/shard_map/ppermute | solution.py:496
  113.9 25.9 %copy-start.8 = (bf16[1024,128]{1,0:T(8,128)(2,1)S(1)}, bf16[1024,128]{1,0:T(8,128)(2,1)}, u32[]{:S(2)}) copy-start(bf16[1024,128]{1,0:T(8,128)(2,1)} %copy-done.7) | copy-start | bytes 786436
  113.9 25.9 %copy-start.10 = (bf16[1024,128]{1,0:T(8,128)(2,1)S(1)}, bf16[1024,128]{1,0:T(8,128)(2,1)}, u32[]{:S(2)}) copy-start(bf16[1024,128]{1,0:T(8,128)(2,1)} %copy-done.9) | copy-start | bytes 786436
  113.9 25.9 %copy-start.12 = (bf16[1024,128]{1,0:T(8,128)(2,1)S(1)}, bf16[1024,128]{1,0:T(8,128)(2,1)}, u32[]{:S(2)}) copy-start(bf16[1024,128]{1,0:T(8,128)(2,1)} %copy-done.11) | copy-start | bytes 786436
  113.9 25.9 %copy-start.14 = (bf16[1024,128]{1,0:T(8,128)(2,1)S(1)}, bf16[1024,128]{1,0:T(8,128)(2,1)}, u32[]{:S(2)}) copy-start(bf16[1024,128]{1,0:T(8,128)(2,1)} %copy-done.13) | copy-start | bytes 786436
  113.9 25.9 %copy-start.16 = (bf16[1024,128]{1,0:T(8,128)(2,1)S(1)}, bf16[1024,128]{1,0:T(8,128)(2,1)}, u32[]{:S(2)}) copy-start(bf16[1024,128]{1,0:T(8,128)(2,1)} %copy-done.15) | copy-start | bytes 786436
  113.9 25.9 %copy-start.19 = (bf16[1024,128]{1,0:T(8,128)(2,1)S(1)}, bf16[1024,128]{1,0:T(8,128)(2,1)}, u32[]{:S(2)}) copy-start(bf16[1024,128]{1,0:T(8,128)(2,1)} %copy-done.17) | copy-start | bytes 786436
  113.9 25.9 %copy-start.22 = (bf16[1024,128]{1,0:T(8,128)(2,1)S(1)}, bf16[1024,128]{1,0:T(8,128)(2,1)}, u32[]{:S(2)}) copy-start(bf16[1024,128]{1,0:T(8,128)(2,1)} %copy-done.20) | copy-start | bytes 786436
  114.0 25.9 %copy-start.24 = (bf16[1024,128]{1,0:T(8,128)(2,1)S(1)}, bf16[1024,128]{1,0:T(8,128)(2,1)}, u32[]{:S(2)}) copy-start(bf16[1024,128]{1,0:T(8,128)(2,1)} %copy-done.23) | copy-start | bytes 786436
  125.1 21.8 %collective-permute-start.32 = (bf16[4096,128]{1,0:T(8,128)(2,1)S(1)}, bf16[4096,128]{1,0:T(8,128)(2,1)S(1)}, u32[]{:S(2)}, u32[]{:S(2)}) collective-permute-start(bf16[4096,128]{1,0:T(8,128)(2,1)S(1)} %get-tuple-element.54.refs_20_), channel_id=1, source_target_pairs={{0,4},{4,0},{8,12},{12,8},{16,20},{20,16},{24,28},{28,24},{1,5},{5... | collective-permute-start | bytes 3145736 | tf_op jit(solution)/shard_map/ppermute | solution.py:496
  125.1 5.6 %collective-permute-start.39 = (f32[112,256]{1,0:T(8,128)S(1)}, f32[112,256]{1,0:T(8,128)S(1)}, u32[]{:S(2)}, u32[]{:S(2)}) collective-permute-start(f32[112,256]{1,0:T(8,128)S(1)} %slice_add_fusion.2.refs_9_), channel_id=1, source_target_pairs={{0,1},{1,0},{2,3},{3,2},{4,5},{5,4},{6,7},{7,6},{8,9},{9,8},{10,11... | collective-permute-start | bytes 344072 | tf_op jit(solution)/shard_map/ppermute | solution.py:500
  130.7 7.9 %collective-permute-start.40 = (f32[112,256]{1,0:T(8,128)S(1)}, f32[112,256]{1,0:T(8,128)S(1)}, u32[]{:S(2)}, u32[]{:S(2)}) collective-permute-start(f32[112,256]{1,0:T(8,128)S(1)} %add.102), channel_id=1, source_target_pairs={{0,3},{3,0},{1,2},{2,1},{4,7},{7,4},{5,6},{6,5},{8,11},{11,8},{9,1... | collective-permute-start | bytes 344072 | tf_op jit(solution)/shard_map/ppermute | solution.py:504
  133.6 13.5 %collective-permute-start.36 = (bf16[1024,128]{1,0:T(8,128)(2,1)S(1)}, bf16[1024,128]{1,0:T(8,128)(2,1)S(1)}, u32[]{:S(2)}, u32[]{:S(2)}) collective-permute-start(bf16[1024,128]{1,0:T(8,128)(2,1)S(1)} %collective-permute-done.28.refs_8_.refs_2_), channel_id=1, source_target_pairs={{0,1},{1,0},{2,3},{3,2},{4,5},{5,4},{6,7},{7,6},{8,9},{9,8},{10,11... | collective-permute-start | bytes 786440 | tf_op jit(solution)/shard_map/ppermute | solution.py:500
  133.6 12.1 %collective-permute-start.37 = (bf16[1024,128]{1,0:T(8,128)(2,1)S(1)}, bf16[1024,128]{1,0:T(8,128)(2,1)S(1)}, u32[]{:S(2)}, u32[]{:S(2)}) collective-permute-start(bf16[1024,128]{1,0:T(8,128)(2,1)S(1)} %collective-permute-done.27.refs_7_.refs_3_.refs_1_), channel_id=1, source_target_pairs={{0,0},{1,2},{2,1},{3,3},{4,4},{5,6},{6,5},{7,7},{8,8},{9,10},{10,9... | collective-permute-start | bytes 786440 | tf_op jit(solution)/shard_map/ppermute | solution.py:508
  138.7 8.0 %collective-permute-start.45 = (bf16[112,256]{1,0:T(8,128)(2,1)S(1)}, bf16[112,256]{1,0:T(8,128)(2,1)S(1)}, u32[]{:S(2)}, u32[]{:S(2)}) collective-permute-start(bf16[112,256]{1,0:T(8,128)(2,1)S(1)} %get-tuple-element.72), channel_id=1, source_target_pairs={{0,16},{4,20},{8,24},{12,28},{16,0},{20,4},{24,8},{28,12},{1,17},{... | collective-permute-start | bytes 172040 | tf_op jit(solution)/shard_map/ppermute | solution.py:496
  145.7 6.4 %collective-permute-start.38 = (bf16[1024,128]{1,0:T(8,128)(2,1)S(1)}, bf16[1024,128]{1,0:T(8,128)(2,1)S(1)}, u32[]{:S(2)}, u32[]{:S(2)}) collective-permute-start(bf16[1024,128]{1,0:T(8,128)(2,1)S(1)} %collective-permute-done.37.refs_4_.refs_10_), channel_id=1, source_target_pairs={{0,1},{1,0},{2,3},{3,2},{4,5},{5,4},{6,7},{7,6},{8,9},{9,8},{10,11... | collective-permute-start | bytes 786440 | tf_op jit(solution)/shard_map/ppermute | solution.py:500
  146.7 13.2 %collective-permute-start.46 = (bf16[224,256]{1,0:T(8,128)(2,1)S(1)}, bf16[224,256]{1,0:T(8,128)(2,1)S(1)}, u32[]{:S(2)}, u32[]{:S(2)}) collective-permute-start(bf16[224,256]{1,0:T(8,128)(2,1)S(1)} %pad_maximum_fusion.2), channel_id=1, source_target_pairs={{0,8},{4,12},{8,0},{12,4},{16,24},{20,28},{24,16},{28,20},{1,9},{5... | collective-permute-start | bytes 344072 | tf_op jit(solution)/shard_map/ppermute | solution.py:496
  159.8 15.7 %collective-permute-start.41 = (bf16[4096,128]{1,0:T(8,128)(2,1)S(1)}, bf16[4096,128]{1,0:T(8,128)(2,1)S(1)}, u32[]{:S(2)}, u32[]{:S(2)}) collective-permute-start(bf16[4096,128]{1,0:T(8,128)(2,1)S(1)} %get-tuple-element.56), channel_id=1, source_target_pairs={{0,4},{4,0},{8,12},{12,8},{16,20},{20,16},{24,28},{28,24},{1,5},{5... | collective-permute-start | bytes 3145736 | tf_op jit(solution)/shard_map/ppermute | solution.py:496
  159.9 4.0 %collective-permute-start.47 = (bf16[448,256]{1,0:T(8,128)(2,1)S(1)}, bf16[448,256]{1,0:T(8,128)(2,1)S(1)}, u32[]{:S(2)}, u32[]{:S(2)}) collective-permute-start(bf16[448,256]{1,0:T(8,128)(2,1)S(1)} %pad_maximum_fusion.1), channel_id=1, source_target_pairs={{0,4},{4,0},{8,12},{12,8},{16,20},{20,16},{24,28},{28,24},{1,5},{5... | collective-permute-start | bytes 688136 | tf_op jit(solution)/shard_map/ppermute | solution.py:496
  160.5 10.1 %collective-permute-start.35 = (bf16[1024,128]{1,0:T(8,128)(2,1)S(1)}, bf16[1024,128]{1,0:T(8,128)(2,1)S(1)}, u32[]{:S(2)}, u32[]{:S(2)}) collective-permute-start(bf16[1024,128]{1,0:T(8,128)(2,1)S(1)} %get-tuple-element.77.refs_9_), channel_id=1, source_target_pairs={{0,24},{4,28},{8,16},{12,20},{16,8},{20,12},{24,0},{28,4},{1,25},{... | collective-permute-start | bytes 786440 | tf_op jit(solution)/shard_map/ppermute | solution.py:496
  162.0 13.3 %collective-permute-start.34 = (bf16[1024,128]{1,0:T(8,128)(2,1)S(1)}, bf16[1024,128]{1,0:T(8,128)(2,1)S(1)}, u32[]{:S(2)}, u32[]{:S(2)}) collective-permute-start(bf16[1024,128]{1,0:T(8,128)(2,1)S(1)} %get-tuple-element.78.refs_8_), channel_id=1, source_target_pairs={{0,16},{4,20},{8,24},{12,28},{16,0},{20,4},{24,8},{28,12},{1,17},{... | collective-permute-start | bytes 786440 | tf_op jit(solution)/shard_map/ppermute | solution.py:496
  162.3 13.0 %collective-permute-start.33 = (bf16[1024,128]{1,0:T(8,128)(2,1)S(1)}, bf16[1024,128]{1,0:T(8,128)(2,1)S(1)}, u32[]{:S(2)}, u32[]{:S(2)}) collective-permute-start(bf16[1024,128]{1,0:T(8,128)(2,1)S(1)} %get-tuple-element.79.refs_7_), channel_id=1, source_target_pairs={{0,8},{4,12},{8,0},{12,4},{16,24},{20,28},{24,16},{28,20},{1,9},{5... | collective-permute-start | bytes 786440 | tf_op jit(solution)/shard_map/ppermute | solution.py:496
  175.7 9.2 %collective-permute-start.42 = (bf16[1024,128]{1,0:T(8,128)(2,1)S(1)}, bf16[1024,128]{1,0:T(8,128)(2,1)S(1)}, u32[]{:S(2)}, u32[]{:S(2)}) collective-permute-start(bf16[1024,128]{1,0:T(8,128)(2,1)S(1)} %get-tuple-element.74.refs_29_), channel_id=1, source_target_pairs={{0,8},{4,12},{8,0},{12,4},{16,24},{20,28},{24,16},{28,20},{1,9},{5... | collective-permute-start | bytes 786440 | tf_op jit(solution)/shard_map/ppermute | solution.py:496
  176.4 13.1 %collective-permute-start.44 = (bf16[1024,128]{1,0:T(8,128)(2,1)S(1)}, bf16[1024,128]{1,0:T(8,128)(2,1)S(1)}, u32[]{:S(2)}, u32[]{:S(2)}) collective-permute-start(bf16[1024,128]{1,0:T(8,128)(2,1)S(1)} %get-tuple-element.75.refs_31_), channel_id=1, source_target_pairs={{0,24},{4,28},{8,16},{12,20},{16,8},{20,12},{24,0},{28,4},{1,25},{... | collective-permute-start | bytes 786440 | tf_op jit(solution)/shard_map/ppermute | solution.py:496
  177.8 13.1 %collective-permute-start.43 = (bf16[1024,128]{1,0:T(8,128)(2,1)S(1)}, bf16[1024,128]{1,0:T(8,128)(2,1)S(1)}, u32[]{:S(2)}, u32[]{:S(2)}) collective-permute-start(bf16[1024,128]{1,0:T(8,128)(2,1)S(1)} %get-tuple-element.76.refs_30_), channel_id=1, source_target_pairs={{0,16},{4,20},{8,24},{12,28},{16,0},{20,4},{24,8},{28,12},{1,17},{... | collective-permute-start | bytes 786440 | tf_op jit(solution)/shard_map/ppermute | solution.py:496
  (27 other events, 246.0 us)

commit v5 on v4

--- a/solution.py
+++ b/solution.py
@@ -10,6 +10,7 @@
 F32 = jnp.float32
 BF16 = jnp.bfloat16
 ANY = pl.BlockSpec(memory_space=pl.ANY)
+HBM = pl.BlockSpec(memory_space=pltpu.HBM)
 SMEM = pl.BlockSpec(memory_space=pltpu.SMEM)
 VMEM = pl.BlockSpec(memory_space=pltpu.VMEM)
 MIB = 1 << 20
@@ -52,7 +53,11 @@
     return copies
 
 
-def forward_kernel(outputs, n_pieces, cols, order, *refs):
+def masked_tile(tile, live):
+    return jnp.where(live, tile, jnp.zeros_like(tile))
+
+
+def forward_kernel(outputs, n_pieces, cols, counts, order, *refs):
     pieces, tiles = refs[:n_pieces], refs[n_pieces]
     outs = refs[n_pieces + 1 : n_pieces + 1 + len(outputs)]
     nodes_v, tiles_v, sem, tile_sem = refs[n_pieces + 1 + len(outputs) :]
@@ -78,10 +83,13 @@
 
         def step(i, carry, first=first, out=out, index=index, place=place):
             row = first + i
+            count = counts[row]
             parts = []
             for pair in range(slots // 2):
                 both = (2 * pair, 2 * pair + 1)
-                tile = jnp.concatenate([tiles_v[place * blocks + i, slot] for slot in both], axis=1)
+                tile = jnp.concatenate(
+                    [masked_tile(tiles_v[place * blocks + i, slot], slot < count) for slot in both], axis=1
+                )
                 node = jnp.concatenate(
                     [nodes_v[block_at(cols[row * slots + slot], block)] for slot in both], axis=0
                 )
@@ -95,7 +103,7 @@
         lax.fori_loop(0, blocks, step, 0, unroll=4)
 
 
-def forward_call(cols, order, pieces, tiles, outputs, rows):
+def forward_call(cols, counts, order, pieces, tiles, outputs, rows):
     width = pieces[0].shape[1]
     gathered = sum(piece.shape[0] for piece in pieces)
     slots, block = tiles.shape[1], tiles.shape[2]
@@ -103,7 +111,7 @@
     return pl.pallas_call(
         functools.partial(forward_kernel, outputs, len(pieces)),
         out_shape=[jax.ShapeDtypeStruct((len(picks) * rows, width), BF16) for picks in outputs],
-        in_specs=[SMEM, SMEM] + [ANY] * (len(pieces) + 1),
+        in_specs=[SMEM] * 3 + [ANY] * len(pieces) + [HBM],
         out_specs=[VMEM] * len(outputs),
         scratch_shapes=[
             pltpu.VMEM((gathered, width), BF16),
@@ -114,10 +122,31 @@
         compiler_params=params(16 if gathered <= 8192 else 40),
         cost_estimate=cost(2.0),
         name="partial_messages",
-    )(cols, order, *pieces, tiles)
-
-
-def mlp_kernel(kinds, middle, nodes, cot, *refs):
+    )(cols, counts, order, *pieces, tiles)
+
+
+def mlp_kernel(kinds, middle, nodes_ref, cot_ref, *refs):
+    nodes_v, cot_v, sem = refs[-3:]
+    refs = refs[:-3]
+    step = pl.program_id(0)
+    rows = nodes_v.shape[1]
+
+    def loads(index):
+        where = block_at(index, rows)
+        return (
+            pltpu.make_async_copy(nodes_ref.at[where], nodes_v.at[index], sem.at[0, index]),
+            pltpu.make_async_copy(cot_ref.at[where], cot_v.at[index], sem.at[1, index]),
+        )
+
+    @pl.when(step == 0)
+    def _():
+        for index in range(nodes_v.shape[0]):
+            for copy in loads(index):
+                copy.start()
+
+    for copy in loads(step):
+        copy.wait()
+    nodes, cot = nodes_v.at[step], cot_v.at[step]
     n_parts = sum(len(chunk) for chunk in kinds)
     parts = refs[:n_parts]
     w_in, bias, w_out, gain, shift, updated, gpre_o, act_o, gproj_o, msg_o, vec = refs[
@@ -198,9 +227,14 @@
         functools.partial(mlp_kernel, kinds),
         grid=(rows // step,),
         out_shape=outs,
-        in_specs=[SMEM] + [blocked(a) for a in (nodes, cot, *flat)] + [whole(a) for a in weights],
+        in_specs=[SMEM, HBM, HBM] + [blocked(a) for a in flat] + [whole(a) for a in weights],
         out_specs=[blocked(a) for a in outs[:5]] + [whole(outs[5])] + [blocked(a) for a in outs[6:]],
-        compiler_params=params(20),
+        scratch_shapes=[
+            pltpu.VMEM((rows // step, step, width), BF16),
+            pltpu.VMEM((rows // step, step, width), BF16),
+            pltpu.SemaphoreType.DMA((2, rows // step)),
+        ],
+        compiler_params=params(24),
         cost_estimate=cost(5.0),
         name="mlp",
     )(middle, nodes, cot, *flat, *weights)
@@ -366,7 +400,7 @@
     return pl.pallas_call(
         functools.partial(back_kernel, rows, slots, len(grads), len(after), out_pieces),
         out_shape=[jax.ShapeDtypeStruct((len(m) * piece, width), BF16) for m in out_pieces],
-        in_specs=[SMEM] * 4 + [ANY] * (len(grads) + 1 + len(after)),
+        in_specs=[SMEM] * 4 + [ANY] * len(grads) + [HBM] + [ANY] * len(after),
         out_specs=[VMEM] * len(out_pieces),
         scratch_shapes=[
             pltpu.VMEM((total, width), BF16),
@@ -376,7 +410,7 @@
             pltpu.SemaphoreType.DMA((len(grads),)),
             pltpu.SemaphoreType.DMA((1,)),
         ],
-        compiler_params=params(24 if gathered <= 8192 else 56),
+        compiler_params=params(28 if gathered <= 8192 else 56),
         cost_estimate=cost(5.0),
         name="back_terms",
     )(cols, counts, order, middle, *grads, tiles.reshape(row_blocks * slots, block, block), *after)
@@ -557,15 +591,6 @@
     return own, pair_in, near_sum
 
 
-def reduce_line_joint(both, pair, own, inner):
-    rows = own.shape[0]
-    both_in = outer_swap(both)
-    both_sum = inner_swap(add(both, both_in))
-    far_sum = both_sum[:rows]
-    pair_in = outer_swap(add(pair, jnp.where(inner, far_sum, jnp.zeros_like(far_sum))))
-    return (own, pair_in, both_sum[rows:]), both_in
-
-
 def gather_line(own):
     pair = outer_swap(own)
     near_inner = inner_swap(own)
@@ -584,8 +609,6 @@
     blocks = rows // block
     gathered, total = n_row * rows, n_col * rows
     square_line = n_row == 8 and n_col == 4
-    live = lax.broadcasted_iota(jnp.int32, (row_blocks, slots), 1) < counts[:, None]
-    tile_live = jnp.where(live[:, :, None, None], tile_local, jnp.zeros_like(tile_local))
     if square_line:
         mine = lax.axis_index("row").astype(jnp.int32)
         cols = ((cols // blocks) ^ mine) * blocks + cols % blocks
@@ -594,22 +617,16 @@
         order = jnp.stack([jnp.where(low, 3, 0), jnp.where(low, 2, 1), level ^ 1, level]).astype(jnp.int32)
         inner = (level == 1) | (level == 2)
         middle = inner.astype(jnp.int32).reshape(1)
-        part = width // 2
-        left = gather_square(nodes[:, :part])
-        right = gather_square(held(nodes[:, part:], left[2], left[4], left[6]))
-        pieces = [left, right]
-        (both,) = forward_call(cols, order, left, tile_live, ((0, 1),), rows)
-        pair, own = forward_call(cols, order, left, tile_live, ((2,), (3,)), rows)
-        left_parts, both_in = reduce_line_joint(both, pair, own, inner)
-        far, near = forward_call(cols, order, right, tile_live, ((0,), (1,)), rows)
-        pair, own = forward_call(cols, order, right, tile_live, ((2,), (3,)), rows)
-        parts = [left_parts, reduce_line(held(far, both_in), near, pair, own, inner)]
-        kinds = [("all", "all", "inner")] * 2
+        pieces = [gather_square(nodes)]
+        far, near = forward_call(cols, counts, order, pieces[0], tile_local, ((0,), (1,)), rows)
+        pair, own = forward_call(cols, counts, order, pieces[0], tile_local, ((2,), (3,)), rows)
+        parts = [reduce_line(far, near, pair, own, inner)]
+        kinds = [("all", "all", "inner")]
     else:
         order = jnp.arange(n_col, dtype=jnp.int32)
         middle = jnp.zeros((1,), jnp.int32)
         pieces = [[lax.all_gather(nodes, "row", axis=0, tiled=True)]]
-        (partial,) = forward_call(cols, order, pieces[0], tile_live, (tuple(range(n_col)),), rows)
+        (partial,) = forward_call(cols, counts, order, pieces[0], tile_local, (tuple(range(n_col)),), rows)
         parts = [[lax.psum_scatter(partial, "col", scatter_dimension=0, tiled=True)]]
         kinds = [("all",)]
     vectors = [v.reshape(1, width) for v in (bias_in, ln_gain, ln_shift)]
@@ -623,31 +640,18 @@
     )
     if square_line:
         halves = ((1, 3, 5, 7), (0, 2, 4, 6))
-        first = gather_line(gmsgs[0])
-        second = gather_line(held(gmsgs[1], first[4]))
-        grads = [first, second]
-        row_weights = scatter_weights(weight_terms)
+        grads = [gather_line(gmsgs[0])]
+        near_grads = tile_grad_call(
+            cols, counts, order, middle, [grads[0][:2]], pieces, tile_local.shape, rows, (3, 2)
+        )
+        all_weights = level_weights(scatter_weights(weight_terms))
         odd, even = back_call(
-            cols, counts, order, middle, first, tile_live, total, gathered, halves,
-            (second[1], second[2], row_weights),
+            cols, counts, order, middle, grads[0], tile_local, total, gathered, halves, (all_weights, near_grads)
         )
         own_terms, sums = pair_sums(even, odd, rows)
-        near_grads = tile_grad_call(
-            cols, counts, order, middle, [chunk[:2] for chunk in grads], pieces, tile_local.shape, rows, (3, 2),
-            after=(odd,),
-        )
-        all_weights = level_weights(row_weights)
-        odd, even = back_call(
-            cols, counts, order, middle, second, tile_live, total, gathered, halves,
-            (*sums, all_weights, near_grads),
-        )
-        left_terms = (*own_terms, *reduce_square(sums))
-        own_terms, sums = pair_sums(even, odd, rows)
-        right_terms = (*own_terms, *reduce_square(sums))
+        terms = (*own_terms, *reduce_square(sums))
         weights = gather_weights(all_weights, width, mine)
-        back = jnp.concatenate(
-            [sum(term.astype(F32) for term in terms) for terms in (left_terms, right_terms)], axis=1
-        )
+        back = sum(term.astype(F32) for term in terms)
         grad_tiles = tile_grad_call(
             cols, counts, order, middle, grads, pieces, tile_local.shape, rows, (1, 0), near_grads, sums
         )
@@ -660,7 +664,7 @@
             weight_sums[3 * width : 3 * width + 3],
         )
         (terms,) = back_call(
-            cols, counts, order, middle, grads[0], tile_live, total, gathered, (tuple(range(n_row)),)
+            cols, counts, order, middle, grads[0], tile_local, total, gathered, (tuple(range(n_row)),)
         )
         back = lax.psum_scatter(terms, "row", scatter_dimension=0, tiled=True).astype(F32)
         grad_tiles = tile_grad_call(

time: 193 us -> 204 us (1.057)
  waiting for transfers between devices: 58.5 us -> 98 us
  starting transfers between devices: 63.4 us -> 51.2 us
  Pallas kernels: 40.2 us -> 30.3 us
  other arithmetic: 12.8 us -> 5.87 us
    ppermute x28 -> x17, waiting for transfers between devices: 29.2 us -> 52 us  [swap(): return lax.ppermute(value, 'row', [(i, i ^ bit) for i in range(8)])]
    ppermute x12 -> x7, waiting for transfers between devices: 24.9 us -> 39.3 us  [outer_swap(): return lax.ppermute(value, 'col', [(0, 1), (1, 0), (2, 3), (3, 2)])]
    select_n x2 -> x0, other arithmetic: 7.11 us -> none  [body(): jnp.where(live[:, :, None, None], tile_local, jnp.zeros_like(tile_local))]
    ppermute x12 -> x7, starting transfers between devices: 29 us -> 22 us  [outer_swap(): return lax.ppermute(value, 'col', [(0, 1), (1, 0), (2, 3), (3, 2)])]
    pallas_call x2 -> x1, Pallas kernels: 10.8 us -> 4.48 us  [back_call(): pl.pallas_call(functools.partial(back_kernel, rows, slots, len(grads), le...]
    ppermute x28 -> x17, starting transfers between devices: 21.4 us -> 15.8 us  [swap(): return lax.ppermute(value, 'row', [(i, i ^ bit) for i in range(8)])]
    pallas_call x4 -> x2, Pallas kernels: 10.7 us -> 7.19 us  [forward_call(): pl.pallas_call(functools.partial(forward_kernel, outputs, len(pieces)), o...]
    pallas_call x2, Pallas kernels: 11.4 us -> 8.88 us  [tile_grad_call(): pl.pallas_call(functools.partial(tile_grad_kernel, rows, slots, len(grads...]
  transfers between devices with their start and end apart: 48 -> 29, of which waited for: 20 -> 17; matrix products, arithmetic and copies ran while one was open for 7% -> 2% of each run, Pallas kernels for 15% -> 6%
where the time goes in v5:
time: 204 us; the launch traced here: 202 us
  waiting for transfers between devices  98 us (48%)
  starting transfers between devices  51.2 us (25%)
  Pallas kernels  30.3 us (15%)
  local copies, waits for them, and re-layouts  15.5 us (8%)
  other arithmetic  5.87 us (3%)
    ppermute x17, waiting for transfers between devices, swap(): return lax.ppermute(value, 'row', [(i, i ^ bit) for i in range(8)])  52 us
    ppermute x7, waiting for transfers between devices, outer_swap(): return lax.ppermute(value, 'col', [(0, 1), (1, 0), (2, 3), (3, 2)])  39.3 us
    ppermute x7, starting transfers between devices, outer_swap(): return lax.ppermute(value, 'col', [(0, 1), (1, 0), (2, 3), (3, 2)])  22 us
    ppermute x17, starting transfers between devices, swap(): return lax.ppermute(value, 'row', [(i, i ^ bit) for i in range(8)])  15.8 us
    unnamed x41, local copies, waits for them, and re-layouts  15.4 us
    ppermute x4, starting transfers between devices, inner_swap(): return lax.ppermute(value, 'col', [(0, 0), (1, 2), (2, 1), (3, 3)])  12.1 us
    pallas_call x2, Pallas kernels, tile_grad_call(): pl.pallas_call(functools.partial(tile_grad_kernel, rows, slots, len(grads...  8.88 us
    pallas_call x1, Pallas kernels, mlp_call(): pl.pallas_call(functools.partial(mlp_kernel, kinds), grid=(rows // step,)...  7.2 us
  transfers between devices with their start and end apart: 29, of which 17 were waited for; matrix products, arithmetic and copies ran while one was open for 2% of the time, Pallas kernels for 6%

profile of v5, /device:TPU:0, one launch (start us, length us, event | category | flops | bytes accessed | tf_op | source)
XLA Modules:
  0.0 201.8 jit_solution(5592112308555772330)
XLA Ops:
  0.6 3.0 %collective-permute-start.1 = (bf16[1024,256]{1,0:T(8,128)(2,1)}, bf16[1024,256]{1,0:T(8,128)(2,1)S(1)}, u32[]{:S(2)}, u32[]{:S(2)}) collective-permute-start(bf16[1024,256]{1,0:T(8,128)(2,1)} %refs_6_.1), channel_id=1, source_target_pairs={{0,8},{4,12},{8,0},{12,4},{16,24},{20,28},{24,16},{28,20},{1,9},{5... | collective-permute-start | bytes 1572872 | tf_op jit(solution)/shard_map/ppermute | solution.py:530
  3.6 1.5 collective-permute-start.3
  5.2 11.4 %collective-permute-done.1.refs_2_.refs_4_.refs_8_ = bf16[1024,256]{1,0:T(8,128)(2,1)S(1)} collective-permute-done((bf16[1024,256]{1,0:T(8,128)(2,1)}, bf16[1024,256]{1,0:T(8,128)(2,1)S(1)}, u32[]{:S(2)}, u32[]{:S(2)}) %collective-permute-start.1) | collective-permute-done | bytes 524320 | tf_op jit(solution)/shard_map/ppermute | solution.py:530
  16.6 11.9 %collective-permute-done.3.refs_4_.refs_6_.refs_10_ = bf16[1024,256]{1,0:T(8,128)(2,1)S(1)} collective-permute-done((bf16[1024,256]{1,0:T(8,128)(2,1)}, bf16[1024,256]{1,0:T(8,128)(2,1)S(1)}, u32[]{:S(2)}, u32[]{:S(2)}) %collective-permute-start.3) | collective-permute-done | bytes 524320 | tf_op jit(solution)/shard_map/ppermute | solution.py:530
  28.5 0.5 collective-permute-start.6
  29.0 0.8 copy.19
  29.7 0.1 reshape.43
  30.0 1.1 collective-permute-done.4.refs_5_.refs_7_.refs_11_
  31.0 0.8 copy-done.3
  31.8 1.0 copy-done.1
  32.9 1.0 copy-done.4
  33.9 0.7 copy-done.7
  34.6 2.2 %copy-done.9 = bf16[32,1,4,128,128]{4,3,2,1,0:T(8,128)(2,1)S(1)} copy-done((bf16[32,1,4,128,128]{4,3,2,1,0:T(8,128)(2,1)S(1)}, bf16[32,1,4,128,128]{4,3,2,1,0:T(8,128)(2,1)}, u32[]{:S(2)}) %copy-start.9) | copy-done | bytes 4194328
  36.8 4.0 %partial_messages.3 = (bf16[1024,256]{1,0:T(8,128)(2,1)S(1)}, bf16[1024,256]{1,0:T(8,128)(2,1)}) custom-call(s32[128]{0:T(128)S(1)} %fusion.cols, s32[32]{0:T(128)S(1)} %bitcast.18, s32[4]{0:T(128)S(1)} %pad_add_fusion.order, bf16[1024,256]{1,0:T(8,128)(2,1)S(1)} %copy-done.1, bf16[1024,256]{1,0:T(8,128)(2,1)S(1)} %collective-permute-done.refs_1_.refs_3_.refs_7_, ...), custom_call_target="tpu_custom_call" | custom-call | flops 2307000064 | bytes 1048576 | tf_op jit(solution)/shard_map/partial_messages/pallas_call | solution.py:111
  40.8 1.6 collective-permute-start.7
  42.4 12.4 %collective-permute-done.7 = bf16[1024,256]{1,0:T(8,128)(2,1)S(1)} collective-permute-done((bf16[1024,256]{1,0:T(8,128)(2,1)S(1)}, bf16[1024,256]{1,0:T(8,128)(2,1)S(1)}, u32[]{:S(2)}, u32[]{:S(2)}) %collective-permute-start.7) | collective-permute-done | bytes 524320 | tf_op jit(solution)/shard_map/ppermute | solution.py:534
  54.8 0.9 add_convert_fusion.6
  55.8 5.4 %collective-permute-start.8 = (bf16[1024,256]{1,0:T(8,128)(2,1)}, bf16[1024,256]{1,0:T(8,128)(2,1)}, u32[]{:S(2)}, u32[]{:S(2)}) collective-permute-start(bf16[1024,256]{1,0:T(8,128)(2,1)} %add_convert_fusion.6), channel_id=1, source_target_pairs={{0,0},{1,2},{2,1},{3,3},{4,4},{5,6},{6,5},{7,7},{8,8},{9,10},{10,9... | collective-permute-start | bytes 1572872 | tf_op jit(solution)/shard_map/ppermute | solution.py:542
  61.1 1.0 copy-done.5
  62.2 2.2 %copy-done.10 = bf16[32,1,4,128,128]{4,3,2,1,0:T(8,128)(2,1)S(1)} copy-done((bf16[32,1,4,128,128]{4,3,2,1,0:T(8,128)(2,1)S(1)}, bf16[32,1,4,128,128]{4,3,2,1,0:T(8,128)(2,1)}, u32[]{:S(2)}) %copy-start.10) | copy-done | bytes 4194328
  64.4 3.2 %partial_messages.2 = (bf16[1024,256]{1,0:T(8,128)(2,1)S(1)}, bf16[1024,256]{1,0:T(8,128)(2,1)S(1)}) custom-call(s32[128]{0:T(128)S(1)} %fusion.cols, s32[32]{0:T(128)S(1)} %bitcast.19, s32[4]{0:T(128)S(1)} %pad_add_fusion.order, bf16[1024,256]{1,0:T(8,128)(2,1)S(1)} %copy-done.2, bf16[1024,256]{1,0:T(8,128)(2,1)S(1)} %collective-permute-done.refs_1_.refs_3_.refs_7_, ...), custom_call_target="tpu_custom_call" | custom-call | flops 2307000064 | bytes 1048576 | tf_op jit(solution)/shard_map/partial_messages/pallas_call | solution.py:111
  67.6 1.0 add_convert_fusion.5
  68.6 6.0 %collective-permute-start.9 = (bf16[1024,256]{1,0:T(8,128)(2,1)}, bf16[1024,256]{1,0:T(8,128)(2,1)}, u32[]{:S(2)}, u32[]{:S(2)}) collective-permute-start(bf16[1024,256]{1,0:T(8,128)(2,1)} %add_convert_fusion.5), channel_id=1, source_target_pairs={{0,1},{1,0},{2,3},{3,2},{4,5},{5,4},{6,7},{7,6},{8,9},{9,8},{10,11... | collective-permute-start | bytes 1572872 | tf_op jit(solution)/shard_map/ppermute | solution.py:534
  74.7 0.2 collective-permute-done.10
  74.9 2.1 %add_convert_fusion.4 = bf16[1024,256]{1,0:T(8,128)(2,1)} fusion(bf16[1024,256]{1,0:T(8,128)(2,1)} %collective-permute-done.10, bf16[1024,256]{1,0:T(8,128)(2,1)} %get-tuple-element.29), kind=kLoop, calls=%fused_computation.4 | loop fusion | flops 1048576 | bytes 1572864 | tf_op jit(solution)/shard_map/convert_element_type | solution.py:526
  77.0 5.4 %collective-permute-start.11 = (bf16[1024,256]{1,0:T(8,128)(2,1)}, bf16[1024,256]{1,0:T(8,128)(2,1)}, u32[]{:S(2)}, u32[]{:S(2)}) collective-permute-start(bf16[1024,256]{1,0:T(8,128)(2,1)} %add_convert_fusion.4), channel_id=1, source_target_pairs={{0,0},{1,2},{2,1},{3,3},{4,4},{5,6},{6,5},{7,7},{8,8},{9,10},{10,9... | collective-permute-start | bytes 1572872 | tf_op jit(solution)/shard_map/ppermute | solution.py:542
  82.3 3.4 %collective-permute-done.9.refs_1_ = bf16[1024,256]{1,0:T(8,128)(2,1)} collective-permute-done((bf16[1024,256]{1,0:T(8,128)(2,1)}, bf16[1024,256]{1,0:T(8,128)(2,1)}, u32[]{:S(2)}, u32[]{:S(2)}) %collective-permute-start.9) | collective-permute-done | bytes 524320 | tf_op jit(solution)/shard_map/ppermute | solution.py:534
  85.8 1.0 copy-done.12
  86.9 0.7 copy-done.16
  87.5 0.7 copy-done.17
  88.2 1.0 copy-done.19
  89.3 7.2 %mlp.1 = (bf16[1024,256]{1,0:T(8,128)(2,1)}, bf16[1024,256]{1,0:T(8,128)(2,1)S(1)}, bf16[1024,256]{1,0:T(8,128)(2,1)S(1)}, bf16[1024,256]{1,0:T(8,128)(2,1)S(1)}...) custom-call(s32[1]{0:T(128)} %bitcast.middle, ...), custom_call_target="tpu_custom_call" | custom-call | flops 5767499776 | bytes 1048576 | tf_op jit(solution)/shard_map/mlp/pallas_call | solution.py:226
  96.5 1.5 weight_grads.1
  98.2 6.9 %collective-permute-start.12 = (bf16[1024,256]{1,0:T(8,128)(2,1)S(1)}, bf16[1024,256]{1,0:T(8,128)(2,1)S(1)}, u32[]{:S(2)}, u32[]{:S(2)}) collective-permute-start(bf16[1024,256]{1,0:T(8,128)(2,1)S(1)} %get-tuple-element.37.refs_0_), channel_id=1, source_target_pairs={{0,1},{1,0},{2,3},{3,2},{4,5},{5,4},{6,7},{7,6},{8,9},{9,8},{10,11... | collective-permute-start | bytes 1572872 | tf_op jit(solution)/shard_map/ppermute | solution.py:534
  105.1 0.4 collective-permute-start.18
  105.5 0.7 collective-permute-start.13
  106.2 11.3 %collective-permute-done.12.refs_1_ = bf16[1024,256]{1,0:T(8,128)(2,1)S(1)} collective-permute-done((bf16[1024,256]{1,0:T(8,128)(2,1)S(1)}, bf16[1024,256]{1,0:T(8,128)(2,1)S(1)}, u32[]{:S(2)}, u32[]{:S(2)}) %collective-permute-start.12) | collective-permute-done | bytes 524320 | tf_op jit(solution)/shard_map/ppermute | solution.py:534
  117.6 0.7 collective-permute-start.15
  118.3 1.6 collective-permute-start.19
  119.9 3.4 %collective-permute-done.19 = f32[112,256]{1,0:T(8,128)S(1)} collective-permute-done((f32[112,256]{1,0:T(8,128)S(1)}, f32[112,256]{1,0:T(8,128)S(1)}, u32[]{:S(2)}, u32[]{:S(2)}) %collective-permute-start.19) | collective-permute-done | bytes 114720 | tf_op jit(solution)/shard_map/ppermute | solution.py:530
  123.3 4.7 %collective-permute-start.20 = (f32[112,256]{1,0:T(8,128)S(1)}, f32[112,256]{1,0:T(8,128)S(1)}, u32[]{:S(2)}, u32[]{:S(2)}) collective-permute-start(f32[112,256]{1,0:T(8,128)S(1)} %slice_add_fusion.2), channel_id=1, source_target_pairs={{0,1},{1,0},{2,3},{3,2},{4,5},{5,4},{6,7},{7,6},{8,9},{9,8},{10,11... | collective-permute-start | bytes 344072 | tf_op jit(solution)/shard_map/ppermute | solution.py:534
  128.1 3.9 %collective-permute-done.20 = f32[112,256]{1,0:T(8,128)S(1)} collective-permute-done((f32[112,256]{1,0:T(8,128)S(1)}, f32[112,256]{1,0:T(8,128)S(1)}, u32[]{:S(2)}, u32[]{:S(2)}) %collective-permute-start.20) | collective-permute-done | bytes 114720 | tf_op jit(solution)/shard_map/ppermute | solution.py:534
  132.0 1.2 collective-permute-start.21
  133.2 2.7 %collective-permute-start.16 = (bf16[1024,256]{1,0:T(8,128)(2,1)S(1)}, bf16[1024,256]{1,0:T(8,128)(2,1)S(1)}, u32[]{:S(2)}, u32[]{:S(2)}) collective-permute-start(bf16[1024,256]{1,0:T(8,128)(2,1)S(1)} %collective-permute-done.15.refs_4_), channel_id=1, source_target_pairs={{0,1},{1,0},{2,3},{3,2},{4,5},{5,4},{6,7},{7,6},{8,9},{9,8},{10,11... | collective-permute-start | bytes 1572872 | tf_op jit(solution)/shard_map/ppermute | solution.py:534
  135.9 4.4 %tile_grads.2.refs_8_.refs_14_ = bf16[128,128,128]{2,1,0:T(8,128)(2,1)} custom-call(s32[128]{0:T(128)S(1)} %fusion.cols, s32[32]{0:T(128)S(1)} %bitcast.20, s32[4]{0:T(128)S(1)} %pad_add_fusion.order, s32[1]{0:T(128)} %bitcast.middle, bf16[1024,256]{1,0:T(8,128)(2,1)S(1)} %get-tuple-element.37.refs_0_, ...), custom_call_target="tpu_custom_call" | custom-call | flops 4614000128 | bytes 1048576 | tf_op jit(solution)/shard_map/tile_grads/pallas_call | solution.py:498
  140.3 6.6 %collective-permute-done.21 = f32[112,256]{1,0:T(8,128)S(1)} collective-permute-done((f32[112,256]{1,0:T(8,128)S(1)}, f32[112,256]{1,0:T(8,128)S(1)}, u32[]{:S(2)}, u32[]{:S(2)}) %collective-permute-start.21) | collective-permute-done | bytes 114720 | tf_op jit(solution)/shard_map/ppermute | solution.py:538
  147.0 8.0 %collective-permute-done.16.refs_5_ = bf16[1024,256]{1,0:T(8,128)(2,1)S(1)} collective-permute-done((bf16[1024,256]{1,0:T(8,128)(2,1)S(1)}, bf16[1024,256]{1,0:T(8,128)(2,1)S(1)}, u32[]{:S(2)}, u32[]{:S(2)}) %collective-permute-start.16) | collective-permute-done | bytes 524320 | tf_op jit(solution)/shard_map/ppermute | solution.py:534
  155.0 2.2 %copy-done = bf16[128,128,128]{2,1,0:T(8,128)(2,1)S(1)} copy-done((bf16[128,128,128]{2,1,0:T(8,128)(2,1)S(1)}, bf16[128,128,128]{2,1,0:T(8,128)(2,1)}, u32[]{:S(2)}) %copy-start) | copy-done | bytes 4194328
  157.2 4.5 %back_terms.1 = (bf16[4096,256]{1,0:T(8,128)(2,1)S(1)}, bf16[4096,256]{1,0:T(8,128)(2,1)S(1)}) custom-call(s32[128]{0:T(128)S(1)} %fusion.cols, s32[32]{0:T(128)S(1)} %bitcast.21, s32[4]{0:T(128)S(1)} %pad_add_fusion.order, s32[1]{0:T(128)} %bitcast.middle, bf16[1024,256]{1,0:T(8,128)(2,1)S(1)} %get-tuple-element.37.refs_0_, ...), custom_call_target="tpu_custom_call" | custom-call | flops 5767499776 | bytes 1048576 | tf_op jit(solution)/shard_map/back_terms/pallas_call | solution.py:400
  161.7 3.0 %collective-permute-start.26 = (bf16[112,256]{1,0:T(8,128)(2,1)S(1)}, bf16[112,256]{1,0:T(8,128)(2,1)S(1)}, u32[]{:S(2)}, u32[]{:S(2)}) collective-permute-start(bf16[112,256]{1,0:T(8,128)(2,1)S(1)} %get-tuple-element.56), channel_id=1, source_target_pairs={{0,16},{4,20},{8,24},{12,28},{16,0},{20,4},{24,8},{28,12},{1,17},{... | collective-permute-start | bytes 172040 | tf_op jit(solution)/shard_map/ppermute | solution.py:530
  164.8 2.5 %collective-permute-done.26 = bf16[112,256]{1,0:T(8,128)(2,1)S(1)} collective-permute-done((bf16[112,256]{1,0:T(8,128)(2,1)S(1)}, bf16[112,256]{1,0:T(8,128)(2,1)S(1)}, u32[]{:S(2)}, u32[]{:S(2)}) %collective-permute-start.26) | collective-permute-done | bytes 57376 | tf_op jit(solution)/shard_map/ppermute | solution.py:530
  167.3 2.0 %collective-permute-start.27 = (bf16[224,256]{1,0:T(8,128)(2,1)S(1)}, bf16[224,256]{1,0:T(8,128)(2,1)S(1)}, u32[]{:S(2)}, u32[]{:S(2)}) collective-permute-start(bf16[224,256]{1,0:T(8,128)(2,1)S(1)} %pad_maximum_fusion.2), channel_id=1, source_target_pairs={{0,8},{4,12},{8,0},{12,4},{16,24},{20,28},{24,16},{28,20},{1,9},{5... | collective-permute-start | bytes 344072 | tf_op jit(solution)/shard_map/ppermute | solution.py:530
  169.3 3.0 %collective-permute-done.27 = bf16[224,256]{1,0:T(8,128)(2,1)S(1)} collective-permute-done((bf16[224,256]{1,0:T(8,128)(2,1)S(1)}, bf16[224,256]{1,0:T(8,128)(2,1)S(1)}, u32[]{:S(2)}, u32[]{:S(2)}) %collective-permute-start.27) | collective-permute-done | bytes 114720 | tf_op jit(solution)/shard_map/ppermute | solution.py:530
  172.4 1.5 collective-permute-done.28
  173.9 0.4 add_convert_fusion.3
  174.3 1.9 collective-permute-start.25
  176.2 1.5 collective-permute-start.24
  177.6 0.2 collective-permute-start.23
  177.8 1.0 weight_unpack.1
  178.8 4.5 %tile_grads.3 = bf16[128,128,128]{2,1,0:T(8,128)(2,1)} custom-call(s32[128]{0:T(128)S(1)} %fusion.cols, s32[32]{0:T(128)S(1)} %bitcast.22, s32[4]{0:T(128)S(1)} %pad_add_fusion.order, s32[1]{0:T(128)} %bitcast.middle, bf16[1024,256]{1,0:T(8,128)(2,1)S(1)} %get-tuple-element.37.refs_0_, ...), custom_call_target="tpu_custom_call", output_to_operand_aliasing={{}: (18, {})} | custom-call | flops 4614000128 | bytes 1048576 | tf_op jit(solution)/shard_map/tile_grads/pallas_call | solution.py:498
  183.3 6.7 %collective-permute-done.25 = bf16[1024,256]{1,0:T(8,128)(2,1)S(1)} collective-permute-done((bf16[1024,256]{1,0:T(8,128)(2,1)S(1)}, bf16[1024,256]{1,0:T(8,128)(2,1)S(1)}, u32[]{:S(2)}, u32[]{:S(2)}) %collective-permute-start.25) | collective-permute-done | bytes 524320 | tf_op jit(solution)/shard_map/ppermute | solution.py:530
  190.1 10.4 %collective-permute-done.24 = bf16[1024,256]{1,0:T(8,128)(2,1)S(1)} collective-permute-done((bf16[1024,256]{1,0:T(8,128)(2,1)S(1)}, bf16[1024,256]{1,0:T(8,128)(2,1)S(1)}, u32[]{:S(2)}, u32[]{:S(2)}) %collective-permute-start.24) | collective-permute-done | bytes 524320 | tf_op jit(solution)/shard_map/ppermute | solution.py:530
  200.4 0.2 collective-permute-done.23
  200.6 1.2 add_convert_fusion
  (62 shorter events, 0.8 us)
Async XLA Ops:
  0.6 16.0 %collective-permute-start.1 = (bf16[1024,256]{1,0:T(8,128)(2,1)}, bf16[1024,256]{1,0:T(8,128)(2,1)S(1)}, u32[]{:S(2)}, u32[]{:S(2)}) collective-permute-start(bf16[1024,256]{1,0:T(8,128)(2,1)} %refs_6_.1), channel_id=1, source_target_pairs={{0,8},{4,12},{8,0},{12,4},{16,24},{20,28},{24,16},{28,20},{1,9},{5... | collective-permute-start | bytes 1572872 | tf_op jit(solution)/shard_map/ppermute | solution.py:530
  3.6 24.8 %collective-permute-start.3 = (bf16[1024,256]{1,0:T(8,128)(2,1)}, bf16[1024,256]{1,0:T(8,128)(2,1)S(1)}, u32[]{:S(2)}, u32[]{:S(2)}) collective-permute-start(bf16[1024,256]{1,0:T(8,128)(2,1)} %refs_6_.1), channel_id=1, source_target_pairs={{0,16},{4,20},{8,24},{12,28},{16,0},{20,4},{24,8},{28,12},{1,17},{... | collective-permute-start | bytes 1572872 | tf_op jit(solution)/shard_map/ppermute | solution.py:530
  5.2 23.3 %collective-permute-start.5 = (bf16[1024,256]{1,0:T(8,128)(2,1)}, bf16[1024,256]{1,0:T(8,128)(2,1)S(1)}, u32[]{:S(2)}, u32[]{:S(2)}) collective-permute-start(bf16[1024,256]{1,0:T(8,128)(2,1)} %refs_6_.1), channel_id=1, source_target_pairs={{0,24},{4,28},{8,16},{12,20},{16,8},{20,12},{24,0},{28,4},{1,25},{... | collective-permute-start | bytes 1572872 | tf_op jit(solution)/shard_map/ppermute | solution.py:530
  5.2 24.8 %collective-permute-start = (bf16[1024,256]{1,0:T(8,128)(2,1)}, bf16[1024,256]{1,0:T(8,128)(2,1)S(1)}, u32[]{:S(2)}, u32[]{:S(2)}) collective-permute-start(bf16[1024,256]{1,0:T(8,128)(2,1)} %refs_6_.1), channel_id=1, source_target_pairs={{0,4},{4,0},{8,12},{12,8},{16,20},{20,16},{24,28},{28,24},{1,5},{5... | collective-permute-start | bytes 1572872 | tf_op jit(solution)/shard_map/ppermute | solution.py:530
  16.6 13.4 %collective-permute-start.2 = (bf16[1024,256]{1,0:T(8,128)(2,1)S(1)}, bf16[1024,256]{1,0:T(8,128)(2,1)S(1)}, u32[]{:S(2)}, u32[]{:S(2)}) collective-permute-start(bf16[1024,256]{1,0:T(8,128)(2,1)S(1)} %collective-permute-done.1.refs_2_.refs_4_.refs_8_), channel_id=1, source_target_pairs={{0,4},{4,0},{8,12},{12,8},{16,20},{20,16},{24,28},{28,24},{1,5},{5... | collective-permute-start | bytes 1572872 | tf_op jit(solution)/shard_map/ppermute | solution.py:530
  28.5 2.6 %collective-permute-start.4 = (bf16[1024,256]{1,0:T(8,128)(2,1)S(1)}, bf16[1024,256]{1,0:T(8,128)(2,1)S(1)}, u32[]{:S(2)}, u32[]{:S(2)}) collective-permute-start(bf16[1024,256]{1,0:T(8,128)(2,1)S(1)} %collective-permute-done.3.refs_4_.refs_6_.refs_10_), channel_id=1, source_target_pairs={{0,4},{4,0},{8,12},{12,8},{16,20},{20,16},{24,28},{28,24},{1,5},{5... | collective-permute-start | bytes 1572872 | tf_op jit(solution)/shard_map/ppermute | solution.py:530
  28.5 3.4 %collective-permute-start.6 = (bf16[1024,256]{1,0:T(8,128)(2,1)S(1)}, bf16[1024,256]{1,0:T(8,128)(2,1)}, u32[]{:S(2)}, u32[]{:S(2)}) collective-permute-start(bf16[1024,256]{1,0:T(8,128)(2,1)S(1)} %collective-permute-done.5.refs_6_.refs_8_.refs_12_), channel_id=1, source_target_pairs={{0,4},{4,0},{8,12},{12,8},{16,20},{20,16},{24,28},{28,24},{1,5},{5... | collective-permute-start | bytes 1572872 | tf_op jit(solution)/shard_map/ppermute | solution.py:530
  31.0 0.8 copy-start.3
  31.8 1.0 copy-start.1
  32.9 1.0 copy-start.4
  33.9 0.7 copy-start.7
  34.6 2.2 %copy-start.9 = (bf16[32,1,4,128,128]{4,3,2,1,0:T(8,128)(2,1)S(1)}, bf16[32,1,4,128,128]{4,3,2,1,0:T(8,128)(2,1)}, u32[]{:S(2)}) copy-start(bf16[32,1,4,128,128]{4,3,2,1,0:T(8,128)(2,1)} %param.11) | copy-start | bytes 12582916
  36.8 24.4 %copy-start.2 = (bf16[1024,256]{1,0:T(8,128)(2,1)S(1)}, bf16[1024,256]{1,0:T(8,128)(2,1)}, u32[]{:S(2)}) copy-start(bf16[1024,256]{1,0:T(8,128)(2,1)} %refs_6_.1) | copy-start | bytes 1572868
  36.8 24.4 %copy-start.8 = (s32[32,1]{0,1:T(1,128)S(1)}, s32[32,1]{0,1:T(1,128)}, u32[]{:S(2)}) copy-start(s32[32,1]{0,1:T(1,128)} %param.13) | copy-start | bytes 388
  40.8 14.0 %collective-permute-start.7 = (bf16[1024,256]{1,0:T(8,128)(2,1)S(1)}, bf16[1024,256]{1,0:T(8,128)(2,1)S(1)}, u32[]{:S(2)}, u32[]{:S(2)}) collective-permute-start(bf16[1024,256]{1,0:T(8,128)(2,1)S(1)} %get-tuple-element.27), channel_id=1, source_target_pairs={{0,1},{1,0},{2,3},{3,2},{4,5},{5,4},{6,7},{7,6},{8,9},{9,8},{10,11... | collective-permute-start | bytes 1572872 | tf_op jit(solution)/shard_map/ppermute | solution.py:534
  55.8 11.9 %collective-permute-start.8 = (bf16[1024,256]{1,0:T(8,128)(2,1)}, bf16[1024,256]{1,0:T(8,128)(2,1)}, u32[]{:S(2)}, u32[]{:S(2)}) collective-permute-start(bf16[1024,256]{1,0:T(8,128)(2,1)} %add_convert_fusion.6), channel_id=1, source_target_pairs={{0,0},{1,2},{2,1},{3,3},{4,4},{5,6},{6,5},{7,7},{8,8},{9,10},{10,9... | collective-permute-start | bytes 1572872 | tf_op jit(solution)/shard_map/ppermute | solution.py:542
  61.1 13.7 %collective-permute-start.10 = (bf16[1024,256]{1,0:T(8,128)(2,1)}, bf16[1024,256]{1,0:T(8,128)(2,1)}, u32[]{:S(2)}, u32[]{:S(2)}) collective-permute-start(bf16[1024,256]{1,0:T(8,128)(2,1)} %get-tuple-element.29), channel_id=1, source_target_pairs={{0,1},{1,0},{2,3},{3,2},{4,5},{5,4},{6,7},{7,6},{8,9},{9,8},{10,11... | collective-permute-start | bytes 1572872 | tf_op jit(solution)/shard_map/ppermute | solution.py:534
  61.1 1.0 copy-start.5
  62.2 2.2 %copy-start.10 = (bf16[32,1,4,128,128]{4,3,2,1,0:T(8,128)(2,1)S(1)}, bf16[32,1,4,128,128]{4,3,2,1,0:T(8,128)(2,1)}, u32[]{:S(2)}) copy-start(bf16[32,1,4,128,128]{4,3,2,1,0:T(8,128)(2,1)} %param.11) | copy-start | bytes 12582916
  67.6 1.0 copy-start.18
  67.6 18.2 %copy-start.13 = (bf16[512,256]{1,0:T(8,128)(2,1)S(1)}, bf16[512,256]{1,0:T(8,128)(2,1)}, u32[]{:S(2)}) copy-start(bf16[512,256]{1,0:T(8,128)(2,1)} %w_in.1) | copy-start | bytes 786436
  67.6 18.2 %copy-start.14 = (bf16[256,256]{1,0:T(8,128)(2,1)S(1)}, bf16[256,256]{1,0:T(8,128)(2,1)}, u32[]{:S(2)}) copy-start(bf16[256,256]{1,0:T(8,128)(2,1)} %refs_5_.1) | copy-start | bytes 393220
  67.6 18.2 %copy-start.15 = (f32[256]{0:T(256)S(1)}, f32[256]{0:T(256)}, u32[]{:S(2)}) copy-start(f32[256]{0:T(256)} %param.15) | copy-start | bytes 3076
  68.6 17.2 %collective-permute-start.9 = (bf16[1024,256]{1,0:T(8,128)(2,1)}, bf16[1024,256]{1,0:T(8,128)(2,1)}, u32[]{:S(2)}, u32[]{:S(2)}) collective-permute-start(bf16[1024,256]{1,0:T(8,128)(2,1)} %add_convert_fusion.5), channel_id=1, source_target_pairs={{0,1},{1,0},{2,3},{3,2},{4,5},{5,4},{6,7},{7,6},{8,9},{9,8},{10,11... | collective-permute-start | bytes 1572872 | tf_op jit(solution)/shard_map/ppermute | solution.py:534
  77.0 8.8 %collective-permute-start.11 = (bf16[1024,256]{1,0:T(8,128)(2,1)}, bf16[1024,256]{1,0:T(8,128)(2,1)}, u32[]{:S(2)}, u32[]{:S(2)}) collective-permute-start(bf16[1024,256]{1,0:T(8,128)(2,1)} %add_convert_fusion.4), channel_id=1, source_target_pairs={{0,0},{1,2},{2,1},{3,3},{4,4},{5,6},{6,5},{7,7},{8,8},{9,10},{10,9... | collective-permute-start | bytes 1572872 | tf_op jit(solution)/shard_map/ppermute | solution.py:542
  85.8 1.0 copy-start.12
  86.9 0.7 copy-start.16
  87.5 0.7 copy-start.17
  88.2 1.0 copy-start.19
  98.0 37.9 %copy-start.6 = (bf16[1024,256]{1,0:T(8,128)(2,1)S(1)}, bf16[1024,256]{1,0:T(8,128)(2,1)}, u32[]{:S(2)}) copy-start(bf16[1024,256]{1,0:T(8,128)(2,1)} %copy-done.3) | copy-start | bytes 1572868
  98.1 7.0 %collective-permute-start.17 = (f32[448,256]{1,0:T(8,128)S(1)}, f32[448,256]{1,0:T(8,128)S(1)}, u32[]{:S(2)}, u32[]{:S(2)}) collective-permute-start(f32[448,256]{1,0:T(8,128)S(1)} %slice.43), channel_id=1, source_target_pairs={{0,4},{4,0},{8,12},{12,8},{16,20},{20,16},{24,28},{28,24},{1,5},{5... | collective-permute-start | bytes 1376264 | tf_op jit(solution)/shard_map/ppermute | solution.py:530
  98.2 19.4 %collective-permute-start.12 = (bf16[1024,256]{1,0:T(8,128)(2,1)S(1)}, bf16[1024,256]{1,0:T(8,128)(2,1)S(1)}, u32[]{:S(2)}, u32[]{:S(2)}) collective-permute-start(bf16[1024,256]{1,0:T(8,128)(2,1)S(1)} %get-tuple-element.37.refs_0_), channel_id=1, source_target_pairs={{0,1},{1,0},{2,3},{3,2},{4,5},{5,4},{6,7},{7,6},{8,9},{9,8},{10,11... | collective-permute-start | bytes 1572872 | tf_op jit(solution)/shard_map/ppermute | solution.py:534
  105.1 13.1 %collective-permute-start.18 = (f32[224,256]{1,0:T(8,128)S(1)}, f32[224,256]{1,0:T(8,128)S(1)}, u32[]{:S(2)}, u32[]{:S(2)}) collective-permute-start(f32[224,256]{1,0:T(8,128)S(1)} %slice.57), channel_id=1, source_target_pairs={{0,8},{4,12},{8,0},{12,4},{16,24},{20,28},{24,16},{28,20},{1,9},{5... | collective-permute-start | bytes 688136 | tf_op jit(solution)/shard_map/ppermute | solution.py:530
  105.5 22.4 %collective-permute-start.13 = (bf16[1024,256]{1,0:T(8,128)(2,1)S(1)}, bf16[1024,256]{1,0:T(8,128)(2,1)S(1)}, u32[]{:S(2)}, u32[]{:S(2)}) collective-permute-start(bf16[1024,256]{1,0:T(8,128)(2,1)S(1)} %get-tuple-element.37.refs_0_), channel_id=1, source_target_pairs={{0,0},{1,2},{2,1},{3,3},{4,4},{5,6},{6,5},{7,7},{8,8},{9,10},{10,9... | collective-permute-start | bytes 1572872 | tf_op jit(solution)/shard_map/ppermute | solution.py:542
  117.6 15.6 %collective-permute-start.15 = (bf16[1024,256]{1,0:T(8,128)(2,1)S(1)}, bf16[1024,256]{1,0:T(8,128)(2,1)S(1)}, u32[]{:S(2)}, u32[]{:S(2)}) collective-permute-start(bf16[1024,256]{1,0:T(8,128)(2,1)S(1)} %collective-permute-done.12.refs_1_), channel_id=1, source_target_pairs={{0,0},{1,2},{2,1},{3,3},{4,4},{5,6},{6,5},{7,7},{8,8},{9,10},{10,9... | collective-permute-start | bytes 1572872 | tf_op jit(solution)/shard_map/ppermute | solution.py:542
  118.3 5.0 %collective-permute-start.19 = (f32[112,256]{1,0:T(8,128)S(1)}, f32[112,256]{1,0:T(8,128)S(1)}, u32[]{:S(2)}, u32[]{:S(2)}) collective-permute-start(f32[112,256]{1,0:T(8,128)S(1)} %slice.59), channel_id=1, source_target_pairs={{0,16},{4,20},{8,24},{12,28},{16,0},{20,4},{24,8},{28,12},{1,17},{... | collective-permute-start | bytes 344072 | tf_op jit(solution)/shard_map/ppermute | solution.py:530
  123.3 8.6 %collective-permute-start.20 = (f32[112,256]{1,0:T(8,128)S(1)}, f32[112,256]{1,0:T(8,128)S(1)}, u32[]{:S(2)}, u32[]{:S(2)}) collective-permute-start(f32[112,256]{1,0:T(8,128)S(1)} %slice_add_fusion.2), channel_id=1, source_target_pairs={{0,1},{1,0},{2,3},{3,2},{4,5},{5,4},{6,7},{7,6},{8,9},{9,8},{10,11... | collective-permute-start | bytes 344072 | tf_op jit(solution)/shard_map/ppermute | solution.py:534
  128.0 19.0 %collective-permute-start.14 = (bf16[1024,256]{1,0:T(8,128)(2,1)S(1)}, bf16[1024,256]{1,0:T(8,128)(2,1)S(1)}, u32[]{:S(2)}, u32[]{:S(2)}) collective-permute-start(bf16[1024,256]{1,0:T(8,128)(2,1)S(1)} %collective-permute-done.13.refs_2_), channel_id=1, source_target_pairs={{0,1},{1,0},{2,3},{3,2},{4,5},{5,4},{6,7},{7,6},{8,9},{9,8},{10,11... | collective-permute-start | bytes 1572872 | tf_op jit(solution)/shard_map/ppermute | solution.py:534
  132.0 23.0 %copy-start.11 = (bf16[32,1,4,128,128]{4,3,2,1,0:T(8,128)(2,1)S(1)}, bf16[32,1,4,128,128]{4,3,2,1,0:T(8,128)(2,1)}, u32[]{:S(2)}) copy-start(bf16[32,1,4,128,128]{4,3,2,1,0:T(8,128)(2,1)} %param.11) | copy-start | bytes 12582916
  132.0 15.0 %collective-permute-start.21 = (f32[112,256]{1,0:T(8,128)S(1)}, f32[112,256]{1,0:T(8,128)S(1)}, u32[]{:S(2)}, u32[]{:S(2)}) collective-permute-start(f32[112,256]{1,0:T(8,128)S(1)} %add.66), channel_id=1, source_target_pairs={{0,3},{3,0},{1,2},{2,1},{4,7},{7,4},{5,6},{6,5},{8,11},{11,8},{9,1... | collective-permute-start | bytes 344072 | tf_op jit(solution)/shard_map/ppermute | solution.py:538
  133.2 21.8 %collective-permute-start.16 = (bf16[1024,256]{1,0:T(8,128)(2,1)S(1)}, bf16[1024,256]{1,0:T(8,128)(2,1)S(1)}, u32[]{:S(2)}, u32[]{:S(2)}) collective-permute-start(bf16[1024,256]{1,0:T(8,128)(2,1)S(1)} %collective-permute-done.15.refs_4_), channel_id=1, source_target_pairs={{0,1},{1,0},{2,3},{3,2},{4,5},{5,4},{6,7},{7,6},{8,9},{9,8},{10,11... | collective-permute-start | bytes 1572872 | tf_op jit(solution)/shard_map/ppermute | solution.py:534
  155.0 2.2 %copy-start = (bf16[128,128,128]{2,1,0:T(8,128)(2,1)S(1)}, bf16[128,128,128]{2,1,0:T(8,128)(2,1)}, u32[]{:S(2)}) copy-start(bf16[128,128,128]{2,1,0:T(8,128)(2,1)} %tile_grads.2.refs_8_.refs_14_) | copy-start | bytes 12582916
  161.7 12.2 %collective-permute-start.22 = (bf16[4096,256]{1,0:T(8,128)(2,1)S(1)}, bf16[4096,256]{1,0:T(8,128)(2,1)S(1)}, u32[]{:S(2)}, u32[]{:S(2)}) collective-permute-start(bf16[4096,256]{1,0:T(8,128)(2,1)S(1)} %get-tuple-element.40), channel_id=1, source_target_pairs={{0,4},{4,0},{8,12},{12,8},{16,20},{20,16},{24,28},{28,24},{1,5},{5... | collective-permute-start | bytes 6291464 | tf_op jit(solution)/shard_map/ppermute | solution.py:530
  161.7 5.5 %collective-permute-start.26 = (bf16[112,256]{1,0:T(8,128)(2,1)S(1)}, bf16[112,256]{1,0:T(8,128)(2,1)S(1)}, u32[]{:S(2)}, u32[]{:S(2)}) collective-permute-start(bf16[112,256]{1,0:T(8,128)(2,1)S(1)} %get-tuple-element.56), channel_id=1, source_target_pairs={{0,16},{4,20},{8,24},{12,28},{16,0},{20,4},{24,8},{28,12},{1,17},{... | collective-permute-start | bytes 172040 | tf_op jit(solution)/shard_map/ppermute | solution.py:530
  167.3 5.0 %collective-permute-start.27 = (bf16[224,256]{1,0:T(8,128)(2,1)S(1)}, bf16[224,256]{1,0:T(8,128)(2,1)S(1)}, u32[]{:S(2)}, u32[]{:S(2)}) collective-permute-start(bf16[224,256]{1,0:T(8,128)(2,1)S(1)} %pad_maximum_fusion.2), channel_id=1, source_target_pairs={{0,8},{4,12},{8,0},{12,4},{16,24},{20,28},{24,16},{28,20},{1,9},{5... | collective-permute-start | bytes 344072 | tf_op jit(solution)/shard_map/ppermute | solution.py:530
  172.3 1.6 collective-permute-start.28
  174.3 15.8 %collective-permute-start.25 = (bf16[1024,256]{1,0:T(8,128)(2,1)S(1)}, bf16[1024,256]{1,0:T(8,128)(2,1)S(1)}, u32[]{:S(2)}, u32[]{:S(2)}) collective-permute-start(bf16[1024,256]{1,0:T(8,128)(2,1)S(1)} %get-tuple-element.59.refs_17_), channel_id=1, source_target_pairs={{0,24},{4,28},{8,16},{12,20},{16,8},{20,12},{24,0},{28,4},{1,25},{... | collective-permute-start | bytes 1572872 | tf_op jit(solution)/shard_map/ppermute | solution.py:530
  176.2 24.3 %collective-permute-start.24 = (bf16[1024,256]{1,0:T(8,128)(2,1)S(1)}, bf16[1024,256]{1,0:T(8,128)(2,1)S(1)}, u32[]{:S(2)}, u32[]{:S(2)}) collective-permute-start(bf16[1024,256]{1,0:T(8,128)(2,1)S(1)} %get-tuple-element.60.refs_16_), channel_id=1, source_target_pairs={{0,16},{4,20},{8,24},{12,28},{16,0},{20,4},{24,8},{28,12},{1,17},{... | collective-permute-start | bytes 1572872 | tf_op jit(solution)/shard_map/ppermute | solution.py:530
  177.6 23.0 %collective-permute-start.23 = (bf16[1024,256]{1,0:T(8,128)(2,1)S(1)}, bf16[1024,256]{1,0:T(8,128)(2,1)S(1)}, u32[]{:S(2)}, u32[]{:S(2)}) collective-permute-start(bf16[1024,256]{1,0:T(8,128)(2,1)S(1)} %get-tuple-element.58.refs_15_), channel_id=1, source_target_pairs={{0,8},{4,12},{8,0},{12,4},{16,24},{20,28},{24,16},{28,20},{1,9},{5... | collective-permute-start | bytes 1572872 | tf_op jit(solution)/shard_map/ppermute | solution.py:530

commit v6 on v5

--- a/solution.py
+++ b/solution.py
@@ -119,34 +119,13 @@
             pltpu.SemaphoreType.DMA((len(pieces),)),
             pltpu.SemaphoreType.DMA((n_picks,)),
         ],
-        compiler_params=params(16 if gathered <= 8192 else 40),
+        compiler_params=params(60),
         cost_estimate=cost(2.0),
         name="partial_messages",
     )(cols, counts, order, *pieces, tiles)
 
 
-def mlp_kernel(kinds, middle, nodes_ref, cot_ref, *refs):
-    nodes_v, cot_v, sem = refs[-3:]
-    refs = refs[:-3]
-    step = pl.program_id(0)
-    rows = nodes_v.shape[1]
-
-    def loads(index):
-        where = block_at(index, rows)
-        return (
-            pltpu.make_async_copy(nodes_ref.at[where], nodes_v.at[index], sem.at[0, index]),
-            pltpu.make_async_copy(cot_ref.at[where], cot_v.at[index], sem.at[1, index]),
-        )
-
-    @pl.when(step == 0)
-    def _():
-        for index in range(nodes_v.shape[0]):
-            for copy in loads(index):
-                copy.start()
-
-    for copy in loads(step):
-        copy.wait()
-    nodes, cot = nodes_v.at[step], cot_v.at[step]
+def mlp_kernel(kinds, middle, nodes, cot, *refs):
     n_parts = sum(len(chunk) for chunk in kinds)
     parts = refs[:n_parts]
     w_in, bias, w_out, gain, shift, updated, gpre_o, act_o, gproj_o, msg_o, vec = refs[
@@ -227,14 +206,9 @@
         functools.partial(mlp_kernel, kinds),
         grid=(rows // step,),
         out_shape=outs,
-        in_specs=[SMEM, HBM, HBM] + [blocked(a) for a in flat] + [whole(a) for a in weights],
+        in_specs=[SMEM] + [blocked(a) for a in (nodes, cot, *flat)] + [whole(a) for a in weights],
         out_specs=[blocked(a) for a in outs[:5]] + [whole(outs[5])] + [blocked(a) for a in outs[6:]],
-        scratch_shapes=[
-            pltpu.VMEM((rows // step, step, width), BF16),
-            pltpu.VMEM((rows // step, step, width), BF16),
-            pltpu.SemaphoreType.DMA((2, rows // step)),
-        ],
-        compiler_params=params(24),
+        compiler_params=params(40),
         cost_estimate=cost(5.0),
         name="mlp",
     )(middle, nodes, cot, *flat, *weights)
@@ -286,7 +260,7 @@
         in_specs=[SMEM] + [blocked] * 6 + [whole(w_in.shape), whole(vec.shape)],
         out_specs=[whole(out.shape), blocked],
         scratch_shapes=[pltpu.VMEM(padded, F32)],
-        compiler_params=params(16),
+        compiler_params=params(40),
         cost_estimate=cost(3.0),
         name="weight_grads",
     )(mine, nodes, msg, act, gpre, gproj, cot, w_in, vec)
@@ -410,7 +384,7 @@
             pltpu.SemaphoreType.DMA((len(grads),)),
             pltpu.SemaphoreType.DMA((1,)),
         ],
-        compiler_params=params(28 if gathered <= 8192 else 56),
+        compiler_params=params(60),
         cost_estimate=cost(5.0),
         name="back_terms",
     )(cols, counts, order, middle, *grads, tiles.reshape(row_blocks * slots, block, block), *after)
@@ -422,7 +396,8 @@
     grads = refs[: n_grads * n_chunks]
     refs = refs[n_grads * n_chunks :]
     pieces = refs[: n_pieces * n_chunks]
-    out, grad_v, nodes_v, tiles_v, live, source, sem, piece_sem, out_sem = refs[n_pieces * n_chunks + n_after :]
+    out, token, grad_v, nodes_v, tiles_v, live, source, sem, piece_sem, out_sem = refs[n_pieces * n_chunks + n_after :]
+    token[...] = jnp.zeros_like(token)
     block = out.shape[1]
     width = nodes_v.shape[1]
     part = width // n_chunks
@@ -499,9 +474,12 @@
         functools.partial(
             tile_grad_kernel, rows, slots, len(grads[0]), len(pieces[0]), chunks, len(after), groups
         ),
-        out_shape=jax.ShapeDtypeStruct((row_blocks * slots, block, block), BF16),
+        out_shape=[
+            jax.ShapeDtypeStruct((row_blocks * slots, block, block), BF16),
+            jax.ShapeDtypeStruct((8, 128), F32),
+        ],
         in_specs=[SMEM] * 4 + [ANY] * (len(flat) + len(after)),
-        out_specs=ANY,
+        out_specs=[ANY, VMEM],
         input_output_aliases={} if base is None else {4 + len(flat): 0},
         scratch_shapes=[
             pltpu.VMEM((len(groups) * rows, width), BF16),
@@ -513,7 +491,7 @@
             pltpu.SemaphoreType.DMA((chunks, len(pieces[0]))),
             pltpu.SemaphoreType.DMA((len(groups),)),
         ],
-        compiler_params=params(16 if gathered <= 8192 else 40),
+        compiler_params=params(60),
         cost_estimate=cost(4.0),
         name="tile_grads",
     )(cols, counts, order, middle, *flat, *after)
@@ -539,7 +517,12 @@
 
 
 def inner_swap(value):
-    return lax.ppermute(value, "col", [(0, 0), (1, 2), (2, 1), (3, 3)])
+    pairs = []
+    for row in range(8):
+        for col in range(4):
+            partner = (row, 3 - col) if col in (1, 2) else (row ^ 1, col)
+            pairs.append((row * 4 + col, partner[0] * 4 + partner[1]))
+    return lax.ppermute(value, ("row", "col"), pairs)
 
 
 def held(value, *others):
@@ -641,18 +624,21 @@
     if square_line:
         halves = ((1, 3, 5, 7), (0, 2, 4, 6))
         grads = [gather_line(gmsgs[0])]
-        near_grads = tile_grad_call(
-            cols, counts, order, middle, [grads[0][:2]], pieces, tile_local.shape, rows, (3, 2)
-        )
-        all_weights = level_weights(scatter_weights(weight_terms))
+        near_grads, token = tile_grad_call(
+            cols, counts, order, middle, [grads[0][:2]], pieces, tile_local.shape, rows, (3, 2),
+            after=(grads[0][3], grads[0][4]),
+        )
+        row_weights = scatter_weights(held(weight_terms, token))
         odd, even = back_call(
-            cols, counts, order, middle, grads[0], tile_local, total, gathered, halves, (all_weights, near_grads)
-        )
+            cols, counts, order, middle, grads[0], tile_local, total, gathered, halves, (row_weights,)
+        )
+        all_weights = level_weights(row_weights)
         own_terms, sums = pair_sums(even, odd, rows)
         terms = (*own_terms, *reduce_square(sums))
-        weights = gather_weights(all_weights, width, mine)
+        weights = gather_weights(held(all_weights, *sums), width, mine)
+        terms = held(terms, *weights)
         back = sum(term.astype(F32) for term in terms)
-        grad_tiles = tile_grad_call(
+        grad_tiles, _ = tile_grad_call(
             cols, counts, order, middle, grads, pieces, tile_local.shape, rows, (1, 0), near_grads, sums
         )
     else:
@@ -667,7 +653,7 @@
             cols, counts, order, middle, grads[0], tile_local, total, gathered, (tuple(range(n_row)),)
         )
         back = lax.psum_scatter(terms, "row", scatter_dimension=0, tiled=True).astype(F32)
-        grad_tiles = tile_grad_call(
+        grad_tiles, _ = tile_grad_call(
             cols, counts, order, middle, grads, pieces, tile_local.shape, rows, tuple(range(n_col))
         )
     grad_nodes = (direct + back).astype(BF16)

time: 204 us -> 197 us (0.966)
  Pallas kernels: 30.3 us -> 42.5 us
  local copies, waits for them, and re-layouts: 15.5 us -> 4.91 us
  starting transfers between devices: 51.2 us -> 41.3 us
  other arithmetic: 5.87 us -> 12.1 us
  waiting for transfers between devices: 98 us -> 94.7 us
    unnamed x41 -> x47, local copies, waits for them, and re-layouts: 15.4 us -> 3.67 us
    ppermute x4, starting transfers between devices: 12.1 us -> 0.57 us  [inner_swap(): return lax.ppermute(value, ('row', 'col'), pairs)]
    ppermute x17, waiting for transfers between devices: 52 us -> 41.3 us  [swap(): return lax.ppermute(value, 'row', [(i, i ^ bit) for i in range(8)])]
    ppermute x7, waiting for transfers between devices: 39.3 us -> 48.8 us  [outer_swap(): return lax.ppermute(value, 'col', [(0, 1), (1, 0), (2, 3), (3, 2)])]
    pallas_call x1, Pallas kernels: 4.48 us -> 10.3 us  [back_call(): pl.pallas_call(functools.partial(back_kernel, rows, slots, len(grads), le...]
    pallas_call x2, Pallas kernels: 8.88 us -> 14.2 us  [tile_grad_call(): pl.pallas_call(functools.partial(tile_grad_kernel, rows, slots, len(grads...]
    pallas_call x2, Pallas kernels: 7.19 us -> 10.8 us  [forward_call(): pl.pallas_call(functools.partial(forward_kernel, outputs, len(pieces)), o...]
    ppermute x7, starting transfers between devices: 22 us -> 25.1 us  [outer_swap(): return lax.ppermute(value, 'col', [(0, 1), (1, 0), (2, 3), (3, 2)])]
  transfers between devices with their start and end apart: 29 -> 29, of which waited for: 17 -> 16; matrix products, arithmetic and copies ran while one was open for 2% -> 4% of each run, Pallas kernels for 6% -> 11%
where the time goes in v6:
time: 197 us; the launch traced here: 196 us
  waiting for transfers between devices  94.7 us (48%)
  Pallas kernels  42.5 us (22%)
  starting transfers between devices  41.3 us (21%)
  other arithmetic  12.1 us (6%)
  local copies, waits for them, and re-layouts  4.91 us (2%)
    ppermute x7, waiting for transfers between devices, outer_swap(): return lax.ppermute(value, 'col', [(0, 1), (1, 0), (2, 3), (3, 2)])  48.8 us
    ppermute x17, waiting for transfers between devices, swap(): return lax.ppermute(value, 'row', [(i, i ^ bit) for i in range(8)])  41.3 us
    ppermute x7, starting transfers between devices, outer_swap(): return lax.ppermute(value, 'col', [(0, 1), (1, 0), (2, 3), (3, 2)])  25.1 us
    pallas_call x2, Pallas kernels, tile_grad_call(): pl.pallas_call(functools.partial(tile_grad_kernel, rows, slots, len(grads...  14.2 us
    ppermute x17, starting transfers between devices, swap(): return lax.ppermute(value, 'row', [(i, i ^ bit) for i in range(8)])  13.4 us
    pallas_call x2, Pallas kernels, forward_call(): pl.pallas_call(functools.partial(forward_kernel, outputs, len(pieces)), o...  10.8 us
    pallas_call x1, Pallas kernels, back_call(): pl.pallas_call(functools.partial(back_kernel, rows, slots, len(grads), le...  10.3 us
    convert_element_type x4, other arithmetic, add(): return value.astype(BF16)  6.79 us
  transfers between devices with their start and end apart: 29, of which 16 were waited for; matrix products, arithmetic and copies ran while one was open for 4% of the time, Pallas kernels for 11%

profile of v6, /device:TPU:0, one launch (start us, length us, event | category | flops | bytes accessed | tf_op | source)
XLA Modules:
  0.0 196.4 jit_solution(12985207531588584295)
XLA Ops:
  0.6 4.0 %collective-permute-start.5 = (bf16[1024,256]{1,0:T(8,128)(2,1)}, bf16[1024,256]{1,0:T(8,128)(2,1)S(1)}, u32[]{:S(2)}, u32[]{:S(2)}) collective-permute-start(bf16[1024,256]{1,0:T(8,128)(2,1)} %refs_6_.1), channel_id=1, source_target_pairs={{0,24},{4,28},{8,16},{12,20},{16,8},{20,12},{24,0},{28,4},{1,25},{... | collective-permute-start | bytes 1572872 | tf_op jit(solution)/shard_map/ppermute | solution.py:508
  4.6 0.5 collective-permute-start.3
  5.1 0.1 collective-permute-start.1
  5.2 12.4 %collective-permute-done.5.refs_6_.refs_8_.refs_12_ = bf16[1024,256]{1,0:T(8,128)(2,1)S(1)} collective-permute-done((bf16[1024,256]{1,0:T(8,128)(2,1)}, bf16[1024,256]{1,0:T(8,128)(2,1)S(1)}, u32[]{:S(2)}, u32[]{:S(2)}) %collective-permute-start.5) | collective-permute-done | bytes 524320 | tf_op jit(solution)/shard_map/ppermute | solution.py:508
  17.6 10.4 %collective-permute-done.3.refs_4_.refs_6_.refs_10_ = bf16[1024,256]{1,0:T(8,128)(2,1)S(1)} collective-permute-done((bf16[1024,256]{1,0:T(8,128)(2,1)}, bf16[1024,256]{1,0:T(8,128)(2,1)S(1)}, u32[]{:S(2)}, u32[]{:S(2)}) %collective-permute-start.3) | collective-permute-done | bytes 524320 | tf_op jit(solution)/shard_map/ppermute | solution.py:508
  28.0 0.3 collective-permute-done.1.refs_2_.refs_4_.refs_8_
  28.3 0.2 collective-permute-start.2
  28.5 0.8 copy.19
  29.2 0.1 reshape.43
  29.4 0.7 pad_add_fusion.order
  30.0 0.6 fusion.cols
  30.6 0.2 collective-permute-done.2.refs_3_.refs_5_.refs_9_
  30.8 0.6 copy-done.15
  31.4 0.2 copy-done.16
  31.5 0.2 copy-done.17
  31.7 5.4 %partial_messages.3 = (bf16[1024,256]{1,0:T(8,128)(2,1)}, bf16[1024,256]{1,0:T(8,128)(2,1)}) custom-call(s32[128]{0:T(128)} %fusion.cols, s32[32]{0:T(128)} %bitcast.23, s32[4]{0:T(128)} %pad_add_fusion.order, bf16[1024,256]{1,0:T(8,128)(2,1)} %refs_6_.1, bf16[1024,256]{1,0:T(8,128)(2,1)} %copy-done.15, bf16[1024,256]{1,0:T(8,128)(2,1)} %copy-done.14, ...), custom_call_target="tpu_custom_call" | custom-call | flops 2307000064 | bytes 1048576 | tf_op jit(solution)/shard_map/partial_messages/pallas_call | solution.py:111
  37.1 1.8 collective-permute-start.7
  38.9 12.6 %collective-permute-done.7 = bf16[1024,256]{1,0:T(8,128)(2,1)S(1)} collective-permute-done((bf16[1024,256]{1,0:T(8,128)(2,1)}, bf16[1024,256]{1,0:T(8,128)(2,1)S(1)}, u32[]{:S(2)}, u32[]{:S(2)}) %collective-permute-start.7) | collective-permute-done | bytes 524320 | tf_op jit(solution)/shard_map/ppermute | solution.py:512
  51.5 1.6 collective-permute-start.10
  53.1 1.2 add_convert_fusion.6
  54.3 0.1 collective-permute-start.8
  54.4 5.5 %partial_messages.2 = (bf16[1024,256]{1,0:T(8,128)(2,1)}, bf16[1024,256]{1,0:T(8,128)(2,1)}) custom-call(s32[128]{0:T(128)} %fusion.cols, s32[32]{0:T(128)} %bitcast.24, s32[4]{0:T(128)} %pad_add_fusion.order, bf16[1024,256]{1,0:T(8,128)(2,1)} %refs_6_.1, bf16[1024,256]{1,0:T(8,128)(2,1)} %copy-done.15, bf16[1024,256]{1,0:T(8,128)(2,1)} %copy-done.14, ...), custom_call_target="tpu_custom_call" | custom-call | flops 2307000064 | bytes 1048576 | tf_op jit(solution)/shard_map/partial_messages/pallas_call | solution.py:111
  59.9 5.0 %collective-permute-done.10 = bf16[1024,256]{1,0:T(8,128)(2,1)S(1)} collective-permute-done((bf16[1024,256]{1,0:T(8,128)(2,1)}, bf16[1024,256]{1,0:T(8,128)(2,1)S(1)}, u32[]{:S(2)}, u32[]{:S(2)}) %collective-permute-start.10) | collective-permute-done | bytes 524320 | tf_op jit(solution)/shard_map/ppermute | solution.py:512
  65.0 0.9 add_convert_fusion.4
  65.9 1.2 add_convert_fusion.5
  67.1 3.1 %collective-permute-start.9 = (bf16[1024,256]{1,0:T(8,128)(2,1)S(1)}, bf16[1024,256]{1,0:T(8,128)(2,1)S(1)}, u32[]{:S(2)}, u32[]{:S(2)}) collective-permute-start(bf16[1024,256]{1,0:T(8,128)(2,1)S(1)} %add_convert_fusion.5), channel_id=1, source_target_pairs={{0,1},{1,0},{2,3},{3,2},{4,5},{5,4},{6,7},{7,6},{8,9},{9,8},{10,11... | collective-permute-start | bytes 1572872 | tf_op jit(solution)/shard_map/ppermute | solution.py:512
  70.2 11.3 %collective-permute-done.9.refs_1_ = bf16[1024,256]{1,0:T(8,128)(2,1)S(1)} collective-permute-done((bf16[1024,256]{1,0:T(8,128)(2,1)S(1)}, bf16[1024,256]{1,0:T(8,128)(2,1)S(1)}, u32[]{:S(2)}, u32[]{:S(2)}) %collective-permute-start.9) | collective-permute-done | bytes 524320 | tf_op jit(solution)/shard_map/ppermute | solution.py:512
  81.6 1.0 copy-done.8
  82.6 4.6 %mlp.1 = (bf16[1024,256]{1,0:T(8,128)(2,1)}, bf16[1024,256]{1,0:T(8,128)(2,1)S(1)}, bf16[1024,256]{1,0:T(8,128)(2,1)S(1)}, bf16[1024,256]{1,0:T(8,128)(2,1)S(1)}...) custom-call(s32[1]{0:T(128)} %bitcast.middle, ...), custom_call_target="tpu_custom_call" | custom-call | flops 5767499776 | bytes 1048576 | tf_op jit(solution)/shard_map/mlp/pallas_call | solution.py:205
  87.3 0.6 collective-permute-start.12
  87.8 1.5 weight_grads.1
  89.4 0.1 collective-permute-start.17
  89.5 0.5 collective-permute-start.13
  90.0 9.7 %collective-permute-done.12.refs_1_ = bf16[1024,256]{1,0:T(8,128)(2,1)S(1)} collective-permute-done((bf16[1024,256]{1,0:T(8,128)(2,1)S(1)}, bf16[1024,256]{1,0:T(8,128)(2,1)S(1)}, u32[]{:S(2)}, u32[]{:S(2)}) %collective-permute-start.12) | collective-permute-done | bytes 524320 | tf_op jit(solution)/shard_map/ppermute | solution.py:512
  99.8 1.2 collective-permute-start.18
  101.0 5.4 %collective-permute-start.14 = (bf16[1024,256]{1,0:T(8,128)(2,1)S(1)}, bf16[1024,256]{1,0:T(8,128)(2,1)S(1)}, u32[]{:S(2)}, u32[]{:S(2)}) collective-permute-start(bf16[1024,256]{1,0:T(8,128)(2,1)S(1)} %collective-permute-done.13.refs_2_), channel_id=1, source_target_pairs={{0,1},{1,0},{2,3},{3,2},{4,5},{5,4},{6,7},{7,6},{8,9},{9,8},{10,11... | collective-permute-start | bytes 1572872 | tf_op jit(solution)/shard_map/ppermute | solution.py:512
  106.4 11.0 %collective-permute-start.16 = (bf16[1024,256]{1,0:T(8,128)(2,1)S(1)}, bf16[1024,256]{1,0:T(8,128)(2,1)S(1)}, u32[]{:S(2)}, u32[]{:S(2)}) collective-permute-start(bf16[1024,256]{1,0:T(8,128)(2,1)S(1)} %collective-permute-done.15.refs_4_.refs_11_), channel_id=1, source_target_pairs={{0,1},{1,0},{2,3},{3,2},{4,5},{5,4},{6,7},{7,6},{8,9},{9,8},{10,11... | collective-permute-start | bytes 1572872 | tf_op jit(solution)/shard_map/ppermute | solution.py:512
  117.4 1.5 collective-permute-start.19
  119.0 3.3 %collective-permute-done.19 = f32[112,256]{1,0:T(8,128)S(1)} collective-permute-done((f32[112,256]{1,0:T(8,128)S(1)}, f32[112,256]{1,0:T(8,128)S(1)}, u32[]{:S(2)}, u32[]{:S(2)}) %collective-permute-start.19) | collective-permute-done | bytes 114720 | tf_op jit(solution)/shard_map/ppermute | solution.py:508
  122.3 0.7 slice_add_fusion.2.refs_7_
  122.9 6.4 %collective-permute-done.16.refs_5_ = bf16[1024,256]{1,0:T(8,128)(2,1)S(1)} collective-permute-done((bf16[1024,256]{1,0:T(8,128)(2,1)S(1)}, bf16[1024,256]{1,0:T(8,128)(2,1)S(1)}, u32[]{:S(2)}, u32[]{:S(2)}) %collective-permute-start.16) | collective-permute-done | bytes 524320 | tf_op jit(solution)/shard_map/ppermute | solution.py:512
  129.3 0.8 copy-done.22
  130.1 10.3 %back_terms.1 = (bf16[4096,256]{1,0:T(8,128)(2,1)}, bf16[4096,256]{1,0:T(8,128)(2,1)}) custom-call(s32[128]{0:T(128)} %fusion.cols, s32[32]{0:T(128)} %bitcast.25, s32[4]{0:T(128)} %pad_add_fusion.order, s32[1]{0:T(128)} %bitcast.middle, bf16[1024,256]{1,0:T(8,128)(2,1)} %copy-done.2, bf16[1024,256]{1,0:T(8,128)(2,1)} %copy-done.18, ...), custom_call_target="tpu_custom_call" | custom-call | flops 5767499776 | bytes 1048576 | tf_op jit(solution)/shard_map/back_terms/pallas_call | solution.py:374
  140.4 0.1 collective-permute-start.20
  140.6 1.7 collective-permute-start.24
  142.3 3.8 %collective-permute-done.24 = f32[112,256]{1,0:T(8,128)S(1)} collective-permute-done((f32[112,256]{1,0:T(8,128)S(1)}, f32[112,256]{1,0:T(8,128)S(1)}, u32[]{:S(2)}, u32[]{:S(2)}) %collective-permute-start.24) | collective-permute-done | bytes 114720 | tf_op jit(solution)/shard_map/ppermute | solution.py:512
  146.1 2.2 %collective-permute-start.25 = (f32[112,256]{1,0:T(8,128)S(1)}, f32[112,256]{1,0:T(8,128)S(1)}, u32[]{:S(2)}, u32[]{:S(2)}) collective-permute-start(f32[112,256]{1,0:T(8,128)S(1)} %add.69), channel_id=1, source_target_pairs={{0,3},{3,0},{1,2},{2,1},{4,7},{7,4},{5,6},{6,5},{8,11},{11,8},{9,1... | collective-permute-start | bytes 344072 | tf_op jit(solution)/shard_map/ppermute | solution.py:516
  148.3 4.5 %collective-permute-done.25 = f32[112,256]{1,0:T(8,128)S(1)} collective-permute-done((f32[112,256]{1,0:T(8,128)S(1)}, f32[112,256]{1,0:T(8,128)S(1)}, u32[]{:S(2)}, u32[]{:S(2)}) %collective-permute-start.25) | collective-permute-done | bytes 114720 | tf_op jit(solution)/shard_map/ppermute | solution.py:516
  152.9 3.5 %add_convert_fusion.1 = (bf16[1024,256]{1,0:T(8,128)(2,1)}, bf16[1024,256]{1,0:T(8,128)(2,1)}, bf16[1024,256]{1,0:T(8,128)(2,1)}) fusion(bf16[4096,256]{1,0:T(8,128)(2,1)S(1)} %collective-permute-done.20, bf16[4096,256]{1,0:T(8,128)(2,1)} %get-tuple-element.47), kind=kLoop, calls=%fused_computation.1 | loop fusion | flops 3145728 | bytes 4718592 | tf_op jit(solution)/shard_map/convert_element_type | solution.py:504
  156.3 1.1 collective-permute-start.26
  157.4 3.1 %collective-permute-done.26 = bf16[112,256]{1,0:T(8,128)(2,1)S(1)} collective-permute-done((bf16[112,256]{1,0:T(8,128)(2,1)S(1)}, bf16[112,256]{1,0:T(8,128)(2,1)S(1)}, u32[]{:S(2)}, u32[]{:S(2)}) %collective-permute-start.26) | collective-permute-done | bytes 57376 | tf_op jit(solution)/shard_map/ppermute | solution.py:508
  160.5 0.9 collective-permute-start.27
  161.5 7.7 %tile_grads.2 = (bf16[128,128,128]{2,1,0:T(8,128)(2,1)}, f32[8,128]{1,0:T(8,128)}) custom-call(s32[128]{0:T(128)} %fusion.cols, s32[32]{0:T(128)} %bitcast.26, s32[4]{0:T(128)} %pad_add_fusion.order, s32[1]{0:T(128)} %bitcast.middle, bf16[1024,256]{1,0:T(8,128)(2,1)} %copy-done.2, bf16[1024,256]{1,0:T(8,128)(2,1)} %copy-done.18, bf16[1024,256]{1,0:T(8,128)(2,1)} %refs_6_.1, ...), custom_call_target="tpu_custom_call" | custom-call | flops 4614000128 | bytes 1048576 | tf_op jit(solution)/shard_map/tile_grads/pallas_call | solution.py:473
  169.2 1.1 slice.48
  170.2 1.3 collective-permute-start.23
  171.5 0.3 collective-permute-start.22
  171.8 2.0 %collective-permute-start.21 = (bf16[1024,256]{1,0:T(8,128)(2,1)}, bf16[1024,256]{1,0:T(8,128)(2,1)}, u32[]{:S(2)}, u32[]{:S(2)}) collective-permute-start(bf16[1024,256]{1,0:T(8,128)(2,1)} %get-tuple-element.74.refs_15_), channel_id=1, source_target_pairs={{0,8},{4,12},{8,0},{12,4},{16,24},{20,28},{24,16},{28,20},{1,9},{5... | collective-permute-start | bytes 1572872 | tf_op jit(solution)/shard_map/ppermute | solution.py:508
  173.8 0.7 pad_maximum_fusion.1
  174.5 6.5 %tile_grads.3 = (bf16[128,128,128]{2,1,0:T(8,128)(2,1)}, f32[8,128]{1,0:T(8,128)}) custom-call(s32[128]{0:T(128)} %fusion.cols, s32[32]{0:T(128)} %bitcast.27, s32[4]{0:T(128)} %pad_add_fusion.order, s32[1]{0:T(128)} %bitcast.middle, bf16[1024,256]{1,0:T(8,128)(2,1)} %copy-done.2, bf16[1024,256]{1,0:T(8,128)(2,1)} %copy-done.18, ...), custom_call_target="tpu_custom_call", output_to_operand_aliasing={{0}: (18, {})} | custom-call | flops 4614000128 | bytes 1048576 | tf_op jit(solution)/shard_map/tile_grads/pallas_call | solution.py:473
  181.1 1.0 weight_unpack.1
  182.1 4.3 %collective-permute-done.23 = bf16[1024,256]{1,0:T(8,128)(2,1)} collective-permute-done((bf16[1024,256]{1,0:T(8,128)(2,1)}, bf16[1024,256]{1,0:T(8,128)(2,1)}, u32[]{:S(2)}, u32[]{:S(2)}) %collective-permute-start.23) | collective-permute-done | bytes 524320 | tf_op jit(solution)/shard_map/ppermute | solution.py:508
  186.4 6.6 %collective-permute-done.22 = bf16[1024,256]{1,0:T(8,128)(2,1)} collective-permute-done((bf16[1024,256]{1,0:T(8,128)(2,1)}, bf16[1024,256]{1,0:T(8,128)(2,1)}, u32[]{:S(2)}, u32[]{:S(2)}) %collective-permute-start.22) | collective-permute-done | bytes 524320 | tf_op jit(solution)/shard_map/ppermute | solution.py:508
  193.0 0.9 collective-permute-done.21
  193.9 2.5 %add_convert_fusion = bf16[1024,256]{1,0:T(8,128)(2,1)} fusion(f32[1024,256]{1,0:T(8,128)S(1)} %get-tuple-element.44, bf16[1024,256]{1,0:T(8,128)(2,1)} %collective-permute-done.23, bf16[1024,256]{1,0:T(8,128)(2,1)} %collective-permute-done.22, bf16[1024,256]{1,0:T(8,128)(2,1)} %collective-permute-done.21, bf16[1024,256]{1,0:T(8,128)(2,1)S(1)} %slice-done, ...), kind=kLoop, calls=%fused_computation | loop fusion | flops 2883584 | bytes 4194304 | tf_op jit(solution)/shard_map/convert_element_type | solution.py:659
  (71 shorter events, 0.4 us)
Async XLA Ops:
  0.6 17.0 %collective-permute-start.5 = (bf16[1024,256]{1,0:T(8,128)(2,1)}, bf16[1024,256]{1,0:T(8,128)(2,1)S(1)}, u32[]{:S(2)}, u32[]{:S(2)}) collective-permute-start(bf16[1024,256]{1,0:T(8,128)(2,1)} %refs_6_.1), channel_id=1, source_target_pairs={{0,24},{4,28},{8,16},{12,20},{16,8},{20,12},{24,0},{28,4},{1,25},{... | collective-permute-start | bytes 1572872 | tf_op jit(solution)/shard_map/ppermute | solution.py:508
  4.6 23.4 %collective-permute-start.3 = (bf16[1024,256]{1,0:T(8,128)(2,1)}, bf16[1024,256]{1,0:T(8,128)(2,1)S(1)}, u32[]{:S(2)}, u32[]{:S(2)}) collective-permute-start(bf16[1024,256]{1,0:T(8,128)(2,1)} %refs_6_.1), channel_id=1, source_target_pairs={{0,16},{4,20},{8,24},{12,28},{16,0},{20,4},{24,8},{28,12},{1,17},{... | collective-permute-start | bytes 1572872 | tf_op jit(solution)/shard_map/ppermute | solution.py:508
  5.1 23.2 %collective-permute-start.1 = (bf16[1024,256]{1,0:T(8,128)(2,1)}, bf16[1024,256]{1,0:T(8,128)(2,1)S(1)}, u32[]{:S(2)}, u32[]{:S(2)}) collective-permute-start(bf16[1024,256]{1,0:T(8,128)(2,1)} %refs_6_.1), channel_id=1, source_target_pairs={{0,8},{4,12},{8,0},{12,4},{16,24},{20,28},{24,16},{28,20},{1,9},{5... | collective-permute-start | bytes 1572872 | tf_op jit(solution)/shard_map/ppermute | solution.py:508
  5.2 25.3 %collective-permute-start = (bf16[1024,256]{1,0:T(8,128)(2,1)}, bf16[1024,256]{1,0:T(8,128)(2,1)S(1)}, u32[]{:S(2)}, u32[]{:S(2)}) collective-permute-start(bf16[1024,256]{1,0:T(8,128)(2,1)} %refs_6_.1), channel_id=1, source_target_pairs={{0,4},{4,0},{8,12},{12,8},{16,20},{20,16},{24,28},{28,24},{1,5},{5... | collective-permute-start | bytes 1572872 | tf_op jit(solution)/shard_map/ppermute | solution.py:508
  17.6 13.2 %copy-start.12 = (bf16[1024,256]{1,0:T(8,128)(2,1)}, bf16[1024,256]{1,0:T(8,128)(2,1)S(1)}, u32[]{:S(2)}) copy-start(bf16[1024,256]{1,0:T(8,128)(2,1)S(1)} %collective-permute-done.5.refs_6_.refs_8_.refs_12_) | copy-start | bytes 1572868
  17.6 13.0 %collective-permute-start.6 = (bf16[1024,256]{1,0:T(8,128)(2,1)S(1)}, bf16[1024,256]{1,0:T(8,128)(2,1)S(1)}, u32[]{:S(2)}, u32[]{:S(2)}) collective-permute-start(bf16[1024,256]{1,0:T(8,128)(2,1)S(1)} %collective-permute-done.5.refs_6_.refs_8_.refs_12_), channel_id=1, source_target_pairs={{0,4},{4,0},{8,12},{12,8},{16,20},{20,16},{24,28},{28,24},{1,5},{5... | collective-permute-start | bytes 1572872 | tf_op jit(solution)/shard_map/ppermute | solution.py:508
  28.0 2.8 %copy-start.13 = (bf16[1024,256]{1,0:T(8,128)(2,1)}, bf16[1024,256]{1,0:T(8,128)(2,1)S(1)}, u32[]{:S(2)}) copy-start(bf16[1024,256]{1,0:T(8,128)(2,1)S(1)} %collective-permute-done.3.refs_4_.refs_6_.refs_10_) | copy-start | bytes 1572868
  28.0 2.6 %collective-permute-start.4 = (bf16[1024,256]{1,0:T(8,128)(2,1)S(1)}, bf16[1024,256]{1,0:T(8,128)(2,1)S(1)}, u32[]{:S(2)}, u32[]{:S(2)}) collective-permute-start(bf16[1024,256]{1,0:T(8,128)(2,1)S(1)} %collective-permute-done.3.refs_4_.refs_6_.refs_10_), channel_id=1, source_target_pairs={{0,4},{4,0},{8,12},{12,8},{16,20},{20,16},{24,28},{28,24},{1,5},{5... | collective-permute-start | bytes 1572872 | tf_op jit(solution)/shard_map/ppermute | solution.py:508
  28.3 2.5 %copy-start.14 = (bf16[1024,256]{1,0:T(8,128)(2,1)}, bf16[1024,256]{1,0:T(8,128)(2,1)S(1)}, u32[]{:S(2)}) copy-start(bf16[1024,256]{1,0:T(8,128)(2,1)S(1)} %collective-permute-done.1.refs_2_.refs_4_.refs_8_) | copy-start | bytes 1572868
  28.3 2.5 %collective-permute-start.2 = (bf16[1024,256]{1,0:T(8,128)(2,1)S(1)}, bf16[1024,256]{1,0:T(8,128)(2,1)}, u32[]{:S(2)}, u32[]{:S(2)}) collective-permute-start(bf16[1024,256]{1,0:T(8,128)(2,1)S(1)} %collective-permute-done.1.refs_2_.refs_4_.refs_8_), channel_id=1, source_target_pairs={{0,4},{4,0},{8,12},{12,8},{16,20},{20,16},{24,28},{28,24},{1,5},{5... | collective-permute-start | bytes 1572872 | tf_op jit(solution)/shard_map/ppermute | solution.py:508
  30.6 0.8 copy-start.15
  30.6 1.0 copy-start.16
  30.6 1.1 copy-start.17
  37.1 14.4 %collective-permute-start.7 = (bf16[1024,256]{1,0:T(8,128)(2,1)}, bf16[1024,256]{1,0:T(8,128)(2,1)S(1)}, u32[]{:S(2)}, u32[]{:S(2)}) collective-permute-start(bf16[1024,256]{1,0:T(8,128)(2,1)} %get-tuple-element.35), channel_id=1, source_target_pairs={{0,1},{1,0},{2,3},{3,2},{4,5},{5,4},{6,7},{7,6},{8,9},{9,8},{10,11... | collective-permute-start | bytes 1572872 | tf_op jit(solution)/shard_map/ppermute | solution.py:512
  51.5 13.5 %collective-permute-start.10 = (bf16[1024,256]{1,0:T(8,128)(2,1)}, bf16[1024,256]{1,0:T(8,128)(2,1)S(1)}, u32[]{:S(2)}, u32[]{:S(2)}) collective-permute-start(bf16[1024,256]{1,0:T(8,128)(2,1)} %get-tuple-element.37), channel_id=1, source_target_pairs={{0,1},{1,0},{2,3},{3,2},{4,5},{5,4},{6,7},{7,6},{8,9},{9,8},{10,11... | collective-permute-start | bytes 1572872 | tf_op jit(solution)/shard_map/ppermute | solution.py:512
  54.3 11.7 %collective-permute-start.8 = (bf16[1024,256]{1,0:T(8,128)(2,1)S(1)}, bf16[1024,256]{1,0:T(8,128)(2,1)S(1)}, u32[]{:S(2)}, u32[]{:S(2)}) collective-permute-start(bf16[1024,256]{1,0:T(8,128)(2,1)S(1)} %add_convert_fusion.6), channel_id=1, source_target_pairs={{0,4},{1,2},{2,1},{3,7},{4,0},{5,6},{6,5},{7,3},{8,12},{9,10},{10,... | collective-permute-start | bytes 1572872 | tf_op jit(solution)/shard_map/ppermute | solution.py:525
  54.3 10.6 %copy-start.10 = (bf16[1024,256]{1,0:T(8,128)(2,1)S(1)}, bf16[1024,256]{1,0:T(8,128)(2,1)}, u32[]{:S(2)}) copy-start(bf16[1024,256]{1,0:T(8,128)(2,1)} %get-tuple-element.37) | copy-start | bytes 1572868
  59.8 21.7 %copy-start = (bf16[1024,256]{1,0:T(8,128)(2,1)S(1)}, bf16[1024,256]{1,0:T(8,128)(2,1)}, u32[]{:S(2)}) copy-start(bf16[1024,256]{1,0:T(8,128)(2,1)} %cot.3) | copy-start | bytes 1572868
  59.9 21.7 %copy-start.1 = (bf16[1024,256]{1,0:T(8,128)(2,1)S(1)}, bf16[1024,256]{1,0:T(8,128)(2,1)}, u32[]{:S(2)}) copy-start(bf16[1024,256]{1,0:T(8,128)(2,1)} %refs_6_.1) | copy-start | bytes 1572868
  59.9 21.7 %copy-start.3 = (bf16[512,256]{1,0:T(8,128)(2,1)S(1)}, bf16[512,256]{1,0:T(8,128)(2,1)}, u32[]{:S(2)}) copy-start(bf16[512,256]{1,0:T(8,128)(2,1)} %w_in.1) | copy-start | bytes 786436
  59.9 21.7 %copy-start.4 = (bf16[256,256]{1,0:T(8,128)(2,1)S(1)}, bf16[256,256]{1,0:T(8,128)(2,1)}, u32[]{:S(2)}) copy-start(bf16[256,256]{1,0:T(8,128)(2,1)} %refs_5_.1) | copy-start | bytes 393220
  59.9 21.7 %copy-start.5 = (f32[256]{0:T(256)S(1)}, f32[256]{0:T(256)}, u32[]{:S(2)}) copy-start(f32[256]{0:T(256)} %param.15) | copy-start | bytes 3076
  59.9 21.7 %copy-start.6 = (f32[256]{0:T(256)S(1)}, f32[256]{0:T(256)}, u32[]{:S(2)}) copy-start(f32[256]{0:T(256)} %param.17) | copy-start | bytes 3076
  59.9 21.6 %copy-start.7 = (f32[256]{0:T(256)S(1)}, f32[256]{0:T(256)}, u32[]{:S(2)}) copy-start(f32[256]{0:T(256)} %param.18) | copy-start | bytes 3076
  65.9 4.3 %collective-permute-start.11 = (bf16[1024,256]{1,0:T(8,128)(2,1)}, bf16[1024,256]{1,0:T(8,128)(2,1)S(1)}, u32[]{:S(2)}, u32[]{:S(2)}) collective-permute-start(bf16[1024,256]{1,0:T(8,128)(2,1)} %add_convert_fusion.4), channel_id=1, source_target_pairs={{0,4},{1,2},{2,1},{3,7},{4,0},{5,6},{6,5},{7,3},{8,12},{9,10},{10,... | collective-permute-start | bytes 1572872 | tf_op jit(solution)/shard_map/ppermute | solution.py:525
  67.1 14.4 %collective-permute-start.9 = (bf16[1024,256]{1,0:T(8,128)(2,1)S(1)}, bf16[1024,256]{1,0:T(8,128)(2,1)S(1)}, u32[]{:S(2)}, u32[]{:S(2)}) collective-permute-start(bf16[1024,256]{1,0:T(8,128)(2,1)S(1)} %add_convert_fusion.5), channel_id=1, source_target_pairs={{0,1},{1,0},{2,3},{3,2},{4,5},{5,4},{6,7},{7,6},{8,9},{9,8},{10,11... | collective-permute-start | bytes 1572872 | tf_op jit(solution)/shard_map/ppermute | solution.py:512
  81.6 1.0 copy-start.8
  87.3 2.2 %copy-start.2 = (bf16[1024,256]{1,0:T(8,128)(2,1)}, bf16[1024,256]{1,0:T(8,128)(2,1)S(1)}, u32[]{:S(2)}) copy-start(bf16[1024,256]{1,0:T(8,128)(2,1)S(1)} %get-tuple-element.45.refs_0_) | copy-start | bytes 1572868
  87.3 12.4 %collective-permute-start.12 = (bf16[1024,256]{1,0:T(8,128)(2,1)S(1)}, bf16[1024,256]{1,0:T(8,128)(2,1)S(1)}, u32[]{:S(2)}, u32[]{:S(2)}) collective-permute-start(bf16[1024,256]{1,0:T(8,128)(2,1)S(1)} %get-tuple-element.45.refs_0_), channel_id=1, source_target_pairs={{0,1},{1,0},{2,3},{3,2},{4,5},{5,4},{6,7},{7,6},{8,9},{9,8},{10,11... | collective-permute-start | bytes 1572872 | tf_op jit(solution)/shard_map/ppermute | solution.py:512
  89.4 10.3 %collective-permute-start.17 = (f32[448,256]{1,0:T(8,128)S(1)}, f32[448,256]{1,0:T(8,128)S(1)}, u32[]{:S(2)}, u32[]{:S(2)}) collective-permute-start(f32[448,256]{1,0:T(8,128)S(1)} %slice.57), channel_id=1, source_target_pairs={{0,4},{4,0},{8,12},{12,8},{16,20},{20,16},{24,28},{28,24},{1,5},{5... | collective-permute-start | bytes 1376264 | tf_op jit(solution)/shard_map/ppermute | solution.py:508
  89.5 11.5 %collective-permute-start.13 = (bf16[1024,256]{1,0:T(8,128)(2,1)S(1)}, bf16[1024,256]{1,0:T(8,128)(2,1)S(1)}, u32[]{:S(2)}, u32[]{:S(2)}) collective-permute-start(bf16[1024,256]{1,0:T(8,128)(2,1)S(1)} %get-tuple-element.45.refs_0_), channel_id=1, source_target_pairs={{0,4},{1,2},{2,1},{3,7},{4,0},{5,6},{6,5},{7,3},{8,12},{9,10},{10,... | collective-permute-start | bytes 1572872 | tf_op jit(solution)/shard_map/ppermute | solution.py:525
  99.7 30.4 %copy-start.18 = (bf16[1024,256]{1,0:T(8,128)(2,1)}, bf16[1024,256]{1,0:T(8,128)(2,1)S(1)}, u32[]{:S(2)}) copy-start(bf16[1024,256]{1,0:T(8,128)(2,1)S(1)} %collective-permute-done.12.refs_1_) | copy-start | bytes 1572868
  99.7 6.7 %collective-permute-start.15 = (bf16[1024,256]{1,0:T(8,128)(2,1)S(1)}, bf16[1024,256]{1,0:T(8,128)(2,1)S(1)}, u32[]{:S(2)}, u32[]{:S(2)}) collective-permute-start(bf16[1024,256]{1,0:T(8,128)(2,1)S(1)} %collective-permute-done.12.refs_1_), channel_id=1, source_target_pairs={{0,4},{1,2},{2,1},{3,7},{4,0},{5,6},{6,5},{7,3},{8,12},{9,10},{10,... | collective-permute-start | bytes 1572872 | tf_op jit(solution)/shard_map/ppermute | solution.py:525
  99.8 17.5 %collective-permute-start.18 = (f32[224,256]{1,0:T(8,128)S(1)}, f32[224,256]{1,0:T(8,128)S(1)}, u32[]{:S(2)}, u32[]{:S(2)}) collective-permute-start(f32[224,256]{1,0:T(8,128)S(1)} %slice.59), channel_id=1, source_target_pairs={{0,8},{4,12},{8,0},{12,4},{16,24},{20,28},{24,16},{28,20},{1,9},{5... | collective-permute-start | bytes 688136 | tf_op jit(solution)/shard_map/ppermute | solution.py:508
  101.0 29.1 %copy-start.19 = (bf16[1024,256]{1,0:T(8,128)(2,1)}, bf16[1024,256]{1,0:T(8,128)(2,1)S(1)}, u32[]{:S(2)}) copy-start(bf16[1024,256]{1,0:T(8,128)(2,1)S(1)} %collective-permute-done.13.refs_2_) | copy-start | bytes 1572868
  101.0 21.9 %collective-permute-start.14 = (bf16[1024,256]{1,0:T(8,128)(2,1)S(1)}, bf16[1024,256]{1,0:T(8,128)(2,1)S(1)}, u32[]{:S(2)}, u32[]{:S(2)}) collective-permute-start(bf16[1024,256]{1,0:T(8,128)(2,1)S(1)} %collective-permute-done.13.refs_2_), channel_id=1, source_target_pairs={{0,1},{1,0},{2,3},{3,2},{4,5},{5,4},{6,7},{7,6},{8,9},{9,8},{10,11... | collective-permute-start | bytes 1572872 | tf_op jit(solution)/shard_map/ppermute | solution.py:512
  106.4 22.9 %copy-start.20 = (bf16[1024,256]{1,0:T(8,128)(2,1)}, bf16[1024,256]{1,0:T(8,128)(2,1)S(1)}, u32[]{:S(2)}) copy-start(bf16[1024,256]{1,0:T(8,128)(2,1)S(1)} %collective-permute-done.15.refs_4_.refs_11_) | copy-start | bytes 1572868
  106.4 22.9 %collective-permute-start.16 = (bf16[1024,256]{1,0:T(8,128)(2,1)S(1)}, bf16[1024,256]{1,0:T(8,128)(2,1)S(1)}, u32[]{:S(2)}, u32[]{:S(2)}) collective-permute-start(bf16[1024,256]{1,0:T(8,128)(2,1)S(1)} %collective-permute-done.15.refs_4_.refs_11_), channel_id=1, source_target_pairs={{0,1},{1,0},{2,3},{3,2},{4,5},{5,4},{6,7},{7,6},{8,9},{9,8},{10,11... | collective-permute-start | bytes 1572872 | tf_op jit(solution)/shard_map/ppermute | solution.py:512
  117.4 4.9 %collective-permute-start.19 = (f32[112,256]{1,0:T(8,128)S(1)}, f32[112,256]{1,0:T(8,128)S(1)}, u32[]{:S(2)}, u32[]{:S(2)}) collective-permute-start(f32[112,256]{1,0:T(8,128)S(1)} %slice.61), channel_id=1, source_target_pairs={{0,16},{4,20},{8,24},{12,28},{16,0},{20,4},{24,8},{28,12},{1,17},{... | collective-permute-start | bytes 344072 | tf_op jit(solution)/shard_map/ppermute | solution.py:508
  122.9 7.2 %copy-start.21 = (bf16[1024,256]{1,0:T(8,128)(2,1)}, bf16[1024,256]{1,0:T(8,128)(2,1)S(1)}, u32[]{:S(2)}) copy-start(bf16[1024,256]{1,0:T(8,128)(2,1)S(1)} %collective-permute-done.14.refs_3_.refs_10_) | copy-start | bytes 1572868
  129.3 0.8 copy-start.22
  130.1 10.5 %copy-start.11 = (f32[112,256]{1,0:T(8,128)S(1)}, f32[112,256]{1,0:T(8,128)}, u32[]{:S(2)}) copy-start(f32[112,256]{1,0:T(8,128)} %slice_add_fusion.2.refs_7_) | copy-start | bytes 344068
  140.4 12.4 %collective-permute-start.20 = (bf16[4096,256]{1,0:T(8,128)(2,1)}, bf16[4096,256]{1,0:T(8,128)(2,1)S(1)}, u32[]{:S(2)}, u32[]{:S(2)}) collective-permute-start(bf16[4096,256]{1,0:T(8,128)(2,1)} %get-tuple-element.48), channel_id=1, source_target_pairs={{0,4},{4,0},{8,12},{12,8},{16,20},{20,16},{24,28},{28,24},{1,5},{5... | collective-permute-start | bytes 6291464 | tf_op jit(solution)/shard_map/ppermute | solution.py:508
  140.6 5.5 %collective-permute-start.24 = (f32[112,256]{1,0:T(8,128)S(1)}, f32[112,256]{1,0:T(8,128)S(1)}, u32[]{:S(2)}, u32[]{:S(2)}) collective-permute-start(f32[112,256]{1,0:T(8,128)S(1)} %copy-done.11), channel_id=1, source_target_pairs={{0,1},{1,0},{2,3},{3,2},{4,5},{5,4},{6,7},{7,6},{8,9},{9,8},{10,11... | collective-permute-start | bytes 344072 | tf_op jit(solution)/shard_map/ppermute | solution.py:512
  146.1 6.7 %collective-permute-start.25 = (f32[112,256]{1,0:T(8,128)S(1)}, f32[112,256]{1,0:T(8,128)S(1)}, u32[]{:S(2)}, u32[]{:S(2)}) collective-permute-start(f32[112,256]{1,0:T(8,128)S(1)} %add.69), channel_id=1, source_target_pairs={{0,3},{3,0},{1,2},{2,1},{4,7},{7,4},{5,6},{6,5},{8,11},{11,8},{9,1... | collective-permute-start | bytes 344072 | tf_op jit(solution)/shard_map/ppermute | solution.py:516
  152.8 28.2 %copy-start.9 = (bf16[4096,256]{1,0:T(8,128)(2,1)}, bf16[4096,256]{1,0:T(8,128)(2,1)S(1)}, u32[]{:S(2)}) copy-start(bf16[4096,256]{1,0:T(8,128)(2,1)S(1)} %collective-permute-done.20) | copy-start | bytes 6291460
  156.3 4.2 %collective-permute-start.26 = (bf16[112,256]{1,0:T(8,128)(2,1)S(1)}, bf16[112,256]{1,0:T(8,128)(2,1)S(1)}, u32[]{:S(2)}, u32[]{:S(2)}) collective-permute-start(bf16[112,256]{1,0:T(8,128)(2,1)S(1)} %add.70), channel_id=1, source_target_pairs={{0,16},{4,20},{8,24},{12,28},{16,0},{20,4},{24,8},{28,12},{1,17},{... | collective-permute-start | bytes 172040 | tf_op jit(solution)/shard_map/ppermute | solution.py:508
  160.5 13.3 %collective-permute-start.27 = (bf16[224,256]{1,0:T(8,128)(2,1)S(1)}, bf16[224,256]{1,0:T(8,128)(2,1)S(1)}, u32[]{:S(2)}, u32[]{:S(2)}) collective-permute-start(bf16[224,256]{1,0:T(8,128)(2,1)S(1)} %pad_maximum_fusion.2), channel_id=1, source_target_pairs={{0,8},{4,12},{8,0},{12,4},{16,24},{20,28},{24,16},{28,20},{1,9},{5... | collective-permute-start | bytes 344072 | tf_op jit(solution)/shard_map/ppermute | solution.py:508
  170.2 16.1 %collective-permute-start.23 = (bf16[1024,256]{1,0:T(8,128)(2,1)}, bf16[1024,256]{1,0:T(8,128)(2,1)}, u32[]{:S(2)}, u32[]{:S(2)}) collective-permute-start(bf16[1024,256]{1,0:T(8,128)(2,1)} %get-tuple-element.72.refs_17_), channel_id=1, source_target_pairs={{0,24},{4,28},{8,16},{12,20},{16,8},{20,12},{24,0},{28,4},{1,25},{... | collective-permute-start | bytes 1572872 | tf_op jit(solution)/shard_map/ppermute | solution.py:508
  171.5 21.5 %collective-permute-start.22 = (bf16[1024,256]{1,0:T(8,128)(2,1)}, bf16[1024,256]{1,0:T(8,128)(2,1)}, u32[]{:S(2)}, u32[]{:S(2)}) collective-permute-start(bf16[1024,256]{1,0:T(8,128)(2,1)} %get-tuple-element.73.refs_16_), channel_id=1, source_target_pairs={{0,16},{4,20},{8,24},{12,28},{16,0},{20,4},{24,8},{28,12},{1,17},{... | collective-permute-start | bytes 1572872 | tf_op jit(solution)/shard_map/ppermute | solution.py:508
  171.8 22.1 %collective-permute-start.21 = (bf16[1024,256]{1,0:T(8,128)(2,1)}, bf16[1024,256]{1,0:T(8,128)(2,1)}, u32[]{:S(2)}, u32[]{:S(2)}) collective-permute-start(bf16[1024,256]{1,0:T(8,128)(2,1)} %get-tuple-element.74.refs_15_), channel_id=1, source_target_pairs={{0,8},{4,12},{8,0},{12,4},{16,24},{20,28},{24,16},{28,20},{1,9},{5... | collective-permute-start | bytes 1572872 | tf_op jit(solution)/shard_map/ppermute | solution.py:508
  174.5 6.6 %collective-permute-start.28 = (bf16[448,256]{1,0:T(8,128)(2,1)}, bf16[448,256]{1,0:T(8,128)(2,1)S(1)}, u32[]{:S(2)}, u32[]{:S(2)}) collective-permute-start(bf16[448,256]{1,0:T(8,128)(2,1)} %pad_maximum_fusion.1), channel_id=1, source_target_pairs={{0,4},{4,0},{8,12},{12,8},{16,20},{20,16},{24,28},{28,24},{1,5},{5... | collective-permute-start | bytes 688136 | tf_op jit(solution)/shard_map/ppermute | solution.py:508
  181.1 12.8 %slice-start = ((bf16[4096,256]{1,0:T(8,128)(2,1)}), bf16[1024,256]{1,0:T(8,128)(2,1)S(1)}, s32[]{:S(2)}) async-start(bf16[4096,256]{1,0:T(8,128)(2,1)} %copy-done.9), calls=%async_computation | async-start | bytes 1048576 | tf_op jit(solution)/shard_map/slice | solution.py:542

commit v7 on v6

--- a/solution.py
+++ b/solution.py
@@ -16,7 +16,7 @@
 MIB = 1 << 20
 TN = (((0,), (0,)), ((), ()))
 NT = (((1,), (1,)), ((), ()))
-PEAK_FLOPS_PER_US = 1153.5e6
+SMALL = pl.CostEstimate(flops=1 << 20, bytes_accessed=1 << 16, transcendentals=0)
 
 
 LIVE_STEP = 4
@@ -26,10 +26,6 @@
 
 def params(mib):
     return pltpu.CompilerParams(vmem_limit_bytes=mib * MIB)
-
-
-def cost(microseconds):
-    return pl.CostEstimate(flops=int(microseconds * PEAK_FLOPS_PER_US), bytes_accessed=MIB, transcendentals=0)
 
 
 def mm(a, b, dims=(((1,), (0,)), ((), ()))):
@@ -120,7 +116,7 @@
             pltpu.SemaphoreType.DMA((n_picks,)),
         ],
         compiler_params=params(60),
-        cost_estimate=cost(2.0),
+        cost_estimate=SMALL,
         name="partial_messages",
     )(cols, counts, order, *pieces, tiles)
 
@@ -209,13 +205,14 @@
         in_specs=[SMEM] + [blocked(a) for a in (nodes, cot, *flat)] + [whole(a) for a in weights],
         out_specs=[blocked(a) for a in outs[:5]] + [whole(outs[5])] + [blocked(a) for a in outs[6:]],
         compiler_params=params(40),
-        cost_estimate=cost(5.0),
+        cost_estimate=SMALL,
         name="mlp",
     )(middle, nodes, cot, *flat, *weights)
     return result[:6], result[6:]
 
 
-def weight_kernel(factor, pieces, mine, nodes, msg, act, gpre, gproj, cot, w_in, vec, out, direct, grads):
+def weight_kernel(factor, pieces, n_after, mine, nodes, msg, act, gpre, gproj, cot, w_in, vec, *refs):
+    *outs, direct, grads = refs[n_after:]
     width = nodes.shape[1]
 
     @pl.when(pl.program_id(0) == 0)
@@ -232,15 +229,16 @@
     @pl.when(pl.program_id(0) == pl.num_programs(0) - 1)
     def _():
         if pieces == 1:
-            out[...] = grads[: out.shape[0]]
+            outs[0][...] = grads[: outs[0].shape[0]]
         else:
             rows = grads.shape[0] // pieces
             for place, member in enumerate(SWAP_ORDER):
                 where = pl.ds(pl.multiple_of((mine[0] ^ member) * rows, 8), rows)
-                out[place * rows : (place + 1) * rows] = grads[where]
-
-
-def weight_call(factor, pieces, mine, nodes, msg, act, gpre, gproj, cot, w_in, vec):
+                out, index = outs[2 * place // pieces], place % (pieces // 2)
+                out[index * rows : (index + 1) * rows] = grads[where]
+
+
+def weight_call(factor, pieces, mine, nodes, msg, act, gpre, gproj, cot, w_in, vec, after=()):
     rows, width = nodes.shape
     step = min(rows, 256)
     blocked = pl.BlockSpec((step, width), lambda i: (i, 0))
@@ -250,20 +248,20 @@
 
     padded = (3 * width + width // 2, width)
     if pieces == 1:
-        out = jax.ShapeDtypeStruct((3 * width + 8, width), F32)
+        outs = [jax.ShapeDtypeStruct((3 * width + 8, width), F32)]
     else:
-        out = jax.ShapeDtypeStruct(padded, F32)
+        outs = [jax.ShapeDtypeStruct((padded[0] // 2, width), F32)] * 2
     return pl.pallas_call(
-        functools.partial(weight_kernel, factor, pieces),
+        functools.partial(weight_kernel, factor, pieces, len(after)),
         grid=(rows // step,),
-        out_shape=[out, jax.ShapeDtypeStruct((rows, width), F32)],
-        in_specs=[SMEM] + [blocked] * 6 + [whole(w_in.shape), whole(vec.shape)],
-        out_specs=[whole(out.shape), blocked],
+        out_shape=[*outs, jax.ShapeDtypeStruct((rows, width), F32)],
+        in_specs=[SMEM] + [blocked] * 6 + [whole(w_in.shape), whole(vec.shape)] + [ANY] * len(after),
+        out_specs=[whole(out.shape) for out in outs] + [blocked],
         scratch_shapes=[pltpu.VMEM(padded, F32)],
         compiler_params=params(40),
-        cost_estimate=cost(3.0),
+        cost_estimate=SMALL,
         name="weight_grads",
-    )(mine, nodes, msg, act, gpre, gproj, cot, w_in, vec)
+    )(mine, nodes, msg, act, gpre, gproj, cot, w_in, vec, *after)
 
 
 def unpack_kernel(mine, parts, w_in, w_out, vectors, grads):
@@ -286,7 +284,7 @@
         out_specs=[VMEM] * 3,
         scratch_shapes=[pltpu.VMEM((3 * width + width // 2, width), F32)],
         compiler_params=params(16),
-        cost_estimate=cost(2.0),
+        cost_estimate=SMALL,
         name="weight_unpack",
     )(mine, parts)
 
@@ -384,8 +382,8 @@
             pltpu.SemaphoreType.DMA((len(grads),)),
             pltpu.SemaphoreType.DMA((1,)),
         ],
-        compiler_params=params(60),
-        cost_estimate=cost(5.0),
+        compiler_params=params(28 if gathered <= 8192 else 56),
+        cost_estimate=SMALL,
         name="back_terms",
     )(cols, counts, order, middle, *grads, tiles.reshape(row_blocks * slots, block, block), *after)
 
@@ -491,17 +489,10 @@
             pltpu.SemaphoreType.DMA((chunks, len(pieces[0]))),
             pltpu.SemaphoreType.DMA((len(groups),)),
         ],
-        compiler_params=params(60),
-        cost_estimate=cost(4.0),
+        compiler_params=params(16 if gathered <= 8192 else 40),
+        cost_estimate=SMALL,
         name="tile_grads",
     )(cols, counts, order, middle, *flat, *after)
-
-
-def add(*terms):
-    value = terms[0].astype(F32)
-    for term in terms[1:]:
-        value = value + term.astype(F32)
-    return value.astype(BF16)
 
 
 def swap(value, bit):
@@ -525,10 +516,6 @@
     return lax.ppermute(value, ("row", "col"), pairs)
 
 
-def held(value, *others):
-    return lax.optimization_barrier((value, *others))[0]
-
-
 def gather_square(nodes):
     pieces = []
     for piece in (nodes, swap(nodes, 2), swap(nodes, 4), swap(nodes, 6)):
@@ -536,41 +523,62 @@
     return pieces
 
 
-def pair_sums(even, odd, rows):
-    other = swap(odd, 1)
-    places = [slice(place * rows, (place + 1) * rows) for place in range(4)]
-    return (even[places[0]], other[places[0]]), [add(even[p], other[p]) for p in places[1:]]
-
-
-def reduce_square(sums):
-    return [swap(value, bit) for value, bit in zip(sums, (2, 4, 6))]
-
-
-def scatter_weights(terms):
-    for bit in (1, 2, 4):
+def sum_kernel(n_terms, n_gated, *refs):
+    flag, refs = refs[0], refs[1:]
+    total = None
+    for index, ref in enumerate(refs[: n_terms + n_gated]):
+        term = ref[...].astype(F32)
+        if index >= n_terms:
+            term = jnp.where(flag[0] > 0, term, 0.0)
+        total = term if total is None else total + term
+    refs[-1][...] = total.astype(refs[-1].dtype)
+
+
+def sum_call(flag, rows, terms, gated=(), dtype=BF16, after=()):
+    both = [*terms, *gated]
+    width = both[0][0].shape[1]
+    step = min(rows, 256)
+    steps = rows // step
+    return pl.pallas_call(
+        functools.partial(sum_kernel, len(terms), len(gated)),
+        grid=(steps,),
+        out_shape=jax.ShapeDtypeStruct((rows, width), dtype),
+        in_specs=[SMEM]
+        + [pl.BlockSpec((step, width), lambda i, piece=piece: (piece * steps + i, 0)) for _, piece in both]
+        + [ANY] * len(after),
+        out_specs=pl.BlockSpec((step, width), lambda i: (i, 0)),
+        compiler_params=params(8),
+        cost_estimate=SMALL,
+        name="sum_terms",
+    )(flag, *(array for array, _ in both), *after)
+
+
+def scatter_weights(kept, sent):
+    for bit in (1, 2):
+        terms = kept + swap(sent, bit)
         half = terms.shape[0] // 2
-        terms = terms[:half] + swap(terms[half:], bit)
-    return terms
-
-
-def level_weights(value):
-    value = value + outer_swap(value)
-    return value + mirror_swap(value)
+        kept, sent = terms[:half], terms[half:]
+    return kept, swap(sent, 4)
+
+
+def level_weights(flag, kept, received):
+    rows = kept.shape[0]
+    value = sum_call(flag, rows, [(kept, 0), (received, 0)], dtype=BF16)
+    value = sum_call(flag, rows, [(value, 0), (outer_swap(value), 0)])
+    return sum_call(flag, rows, [(value, 0), (mirror_swap(value), 0)])
 
 
 def gather_weights(value, width, mine):
-    value = value.astype(BF16)
     for bit in (4, 2, 1):
         value = jnp.concatenate([value, swap(value, bit)], axis=0)
     return unpack_call(mine, value, width)
 
 
-def reduce_line(far, near, pair, own, inner):
-    far_in = outer_swap(far)
-    near_in = outer_swap(held(near, far_in))
-    far_sum = inner_swap(add(far, far_in))
-    near_sum = inner_swap(add(near, near_in))
-    pair_in = outer_swap(add(pair, jnp.where(inner, far_sum, jnp.zeros_like(far_sum))))
+def reduce_line(far, near, pair, own, flag):
+    rows = own.shape[0]
+    far_sum = inner_swap(sum_call(flag, rows, [(far, 0), (outer_swap(far), 0)]))
+    near_sum = inner_swap(sum_call(flag, rows, [(near, 0), (outer_swap(near), 0)]))
+    pair_in = outer_swap(sum_call(flag, rows, [(pair, 0)], [(far_sum, 0)]))
     return own, pair_in, near_sum
 
 
@@ -603,7 +611,7 @@
         pieces = [gather_square(nodes)]
         far, near = forward_call(cols, counts, order, pieces[0], tile_local, ((0,), (1,)), rows)
         pair, own = forward_call(cols, counts, order, pieces[0], tile_local, ((2,), (3,)), rows)
-        parts = [reduce_line(far, near, pair, own, inner)]
+        parts = [reduce_line(far, near, pair, own, middle)]
         kinds = [("all", "all", "inner")]
     else:
         order = jnp.arange(n_col, dtype=jnp.int32)
@@ -618,31 +626,32 @@
     )
     factor = float(rows * n_row * n_col) ** -0.5
     mine = lax.axis_index("row").astype(jnp.int32).reshape(1)
-    weight_terms, direct = weight_call(
-        factor, n_row if square_line else 1, mine, nodes, message, act, gpre_b, gproj, cotangent, w_in, vec
-    )
+    weight_args = (mine, nodes, message, act, gpre_b, gproj, cotangent, w_in, vec)
     if square_line:
         halves = ((1, 3, 5, 7), (0, 2, 4, 6))
         grads = [gather_line(gmsgs[0])]
+        kept, sent, direct = weight_call(factor, n_row, *weight_args, (grads[0][1], grads[0][2]))
+        all_weights = level_weights(middle, *scatter_weights(kept, sent))
+        weights = gather_weights(all_weights, width, mine)
         near_grads, token = tile_grad_call(
             cols, counts, order, middle, [grads[0][:2]], pieces, tile_local.shape, rows, (3, 2),
             after=(grads[0][3], grads[0][4]),
         )
-        row_weights = scatter_weights(held(weight_terms, token))
         odd, even = back_call(
-            cols, counts, order, middle, grads[0], tile_local, total, gathered, halves, (row_weights,)
-        )
-        all_weights = level_weights(row_weights)
-        own_terms, sums = pair_sums(even, odd, rows)
-        terms = (*own_terms, *reduce_square(sums))
-        weights = gather_weights(held(all_weights, *sums), width, mine)
-        terms = held(terms, *weights)
-        back = sum(term.astype(F32) for term in terms)
+            cols, counts, order, middle, grads[0], tile_local, total, gathered, halves, (token, weights[2])
+        )
+        other = swap(odd, 1)
+        sums = [sum_call(middle, rows, [(even, piece), (other, piece)]) for piece in (1, 2, 3)]
+        x_side, y_side, diagonal = [swap(value, bit) for value, bit in zip(sums, (2, 4, 6))]
         grad_tiles, _ = tile_grad_call(
             cols, counts, order, middle, grads, pieces, tile_local.shape, rows, (1, 0), near_grads, sums
         )
+        grad_nodes = sum_call(
+            middle, rows, [(term, 0) for term in (direct, even, other, x_side, y_side, diagonal)]
+        )
     else:
         grads = [[lax.all_gather(gmsgs[0], "col", axis=0, tiled=True)]]
+        weight_terms, direct = weight_call(factor, 1, *weight_args)
         weight_sums = lax.psum(weight_terms, ("row", "col"))
         weights = (
             weight_sums[: 2 * width],
@@ -652,11 +661,11 @@
         (terms,) = back_call(
             cols, counts, order, middle, grads[0], tile_local, total, gathered, (tuple(range(n_row)),)
         )
-        back = lax.psum_scatter(terms, "row", scatter_dimension=0, tiled=True).astype(F32)
+        back = lax.psum_scatter(terms, "row", scatter_dimension=0, tiled=True)
+        grad_nodes = sum_call(middle, rows, [(direct, 0), (back, 0)])
         grad_tiles, _ = tile_grad_call(
             cols, counts, order, middle, grads, pieces, tile_local.shape, rows, tuple(range(n_col))
         )
-    grad_nodes = (direct + back).astype(BF16)
     grad_tiles = grad_tiles.reshape(tiles.shape)
     return (updated, grad_nodes, grad_tiles, *weights)
 

time: 197 us -> 186 us (0.944)
  waiting for transfers between devices: 94.7 us -> 106 us
  other arithmetic: 12.1 us -> 1.25 us
  starting transfers between devices: 41.3 us -> 31.7 us
  Pallas kernels: 42.5 us -> 39.1 us
    ppermute x17, waiting for transfers between devices: 41.3 us -> 58.8 us  [swap(): return lax.ppermute(value, 'row', [(i, i ^ bit) for i in range(8)])]
    ppermute x7, starting transfers between devices: 25.1 us -> 13.4 us  [outer_swap(): return lax.ppermute(value, 'col', [(0, 1), (1, 0), (2, 3), (3, 2)])]
    convert_element_type x5 -> x0, other arithmetic: 9.32 us -> none  [the longest x4 6.79 us: add(): return value.astype(BF16)]
    ppermute x7, waiting for transfers between devices: 48.8 us -> 44.3 us  [outer_swap(): return lax.ppermute(value, 'col', [(0, 1), (1, 0), (2, 3), (3, 2)])]
    pallas_call x1, Pallas kernels: 10.3 us -> 6.8 us  [back_call(): pl.pallas_call(functools.partial(back_kernel, rows, slots, len(grads), le...]
    pallas_call x1 -> x11, Pallas kernels: 1.52 us -> 4.36 us  [the longest x10 2.82 us: sum_call(): pl.pallas_call(functools.partial(sum_kernel, len(terms), len(gated)), gri...]
    pallas_call x2, Pallas kernels: 14.2 us -> 11.5 us  [tile_grad_call(): pl.pallas_call(functools.partial(tile_grad_kernel, rows, slots, len(grads...]
    unnamed x47 -> x57, local copies, waits for them, and re-layouts: 3.67 us -> 5.53 us
  transfers between devices with their start and end apart: 29 -> 29, of which waited for: 16 -> 19; matrix products, arithmetic and copies ran while one was open for 4% -> 1% of each run, Pallas kernels for 11% -> 10%
where the time goes in v7:
time: 186 us; the launch traced here: 185 us
  waiting for transfers between devices  106 us (57%)
  Pallas kernels  39.1 us (21%)
  starting transfers between devices  31.7 us (17%)
  local copies, waits for them, and re-layouts  5.67 us (3%)
    ppermute x17, waiting for transfers between devices, swap(): return lax.ppermute(value, 'row', [(i, i ^ bit) for i in range(8)])  58.8 us
    ppermute x7, waiting for transfers between devices, outer_swap(): return lax.ppermute(value, 'col', [(0, 1), (1, 0), (2, 3), (3, 2)])  44.3 us
    ppermute x17, starting transfers between devices, swap(): return lax.ppermute(value, 'row', [(i, i ^ bit) for i in range(8)])  15.2 us
    ppermute x7, starting transfers between devices, outer_swap(): return lax.ppermute(value, 'col', [(0, 1), (1, 0), (2, 3), (3, 2)])  13.4 us
    pallas_call x2, Pallas kernels, tile_grad_call(): pl.pallas_call(functools.partial(tile_grad_kernel, rows, slots, len(grads...  11.5 us
    pallas_call x2, Pallas kernels, forward_call(): pl.pallas_call(functools.partial(forward_kernel, outputs, len(pieces)), o...  10.8 us
    pallas_call x1, Pallas kernels, back_call(): pl.pallas_call(functools.partial(back_kernel, rows, slots, len(grads), le...  6.8 us
    unnamed x57, local copies, waits for them, and re-layouts  5.53 us
  transfers between devices with their start and end apart: 29, of which 19 were waited for; matrix products, arithmetic and copies ran while one was open for 1% of the time, Pallas kernels for 10%

profile of v7, /device:TPU:0, one launch (start us, length us, event | category | flops | bytes accessed | tf_op | source)
XLA Modules:
  0.0 185.2 jit_solution(584946834689191231)
XLA Ops:
  0.6 3.0 %collective-permute-start.1 = (bf16[1024,256]{1,0:T(8,128)(2,1)}, bf16[1024,256]{1,0:T(8,128)(2,1)S(1)}, u32[]{:S(2)}, u32[]{:S(2)}) collective-permute-start(bf16[1024,256]{1,0:T(8,128)(2,1)} %refs_6_.1), channel_id=1, source_target_pairs={{0,8},{4,12},{8,0},{12,4},{16,24},{20,28},{24,16},{28,20},{1,9},{5... | collective-permute-start | bytes 1572872 | tf_op jit(solution)/shard_map/ppermute | solution.py:499
  3.6 1.5 collective-permute-start.3
  5.2 11.4 %collective-permute-done.1.refs_2_.refs_4_.refs_8_ = bf16[1024,256]{1,0:T(8,128)(2,1)S(1)} collective-permute-done((bf16[1024,256]{1,0:T(8,128)(2,1)}, bf16[1024,256]{1,0:T(8,128)(2,1)S(1)}, u32[]{:S(2)}, u32[]{:S(2)}) %collective-permute-start.1) | collective-permute-done | bytes 524320 | tf_op jit(solution)/shard_map/ppermute | solution.py:499
  16.6 11.9 %collective-permute-done.3.refs_4_.refs_6_.refs_10_ = bf16[1024,256]{1,0:T(8,128)(2,1)S(1)} collective-permute-done((bf16[1024,256]{1,0:T(8,128)(2,1)}, bf16[1024,256]{1,0:T(8,128)(2,1)S(1)}, u32[]{:S(2)}, u32[]{:S(2)}) %collective-permute-start.3) | collective-permute-done | bytes 524320 | tf_op jit(solution)/shard_map/ppermute | solution.py:499
  28.5 0.5 collective-permute-start.6
  29.0 0.8 copy.19
  29.7 0.1 reshape.43
  29.9 0.6 pad_add_fusion.order
  30.5 0.5 fusion.cols
  31.0 0.2 collective-permute-done.6.refs_7_.refs_9_.refs_13_
  31.3 0.5 copy-done.8
  31.8 0.2 copy-done.10
  31.9 0.2 copy-done.12
  32.1 5.3 %partial_messages.3 = (bf16[1024,256]{1,0:T(8,128)(2,1)}, bf16[1024,256]{1,0:T(8,128)(2,1)}) custom-call(s32[128]{0:T(128)} %fusion.cols, s32[32]{0:T(128)} %bitcast.20, s32[4]{0:T(128)} %pad_add_fusion.order, bf16[1024,256]{1,0:T(8,128)(2,1)} %refs_6_.1, bf16[1024,256]{1,0:T(8,128)(2,1)} %copy-done.8, bf16[1024,256]{1,0:T(8,128)(2,1)} %copy-done.2, ...), custom_call_target="tpu_custom_call" | custom-call | flops 1048576 | bytes 65536 | tf_op jit(solution)/shard_map/partial_messages/pallas_call | solution.py:107
  37.5 1.7 collective-permute-start.7
  39.1 0.4 collective-permute-start.10
  39.6 13.0 %collective-permute-done.7.refs_2_ = bf16[1024,256]{1,0:T(8,128)(2,1)S(1)} collective-permute-done((bf16[1024,256]{1,0:T(8,128)(2,1)}, bf16[1024,256]{1,0:T(8,128)(2,1)S(1)}, u32[]{:S(2)}, u32[]{:S(2)}) %collective-permute-start.7) | collective-permute-done | bytes 524320 | tf_op jit(solution)/shard_map/ppermute | solution.py:503
  52.5 1.0 copy-done.17
  53.5 0.2 sum_terms.10
  53.8 0.1 collective-permute-start.8
  53.9 5.5 %partial_messages.2 = (bf16[1024,256]{1,0:T(8,128)(2,1)}, bf16[1024,256]{1,0:T(8,128)(2,1)}) custom-call(s32[128]{0:T(128)} %fusion.cols, s32[32]{0:T(128)} %bitcast.21, s32[4]{0:T(128)} %pad_add_fusion.order, bf16[1024,256]{1,0:T(8,128)(2,1)} %refs_6_.1, bf16[1024,256]{1,0:T(8,128)(2,1)} %copy-done.8, bf16[1024,256]{1,0:T(8,128)(2,1)} %copy-done.2, ...), custom_call_target="tpu_custom_call" | custom-call | flops 1048576 | bytes 65536 | tf_op jit(solution)/shard_map/partial_messages/pallas_call | solution.py:107
  59.4 3.6 %collective-permute-done.10.refs_2_ = bf16[1024,256]{1,0:T(8,128)(2,1)S(1)} collective-permute-done((bf16[1024,256]{1,0:T(8,128)(2,1)}, bf16[1024,256]{1,0:T(8,128)(2,1)S(1)}, u32[]{:S(2)}, u32[]{:S(2)}) %collective-permute-start.10) | collective-permute-done | bytes 524320 | tf_op jit(solution)/shard_map/ppermute | solution.py:503
  62.9 0.2 sum_terms.12
  63.1 0.1 collective-permute-start.11
  63.2 1.0 copy-done.18
  64.3 0.2 sum_terms.11
  64.5 5.7 %collective-permute-start.9 = (bf16[1024,256]{1,0:T(8,128)(2,1)S(1)}, bf16[1024,256]{1,0:T(8,128)(2,1)S(1)}, u32[]{:S(2)}, u32[]{:S(2)}) collective-permute-start(bf16[1024,256]{1,0:T(8,128)(2,1)S(1)} %sum_terms.11), channel_id=1, source_target_pairs={{0,1},{1,0},{2,3},{3,2},{4,5},{5,4},{6,7},{7,6},{8,9},{9,8},{10,11... | collective-permute-start | bytes 1572872 | tf_op jit(solution)/shard_map/ppermute | solution.py:503
  70.2 8.7 %collective-permute-done.9.refs_1_ = bf16[1024,256]{1,0:T(8,128)(2,1)S(1)} collective-permute-done((bf16[1024,256]{1,0:T(8,128)(2,1)S(1)}, bf16[1024,256]{1,0:T(8,128)(2,1)S(1)}, u32[]{:S(2)}, u32[]{:S(2)}) %collective-permute-start.9) | collective-permute-done | bytes 524320 | tf_op jit(solution)/shard_map/ppermute | solution.py:503
  78.9 1.0 copy-done.19
  80.0 4.7 %mlp.1 = (bf16[1024,256]{1,0:T(8,128)(2,1)}, bf16[1024,256]{1,0:T(8,128)(2,1)S(1)}, bf16[1024,256]{1,0:T(8,128)(2,1)S(1)}, bf16[1024,256]{1,0:T(8,128)(2,1)S(1)}...) custom-call(s32[1]{0:T(128)} %bitcast.refs_0_.middle, ...), custom_call_target="tpu_custom_call" | custom-call | flops 1048576 | bytes 65536 | tf_op jit(solution)/shard_map/mlp/pallas_call | solution.py:201
  84.6 1.6 collective-permute-start.12
  86.2 9.7 %collective-permute-done.12.refs_0_.refs_1_ = bf16[1024,256]{1,0:T(8,128)(2,1)S(1)} collective-permute-done((bf16[1024,256]{1,0:T(8,128)(2,1)S(1)}, bf16[1024,256]{1,0:T(8,128)(2,1)S(1)}, u32[]{:S(2)}, u32[]{:S(2)}) %collective-permute-start.12) | collective-permute-done | bytes 524320 | tf_op jit(solution)/shard_map/ppermute | solution.py:503
  96.0 1.5 weight_grads.1
  97.5 0.1 collective-permute-start.17
  97.6 1.8 collective-permute-done.17
  99.5 1.7 collective-permute-start.18
  101.2 6.0 %collective-permute-done.18 = f32[224,256]{1,0:T(8,128)S(1)} collective-permute-done((f32[224,256]{1,0:T(8,128)S(1)}, f32[224,256]{1,0:T(8,128)S(1)}, u32[]{:S(2)}, u32[]{:S(2)}) %collective-permute-start.18) | collective-permute-done | bytes 229408 | tf_op jit(solution)/shard_map/ppermute | solution.py:499
  107.3 1.6 collective-permute-start.19
  108.9 3.2 %collective-permute-done.19.refs_2_ = f32[112,256]{1,0:T(8,128)S(1)} collective-permute-done((f32[112,256]{1,0:T(8,128)S(1)}, f32[112,256]{1,0:T(8,128)S(1)}, u32[]{:S(2)}, u32[]{:S(2)}) %collective-permute-start.19) | collective-permute-done | bytes 114720 | tf_op jit(solution)/shard_map/ppermute | solution.py:499
  112.1 2.4 %collective-permute-start.20 = (bf16[112,256]{1,0:T(8,128)(2,1)S(1)}, bf16[112,256]{1,0:T(8,128)(2,1)S(1)}, u32[]{:S(2)}, u32[]{:S(2)}) collective-permute-start(bf16[112,256]{1,0:T(8,128)(2,1)S(1)} %sum_terms.13.refs_1_), channel_id=1, source_target_pairs={{0,1},{1,0},{2,3},{3,2},{4,5},{5,4},{6,7},{7,6},{8,9},{9,8},{10,11... | collective-permute-start | bytes 172040 | tf_op jit(solution)/shard_map/ppermute | solution.py:503
  114.5 2.2 %collective-permute-done.20.refs_2_ = bf16[112,256]{1,0:T(8,128)(2,1)S(1)} collective-permute-done((bf16[112,256]{1,0:T(8,128)(2,1)S(1)}, bf16[112,256]{1,0:T(8,128)(2,1)S(1)}, u32[]{:S(2)}, u32[]{:S(2)}) %collective-permute-start.20) | collective-permute-done | bytes 57376 | tf_op jit(solution)/shard_map/ppermute | solution.py:503
  116.7 3.0 %collective-permute-start.21 = (bf16[112,256]{1,0:T(8,128)(2,1)S(1)}, bf16[112,256]{1,0:T(8,128)(2,1)S(1)}, u32[]{:S(2)}, u32[]{:S(2)}) collective-permute-start(bf16[112,256]{1,0:T(8,128)(2,1)S(1)} %sum_terms.14.refs_1_), channel_id=1, source_target_pairs={{0,3},{3,0},{1,2},{2,1},{4,7},{7,4},{5,6},{6,5},{8,11},{11,8},{9,1... | collective-permute-start | bytes 172040 | tf_op jit(solution)/shard_map/ppermute | solution.py:507
  119.7 3.2 %collective-permute-done.21.refs_2_ = bf16[112,256]{1,0:T(8,128)(2,1)S(1)} collective-permute-done((bf16[112,256]{1,0:T(8,128)(2,1)S(1)}, bf16[112,256]{1,0:T(8,128)(2,1)S(1)}, u32[]{:S(2)}, u32[]{:S(2)}) %collective-permute-start.21) | collective-permute-done | bytes 57376 | tf_op jit(solution)/shard_map/ppermute | solution.py:507
  122.8 1.6 collective-permute-start.22
  124.4 1.0 collective-permute-start.14
  125.4 1.6 collective-permute-done.22
  127.1 1.4 collective-permute-start.23
  128.5 0.6 collective-permute-start.16
  129.1 2.8 %collective-permute-done.23 = bf16[224,256]{1,0:T(8,128)(2,1)S(1)} collective-permute-done((bf16[224,256]{1,0:T(8,128)(2,1)S(1)}, bf16[224,256]{1,0:T(8,128)(2,1)S(1)}, u32[]{:S(2)}, u32[]{:S(2)}) %collective-permute-start.23) | collective-permute-done | bytes 114720 | tf_op jit(solution)/shard_map/ppermute | solution.py:499
  132.0 0.1 collective-permute-start.24
  132.1 7.2 %collective-permute-done.14.refs_10_.refs_3_ = bf16[1024,256]{1,0:T(8,128)(2,1)S(1)} collective-permute-done((bf16[1024,256]{1,0:T(8,128)(2,1)S(1)}, bf16[1024,256]{1,0:T(8,128)(2,1)S(1)}, u32[]{:S(2)}, u32[]{:S(2)}) %collective-permute-start.14) | collective-permute-done | bytes 524320 | tf_op jit(solution)/shard_map/ppermute | solution.py:503
  139.4 5.7 %tile_grads.2 = (bf16[128,128,128]{2,1,0:T(8,128)(2,1)}, f32[8,128]{1,0:T(8,128)S(1)}) custom-call(s32[128]{0:T(128)S(1)} %copy-done.23, s32[32]{0:T(128)S(1)} %bitcast.22, s32[4]{0:T(128)S(1)} %copy-done.21, s32[1]{0:T(128)} %bitcast.refs_0_.middle, bf16[1024,256]{1,0:T(8,128)(2,1)S(1)} %get-tuple-element.38.refs_0_, ...), custom_call_target="tpu_custom_call" | custom-call | flops 1048576 | bytes 65536 | tf_op jit(solution)/shard_map/tile_grads/pallas_call | solution.py:471
  145.1 1.0 weight_unpack.1
  146.1 0.7 copy-done.24
  146.8 6.8 %back_terms.1 = (bf16[4096,256]{1,0:T(8,128)(2,1)S(1)}, bf16[4096,256]{1,0:T(8,128)(2,1)S(1)}) custom-call(s32[128]{0:T(128)S(1)} %copy-done.23, s32[32]{0:T(128)S(1)} %bitcast.23, s32[4]{0:T(128)S(1)} %copy-done.21, s32[1]{0:T(128)} %bitcast.refs_0_.middle, bf16[1024,256]{1,0:T(8,128)(2,1)S(1)} %get-tuple-element.38.refs_0_, ...), custom_call_target="tpu_custom_call" | custom-call | flops 1048576 | bytes 65536 | tf_op jit(solution)/shard_map/back_terms/pallas_call | solution.py:372
  153.7 4.1 %collective-permute-done.25.refs_2_.refs_3_ = bf16[4096,256]{1,0:T(8,128)(2,1)S(1)} collective-permute-done((bf16[4096,256]{1,0:T(8,128)(2,1)S(1)}, bf16[4096,256]{1,0:T(8,128)(2,1)S(1)}, u32[]{:S(2)}, u32[]{:S(2)}) %collective-permute-start.25) | collective-permute-done | bytes 2097184 | tf_op jit(solution)/shard_map/ppermute | solution.py:499
  157.8 0.2 sum_terms.16.refs_15_
  158.1 0.2 sum_terms.17.refs_16_
  158.4 0.2 sum_terms.18.refs_17_
  158.6 3.5 %collective-permute-start.28 = (bf16[1024,256]{1,0:T(8,128)(2,1)S(1)}, bf16[1024,256]{1,0:T(8,128)(2,1)S(1)}, u32[]{:S(2)}, u32[]{:S(2)}) collective-permute-start(bf16[1024,256]{1,0:T(8,128)(2,1)S(1)} %sum_terms.18.refs_17_), channel_id=1, source_target_pairs={{0,24},{4,28},{8,16},{12,20},{16,8},{20,12},{24,0},{28,4},{1,25},{... | collective-permute-start | bytes 1572872 | tf_op jit(solution)/shard_map/ppermute | solution.py:499
  162.1 5.9 %tile_grads.3 = (bf16[128,128,128]{2,1,0:T(8,128)(2,1)}, f32[8,128]{1,0:T(8,128)}) custom-call(s32[128]{0:T(128)S(1)} %copy-done.23, s32[32]{0:T(128)S(1)} %bitcast.24, s32[4]{0:T(128)S(1)} %copy-done.21, s32[1]{0:T(128)} %bitcast.refs_0_.middle, bf16[1024,256]{1,0:T(8,128)(2,1)S(1)} %get-tuple-element.38.refs_0_, ...), custom_call_target="tpu_custom_call", output_to_operand_aliasing={{0}: (18, {})} | custom-call | flops 1048576 | bytes 65536 | tf_op jit(solution)/shard_map/tile_grads/pallas_call | solution.py:471
  167.9 4.9 %collective-permute-done.26.refs_4_ = bf16[1024,256]{1,0:T(8,128)(2,1)S(1)} collective-permute-done((bf16[1024,256]{1,0:T(8,128)(2,1)S(1)}, bf16[1024,256]{1,0:T(8,128)(2,1)S(1)}, u32[]{:S(2)}, u32[]{:S(2)}) %collective-permute-start.26) | collective-permute-done | bytes 524320 | tf_op jit(solution)/shard_map/ppermute | solution.py:499
  172.8 10.7 %collective-permute-done.27.refs_5_ = bf16[1024,256]{1,0:T(8,128)(2,1)S(1)} collective-permute-done((bf16[1024,256]{1,0:T(8,128)(2,1)S(1)}, bf16[1024,256]{1,0:T(8,128)(2,1)S(1)}, u32[]{:S(2)}, u32[]{:S(2)}) %collective-permute-start.27) | collective-permute-done | bytes 524320 | tf_op jit(solution)/shard_map/ppermute | solution.py:499
  183.6 1.6 sum_terms.19
  (79 shorter events, 0.7 us)
Async XLA Ops:
  0.6 16.0 %collective-permute-start.1 = (bf16[1024,256]{1,0:T(8,128)(2,1)}, bf16[1024,256]{1,0:T(8,128)(2,1)S(1)}, u32[]{:S(2)}, u32[]{:S(2)}) collective-permute-start(bf16[1024,256]{1,0:T(8,128)(2,1)} %refs_6_.1), channel_id=1, source_target_pairs={{0,8},{4,12},{8,0},{12,4},{16,24},{20,28},{24,16},{28,20},{1,9},{5... | collective-permute-start | bytes 1572872 | tf_op jit(solution)/shard_map/ppermute | solution.py:499
  3.6 24.8 %collective-permute-start.3 = (bf16[1024,256]{1,0:T(8,128)(2,1)}, bf16[1024,256]{1,0:T(8,128)(2,1)S(1)}, u32[]{:S(2)}, u32[]{:S(2)}) collective-permute-start(bf16[1024,256]{1,0:T(8,128)(2,1)} %refs_6_.1), channel_id=1, source_target_pairs={{0,16},{4,20},{8,24},{12,28},{16,0},{20,4},{24,8},{28,12},{1,17},{... | collective-permute-start | bytes 1572872 | tf_op jit(solution)/shard_map/ppermute | solution.py:499
  5.2 23.3 %collective-permute-start.5 = (bf16[1024,256]{1,0:T(8,128)(2,1)}, bf16[1024,256]{1,0:T(8,128)(2,1)S(1)}, u32[]{:S(2)}, u32[]{:S(2)}) collective-permute-start(bf16[1024,256]{1,0:T(8,128)(2,1)} %refs_6_.1), channel_id=1, source_target_pairs={{0,24},{4,28},{8,16},{12,20},{16,8},{20,12},{24,0},{28,4},{1,25},{... | collective-permute-start | bytes 1572872 | tf_op jit(solution)/shard_map/ppermute | solution.py:499
  5.2 25.8 %collective-permute-start = (bf16[1024,256]{1,0:T(8,128)(2,1)}, bf16[1024,256]{1,0:T(8,128)(2,1)S(1)}, u32[]{:S(2)}, u32[]{:S(2)}) collective-permute-start(bf16[1024,256]{1,0:T(8,128)(2,1)} %refs_6_.1), channel_id=1, source_target_pairs={{0,4},{4,0},{8,12},{12,8},{16,20},{20,16},{24,28},{28,24},{1,5},{5... | collective-permute-start | bytes 1572872 | tf_op jit(solution)/shard_map/ppermute | solution.py:499
  16.6 14.7 %copy-start.2 = (bf16[1024,256]{1,0:T(8,128)(2,1)}, bf16[1024,256]{1,0:T(8,128)(2,1)S(1)}, u32[]{:S(2)}) copy-start(bf16[1024,256]{1,0:T(8,128)(2,1)S(1)} %collective-permute-done.1.refs_2_.refs_4_.refs_8_) | copy-start | bytes 1572868
  16.6 14.4 %collective-permute-start.2 = (bf16[1024,256]{1,0:T(8,128)(2,1)S(1)}, bf16[1024,256]{1,0:T(8,128)(2,1)S(1)}, u32[]{:S(2)}, u32[]{:S(2)}) collective-permute-start(bf16[1024,256]{1,0:T(8,128)(2,1)S(1)} %collective-permute-done.1.refs_2_.refs_4_.refs_8_), channel_id=1, source_target_pairs={{0,4},{4,0},{8,12},{12,8},{16,20},{20,16},{24,28},{28,24},{1,5},{5... | collective-permute-start | bytes 1572872 | tf_op jit(solution)/shard_map/ppermute | solution.py:499
  28.5 2.8 %copy-start.4 = (bf16[1024,256]{1,0:T(8,128)(2,1)}, bf16[1024,256]{1,0:T(8,128)(2,1)S(1)}, u32[]{:S(2)}) copy-start(bf16[1024,256]{1,0:T(8,128)(2,1)S(1)} %collective-permute-done.3.refs_4_.refs_6_.refs_10_) | copy-start | bytes 1572868
  28.5 2.5 %collective-permute-start.4 = (bf16[1024,256]{1,0:T(8,128)(2,1)S(1)}, bf16[1024,256]{1,0:T(8,128)(2,1)S(1)}, u32[]{:S(2)}, u32[]{:S(2)}) collective-permute-start(bf16[1024,256]{1,0:T(8,128)(2,1)S(1)} %collective-permute-done.3.refs_4_.refs_6_.refs_10_), channel_id=1, source_target_pairs={{0,4},{4,0},{8,12},{12,8},{16,20},{20,16},{24,28},{28,24},{1,5},{5... | collective-permute-start | bytes 1572872 | tf_op jit(solution)/shard_map/ppermute | solution.py:499
  28.5 2.8 %copy-start.6 = (bf16[1024,256]{1,0:T(8,128)(2,1)}, bf16[1024,256]{1,0:T(8,128)(2,1)S(1)}, u32[]{:S(2)}) copy-start(bf16[1024,256]{1,0:T(8,128)(2,1)S(1)} %collective-permute-done.5.refs_6_.refs_8_.refs_12_) | copy-start | bytes 1572868
  28.5 2.8 %collective-permute-start.6 = (bf16[1024,256]{1,0:T(8,128)(2,1)S(1)}, bf16[1024,256]{1,0:T(8,128)(2,1)}, u32[]{:S(2)}, u32[]{:S(2)}) collective-permute-start(bf16[1024,256]{1,0:T(8,128)(2,1)S(1)} %collective-permute-done.5.refs_6_.refs_8_.refs_12_), channel_id=1, source_target_pairs={{0,4},{4,0},{8,12},{12,8},{16,20},{20,16},{24,28},{28,24},{1,5},{5... | collective-permute-start | bytes 1572872 | tf_op jit(solution)/shard_map/ppermute | solution.py:499
  31.0 0.8 copy-start.8
  31.0 1.0 copy-start.10
  31.0 1.1 copy-start.12
  37.5 15.0 %collective-permute-start.7 = (bf16[1024,256]{1,0:T(8,128)(2,1)}, bf16[1024,256]{1,0:T(8,128)(2,1)S(1)}, u32[]{:S(2)}, u32[]{:S(2)}) collective-permute-start(bf16[1024,256]{1,0:T(8,128)(2,1)} %get-tuple-element.30.refs_1_), channel_id=1, source_target_pairs={{0,1},{1,0},{2,3},{3,2},{4,5},{5,4},{6,7},{7,6},{8,9},{9,8},{10,11... | collective-permute-start | bytes 1572872 | tf_op jit(solution)/shard_map/ppermute | solution.py:503
  39.1 23.8 %collective-permute-start.10 = (bf16[1024,256]{1,0:T(8,128)(2,1)}, bf16[1024,256]{1,0:T(8,128)(2,1)S(1)}, u32[]{:S(2)}, u32[]{:S(2)}) collective-permute-start(bf16[1024,256]{1,0:T(8,128)(2,1)} %get-tuple-element.31.refs_1_), channel_id=1, source_target_pairs={{0,1},{1,0},{2,3},{3,2},{4,5},{5,4},{6,7},{7,6},{8,9},{9,8},{10,11... | collective-permute-start | bytes 1572872 | tf_op jit(solution)/shard_map/ppermute | solution.py:503
  52.5 1.0 copy-start.17
  53.7 9.2 %copy-start.16 = (bf16[1024,256]{1,0:T(8,128)(2,1)S(1)}, bf16[1024,256]{1,0:T(8,128)(2,1)}, u32[]{:S(2)}) copy-start(bf16[1024,256]{1,0:T(8,128)(2,1)} %get-tuple-element.31.refs_1_) | copy-start | bytes 1572868
  53.7 25.1 %copy-start.1 = (bf16[1024,256]{1,0:T(8,128)(2,1)S(1)}, bf16[1024,256]{1,0:T(8,128)(2,1)}, u32[]{:S(2)}) copy-start(bf16[1024,256]{1,0:T(8,128)(2,1)} %refs_6_.1) | copy-start | bytes 1572868
  53.7 25.1 %copy-start.14 = (bf16[1024,256]{1,0:T(8,128)(2,1)S(1)}, bf16[1024,256]{1,0:T(8,128)(2,1)}, u32[]{:S(2)}) copy-start(bf16[1024,256]{1,0:T(8,128)(2,1)} %cot.3) | copy-start | bytes 1572868
  53.8 25.1 %copy-start.15 = (bf16[512,256]{1,0:T(8,128)(2,1)S(1)}, bf16[512,256]{1,0:T(8,128)(2,1)}, u32[]{:S(2)}) copy-start(bf16[512,256]{1,0:T(8,128)(2,1)} %w_in.1) | copy-start | bytes 786436
  53.8 25.1 %copy-start.20 = (bf16[256,256]{1,0:T(8,128)(2,1)S(1)}, bf16[256,256]{1,0:T(8,128)(2,1)}, u32[]{:S(2)}) copy-start(bf16[256,256]{1,0:T(8,128)(2,1)} %refs_5_.1) | copy-start | bytes 393220
  53.8 25.1 %copy-start.25 = (f32[256]{0:T(256)S(1)}, f32[256]{0:T(256)}, u32[]{:S(2)}) copy-start(f32[256]{0:T(256)} %param.15) | copy-start | bytes 3076
  53.8 25.1 %copy-start.26 = (f32[256]{0:T(256)S(1)}, f32[256]{0:T(256)}, u32[]{:S(2)}) copy-start(f32[256]{0:T(256)} %param.17) | copy-start | bytes 3076
  53.8 25.1 %copy-start.27 = (f32[256]{0:T(256)S(1)}, f32[256]{0:T(256)}, u32[]{:S(2)}) copy-start(f32[256]{0:T(256)} %param.18) | copy-start | bytes 3076
  53.8 9.4 %collective-permute-start.8 = (bf16[1024,256]{1,0:T(8,128)(2,1)S(1)}, bf16[1024,256]{1,0:T(8,128)(2,1)S(1)}, u32[]{:S(2)}, u32[]{:S(2)}) collective-permute-start(bf16[1024,256]{1,0:T(8,128)(2,1)S(1)} %sum_terms.10), channel_id=1, source_target_pairs={{0,4},{1,2},{2,1},{3,7},{4,0},{5,6},{6,5},{7,3},{8,12},{9,10},{10,... | collective-permute-start | bytes 1572872 | tf_op jit(solution)/shard_map/ppermute | solution.py:516
  63.1 7.1 %collective-permute-start.11 = (bf16[1024,256]{1,0:T(8,128)(2,1)S(1)}, bf16[1024,256]{1,0:T(8,128)(2,1)S(1)}, u32[]{:S(2)}, u32[]{:S(2)}) collective-permute-start(bf16[1024,256]{1,0:T(8,128)(2,1)S(1)} %sum_terms.12), channel_id=1, source_target_pairs={{0,4},{1,2},{2,1},{3,7},{4,0},{5,6},{6,5},{7,3},{8,12},{9,10},{10,... | collective-permute-start | bytes 1572872 | tf_op jit(solution)/shard_map/ppermute | solution.py:516
  63.2 1.0 copy-start.18
  64.5 14.4 %collective-permute-start.9 = (bf16[1024,256]{1,0:T(8,128)(2,1)S(1)}, bf16[1024,256]{1,0:T(8,128)(2,1)S(1)}, u32[]{:S(2)}, u32[]{:S(2)}) collective-permute-start(bf16[1024,256]{1,0:T(8,128)(2,1)S(1)} %sum_terms.11), channel_id=1, source_target_pairs={{0,1},{1,0},{2,3},{3,2},{4,5},{5,4},{6,7},{7,6},{8,9},{9,8},{10,11... | collective-permute-start | bytes 1572872 | tf_op jit(solution)/shard_map/ppermute | solution.py:503
  78.9 1.0 copy-start.19
  84.6 11.3 %collective-permute-start.12 = (bf16[1024,256]{1,0:T(8,128)(2,1)S(1)}, bf16[1024,256]{1,0:T(8,128)(2,1)S(1)}, u32[]{:S(2)}, u32[]{:S(2)}) collective-permute-start(bf16[1024,256]{1,0:T(8,128)(2,1)S(1)} %get-tuple-element.38.refs_0_), channel_id=1, source_target_pairs={{0,1},{1,0},{2,3},{3,2},{4,5},{5,4},{6,7},{7,6},{8,9},{9,8},{10,11... | collective-permute-start | bytes 1572872 | tf_op jit(solution)/shard_map/ppermute | solution.py:503
  86.2 9.7 %collective-permute-start.13 = (bf16[1024,256]{1,0:T(8,128)(2,1)S(1)}, bf16[1024,256]{1,0:T(8,128)(2,1)S(1)}, u32[]{:S(2)}, u32[]{:S(2)}) collective-permute-start(bf16[1024,256]{1,0:T(8,128)(2,1)S(1)} %get-tuple-element.38.refs_0_), channel_id=1, source_target_pairs={{0,4},{1,2},{2,1},{3,7},{4,0},{5,6},{6,5},{7,3},{8,12},{9,10},{10,... | collective-permute-start | bytes 1572872 | tf_op jit(solution)/shard_map/ppermute | solution.py:516
  95.9 43.4 %copy-start.3 = (bf16[1024,256]{1,0:T(8,128)(2,1)S(1)}, bf16[1024,256]{1,0:T(8,128)(2,1)}, u32[]{:S(2)}) copy-start(bf16[1024,256]{1,0:T(8,128)(2,1)} %copy-done.2) | copy-start | bytes 1572868
  95.9 43.4 %copy-start.5 = (bf16[1024,256]{1,0:T(8,128)(2,1)S(1)}, bf16[1024,256]{1,0:T(8,128)(2,1)}, u32[]{:S(2)}) copy-start(bf16[1024,256]{1,0:T(8,128)(2,1)} %copy-done.4) | copy-start | bytes 1572868
  95.9 43.4 %copy-start.7 = (bf16[1024,256]{1,0:T(8,128)(2,1)S(1)}, bf16[1024,256]{1,0:T(8,128)(2,1)}, u32[]{:S(2)}) copy-start(bf16[1024,256]{1,0:T(8,128)(2,1)} %copy-done.6) | copy-start | bytes 1572868
  95.9 43.4 %copy-start.9 = (bf16[1024,256]{1,0:T(8,128)(2,1)S(1)}, bf16[1024,256]{1,0:T(8,128)(2,1)}, u32[]{:S(2)}) copy-start(bf16[1024,256]{1,0:T(8,128)(2,1)} %copy-done.8) | copy-start | bytes 1572868
  95.9 43.4 %copy-start.11 = (bf16[1024,256]{1,0:T(8,128)(2,1)S(1)}, bf16[1024,256]{1,0:T(8,128)(2,1)}, u32[]{:S(2)}) copy-start(bf16[1024,256]{1,0:T(8,128)(2,1)} %copy-done.10) | copy-start | bytes 1572868
  95.9 43.4 %copy-start.13 = (bf16[1024,256]{1,0:T(8,128)(2,1)S(1)}, bf16[1024,256]{1,0:T(8,128)(2,1)}, u32[]{:S(2)}) copy-start(bf16[1024,256]{1,0:T(8,128)(2,1)} %copy-done.12) | copy-start | bytes 1572868
  95.9 43.4 %copy-start.21 = (s32[4]{0:T(128)S(1)}, s32[4]{0:T(128)}, u32[]{:S(2)}) copy-start(s32[4]{0:T(128)} %pad_add_fusion.order) | copy-start | bytes 52
  96.0 43.4 %copy-start.22 = (s32[32,1]{0,1:T(1,128)S(1)}, s32[32,1]{0,1:T(1,128)}, u32[]{:S(2)}) copy-start(s32[32,1]{0,1:T(1,128)} %param.13) | copy-start | bytes 388
  96.0 43.4 %copy-start.23 = (s32[128]{0:T(128)S(1)}, s32[128]{0:T(128)}, u32[]{:S(2)}) copy-start(s32[128]{0:T(128)} %fusion.cols) | copy-start | bytes 1540
  97.5 1.9 %collective-permute-start.17 = (f32[448,256]{1,0:T(8,128)S(1)}, f32[448,256]{1,0:T(8,128)S(1)}, u32[]{:S(2)}, u32[]{:S(2)}) collective-permute-start(f32[448,256]{1,0:T(8,128)S(1)} %get-tuple-element.42), channel_id=1, source_target_pairs={{0,4},{4,0},{8,12},{12,8},{16,20},{20,16},{24,28},{28,24},{1,5},{5... | collective-permute-start | bytes 1376264 | tf_op jit(solution)/shard_map/ppermute | solution.py:499
  99.5 7.7 %collective-permute-start.18 = (f32[224,256]{1,0:T(8,128)S(1)}, f32[224,256]{1,0:T(8,128)S(1)}, u32[]{:S(2)}, u32[]{:S(2)}) collective-permute-start(f32[224,256]{1,0:T(8,128)S(1)} %slice.17), channel_id=1, source_target_pairs={{0,8},{4,12},{8,0},{12,4},{16,24},{20,28},{24,16},{28,20},{1,9},{5... | collective-permute-start | bytes 688136 | tf_op jit(solution)/shard_map/ppermute | solution.py:499
  101.2 27.3 %collective-permute-start.15 = (bf16[1024,256]{1,0:T(8,128)(2,1)S(1)}, bf16[1024,256]{1,0:T(8,128)(2,1)S(1)}, u32[]{:S(2)}, u32[]{:S(2)}) collective-permute-start(bf16[1024,256]{1,0:T(8,128)(2,1)S(1)} %collective-permute-done.12.refs_0_.refs_1_), channel_id=1, source_target_pairs={{0,4},{1,2},{2,1},{3,7},{4,0},{5,6},{6,5},{7,3},{8,12},{9,10},{10,... | collective-permute-start | bytes 1572872 | tf_op jit(solution)/shard_map/ppermute | solution.py:516
  107.3 4.9 %collective-permute-start.19 = (f32[112,256]{1,0:T(8,128)S(1)}, f32[112,256]{1,0:T(8,128)S(1)}, u32[]{:S(2)}, u32[]{:S(2)}) collective-permute-start(f32[112,256]{1,0:T(8,128)S(1)} %get-tuple-element.62), channel_id=1, source_target_pairs={{0,16},{4,20},{8,24},{12,28},{16,0},{20,4},{24,8},{28,12},{1,17},{... | collective-permute-start | bytes 344072 | tf_op jit(solution)/shard_map/ppermute | solution.py:499
  112.1 4.5 %collective-permute-start.20 = (bf16[112,256]{1,0:T(8,128)(2,1)S(1)}, bf16[112,256]{1,0:T(8,128)(2,1)S(1)}, u32[]{:S(2)}, u32[]{:S(2)}) collective-permute-start(bf16[112,256]{1,0:T(8,128)(2,1)S(1)} %sum_terms.13.refs_1_), channel_id=1, source_target_pairs={{0,1},{1,0},{2,3},{3,2},{4,5},{5,4},{6,7},{7,6},{8,9},{9,8},{10,11... | collective-permute-start | bytes 172040 | tf_op jit(solution)/shard_map/ppermute | solution.py:503
  116.7 6.1 %collective-permute-start.21 = (bf16[112,256]{1,0:T(8,128)(2,1)S(1)}, bf16[112,256]{1,0:T(8,128)(2,1)S(1)}, u32[]{:S(2)}, u32[]{:S(2)}) collective-permute-start(bf16[112,256]{1,0:T(8,128)(2,1)S(1)} %sum_terms.14.refs_1_), channel_id=1, source_target_pairs={{0,3},{3,0},{1,2},{2,1},{4,7},{7,4},{5,6},{6,5},{8,11},{11,8},{9,1... | collective-permute-start | bytes 172040 | tf_op jit(solution)/shard_map/ppermute | solution.py:507
  122.8 23.3 %copy-start = (bf16[32,1,4,128,128]{4,3,2,1,0:T(8,128)(2,1)S(1)}, bf16[32,1,4,128,128]{4,3,2,1,0:T(8,128)(2,1)}, u32[]{:S(2)}) copy-start(bf16[32,1,4,128,128]{4,3,2,1,0:T(8,128)(2,1)} %param.11) | copy-start | bytes 12582916
  122.8 4.2 %collective-permute-start.22 = (bf16[112,256]{1,0:T(8,128)(2,1)S(1)}, bf16[112,256]{1,0:T(8,128)(2,1)S(1)}, u32[]{:S(2)}, u32[]{:S(2)}) collective-permute-start(bf16[112,256]{1,0:T(8,128)(2,1)S(1)} %sum_terms.15), channel_id=1, source_target_pairs={{0,16},{4,20},{8,24},{12,28},{16,0},{20,4},{24,8},{28,12},{1,17},{... | collective-permute-start | bytes 172040 | tf_op jit(solution)/shard_map/ppermute | solution.py:499
  124.4 14.9 %collective-permute-start.14 = (bf16[1024,256]{1,0:T(8,128)(2,1)S(1)}, bf16[1024,256]{1,0:T(8,128)(2,1)S(1)}, u32[]{:S(2)}, u32[]{:S(2)}) collective-permute-start(bf16[1024,256]{1,0:T(8,128)(2,1)S(1)} %collective-permute-done.13.refs_1_.refs_2_), channel_id=1, source_target_pairs={{0,1},{1,0},{2,3},{3,2},{4,5},{5,4},{6,7},{7,6},{8,9},{9,8},{10,11... | collective-permute-start | bytes 1572872 | tf_op jit(solution)/shard_map/ppermute | solution.py:503
  127.1 4.9 %collective-permute-start.23 = (bf16[224,256]{1,0:T(8,128)(2,1)S(1)}, bf16[224,256]{1,0:T(8,128)(2,1)S(1)}, u32[]{:S(2)}, u32[]{:S(2)}) collective-permute-start(bf16[224,256]{1,0:T(8,128)(2,1)S(1)} %pad_maximum_fusion.2), channel_id=1, source_target_pairs={{0,8},{4,12},{8,0},{12,4},{16,24},{20,28},{24,16},{28,20},{1,9},{5... | collective-permute-start | bytes 344072 | tf_op jit(solution)/shard_map/ppermute | solution.py:499
  128.5 17.6 %collective-permute-start.16 = (bf16[1024,256]{1,0:T(8,128)(2,1)S(1)}, bf16[1024,256]{1,0:T(8,128)(2,1)S(1)}, u32[]{:S(2)}, u32[]{:S(2)}) collective-permute-start(bf16[1024,256]{1,0:T(8,128)(2,1)S(1)} %collective-permute-done.15.refs_11_.refs_4_), channel_id=1, source_target_pairs={{0,1},{1,0},{2,3},{3,2},{4,5},{5,4},{6,7},{7,6},{8,9},{9,8},{10,11... | collective-permute-start | bytes 1572872 | tf_op jit(solution)/shard_map/ppermute | solution.py:503
  132.0 13.1 %collective-permute-start.24 = (bf16[448,256]{1,0:T(8,128)(2,1)S(1)}, bf16[448,256]{1,0:T(8,128)(2,1)S(1)}, u32[]{:S(2)}, u32[]{:S(2)}) collective-permute-start(bf16[448,256]{1,0:T(8,128)(2,1)S(1)} %pad_maximum_fusion.1), channel_id=1, source_target_pairs={{0,4},{4,0},{8,12},{12,8},{16,20},{20,16},{24,28},{28,24},{1,5},{5... | collective-permute-start | bytes 688136 | tf_op jit(solution)/shard_map/ppermute | solution.py:499
  146.1 0.7 copy-start.24
  153.6 4.2 %collective-permute-start.25 = (bf16[4096,256]{1,0:T(8,128)(2,1)S(1)}, bf16[4096,256]{1,0:T(8,128)(2,1)S(1)}, u32[]{:S(2)}, u32[]{:S(2)}) collective-permute-start(bf16[4096,256]{1,0:T(8,128)(2,1)S(1)} %get-tuple-element.45), channel_id=1, source_target_pairs={{0,4},{4,0},{8,12},{12,8},{16,20},{20,16},{24,28},{28,24},{1,5},{5... | collective-permute-start | bytes 6291464 | tf_op jit(solution)/shard_map/ppermute | solution.py:499
  158.0 14.8 %collective-permute-start.26 = (bf16[1024,256]{1,0:T(8,128)(2,1)S(1)}, bf16[1024,256]{1,0:T(8,128)(2,1)S(1)}, u32[]{:S(2)}, u32[]{:S(2)}) collective-permute-start(bf16[1024,256]{1,0:T(8,128)(2,1)S(1)} %sum_terms.16.refs_15_), channel_id=1, source_target_pairs={{0,8},{4,12},{8,0},{12,4},{16,24},{20,28},{24,16},{28,20},{1,9},{5... | collective-permute-start | bytes 1572872 | tf_op jit(solution)/shard_map/ppermute | solution.py:499
  158.3 25.3 %collective-permute-start.27 = (bf16[1024,256]{1,0:T(8,128)(2,1)S(1)}, bf16[1024,256]{1,0:T(8,128)(2,1)S(1)}, u32[]{:S(2)}, u32[]{:S(2)}) collective-permute-start(bf16[1024,256]{1,0:T(8,128)(2,1)S(1)} %sum_terms.17.refs_16_), channel_id=1, source_target_pairs={{0,16},{4,20},{8,24},{12,28},{16,0},{20,4},{24,8},{28,12},{1,17},{... | collective-permute-start | bytes 1572872 | tf_op jit(solution)/shard_map/ppermute | solution.py:499
  158.6 25.0 %collective-permute-start.28 = (bf16[1024,256]{1,0:T(8,128)(2,1)S(1)}, bf16[1024,256]{1,0:T(8,128)(2,1)S(1)}, u32[]{:S(2)}, u32[]{:S(2)}) collective-permute-start(bf16[1024,256]{1,0:T(8,128)(2,1)S(1)} %sum_terms.18.refs_17_), channel_id=1, source_target_pairs={{0,24},{4,28},{8,16},{12,20},{16,8},{20,12},{24,0},{28,4},{1,25},{... | collective-permute-start | bytes 1572872 | tf_op jit(solution)/shard_map/ppermute | solution.py:499

commit v8 on v7

v8 whole, which is shorter than its diff:
```python
import functools

import jax
import jax.numpy as jnp
from jax import lax
from jax.experimental import pallas as pl
from jax.experimental.pallas import tpu as pltpu
from jax.sharding import PartitionSpec as P

F32 = jnp.float32
BF16 = jnp.bfloat16
ANY = pl.BlockSpec(memory_space=pl.ANY)
HBM = pl.BlockSpec(memory_space=pltpu.HBM)
SMEM = pl.BlockSpec(memory_space=pltpu.SMEM)
VMEM = pl.BlockSpec(memory_space=pltpu.VMEM)
MIB = 1 << 20
TN = (((0,), (0,)), ((), ()))
NT = (((1,), (1,)), ((), ()))
SMALL = pl.CostEstimate(flops=1 << 20, bytes_accessed=1 << 16, transcendentals=0)


LIVE_STEP = 4
SWAP_ORDER = (0, 4, 2, 6, 1, 5, 3, 7)


def params(mib):
    return pltpu.CompilerParams(vmem_limit_bytes=mib * MIB)


def mm(a, b, dims=(((1,), (0,)), ((), ()))):
    return lax.dot_general(a, b, dims, preferred_element_type=F32)


def block_at(index, block):
    return pl.ds(pl.multiple_of(index * block, block), block)


class Place:
    def __init__(self, ref, paired=True, blocks=1):
        self.mine, self.level = lax.shift_right_logical(ref[0], 2), ref[0] & 3
        self.paired, self.blocks = paired, blocks

    def source(self, col):
        if not self.paired:
            return col
        shift = self.blocks.bit_length() - 1
        if 1 << shift == self.blocks:
            return col ^ lax.shift_left(self.mine, jnp.int32(shift))
        return (lax.div(col, self.blocks) ^ self.mine) * self.blocks + lax.rem(col, self.blocks)


def load_pieces(pieces, dst, sem, first):
    copies = []
    offset = 0
    for index, piece in enumerate(pieces):
        copy = pltpu.make_async_copy(
            piece, dst.at[pl.ds(offset, piece.shape[0])], sem.at[first + index]
        )
        copy.start()
        copies.append(copy)
        offset += piece.shape[0]
    return copies


def masked_tile(tile, live):
    return jnp.where(live, tile, jnp.zeros_like(tile))


def forward_kernel(outputs, n_pieces, paired, here, cols, counts, *refs):
    pieces, tiles = refs[:n_pieces], refs[n_pieces]
    outs = refs[n_pieces + 1 : n_pieces + 1 + len(outputs)]
    nodes_v, tiles_v, sem, tile_sem = refs[n_pieces + 1 + len(outputs) :]
    rows = outs[0].shape[0] // len(outputs[0])
    slots, block = tiles.shape[1], tiles.shape[2]
    blocks = rows // block
    here = Place(here, paired, blocks)
    copies = load_pieces(pieces, nodes_v, sem, 0)
    places = [(pick, out, index) for out, picks in zip(outs, outputs) for index, pick in enumerate(picks)]
    tile_copies = []
    for place, (pick, _, _) in enumerate(places):
        copy = pltpu.make_async_copy(
            tiles.at[pl.ds(pick * blocks, blocks)],
            tiles_v.at[pl.ds(place * blocks, blocks)],
            tile_sem.at[place],
        )
        copy.start()
        tile_copies.append(copy)
    for copy in copies:
        copy.wait()
    for place, (pick, out, index) in enumerate(places):
        tile_copies[place].wait()
        first = pick * blocks

        def step(i, carry, first=first, out=out, index=index, place=place):
            row = first + i
            count = counts[row]
            parts = []
            for pair in range(slots // 2):
                both = (2 * pair, 2 * pair + 1)
                tile = jnp.concatenate(
                    [masked_tile(tiles_v[place * blocks + i, slot], slot < count) for slot in both], axis=1
                )
                node = jnp.concatenate(
                    [nodes_v[block_at(here.source(cols[slot, row]), block)] for slot in both], axis=0
                )
                parts.append(mm(tile, node))
            value = parts[0]
            for part in parts[1:]:
                value = value + part
            out[block_at(index * blocks + i, block)] = value.astype(BF16)
            return carry

        lax.fori_loop(0, blocks, step, 0, unroll=4)


def forward_call(paired, here, cols, counts, pieces, tiles, outputs, rows):
    width = pieces[0].shape[1]
    gathered = sum(piece.shape[0] for piece in pieces)
    slots, block = tiles.shape[1], tiles.shape[2]
    n_picks = sum(len(picks) for picks in outputs)
    return pl.pallas_call(
        functools.partial(forward_kernel, outputs, len(pieces), paired),
        out_shape=[jax.ShapeDtypeStruct((len(picks) * rows, width), BF16) for picks in outputs],
        in_specs=[SMEM] * 3 + [ANY] * len(pieces) + [HBM],
        out_specs=[VMEM] * len(outputs),
        scratch_shapes=[
            pltpu.VMEM((gathered, width), BF16),
            pltpu.VMEM((n_picks * (rows // block),) + tiles.shape[1:], BF16),
            pltpu.SemaphoreType.DMA((len(pieces),)),
            pltpu.SemaphoreType.DMA((n_picks,)),
        ],
        compiler_params=params(60),
        cost_estimate=SMALL,
        name="partial_messages",
    )(here, cols, counts, *pieces, tiles)


def mlp_kernel(kinds, nodes, cot, *refs):
    n_parts = sum(kinds)
    parts = refs[:n_parts]
    w_in, bias, w_out, gain, shift, updated, gpre_o, act_o, gproj_o, msg_o, vec = refs[
        n_parts : n_parts + 11
    ]
    gmsgs = refs[n_parts + 11 :]
    width = nodes.shape[1]
    messages = []
    place = 0
    for chunk in kinds:
        total = None
        for _ in range(chunk):
            term = parts[place][...].astype(F32)
            place += 1
            total = term if total is None else total + term
        messages.append(total.astype(BF16))
    message = jnp.concatenate(messages, axis=1) if len(messages) > 1 else messages[0]
    node = nodes[...]
    pre = mm(node, w_in[:width]) + mm(message, w_in[width:]) + bias[...]
    sig = jax.nn.sigmoid(pre)
    act = (pre * sig).astype(BF16)
    proj = mm(act, w_out[...])
    mean = jnp.mean(proj, axis=-1, keepdims=True)
    var = jnp.mean((proj - mean) ** 2, axis=-1, keepdims=True)
    rstd = 1.0 / jnp.sqrt(var + 1e-05)
    normed = (proj - mean) * rstd
    updated[...] = (node.astype(F32) + normed * gain[...] + shift[...]).astype(BF16)
    grad_out = cot[...].astype(F32)
    gscaled = grad_out * gain[...]
    gproj = (
        (
            gscaled
            - jnp.mean(gscaled, axis=-1, keepdims=True)
            - normed * jnp.mean(gscaled * normed, axis=-1, keepdims=True)
        )
        * rstd
    ).astype(BF16)
    gact = mm(gproj, w_out[...], NT)
    gpre = gact * sig * (1.0 + pre * (1.0 - sig))
    gpre_b = gpre.astype(BF16)
    gmsg = mm(gpre_b, w_in[width:], NT).astype(BF16)
    part = width // len(gmsgs)
    for index, out in enumerate(gmsgs):
        out[...] = gmsg[:, index * part : (index + 1) * part]
    gpre_o[...] = gpre_b
    act_o[...] = act
    gproj_o[...] = gproj
    msg_o[...] = message

    @pl.when(pl.program_id(0) == 0)
    def _():
        vec[...] = jnp.zeros_like(vec)

    vec[0:1] += jnp.sum(gpre, axis=0, keepdims=True)
    vec[1:2] += jnp.sum(grad_out * normed, axis=0, keepdims=True)
    vec[2:3] += jnp.sum(grad_out, axis=0, keepdims=True)


def mlp_call(nodes, cot, parts, w_in, bias, w_out, gain, shift):
    rows, width = nodes.shape
    step = min(rows, 256)

    def blocked(array):
        return pl.BlockSpec((step, array.shape[1]), lambda i: (i, 0))

    def whole(array):
        return pl.BlockSpec(array.shape, lambda i: (0, 0))

    flat = [term for chunk in parts for term in chunk]
    row_like = jax.ShapeDtypeStruct((rows, width), BF16)
    chunk_like = jax.ShapeDtypeStruct((rows, width // len(parts)), BF16)
    outs = [row_like] * 5 + [jax.ShapeDtypeStruct((8, width), F32)] + [chunk_like] * len(parts)
    weights = (w_in, bias, w_out, gain, shift)
    result = pl.pallas_call(
        functools.partial(mlp_kernel, [len(chunk) for chunk in parts]),
        grid=(rows // step,),
        out_shape=outs,
        in_specs=[blocked(a) for a in (nodes, cot, *flat)] + [whole(a) for a in weights],
        out_specs=[blocked(a) for a in outs[:5]] + [whole(outs[5])] + [blocked(a) for a in outs[6:]],
        compiler_params=params(40),
        cost_estimate=SMALL,
        name="mlp",
    )(nodes, cot, *flat, *weights)
    return result[:6], result[6:]


def weight_kernel(factor, pieces, n_after, here, nodes, msg, act, gpre, gproj, cot, w_in, vec, *refs):
    *outs, direct, grads = refs[n_after:]
    width = nodes.shape[1]

    @pl.when(pl.program_id(0) == 0)
    def _():
        grads[...] = jnp.zeros_like(grads)
        grads[3 * width : 3 * width + 8] = vec[...] * factor

    gpre_b = gpre[...]
    grads[:width] += mm(nodes[...], gpre_b, TN) * factor
    grads[width : 2 * width] += mm(msg[...], gpre_b, TN) * factor
    grads[2 * width : 3 * width] += mm(act[...], gproj[...], TN) * factor
    direct[...] = cot[...].astype(F32) + mm(gpre_b, w_in[:width], NT)

    @pl.when(pl.program_id(0) == pl.num_programs(0) - 1)
    def _():
        if pieces == 1:
            outs[0][...] = grads[: outs[0].shape[0]]
        else:
            rows = grads.shape[0] // pieces
            for place, member in enumerate(SWAP_ORDER):
                where = pl.ds(pl.multiple_of((Place(here).mine ^ member) * rows, 8), rows)
                out, index = outs[2 * place // pieces], place % (pieces // 2)
                out[index * rows : (index + 1) * rows] = grads[where]


def weight_call(factor, pieces, here, nodes, msg, act, gpre, gproj, cot, w_in, vec, after=()):
    rows, width = nodes.shape
    step = min(rows, 256)
    blocked = pl.BlockSpec((step, width), lambda i: (i, 0))

    def whole(shape):
        return pl.BlockSpec(shape, lambda i: (0, 0))

    padded = (3 * width + width // 2, width)
    if pieces == 1:
        outs = [jax.ShapeDtypeStruct((3 * width + 8, width), F32)]
    else:
        outs = [jax.ShapeDtypeStruct((padded[0] // 2, width), F32)] * 2
    return pl.pallas_call(
        functools.partial(weight_kernel, factor, pieces, len(after)),
        grid=(rows // step,),
        out_shape=[*outs, jax.ShapeDtypeStruct((rows, width), F32)],
        in_specs=[SMEM] + [blocked] * 6 + [whole(w_in.shape), whole(vec.shape)] + [ANY] * len(after),
        out_specs=[whole(out.shape) for out in outs] + [blocked],
        scratch_shapes=[pltpu.VMEM(padded, F32)],
        compiler_params=params(40),
        cost_estimate=SMALL,
        name="weight_grads",
    )(here, nodes, msg, act, gpre, gproj, cot, w_in, vec, *after)


def unpack_kernel(here, even, odd, w_in, w_out, vectors, grads):
    width = w_in.shape[1]
    rows = grads.shape[0] // 8
    for member in range(8):
        part = (even, odd)[member % 2]
        first = member // 2 * rows
        where = pl.ds(pl.multiple_of((Place(here).mine ^ member) * rows, 8), rows)
        grads[where] = part[first : first + rows].astype(F32)
    w_in[...] = grads[: 2 * width]
    w_out[...] = grads[2 * width : 3 * width]
    vectors[...] = grads[3 * width : 3 * width + 3]


def unpack_call(here, even, odd, width):
    shapes = ((2 * width, width), (width, width), (3, width))
    return pl.pallas_call(
        unpack_kernel,
        out_shape=[jax.ShapeDtypeStruct(shape, F32) for shape in shapes],
        in_specs=[SMEM, VMEM, VMEM],
        out_specs=[VMEM] * 3,
        scratch_shapes=[pltpu.VMEM((3 * width + width // 2, width), F32)],
        compiler_params=params(16),
        cost_estimate=SMALL,
        name="weight_unpack",
    )(here, even, odd)


def for_live(found, entry):
    def several(i, carry):
        for index in range(LIVE_STEP):
            entry(i * LIVE_STEP + index)
        return carry

    def one(i, carry):
        entry(i)
        return carry

    full = found // LIVE_STEP
    lax.fori_loop(0, full, several, 0)
    lax.fori_loop(full * LIVE_STEP, found, one, 0)


def back_kernel(blocks, slots, n_after, out_pieces, paired, here, cols, counts, grad, tiles, *refs):
    refs = refs[n_after:]
    outs = refs[: len(out_pieces)]
    grad_v, tiles_v, acc, live, source, sem = refs[len(out_pieces) :]
    n_tiles, block = tiles.shape[:2]
    here = Place(here, paired, blocks)
    copies = [
        pltpu.make_async_copy(grad, grad_v, sem.at[0]),
        pltpu.make_async_copy(tiles, tiles_v, sem.at[1]),
    ]
    for copy in copies:
        copy.start()
    acc[...] = jnp.zeros_like(acc)

    def collect(row, found):
        count = counts[row]
        for slot in range(slots):
            live[found] = row * slots + slot
            source[found] = here.source(cols[slot, row])
            found = found + (slot < count).astype(jnp.int32)
        return found

    found = lax.fori_loop(0, n_tiles // slots, collect, jnp.int32(0))
    for copy in copies:
        copy.wait()

    def entry(place):
        tile_index = live[place]
        part = mm(tiles_v[tile_index], grad_v[block_at(tile_index // slots, block)], TN)
        acc[block_at(source[place], block)] += part

    for_live(found, entry)
    piece = acc.shape[0] // sum(len(members) for members in out_pieces)
    for out, members in zip(outs, out_pieces):
        for index, member in enumerate(members):
            out[pl.ds(index * piece, piece)] = acc[pl.ds(member * piece, piece)].astype(BF16)


def back_call(paired, here, cols, counts, grad, tiles, rows, gathered, out_pieces, after=()):
    width = grad.shape[1]
    row_blocks, slots, block = tiles.shape[:3]
    piece = gathered // sum(len(members) for members in out_pieces)
    return pl.pallas_call(
        functools.partial(back_kernel, rows // block, slots, len(after), out_pieces, paired),
        out_shape=[jax.ShapeDtypeStruct((len(m) * piece, width), BF16) for m in out_pieces],
        in_specs=[SMEM] * 3 + [ANY, HBM] + [ANY] * len(after),
        out_specs=[VMEM] * len(out_pieces),
        scratch_shapes=[
            pltpu.VMEM(grad.shape, BF16),
            pltpu.VMEM((row_blocks * slots, block, block), BF16),
            pltpu.VMEM((gathered, width), F32),
            pltpu.SMEM((row_blocks * slots + 8,), jnp.int32),
            pltpu.SMEM((row_blocks * slots + 8,), jnp.int32),
            pltpu.SemaphoreType.DMA((2,)),
        ],
        compiler_params=params(28 if gathered <= 8192 else 56),
        cost_estimate=SMALL,
        name="back_terms",
    )(here, cols, counts, grad, tiles.reshape(row_blocks * slots, block, block), *after)


def tile_grad_kernel(blocks, n_pieces, n_chunks, n_after, paired, here, cols, counts, *refs):
    grads, refs = refs[:n_chunks], refs[n_chunks:]
    pieces = refs[: n_pieces * n_chunks]
    out, grad_v, nodes_v, tiles_v, live, source, sem, piece_sem, out_sem = refs[n_pieces * n_chunks + n_after :]
    block = out.shape[1]
    slots = out.shape[0] // counts.shape[0]
    width = nodes_v.shape[1]
    part = width // n_chunks
    scale = float(width) ** -0.5
    here = Place(here, paired, blocks)
    copies = []
    for chunk in range(n_chunks):
        columns = pl.ds(chunk * part, part)
        copy = pltpu.make_async_copy(grads[chunk], grad_v.at[:, columns], sem.at[chunk])
        copy.start()
        copies.append(copy)
        copies += load_pieces(
            pieces[chunk * n_pieces : (chunk + 1) * n_pieces],
            nodes_v.at[:, columns],
            piece_sem.at[chunk],
            0,
        )
    tiles_v[...] = jnp.zeros_like(tiles_v)

    def collect(row, found):
        count = counts[row]
        for slot in range(slots):
            live[found] = row * slots + slot
            source[found] = here.source(cols[slot, row])
            found = found + (slot < count).astype(jnp.int32)
        return found

    found = lax.fori_loop(0, counts.shape[0], collect, jnp.int32(0))
    for copy in copies:
        copy.wait()

    def entry(place):
        tile_index = live[place]
        grad = grad_v[block_at(tile_index // slots, block)]
        node = nodes_v[block_at(source[place], block)]
        tiles_v[tile_index] = (mm(grad, node, NT) * scale).astype(BF16)

    for_live(found, entry)
    copy = pltpu.make_async_copy(tiles_v, out, out_sem.at[0])
    copy.start()
    copy.wait()


def tile_grad_call(paired, here, cols, counts, grads, pieces, tiles, rows, after=()):
    row_blocks, slots, block = tiles.shape[:3]
    chunks = len(grads)
    width = grads[0].shape[1] * chunks
    gathered = sum(piece.shape[0] for piece in pieces[0])
    flat = [*grads, *(a for chunk in pieces for a in chunk)]
    entries = row_blocks * slots
    return pl.pallas_call(
        functools.partial(tile_grad_kernel, rows // block, len(pieces[0]), chunks, len(after), paired),
        out_shape=jax.ShapeDtypeStruct((entries, block, block), BF16),
        in_specs=[SMEM] * 3 + [ANY] * (len(flat) + len(after)),
        out_specs=ANY,
        scratch_shapes=[
            pltpu.VMEM((grads[0].shape[0], width), BF16),
            pltpu.VMEM((gathered, width), BF16),
            pltpu.VMEM((entries, block, block), BF16),
            pltpu.SMEM((entries + 8,), jnp.int32),
            pltpu.SMEM((entries + 8,), jnp.int32),
            pltpu.SemaphoreType.DMA((chunks,)),
            pltpu.SemaphoreType.DMA((chunks, len(pieces[0]))),
            pltpu.SemaphoreType.DMA((1,)),
        ],
        compiler_params=params(24 if gathered <= 8192 else 48),
        cost_estimate=SMALL,
        name="tile_grads",
    )(here, cols, counts, *flat, *after)


def swap(value, bit):
    return lax.ppermute(value, "row", [(i, i ^ bit) for i in range(8)])


def turn(value, by):
    return lax.ppermute(value, "col", [(i, (i + by) % 4) for i in range(4)])


def gather_square(nodes):
    pieces = []
    for piece in (nodes, swap(nodes, 2), swap(nodes, 4), swap(nodes, 6)):
        pieces += [piece, swap(piece, 1)]
    return pieces


def reduce_square(even, odd, rows):
    other = swap(odd, 1)
    sums = [sum_call(rows, [(even, piece), (other, piece)]) for piece in (1, 2, 3)]
    arrived = [swap(value, bits) for value, bits in zip(sums, (2, 4, 6))]
    return [even, other, *arrived]


def sum_kernel(n_terms, *refs):
    total = refs[0][...].astype(F32)
    for ref in refs[1:n_terms]:
        total = total + ref[...].astype(F32)
    refs[-1][...] = total.astype(refs[-1].dtype)


def sum_call(rows, terms, dtype=BF16, after=()):
    width = terms[0][0].shape[1]
    step = min(rows, 512)
    steps = rows // step
    return pl.pallas_call(
        functools.partial(sum_kernel, len(terms)),
        grid=(steps,),
        out_shape=jax.ShapeDtypeStruct((rows, width), dtype),
        in_specs=[
            pl.BlockSpec((step, width), lambda i, piece=piece: (piece * steps + i, 0)) for _, piece in terms
        ]
        + [ANY] * len(after),
        out_specs=pl.BlockSpec((step, width), lambda i: (i, 0)),
        compiler_params=params(8),
        cost_estimate=SMALL,
        name="sum_terms",
    )(*(array for array, _ in terms), *after)


def join_kernel(n_chunks, direct, *refs):
    *terms, out = refs
    part = out.shape[1] // n_chunks
    each = len(terms) // n_chunks
    for chunk in range(n_chunks):
        columns = slice(chunk * part, (chunk + 1) * part)
        total = direct[:, columns]
        for term in terms[chunk * each : (chunk + 1) * each]:
            total = total + term[...].astype(F32)
        out[:, columns] = total.astype(out.dtype)


def join_call(direct, chunks):
    rows, width = direct.shape
    step = min(rows, 512)
    terms = [term for chunk in chunks for term in chunk]

    def blocked(columns):
        return pl.BlockSpec((step, columns), lambda i: (i, 0))

    return pl.pallas_call(
        functools.partial(join_kernel, len(chunks)),
        grid=(rows // step,),
        out_shape=jax.ShapeDtypeStruct((rows, width), BF16),
        in_specs=[blocked(width)] + [blocked(term.shape[1]) for term in terms],
        out_specs=blocked(width),
        compiler_params=params(16),
        cost_estimate=SMALL,
        name="node_grads",
    )(direct, *terms)


def scatter_weights(kept, received):
    for bit in (2, 4):
        terms = kept + received
        half = terms.shape[0] // 2
        kept, received = terms[:half], swap(terms[half:], bit)
    return kept, received


def level_weights(kept, received):
    rows = kept.shape[0]
    value = sum_call(rows, [(kept, 0), (received, 0)], dtype=BF16)
    return sum_call(rows, [(term, 0) for term in (value, *(turn(value, by) for by in (1, 2, 3)))])


def gather_weights(here, value, width):
    near = [value, swap(value, 2), swap(value, 4), swap(value, 6)]
    joint = jnp.concatenate(near, axis=0)
    other = swap(joint, 1)
    return unpack_call(here, joint, other, width)


def body(n_row, n_col, nodes, tiles, tile_col, tile_count, w_in, bias_in, w_out, ln_gain, ln_shift, cotangent):
    rows, width = nodes.shape
    row_blocks, _, slots, block = tiles.shape[:4]
    tile_local = tiles.reshape(row_blocks, slots, block, block)
    cols = tile_col.reshape(row_blocks, slots).T
    counts = tile_count.reshape(row_blocks)
    gathered, total = n_row * rows, n_col * rows
    paired = n_row == 8 and n_col == 4
    here = lax.axis_index(("row", "col")).astype(jnp.int32).reshape(1)
    known = (paired, here, cols, counts)
    groups = (tuple(range(n_col)),)
    members = ((1, 3, 5, 7), (0, 2, 4, 6)) if paired else (tuple(range(n_row)),)
    chunks = 2 if paired else 1
    part = width // chunks
    pieces, parts = [], []
    for chunk in range(chunks):
        columns = nodes[:, chunk * part : (chunk + 1) * part]
        if paired:
            pieces.append(gather_square(columns))
        else:
            pieces.append([lax.all_gather(columns, "row", axis=0, tiled=True)])
        (partial,) = forward_call(*known, pieces[-1], tile_local, groups, rows)
        parts.append([lax.psum_scatter(partial, "col", scatter_dimension=0, tiled=True)])
    vectors = [v.reshape(1, width) for v in (bias_in, ln_gain, ln_shift)]
    (updated, gpre_b, act, gproj, message, vec), gmsgs = mlp_call(
        nodes, cotangent, parts, w_in, vectors[0], w_out, vectors[1], vectors[2]
    )
    factor = float(rows * n_row * n_col) ** -0.5
    weight_args = (here, nodes, message, act, gpre_b, gproj, cotangent, w_in, vec)
    if paired:
        first = lax.all_gather(gmsgs[0], "col", axis=0, tiled=True)
        second = lax.all_gather(gmsgs[1], "col", axis=0, tiled=True)
        grads = [first, second]
        kept, sent, direct = weight_call(factor, n_row, *weight_args)
        received = swap(sent, 1)
        row_weights = scatter_weights(kept, received)
        weights = gather_weights(here, level_weights(*row_weights), width)
        odd, even = back_call(*known, first, tile_local, rows, gathered, members, (received,))
        left = reduce_square(even, odd, rows)
        odd, even = back_call(*known, second, tile_local, rows, gathered, members, (*left[2:], weights[2]))
        right = reduce_square(even, odd, rows)
        grad_tiles = tile_grad_call(*known, grads, pieces, tile_local, rows, (right[1],))
        grad_nodes = join_call(direct, [left, right])
    else:
        grads = [lax.all_gather(gmsgs[0], "col", axis=0, tiled=True)]
        weight_terms, direct = weight_call(factor, 1, *weight_args)
        weight_sums = lax.psum(weight_terms, ("row", "col"))
        weights = (
            weight_sums[: 2 * width],
            weight_sums[2 * width : 3 * width],
            weight_sums[3 * width : 3 * width + 3],
        )
        (terms,) = back_call(*known, grads[0], tile_local, rows, gathered, members)
        back = lax.psum_scatter(terms, "row", scatter_dimension=0, tiled=True)
        grad_nodes = join_call(direct, [[back]])
        grad_tiles = tile_grad_call(*known, grads, pieces, tile_local, rows)
    grad_tiles = grad_tiles.reshape(tiles.shape)
    return (updated, grad_nodes, grad_tiles, *weights)


def solution(mesh):
    placed = (
        P(("row", "col"), None),
        P("row", "col", None, None, None),
        P("row", "col", None),
        P("row", "col"),
        P(),
        P(),
        P(),
        P(),
        P(),
        P(("row", "col"), None),
    )
    return jax.shard_map(
        functools.partial(body, mesh.shape["row"], mesh.shape["col"]),
        mesh=mesh,
        in_specs=placed,
        out_specs=(
            P(("row", "col"), None),
            P(("row", "col"), None),
            P("row", "col", None, None, None),
            P(),
            P(),
            P(),
        ),
        check_vma=False,
    )
```

time: 186 us -> 213 us (1.15)
  between operations: 1.17 us -> 14.4 us
  local copies, waits for them, and re-layouts: 5.67 us -> 17.2 us
  Pallas kernels: 39.1 us -> 44 us
  starting transfers between devices: 31.7 us -> 27 us
  waiting for transfers between devices: 106 us -> 110 us
    ppermute x12 -> x3, waiting for transfers between devices: 47.5 us -> 6.4 us  [turn(): return lax.ppermute(value, 'col', [(i, (i + by) % 4) for i in range(4)])]
    reduce_scatter x0 -> x2, waiting for transfers between devices: none -> 31.8 us  [body(): lax.psum_scatter(partial, 'col', scatter_dimension=0, tiled=True)]
    all_gather x0 -> x2, waiting for transfers between devices: none -> 20.6 us  [the longest x1 20.6 us: body(): first = lax.all_gather(gmsgs[0], 'col', axis=0, tiled=True)]
    ppermute x12 -> x3, starting transfers between devices: 16.5 us -> 4.52 us  [turn(): return lax.ppermute(value, 'col', [(i, (i + by) % 4) for i in range(4)])]
    unnamed x57 -> x110, local copies, waits for them, and re-layouts: 5.53 us -> 16.1 us
    ppermute x17 -> x29, waiting for transfers between devices: 58.8 us -> 51 us  [swap(): return lax.ppermute(value, 'row', [(i, i ^ bit) for i in range(8)])]
    ppermute x17 -> x29, starting transfers between devices: 15.2 us -> 22.3 us  [swap(): return lax.ppermute(value, 'row', [(i, i ^ bit) for i in range(8)])]
    pallas_call x16 -> x15, Pallas kernels: 36.6 us -> 40.8 us  [the longest x2 13.2 us: forward_call(): pl.pallas_call(functools.partial(forward_kernel, outputs, len(pieces), pa...]
  transfers between devices with their start and end apart: 29 -> 36, of which waited for: 19 -> 23; matrix products, arithmetic and copies ran while one was open for 1% -> 0% of each run, Pallas kernels for 10% -> 12%
where the time goes in v8:
time: 213 us
  waiting for transfers between devices  110 us (52%)
  Pallas kernels  44 us (21%)
  starting transfers between devices  27 us (13%)
  local copies, waits for them, and re-layouts  17.2 us (8%)
  between operations  14.4 us (7%)
    ppermute x29, waiting for transfers between devices, swap(): return lax.ppermute(value, 'row', [(i, i ^ bit) for i in range(8)])  51 us
    reduce_scatter x2, waiting for transfers between devices, body(): lax.psum_scatter(partial, 'col', scatter_dimension=0, tiled=True)  31.8 us
    ppermute x29, starting transfers between devices, swap(): return lax.ppermute(value, 'row', [(i, i ^ bit) for i in range(8)])  22.3 us
    all_gather x1, waiting for transfers between devices, body(): first = lax.all_gather(gmsgs[0], 'col', axis=0, tiled=True)  20.6 us
    unnamed x110, local copies, waits for them, and re-layouts  16.1 us
    pallas_call x2, Pallas kernels, forward_call(): pl.pallas_call(functools.partial(forward_kernel, outputs, len(pieces), pa...  13.2 us
    pallas_call x2, Pallas kernels, back_call(): pl.pallas_call(functools.partial(back_kernel, rows // block, slots, len(a...  11.6 us
    pallas_call x1, Pallas kernels, tile_grad_call(): pl.pallas_call(functools.partial(tile_grad_kernel, rows // block, len(pie...  9.02 us
  transfers between devices with their start and end apart: 36, of which 23 were waited for; matrix products, arithmetic and copies ran while one was open for 0% of the time, Pallas kernels for 12%

profile of v8, /device:TPU:0, one launch (start us, length us, event | category | flops | bytes accessed | tf_op | source)
XLA Modules:
  0.0 212.7 jit_solution(686418306941770226)
XLA Ops:
  7.2 1.1 fusion
  8.3 3.0 %collective-permute-start.1 = (bf16[1024,128]{1,0:T(8,128)(2,1)S(1)}, bf16[1024,128]{1,0:T(8,128)(2,1)S(1)}, u32[]{:S(2)}, u32[]{:S(2)}) collective-permute-start(bf16[1024,128]{1,0:T(8,128)(2,1)S(1)} %get-tuple-element.49.refs_0_.refs_2_), channel_id=1, source_target_pairs={{0,8},{4,12},{8,0},{12,4},{16,24},{20,28},{24,16},{28,20},{1,9},{5... | collective-permute-start | bytes 786440 | tf_op jit(solution)/shard_map/ppermute | solution.py:458
  11.3 1.5 collective-permute-start.3
  12.9 5.6 %collective-permute-done.1.refs_2_.refs_4_ = bf16[1024,128]{1,0:T(8,128)(2,1)S(1)} collective-permute-done((bf16[1024,128]{1,0:T(8,128)(2,1)S(1)}, bf16[1024,128]{1,0:T(8,128)(2,1)S(1)}, u32[]{:S(2)}, u32[]{:S(2)}) %collective-permute-start.1) | collective-permute-done | bytes 262176 | tf_op jit(solution)/shard_map/ppermute | solution.py:458
  18.4 6.2 %collective-permute-done.3.refs_4_.refs_6_ = bf16[1024,128]{1,0:T(8,128)(2,1)S(1)} collective-permute-done((bf16[1024,128]{1,0:T(8,128)(2,1)S(1)}, bf16[1024,128]{1,0:T(8,128)(2,1)S(1)}, u32[]{:S(2)}, u32[]{:S(2)}) %collective-permute-start.3) | collective-permute-done | bytes 262176 | tf_op jit(solution)/shard_map/ppermute | solution.py:458
  25.2 1.0 collective-permute-done.4.refs_5_.refs_7_
  27.3 6.6 %partial_messages.2 = bf16[4096,128]{1,0:T(8,128)(2,1)} custom-call(s32[1]{0:T(128)} %bitcast.here, s32[4,32]{1,0:T(4,128)} %bitcast.17, s32[32]{0:T(128)} %bitcast.22, bf16[1024,128]{1,0:T(8,128)(2,1)} %copy-done.8, bf16[1024,128]{1,0:T(8,128)(2,1)} %copy-done.20, bf16[1024,128]{1,0:T(8,128)(2,1)} %copy-done.14, bf16[1024,128]{1,0:T(8,128)(2,1)} %copy-done.22, ...), custom_call_target="tpu_custom_call" | custom-call | flops 1048576 | bytes 65536 | tf_op jit(solution)/shard_map/partial_messages/pallas_call | solution.py:121
  34.0 0.9 collective-permute-start.8
  35.0 1.2 collective-permute-start.10
  36.1 1.4 collective-permute-start.12
  37.6 5.7 %collective-permute-done.8.refs_2_.refs_12_ = bf16[1024,128]{1,0:T(8,128)(2,1)S(1)} collective-permute-done((bf16[1024,128]{1,0:T(8,128)(2,1)S(1)}, bf16[1024,128]{1,0:T(8,128)(2,1)S(1)}, u32[]{:S(2)}, u32[]{:S(2)}) %collective-permute-start.8) | collective-permute-done | bytes 262176 | tf_op jit(solution)/shard_map/ppermute | solution.py:458
  43.3 4.1 %collective-permute-done.10.refs_4_.refs_14_ = bf16[1024,128]{1,0:T(8,128)(2,1)S(1)} collective-permute-done((bf16[1024,128]{1,0:T(8,128)(2,1)S(1)}, bf16[1024,128]{1,0:T(8,128)(2,1)S(1)}, u32[]{:S(2)}, u32[]{:S(2)}) %collective-permute-start.10) | collective-permute-done | bytes 262176 | tf_op jit(solution)/shard_map/ppermute | solution.py:458
  47.4 1.6 collective-permute-done.12.refs_6_.refs_16_
  49.1 1.5 collective-permute-done.13.refs_7_.refs_17_
  50.6 0.7 copy-done.40
  51.3 6.6 %partial_messages.3 = bf16[4096,128]{1,0:T(8,128)(2,1)} custom-call(s32[1]{0:T(128)} %bitcast.here, s32[4,32]{1,0:T(4,128)} %bitcast.18, s32[32]{0:T(128)} %bitcast.23, bf16[1024,128]{1,0:T(8,128)(2,1)} %copy-done.6, bf16[1024,128]{1,0:T(8,128)(2,1)} %copy-done.34, bf16[1024,128]{1,0:T(8,128)(2,1)} %copy-done.28, bf16[1024,128]{1,0:T(8,128)(2,1)} %copy-done.36, ...), custom_call_target="tpu_custom_call" | custom-call | flops 1048576 | bytes 65536 | tf_op jit(solution)/shard_map/partial_messages/pallas_call | solution.py:121
  58.0 3.6 %reduce-scatter.3.cloned.1.call-done.refs_0_ = bf16[1024,128]{1,0:T(8,128)(2,1)} async-done(((bf16[4096,128]{1,0:T(8,128)(2,1)}), bf16[1024,128]{1,0:T(8,128)(2,1)}) %reduce-scatter.3.cloned.1.call-update) | async-done | bytes 262160 | tf_op jit(solution)/shard_map/reduce_scatter | solution.py:580
  61.6 28.2 %reduce-scatter.5.cloned.1.call-done.refs_1_ = bf16[1024,128]{1,0:T(8,128)(2,1)} async-done(((bf16[4096,128]{1,0:T(8,128)(2,1)}), bf16[1024,128]{1,0:T(8,128)(2,1)}) %reduce-scatter.5.cloned.1.call-update) | async-done | bytes 262160 | tf_op jit(solution)/shard_map/reduce_scatter | solution.py:580
  89.8 0.9 copy-done.44
  90.8 0.9 copy-done.45
  91.7 0.7 copy-done.52
  92.4 0.7 copy-done.53
  93.1 0.7 copy-done.54
  93.7 4.7 %mlp.1 = (bf16[1024,256]{1,0:T(8,128)(2,1)}, bf16[1024,256]{1,0:T(8,128)(2,1)S(1)}, bf16[1024,256]{1,0:T(8,128)(2,1)S(1)}, bf16[1024,256]{1,0:T(8,128)(2,1)S(1)}...) custom-call(bf16[1024,256]{1,0:T(8,128)(2,1)S(1)} %copy-done.2, ...), custom_call_target="tpu_custom_call" | custom-call | flops 1048576 | bytes 65536 | tf_op jit(solution)/shard_map/mlp/pallas_call | solution.py:212
  98.4 0.7 copy-done.46
  99.1 0.7 copy-done.47
  99.9 2.3 %weight_grads.1 = (f32[448,256]{1,0:T(8,128)S(1)}, f32[448,256]{1,0:T(8,128)}, f32[1024,256]{1,0:T(8,128)S(1)}) custom-call(s32[1]{0:T(128)} %bitcast.here, bf16[1024,256]{1,0:T(8,128)(2,1)S(1)} %copy-done.2, bf16[1024,256]{1,0:T(8,128)(2,1)S(1)} %get-tuple-element.25.msg, bf16[1024,256]{1,0:T(8,128)(2,1)S(1)} %get-tuple-element.26.act, ...), custom_call_target="tpu_custom_call" | custom-call | flops 1048576 | bytes 65536 | tf_op jit(solution)/shard_map/weight_grads/pallas_call | solution.py:265
  102.2 1.0 copy-done.11
  103.1 0.8 copy-done.42
  103.9 2.0 collective-permute-done.14.refs_0_
  105.9 20.6 %all-gather.3.cloned.1.call-done.grad.refs_0_ = bf16[4096,128]{1,0:T(8,128)(2,1)} async-done(((bf16[1024,128]{1,0:T(8,128)(2,1)}), bf16[4096,128]{1,0:T(8,128)(2,1)}) %all-gather.3.cloned.1.call-update) | async-done | bytes 1048592 | tf_op jit(solution)/shard_map/all_gather | solution.py:588
  126.6 2.2 %copy-done = bf16[32,1,4,128,128]{4,3,2,1,0:T(8,128)(2,1)S(1)} copy-done((bf16[32,1,4,128,128]{4,3,2,1,0:T(8,128)(2,1)S(1)}, bf16[32,1,4,128,128]{4,3,2,1,0:T(8,128)(2,1)}, u32[]{:S(2)}) %copy-start) | copy-done | bytes 4194328
  128.8 1.2 copy-done.3
  130.0 5.8 %back_terms.2 = (bf16[4096,128]{1,0:T(8,128)(2,1)S(1)}, bf16[4096,128]{1,0:T(8,128)(2,1)S(1)}) custom-call(s32[1]{0:T(128)} %bitcast.here, s32[4,32]{1,0:T(4,128)S(1)} %bitcast.19, s32[32]{0:T(128)S(1)} %bitcast.24, bf16[4096,128]{1,0:T(8,128)(2,1)S(1)} %copy-done.3, bf16[128,128,128]{2,1,0:T(8,128)(2,1)S(1)} %bitcast.15, ...), custom_call_target="tpu_custom_call" | custom-call | flops 1048576 | bytes 65536 | tf_op jit(solution)/shard_map/back_terms/pallas_call | solution.py:362
  136.0 1.2 collective-permute-start.19
  137.2 6.9 %collective-permute-done.19 = f32[224,256]{1,0:T(8,128)S(1)} collective-permute-done((f32[224,256]{1,0:T(8,128)S(1)}, f32[224,256]{1,0:T(8,128)S(1)}, u32[]{:S(2)}, u32[]{:S(2)}) %collective-permute-start.19) | collective-permute-done | bytes 229408 | tf_op jit(solution)/shard_map/ppermute | solution.py:458
  144.1 1.3 collective-permute-start.20
  145.4 3.6 %collective-permute-done.20.refs_1_ = f32[112,256]{1,0:T(8,128)S(1)} collective-permute-done((f32[112,256]{1,0:T(8,128)S(1)}, f32[112,256]{1,0:T(8,128)S(1)}, u32[]{:S(2)}, u32[]{:S(2)}) %collective-permute-start.20) | collective-permute-done | bytes 114720 | tf_op jit(solution)/shard_map/ppermute | solution.py:458
  149.0 1.1 collective-permute-start.21
  150.1 1.2 collective-permute-start.22
  151.3 2.3 %collective-permute-start.23 = (bf16[112,256]{1,0:T(8,128)(2,1)S(1)}, bf16[112,256]{1,0:T(8,128)(2,1)S(1)}, u32[]{:S(2)}, u32[]{:S(2)}) collective-permute-start(bf16[112,256]{1,0:T(8,128)(2,1)S(1)} %sum_terms.11.refs_0_), channel_id=1, source_target_pairs={{0,3},{1,0},{2,1},{3,2},{4,7},{5,4},{6,5},{7,6},{8,11},{9,8},{10,9... | collective-permute-start | bytes 172040 | tf_op jit(solution)/shard_map/ppermute | solution.py:462
  153.6 3.3 %collective-permute-done.21.refs_1_ = bf16[112,256]{1,0:T(8,128)(2,1)S(1)} collective-permute-done((bf16[112,256]{1,0:T(8,128)(2,1)S(1)}, bf16[112,256]{1,0:T(8,128)(2,1)S(1)}, u32[]{:S(2)}, u32[]{:S(2)}) %collective-permute-start.21) | collective-permute-done | bytes 57376 | tf_op jit(solution)/shard_map/ppermute | solution.py:462
  156.9 3.1 %collective-permute-done.22.refs_2_ = bf16[112,256]{1,0:T(8,128)(2,1)S(1)} collective-permute-done((bf16[112,256]{1,0:T(8,128)(2,1)S(1)}, bf16[112,256]{1,0:T(8,128)(2,1)S(1)}, u32[]{:S(2)}, u32[]{:S(2)}) %collective-permute-start.22) | collective-permute-done | bytes 57376 | tf_op jit(solution)/shard_map/ppermute | solution.py:462
  160.0 2.6 %collective-permute-start.26 = (bf16[112,256]{1,0:T(8,128)(2,1)S(1)}, bf16[112,256]{1,0:T(8,128)(2,1)S(1)}, u32[]{:S(2)}, u32[]{:S(2)}) collective-permute-start(bf16[112,256]{1,0:T(8,128)(2,1)S(1)} %sum_terms.12), channel_id=1, source_target_pairs={{0,24},{4,28},{8,16},{12,20},{16,8},{20,12},{24,0},{28,4},{1,25},{... | collective-permute-start | bytes 172040 | tf_op jit(solution)/shard_map/ppermute | solution.py:458
  163.0 0.5 collective-permute-start.24
  163.7 1.5 collective-permute-start.16
  165.3 1.7 collective-permute-start.17
  167.0 0.7 sum_terms.10
  167.7 0.6 collective-permute-start.18
  168.4 1.5 collective-permute-done.27.odd
  169.9 1.0 weight_unpack.1
  170.8 2.7 %collective-permute-done.16.refs_0_.refs_2_ = bf16[1024,128]{1,0:T(8,128)(2,1)S(1)} collective-permute-done((bf16[1024,128]{1,0:T(8,128)(2,1)S(1)}, bf16[1024,128]{1,0:T(8,128)(2,1)S(1)}, u32[]{:S(2)}, u32[]{:S(2)}) %collective-permute-start.16) | collective-permute-done | bytes 262176 | tf_op jit(solution)/shard_map/ppermute | solution.py:458
  173.5 3.0 %collective-permute-done.17.refs_1_.refs_3_ = bf16[1024,128]{1,0:T(8,128)(2,1)S(1)} collective-permute-done((bf16[1024,128]{1,0:T(8,128)(2,1)S(1)}, bf16[1024,128]{1,0:T(8,128)(2,1)S(1)}, u32[]{:S(2)}, u32[]{:S(2)}) %collective-permute-start.17) | collective-permute-done | bytes 262176 | tf_op jit(solution)/shard_map/ppermute | solution.py:458
  176.5 1.2 collective-permute-done.18.refs_2_.refs_4_
  177.7 2.2 %copy-done.1 = bf16[32,1,4,128,128]{4,3,2,1,0:T(8,128)(2,1)S(1)} copy-done((bf16[32,1,4,128,128]{4,3,2,1,0:T(8,128)(2,1)S(1)}, bf16[32,1,4,128,128]{4,3,2,1,0:T(8,128)(2,1)}, u32[]{:S(2)}) %copy-start.1) | copy-done | bytes 4194328
  179.9 1.2 copy-done.5
  181.1 0.7 copy-done.51
  181.8 5.8 %back_terms.3 = (bf16[4096,128]{1,0:T(8,128)(2,1)S(1)}, bf16[4096,128]{1,0:T(8,128)(2,1)S(1)}) custom-call(s32[1]{0:T(128)} %bitcast.here, s32[4,32]{1,0:T(4,128)S(1)} %bitcast.20, s32[32]{0:T(128)S(1)} %bitcast.25, bf16[4096,128]{1,0:T(8,128)(2,1)S(1)} %copy-done.5, bf16[128,128,128]{2,1,0:T(8,128)(2,1)S(1)} %bitcast.16, ...), custom_call_target="tpu_custom_call" | custom-call | flops 1048576 | bytes 65536 | tf_op jit(solution)/shard_map/back_terms/pallas_call | solution.py:362
  187.9 2.6 %collective-permute-done.28.refs_1_.refs_6_.refs_18_ = bf16[4096,128]{1,0:T(8,128)(2,1)S(1)} collective-permute-done((bf16[4096,128]{1,0:T(8,128)(2,1)S(1)}, bf16[4096,128]{1,0:T(8,128)(2,1)S(1)}, u32[]{:S(2)}, u32[]{:S(2)}) %collective-permute-start.28) | collective-permute-done | bytes 1048608 | tf_op jit(solution)/shard_map/ppermute | solution.py:458
  191.2 1.6 collective-permute-start.30
  192.9 1.6 collective-permute-start.31
  194.6 9.0 %tile_grads.1 = bf16[128,128,128]{2,1,0:T(8,128)(2,1)} custom-call(s32[1]{0:T(128)} %bitcast.here, s32[4,32]{1,0:T(4,128)S(1)} %bitcast.21, s32[32]{0:T(128)S(1)} %bitcast.26, bf16[4096,128]{1,0:T(8,128)(2,1)S(1)} %copy-done.4, bf16[4096,128]{1,0:T(8,128)(2,1)S(1)} %copy-done.5, bf16[1024,128]{1,0:T(8,128)(2,1)S(1)} %copy-done.9, ...), custom_call_target="tpu_custom_call" | custom-call | flops 1048576 | bytes 65536 | tf_op jit(solution)/shard_map/tile_grads/pallas_call | solution.py:436
  204.1 1.0 collective-permute-done.31.refs_9_
  205.1 1.1 node_grads.1
  (145 shorter events, 4.2 us)
Async XLA Ops:
  7.2 54.4 %reduce-scatter.3.cloned.1.call-start = ((), (), s32[]{:S(2)}) async-start(), calls=%async_computation.2 | async-start | bytes 1310720 | tf_op jit(solution)/shard_map/reduce_scatter | solution.py:580
  8.3 18.3 %copy-start.8 = (bf16[1024,128]{1,0:T(8,128)(2,1)}, bf16[1024,128]{1,0:T(8,128)(2,1)S(1)}, u32[]{:S(2)}) copy-start(bf16[1024,128]{1,0:T(8,128)(2,1)S(1)} %get-tuple-element.49.refs_0_.refs_2_) | copy-start | bytes 786436
  8.3 29.3 %copy-start.6 = (bf16[1024,128]{1,0:T(8,128)(2,1)}, bf16[1024,128]{1,0:T(8,128)(2,1)S(1)}, u32[]{:S(2)}) copy-start(bf16[1024,128]{1,0:T(8,128)(2,1)S(1)} %get-tuple-element.48.refs_0_.refs_10_) | copy-start | bytes 786436
  8.3 10.1 %collective-permute-start.1 = (bf16[1024,128]{1,0:T(8,128)(2,1)S(1)}, bf16[1024,128]{1,0:T(8,128)(2,1)S(1)}, u32[]{:S(2)}, u32[]{:S(2)}) collective-permute-start(bf16[1024,128]{1,0:T(8,128)(2,1)S(1)} %get-tuple-element.49.refs_0_.refs_2_), channel_id=1, source_target_pairs={{0,8},{4,12},{8,0},{12,4},{16,24},{20,28},{24,16},{28,20},{1,9},{5... | collective-permute-start | bytes 786440 | tf_op jit(solution)/shard_map/ppermute | solution.py:458
  11.3 13.4 %collective-permute-start.3 = (bf16[1024,128]{1,0:T(8,128)(2,1)S(1)}, bf16[1024,128]{1,0:T(8,128)(2,1)S(1)}, u32[]{:S(2)}, u32[]{:S(2)}) collective-permute-start(bf16[1024,128]{1,0:T(8,128)(2,1)S(1)} %get-tuple-element.49.refs_0_.refs_2_), channel_id=1, source_target_pairs={{0,16},{4,20},{8,24},{12,28},{16,0},{20,4},{24,8},{28,12},{1,17},{... | collective-permute-start | bytes 786440 | tf_op jit(solution)/shard_map/ppermute | solution.py:458
  12.8 11.9 %collective-permute-start.5 = (bf16[1024,128]{1,0:T(8,128)(2,1)S(1)}, bf16[1024,128]{1,0:T(8,128)(2,1)S(1)}, u32[]{:S(2)}, u32[]{:S(2)}) collective-permute-start(bf16[1024,128]{1,0:T(8,128)(2,1)S(1)} %get-tuple-element.49.refs_0_.refs_2_), channel_id=1, source_target_pairs={{0,24},{4,28},{8,16},{12,20},{16,8},{20,12},{24,0},{28,4},{1,25},{... | collective-permute-start | bytes 786440 | tf_op jit(solution)/shard_map/ppermute | solution.py:458
  12.8 12.4 %collective-permute-start = (bf16[1024,128]{1,0:T(8,128)(2,1)S(1)}, bf16[1024,128]{1,0:T(8,128)(2,1)S(1)}, u32[]{:S(2)}, u32[]{:S(2)}) collective-permute-start(bf16[1024,128]{1,0:T(8,128)(2,1)S(1)} %get-tuple-element.49.refs_0_.refs_2_), channel_id=1, source_target_pairs={{0,4},{4,0},{8,12},{12,8},{16,20},{20,16},{24,28},{28,24},{1,5},{5... | collective-permute-start | bytes 786440 | tf_op jit(solution)/shard_map/ppermute | solution.py:458
  18.4 8.2 %copy-start.14 = (bf16[1024,128]{1,0:T(8,128)(2,1)}, bf16[1024,128]{1,0:T(8,128)(2,1)S(1)}, u32[]{:S(2)}) copy-start(bf16[1024,128]{1,0:T(8,128)(2,1)S(1)} %collective-permute-done.1.refs_2_.refs_4_) | copy-start | bytes 786436
  18.4 6.8 %collective-permute-start.2 = (bf16[1024,128]{1,0:T(8,128)(2,1)S(1)}, bf16[1024,128]{1,0:T(8,128)(2,1)S(1)}, u32[]{:S(2)}, u32[]{:S(2)}) collective-permute-start(bf16[1024,128]{1,0:T(8,128)(2,1)S(1)} %collective-permute-done.1.refs_2_.refs_4_), channel_id=1, source_target_pairs={{0,4},{4,0},{8,12},{12,8},{16,20},{20,16},{24,28},{28,24},{1,5},{5... | collective-permute-start | bytes 786440 | tf_op jit(solution)/shard_map/ppermute | solution.py:458
  24.7 1.5 collective-permute-start.4
  24.7 1.9 collective-permute-start.6
  33.9 55.9 %reduce-scatter.5.cloned.1.call-start = ((), (), s32[]{:S(2)}) async-start(), calls=%async_computation.3 | async-start | bytes 1310720 | tf_op jit(solution)/shard_map/reduce_scatter | solution.py:580
  34.0 55.8 %copy-start.2 = (bf16[1024,256]{1,0:T(8,128)(2,1)S(1)}, bf16[1024,256]{1,0:T(8,128)(2,1)}, u32[]{:S(2)}) copy-start(bf16[1024,256]{1,0:T(8,128)(2,1)} %nodes.3) | copy-start | bytes 1572868
  34.0 55.8 %copy-start.10 = (bf16[1024,256]{1,0:T(8,128)(2,1)S(1)}, bf16[1024,256]{1,0:T(8,128)(2,1)}, u32[]{:S(2)}) copy-start(bf16[1024,256]{1,0:T(8,128)(2,1)} %cot.3) | copy-start | bytes 1572868
  34.0 55.8 %copy-start.13 = (bf16[512,256]{1,0:T(8,128)(2,1)S(1)}, bf16[512,256]{1,0:T(8,128)(2,1)}, u32[]{:S(2)}) copy-start(bf16[512,256]{1,0:T(8,128)(2,1)} %w_in.1) | copy-start | bytes 786436
  34.0 55.8 %copy-start.48 = (bf16[256,256]{1,0:T(8,128)(2,1)S(1)}, bf16[256,256]{1,0:T(8,128)(2,1)}, u32[]{:S(2)}) copy-start(bf16[256,256]{1,0:T(8,128)(2,1)} %refs_4_.1) | copy-start | bytes 393220
  34.0 9.2 %collective-permute-start.8 = (bf16[1024,128]{1,0:T(8,128)(2,1)S(1)}, bf16[1024,128]{1,0:T(8,128)(2,1)S(1)}, u32[]{:S(2)}, u32[]{:S(2)}) collective-permute-start(bf16[1024,128]{1,0:T(8,128)(2,1)S(1)} %get-tuple-element.48.refs_0_.refs_10_), channel_id=1, source_target_pairs={{0,8},{4,12},{8,0},{12,4},{16,24},{20,28},{24,16},{28,20},{1,9},{5... | collective-permute-start | bytes 786440 | tf_op jit(solution)/shard_map/ppermute | solution.py:458
  35.0 12.4 %collective-permute-start.10 = (bf16[1024,128]{1,0:T(8,128)(2,1)S(1)}, bf16[1024,128]{1,0:T(8,128)(2,1)S(1)}, u32[]{:S(2)}, u32[]{:S(2)}) collective-permute-start(bf16[1024,128]{1,0:T(8,128)(2,1)S(1)} %get-tuple-element.48.refs_0_.refs_10_), channel_id=1, source_target_pairs={{0,16},{4,20},{8,24},{12,28},{16,0},{20,4},{24,8},{28,12},{1,17},{... | collective-permute-start | bytes 786440 | tf_op jit(solution)/shard_map/ppermute | solution.py:458
  36.1 12.9 %collective-permute-start.12 = (bf16[1024,128]{1,0:T(8,128)(2,1)S(1)}, bf16[1024,128]{1,0:T(8,128)(2,1)S(1)}, u32[]{:S(2)}, u32[]{:S(2)}) collective-permute-start(bf16[1024,128]{1,0:T(8,128)(2,1)S(1)} %get-tuple-element.48.refs_0_.refs_10_), channel_id=1, source_target_pairs={{0,24},{4,28},{8,16},{12,20},{16,8},{20,12},{24,0},{28,4},{1,25},{... | collective-permute-start | bytes 786440 | tf_op jit(solution)/shard_map/ppermute | solution.py:458
  37.6 11.4 %collective-permute-start.7 = (bf16[1024,128]{1,0:T(8,128)(2,1)S(1)}, bf16[1024,128]{1,0:T(8,128)(2,1)S(1)}, u32[]{:S(2)}, u32[]{:S(2)}) collective-permute-start(bf16[1024,128]{1,0:T(8,128)(2,1)S(1)} %get-tuple-element.48.refs_0_.refs_10_), channel_id=1, source_target_pairs={{0,4},{4,0},{8,12},{12,8},{16,20},{20,16},{24,28},{28,24},{1,5},{5... | collective-permute-start | bytes 786440 | tf_op jit(solution)/shard_map/ppermute | solution.py:458
  43.2 7.3 %copy-start.28 = (bf16[1024,128]{1,0:T(8,128)(2,1)}, bf16[1024,128]{1,0:T(8,128)(2,1)S(1)}, u32[]{:S(2)}) copy-start(bf16[1024,128]{1,0:T(8,128)(2,1)S(1)} %collective-permute-done.8.refs_2_.refs_12_) | copy-start | bytes 786436
  43.2 5.8 %collective-permute-start.9 = (bf16[1024,128]{1,0:T(8,128)(2,1)S(1)}, bf16[1024,128]{1,0:T(8,128)(2,1)S(1)}, u32[]{:S(2)}, u32[]{:S(2)}) collective-permute-start(bf16[1024,128]{1,0:T(8,128)(2,1)S(1)} %collective-permute-done.8.refs_2_.refs_12_), channel_id=1, source_target_pairs={{0,4},{4,0},{8,12},{12,8},{16,20},{20,16},{24,28},{28,24},{1,5},{5... | collective-permute-start | bytes 786440 | tf_op jit(solution)/shard_map/ppermute | solution.py:458
  47.4 1.7 collective-permute-start.11
  49.0 1.5 collective-permute-start.13
  57.9 68.7 %copy-start.49 = (s32[32,1,4]{0,2,1:T(4,128)S(1)}, s32[32,1,4]{0,2,1:T(4,128)}, u32[]{:S(2)}) copy-start(s32[32,1,4]{0,2,1:T(4,128)} %param.12) | copy-start | bytes 1540
  57.9 68.7 %copy-start.50 = (s32[32,1]{0,1:T(1,128)S(1)}, s32[32,1]{0,1:T(1,128)}, u32[]{:S(2)}) copy-start(s32[32,1]{0,1:T(1,128)} %param.13) | copy-start | bytes 388
  57.9 68.6 %all-gather.3.cloned.1.call-start = ((), (), s32[]{:S(2)}) async-start(), calls=%async_computation.4 | async-start | bytes 1310720 | tf_op jit(solution)/shard_map/all_gather | solution.py:588
  99.8 71.0 %all-gather.5.cloned.1.call-start = ((), (), s32[]{:S(2)}) async-start(), calls=%async_computation.5 | async-start | bytes 1310720 | tf_op jit(solution)/shard_map/all_gather | solution.py:589
  103.9 2.0 collective-permute-start.14
  135.8 27.8 %collective-permute-start.15 = (bf16[4096,128]{1,0:T(8,128)(2,1)S(1)}, bf16[4096,128]{1,0:T(8,128)(2,1)S(1)}, u32[]{:S(2)}, u32[]{:S(2)}) collective-permute-start(bf16[4096,128]{1,0:T(8,128)(2,1)S(1)} %get-tuple-element.34), channel_id=1, source_target_pairs={{0,4},{4,0},{8,12},{12,8},{16,20},{20,16},{24,28},{28,24},{1,5},{5... | collective-permute-start | bytes 3145736 | tf_op jit(solution)/shard_map/ppermute | solution.py:458
  136.0 8.1 %collective-permute-start.19 = (f32[224,256]{1,0:T(8,128)S(1)}, f32[224,256]{1,0:T(8,128)S(1)}, u32[]{:S(2)}, u32[]{:S(2)}) collective-permute-start(f32[224,256]{1,0:T(8,128)S(1)} %slice.25), channel_id=1, source_target_pairs={{0,8},{4,12},{8,0},{12,4},{16,24},{20,28},{24,16},{28,20},{1,9},{5... | collective-permute-start | bytes 688136 | tf_op jit(solution)/shard_map/ppermute | solution.py:458
  144.1 4.9 %collective-permute-start.20 = (f32[112,256]{1,0:T(8,128)S(1)}, f32[112,256]{1,0:T(8,128)S(1)}, u32[]{:S(2)}, u32[]{:S(2)}) collective-permute-start(f32[112,256]{1,0:T(8,128)S(1)} %get-tuple-element.50), channel_id=1, source_target_pairs={{0,16},{4,20},{8,24},{12,28},{16,0},{20,4},{24,8},{28,12},{1,17},{... | collective-permute-start | bytes 344072 | tf_op jit(solution)/shard_map/ppermute | solution.py:458
  149.0 7.8 %collective-permute-start.21 = (bf16[112,256]{1,0:T(8,128)(2,1)S(1)}, bf16[112,256]{1,0:T(8,128)(2,1)S(1)}, u32[]{:S(2)}, u32[]{:S(2)}) collective-permute-start(bf16[112,256]{1,0:T(8,128)(2,1)S(1)} %sum_terms.11.refs_0_), channel_id=1, source_target_pairs={{0,1},{1,2},{2,3},{3,0},{4,5},{5,6},{6,7},{7,4},{8,9},{9,10},{10,1... | collective-permute-start | bytes 172040 | tf_op jit(solution)/shard_map/ppermute | solution.py:462
  150.1 9.8 %collective-permute-start.22 = (bf16[112,256]{1,0:T(8,128)(2,1)S(1)}, bf16[112,256]{1,0:T(8,128)(2,1)S(1)}, u32[]{:S(2)}, u32[]{:S(2)}) collective-permute-start(bf16[112,256]{1,0:T(8,128)(2,1)S(1)} %sum_terms.11.refs_0_), channel_id=1, source_target_pairs={{0,2},{1,3},{2,0},{3,1},{4,6},{5,7},{6,4},{7,5},{8,10},{9,11},{10,... | collective-permute-start | bytes 172040 | tf_op jit(solution)/shard_map/ppermute | solution.py:462
  151.3 8.7 %collective-permute-start.23 = (bf16[112,256]{1,0:T(8,128)(2,1)S(1)}, bf16[112,256]{1,0:T(8,128)(2,1)S(1)}, u32[]{:S(2)}, u32[]{:S(2)}) collective-permute-start(bf16[112,256]{1,0:T(8,128)(2,1)S(1)} %sum_terms.11.refs_0_), channel_id=1, source_target_pairs={{0,3},{1,0},{2,1},{3,2},{4,7},{5,4},{6,5},{7,6},{8,11},{9,8},{10,9... | collective-permute-start | bytes 172040 | tf_op jit(solution)/shard_map/ppermute | solution.py:462
  160.0 7.7 %collective-permute-start.26 = (bf16[112,256]{1,0:T(8,128)(2,1)S(1)}, bf16[112,256]{1,0:T(8,128)(2,1)S(1)}, u32[]{:S(2)}, u32[]{:S(2)}) collective-permute-start(bf16[112,256]{1,0:T(8,128)(2,1)S(1)} %sum_terms.12), channel_id=1, source_target_pairs={{0,24},{4,28},{8,16},{12,20},{16,8},{20,12},{24,0},{28,4},{1,25},{... | collective-permute-start | bytes 172040 | tf_op jit(solution)/shard_map/ppermute | solution.py:458
  162.6 5.7 %collective-permute-start.25 = (bf16[112,256]{1,0:T(8,128)(2,1)S(1)}, bf16[112,256]{1,0:T(8,128)(2,1)S(1)}, u32[]{:S(2)}, u32[]{:S(2)}) collective-permute-start(bf16[112,256]{1,0:T(8,128)(2,1)S(1)} %sum_terms.12), channel_id=1, source_target_pairs={{0,16},{4,20},{8,24},{12,28},{16,0},{20,4},{24,8},{28,12},{1,17},{... | collective-permute-start | bytes 172040 | tf_op jit(solution)/shard_map/ppermute | solution.py:458
  163.0 5.3 %collective-permute-start.24 = (bf16[112,256]{1,0:T(8,128)(2,1)S(1)}, bf16[112,256]{1,0:T(8,128)(2,1)S(1)}, u32[]{:S(2)}, u32[]{:S(2)}) collective-permute-start(bf16[112,256]{1,0:T(8,128)(2,1)S(1)} %sum_terms.12), channel_id=1, source_target_pairs={{0,8},{4,12},{8,0},{12,4},{16,24},{20,28},{24,16},{28,20},{1,9},{5... | collective-permute-start | bytes 172040 | tf_op jit(solution)/shard_map/ppermute | solution.py:458
  163.7 9.8 %collective-permute-start.16 = (bf16[1024,128]{1,0:T(8,128)(2,1)S(1)}, bf16[1024,128]{1,0:T(8,128)(2,1)S(1)}, u32[]{:S(2)}, u32[]{:S(2)}) collective-permute-start(bf16[1024,128]{1,0:T(8,128)(2,1)S(1)} %sum_terms.8), channel_id=1, source_target_pairs={{0,8},{4,12},{8,0},{12,4},{16,24},{20,28},{24,16},{28,20},{1,9},{5... | collective-permute-start | bytes 786440 | tf_op jit(solution)/shard_map/ppermute | solution.py:458
  165.3 11.2 %collective-permute-start.17 = (bf16[1024,128]{1,0:T(8,128)(2,1)S(1)}, bf16[1024,128]{1,0:T(8,128)(2,1)S(1)}, u32[]{:S(2)}, u32[]{:S(2)}) collective-permute-start(bf16[1024,128]{1,0:T(8,128)(2,1)S(1)} %sum_terms.9), channel_id=1, source_target_pairs={{0,16},{4,20},{8,24},{12,28},{16,0},{20,4},{24,8},{28,12},{1,17},{... | collective-permute-start | bytes 786440 | tf_op jit(solution)/shard_map/ppermute | solution.py:458
  167.7 10.0 %collective-permute-start.18 = (bf16[1024,128]{1,0:T(8,128)(2,1)}, bf16[1024,128]{1,0:T(8,128)(2,1)S(1)}, u32[]{:S(2)}, u32[]{:S(2)}) collective-permute-start(bf16[1024,128]{1,0:T(8,128)(2,1)} %sum_terms.10), channel_id=1, source_target_pairs={{0,24},{4,28},{8,16},{12,20},{16,8},{20,12},{24,0},{28,4},{1,25},{... | collective-permute-start | bytes 786440 | tf_op jit(solution)/shard_map/ppermute | solution.py:458
  168.3 1.6 collective-permute-start.27
  187.6 6.9 %copy-start.4 = (bf16[4096,128]{1,0:T(8,128)(2,1)S(1)}, bf16[4096,128]{1,0:T(8,128)(2,1)}, u32[]{:S(2)}) copy-start(bf16[4096,128]{1,0:T(8,128)(2,1)} %all-gather.3.cloned.1.call-done.grad.refs_0_) | copy-start | bytes 3145732
  187.6 6.9 %copy-start.7 = (bf16[1024,128]{1,0:T(8,128)(2,1)S(1)}, bf16[1024,128]{1,0:T(8,128)(2,1)}, u32[]{:S(2)}) copy-start(bf16[1024,128]{1,0:T(8,128)(2,1)} %copy-done.6) | copy-start | bytes 786436
  187.6 6.9 %copy-start.9 = (bf16[1024,128]{1,0:T(8,128)(2,1)S(1)}, bf16[1024,128]{1,0:T(8,128)(2,1)}, u32[]{:S(2)}) copy-start(bf16[1024,128]{1,0:T(8,128)(2,1)} %copy-done.8) | copy-start | bytes 786436
  187.7 6.9 %copy-start.15 = (bf16[1024,128]{1,0:T(8,128)(2,1)S(1)}, bf16[1024,128]{1,0:T(8,128)(2,1)}, u32[]{:S(2)}) copy-start(bf16[1024,128]{1,0:T(8,128)(2,1)} %copy-done.14) | copy-start | bytes 786436
  187.7 6.9 %copy-start.17 = (bf16[1024,128]{1,0:T(8,128)(2,1)S(1)}, bf16[1024,128]{1,0:T(8,128)(2,1)}, u32[]{:S(2)}) copy-start(bf16[1024,128]{1,0:T(8,128)(2,1)} %copy-done.16) | copy-start | bytes 786436
  187.7 6.9 %copy-start.19 = (bf16[1024,128]{1,0:T(8,128)(2,1)S(1)}, bf16[1024,128]{1,0:T(8,128)(2,1)}, u32[]{:S(2)}) copy-start(bf16[1024,128]{1,0:T(8,128)(2,1)} %copy-done.18) | copy-start | bytes 786436
  187.7 6.9 %copy-start.21 = (bf16[1024,128]{1,0:T(8,128)(2,1)S(1)}, bf16[1024,128]{1,0:T(8,128)(2,1)}, u32[]{:S(2)}) copy-start(bf16[1024,128]{1,0:T(8,128)(2,1)} %copy-done.20) | copy-start | bytes 786436
  187.7 6.9 %copy-start.23 = (bf16[1024,128]{1,0:T(8,128)(2,1)S(1)}, bf16[1024,128]{1,0:T(8,128)(2,1)}, u32[]{:S(2)}) copy-start(bf16[1024,128]{1,0:T(8,128)(2,1)} %copy-done.22) | copy-start | bytes 786436
  187.7 6.9 %copy-start.25 = (bf16[1024,128]{1,0:T(8,128)(2,1)S(1)}, bf16[1024,128]{1,0:T(8,128)(2,1)}, u32[]{:S(2)}) copy-start(bf16[1024,128]{1,0:T(8,128)(2,1)} %copy-done.24) | copy-start | bytes 786436
  187.7 6.9 %copy-start.27 = (bf16[1024,128]{1,0:T(8,128)(2,1)S(1)}, bf16[1024,128]{1,0:T(8,128)(2,1)}, u32[]{:S(2)}) copy-start(bf16[1024,128]{1,0:T(8,128)(2,1)} %copy-done.26) | copy-start | bytes 786436
  187.7 6.9 %copy-start.29 = (bf16[1024,128]{1,0:T(8,128)(2,1)S(1)}, bf16[1024,128]{1,0:T(8,128)(2,1)}, u32[]{:S(2)}) copy-start(bf16[1024,128]{1,0:T(8,128)(2,1)} %copy-done.28) | copy-start | bytes 786436
  187.7 6.9 %copy-start.31 = (bf16[1024,128]{1,0:T(8,128)(2,1)S(1)}, bf16[1024,128]{1,0:T(8,128)(2,1)}, u32[]{:S(2)}) copy-start(bf16[1024,128]{1,0:T(8,128)(2,1)} %copy-done.30) | copy-start | bytes 786436
  187.7 6.9 %copy-start.33 = (bf16[1024,128]{1,0:T(8,128)(2,1)S(1)}, bf16[1024,128]{1,0:T(8,128)(2,1)}, u32[]{:S(2)}) copy-start(bf16[1024,128]{1,0:T(8,128)(2,1)} %copy-done.32) | copy-start | bytes 786436
  187.8 6.9 %copy-start.35 = (bf16[1024,128]{1,0:T(8,128)(2,1)S(1)}, bf16[1024,128]{1,0:T(8,128)(2,1)}, u32[]{:S(2)}) copy-start(bf16[1024,128]{1,0:T(8,128)(2,1)} %copy-done.34) | copy-start | bytes 786436
  187.8 6.9 %copy-start.37 = (bf16[1024,128]{1,0:T(8,128)(2,1)S(1)}, bf16[1024,128]{1,0:T(8,128)(2,1)}, u32[]{:S(2)}) copy-start(bf16[1024,128]{1,0:T(8,128)(2,1)} %copy-done.36) | copy-start | bytes 786436
  187.8 6.9 %copy-start.39 = (bf16[1024,128]{1,0:T(8,128)(2,1)S(1)}, bf16[1024,128]{1,0:T(8,128)(2,1)}, u32[]{:S(2)}) copy-start(bf16[1024,128]{1,0:T(8,128)(2,1)} %copy-done.38) | copy-start | bytes 786436
  187.8 6.9 %copy-start.41 = (bf16[1024,128]{1,0:T(8,128)(2,1)S(1)}, bf16[1024,128]{1,0:T(8,128)(2,1)}, u32[]{:S(2)}) copy-start(bf16[1024,128]{1,0:T(8,128)(2,1)} %copy-done.40) | copy-start | bytes 786436
  187.8 2.7 %collective-permute-start.28 = (bf16[4096,128]{1,0:T(8,128)(2,1)S(1)}, bf16[4096,128]{1,0:T(8,128)(2,1)S(1)}, u32[]{:S(2)}, u32[]{:S(2)}) collective-permute-start(bf16[4096,128]{1,0:T(8,128)(2,1)S(1)} %get-tuple-element.39), channel_id=1, source_target_pairs={{0,4},{4,0},{8,12},{12,8},{16,20},{20,16},{24,28},{28,24},{1,5},{5... | collective-permute-start | bytes 3145736 | tf_op jit(solution)/shard_map/ppermute | solution.py:458
  190.6 13.1 %collective-permute-start.29 = (bf16[1024,128]{1,0:T(8,128)(2,1)S(1)}, bf16[1024,128]{1,0:T(8,128)(2,1)S(1)}, u32[]{:S(2)}, u32[]{:S(2)}) collective-permute-start(bf16[1024,128]{1,0:T(8,128)(2,1)S(1)} %sum_terms.13), channel_id=1, source_target_pairs={{0,8},{4,12},{8,0},{12,4},{16,24},{20,28},{24,16},{28,20},{1,9},{5... | collective-permute-start | bytes 786440 | tf_op jit(solution)/shard_map/ppermute | solution.py:458
  191.2 12.8 %collective-permute-start.30 = (bf16[1024,128]{1,0:T(8,128)(2,1)S(1)}, bf16[1024,128]{1,0:T(8,128)(2,1)S(1)}, u32[]{:S(2)}, u32[]{:S(2)}) collective-permute-start(bf16[1024,128]{1,0:T(8,128)(2,1)S(1)} %sum_terms.14), channel_id=1, source_target_pairs={{0,16},{4,20},{8,24},{12,28},{16,0},{20,4},{24,8},{28,12},{1,17},{... | collective-permute-start | bytes 786440 | tf_op jit(solution)/shard_map/ppermute | solution.py:458
  192.9 12.2 %copy-start.12 = (f32[1024,256]{1,0:T(8,128)S(1)}, f32[1024,256]{1,0:T(8,128)}, u32[]{:S(2)}) copy-start(f32[1024,256]{1,0:T(8,128)} %copy-done.11) | copy-start | bytes 3145732
  192.9 12.2 %collective-permute-start.31 = (bf16[1024,128]{1,0:T(8,128)(2,1)S(1)}, bf16[1024,128]{1,0:T(8,128)(2,1)S(1)}, u32[]{:S(2)}, u32[]{:S(2)}) collective-permute-start(bf16[1024,128]{1,0:T(8,128)(2,1)S(1)} %sum_terms.15), channel_id=1, source_target_pairs={{0,24},{4,28},{8,16},{12,20},{16,8},{20,12},{24,0},{28,4},{1,25},{... | collective-permute-start | bytes 786440 | tf_op jit(solution)/shard_map/ppermute | solution.py:458
  (27 other events, 38.6 us)
Sparse Core Ops, SparseCore 0:
  34.1 27.4 reduce-scatter.2
  64.0 25.7 reduce-scatter.4
  99.9 26.5 all-gather.2
  128.6 32.2 all-gather.4

commit v9 on v7

--- a/solution.py
+++ b/solution.py
@@ -36,6 +36,30 @@
     return pl.ds(pl.multiple_of(index * block, block), block)
 
 
+class Place:
+    def __init__(self, ref, paired=True, blocks=1):
+        self.mine, self.level = lax.shift_right_logical(ref[0], 2), ref[0] & 3
+        self.paired, self.blocks = paired, blocks
+
+    def inner(self):
+        return (self.level == 1) | (self.level == 2)
+
+    def group(self, pick):
+        if not self.paired:
+            return pick
+        low = self.level < 2
+        choices = (jnp.where(low, 3, 0), jnp.where(low, 2, 1), self.level ^ 1, self.level)
+        return choices[pick]
+
+    def source(self, col):
+        if not self.paired:
+            return col
+        shift = self.blocks.bit_length() - 1
+        if 1 << shift == self.blocks:
+            return col ^ lax.shift_left(self.mine, jnp.int32(shift))
+        return (lax.div(col, self.blocks) ^ self.mine) * self.blocks + lax.rem(col, self.blocks)
+
+
 def load_pieces(pieces, dst, sem, first):
     copies = []
     offset = 0
@@ -53,19 +77,20 @@
     return jnp.where(live, tile, jnp.zeros_like(tile))
 
 
-def forward_kernel(outputs, n_pieces, cols, counts, order, *refs):
+def forward_kernel(outputs, n_pieces, paired, here, cols, counts, *refs):
     pieces, tiles = refs[:n_pieces], refs[n_pieces]
     outs = refs[n_pieces + 1 : n_pieces + 1 + len(outputs)]
     nodes_v, tiles_v, sem, tile_sem = refs[n_pieces + 1 + len(outputs) :]
     rows = outs[0].shape[0] // len(outputs[0])
     slots, block = tiles.shape[1], tiles.shape[2]
     blocks = rows // block
+    here = Place(here, paired, blocks)
     copies = load_pieces(pieces, nodes_v, sem, 0)
     places = [(pick, out, index) for out, picks in zip(outs, outputs) for index, pick in enumerate(picks)]
     tile_copies = []
     for place, (pick, _, _) in enumerate(places):
         copy = pltpu.make_async_copy(
-            tiles.at[pl.ds(order[pick] * blocks, blocks)],
+            tiles.at[pl.ds(here.group(pick) * blocks, blocks)],
             tiles_v.at[pl.ds(place * blocks, blocks)],
             tile_sem.at[place],
         )
@@ -75,7 +100,7 @@
         copy.wait()
     for place, (pick, out, index) in enumerate(places):
         tile_copies[place].wait()
-        first = order[pick] * blocks
+        first = here.group(pick) * blocks
 
         def step(i, carry, first=first, out=out, index=index, place=place):
             row = first + i
@@ -87,7 +112,7 @@
                     [masked_tile(tiles_v[place * blocks + i, slot], slot < count) for slot in both], axis=1
                 )
                 node = jnp.concatenate(
-                    [nodes_v[block_at(cols[row * slots + slot], block)] for slot in both], axis=0
+                    [nodes_v[block_at(here.source(cols[slot, row]), block)] for slot in both], axis=0
                 )
                 parts.append(mm(tile, node))
             value = parts[0]
@@ -99,13 +124,13 @@
         lax.fori_loop(0, blocks, step, 0, unroll=4)
 
 
-def forward_call(cols, counts, order, pieces, tiles, outputs, rows):
+def forward_call(paired, here, cols, counts, pieces, tiles, outputs, rows):
     width = pieces[0].shape[1]
     gathered = sum(piece.shape[0] for piece in pieces)
     slots, block = tiles.shape[1], tiles.shape[2]
     n_picks = sum(len(picks) for picks in outputs)
     return pl.pallas_call(
-        functools.partial(forward_kernel, outputs, len(pieces)),
+        functools.partial(forward_kernel, outputs, len(pieces), paired),
         out_shape=[jax.ShapeDtypeStruct((len(picks) * rows, width), BF16) for picks in outputs],
         in_specs=[SMEM] * 3 + [ANY] * len(pieces) + [HBM],
         out_specs=[VMEM] * len(outputs),
@@ -118,10 +143,10 @@
         compiler_params=params(60),
         cost_estimate=SMALL,
         name="partial_messages",
-    )(cols, counts, order, *pieces, tiles)
-
-
-def mlp_kernel(kinds, middle, nodes, cot, *refs):
+    )(here, cols, counts, *pieces, tiles)
+
+
+def mlp_kernel(kinds, here, nodes, cot, *refs):
     n_parts = sum(len(chunk) for chunk in kinds)
     parts = refs[:n_parts]
     w_in, bias, w_out, gain, shift, updated, gpre_o, act_o, gproj_o, msg_o, vec = refs[
@@ -129,7 +154,7 @@
     ]
     gmsgs = refs[n_parts + 11 :]
     width = nodes.shape[1]
-    inner = middle[0] > 0
+    inner = Place(here).inner()
     messages = []
     place = 0
     for chunk in kinds:
@@ -183,7 +208,7 @@
     vec[2:3] += jnp.sum(grad_out, axis=0, keepdims=True)
 
 
-def mlp_call(middle, nodes, cot, parts, kinds, w_in, bias, w_out, gain, shift):
+def mlp_call(here, nodes, cot, parts, kinds, w_in, bias, w_out, gain, shift):
     rows, width = nodes.shape
     step = min(rows, 256)
 
@@ -207,11 +232,11 @@
         compiler_params=params(40),
         cost_estimate=SMALL,
         name="mlp",
-    )(middle, nodes, cot, *flat, *weights)
+    )(here, nodes, cot, *flat, *weights)
     return result[:6], result[6:]
 
 
-def weight_kernel(factor, pieces, n_after, mine, nodes, msg, act, gpre, gproj, cot, w_in, vec, *refs):
+def weight_kernel(factor, pieces, n_after, here, nodes, msg, act, gpre, gproj, cot, w_in, vec, *refs):
     *outs, direct, grads = refs[n_after:]
     width = nodes.shape[1]
 
@@ -233,12 +258,12 @@
         else:
             rows = grads.shape[0] // pieces
             for place, member in enumerate(SWAP_ORDER):
-                where = pl.ds(pl.multiple_of((mine[0] ^ member) * rows, 8), rows)
+                where = pl.ds(pl.multiple_of((Place(here).mine ^ member) * rows, 8), rows)
                 out, index = outs[2 * place // pieces], place % (pieces // 2)
                 out[index * rows : (index + 1) * rows] = grads[where]
 
 
-def weight_call(factor, pieces, mine, nodes, msg, act, gpre, gproj, cot, w_in, vec, after=()):
+def weight_call(factor, pieces, here, nodes, msg, act, gpre, gproj, cot, w_in, vec, after=()):
     rows, width = nodes.shape
     step = min(rows, 256)
     blocked = pl.BlockSpec((step, width), lambda i: (i, 0))
@@ -261,42 +286,45 @@
         compiler_params=params(40),
         cost_estimate=SMALL,
         name="weight_grads",
-    )(mine, nodes, msg, act, gpre, gproj, cot, w_in, vec, *after)
-
-
-def unpack_kernel(mine, parts, w_in, w_out, vectors, grads):
+    )(here, nodes, msg, act, gpre, gproj, cot, w_in, vec, *after)
+
+
+def unpack_kernel(here, even, odd, w_in, w_out, vectors, grads):
     width = w_in.shape[1]
-    rows = grads.shape[0] // len(SWAP_ORDER)
-    for place, member in enumerate(SWAP_ORDER):
-        where = pl.ds(pl.multiple_of((mine[0] ^ member) * rows, 8), rows)
-        grads[where] = parts[place * rows : (place + 1) * rows].astype(F32)
+    rows = grads.shape[0] // 8
+    for member in range(8):
+        part = (even, odd)[member % 2]
+        first = member // 2 * rows
+        where = pl.ds(pl.multiple_of((Place(here).mine ^ member) * rows, 8), rows)
+        grads[where] = part[first : first + rows].astype(F32)
     w_in[...] = grads[: 2 * width]
     w_out[...] = grads[2 * width : 3 * width]
     vectors[...] = grads[3 * width : 3 * width + 3]
 
 
-def unpack_call(mine, parts, width):
+def unpack_call(here, even, odd, width):
     shapes = ((2 * width, width), (width, width), (3, width))
     return pl.pallas_call(
         unpack_kernel,
         out_shape=[jax.ShapeDtypeStruct(shape, F32) for shape in shapes],
-        in_specs=[SMEM, VMEM],
+        in_specs=[SMEM, VMEM, VMEM],
         out_specs=[VMEM] * 3,
         scratch_shapes=[pltpu.VMEM((3 * width + width // 2, width), F32)],
         compiler_params=params(16),
         cost_estimate=SMALL,
         name="weight_unpack",
-    )(mine, parts)
-
-
-def grad_jobs(rows, refs, dst, sem, order, middle, groups=None):
+    )(here, even, odd)
+
+
+def grad_jobs(rows, refs, dst, sem, here, groups=None):
     if len(refs) == 1:
         return [(None, pltpu.make_async_copy(refs[0], dst, sem.at[0]))]
-    conditions = {None: None, "inner": middle[0] > 0, "outer": middle[0] == 0}
+    inner = here.inner()
+    conditions = {None: None, "inner": inner, "outer": jnp.logical_not(inner)}
     jobs = []
     for group, index, kind in GRAD_PLAN:
         if groups is None:
-            where = block_at(order[group], rows)
+            where = block_at(here.group(group), rows)
         elif group in groups:
             where = pl.ds(groups.index(group) * rows, rows)
         else:
@@ -329,13 +357,14 @@
     lax.fori_loop(full * LIVE_STEP, found, one, 0)
 
 
-def back_kernel(rows, slots, n_grads, n_after, out_pieces, cols, counts, order, middle, *refs):
+def back_kernel(rows, slots, n_grads, n_after, out_pieces, paired, here, cols, counts, *refs):
     grads, tiles = refs[:n_grads], refs[n_grads]
     refs = refs[n_grads + 1 + n_after :]
     outs = refs[: len(out_pieces)]
-    grad_v, tiles_v, acc, live, sem, tile_sem = refs[len(out_pieces) :]
+    grad_v, tiles_v, acc, live, source, sem, tile_sem = refs[len(out_pieces) :]
     n_tiles, block = tiles.shape[:2]
-    jobs = grad_jobs(rows, grads, grad_v, sem, order, middle)
+    here = Place(here, paired, rows // block)
+    jobs = grad_jobs(rows, grads, grad_v, sem, here)
     run_jobs(jobs, "start")
     tile_copy = pltpu.make_async_copy(tiles, tiles_v, tile_sem.at[0])
     tile_copy.start()
@@ -345,6 +374,7 @@
         count = counts[row]
         for slot in range(slots):
             live[found] = row * slots + slot
+            source[found] = here.source(cols[slot, row])
             found = found + (slot < count).astype(jnp.int32)
         return found
 
@@ -355,7 +385,7 @@
     def entry(place):
         tile_index = live[place]
         part = mm(tiles_v[tile_index], grad_v[block_at(tile_index // slots, block)], TN)
-        acc[block_at(cols[tile_index], block)] += part
+        acc[block_at(source[place], block)] += part
 
     for_live(found, entry)
     piece = acc.shape[0] // sum(len(members) for members in out_pieces)
@@ -364,20 +394,21 @@
             out[pl.ds(index * piece, piece)] = acc[pl.ds(member * piece, piece)].astype(BF16)
 
 
-def back_call(cols, counts, order, middle, grads, tiles, total, gathered, out_pieces, after=()):
+def back_call(paired, here, cols, counts, grads, tiles, total, gathered, out_pieces, after=()):
     rows, width = grads[0].shape
     rows = total if len(grads) == 1 else rows
     row_blocks, slots, block = tiles.shape[:3]
     piece = gathered // sum(len(members) for members in out_pieces)
     return pl.pallas_call(
-        functools.partial(back_kernel, rows, slots, len(grads), len(after), out_pieces),
+        functools.partial(back_kernel, rows, slots, len(grads), len(after), out_pieces, paired),
         out_shape=[jax.ShapeDtypeStruct((len(m) * piece, width), BF16) for m in out_pieces],
-        in_specs=[SMEM] * 4 + [ANY] * len(grads) + [HBM] + [ANY] * len(after),
+        in_specs=[SMEM] * 3 + [ANY] * len(grads) + [HBM] + [ANY] * len(after),
         out_specs=[VMEM] * len(out_pieces),
         scratch_shapes=[
             pltpu.VMEM((total, width), BF16),
             pltpu.VMEM((row_blocks * slots, block, block), BF16),
             pltpu.VMEM((gathered, width), F32),
+            pltpu.SMEM((row_blocks * slots + 8,), jnp.int32),
             pltpu.SMEM((row_blocks * slots + 8,), jnp.int32),
             pltpu.SemaphoreType.DMA((len(grads),)),
             pltpu.SemaphoreType.DMA((1,)),
@@ -385,11 +416,11 @@
         compiler_params=params(28 if gathered <= 8192 else 56),
         cost_estimate=SMALL,
         name="back_terms",
-    )(cols, counts, order, middle, *grads, tiles.reshape(row_blocks * slots, block, block), *after)
+    )(here, cols, counts, *grads, tiles.reshape(row_blocks * slots, block, block), *after)
 
 
 def tile_grad_kernel(
-    rows, slots, n_grads, n_pieces, n_chunks, n_after, groups, cols, counts, order, middle, *refs
+    rows, slots, n_grads, n_pieces, n_chunks, n_after, groups, paired, here, cols, counts, *refs
 ):
     grads = refs[: n_grads * n_chunks]
     refs = refs[n_grads * n_chunks :]
@@ -401,6 +432,7 @@
     part = width // n_chunks
     scale = float(width) ** -0.5
     blocks = grad_v.shape[0] // (block * len(groups))
+    here = Place(here, paired, blocks)
     jobs, copies = [], []
     for chunk in range(n_chunks):
         columns = pl.ds(chunk * part, part)
@@ -409,8 +441,7 @@
             grads[chunk * n_grads : (chunk + 1) * n_grads],
             grad_v.at[:, columns],
             sem.at[chunk],
-            order,
-            middle,
+            here,
             groups,
         )
         copies += load_pieces(
@@ -423,14 +454,14 @@
     tiles_v[...] = jnp.zeros_like(tiles_v)
     found = jnp.int32(0)
     for index, group in enumerate(groups):
-        first = order[group] * blocks
+        first = here.group(group) * blocks
 
         def collect(i, found, first=first, index=index):
             row = first + i
             count = counts[row]
             for slot in range(slots):
                 live[found] = (index * blocks + i) * slots + slot
-                source[found] = cols[row * slots + slot]
+                source[found] = here.source(cols[slot, row])
                 found = found + (slot < count).astype(jnp.int32)
             return found
 
@@ -451,7 +482,7 @@
     for index, group in enumerate(groups):
         copy = pltpu.make_async_copy(
             tiles_v.at[pl.ds(index * size, size)],
-            out.at[pl.ds(order[group] * size, size)],
+            out.at[pl.ds(here.group(group) * size, size)],
             out_sem.at[index],
         )
         copy.start()
@@ -460,7 +491,7 @@
         copy.wait()
 
 
-def tile_grad_call(cols, counts, order, middle, grads, pieces, shape, rows, groups, base=None, after=()):
+def tile_grad_call(paired, here, cols, counts, grads, pieces, shape, rows, groups, base=None, after=()):
     row_blocks, slots, block = shape[:3]
     chunks = len(grads)
     width = grads[0][0].shape[1] * chunks
@@ -470,15 +501,15 @@
     entries = len(groups) * rows // block * slots
     return pl.pallas_call(
         functools.partial(
-            tile_grad_kernel, rows, slots, len(grads[0]), len(pieces[0]), chunks, len(after), groups
+            tile_grad_kernel, rows, slots, len(grads[0]), len(pieces[0]), chunks, len(after), groups, paired
         ),
         out_shape=[
             jax.ShapeDtypeStruct((row_blocks * slots, block, block), BF16),
             jax.ShapeDtypeStruct((8, 128), F32),
         ],
-        in_specs=[SMEM] * 4 + [ANY] * (len(flat) + len(after)),
+        in_specs=[SMEM] * 3 + [ANY] * (len(flat) + len(after)),
         out_specs=[ANY, VMEM],
-        input_output_aliases={} if base is None else {4 + len(flat): 0},
+        input_output_aliases={} if base is None else {3 + len(flat): 0},
         scratch_shapes=[
             pltpu.VMEM((len(groups) * rows, width), BF16),
             pltpu.VMEM((gathered, width), BF16),
@@ -492,7 +523,7 @@
         compiler_params=params(16 if gathered <= 8192 else 40),
         cost_estimate=SMALL,
         name="tile_grads",
-    )(cols, counts, order, middle, *flat, *after)
+    )(here, cols, counts, *flat, *after)
 
 
 def swap(value, bit):
@@ -503,8 +534,8 @@
     return lax.ppermute(value, "col", [(0, 1), (1, 0), (2, 3), (3, 2)])
 
 
-def mirror_swap(value):
-    return lax.ppermute(value, "col", [(0, 3), (3, 0), (1, 2), (2, 1)])
+def turn(value, by):
+    return lax.ppermute(value, "col", [(i, (i + by) % 4) for i in range(4)])
 
 
 def inner_swap(value):
@@ -517,40 +548,59 @@
 
 
 def gather_square(nodes):
-    pieces = []
-    for piece in (nodes, swap(nodes, 2), swap(nodes, 4), swap(nodes, 6)):
-        pieces += [piece, swap(piece, 1)]
+    half = nodes.shape[0] // 2
+    lower, upper = nodes[:half], nodes[half:]
+    y_lower, x_upper = swap(lower, 4), swap(upper, 2)
+    x_lower, y_upper = swap(lower, 2), swap(upper, 4)
+    d_lower, d_upper = swap(y_lower, 2), swap(x_upper, 4)
+    pieces = [nodes, swap(nodes, 1)]
+    for pair in ((x_lower, x_upper), (y_lower, y_upper), (d_lower, d_upper)):
+        pieces += [*pair, *(swap(piece, 1) for piece in pair)]
     return pieces
 
 
-def sum_kernel(n_terms, n_gated, *refs):
-    flag, refs = refs[0], refs[1:]
+def reduce_square(here, even, other, rows, after):
+    sums = [sum_call(here, rows, [(even, piece), (other, piece)], after=after) for piece in (1, 2, 3)]
+    return [swap(value, bits) for value, bits in zip(sums, (2, 4, 6))], sums
+
+
+def sum_kernel(n_terms, n_gated, n_split, *refs):
+    inner, refs = Place(refs[0]).inner(), refs[1:]
     total = None
     for index, ref in enumerate(refs[: n_terms + n_gated]):
         term = ref[...].astype(F32)
         if index >= n_terms:
-            term = jnp.where(flag[0] > 0, term, 0.0)
+            term = jnp.where(inner, term, 0.0)
         total = term if total is None else total + term
+    for index in range(n_split):
+        first, second = refs[n_terms + n_gated + 2 * index :][:2]
+        early = pl.program_id(0) < pl.num_programs(0) // 2
+        total = total + jnp.where(early, first[...], second[...]).astype(F32)
     refs[-1][...] = total.astype(refs[-1].dtype)
 
 
-def sum_call(flag, rows, terms, gated=(), dtype=BF16, after=()):
+def sum_call(here, rows, terms, gated=(), split=(), dtype=BF16, after=()):
     both = [*terms, *gated]
     width = both[0][0].shape[1]
     step = min(rows, 256)
     steps = rows // step
     return pl.pallas_call(
-        functools.partial(sum_kernel, len(terms), len(gated)),
+        functools.partial(sum_kernel, len(terms), len(gated), len(split)),
         grid=(steps,),
         out_shape=jax.ShapeDtypeStruct((rows, width), dtype),
         in_specs=[SMEM]
         + [pl.BlockSpec((step, width), lambda i, piece=piece: (piece * steps + i, 0)) for _, piece in both]
+        + [
+            pl.BlockSpec((step, width), lambda i: (jnp.minimum(i, steps // 2 - 1), 0)),
+            pl.BlockSpec((step, width), lambda i: (jnp.maximum(i - steps // 2, 0), 0)),
+        ]
+        * len(split)
         + [ANY] * len(after),
         out_specs=pl.BlockSpec((step, width), lambda i: (i, 0)),
         compiler_params=params(8),
         cost_estimate=SMALL,
         name="sum_terms",
-    )(flag, *(array for array, _ in both), *after)
+    )(here, *(array for array, _ in both), *(half for pair in split for half in pair), *after)
 
 
 def scatter_weights(kept, sent):
@@ -561,24 +611,17 @@
     return kept, swap(sent, 4)
 
 
-def level_weights(flag, kept, received):
+def level_weights(here, kept, received, after):
     rows = kept.shape[0]
-    value = sum_call(flag, rows, [(kept, 0), (received, 0)], dtype=BF16)
-    value = sum_call(flag, rows, [(value, 0), (outer_swap(value), 0)])
-    return sum_call(flag, rows, [(value, 0), (mirror_swap(value), 0)])
-
-
-def gather_weights(value, width, mine):
-    for bit in (4, 2, 1):
-        value = jnp.concatenate([value, swap(value, bit)], axis=0)
-    return unpack_call(mine, value, width)
-
-
-def reduce_line(far, near, pair, own, flag):
+    value = sum_call(here, rows, [(kept, 0), (received, 0)], dtype=BF16, after=after)
+    return sum_call(here, rows, [(term, 0) for term in (value, *(turn(value, by) for by in (1, 2, 3)))])
+
+
+def reduce_line(here, far, near, pair, own):
     rows = own.shape[0]
-    far_sum = inner_swap(sum_call(flag, rows, [(far, 0), (outer_swap(far), 0)]))
-    near_sum = inner_swap(sum_call(flag, rows, [(near, 0), (outer_swap(near), 0)]))
-    pair_in = outer_swap(sum_call(flag, rows, [(pair, 0)], [(far_sum, 0)]))
+    far_sum = inner_swap(sum_call(here, rows, [(far, 0), (outer_swap(far), 0)]))
+    near_sum = inner_swap(sum_call(here, rows, [(near, 0), (outer_swap(near), 0)]))
+    pair_in = outer_swap(sum_call(here, rows, [(pair, 0)], [(far_sum, 0)]))
     return own, pair_in, near_sum
 
 
@@ -595,59 +638,48 @@
     rows, width = nodes.shape
     row_blocks, _, slots, block = tiles.shape[:4]
     tile_local = tiles.reshape(row_blocks, slots, block, block)
-    cols = tile_col.reshape(row_blocks * slots)
+    cols = tile_col.reshape(row_blocks, slots).T
     counts = tile_count.reshape(row_blocks)
-    blocks = rows // block
     gathered, total = n_row * rows, n_col * rows
-    square_line = n_row == 8 and n_col == 4
-    if square_line:
-        mine = lax.axis_index("row").astype(jnp.int32)
-        cols = ((cols // blocks) ^ mine) * blocks + cols % blocks
-        level = lax.axis_index("col").astype(jnp.int32)
-        low = level < 2
-        order = jnp.stack([jnp.where(low, 3, 0), jnp.where(low, 2, 1), level ^ 1, level]).astype(jnp.int32)
-        inner = (level == 1) | (level == 2)
-        middle = inner.astype(jnp.int32).reshape(1)
+    paired = n_row == 8 and n_col == 4
+    here = lax.axis_index(("row", "col")).astype(jnp.int32).reshape(1)
+    known = (paired, here, cols, counts)
+    if paired:
         pieces = [gather_square(nodes)]
-        far, near = forward_call(cols, counts, order, pieces[0], tile_local, ((0,), (1,)), rows)
-        pair, own = forward_call(cols, counts, order, pieces[0], tile_local, ((2,), (3,)), rows)
-        parts = [reduce_line(far, near, pair, own, middle)]
+        far, near = forward_call(*known, pieces[0], tile_local, ((0,), (1,)), rows)
+        pair, own = forward_call(*known, pieces[0], tile_local, ((2,), (3,)), rows)
+        parts = [reduce_line(here, far, near, pair, own)]
         kinds = [("all", "all", "inner")]
     else:
-        order = jnp.arange(n_col, dtype=jnp.int32)
-        middle = jnp.zeros((1,), jnp.int32)
         pieces = [[lax.all_gather(nodes, "row", axis=0, tiled=True)]]
-        (partial,) = forward_call(cols, counts, order, pieces[0], tile_local, (tuple(range(n_col)),), rows)
+        (partial,) = forward_call(*known, pieces[0], tile_local, (tuple(range(n_col)),), rows)
         parts = [[lax.psum_scatter(partial, "col", scatter_dimension=0, tiled=True)]]
         kinds = [("all",)]
     vectors = [v.reshape(1, width) for v in (bias_in, ln_gain, ln_shift)]
     (updated, gpre_b, act, gproj, message, vec), gmsgs = mlp_call(
-        middle, nodes, cotangent, parts, kinds, w_in, vectors[0], w_out, vectors[1], vectors[2]
+        here, nodes, cotangent, parts, kinds, w_in, vectors[0], w_out, vectors[1], vectors[2]
     )
     factor = float(rows * n_row * n_col) ** -0.5
-    mine = lax.axis_index("row").astype(jnp.int32).reshape(1)
-    weight_args = (mine, nodes, message, act, gpre_b, gproj, cotangent, w_in, vec)
-    if square_line:
+    weight_args = (here, nodes, message, act, gpre_b, gproj, cotangent, w_in, vec)
+    if paired:
         halves = ((1, 3, 5, 7), (0, 2, 4, 6))
         grads = [gather_line(gmsgs[0])]
-        kept, sent, direct = weight_call(factor, n_row, *weight_args, (grads[0][1], grads[0][2]))
-        all_weights = level_weights(middle, *scatter_weights(kept, sent))
-        weights = gather_weights(all_weights, width, mine)
+        kept, sent, direct = weight_call(factor, n_row, *weight_args, ())
+        row_weights = scatter_weights(kept, sent)
         near_grads, token = tile_grad_call(
-            cols, counts, order, middle, [grads[0][:2]], pieces, tile_local.shape, rows, (3, 2),
-            after=(grads[0][3], grads[0][4]),
-        )
-        odd, even = back_call(
-            cols, counts, order, middle, grads[0], tile_local, total, gathered, halves, (token, weights[2])
-        )
+            *known, [grads[0][:2]], pieces, tile_local.shape, rows, (3, 2), after=(grads[0][3], grads[0][4])
+        )
+        all_weights = level_weights(here, *row_weights, (token,))
+        odd, even = back_call(*known, grads[0], tile_local, total, gathered, halves, (token, all_weights))
         other = swap(odd, 1)
-        sums = [sum_call(middle, rows, [(even, piece), (other, piece)]) for piece in (1, 2, 3)]
-        x_side, y_side, diagonal = [swap(value, bit) for value, bit in zip(sums, (2, 4, 6))]
+        joint = jnp.concatenate([all_weights] + [swap(all_weights, bits) for bits in (2, 4, 6)], axis=0)
+        arrived, sums = reduce_square(here, even, other, rows, (joint,))
+        weights = unpack_call(here, joint, swap(joint, 1), width)
         grad_tiles, _ = tile_grad_call(
-            cols, counts, order, middle, grads, pieces, tile_local.shape, rows, (1, 0), near_grads, sums
+            *known, grads, pieces, tile_local.shape, rows, (1, 0), near_grads, sums
         )
         grad_nodes = sum_call(
-            middle, rows, [(term, 0) for term in (direct, even, other, x_side, y_side, diagonal)]
+            here, rows, [(direct, 0), (even, 0), (other, 0)] + [(term, 0) for term in arrived]
         )
     else:
         grads = [[lax.all_gather(gmsgs[0], "col", axis=0, tiled=True)]]
@@ -658,13 +690,11 @@
             weight_sums[2 * width : 3 * width],
             weight_sums[3 * width : 3 * width + 3],
         )
-        (terms,) = back_call(
-            cols, counts, order, middle, grads[0], tile_local, total, gathered, (tuple(range(n_row)),)
-        )
+        (terms,) = back_call(*known, grads[0], tile_local, total, gathered, (tuple(range(n_row)),))
         back = lax.psum_scatter(terms, "row", scatter_dimension=0, tiled=True)
-        grad_nodes = sum_call(middle, rows, [(direct, 0), (back, 0)])
+        grad_nodes = sum_call(here, rows, [(direct, 0), (back, 0)])
         grad_tiles, _ = tile_grad_call(
-            cols, counts, order, middle, grads, pieces, tile_local.shape, rows, tuple(range(n_col))
+            *known, grads, pieces, tile_local.shape, rows, tuple(range(n_col))
         )
     grad_tiles = grad_tiles.reshape(tiles.shape)
     return (updated, grad_nodes, grad_tiles, *weights)

time: 186 us -> 169 us (0.909)
  waiting for transfers between devices: 106 us -> 71.7 us
  starting transfers between devices: 31.7 us -> 49.6 us
  Pallas kernels: 39.1 us -> 41.8 us
    ppermute x17 -> x24, waiting for transfers between devices: 58.8 us -> 34.1 us  [swap(): return lax.ppermute(value, 'row', [(i, i ^ bit) for i in range(8)])]
    ppermute x7 -> x6, starting transfers between devices: 13.4 us -> 26.8 us  [outer_swap(): return lax.ppermute(value, 'col', [(0, 1), (1, 0), (2, 3), (3, 2)])]
    ppermute x7 -> x6, waiting for transfers between devices: 44.3 us -> 32.6 us  [outer_swap(): return lax.ppermute(value, 'col', [(0, 1), (1, 0), (2, 3), (3, 2)])]
    ppermute x17 -> x24, starting transfers between devices: 15.2 us -> 18.3 us  [swap(): return lax.ppermute(value, 'row', [(i, i ^ bit) for i in range(8)])]
    unnamed x57 -> x76, local copies, waits for them, and re-layouts: 5.53 us -> 3.28 us
    ppermute x1 -> x3, waiting for transfers between devices: 3.16 us -> 5.02 us  [turn(): return lax.ppermute(value, 'col', [(i, (i + by) % 4) for i in range(4)])]
    ppermute x1 -> x3, starting transfers between devices: 2.99 us -> 3.88 us  [turn(): return lax.ppermute(value, 'col', [(i, (i + by) % 4) for i in range(4)])]
    pallas_call x12 -> x11, Pallas kernels: 13.6 us -> 13.7 us  [the longest x2 10.9 us: forward_call(): pl.pallas_call(functools.partial(forward_kernel, outputs, len(pieces), pa...]
  transfers between devices with their start and end apart: 29 -> 37, of which waited for: 19 -> 16; matrix products, arithmetic and copies ran while one was open for 1% -> 1% of each run, Pallas kernels for 10% -> 13%
where the time goes in v9:
time: 169 us
  waiting for transfers between devices  71.7 us (42%)
  starting transfers between devices  49.6 us (29%)
  Pallas kernels  41.8 us (25%)
  local copies, waits for them, and re-layouts  4.38 us (3%)
    ppermute x24, waiting for transfers between devices, swap(): return lax.ppermute(value, 'row', [(i, i ^ bit) for i in range(8)])  34.1 us
    ppermute x6, waiting for transfers between devices, outer_swap(): return lax.ppermute(value, 'col', [(0, 1), (1, 0), (2, 3), (3, 2)])  32.6 us
    ppermute x6, starting transfers between devices, outer_swap(): return lax.ppermute(value, 'col', [(0, 1), (1, 0), (2, 3), (3, 2)])  26.8 us
    ppermute x24, starting transfers between devices, swap(): return lax.ppermute(value, 'row', [(i, i ^ bit) for i in range(8)])  18.3 us
    pallas_call x2, Pallas kernels, tile_grad_call(): pl.pallas_call(functools.partial(tile_grad_kernel, rows, slots, len(grads...  12.4 us
    pallas_call x2, Pallas kernels, forward_call(): pl.pallas_call(functools.partial(forward_kernel, outputs, len(pieces), pa...  10.9 us
    pallas_call x1, Pallas kernels, back_call(): pl.pallas_call(functools.partial(back_kernel, rows, slots, len(grads), le...  8.54 us
    ppermute x3, waiting for transfers between devices, turn(): return lax.ppermute(value, 'col', [(i, (i + by) % 4) for i in range(4)])  5.02 us
  transfers between devices with their start and end apart: 37, of which 16 were waited for; matrix products, arithmetic and copies ran while one was open for 1% of the time, Pallas kernels for 13%

profile of v9, /device:TPU:0, one launch (start us, length us, event | category | flops | bytes accessed | tf_op | source)
XLA Modules:
  0.0 168.9 jit_solution(10637695416231372944)
XLA Ops:
  0.6 0.5 collective-permute-start
  1.1 1.1 fusion
  2.2 2.6 %collective-permute-start.1 = (bf16[512,256]{1,0:T(8,128)(2,1)S(1)}, bf16[512,256]{1,0:T(8,128)(2,1)S(1)}, u32[]{:S(2)}, u32[]{:S(2)}) collective-permute-start(bf16[512,256]{1,0:T(8,128)(2,1)S(1)} %get-tuple-element.57), channel_id=1, source_target_pairs={{0,8},{4,12},{8,0},{12,4},{16,24},{20,28},{24,16},{28,20},{1,9},{5... | collective-permute-start | bytes 786440 | tf_op jit(solution)/shard_map/ppermute | solution.py:530
  4.8 1.5 collective-permute-start.5
  6.3 0.5 collective-permute-start.2
  6.9 5.0 %collective-permute-done.1.refs_2_.refs_4_.refs_8_ = bf16[512,256]{1,0:T(8,128)(2,1)S(1)} collective-permute-done((bf16[512,256]{1,0:T(8,128)(2,1)S(1)}, bf16[512,256]{1,0:T(8,128)(2,1)S(1)}, u32[]{:S(2)}, u32[]{:S(2)}) %collective-permute-start.1) | collective-permute-done | bytes 262176 | tf_op jit(solution)/shard_map/ppermute | solution.py:530
  11.9 2.0 %collective-permute-done.5.refs_6_.refs_8_.refs_12_ = bf16[512,256]{1,0:T(8,128)(2,1)S(1)} collective-permute-done((bf16[512,256]{1,0:T(8,128)(2,1)S(1)}, bf16[512,256]{1,0:T(8,128)(2,1)S(1)}, u32[]{:S(2)}, u32[]{:S(2)}) %collective-permute-start.5) | collective-permute-done | bytes 262176 | tf_op jit(solution)/shard_map/ppermute | solution.py:530
  14.0 3.6 %collective-permute-done.2.refs_3_.refs_5_.refs_9_ = bf16[512,256]{1,0:T(8,128)(2,1)S(1)} collective-permute-done((bf16[512,256]{1,0:T(8,128)(2,1)S(1)}, bf16[512,256]{1,0:T(8,128)(2,1)S(1)}, u32[]{:S(2)}, u32[]{:S(2)}) %collective-permute-start.2) | collective-permute-done | bytes 262176 | tf_op jit(solution)/shard_map/ppermute | solution.py:530
  17.6 2.0 %collective-permute-start.10 = (bf16[512,256]{1,0:T(8,128)(2,1)S(1)}, bf16[512,256]{1,0:T(8,128)(2,1)S(1)}, u32[]{:S(2)}, u32[]{:S(2)}) collective-permute-start(bf16[512,256]{1,0:T(8,128)(2,1)S(1)} %collective-permute-done.2.refs_3_.refs_5_.refs_9_), channel_id=1, source_target_pairs={{0,16},{4,20},{8,24},{12,28},{16,0},{20,4},{24,8},{28,12},{1,17},{... | collective-permute-start | bytes 786440 | tf_op jit(solution)/shard_map/ppermute | solution.py:530
  19.6 0.5 collective-permute-start.7
  20.1 0.1 collective-permute-start.8
  20.2 2.8 %collective-permute-done.9.refs_10_.refs_12_.refs_16_ = bf16[512,256]{1,0:T(8,128)(2,1)S(1)} collective-permute-done((bf16[512,256]{1,0:T(8,128)(2,1)S(1)}, bf16[512,256]{1,0:T(8,128)(2,1)S(1)}, u32[]{:S(2)}, u32[]{:S(2)}) %collective-permute-start.9) | collective-permute-done | bytes 262176 | tf_op jit(solution)/shard_map/ppermute | solution.py:530
  23.0 2.5 %collective-permute-done.10.refs_11_.refs_13_.refs_17_ = bf16[512,256]{1,0:T(8,128)(2,1)S(1)} collective-permute-done((bf16[512,256]{1,0:T(8,128)(2,1)S(1)}, bf16[512,256]{1,0:T(8,128)(2,1)S(1)}, u32[]{:S(2)}, u32[]{:S(2)}) %collective-permute-start.10) | collective-permute-done | bytes 262176 | tf_op jit(solution)/shard_map/ppermute | solution.py:530
  25.6 1.6 collective-permute-done.12.refs_13_.refs_15_.refs_19_
  27.3 5.4 %partial_messages.3 = (bf16[1024,256]{1,0:T(8,128)(2,1)}, bf16[1024,256]{1,0:T(8,128)(2,1)}) custom-call(s32[1]{0:T(128)} %bitcast.here.refs_0_, s32[4,32]{1,0:T(4,128)} %bitcast.16, s32[32]{0:T(128)} %bitcast.21, bf16[1024,256]{1,0:T(8,128)(2,1)} %refs_6_.1, bf16[1024,256]{1,0:T(8,128)(2,1)} %copy-done.2, bf16[512,256]{1,0:T(8,128)(2,1)} %copy-done.4, ...), custom_call_target="tpu_custom_call" | custom-call | flops 1048576 | bytes 65536 | tf_op jit(solution)/shard_map/partial_messages/pallas_call | solution.py:132
  32.6 1.7 collective-permute-start.13
  34.3 0.4 collective-permute-start.16
  34.7 13.0 %collective-permute-done.13.refs_2_ = bf16[1024,256]{1,0:T(8,128)(2,1)S(1)} collective-permute-done((bf16[1024,256]{1,0:T(8,128)(2,1)}, bf16[1024,256]{1,0:T(8,128)(2,1)S(1)}, u32[]{:S(2)}, u32[]{:S(2)}) %collective-permute-start.13) | collective-permute-done | bytes 524320 | tf_op jit(solution)/shard_map/ppermute | solution.py:534
  47.7 1.0 copy-done.30
  48.7 0.2 sum_terms.9
  49.0 0.1 collective-permute-start.14
  49.1 5.5 %partial_messages.2 = (bf16[1024,256]{1,0:T(8,128)(2,1)}, bf16[1024,256]{1,0:T(8,128)(2,1)}) custom-call(s32[1]{0:T(128)} %bitcast.here.refs_0_, s32[4,32]{1,0:T(4,128)} %bitcast.17, s32[32]{0:T(128)} %bitcast.22, bf16[1024,256]{1,0:T(8,128)(2,1)} %refs_6_.1, bf16[1024,256]{1,0:T(8,128)(2,1)} %copy-done.2, bf16[512,256]{1,0:T(8,128)(2,1)} %copy-done.4, ...), custom_call_target="tpu_custom_call" | custom-call | flops 1048576 | bytes 65536 | tf_op jit(solution)/shard_map/partial_messages/pallas_call | solution.py:132
  54.6 3.5 %collective-permute-done.16.refs_2_ = bf16[1024,256]{1,0:T(8,128)(2,1)S(1)} collective-permute-done((bf16[1024,256]{1,0:T(8,128)(2,1)}, bf16[1024,256]{1,0:T(8,128)(2,1)S(1)}, u32[]{:S(2)}, u32[]{:S(2)}) %collective-permute-start.16) | collective-permute-done | bytes 524320 | tf_op jit(solution)/shard_map/ppermute | solution.py:534
  58.1 0.2 sum_terms.11
  58.3 0.1 collective-permute-start.17
  58.4 1.0 copy-done.29
  59.4 0.2 sum_terms.10
  59.6 5.8 %collective-permute-start.15 = (bf16[1024,256]{1,0:T(8,128)(2,1)S(1)}, bf16[1024,256]{1,0:T(8,128)(2,1)S(1)}, u32[]{:S(2)}, u32[]{:S(2)}) collective-permute-start(bf16[1024,256]{1,0:T(8,128)(2,1)S(1)} %sum_terms.10), channel_id=1, source_target_pairs={{0,1},{1,0},{2,3},{3,2},{4,5},{5,4},{6,7},{7,6},{8,9},{9,8},{10,11... | collective-permute-start | bytes 1572872 | tf_op jit(solution)/shard_map/ppermute | solution.py:534
  65.4 8.6 %collective-permute-done.15.refs_1_ = bf16[1024,256]{1,0:T(8,128)(2,1)S(1)} collective-permute-done((bf16[1024,256]{1,0:T(8,128)(2,1)S(1)}, bf16[1024,256]{1,0:T(8,128)(2,1)S(1)}, u32[]{:S(2)}, u32[]{:S(2)}) %collective-permute-start.15) | collective-permute-done | bytes 524320 | tf_op jit(solution)/shard_map/ppermute | solution.py:534
  74.1 1.0 copy-done.31
  75.2 4.7 %mlp.1 = (bf16[1024,256]{1,0:T(8,128)(2,1)}, bf16[1024,256]{1,0:T(8,128)(2,1)S(1)}, bf16[1024,256]{1,0:T(8,128)(2,1)S(1)}, bf16[1024,256]{1,0:T(8,128)(2,1)S(1)}...) custom-call(s32[1]{0:T(128)} %bitcast.here.refs_0_, ...), custom_call_target="tpu_custom_call" | custom-call | flops 1048576 | bytes 65536 | tf_op jit(solution)/shard_map/mlp/pallas_call | solution.py:226
  79.9 1.7 %collective-permute-start.18 = (bf16[1024,256]{1,0:T(8,128)(2,1)S(1)}, bf16[1024,256]{1,0:T(8,128)(2,1)S(1)}, u32[]{:S(2)}, u32[]{:S(2)}) collective-permute-start(bf16[1024,256]{1,0:T(8,128)(2,1)S(1)} %get-tuple-element.39.refs_0_), channel_id=1, source_target_pairs={{0,1},{1,0},{2,3},{3,2},{4,5},{5,4},{6,7},{7,6},{8,9},{9,8},{10,11... | collective-permute-start | bytes 1572872 | tf_op jit(solution)/shard_map/ppermute | solution.py:534
  81.7 1.5 weight_grads.1
  83.2 0.1 collective-permute-start.23
  83.3 0.5 collective-permute-start.19
  83.8 7.5 %collective-permute-done.18.refs_1_ = bf16[1024,256]{1,0:T(8,128)(2,1)S(1)} collective-permute-done((bf16[1024,256]{1,0:T(8,128)(2,1)S(1)}, bf16[1024,256]{1,0:T(8,128)(2,1)S(1)}, u32[]{:S(2)}, u32[]{:S(2)}) %collective-permute-start.18) | collective-permute-done | bytes 524320 | tf_op jit(solution)/shard_map/ppermute | solution.py:534
  91.4 1.5 collective-permute-start.24
  92.9 6.2 %collective-permute-start.20 = (bf16[1024,256]{1,0:T(8,128)(2,1)S(1)}, bf16[1024,256]{1,0:T(8,128)(2,1)S(1)}, u32[]{:S(2)}, u32[]{:S(2)}) collective-permute-start(bf16[1024,256]{1,0:T(8,128)(2,1)S(1)} %collective-permute-done.19.refs_2_), channel_id=1, source_target_pairs={{0,1},{1,0},{2,3},{3,2},{4,5},{5,4},{6,7},{7,6},{8,9},{9,8},{10,11... | collective-permute-start | bytes 1572872 | tf_op jit(solution)/shard_map/ppermute | solution.py:534
  99.2 11.0 %collective-permute-start.22 = (bf16[1024,256]{1,0:T(8,128)(2,1)S(1)}, bf16[1024,256]{1,0:T(8,128)(2,1)S(1)}, u32[]{:S(2)}, u32[]{:S(2)}) collective-permute-start(bf16[1024,256]{1,0:T(8,128)(2,1)S(1)} %collective-permute-done.21.refs_17_.refs_4_), channel_id=1, source_target_pairs={{0,1},{1,0},{2,3},{3,2},{4,5},{5,4},{6,7},{7,6},{8,9},{9,8},{10,11... | collective-permute-start | bytes 1572872 | tf_op jit(solution)/shard_map/ppermute | solution.py:534
  110.2 1.6 collective-permute-start.25
  111.9 5.9 %tile_grads.2 = (bf16[128,128,128]{2,1,0:T(8,128)(2,1)}, f32[8,128]{1,0:T(8,128)S(1)}) custom-call(s32[1]{0:T(128)} %bitcast.here.refs_0_, s32[4,32]{1,0:T(4,128)S(1)} %bitcast.18, s32[32]{0:T(128)S(1)} %bitcast.23, bf16[1024,256]{1,0:T(8,128)(2,1)S(1)} %get-tuple-element.39.refs_0_, bf16[1024,256]{1,0:T(8,128)(2,1)S(1)} %collective-permute-done.18.refs_1_, ...), custom_call_target="tpu_custom_call" | custom-call | flops 1048576 | bytes 65536 | tf_op jit(solution)/shard_map/tile_grads/pallas_call | solution.py:502
  117.8 0.6 collective-permute-start.26
  118.4 2.3 %collective-permute-start.27 = (bf16[112,256]{1,0:T(8,128)(2,1)S(1)}, bf16[112,256]{1,0:T(8,128)(2,1)S(1)}, u32[]{:S(2)}, u32[]{:S(2)}) collective-permute-start(bf16[112,256]{1,0:T(8,128)(2,1)S(1)} %sum_terms.12.refs_1_), channel_id=1, source_target_pairs={{0,2},{1,3},{2,0},{3,1},{4,6},{5,7},{6,4},{7,5},{8,10},{9,11},{10,... | collective-permute-start | bytes 172040 | tf_op jit(solution)/shard_map/ppermute | solution.py:538
  120.7 1.0 collective-permute-start.28
  121.7 5.0 %collective-permute-done.26.refs_2_ = bf16[112,256]{1,0:T(8,128)(2,1)S(1)} collective-permute-done((bf16[112,256]{1,0:T(8,128)(2,1)S(1)}, bf16[112,256]{1,0:T(8,128)(2,1)S(1)}, u32[]{:S(2)}, u32[]{:S(2)}) %collective-permute-start.26) | collective-permute-done | bytes 57376 | tf_op jit(solution)/shard_map/ppermute | solution.py:538
  126.8 8.5 %back_terms.1 = (bf16[4096,256]{1,0:T(8,128)(2,1)S(1)}, bf16[4096,256]{1,0:T(8,128)(2,1)S(1)}) custom-call(s32[1]{0:T(128)} %bitcast.here.refs_0_, s32[4,32]{1,0:T(4,128)S(1)} %bitcast.19, s32[32]{0:T(128)S(1)} %bitcast.24, bf16[1024,256]{1,0:T(8,128)(2,1)S(1)} %get-tuple-element.39.refs_0_, bf16[1024,256]{1,0:T(8,128)(2,1)S(1)} %collective-permute-done.18.refs_1_, ...), custom_call_target="tpu_custom_call" | custom-call | flops 1048576 | bytes 65536 | tf_op jit(solution)/shard_map/back_terms/pallas_call | solution.py:402
  135.3 0.1 collective-permute-start.29
  135.4 0.8 collective-permute-start.32
  136.2 0.7 collective-permute-start.31
  136.9 2.1 %collective-permute-start.30 = (bf16[112,256]{1,0:T(8,128)(2,1)S(1)}, bf16[112,256]{1,0:T(8,128)(2,1)S(1)}, u32[]{:S(2)}, u32[]{:S(2)}) collective-permute-start(bf16[112,256]{1,0:T(8,128)(2,1)S(1)} %sum_terms.13.refs_8_), channel_id=1, source_target_pairs={{0,8},{4,12},{8,0},{12,4},{16,24},{20,28},{24,16},{28,20},{1,9},{5... | collective-permute-start | bytes 172040 | tf_op jit(solution)/shard_map/ppermute | solution.py:530
  139.0 2.1 %collective-permute-done.32 = bf16[112,256]{1,0:T(8,128)(2,1)S(1)} collective-permute-done((bf16[112,256]{1,0:T(8,128)(2,1)S(1)}, bf16[112,256]{1,0:T(8,128)(2,1)S(1)}, u32[]{:S(2)}, u32[]{:S(2)}) %collective-permute-start.32) | collective-permute-done | bytes 57376 | tf_op jit(solution)/shard_map/ppermute | solution.py:530
  141.1 0.4 collective-permute-done.31
  141.5 0.2 sum_terms.14.refs_21_
  141.7 1.7 %collective-permute-start.33 = (bf16[1024,256]{1,0:T(8,128)(2,1)S(1)}, bf16[1024,256]{1,0:T(8,128)(2,1)S(1)}, u32[]{:S(2)}, u32[]{:S(2)}) collective-permute-start(bf16[1024,256]{1,0:T(8,128)(2,1)S(1)} %sum_terms.14.refs_21_), channel_id=1, source_target_pairs={{0,8},{4,12},{8,0},{12,4},{16,24},{20,28},{24,16},{28,20},{1,9},{5... | collective-permute-start | bytes 1572872 | tf_op jit(solution)/shard_map/ppermute | solution.py:530
  143.4 0.2 sum_terms.15.refs_22_
  143.6 0.1 collective-permute-start.34
  143.8 0.2 sum_terms.16.refs_23_
  143.9 1.8 %collective-permute-start.35 = (bf16[1024,256]{1,0:T(8,128)(2,1)S(1)}, bf16[1024,256]{1,0:T(8,128)(2,1)S(1)}, u32[]{:S(2)}, u32[]{:S(2)}) collective-permute-start(bf16[1024,256]{1,0:T(8,128)(2,1)S(1)} %sum_terms.16.refs_23_), channel_id=1, source_target_pairs={{0,24},{4,28},{8,16},{12,20},{16,8},{20,12},{24,0},{28,4},{1,25},{... | collective-permute-start | bytes 1572872 | tf_op jit(solution)/shard_map/ppermute | solution.py:530
  145.7 1.5 collective-permute-done.36.odd
  147.2 1.0 weight_unpack.1
  148.2 6.5 %tile_grads.3 = (bf16[128,128,128]{2,1,0:T(8,128)(2,1)}, f32[8,128]{1,0:T(8,128)}) custom-call(s32[1]{0:T(128)} %bitcast.here.refs_0_, s32[4,32]{1,0:T(4,128)S(1)} %bitcast.20, s32[32]{0:T(128)S(1)} %bitcast.25, bf16[1024,256]{1,0:T(8,128)(2,1)S(1)} %get-tuple-element.39.refs_0_, ...), custom_call_target="tpu_custom_call", output_to_operand_aliasing={{0}: (23, {})} | custom-call | flops 1048576 | bytes 65536 | tf_op jit(solution)/shard_map/tile_grads/pallas_call | solution.py:502
  154.7 1.9 %collective-permute-done.33.refs_4_ = bf16[1024,256]{1,0:T(8,128)(2,1)S(1)} collective-permute-done((bf16[1024,256]{1,0:T(8,128)(2,1)S(1)}, bf16[1024,256]{1,0:T(8,128)(2,1)S(1)}, u32[]{:S(2)}, u32[]{:S(2)}) %collective-permute-start.33) | collective-permute-done | bytes 524320 | tf_op jit(solution)/shard_map/ppermute | solution.py:530
  156.6 10.7 %collective-permute-done.34.refs_5_ = bf16[1024,256]{1,0:T(8,128)(2,1)S(1)} collective-permute-done((bf16[1024,256]{1,0:T(8,128)(2,1)S(1)}, bf16[1024,256]{1,0:T(8,128)(2,1)S(1)}, u32[]{:S(2)}, u32[]{:S(2)}) %collective-permute-start.34) | collective-permute-done | bytes 524320 | tf_op jit(solution)/shard_map/ppermute | solution.py:530
  167.3 1.6 sum_terms.17
  (109 shorter events, 0.5 us)
Async XLA Ops:
  0.6 18.9 %collective-permute-start = (bf16[1024,256]{1,0:T(8,128)(2,1)}, bf16[1024,256]{1,0:T(8,128)(2,1)S(1)}, u32[]{:S(2)}, u32[]{:S(2)}) collective-permute-start(bf16[1024,256]{1,0:T(8,128)(2,1)} %refs_6_.1), channel_id=1, source_target_pairs={{0,4},{4,0},{8,12},{12,8},{16,20},{20,16},{24,28},{28,24},{1,5},{5... | collective-permute-start | bytes 1572872 | tf_op jit(solution)/shard_map/ppermute | solution.py:530
  2.2 9.7 %collective-permute-start.1 = (bf16[512,256]{1,0:T(8,128)(2,1)S(1)}, bf16[512,256]{1,0:T(8,128)(2,1)S(1)}, u32[]{:S(2)}, u32[]{:S(2)}) collective-permute-start(bf16[512,256]{1,0:T(8,128)(2,1)S(1)} %get-tuple-element.57), channel_id=1, source_target_pairs={{0,8},{4,12},{8,0},{12,4},{16,24},{20,28},{24,16},{28,20},{1,9},{5... | collective-permute-start | bytes 786440 | tf_op jit(solution)/shard_map/ppermute | solution.py:530
  4.8 9.1 %collective-permute-start.5 = (bf16[512,256]{1,0:T(8,128)(2,1)S(1)}, bf16[512,256]{1,0:T(8,128)(2,1)S(1)}, u32[]{:S(2)}, u32[]{:S(2)}) collective-permute-start(bf16[512,256]{1,0:T(8,128)(2,1)S(1)} %get-tuple-element.57), channel_id=1, source_target_pairs={{0,16},{4,20},{8,24},{12,28},{16,0},{20,4},{24,8},{28,12},{1,17},{... | collective-permute-start | bytes 786440 | tf_op jit(solution)/shard_map/ppermute | solution.py:530
  6.3 11.3 %collective-permute-start.2 = (bf16[512,256]{1,0:T(8,128)(2,1)S(1)}, bf16[512,256]{1,0:T(8,128)(2,1)S(1)}, u32[]{:S(2)}, u32[]{:S(2)}) collective-permute-start(bf16[512,256]{1,0:T(8,128)(2,1)S(1)} %get-tuple-element.56), channel_id=1, source_target_pairs={{0,8},{4,12},{8,0},{12,4},{16,24},{20,28},{24,16},{28,20},{1,9},{5... | collective-permute-start | bytes 786440 | tf_op jit(solution)/shard_map/ppermute | solution.py:530
  6.8 12.7 %collective-permute-start.6 = (bf16[512,256]{1,0:T(8,128)(2,1)S(1)}, bf16[512,256]{1,0:T(8,128)(2,1)S(1)}, u32[]{:S(2)}, u32[]{:S(2)}) collective-permute-start(bf16[512,256]{1,0:T(8,128)(2,1)S(1)} %get-tuple-element.56), channel_id=1, source_target_pairs={{0,16},{4,20},{8,24},{12,28},{16,0},{20,4},{24,8},{28,12},{1,17},{... | collective-permute-start | bytes 786440 | tf_op jit(solution)/shard_map/ppermute | solution.py:530
  11.9 15.2 %copy-start.4 = (bf16[512,256]{1,0:T(8,128)(2,1)}, bf16[512,256]{1,0:T(8,128)(2,1)S(1)}, u32[]{:S(2)}) copy-start(bf16[512,256]{1,0:T(8,128)(2,1)S(1)} %collective-permute-done.1.refs_2_.refs_4_.refs_8_) | copy-start | bytes 786436
  11.9 8.1 %collective-permute-start.3 = (bf16[512,256]{1,0:T(8,128)(2,1)S(1)}, bf16[512,256]{1,0:T(8,128)(2,1)S(1)}, u32[]{:S(2)}, u32[]{:S(2)}) collective-permute-start(bf16[512,256]{1,0:T(8,128)(2,1)S(1)} %collective-permute-done.1.refs_2_.refs_4_.refs_8_), channel_id=1, source_target_pairs={{0,4},{4,0},{8,12},{12,8},{16,20},{20,16},{24,28},{28,24},{1,5},{5... | collective-permute-start | bytes 786440 | tf_op jit(solution)/shard_map/ppermute | solution.py:530
  13.9 13.2 %copy-start.6 = (bf16[512,256]{1,0:T(8,128)(2,1)}, bf16[512,256]{1,0:T(8,128)(2,1)S(1)}, u32[]{:S(2)}) copy-start(bf16[512,256]{1,0:T(8,128)(2,1)S(1)} %collective-permute-done.5.refs_6_.refs_8_.refs_12_) | copy-start | bytes 786436
  13.9 9.1 %collective-permute-start.9 = (bf16[512,256]{1,0:T(8,128)(2,1)S(1)}, bf16[512,256]{1,0:T(8,128)(2,1)S(1)}, u32[]{:S(2)}, u32[]{:S(2)}) collective-permute-start(bf16[512,256]{1,0:T(8,128)(2,1)S(1)} %collective-permute-done.5.refs_6_.refs_8_.refs_12_), channel_id=1, source_target_pairs={{0,8},{4,12},{8,0},{12,4},{16,24},{20,28},{24,16},{28,20},{1,9},{5... | collective-permute-start | bytes 786440 | tf_op jit(solution)/shard_map/ppermute | solution.py:530
  17.6 9.6 %copy-start.8 = (bf16[512,256]{1,0:T(8,128)(2,1)}, bf16[512,256]{1,0:T(8,128)(2,1)S(1)}, u32[]{:S(2)}) copy-start(bf16[512,256]{1,0:T(8,128)(2,1)S(1)} %collective-permute-done.2.refs_3_.refs_5_.refs_9_) | copy-start | bytes 786436
  17.6 7.9 %collective-permute-start.10 = (bf16[512,256]{1,0:T(8,128)(2,1)S(1)}, bf16[512,256]{1,0:T(8,128)(2,1)S(1)}, u32[]{:S(2)}, u32[]{:S(2)}) collective-permute-start(bf16[512,256]{1,0:T(8,128)(2,1)S(1)} %collective-permute-done.2.refs_3_.refs_5_.refs_9_), channel_id=1, source_target_pairs={{0,16},{4,20},{8,24},{12,28},{16,0},{20,4},{24,8},{28,12},{1,17},{... | collective-permute-start | bytes 786440 | tf_op jit(solution)/shard_map/ppermute | solution.py:530
  19.5 7.6 %copy-start.10 = (bf16[512,256]{1,0:T(8,128)(2,1)}, bf16[512,256]{1,0:T(8,128)(2,1)S(1)}, u32[]{:S(2)}) copy-start(bf16[512,256]{1,0:T(8,128)(2,1)S(1)} %collective-permute-done.6.refs_7_.refs_9_.refs_13_) | copy-start | bytes 786436
  19.5 6.0 %collective-permute-start.4 = (bf16[512,256]{1,0:T(8,128)(2,1)S(1)}, bf16[512,256]{1,0:T(8,128)(2,1)S(1)}, u32[]{:S(2)}, u32[]{:S(2)}) collective-permute-start(bf16[512,256]{1,0:T(8,128)(2,1)S(1)} %collective-permute-done.2.refs_3_.refs_5_.refs_9_), channel_id=1, source_target_pairs={{0,4},{4,0},{8,12},{12,8},{16,20},{20,16},{24,28},{28,24},{1,5},{5... | collective-permute-start | bytes 786440 | tf_op jit(solution)/shard_map/ppermute | solution.py:530
  19.6 5.9 %collective-permute-start.7 = (bf16[512,256]{1,0:T(8,128)(2,1)S(1)}, bf16[512,256]{1,0:T(8,128)(2,1)S(1)}, u32[]{:S(2)}, u32[]{:S(2)}) collective-permute-start(bf16[512,256]{1,0:T(8,128)(2,1)S(1)} %collective-permute-done.5.refs_6_.refs_8_.refs_12_), channel_id=1, source_target_pairs={{0,4},{4,0},{8,12},{12,8},{16,20},{20,16},{24,28},{28,24},{1,5},{5... | collective-permute-start | bytes 786440 | tf_op jit(solution)/shard_map/ppermute | solution.py:530
  20.1 5.5 %collective-permute-start.8 = (bf16[512,256]{1,0:T(8,128)(2,1)S(1)}, bf16[512,256]{1,0:T(8,128)(2,1)S(1)}, u32[]{:S(2)}, u32[]{:S(2)}) collective-permute-start(bf16[512,256]{1,0:T(8,128)(2,1)S(1)} %collective-permute-done.6.refs_7_.refs_9_.refs_13_), channel_id=1, source_target_pairs={{0,4},{4,0},{8,12},{12,8},{16,20},{20,16},{24,28},{28,24},{1,5},{5... | collective-permute-start | bytes 786440 | tf_op jit(solution)/shard_map/ppermute | solution.py:530
  23.0 2.6 %collective-permute-start.11 = (bf16[512,256]{1,0:T(8,128)(2,1)S(1)}, bf16[512,256]{1,0:T(8,128)(2,1)S(1)}, u32[]{:S(2)}, u32[]{:S(2)}) collective-permute-start(bf16[512,256]{1,0:T(8,128)(2,1)S(1)} %collective-permute-done.9.refs_10_.refs_12_.refs_16_), channel_id=1, source_target_pairs={{0,4},{4,0},{8,12},{12,8},{16,20},{20,16},{24,28},{28,24},{1,5},{5... | collective-permute-start | bytes 786440 | tf_op jit(solution)/shard_map/ppermute | solution.py:530
  25.5 1.7 collective-permute-start.12
  32.6 15.0 %collective-permute-start.13 = (bf16[1024,256]{1,0:T(8,128)(2,1)}, bf16[1024,256]{1,0:T(8,128)(2,1)S(1)}, u32[]{:S(2)}, u32[]{:S(2)}) collective-permute-start(bf16[1024,256]{1,0:T(8,128)(2,1)} %get-tuple-element.30.refs_1_), channel_id=1, source_target_pairs={{0,1},{1,0},{2,3},{3,2},{4,5},{5,4},{6,7},{7,6},{8,9},{9,8},{10,11... | collective-permute-start | bytes 1572872 | tf_op jit(solution)/shard_map/ppermute | solution.py:534
  34.3 23.8 %collective-permute-start.16 = (bf16[1024,256]{1,0:T(8,128)(2,1)}, bf16[1024,256]{1,0:T(8,128)(2,1)S(1)}, u32[]{:S(2)}, u32[]{:S(2)}) collective-permute-start(bf16[1024,256]{1,0:T(8,128)(2,1)} %get-tuple-element.31.refs_1_), channel_id=1, source_target_pairs={{0,1},{1,0},{2,3},{3,2},{4,5},{5,4},{6,7},{7,6},{8,9},{9,8},{10,11... | collective-permute-start | bytes 1572872 | tf_op jit(solution)/shard_map/ppermute | solution.py:534
  48.9 9.2 %copy-start.28 = (bf16[1024,256]{1,0:T(8,128)(2,1)S(1)}, bf16[1024,256]{1,0:T(8,128)(2,1)}, u32[]{:S(2)}) copy-start(bf16[1024,256]{1,0:T(8,128)(2,1)} %get-tuple-element.31.refs_1_) | copy-start | bytes 1572868
  48.9 25.1 %copy-start.1 = (bf16[1024,256]{1,0:T(8,128)(2,1)S(1)}, bf16[1024,256]{1,0:T(8,128)(2,1)}, u32[]{:S(2)}) copy-start(bf16[1024,256]{1,0:T(8,128)(2,1)} %refs_6_.1) | copy-start | bytes 1572868
  48.9 25.1 %copy-start.26 = (bf16[1024,256]{1,0:T(8,128)(2,1)S(1)}, bf16[1024,256]{1,0:T(8,128)(2,1)}, u32[]{:S(2)}) copy-start(bf16[1024,256]{1,0:T(8,128)(2,1)} %cot.3) | copy-start | bytes 1572868
  48.9 25.1 %copy-start.27 = (bf16[512,256]{1,0:T(8,128)(2,1)S(1)}, bf16[512,256]{1,0:T(8,128)(2,1)}, u32[]{:S(2)}) copy-start(bf16[512,256]{1,0:T(8,128)(2,1)} %w_in.1) | copy-start | bytes 786436
  49.0 25.1 %copy-start.32 = (bf16[256,256]{1,0:T(8,128)(2,1)S(1)}, bf16[256,256]{1,0:T(8,128)(2,1)}, u32[]{:S(2)}) copy-start(bf16[256,256]{1,0:T(8,128)(2,1)} %refs_5_.1) | copy-start | bytes 393220
  49.0 25.1 %copy-start.35 = (f32[256]{0:T(256)S(1)}, f32[256]{0:T(256)}, u32[]{:S(2)}) copy-start(f32[256]{0:T(256)} %param.15) | copy-start | bytes 3076
  49.0 25.1 %copy-start.36 = (f32[256]{0:T(256)S(1)}, f32[256]{0:T(256)}, u32[]{:S(2)}) copy-start(f32[256]{0:T(256)} %param.17) | copy-start | bytes 3076
  49.0 25.1 %copy-start.37 = (f32[256]{0:T(256)S(1)}, f32[256]{0:T(256)}, u32[]{:S(2)}) copy-start(f32[256]{0:T(256)} %param.18) | copy-start | bytes 3076
  49.0 9.4 %collective-permute-start.14 = (bf16[1024,256]{1,0:T(8,128)(2,1)S(1)}, bf16[1024,256]{1,0:T(8,128)(2,1)S(1)}, u32[]{:S(2)}, u32[]{:S(2)}) collective-permute-start(bf16[1024,256]{1,0:T(8,128)(2,1)S(1)} %sum_terms.9), channel_id=1, source_target_pairs={{0,4},{1,2},{2,1},{3,7},{4,0},{5,6},{6,5},{7,3},{8,12},{9,10},{10,... | collective-permute-start | bytes 1572872 | tf_op jit(solution)/shard_map/ppermute | solution.py:547
  58.3 7.1 %collective-permute-start.17 = (bf16[1024,256]{1,0:T(8,128)(2,1)S(1)}, bf16[1024,256]{1,0:T(8,128)(2,1)S(1)}, u32[]{:S(2)}, u32[]{:S(2)}) collective-permute-start(bf16[1024,256]{1,0:T(8,128)(2,1)S(1)} %sum_terms.11), channel_id=1, source_target_pairs={{0,4},{1,2},{2,1},{3,7},{4,0},{5,6},{6,5},{7,3},{8,12},{9,10},{10,... | collective-permute-start | bytes 1572872 | tf_op jit(solution)/shard_map/ppermute | solution.py:547
  59.6 14.4 %collective-permute-start.15 = (bf16[1024,256]{1,0:T(8,128)(2,1)S(1)}, bf16[1024,256]{1,0:T(8,128)(2,1)S(1)}, u32[]{:S(2)}, u32[]{:S(2)}) collective-permute-start(bf16[1024,256]{1,0:T(8,128)(2,1)S(1)} %sum_terms.10), channel_id=1, source_target_pairs={{0,1},{1,0},{2,3},{3,2},{4,5},{5,4},{6,7},{7,6},{8,9},{9,8},{10,11... | collective-permute-start | bytes 1572872 | tf_op jit(solution)/shard_map/ppermute | solution.py:534
  75.1 36.7 %copy-start.3 = (bf16[1024,256]{1,0:T(8,128)(2,1)S(1)}, bf16[1024,256]{1,0:T(8,128)(2,1)}, u32[]{:S(2)}) copy-start(bf16[1024,256]{1,0:T(8,128)(2,1)} %copy-done.2) | copy-start | bytes 1572868
  75.1 36.7 %copy-start.5 = (bf16[512,256]{1,0:T(8,128)(2,1)S(1)}, bf16[512,256]{1,0:T(8,128)(2,1)}, u32[]{:S(2)}) copy-start(bf16[512,256]{1,0:T(8,128)(2,1)} %copy-done.4) | copy-start | bytes 786436
  75.1 36.7 %copy-start.7 = (bf16[512,256]{1,0:T(8,128)(2,1)S(1)}, bf16[512,256]{1,0:T(8,128)(2,1)}, u32[]{:S(2)}) copy-start(bf16[512,256]{1,0:T(8,128)(2,1)} %copy-done.6) | copy-start | bytes 786436
  75.1 36.7 %copy-start.9 = (bf16[512,256]{1,0:T(8,128)(2,1)S(1)}, bf16[512,256]{1,0:T(8,128)(2,1)}, u32[]{:S(2)}) copy-start(bf16[512,256]{1,0:T(8,128)(2,1)} %copy-done.8) | copy-start | bytes 786436
  75.1 36.7 %copy-start.11 = (bf16[512,256]{1,0:T(8,128)(2,1)S(1)}, bf16[512,256]{1,0:T(8,128)(2,1)}, u32[]{:S(2)}) copy-start(bf16[512,256]{1,0:T(8,128)(2,1)} %copy-done.10) | copy-start | bytes 786436
  75.1 36.7 %copy-start.13 = (bf16[512,256]{1,0:T(8,128)(2,1)S(1)}, bf16[512,256]{1,0:T(8,128)(2,1)}, u32[]{:S(2)}) copy-start(bf16[512,256]{1,0:T(8,128)(2,1)} %copy-done.12) | copy-start | bytes 786436
  75.1 36.7 %copy-start.15 = (bf16[512,256]{1,0:T(8,128)(2,1)S(1)}, bf16[512,256]{1,0:T(8,128)(2,1)}, u32[]{:S(2)}) copy-start(bf16[512,256]{1,0:T(8,128)(2,1)} %copy-done.14) | copy-start | bytes 786436
  75.2 36.7 %copy-start.17 = (bf16[512,256]{1,0:T(8,128)(2,1)S(1)}, bf16[512,256]{1,0:T(8,128)(2,1)}, u32[]{:S(2)}) copy-start(bf16[512,256]{1,0:T(8,128)(2,1)} %copy-done.16) | copy-start | bytes 786436
  75.2 36.7 %copy-start.19 = (bf16[512,256]{1,0:T(8,128)(2,1)S(1)}, bf16[512,256]{1,0:T(8,128)(2,1)}, u32[]{:S(2)}) copy-start(bf16[512,256]{1,0:T(8,128)(2,1)} %copy-done.18) | copy-start | bytes 786436
  75.2 36.7 %copy-start.21 = (bf16[512,256]{1,0:T(8,128)(2,1)S(1)}, bf16[512,256]{1,0:T(8,128)(2,1)}, u32[]{:S(2)}) copy-start(bf16[512,256]{1,0:T(8,128)(2,1)} %copy-done.20) | copy-start | bytes 786436
  75.2 36.7 %copy-start.23 = (bf16[512,256]{1,0:T(8,128)(2,1)S(1)}, bf16[512,256]{1,0:T(8,128)(2,1)}, u32[]{:S(2)}) copy-start(bf16[512,256]{1,0:T(8,128)(2,1)} %copy-done.22) | copy-start | bytes 786436
  75.2 36.7 %copy-start.25 = (bf16[512,256]{1,0:T(8,128)(2,1)S(1)}, bf16[512,256]{1,0:T(8,128)(2,1)}, u32[]{:S(2)}) copy-start(bf16[512,256]{1,0:T(8,128)(2,1)} %copy-done.24) | copy-start | bytes 786436
  75.2 36.7 %copy-start.33 = (s32[32,1,4]{0,2,1:T(4,128)S(1)}, s32[32,1,4]{0,2,1:T(4,128)}, u32[]{:S(2)}) copy-start(s32[32,1,4]{0,2,1:T(4,128)} %param.12) | copy-start | bytes 1540
  75.2 36.7 %copy-start.34 = (s32[32,1]{0,1:T(1,128)S(1)}, s32[32,1]{0,1:T(1,128)}, u32[]{:S(2)}) copy-start(s32[32,1]{0,1:T(1,128)} %param.13) | copy-start | bytes 388
  79.9 11.3 %collective-permute-start.18 = (bf16[1024,256]{1,0:T(8,128)(2,1)S(1)}, bf16[1024,256]{1,0:T(8,128)(2,1)S(1)}, u32[]{:S(2)}, u32[]{:S(2)}) collective-permute-start(bf16[1024,256]{1,0:T(8,128)(2,1)S(1)} %get-tuple-element.39.refs_0_), channel_id=1, source_target_pairs={{0,1},{1,0},{2,3},{3,2},{4,5},{5,4},{6,7},{7,6},{8,9},{9,8},{10,11... | collective-permute-start | bytes 1572872 | tf_op jit(solution)/shard_map/ppermute | solution.py:534
  83.2 8.1 %collective-permute-start.23 = (f32[448,256]{1,0:T(8,128)S(1)}, f32[448,256]{1,0:T(8,128)S(1)}, u32[]{:S(2)}, u32[]{:S(2)}) collective-permute-start(f32[448,256]{1,0:T(8,128)S(1)} %get-tuple-element.42), channel_id=1, source_target_pairs={{0,4},{4,0},{8,12},{12,8},{16,20},{20,16},{24,28},{28,24},{1,5},{5... | collective-permute-start | bytes 1376264 | tf_op jit(solution)/shard_map/ppermute | solution.py:530
  83.3 9.7 %collective-permute-start.19 = (bf16[1024,256]{1,0:T(8,128)(2,1)S(1)}, bf16[1024,256]{1,0:T(8,128)(2,1)S(1)}, u32[]{:S(2)}, u32[]{:S(2)}) collective-permute-start(bf16[1024,256]{1,0:T(8,128)(2,1)S(1)} %get-tuple-element.39.refs_0_), channel_id=1, source_target_pairs={{0,4},{1,2},{2,1},{3,7},{4,0},{5,6},{6,5},{7,3},{8,12},{9,10},{10,... | collective-permute-start | bytes 1572872 | tf_op jit(solution)/shard_map/ppermute | solution.py:547
  91.3 7.9 %collective-permute-start.21 = (bf16[1024,256]{1,0:T(8,128)(2,1)S(1)}, bf16[1024,256]{1,0:T(8,128)(2,1)S(1)}, u32[]{:S(2)}, u32[]{:S(2)}) collective-permute-start(bf16[1024,256]{1,0:T(8,128)(2,1)S(1)} %collective-permute-done.18.refs_1_), channel_id=1, source_target_pairs={{0,4},{1,2},{2,1},{3,7},{4,0},{5,6},{6,5},{7,3},{8,12},{9,10},{10,... | collective-permute-start | bytes 1572872 | tf_op jit(solution)/shard_map/ppermute | solution.py:547
  91.4 35.4 %copy-start = (bf16[32,1,4,128,128]{4,3,2,1,0:T(8,128)(2,1)S(1)}, bf16[32,1,4,128,128]{4,3,2,1,0:T(8,128)(2,1)}, u32[]{:S(2)}) copy-start(bf16[32,1,4,128,128]{4,3,2,1,0:T(8,128)(2,1)} %param.11) | copy-start | bytes 12582916
  91.4 18.7 %collective-permute-start.24 = (f32[224,256]{1,0:T(8,128)S(1)}, f32[224,256]{1,0:T(8,128)S(1)}, u32[]{:S(2)}, u32[]{:S(2)}) collective-permute-start(f32[224,256]{1,0:T(8,128)S(1)} %slice.25), channel_id=1, source_target_pairs={{0,8},{4,12},{8,0},{12,4},{16,24},{20,28},{24,16},{28,20},{1,9},{5... | collective-permute-start | bytes 688136 | tf_op jit(solution)/shard_map/ppermute | solution.py:530
  92.9 18.9 %collective-permute-start.20 = (bf16[1024,256]{1,0:T(8,128)(2,1)S(1)}, bf16[1024,256]{1,0:T(8,128)(2,1)S(1)}, u32[]{:S(2)}, u32[]{:S(2)}) collective-permute-start(bf16[1024,256]{1,0:T(8,128)(2,1)S(1)} %collective-permute-done.19.refs_2_), channel_id=1, source_target_pairs={{0,1},{1,0},{2,3},{3,2},{4,5},{5,4},{6,7},{7,6},{8,9},{9,8},{10,11... | collective-permute-start | bytes 1572872 | tf_op jit(solution)/shard_map/ppermute | solution.py:534
  99.2 27.6 %collective-permute-start.22 = (bf16[1024,256]{1,0:T(8,128)(2,1)S(1)}, bf16[1024,256]{1,0:T(8,128)(2,1)S(1)}, u32[]{:S(2)}, u32[]{:S(2)}) collective-permute-start(bf16[1024,256]{1,0:T(8,128)(2,1)S(1)} %collective-permute-done.21.refs_17_.refs_4_), channel_id=1, source_target_pairs={{0,1},{1,0},{2,3},{3,2},{4,5},{5,4},{6,7},{7,6},{8,9},{9,8},{10,11... | collective-permute-start | bytes 1572872 | tf_op jit(solution)/shard_map/ppermute | solution.py:534
  110.2 7.6 %collective-permute-start.25 = (f32[112,256]{1,0:T(8,128)S(1)}, f32[112,256]{1,0:T(8,128)S(1)}, u32[]{:S(2)}, u32[]{:S(2)}) collective-permute-start(f32[112,256]{1,0:T(8,128)S(1)} %get-tuple-element.58), channel_id=1, source_target_pairs={{0,16},{4,20},{8,24},{12,28},{16,0},{20,4},{24,8},{28,12},{1,17},{... | collective-permute-start | bytes 344072 | tf_op jit(solution)/shard_map/ppermute | solution.py:530
  117.8 8.9 %collective-permute-start.26 = (bf16[112,256]{1,0:T(8,128)(2,1)S(1)}, bf16[112,256]{1,0:T(8,128)(2,1)S(1)}, u32[]{:S(2)}, u32[]{:S(2)}) collective-permute-start(bf16[112,256]{1,0:T(8,128)(2,1)S(1)} %sum_terms.12.refs_1_), channel_id=1, source_target_pairs={{0,1},{1,2},{2,3},{3,0},{4,5},{5,6},{6,7},{7,4},{8,9},{9,10},{10,1... | collective-permute-start | bytes 172040 | tf_op jit(solution)/shard_map/ppermute | solution.py:538
  118.4 8.3 %collective-permute-start.27 = (bf16[112,256]{1,0:T(8,128)(2,1)S(1)}, bf16[112,256]{1,0:T(8,128)(2,1)S(1)}, u32[]{:S(2)}, u32[]{:S(2)}) collective-permute-start(bf16[112,256]{1,0:T(8,128)(2,1)S(1)} %sum_terms.12.refs_1_), channel_id=1, source_target_pairs={{0,2},{1,3},{2,0},{3,1},{4,6},{5,7},{6,4},{7,5},{8,10},{9,11},{10,... | collective-permute-start | bytes 172040 | tf_op jit(solution)/shard_map/ppermute | solution.py:538
  120.7 6.0 %collective-permute-start.28 = (bf16[112,256]{1,0:T(8,128)(2,1)S(1)}, bf16[112,256]{1,0:T(8,128)(2,1)S(1)}, u32[]{:S(2)}, u32[]{:S(2)}) collective-permute-start(bf16[112,256]{1,0:T(8,128)(2,1)S(1)} %sum_terms.12.refs_1_), channel_id=1, source_target_pairs={{0,3},{1,0},{2,1},{3,2},{4,7},{5,4},{6,5},{7,6},{8,11},{9,8},{10,9... | collective-permute-start | bytes 172040 | tf_op jit(solution)/shard_map/ppermute | solution.py:538
  135.3 6.2 %collective-permute-start.29 = (bf16[4096,256]{1,0:T(8,128)(2,1)S(1)}, bf16[4096,256]{1,0:T(8,128)(2,1)S(1)}, u32[]{:S(2)}, u32[]{:S(2)}) collective-permute-start(bf16[4096,256]{1,0:T(8,128)(2,1)S(1)} %get-tuple-element.44), channel_id=1, source_target_pairs={{0,4},{4,0},{8,12},{12,8},{16,20},{20,16},{24,28},{28,24},{1,5},{5... | collective-permute-start | bytes 6291464 | tf_op jit(solution)/shard_map/ppermute | solution.py:530
  135.4 5.7 %collective-permute-start.32 = (bf16[112,256]{1,0:T(8,128)(2,1)S(1)}, bf16[112,256]{1,0:T(8,128)(2,1)S(1)}, u32[]{:S(2)}, u32[]{:S(2)}) collective-permute-start(bf16[112,256]{1,0:T(8,128)(2,1)S(1)} %sum_terms.13.refs_8_), channel_id=1, source_target_pairs={{0,24},{4,28},{8,16},{12,20},{16,8},{20,12},{24,0},{28,4},{1,25},{... | collective-permute-start | bytes 172040 | tf_op jit(solution)/shard_map/ppermute | solution.py:530
  136.2 5.2 %collective-permute-start.31 = (bf16[112,256]{1,0:T(8,128)(2,1)S(1)}, bf16[112,256]{1,0:T(8,128)(2,1)S(1)}, u32[]{:S(2)}, u32[]{:S(2)}) collective-permute-start(bf16[112,256]{1,0:T(8,128)(2,1)S(1)} %sum_terms.13.refs_8_), channel_id=1, source_target_pairs={{0,16},{4,20},{8,24},{12,28},{16,0},{20,4},{24,8},{28,12},{1,17},{... | collective-permute-start | bytes 172040 | tf_op jit(solution)/shard_map/ppermute | solution.py:530
  136.9 4.6 %collective-permute-start.30 = (bf16[112,256]{1,0:T(8,128)(2,1)S(1)}, bf16[112,256]{1,0:T(8,128)(2,1)S(1)}, u32[]{:S(2)}, u32[]{:S(2)}) collective-permute-start(bf16[112,256]{1,0:T(8,128)(2,1)S(1)} %sum_terms.13.refs_8_), channel_id=1, source_target_pairs={{0,8},{4,12},{8,0},{12,4},{16,24},{20,28},{24,16},{28,20},{1,9},{5... | collective-permute-start | bytes 172040 | tf_op jit(solution)/shard_map/ppermute | solution.py:530
  141.7 14.9 %collective-permute-start.33 = (bf16[1024,256]{1,0:T(8,128)(2,1)S(1)}, bf16[1024,256]{1,0:T(8,128)(2,1)S(1)}, u32[]{:S(2)}, u32[]{:S(2)}) collective-permute-start(bf16[1024,256]{1,0:T(8,128)(2,1)S(1)} %sum_terms.14.refs_21_), channel_id=1, source_target_pairs={{0,8},{4,12},{8,0},{12,4},{16,24},{20,28},{24,16},{28,20},{1,9},{5... | collective-permute-start | bytes 1572872 | tf_op jit(solution)/shard_map/ppermute | solution.py:530
  143.6 23.7 %collective-permute-start.34 = (bf16[1024,256]{1,0:T(8,128)(2,1)S(1)}, bf16[1024,256]{1,0:T(8,128)(2,1)S(1)}, u32[]{:S(2)}, u32[]{:S(2)}) collective-permute-start(bf16[1024,256]{1,0:T(8,128)(2,1)S(1)} %sum_terms.15.refs_22_), channel_id=1, source_target_pairs={{0,16},{4,20},{8,24},{12,28},{16,0},{20,4},{24,8},{28,12},{1,17},{... | collective-permute-start | bytes 1572872 | tf_op jit(solution)/shard_map/ppermute | solution.py:530
  143.9 23.3 %collective-permute-start.35 = (bf16[1024,256]{1,0:T(8,128)(2,1)S(1)}, bf16[1024,256]{1,0:T(8,128)(2,1)S(1)}, u32[]{:S(2)}, u32[]{:S(2)}) collective-permute-start(bf16[1024,256]{1,0:T(8,128)(2,1)S(1)} %sum_terms.16.refs_23_), channel_id=1, source_target_pairs={{0,24},{4,28},{8,16},{12,20},{16,8},{20,12},{24,0},{28,4},{1,25},{... | collective-permute-start | bytes 1572872 | tf_op jit(solution)/shard_map/ppermute | solution.py:530
  145.7 1.5 collective-permute-start.36
  (11 other events, 30.7 us)

commit v10 on v9

--- a/solution.py
+++ b/solution.py
@@ -559,9 +559,15 @@
     return pieces
 
 
-def reduce_square(here, even, other, rows, after):
-    sums = [sum_call(here, rows, [(even, piece), (other, piece)], after=after) for piece in (1, 2, 3)]
-    return [swap(value, bits) for value, bits in zip(sums, (2, 4, 6))], sums
+def reduce_square(here, even, other, rows):
+    half = rows // 2
+    first = [
+        sum_call(here, rows, [(even, places), (other, places)]) for places in ((6, 2), (7, 5))
+    ]
+    x_first, y_first = swap(first[0], 2), swap(first[1], 4)
+    y_lower = swap(sum_call(here, half, [(even, 4), (other, 4), (x_first, 0)]), 4)
+    x_upper = swap(sum_call(here, half, [(even, 3), (other, 3), (y_first, 0)]), 2)
+    return [((x_first, 1), (x_upper, 0)), ((y_lower, 0), (y_first, 1))], first
 
 
 def sum_kernel(n_terms, n_gated, n_split, *refs):
@@ -584,23 +590,35 @@
     width = both[0][0].shape[1]
     step = min(rows, 256)
     steps = rows // step
+    half = steps // 2
+
+    def spec(piece):
+        if isinstance(piece, int):
+            return pl.BlockSpec((step, width), lambda i: (piece * steps + i, 0))
+        lower, upper = piece
+        return pl.BlockSpec(
+            (step, width), lambda i: (jnp.where(i < half, lower * half + i, (upper - 1) * half + i), 0)
+        )
+
+    def early(piece):
+        return pl.BlockSpec((step, width), lambda i: (piece * half + jnp.minimum(i, half - 1), 0))
+
+    def late(piece):
+        return pl.BlockSpec((step, width), lambda i: (piece * half + jnp.maximum(i - half, 0), 0))
+
     return pl.pallas_call(
         functools.partial(sum_kernel, len(terms), len(gated), len(split)),
         grid=(steps,),
         out_shape=jax.ShapeDtypeStruct((rows, width), dtype),
         in_specs=[SMEM]
-        + [pl.BlockSpec((step, width), lambda i, piece=piece: (piece * steps + i, 0)) for _, piece in both]
-        + [
-            pl.BlockSpec((step, width), lambda i: (jnp.minimum(i, steps // 2 - 1), 0)),
-            pl.BlockSpec((step, width), lambda i: (jnp.maximum(i - steps // 2, 0), 0)),
-        ]
-        * len(split)
+        + [spec(piece) for _, piece in both]
+        + [spec_of(piece) for pair in split for spec_of, (_, piece) in zip((early, late), pair)]
         + [ANY] * len(after),
         out_specs=pl.BlockSpec((step, width), lambda i: (i, 0)),
         compiler_params=params(8),
         cost_estimate=SMALL,
         name="sum_terms",
-    )(here, *(array for array, _ in both), *(half for pair in split for half in pair), *after)
+    )(here, *(array for array, _ in both), *(array for pair in split for array, _ in pair), *after)
 
 
 def scatter_weights(kept, sent):
@@ -611,10 +629,9 @@
     return kept, swap(sent, 4)
 
 
-def level_weights(here, kept, received, after):
-    rows = kept.shape[0]
-    value = sum_call(here, rows, [(kept, 0), (received, 0)], dtype=BF16, after=after)
-    return sum_call(here, rows, [(term, 0) for term in (value, *(turn(value, by) for by in (1, 2, 3)))])
+def level_weights(here, value, after):
+    terms = [value] + [turn(value, by) for by in (1, 2, 3)]
+    return sum_call(here, value.shape[0], [(term, 0) for term in terms], after=after)
 
 
 def reduce_line(here, far, near, pair, own):
@@ -646,7 +663,8 @@
     known = (paired, here, cols, counts)
     if paired:
         pieces = [gather_square(nodes)]
-        far, near = forward_call(*known, pieces[0], tile_local, ((0,), (1,)), rows)
+        (far,) = forward_call(*known, pieces[0], tile_local, ((0,),), rows)
+        (near,) = forward_call(*known, pieces[0], tile_local, ((1,),), rows)
         pair, own = forward_call(*known, pieces[0], tile_local, ((2,), (3,)), rows)
         parts = [reduce_line(here, far, near, pair, own)]
         kinds = [("all", "all", "inner")]
@@ -669,18 +687,17 @@
         near_grads, token = tile_grad_call(
             *known, [grads[0][:2]], pieces, tile_local.shape, rows, (3, 2), after=(grads[0][3], grads[0][4])
         )
-        all_weights = level_weights(here, *row_weights, (token,))
-        odd, even = back_call(*known, grads[0], tile_local, total, gathered, halves, (token, all_weights))
+        row_weights = sum_call(here, kept.shape[0] // 4, [(term, 0) for term in row_weights], after=(token,))
+        odd, even = back_call(*known, grads[0], tile_local, total, gathered, halves, (row_weights,))
         other = swap(odd, 1)
+        arrived, first = reduce_square(here, even, other, rows)
+        all_weights = level_weights(here, row_weights, first)
         joint = jnp.concatenate([all_weights] + [swap(all_weights, bits) for bits in (2, 4, 6)], axis=0)
-        arrived, sums = reduce_square(here, even, other, rows, (joint,))
         weights = unpack_call(here, joint, swap(joint, 1), width)
         grad_tiles, _ = tile_grad_call(
-            *known, grads, pieces, tile_local.shape, rows, (1, 0), near_grads, sums
-        )
-        grad_nodes = sum_call(
-            here, rows, [(direct, 0), (even, 0), (other, 0)] + [(term, 0) for term in arrived]
-        )
+            *known, grads, pieces, tile_local.shape, rows, (1, 0), near_grads, first
+        )
+        grad_nodes = sum_call(here, rows, [(direct, 0), (even, 0), (other, 0)], split=arrived)
     else:
         grads = [[lax.all_gather(gmsgs[0], "col", axis=0, tiled=True)]]
         weight_terms, direct = weight_call(factor, 1, *weight_args)

time: 169 us -> 161 us (0.953)
  waiting for transfers between devices: 71.7 us -> 64.8 us
    ppermute x24 -> x25, waiting for transfers between devices: 34.1 us -> 25.1 us  [swap(): return lax.ppermute(value, 'row', [(i, i ^ bit) for i in range(8)])]
    pallas_call x2 -> x3, Pallas kernels: 10.9 us -> 15 us  [forward_call(): pl.pallas_call(functools.partial(forward_kernel, outputs, len(pieces), pa...]
    ppermute x6, waiting for transfers between devices: 32.6 us -> 36.3 us  [outer_swap(): return lax.ppermute(value, 'col', [(0, 1), (1, 0), (2, 3), (3, 2)])]
    ppermute x6, starting transfers between devices: 26.8 us -> 24.1 us  [outer_swap(): return lax.ppermute(value, 'col', [(0, 1), (1, 0), (2, 3), (3, 2)])]
    pallas_call x1, Pallas kernels: 8.54 us -> 6.81 us  [back_call(): pl.pallas_call(functools.partial(back_kernel, rows, slots, len(grads), le...]
    ppermute x24 -> x25, starting transfers between devices: 18.3 us -> 19.7 us  [swap(): return lax.ppermute(value, 'row', [(i, i ^ bit) for i in range(8)])]
  transfers between devices with their start and end apart: 37 -> 38, of which waited for: 16 -> 18; matrix products, arithmetic and copies ran while one was open for 1% -> 1% of each run, Pallas kernels for 13% -> 16%
where the time goes in v10:
time: 161 us; the launch traced here: 162 us
  waiting for transfers between devices  64.8 us (40%)
  starting transfers between devices  49.2 us (31%)
  Pallas kernels  43.2 us (27%)
  local copies, waits for them, and re-layouts  3.34 us (2%)
    ppermute x6, waiting for transfers between devices, outer_swap(): return lax.ppermute(value, 'col', [(0, 1), (1, 0), (2, 3), (3, 2)])  36.3 us
    ppermute x25, waiting for transfers between devices, swap(): return lax.ppermute(value, 'row', [(i, i ^ bit) for i in range(8)])  25.1 us
    ppermute x6, starting transfers between devices, outer_swap(): return lax.ppermute(value, 'col', [(0, 1), (1, 0), (2, 3), (3, 2)])  24.1 us
    ppermute x25, starting transfers between devices, swap(): return lax.ppermute(value, 'row', [(i, i ^ bit) for i in range(8)])  19.7 us
    pallas_call x3, Pallas kernels, forward_call(): pl.pallas_call(functools.partial(forward_kernel, outputs, len(pieces), pa...  15 us
    pallas_call x2, Pallas kernels, tile_grad_call(): pl.pallas_call(functools.partial(tile_grad_kernel, rows, slots, len(grads...  11.3 us
    pallas_call x1, Pallas kernels, back_call(): pl.pallas_call(functools.partial(back_kernel, rows, slots, len(grads), le...  6.81 us
    ppermute x3, starting transfers between devices, turn(): return lax.ppermute(value, 'col', [(i, (i + by) % 4) for i in range(4)])  4.73 us
  transfers between devices with their start and end apart: 38, of which 18 were waited for; matrix products, arithmetic and copies ran while one was open for 1% of the time, Pallas kernels for 16%

profile of v10, /device:TPU:0, one launch (start us, length us, event | category | flops | bytes accessed | tf_op | source)
XLA Modules:
  0.0 162.0 jit_solution(9904826127834277280)
XLA Ops:
  0.6 0.5 collective-permute-start
  1.1 1.1 fusion
  2.2 2.6 %collective-permute-start.1 = (bf16[512,256]{1,0:T(8,128)(2,1)S(1)}, bf16[512,256]{1,0:T(8,128)(2,1)S(1)}, u32[]{:S(2)}, u32[]{:S(2)}) collective-permute-start(bf16[512,256]{1,0:T(8,128)(2,1)S(1)} %get-tuple-element.53), channel_id=1, source_target_pairs={{0,8},{4,12},{8,0},{12,4},{16,24},{20,28},{24,16},{28,20},{1,9},{5... | collective-permute-start | bytes 786440 | tf_op jit(solution)/shard_map/ppermute | solution.py:530
  4.8 1.5 collective-permute-start.5
  6.3 0.5 collective-permute-start.2
  6.9 5.0 %collective-permute-done.1.refs_2_.refs_4_.refs_8_ = bf16[512,256]{1,0:T(8,128)(2,1)S(1)} collective-permute-done((bf16[512,256]{1,0:T(8,128)(2,1)S(1)}, bf16[512,256]{1,0:T(8,128)(2,1)S(1)}, u32[]{:S(2)}, u32[]{:S(2)}) %collective-permute-start.1) | collective-permute-done | bytes 262176 | tf_op jit(solution)/shard_map/ppermute | solution.py:530
  11.9 2.0 %collective-permute-done.5.refs_6_.refs_8_.refs_12_ = bf16[512,256]{1,0:T(8,128)(2,1)S(1)} collective-permute-done((bf16[512,256]{1,0:T(8,128)(2,1)S(1)}, bf16[512,256]{1,0:T(8,128)(2,1)S(1)}, u32[]{:S(2)}, u32[]{:S(2)}) %collective-permute-start.5) | collective-permute-done | bytes 262176 | tf_op jit(solution)/shard_map/ppermute | solution.py:530
  14.0 3.6 %collective-permute-done.2.refs_3_.refs_5_.refs_9_ = bf16[512,256]{1,0:T(8,128)(2,1)S(1)} collective-permute-done((bf16[512,256]{1,0:T(8,128)(2,1)S(1)}, bf16[512,256]{1,0:T(8,128)(2,1)S(1)}, u32[]{:S(2)}, u32[]{:S(2)}) %collective-permute-start.2) | collective-permute-done | bytes 262176 | tf_op jit(solution)/shard_map/ppermute | solution.py:530
  17.6 2.0 %collective-permute-start.10 = (bf16[512,256]{1,0:T(8,128)(2,1)S(1)}, bf16[512,256]{1,0:T(8,128)(2,1)S(1)}, u32[]{:S(2)}, u32[]{:S(2)}) collective-permute-start(bf16[512,256]{1,0:T(8,128)(2,1)S(1)} %collective-permute-done.2.refs_3_.refs_5_.refs_9_), channel_id=1, source_target_pairs={{0,16},{4,20},{8,24},{12,28},{16,0},{20,4},{24,8},{28,12},{1,17},{... | collective-permute-start | bytes 786440 | tf_op jit(solution)/shard_map/ppermute | solution.py:530
  19.6 0.5 collective-permute-start.7
  20.1 0.1 collective-permute-start.8
  20.2 2.8 %collective-permute-done.9.refs_10_.refs_12_.refs_16_ = bf16[512,256]{1,0:T(8,128)(2,1)S(1)} collective-permute-done((bf16[512,256]{1,0:T(8,128)(2,1)S(1)}, bf16[512,256]{1,0:T(8,128)(2,1)S(1)}, u32[]{:S(2)}, u32[]{:S(2)}) %collective-permute-start.9) | collective-permute-done | bytes 262176 | tf_op jit(solution)/shard_map/ppermute | solution.py:530
  23.0 2.5 %collective-permute-done.10.refs_11_.refs_13_.refs_17_ = bf16[512,256]{1,0:T(8,128)(2,1)S(1)} collective-permute-done((bf16[512,256]{1,0:T(8,128)(2,1)S(1)}, bf16[512,256]{1,0:T(8,128)(2,1)S(1)}, u32[]{:S(2)}, u32[]{:S(2)}) %collective-permute-start.10) | collective-permute-done | bytes 262176 | tf_op jit(solution)/shard_map/ppermute | solution.py:530
  25.6 1.6 collective-permute-done.12.refs_13_.refs_15_.refs_19_
  27.3 4.8 %partial_messages.4.refs_1_ = bf16[1024,256]{1,0:T(8,128)(2,1)} custom-call(s32[1]{0:T(128)} %bitcast.here.refs_0_, s32[4,32]{1,0:T(4,128)} %bitcast.17, s32[32]{0:T(128)} %bitcast.23, bf16[1024,256]{1,0:T(8,128)(2,1)} %refs_6_.1, bf16[1024,256]{1,0:T(8,128)(2,1)} %copy-done.2, bf16[512,256]{1,0:T(8,128)(2,1)} %copy-done.4, bf16[512,256]{1,0:T(8,128)(2,1)} %copy-done.8, ...), custom_call_target="tpu_custom_call" | custom-call | flops 1048576 | bytes 65536 | tf_op jit(solution)/shard_map/partial_messages/pallas_call | solution.py:132
  32.0 1.7 %collective-permute-start.13 = (bf16[1024,256]{1,0:T(8,128)(2,1)}, bf16[1024,256]{1,0:T(8,128)(2,1)S(1)}, u32[]{:S(2)}, u32[]{:S(2)}) collective-permute-start(bf16[1024,256]{1,0:T(8,128)(2,1)} %partial_messages.4.refs_1_), channel_id=1, source_target_pairs={{0,1},{1,0},{2,3},{3,2},{4,5},{5,4},{6,7},{7,6},{8,9},{9,8},{10,11... | collective-permute-start | bytes 1572872 | tf_op jit(solution)/shard_map/ppermute | solution.py:534
  33.7 4.7 %partial_messages.5.refs_1_ = bf16[1024,256]{1,0:T(8,128)(2,1)} custom-call(s32[1]{0:T(128)} %bitcast.here.refs_0_, s32[4,32]{1,0:T(4,128)} %bitcast.18, s32[32]{0:T(128)} %bitcast.24, bf16[1024,256]{1,0:T(8,128)(2,1)} %refs_6_.1, bf16[1024,256]{1,0:T(8,128)(2,1)} %copy-done.2, bf16[512,256]{1,0:T(8,128)(2,1)} %copy-done.4, bf16[512,256]{1,0:T(8,128)(2,1)} %copy-done.8, ...), custom_call_target="tpu_custom_call" | custom-call | flops 1048576 | bytes 65536 | tf_op jit(solution)/shard_map/partial_messages/pallas_call | solution.py:132
  38.5 0.5 collective-permute-start.16
  39.0 8.1 %collective-permute-done.13.refs_2_ = bf16[1024,256]{1,0:T(8,128)(2,1)S(1)} collective-permute-done((bf16[1024,256]{1,0:T(8,128)(2,1)}, bf16[1024,256]{1,0:T(8,128)(2,1)S(1)}, u32[]{:S(2)}, u32[]{:S(2)}) %collective-permute-start.13) | collective-permute-done | bytes 524320 | tf_op jit(solution)/shard_map/ppermute | solution.py:534
  47.1 0.2 sum_terms.10
  47.4 0.1 collective-permute-start.14
  47.4 5.5 %partial_messages.3 = (bf16[1024,256]{1,0:T(8,128)(2,1)}, bf16[1024,256]{1,0:T(8,128)(2,1)}) custom-call(s32[1]{0:T(128)} %bitcast.here.refs_0_, s32[4,32]{1,0:T(4,128)} %bitcast.19, s32[32]{0:T(128)} %bitcast.25, bf16[1024,256]{1,0:T(8,128)(2,1)} %refs_6_.1, bf16[1024,256]{1,0:T(8,128)(2,1)} %copy-done.2, bf16[512,256]{1,0:T(8,128)(2,1)} %copy-done.4, ...), custom_call_target="tpu_custom_call" | custom-call | flops 1048576 | bytes 65536 | tf_op jit(solution)/shard_map/partial_messages/pallas_call | solution.py:132
  53.0 4.5 %collective-permute-done.16.refs_2_ = bf16[1024,256]{1,0:T(8,128)(2,1)S(1)} collective-permute-done((bf16[1024,256]{1,0:T(8,128)(2,1)}, bf16[1024,256]{1,0:T(8,128)(2,1)S(1)}, u32[]{:S(2)}, u32[]{:S(2)}) %collective-permute-start.16) | collective-permute-done | bytes 524320 | tf_op jit(solution)/shard_map/ppermute | solution.py:534
  57.5 0.2 sum_terms.12
  57.8 1.0 copy-done.30
  58.8 0.2 sum_terms.11
  59.1 3.7 %collective-permute-start.15 = (bf16[1024,256]{1,0:T(8,128)(2,1)S(1)}, bf16[1024,256]{1,0:T(8,128)(2,1)S(1)}, u32[]{:S(2)}, u32[]{:S(2)}) collective-permute-start(bf16[1024,256]{1,0:T(8,128)(2,1)S(1)} %sum_terms.11), channel_id=1, source_target_pairs={{0,1},{1,0},{2,3},{3,2},{4,5},{5,4},{6,7},{7,6},{8,9},{9,8},{10,11... | collective-permute-start | bytes 1572872 | tf_op jit(solution)/shard_map/ppermute | solution.py:534
  62.7 10.7 %collective-permute-done.15.refs_1_ = bf16[1024,256]{1,0:T(8,128)(2,1)S(1)} collective-permute-done((bf16[1024,256]{1,0:T(8,128)(2,1)S(1)}, bf16[1024,256]{1,0:T(8,128)(2,1)S(1)}, u32[]{:S(2)}, u32[]{:S(2)}) %collective-permute-start.15) | collective-permute-done | bytes 524320 | tf_op jit(solution)/shard_map/ppermute | solution.py:534
  73.5 1.0 copy-done.31
  74.7 4.7 %mlp.1 = (bf16[1024,256]{1,0:T(8,128)(2,1)}, bf16[1024,256]{1,0:T(8,128)(2,1)S(1)}, bf16[1024,256]{1,0:T(8,128)(2,1)S(1)}, bf16[1024,256]{1,0:T(8,128)(2,1)S(1)}...) custom-call(s32[1]{0:T(128)} %bitcast.here.refs_0_, ...), custom_call_target="tpu_custom_call" | custom-call | flops 1048576 | bytes 65536 | tf_op jit(solution)/shard_map/mlp/pallas_call | solution.py:226
  79.4 1.7 %collective-permute-start.18 = (bf16[1024,256]{1,0:T(8,128)(2,1)S(1)}, bf16[1024,256]{1,0:T(8,128)(2,1)S(1)}, u32[]{:S(2)}, u32[]{:S(2)}) collective-permute-start(bf16[1024,256]{1,0:T(8,128)(2,1)S(1)} %get-tuple-element.35.refs_0_), channel_id=1, source_target_pairs={{0,1},{1,0},{2,3},{3,2},{4,5},{5,4},{6,7},{7,6},{8,9},{9,8},{10,11... | collective-permute-start | bytes 1572872 | tf_op jit(solution)/shard_map/ppermute | solution.py:534
  81.0 1.5 weight_grads.1
  82.6 0.5 collective-permute-start.19
  83.1 8.0 %collective-permute-done.18.refs_1_ = bf16[1024,256]{1,0:T(8,128)(2,1)S(1)} collective-permute-done((bf16[1024,256]{1,0:T(8,128)(2,1)S(1)}, bf16[1024,256]{1,0:T(8,128)(2,1)S(1)}, u32[]{:S(2)}, u32[]{:S(2)}) %collective-permute-start.18) | collective-permute-done | bytes 524320 | tf_op jit(solution)/shard_map/ppermute | solution.py:534
  91.3 1.7 %collective-permute-start.24 = (f32[224,256]{1,0:T(8,128)S(1)}, f32[224,256]{1,0:T(8,128)S(1)}, u32[]{:S(2)}, u32[]{:S(2)}) collective-permute-start(f32[224,256]{1,0:T(8,128)S(1)} %slice.25), channel_id=1, source_target_pairs={{0,8},{4,12},{8,0},{12,4},{16,24},{20,28},{24,16},{28,20},{1,9},{5... | collective-permute-start | bytes 688136 | tf_op jit(solution)/shard_map/ppermute | solution.py:530
  92.9 5.6 %collective-permute-start.20 = (bf16[1024,256]{1,0:T(8,128)(2,1)S(1)}, bf16[1024,256]{1,0:T(8,128)(2,1)S(1)}, u32[]{:S(2)}, u32[]{:S(2)}) collective-permute-start(bf16[1024,256]{1,0:T(8,128)(2,1)S(1)} %collective-permute-done.19.refs_2_), channel_id=1, source_target_pairs={{0,1},{1,0},{2,3},{3,2},{4,5},{5,4},{6,7},{7,6},{8,9},{9,8},{10,11... | collective-permute-start | bytes 1572872 | tf_op jit(solution)/shard_map/ppermute | solution.py:534
  98.6 11.0 %collective-permute-start.22 = (bf16[1024,256]{1,0:T(8,128)(2,1)S(1)}, bf16[1024,256]{1,0:T(8,128)(2,1)S(1)}, u32[]{:S(2)}, u32[]{:S(2)}) collective-permute-start(bf16[1024,256]{1,0:T(8,128)(2,1)S(1)} %collective-permute-done.21.refs_17_.refs_4_), channel_id=1, source_target_pairs={{0,1},{1,0},{2,3},{3,2},{4,5},{5,4},{6,7},{7,6},{8,9},{9,8},{10,11... | collective-permute-start | bytes 1572872 | tf_op jit(solution)/shard_map/ppermute | solution.py:534
  109.6 1.6 collective-permute-start.25
  111.3 5.2 %tile_grads.2 = (bf16[128,128,128]{2,1,0:T(8,128)(2,1)}, f32[8,128]{1,0:T(8,128)S(1)}) custom-call(s32[1]{0:T(128)} %bitcast.here.refs_0_, s32[4,32]{1,0:T(4,128)S(1)} %bitcast.20, s32[32]{0:T(128)S(1)} %bitcast.26, bf16[1024,256]{1,0:T(8,128)(2,1)S(1)} %get-tuple-element.35.refs_0_, bf16[1024,256]{1,0:T(8,128)(2,1)S(1)} %collective-permute-done.18.refs_1_, ...), custom_call_target="tpu_custom_call" | custom-call | flops 1048576 | bytes 65536 | tf_op jit(solution)/shard_map/tile_grads/pallas_call | solution.py:502
  116.5 4.9 %collective-permute-done.22.refs_5_ = bf16[1024,256]{1,0:T(8,128)(2,1)S(1)} collective-permute-done((bf16[1024,256]{1,0:T(8,128)(2,1)S(1)}, bf16[1024,256]{1,0:T(8,128)(2,1)S(1)}, u32[]{:S(2)}, u32[]{:S(2)}) %collective-permute-start.22) | collective-permute-done | bytes 524320 | tf_op jit(solution)/shard_map/ppermute | solution.py:534
  121.5 6.8 %back_terms.1 = (bf16[4096,256]{1,0:T(8,128)(2,1)S(1)}, bf16[4096,256]{1,0:T(8,128)(2,1)S(1)}) custom-call(s32[1]{0:T(128)} %bitcast.here.refs_0_, s32[4,32]{1,0:T(4,128)S(1)} %bitcast.21, s32[32]{0:T(128)S(1)} %bitcast.27, bf16[1024,256]{1,0:T(8,128)(2,1)S(1)} %get-tuple-element.35.refs_0_, bf16[1024,256]{1,0:T(8,128)(2,1)S(1)} %collective-permute-done.18.refs_1_, ...), custom_call_target="tpu_custom_call" | custom-call | flops 1048576 | bytes 65536 | tf_op jit(solution)/shard_map/back_terms/pallas_call | solution.py:402
  128.3 0.1 collective-permute-start.26
  128.4 4.1 %collective-permute-done.26.refs_2_.refs_3_ = bf16[4096,256]{1,0:T(8,128)(2,1)S(1)} collective-permute-done((bf16[4096,256]{1,0:T(8,128)(2,1)S(1)}, bf16[4096,256]{1,0:T(8,128)(2,1)S(1)}, u32[]{:S(2)}, u32[]{:S(2)}) %collective-permute-start.26) | collective-permute-done | bytes 2097184 | tf_op jit(solution)/shard_map/ppermute | solution.py:530
  132.5 0.2 sum_terms.15.refs_22_.refs_6_
  132.7 2.9 %collective-permute-start.28 = (bf16[1024,256]{1,0:T(8,128)(2,1)S(1)}, bf16[1024,256]{1,0:T(8,128)(2,1)S(1)}, u32[]{:S(2)}, u32[]{:S(2)}) collective-permute-start(bf16[1024,256]{1,0:T(8,128)(2,1)S(1)} %sum_terms.15.refs_22_.refs_6_), channel_id=1, source_target_pairs={{0,16},{4,20},{8,24},{12,28},{16,0},{20,4},{24,8},{28,12},{1,17},{... | collective-permute-start | bytes 1572872 | tf_op jit(solution)/shard_map/ppermute | solution.py:530
  135.6 0.2 sum_terms.14.refs_21_.refs_5_
  135.9 1.7 %collective-permute-start.31 = (bf16[112,256]{1,0:T(8,128)(2,1)S(1)}, bf16[112,256]{1,0:T(8,128)(2,1)S(1)}, u32[]{:S(2)}, u32[]{:S(2)}) collective-permute-start(bf16[112,256]{1,0:T(8,128)(2,1)S(1)} %sum_terms.13.refs_7_.refs_1_), channel_id=1, source_target_pairs={{0,1},{1,2},{2,3},{3,0},{4,5},{5,6},{6,7},{7,4},{8,9},{9,10},{10,1... | collective-permute-start | bytes 172040 | tf_op jit(solution)/shard_map/ppermute | solution.py:538
  137.6 1.1 collective-permute-start.32
  138.7 1.9 %collective-permute-start.33 = (bf16[112,256]{1,0:T(8,128)(2,1)S(1)}, bf16[112,256]{1,0:T(8,128)(2,1)S(1)}, u32[]{:S(2)}, u32[]{:S(2)}) collective-permute-start(bf16[112,256]{1,0:T(8,128)(2,1)S(1)} %sum_terms.13.refs_7_.refs_1_), channel_id=1, source_target_pairs={{0,3},{1,0},{2,1},{3,2},{4,7},{5,4},{6,5},{7,6},{8,11},{9,8},{10,9... | collective-permute-start | bytes 172040 | tf_op jit(solution)/shard_map/ppermute | solution.py:538
  140.6 1.6 %collective-permute-done.31.refs_2_ = bf16[112,256]{1,0:T(8,128)(2,1)S(1)} collective-permute-done((bf16[112,256]{1,0:T(8,128)(2,1)S(1)}, bf16[112,256]{1,0:T(8,128)(2,1)S(1)}, u32[]{:S(2)}, u32[]{:S(2)}) %collective-permute-start.31) | collective-permute-done | bytes 57376 | tf_op jit(solution)/shard_map/ppermute | solution.py:538
  142.3 1.8 %collective-permute-done.32.refs_3_ = bf16[112,256]{1,0:T(8,128)(2,1)S(1)} collective-permute-done((bf16[112,256]{1,0:T(8,128)(2,1)S(1)}, bf16[112,256]{1,0:T(8,128)(2,1)S(1)}, u32[]{:S(2)}, u32[]{:S(2)}) %collective-permute-start.32) | collective-permute-done | bytes 57376 | tf_op jit(solution)/shard_map/ppermute | solution.py:538
  144.1 1.5 collective-permute-start.36
  145.6 2.0 %collective-permute-start.35 = (bf16[112,256]{1,0:T(8,128)(2,1)S(1)}, bf16[112,256]{1,0:T(8,128)(2,1)S(1)}, u32[]{:S(2)}, u32[]{:S(2)}) collective-permute-start(bf16[112,256]{1,0:T(8,128)(2,1)S(1)} %sum_terms.19), channel_id=1, source_target_pairs={{0,16},{4,20},{8,24},{12,28},{16,0},{20,4},{24,8},{28,12},{1,17},{... | collective-permute-start | bytes 172040 | tf_op jit(solution)/shard_map/ppermute | solution.py:530
  147.6 0.3 collective-permute-done.28.refs_3_.refs_7_
  147.9 0.1 sum_terms.16
  148.1 1.8 %collective-permute-start.29 = (bf16[512,256]{1,0:T(8,128)(2,1)S(1)}, bf16[512,256]{1,0:T(8,128)(2,1)S(1)}, u32[]{:S(2)}, u32[]{:S(2)}) collective-permute-start(bf16[512,256]{1,0:T(8,128)(2,1)S(1)} %sum_terms.16), channel_id=1, source_target_pairs={{0,8},{4,12},{8,0},{12,4},{16,24},{20,28},{24,16},{28,20},{1,9},{5... | collective-permute-start | bytes 786440 | tf_op jit(solution)/shard_map/ppermute | solution.py:530
  149.8 0.9 collective-permute-done.27.refs_3_.refs_4_
  150.7 0.1 sum_terms.17
  150.8 0.1 collective-permute-start.30
  151.0 0.2 collective-permute-done.36
  151.2 2.0 %collective-permute-done.34 = bf16[112,256]{1,0:T(8,128)(2,1)S(1)} collective-permute-done((bf16[112,256]{1,0:T(8,128)(2,1)S(1)}, bf16[112,256]{1,0:T(8,128)(2,1)S(1)}, u32[]{:S(2)}, u32[]{:S(2)}) %collective-permute-start.34) | collective-permute-done | bytes 57376 | tf_op jit(solution)/shard_map/ppermute | solution.py:530
  153.2 6.1 %tile_grads.3 = (bf16[128,128,128]{2,1,0:T(8,128)(2,1)}, f32[8,128]{1,0:T(8,128)}) custom-call(s32[1]{0:T(128)} %bitcast.here.refs_0_, s32[4,32]{1,0:T(4,128)S(1)} %bitcast.22, s32[32]{0:T(128)S(1)} %bitcast.28, bf16[1024,256]{1,0:T(8,128)(2,1)S(1)} %get-tuple-element.35.refs_0_, ...), custom_call_target="tpu_custom_call", output_to_operand_aliasing={{0}: (23, {})} | custom-call | flops 1048576 | bytes 65536 | tf_op jit(solution)/shard_map/tile_grads/pallas_call | solution.py:502
  159.4 1.0 weight_unpack.1
  160.4 1.6 sum_terms.18
  (113 shorter events, 0.8 us)
Async XLA Ops:
  0.6 18.9 %collective-permute-start = (bf16[1024,256]{1,0:T(8,128)(2,1)}, bf16[1024,256]{1,0:T(8,128)(2,1)S(1)}, u32[]{:S(2)}, u32[]{:S(2)}) collective-permute-start(bf16[1024,256]{1,0:T(8,128)(2,1)} %refs_6_.1), channel_id=1, source_target_pairs={{0,4},{4,0},{8,12},{12,8},{16,20},{20,16},{24,28},{28,24},{1,5},{5... | collective-permute-start | bytes 1572872 | tf_op jit(solution)/shard_map/ppermute | solution.py:530
  2.2 9.7 %collective-permute-start.1 = (bf16[512,256]{1,0:T(8,128)(2,1)S(1)}, bf16[512,256]{1,0:T(8,128)(2,1)S(1)}, u32[]{:S(2)}, u32[]{:S(2)}) collective-permute-start(bf16[512,256]{1,0:T(8,128)(2,1)S(1)} %get-tuple-element.53), channel_id=1, source_target_pairs={{0,8},{4,12},{8,0},{12,4},{16,24},{20,28},{24,16},{28,20},{1,9},{5... | collective-permute-start | bytes 786440 | tf_op jit(solution)/shard_map/ppermute | solution.py:530
  4.8 9.1 %collective-permute-start.5 = (bf16[512,256]{1,0:T(8,128)(2,1)S(1)}, bf16[512,256]{1,0:T(8,128)(2,1)S(1)}, u32[]{:S(2)}, u32[]{:S(2)}) collective-permute-start(bf16[512,256]{1,0:T(8,128)(2,1)S(1)} %get-tuple-element.53), channel_id=1, source_target_pairs={{0,16},{4,20},{8,24},{12,28},{16,0},{20,4},{24,8},{28,12},{1,17},{... | collective-permute-start | bytes 786440 | tf_op jit(solution)/shard_map/ppermute | solution.py:530
  6.3 11.3 %collective-permute-start.2 = (bf16[512,256]{1,0:T(8,128)(2,1)S(1)}, bf16[512,256]{1,0:T(8,128)(2,1)S(1)}, u32[]{:S(2)}, u32[]{:S(2)}) collective-permute-start(bf16[512,256]{1,0:T(8,128)(2,1)S(1)} %get-tuple-element.52), channel_id=1, source_target_pairs={{0,8},{4,12},{8,0},{12,4},{16,24},{20,28},{24,16},{28,20},{1,9},{5... | collective-permute-start | bytes 786440 | tf_op jit(solution)/shard_map/ppermute | solution.py:530
  6.8 12.7 %collective-permute-start.6 = (bf16[512,256]{1,0:T(8,128)(2,1)S(1)}, bf16[512,256]{1,0:T(8,128)(2,1)S(1)}, u32[]{:S(2)}, u32[]{:S(2)}) collective-permute-start(bf16[512,256]{1,0:T(8,128)(2,1)S(1)} %get-tuple-element.52), channel_id=1, source_target_pairs={{0,16},{4,20},{8,24},{12,28},{16,0},{20,4},{24,8},{28,12},{1,17},{... | collective-permute-start | bytes 786440 | tf_op jit(solution)/shard_map/ppermute | solution.py:530
  11.9 15.2 %copy-start.4 = (bf16[512,256]{1,0:T(8,128)(2,1)}, bf16[512,256]{1,0:T(8,128)(2,1)S(1)}, u32[]{:S(2)}) copy-start(bf16[512,256]{1,0:T(8,128)(2,1)S(1)} %collective-permute-done.1.refs_2_.refs_4_.refs_8_) | copy-start | bytes 786436
  11.9 8.1 %collective-permute-start.3 = (bf16[512,256]{1,0:T(8,128)(2,1)S(1)}, bf16[512,256]{1,0:T(8,128)(2,1)S(1)}, u32[]{:S(2)}, u32[]{:S(2)}) collective-permute-start(bf16[512,256]{1,0:T(8,128)(2,1)S(1)} %collective-permute-done.1.refs_2_.refs_4_.refs_8_), channel_id=1, source_target_pairs={{0,4},{4,0},{8,12},{12,8},{16,20},{20,16},{24,28},{28,24},{1,5},{5... | collective-permute-start | bytes 786440 | tf_op jit(solution)/shard_map/ppermute | solution.py:530
  13.9 13.2 %copy-start.6 = (bf16[512,256]{1,0:T(8,128)(2,1)}, bf16[512,256]{1,0:T(8,128)(2,1)S(1)}, u32[]{:S(2)}) copy-start(bf16[512,256]{1,0:T(8,128)(2,1)S(1)} %collective-permute-done.5.refs_6_.refs_8_.refs_12_) | copy-start | bytes 786436
  13.9 9.1 %collective-permute-start.9 = (bf16[512,256]{1,0:T(8,128)(2,1)S(1)}, bf16[512,256]{1,0:T(8,128)(2,1)S(1)}, u32[]{:S(2)}, u32[]{:S(2)}) collective-permute-start(bf16[512,256]{1,0:T(8,128)(2,1)S(1)} %collective-permute-done.5.refs_6_.refs_8_.refs_12_), channel_id=1, source_target_pairs={{0,8},{4,12},{8,0},{12,4},{16,24},{20,28},{24,16},{28,20},{1,9},{5... | collective-permute-start | bytes 786440 | tf_op jit(solution)/shard_map/ppermute | solution.py:530
  17.6 7.9 %collective-permute-start.10 = (bf16[512,256]{1,0:T(8,128)(2,1)S(1)}, bf16[512,256]{1,0:T(8,128)(2,1)S(1)}, u32[]{:S(2)}, u32[]{:S(2)}) collective-permute-start(bf16[512,256]{1,0:T(8,128)(2,1)S(1)} %collective-permute-done.2.refs_3_.refs_5_.refs_9_), channel_id=1, source_target_pairs={{0,16},{4,20},{8,24},{12,28},{16,0},{20,4},{24,8},{28,12},{1,17},{... | collective-permute-start | bytes 786440 | tf_op jit(solution)/shard_map/ppermute | solution.py:530
  19.5 6.0 %collective-permute-start.4 = (bf16[512,256]{1,0:T(8,128)(2,1)S(1)}, bf16[512,256]{1,0:T(8,128)(2,1)S(1)}, u32[]{:S(2)}, u32[]{:S(2)}) collective-permute-start(bf16[512,256]{1,0:T(8,128)(2,1)S(1)} %collective-permute-done.2.refs_3_.refs_5_.refs_9_), channel_id=1, source_target_pairs={{0,4},{4,0},{8,12},{12,8},{16,20},{20,16},{24,28},{28,24},{1,5},{5... | collective-permute-start | bytes 786440 | tf_op jit(solution)/shard_map/ppermute | solution.py:530
  19.6 5.9 %collective-permute-start.7 = (bf16[512,256]{1,0:T(8,128)(2,1)S(1)}, bf16[512,256]{1,0:T(8,128)(2,1)S(1)}, u32[]{:S(2)}, u32[]{:S(2)}) collective-permute-start(bf16[512,256]{1,0:T(8,128)(2,1)S(1)} %collective-permute-done.5.refs_6_.refs_8_.refs_12_), channel_id=1, source_target_pairs={{0,4},{4,0},{8,12},{12,8},{16,20},{20,16},{24,28},{28,24},{1,5},{5... | collective-permute-start | bytes 786440 | tf_op jit(solution)/shard_map/ppermute | solution.py:530
  20.1 5.5 %collective-permute-start.8 = (bf16[512,256]{1,0:T(8,128)(2,1)S(1)}, bf16[512,256]{1,0:T(8,128)(2,1)S(1)}, u32[]{:S(2)}, u32[]{:S(2)}) collective-permute-start(bf16[512,256]{1,0:T(8,128)(2,1)S(1)} %collective-permute-done.6.refs_7_.refs_9_.refs_13_), channel_id=1, source_target_pairs={{0,4},{4,0},{8,12},{12,8},{16,20},{20,16},{24,28},{28,24},{1,5},{5... | collective-permute-start | bytes 786440 | tf_op jit(solution)/shard_map/ppermute | solution.py:530
  23.0 2.6 %collective-permute-start.11 = (bf16[512,256]{1,0:T(8,128)(2,1)S(1)}, bf16[512,256]{1,0:T(8,128)(2,1)S(1)}, u32[]{:S(2)}, u32[]{:S(2)}) collective-permute-start(bf16[512,256]{1,0:T(8,128)(2,1)S(1)} %collective-permute-done.9.refs_10_.refs_12_.refs_16_), channel_id=1, source_target_pairs={{0,4},{4,0},{8,12},{12,8},{16,20},{20,16},{24,28},{28,24},{1,5},{5... | collective-permute-start | bytes 786440 | tf_op jit(solution)/shard_map/ppermute | solution.py:530
  25.5 1.7 %collective-permute-start.12 = (bf16[512,256]{1,0:T(8,128)(2,1)S(1)}, bf16[512,256]{1,0:T(8,128)(2,1)}, u32[]{:S(2)}, u32[]{:S(2)}) collective-permute-start(bf16[512,256]{1,0:T(8,128)(2,1)S(1)} %collective-permute-done.10.refs_11_.refs_13_.refs_17_), channel_id=1, source_target_pairs={{0,4},{4,0},{8,12},{12,8},{16,20},{20,16},{24,28},{28,24},{1,5},{5... | collective-permute-start | bytes 786440 | tf_op jit(solution)/shard_map/ppermute | solution.py:530
  32.0 15.1 %copy-start.28 = (bf16[1024,256]{1,0:T(8,128)(2,1)S(1)}, bf16[1024,256]{1,0:T(8,128)(2,1)}, u32[]{:S(2)}) copy-start(bf16[1024,256]{1,0:T(8,128)(2,1)} %partial_messages.4.refs_1_) | copy-start | bytes 1572868
  32.0 15.0 %collective-permute-start.13 = (bf16[1024,256]{1,0:T(8,128)(2,1)}, bf16[1024,256]{1,0:T(8,128)(2,1)S(1)}, u32[]{:S(2)}, u32[]{:S(2)}) collective-permute-start(bf16[1024,256]{1,0:T(8,128)(2,1)} %partial_messages.4.refs_1_), channel_id=1, source_target_pairs={{0,1},{1,0},{2,3},{3,2},{4,5},{5,4},{6,7},{7,6},{8,9},{9,8},{10,11... | collective-permute-start | bytes 1572872 | tf_op jit(solution)/shard_map/ppermute | solution.py:534
  38.5 19.0 %collective-permute-start.16 = (bf16[1024,256]{1,0:T(8,128)(2,1)}, bf16[1024,256]{1,0:T(8,128)(2,1)S(1)}, u32[]{:S(2)}, u32[]{:S(2)}) collective-permute-start(bf16[1024,256]{1,0:T(8,128)(2,1)} %partial_messages.5.refs_1_), channel_id=1, source_target_pairs={{0,1},{1,0},{2,3},{3,2},{4,5},{5,4},{6,7},{7,6},{8,9},{9,8},{10,11... | collective-permute-start | bytes 1572872 | tf_op jit(solution)/shard_map/ppermute | solution.py:534
  47.3 10.3 %copy-start.27 = (bf16[1024,256]{1,0:T(8,128)(2,1)S(1)}, bf16[1024,256]{1,0:T(8,128)(2,1)}, u32[]{:S(2)}) copy-start(bf16[1024,256]{1,0:T(8,128)(2,1)} %partial_messages.5.refs_1_) | copy-start | bytes 1572868
  47.3 26.2 %copy-start.1 = (bf16[1024,256]{1,0:T(8,128)(2,1)S(1)}, bf16[1024,256]{1,0:T(8,128)(2,1)}, u32[]{:S(2)}) copy-start(bf16[1024,256]{1,0:T(8,128)(2,1)} %refs_6_.1) | copy-start | bytes 1572868
  47.3 26.2 %copy-start.26 = (bf16[1024,256]{1,0:T(8,128)(2,1)S(1)}, bf16[1024,256]{1,0:T(8,128)(2,1)}, u32[]{:S(2)}) copy-start(bf16[1024,256]{1,0:T(8,128)(2,1)} %cot.3) | copy-start | bytes 1572868
  47.3 26.1 %copy-start.29 = (bf16[512,256]{1,0:T(8,128)(2,1)S(1)}, bf16[512,256]{1,0:T(8,128)(2,1)}, u32[]{:S(2)}) copy-start(bf16[512,256]{1,0:T(8,128)(2,1)} %w_in.1) | copy-start | bytes 786436
  47.3 26.1 %copy-start.32 = (bf16[256,256]{1,0:T(8,128)(2,1)S(1)}, bf16[256,256]{1,0:T(8,128)(2,1)}, u32[]{:S(2)}) copy-start(bf16[256,256]{1,0:T(8,128)(2,1)} %refs_5_.1) | copy-start | bytes 393220
  47.3 26.1 %copy-start.35 = (f32[256]{0:T(256)S(1)}, f32[256]{0:T(256)}, u32[]{:S(2)}) copy-start(f32[256]{0:T(256)} %param.15) | copy-start | bytes 3076
  47.3 26.1 %copy-start.36 = (f32[256]{0:T(256)S(1)}, f32[256]{0:T(256)}, u32[]{:S(2)}) copy-start(f32[256]{0:T(256)} %param.17) | copy-start | bytes 3076
  47.4 26.1 %copy-start.37 = (f32[256]{0:T(256)S(1)}, f32[256]{0:T(256)}, u32[]{:S(2)}) copy-start(f32[256]{0:T(256)} %param.18) | copy-start | bytes 3076
  47.4 10.4 %collective-permute-start.14 = (bf16[1024,256]{1,0:T(8,128)(2,1)S(1)}, bf16[1024,256]{1,0:T(8,128)(2,1)S(1)}, u32[]{:S(2)}, u32[]{:S(2)}) collective-permute-start(bf16[1024,256]{1,0:T(8,128)(2,1)S(1)} %sum_terms.10), channel_id=1, source_target_pairs={{0,4},{1,2},{2,1},{3,7},{4,0},{5,6},{6,5},{7,3},{8,12},{9,10},{10,... | collective-permute-start | bytes 1572872 | tf_op jit(solution)/shard_map/ppermute | solution.py:547
  57.7 5.0 %collective-permute-start.17 = (bf16[1024,256]{1,0:T(8,128)(2,1)S(1)}, bf16[1024,256]{1,0:T(8,128)(2,1)S(1)}, u32[]{:S(2)}, u32[]{:S(2)}) collective-permute-start(bf16[1024,256]{1,0:T(8,128)(2,1)S(1)} %sum_terms.12), channel_id=1, source_target_pairs={{0,4},{1,2},{2,1},{3,7},{4,0},{5,6},{6,5},{7,3},{8,12},{9,10},{10,... | collective-permute-start | bytes 1572872 | tf_op jit(solution)/shard_map/ppermute | solution.py:547
  59.1 14.4 %collective-permute-start.15 = (bf16[1024,256]{1,0:T(8,128)(2,1)S(1)}, bf16[1024,256]{1,0:T(8,128)(2,1)S(1)}, u32[]{:S(2)}, u32[]{:S(2)}) collective-permute-start(bf16[1024,256]{1,0:T(8,128)(2,1)S(1)} %sum_terms.11), channel_id=1, source_target_pairs={{0,1},{1,0},{2,3},{3,2},{4,5},{5,4},{6,7},{7,6},{8,9},{9,8},{10,11... | collective-permute-start | bytes 1572872 | tf_op jit(solution)/shard_map/ppermute | solution.py:534
  74.5 36.6 %copy-start.3 = (bf16[1024,256]{1,0:T(8,128)(2,1)S(1)}, bf16[1024,256]{1,0:T(8,128)(2,1)}, u32[]{:S(2)}) copy-start(bf16[1024,256]{1,0:T(8,128)(2,1)} %copy-done.2) | copy-start | bytes 1572868
  74.5 36.6 %copy-start.5 = (bf16[512,256]{1,0:T(8,128)(2,1)S(1)}, bf16[512,256]{1,0:T(8,128)(2,1)}, u32[]{:S(2)}) copy-start(bf16[512,256]{1,0:T(8,128)(2,1)} %copy-done.4) | copy-start | bytes 786436
  74.5 36.7 %copy-start.7 = (bf16[512,256]{1,0:T(8,128)(2,1)S(1)}, bf16[512,256]{1,0:T(8,128)(2,1)}, u32[]{:S(2)}) copy-start(bf16[512,256]{1,0:T(8,128)(2,1)} %copy-done.6) | copy-start | bytes 786436
  74.5 36.7 %copy-start.9 = (bf16[512,256]{1,0:T(8,128)(2,1)S(1)}, bf16[512,256]{1,0:T(8,128)(2,1)}, u32[]{:S(2)}) copy-start(bf16[512,256]{1,0:T(8,128)(2,1)} %copy-done.8) | copy-start | bytes 786436
  74.6 36.7 %copy-start.11 = (bf16[512,256]{1,0:T(8,128)(2,1)S(1)}, bf16[512,256]{1,0:T(8,128)(2,1)}, u32[]{:S(2)}) copy-start(bf16[512,256]{1,0:T(8,128)(2,1)} %copy-done.10) | copy-start | bytes 786436
  74.6 36.7 %copy-start.13 = (bf16[512,256]{1,0:T(8,128)(2,1)S(1)}, bf16[512,256]{1,0:T(8,128)(2,1)}, u32[]{:S(2)}) copy-start(bf16[512,256]{1,0:T(8,128)(2,1)} %copy-done.12) | copy-start | bytes 786436
  74.6 36.7 %copy-start.15 = (bf16[512,256]{1,0:T(8,128)(2,1)S(1)}, bf16[512,256]{1,0:T(8,128)(2,1)}, u32[]{:S(2)}) copy-start(bf16[512,256]{1,0:T(8,128)(2,1)} %copy-done.14) | copy-start | bytes 786436
  74.6 36.7 %copy-start.17 = (bf16[512,256]{1,0:T(8,128)(2,1)S(1)}, bf16[512,256]{1,0:T(8,128)(2,1)}, u32[]{:S(2)}) copy-start(bf16[512,256]{1,0:T(8,128)(2,1)} %copy-done.16) | copy-start | bytes 786436
  74.6 36.7 %copy-start.19 = (bf16[512,256]{1,0:T(8,128)(2,1)S(1)}, bf16[512,256]{1,0:T(8,128)(2,1)}, u32[]{:S(2)}) copy-start(bf16[512,256]{1,0:T(8,128)(2,1)} %copy-done.18) | copy-start | bytes 786436
  74.6 36.7 %copy-start.21 = (bf16[512,256]{1,0:T(8,128)(2,1)S(1)}, bf16[512,256]{1,0:T(8,128)(2,1)}, u32[]{:S(2)}) copy-start(bf16[512,256]{1,0:T(8,128)(2,1)} %copy-done.20) | copy-start | bytes 786436
  74.6 36.7 %copy-start.23 = (bf16[512,256]{1,0:T(8,128)(2,1)S(1)}, bf16[512,256]{1,0:T(8,128)(2,1)}, u32[]{:S(2)}) copy-start(bf16[512,256]{1,0:T(8,128)(2,1)} %copy-done.22) | copy-start | bytes 786436
  74.6 36.7 %copy-start.25 = (bf16[512,256]{1,0:T(8,128)(2,1)S(1)}, bf16[512,256]{1,0:T(8,128)(2,1)}, u32[]{:S(2)}) copy-start(bf16[512,256]{1,0:T(8,128)(2,1)} %copy-done.24) | copy-start | bytes 786436
  74.6 36.7 %copy-start.33 = (s32[32,1,4]{0,2,1:T(4,128)S(1)}, s32[32,1,4]{0,2,1:T(4,128)}, u32[]{:S(2)}) copy-start(s32[32,1,4]{0,2,1:T(4,128)} %param.12) | copy-start | bytes 1540
  74.6 36.7 %copy-start.34 = (s32[32,1]{0,1:T(1,128)S(1)}, s32[32,1]{0,1:T(1,128)}, u32[]{:S(2)}) copy-start(s32[32,1]{0,1:T(1,128)} %param.13) | copy-start | bytes 388
  79.4 11.8 %collective-permute-start.18 = (bf16[1024,256]{1,0:T(8,128)(2,1)S(1)}, bf16[1024,256]{1,0:T(8,128)(2,1)S(1)}, u32[]{:S(2)}, u32[]{:S(2)}) collective-permute-start(bf16[1024,256]{1,0:T(8,128)(2,1)S(1)} %get-tuple-element.35.refs_0_), channel_id=1, source_target_pairs={{0,1},{1,0},{2,3},{3,2},{4,5},{5,4},{6,7},{7,6},{8,9},{9,8},{10,11... | collective-permute-start | bytes 1572872 | tf_op jit(solution)/shard_map/ppermute | solution.py:534
  82.6 8.6 %collective-permute-start.23 = (f32[448,256]{1,0:T(8,128)S(1)}, f32[448,256]{1,0:T(8,128)S(1)}, u32[]{:S(2)}, u32[]{:S(2)}) collective-permute-start(f32[448,256]{1,0:T(8,128)S(1)} %get-tuple-element.37), channel_id=1, source_target_pairs={{0,4},{4,0},{8,12},{12,8},{16,20},{20,16},{24,28},{28,24},{1,5},{5... | collective-permute-start | bytes 1376264 | tf_op jit(solution)/shard_map/ppermute | solution.py:530
  82.6 10.3 %collective-permute-start.19 = (bf16[1024,256]{1,0:T(8,128)(2,1)S(1)}, bf16[1024,256]{1,0:T(8,128)(2,1)S(1)}, u32[]{:S(2)}, u32[]{:S(2)}) collective-permute-start(bf16[1024,256]{1,0:T(8,128)(2,1)S(1)} %get-tuple-element.35.refs_0_), channel_id=1, source_target_pairs={{0,4},{1,2},{2,1},{3,7},{4,0},{5,6},{6,5},{7,3},{8,12},{9,10},{10,... | collective-permute-start | bytes 1572872 | tf_op jit(solution)/shard_map/ppermute | solution.py:547
  91.1 7.4 %collective-permute-start.21 = (bf16[1024,256]{1,0:T(8,128)(2,1)S(1)}, bf16[1024,256]{1,0:T(8,128)(2,1)S(1)}, u32[]{:S(2)}, u32[]{:S(2)}) collective-permute-start(bf16[1024,256]{1,0:T(8,128)(2,1)S(1)} %collective-permute-done.18.refs_1_), channel_id=1, source_target_pairs={{0,4},{1,2},{2,1},{3,7},{4,0},{5,6},{6,5},{7,3},{8,12},{9,10},{10,... | collective-permute-start | bytes 1572872 | tf_op jit(solution)/shard_map/ppermute | solution.py:547
  91.2 30.3 %copy-start = (bf16[32,1,4,128,128]{4,3,2,1,0:T(8,128)(2,1)S(1)}, bf16[32,1,4,128,128]{4,3,2,1,0:T(8,128)(2,1)}, u32[]{:S(2)}) copy-start(bf16[32,1,4,128,128]{4,3,2,1,0:T(8,128)(2,1)} %param.11) | copy-start | bytes 12582916
  91.3 18.3 %collective-permute-start.24 = (f32[224,256]{1,0:T(8,128)S(1)}, f32[224,256]{1,0:T(8,128)S(1)}, u32[]{:S(2)}, u32[]{:S(2)}) collective-permute-start(f32[224,256]{1,0:T(8,128)S(1)} %slice.25), channel_id=1, source_target_pairs={{0,8},{4,12},{8,0},{12,4},{16,24},{20,28},{24,16},{28,20},{1,9},{5... | collective-permute-start | bytes 688136 | tf_op jit(solution)/shard_map/ppermute | solution.py:530
  92.9 18.3 %collective-permute-start.20 = (bf16[1024,256]{1,0:T(8,128)(2,1)S(1)}, bf16[1024,256]{1,0:T(8,128)(2,1)S(1)}, u32[]{:S(2)}, u32[]{:S(2)}) collective-permute-start(bf16[1024,256]{1,0:T(8,128)(2,1)S(1)} %collective-permute-done.19.refs_2_), channel_id=1, source_target_pairs={{0,1},{1,0},{2,3},{3,2},{4,5},{5,4},{6,7},{7,6},{8,9},{9,8},{10,11... | collective-permute-start | bytes 1572872 | tf_op jit(solution)/shard_map/ppermute | solution.py:534
  98.6 22.9 %collective-permute-start.22 = (bf16[1024,256]{1,0:T(8,128)(2,1)S(1)}, bf16[1024,256]{1,0:T(8,128)(2,1)S(1)}, u32[]{:S(2)}, u32[]{:S(2)}) collective-permute-start(bf16[1024,256]{1,0:T(8,128)(2,1)S(1)} %collective-permute-done.21.refs_17_.refs_4_), channel_id=1, source_target_pairs={{0,1},{1,0},{2,3},{3,2},{4,5},{5,4},{6,7},{7,6},{8,9},{9,8},{10,11... | collective-permute-start | bytes 1572872 | tf_op jit(solution)/shard_map/ppermute | solution.py:534
  109.6 6.9 %collective-permute-start.25 = (f32[112,256]{1,0:T(8,128)S(1)}, f32[112,256]{1,0:T(8,128)S(1)}, u32[]{:S(2)}, u32[]{:S(2)}) collective-permute-start(f32[112,256]{1,0:T(8,128)S(1)} %get-tuple-element.54), channel_id=1, source_target_pairs={{0,16},{4,20},{8,24},{12,28},{16,0},{20,4},{24,8},{28,12},{1,17},{... | collective-permute-start | bytes 344072 | tf_op jit(solution)/shard_map/ppermute | solution.py:530
  128.3 4.2 %collective-permute-start.26 = (bf16[4096,256]{1,0:T(8,128)(2,1)S(1)}, bf16[4096,256]{1,0:T(8,128)(2,1)S(1)}, u32[]{:S(2)}, u32[]{:S(2)}) collective-permute-start(bf16[4096,256]{1,0:T(8,128)(2,1)S(1)} %get-tuple-element.40), channel_id=1, source_target_pairs={{0,4},{4,0},{8,12},{12,8},{16,20},{20,16},{24,28},{28,24},{1,5},{5... | collective-permute-start | bytes 6291464 | tf_op jit(solution)/shard_map/ppermute | solution.py:530
  132.7 15.2 %collective-permute-start.28 = (bf16[1024,256]{1,0:T(8,128)(2,1)S(1)}, bf16[1024,256]{1,0:T(8,128)(2,1)S(1)}, u32[]{:S(2)}, u32[]{:S(2)}) collective-permute-start(bf16[1024,256]{1,0:T(8,128)(2,1)S(1)} %sum_terms.15.refs_22_.refs_6_), channel_id=1, source_target_pairs={{0,16},{4,20},{8,24},{12,28},{16,0},{20,4},{24,8},{28,12},{1,17},{... | collective-permute-start | bytes 1572872 | tf_op jit(solution)/shard_map/ppermute | solution.py:530
  135.8 14.9 %collective-permute-start.27 = (bf16[1024,256]{1,0:T(8,128)(2,1)S(1)}, bf16[1024,256]{1,0:T(8,128)(2,1)S(1)}, u32[]{:S(2)}, u32[]{:S(2)}) collective-permute-start(bf16[1024,256]{1,0:T(8,128)(2,1)S(1)} %sum_terms.14.refs_21_.refs_5_), channel_id=1, source_target_pairs={{0,8},{4,12},{8,0},{12,4},{16,24},{20,28},{24,16},{28,20},{1,9},{5... | collective-permute-start | bytes 1572872 | tf_op jit(solution)/shard_map/ppermute | solution.py:530
  135.9 6.4 %collective-permute-start.31 = (bf16[112,256]{1,0:T(8,128)(2,1)S(1)}, bf16[112,256]{1,0:T(8,128)(2,1)S(1)}, u32[]{:S(2)}, u32[]{:S(2)}) collective-permute-start(bf16[112,256]{1,0:T(8,128)(2,1)S(1)} %sum_terms.13.refs_7_.refs_1_), channel_id=1, source_target_pairs={{0,1},{1,2},{2,3},{3,0},{4,5},{5,6},{6,7},{7,4},{8,9},{9,10},{10,1... | collective-permute-start | bytes 172040 | tf_op jit(solution)/shard_map/ppermute | solution.py:538
  137.6 6.4 %collective-permute-start.32 = (bf16[112,256]{1,0:T(8,128)(2,1)S(1)}, bf16[112,256]{1,0:T(8,128)(2,1)S(1)}, u32[]{:S(2)}, u32[]{:S(2)}) collective-permute-start(bf16[112,256]{1,0:T(8,128)(2,1)S(1)} %sum_terms.13.refs_7_.refs_1_), channel_id=1, source_target_pairs={{0,2},{1,3},{2,0},{3,1},{4,6},{5,7},{6,4},{7,5},{8,10},{9,11},{10,... | collective-permute-start | bytes 172040 | tf_op jit(solution)/shard_map/ppermute | solution.py:538
  138.7 5.3 %collective-permute-start.33 = (bf16[112,256]{1,0:T(8,128)(2,1)S(1)}, bf16[112,256]{1,0:T(8,128)(2,1)S(1)}, u32[]{:S(2)}, u32[]{:S(2)}) collective-permute-start(bf16[112,256]{1,0:T(8,128)(2,1)S(1)} %sum_terms.13.refs_7_.refs_1_), channel_id=1, source_target_pairs={{0,3},{1,0},{2,1},{3,2},{4,7},{5,4},{6,5},{7,6},{8,11},{9,8},{10,9... | collective-permute-start | bytes 172040 | tf_op jit(solution)/shard_map/ppermute | solution.py:538
  144.1 7.1 %collective-permute-start.36 = (bf16[112,256]{1,0:T(8,128)(2,1)S(1)}, bf16[112,256]{1,0:T(8,128)(2,1)S(1)}, u32[]{:S(2)}, u32[]{:S(2)}) collective-permute-start(bf16[112,256]{1,0:T(8,128)(2,1)S(1)} %sum_terms.19), channel_id=1, source_target_pairs={{0,24},{4,28},{8,16},{12,20},{16,8},{20,12},{24,0},{28,4},{1,25},{... | collective-permute-start | bytes 172040 | tf_op jit(solution)/shard_map/ppermute | solution.py:530
  145.6 5.6 %collective-permute-start.35 = (bf16[112,256]{1,0:T(8,128)(2,1)S(1)}, bf16[112,256]{1,0:T(8,128)(2,1)S(1)}, u32[]{:S(2)}, u32[]{:S(2)}) collective-permute-start(bf16[112,256]{1,0:T(8,128)(2,1)S(1)} %sum_terms.19), channel_id=1, source_target_pairs={{0,16},{4,20},{8,24},{12,28},{16,0},{20,4},{24,8},{28,12},{1,17},{... | collective-permute-start | bytes 172040 | tf_op jit(solution)/shard_map/ppermute | solution.py:530
  147.6 5.5 %collective-permute-start.34 = (bf16[112,256]{1,0:T(8,128)(2,1)S(1)}, bf16[112,256]{1,0:T(8,128)(2,1)S(1)}, u32[]{:S(2)}, u32[]{:S(2)}) collective-permute-start(bf16[112,256]{1,0:T(8,128)(2,1)S(1)} %sum_terms.19), channel_id=1, source_target_pairs={{0,8},{4,12},{8,0},{12,4},{16,24},{20,28},{24,16},{28,20},{1,9},{5... | collective-permute-start | bytes 172040 | tf_op jit(solution)/shard_map/ppermute | solution.py:530
  148.1 12.3 %collective-permute-start.29 = (bf16[512,256]{1,0:T(8,128)(2,1)S(1)}, bf16[512,256]{1,0:T(8,128)(2,1)S(1)}, u32[]{:S(2)}, u32[]{:S(2)}) collective-permute-start(bf16[512,256]{1,0:T(8,128)(2,1)S(1)} %sum_terms.16), channel_id=1, source_target_pairs={{0,8},{4,12},{8,0},{12,4},{16,24},{20,28},{24,16},{28,20},{1,9},{5... | collective-permute-start | bytes 786440 | tf_op jit(solution)/shard_map/ppermute | solution.py:530
  150.8 9.5 %collective-permute-start.30 = (bf16[512,256]{1,0:T(8,128)(2,1)S(1)}, bf16[512,256]{1,0:T(8,128)(2,1)S(1)}, u32[]{:S(2)}, u32[]{:S(2)}) collective-permute-start(bf16[512,256]{1,0:T(8,128)(2,1)S(1)} %sum_terms.17), channel_id=1, source_target_pairs={{0,16},{4,20},{8,24},{12,28},{16,0},{20,4},{24,8},{28,12},{1,17},{... | collective-permute-start | bytes 786440 | tf_op jit(solution)/shard_map/ppermute | solution.py:530
  153.2 6.2 %collective-permute-start.37 = (bf16[448,256]{1,0:T(8,128)(2,1)S(1)}, bf16[448,256]{1,0:T(8,128)(2,1)S(1)}, u32[]{:S(2)}, u32[]{:S(2)}) collective-permute-start(bf16[448,256]{1,0:T(8,128)(2,1)S(1)} %pad_maximum_fusion.even), channel_id=1, source_target_pairs={{0,4},{4,0},{8,12},{12,8},{16,20},{20,16},{24,28},{28,24},{1,5},{5... | collective-permute-start | bytes 688136 | tf_op jit(solution)/shard_map/ppermute | solution.py:530
  (12 other events, 46.9 us)

commit v11 on v10

--- a/solution.py
+++ b/solution.py
@@ -169,7 +169,7 @@
     message = jnp.concatenate(messages, axis=1) if len(messages) > 1 else messages[0]
     node = nodes[...]
     pre = mm(node, w_in[:width]) + mm(message, w_in[width:]) + bias[...]
-    sig = jax.nn.sigmoid(pre)
+    sig = 0.5 + 0.5 * jnp.tanh(0.5 * pre)
     act = (pre * sig).astype(BF16)
     proj = mm(act, w_out[...])
     mean = jnp.mean(proj, axis=-1, keepdims=True)
@@ -210,7 +210,7 @@
 
 def mlp_call(here, nodes, cot, parts, kinds, w_in, bias, w_out, gain, shift):
     rows, width = nodes.shape
-    step = min(rows, 256)
+    step = min(rows, 512)
 
     def blocked(array):
         return pl.BlockSpec((step, array.shape[1]), lambda i: (i, 0))
@@ -559,14 +559,15 @@
     return pieces
 
 
-def reduce_square(here, even, other, rows):
+def reduce_square(here, even, urgent, rest, rows):
     half = rows // 2
     first = [
-        sum_call(here, rows, [(even, places), (other, places)]) for places in ((6, 2), (7, 5))
+        sum_call(here, rows, [(even, (6, 2)), (urgent, (0, 2))]),
+        sum_call(here, rows, [(even, (7, 5)), (urgent, (1, 3))]),
     ]
     x_first, y_first = swap(first[0], 2), swap(first[1], 4)
-    y_lower = swap(sum_call(here, half, [(even, 4), (other, 4), (x_first, 0)]), 4)
-    x_upper = swap(sum_call(here, half, [(even, 3), (other, 3), (y_first, 0)]), 2)
+    y_lower = swap(sum_call(here, half, [(even, 4), (rest, 3), (x_first, 0)]), 4)
+    x_upper = swap(sum_call(here, half, [(even, 3), (rest, 2), (y_first, 0)]), 2)
     return [((x_first, 1), (x_upper, 0)), ((y_lower, 0), (y_first, 1))], first
 
 
@@ -621,12 +622,14 @@
     )(here, *(array for array, _ in both), *(array for pair in split for array, _ in pair), *after)
 
 
-def scatter_weights(kept, sent):
-    for bit in (1, 2):
-        terms = kept + swap(sent, bit)
-        half = terms.shape[0] // 2
-        kept, sent = terms[:half], terms[half:]
-    return kept, swap(sent, 4)
+def scatter_weights(here, kept, sent, after):
+    rows = kept.shape[0] // 4
+    received = swap(sent, 1)
+    pieces = [
+        sum_call(here, rows, [(kept, place), (received, place)], dtype=F32) for place in range(4)
+    ]
+    terms = [pieces[0]] + [swap(piece, bits) for piece, bits in zip(pieces[1:], SWAP_ORDER[1:4])]
+    return sum_call(here, rows, [(term, 0) for term in terms], after=after)
 
 
 def level_weights(here, value, after):
@@ -680,24 +683,25 @@
     factor = float(rows * n_row * n_col) ** -0.5
     weight_args = (here, nodes, message, act, gpre_b, gproj, cotangent, w_in, vec)
     if paired:
-        halves = ((1, 3, 5, 7), (0, 2, 4, 6))
+        halves = ((14, 15, 6, 11), (2, 3, 7, 10), (0, 1, 4, 5, 8, 9, 12, 13))
         grads = [gather_line(gmsgs[0])]
-        kept, sent, direct = weight_call(factor, n_row, *weight_args, ())
-        row_weights = scatter_weights(kept, sent)
+        kept, sent, direct = weight_call(factor, n_row, *weight_args, (grads[0][1], grads[0][2]))
         near_grads, token = tile_grad_call(
             *known, [grads[0][:2]], pieces, tile_local.shape, rows, (3, 2), after=(grads[0][3], grads[0][4])
         )
-        row_weights = sum_call(here, kept.shape[0] // 4, [(term, 0) for term in row_weights], after=(token,))
-        odd, even = back_call(*known, grads[0], tile_local, total, gathered, halves, (row_weights,))
-        other = swap(odd, 1)
-        arrived, first = reduce_square(here, even, other, rows)
-        all_weights = level_weights(here, row_weights, first)
+        row_weights = scatter_weights(here, kept, sent, (token,))
+        urgent, rest, even = back_call(
+            *known, grads[0], tile_local, total, gathered, halves, (row_weights,)
+        )
+        urgent, rest = swap(urgent, 1), swap(rest, 1)
+        arrived, first = reduce_square(here, even, urgent, rest, rows)
+        grad_tiles, token = tile_grad_call(
+            *known, grads, pieces, tile_local.shape, rows, (1, 0), near_grads, first
+        )
+        all_weights = level_weights(here, row_weights, (token,))
         joint = jnp.concatenate([all_weights] + [swap(all_weights, bits) for bits in (2, 4, 6)], axis=0)
         weights = unpack_call(here, joint, swap(joint, 1), width)
-        grad_tiles, _ = tile_grad_call(
-            *known, grads, pieces, tile_local.shape, rows, (1, 0), near_grads, first
-        )
-        grad_nodes = sum_call(here, rows, [(direct, 0), (even, 0), (other, 0)], split=arrived)
+        grad_nodes = sum_call(here, rows, [(direct, 0), (even, 0), (rest, 0)], split=arrived)
     else:
         grads = [[lax.all_gather(gmsgs[0], "col", axis=0, tiled=True)]]
         weight_terms, direct = weight_call(factor, 1, *weight_args)

time: 161 us -> 158 us (0.981)
  Pallas kernels: 43.2 us -> 39.4 us
  starting transfers between devices: 49.2 us -> 47.5 us
    ppermute x6, starting transfers between devices: 24.1 us -> 20.5 us  [outer_swap(): return lax.ppermute(value, 'col', [(0, 1), (1, 0), (2, 3), (3, 2)])]
    ppermute x6, waiting for transfers between devices: 36.3 us -> 39.3 us  [outer_swap(): return lax.ppermute(value, 'col', [(0, 1), (1, 0), (2, 3), (3, 2)])]
    ppermute x3, starting transfers between devices: 4.73 us -> 6.64 us  [turn(): return lax.ppermute(value, 'col', [(i, (i + by) % 4) for i in range(4)])]
    ppermute x3, waiting for transfers between devices: 3.39 us -> 1.71 us  [turn(): return lax.ppermute(value, 'col', [(i, (i + by) % 4) for i in range(4)])]
    pallas_call x2, Pallas kernels: 11.3 us -> 9.67 us  [tile_grad_call(): pl.pallas_call(functools.partial(tile_grad_kernel, rows, slots, len(grads...]
    ppermute x25 -> x27, starting transfers between devices: 19.7 us -> 20.2 us  [swap(): return lax.ppermute(value, 'row', [(i, i ^ bit) for i in range(8)])]
    ppermute x25 -> x27, waiting for transfers between devices: 25.1 us -> 24.7 us  [swap(): return lax.ppermute(value, 'row', [(i, i ^ bit) for i in range(8)])]
  transfers between devices with their start and end apart: 38 -> 40, of which waited for: 18 -> 20; matrix products, arithmetic and copies ran while one was open for 1% -> 1% of each run, Pallas kernels for 16% -> 15%
where the time goes in v11:
time: 158 us; the launch traced here: 157 us
  waiting for transfers between devices  65.7 us (42%)
  starting transfers between devices  47.5 us (30%)
  Pallas kernels  39.4 us (25%)
  local copies, waits for them, and re-layouts  3.31 us (2%)
    ppermute x6, waiting for transfers between devices, outer_swap(): return lax.ppermute(value, 'col', [(0, 1), (1, 0), (2, 3), (3, 2)])  39.3 us
    ppermute x27, waiting for transfers between devices, swap(): return lax.ppermute(value, 'row', [(i, i ^ bit) for i in range(8)])  24.7 us
    ppermute x6, starting transfers between devices, outer_swap(): return lax.ppermute(value, 'col', [(0, 1), (1, 0), (2, 3), (3, 2)])  20.5 us
    ppermute x27, starting transfers between devices, swap(): return lax.ppermute(value, 'row', [(i, i ^ bit) for i in range(8)])  20.2 us
    pallas_call x3, Pallas kernels, forward_call(): pl.pallas_call(functools.partial(forward_kernel, outputs, len(pieces), pa...  15 us
    pallas_call x2, Pallas kernels, tile_grad_call(): pl.pallas_call(functools.partial(tile_grad_kernel, rows, slots, len(grads...  9.67 us
    ppermute x3, starting transfers between devices, turn(): return lax.ppermute(value, 'col', [(i, (i + by) % 4) for i in range(4)])  6.64 us
    pallas_call x1, Pallas kernels, back_call(): pl.pallas_call(functools.partial(back_kernel, rows, slots, len(grads), le...  6.15 us
  transfers between devices with their start and end apart: 40, of which 20 were waited for; matrix products, arithmetic and copies ran while one was open for 1% of the time, Pallas kernels for 15%

profile of v11, /device:TPU:0, one launch (start us, length us, event | category | flops | bytes accessed | tf_op | source)
XLA Modules:
  0.0 157.4 jit_solution(1652484472943860356)
XLA Ops:
  0.6 0.5 collective-permute-start
  1.1 1.1 fusion
  2.2 2.6 %collective-permute-start.1 = (bf16[512,256]{1,0:T(8,128)(2,1)S(1)}, bf16[512,256]{1,0:T(8,128)(2,1)S(1)}, u32[]{:S(2)}, u32[]{:S(2)}) collective-permute-start(bf16[512,256]{1,0:T(8,128)(2,1)S(1)} %get-tuple-element.57), channel_id=1, source_target_pairs={{0,8},{4,12},{8,0},{12,4},{16,24},{20,28},{24,16},{28,20},{1,9},{5... | collective-permute-start | bytes 786440 | tf_op jit(solution)/shard_map/ppermute | solution.py:530
  4.8 1.5 collective-permute-start.5
  6.3 0.5 collective-permute-start.2
  6.9 5.0 %collective-permute-done.1.refs_2_.refs_4_.refs_8_ = bf16[512,256]{1,0:T(8,128)(2,1)S(1)} collective-permute-done((bf16[512,256]{1,0:T(8,128)(2,1)S(1)}, bf16[512,256]{1,0:T(8,128)(2,1)S(1)}, u32[]{:S(2)}, u32[]{:S(2)}) %collective-permute-start.1) | collective-permute-done | bytes 262176 | tf_op jit(solution)/shard_map/ppermute | solution.py:530
  11.9 2.0 %collective-permute-done.5.refs_6_.refs_8_.refs_12_ = bf16[512,256]{1,0:T(8,128)(2,1)S(1)} collective-permute-done((bf16[512,256]{1,0:T(8,128)(2,1)S(1)}, bf16[512,256]{1,0:T(8,128)(2,1)S(1)}, u32[]{:S(2)}, u32[]{:S(2)}) %collective-permute-start.5) | collective-permute-done | bytes 262176 | tf_op jit(solution)/shard_map/ppermute | solution.py:530
  14.0 3.6 %collective-permute-done.2.refs_3_.refs_5_.refs_9_ = bf16[512,256]{1,0:T(8,128)(2,1)S(1)} collective-permute-done((bf16[512,256]{1,0:T(8,128)(2,1)S(1)}, bf16[512,256]{1,0:T(8,128)(2,1)S(1)}, u32[]{:S(2)}, u32[]{:S(2)}) %collective-permute-start.2) | collective-permute-done | bytes 262176 | tf_op jit(solution)/shard_map/ppermute | solution.py:530
  17.6 2.0 %collective-permute-start.10 = (bf16[512,256]{1,0:T(8,128)(2,1)S(1)}, bf16[512,256]{1,0:T(8,128)(2,1)S(1)}, u32[]{:S(2)}, u32[]{:S(2)}) collective-permute-start(bf16[512,256]{1,0:T(8,128)(2,1)S(1)} %collective-permute-done.2.refs_3_.refs_5_.refs_9_), channel_id=1, source_target_pairs={{0,16},{4,20},{8,24},{12,28},{16,0},{20,4},{24,8},{28,12},{1,17},{... | collective-permute-start | bytes 786440 | tf_op jit(solution)/shard_map/ppermute | solution.py:530
  19.6 0.5 collective-permute-start.7
  20.2 2.8 %collective-permute-done.9.refs_10_.refs_12_.refs_16_ = bf16[512,256]{1,0:T(8,128)(2,1)S(1)} collective-permute-done((bf16[512,256]{1,0:T(8,128)(2,1)S(1)}, bf16[512,256]{1,0:T(8,128)(2,1)S(1)}, u32[]{:S(2)}, u32[]{:S(2)}) %collective-permute-start.9) | collective-permute-done | bytes 262176 | tf_op jit(solution)/shard_map/ppermute | solution.py:530
  23.0 2.5 %collective-permute-done.10.refs_11_.refs_13_.refs_17_ = bf16[512,256]{1,0:T(8,128)(2,1)S(1)} collective-permute-done((bf16[512,256]{1,0:T(8,128)(2,1)S(1)}, bf16[512,256]{1,0:T(8,128)(2,1)S(1)}, u32[]{:S(2)}, u32[]{:S(2)}) %collective-permute-start.10) | collective-permute-done | bytes 262176 | tf_op jit(solution)/shard_map/ppermute | solution.py:530
  25.6 1.6 %collective-permute-done.12.refs_13_.refs_15_.refs_19_ = bf16[512,256]{1,0:T(8,128)(2,1)} collective-permute-done((bf16[512,256]{1,0:T(8,128)(2,1)S(1)}, bf16[512,256]{1,0:T(8,128)(2,1)}, u32[]{:S(2)}, u32[]{:S(2)}) %collective-permute-start.12) | collective-permute-done | bytes 262176 | tf_op jit(solution)/shard_map/ppermute | solution.py:530
  27.3 4.8 %partial_messages.4.refs_1_ = bf16[1024,256]{1,0:T(8,128)(2,1)} custom-call(s32[1]{0:T(128)} %bitcast.here.refs_0_, s32[4,32]{1,0:T(4,128)} %bitcast.17, s32[32]{0:T(128)} %bitcast.23, bf16[1024,256]{1,0:T(8,128)(2,1)} %refs_6_.1, bf16[1024,256]{1,0:T(8,128)(2,1)} %copy-done.2, bf16[512,256]{1,0:T(8,128)(2,1)} %copy-done.4, bf16[512,256]{1,0:T(8,128)(2,1)} %copy-done.8, ...), custom_call_target="tpu_custom_call" | custom-call | flops 1048576 | bytes 65536 | tf_op jit(solution)/shard_map/partial_messages/pallas_call | solution.py:132
  32.0 1.7 %collective-permute-start.13 = (bf16[1024,256]{1,0:T(8,128)(2,1)}, bf16[1024,256]{1,0:T(8,128)(2,1)S(1)}, u32[]{:S(2)}, u32[]{:S(2)}) collective-permute-start(bf16[1024,256]{1,0:T(8,128)(2,1)} %partial_messages.4.refs_1_), channel_id=1, source_target_pairs={{0,1},{1,0},{2,3},{3,2},{4,5},{5,4},{6,7},{7,6},{8,9},{9,8},{10,11... | collective-permute-start | bytes 1572872 | tf_op jit(solution)/shard_map/ppermute | solution.py:534
  33.7 4.7 %partial_messages.5.refs_1_ = bf16[1024,256]{1,0:T(8,128)(2,1)} custom-call(s32[1]{0:T(128)} %bitcast.here.refs_0_, s32[4,32]{1,0:T(4,128)} %bitcast.18, s32[32]{0:T(128)} %bitcast.24, bf16[1024,256]{1,0:T(8,128)(2,1)} %refs_6_.1, bf16[1024,256]{1,0:T(8,128)(2,1)} %copy-done.2, bf16[512,256]{1,0:T(8,128)(2,1)} %copy-done.4, bf16[512,256]{1,0:T(8,128)(2,1)} %copy-done.8, ...), custom_call_target="tpu_custom_call" | custom-call | flops 1048576 | bytes 65536 | tf_op jit(solution)/shard_map/partial_messages/pallas_call | solution.py:132
  38.5 0.5 collective-permute-start.16
  39.0 8.1 %collective-permute-done.13.refs_2_ = bf16[1024,256]{1,0:T(8,128)(2,1)S(1)} collective-permute-done((bf16[1024,256]{1,0:T(8,128)(2,1)}, bf16[1024,256]{1,0:T(8,128)(2,1)S(1)}, u32[]{:S(2)}, u32[]{:S(2)}) %collective-permute-start.13) | collective-permute-done | bytes 524320 | tf_op jit(solution)/shard_map/ppermute | solution.py:534
  47.1 0.2 sum_terms.14
  47.4 5.5 %partial_messages.3 = (bf16[1024,256]{1,0:T(8,128)(2,1)}, bf16[1024,256]{1,0:T(8,128)(2,1)}) custom-call(s32[1]{0:T(128)} %bitcast.here.refs_0_, s32[4,32]{1,0:T(4,128)} %bitcast.19, s32[32]{0:T(128)} %bitcast.25, bf16[1024,256]{1,0:T(8,128)(2,1)} %refs_6_.1, bf16[1024,256]{1,0:T(8,128)(2,1)} %copy-done.2, bf16[512,256]{1,0:T(8,128)(2,1)} %copy-done.4, ...), custom_call_target="tpu_custom_call" | custom-call | flops 1048576 | bytes 65536 | tf_op jit(solution)/shard_map/partial_messages/pallas_call | solution.py:132
  53.0 4.5 %collective-permute-done.16.refs_2_ = bf16[1024,256]{1,0:T(8,128)(2,1)S(1)} collective-permute-done((bf16[1024,256]{1,0:T(8,128)(2,1)}, bf16[1024,256]{1,0:T(8,128)(2,1)S(1)}, u32[]{:S(2)}, u32[]{:S(2)}) %collective-permute-start.16) | collective-permute-done | bytes 524320 | tf_op jit(solution)/shard_map/ppermute | solution.py:534
  57.5 0.2 sum_terms.16
  57.8 1.0 copy-done.30
  58.8 0.2 sum_terms.15
  59.1 3.7 %collective-permute-start.15 = (bf16[1024,256]{1,0:T(8,128)(2,1)S(1)}, bf16[1024,256]{1,0:T(8,128)(2,1)S(1)}, u32[]{:S(2)}, u32[]{:S(2)}) collective-permute-start(bf16[1024,256]{1,0:T(8,128)(2,1)S(1)} %sum_terms.15), channel_id=1, source_target_pairs={{0,1},{1,0},{2,3},{3,2},{4,5},{5,4},{6,7},{7,6},{8,9},{9,8},{10,11... | collective-permute-start | bytes 1572872 | tf_op jit(solution)/shard_map/ppermute | solution.py:534
  62.7 10.7 %collective-permute-done.15.refs_1_ = bf16[1024,256]{1,0:T(8,128)(2,1)S(1)} collective-permute-done((bf16[1024,256]{1,0:T(8,128)(2,1)S(1)}, bf16[1024,256]{1,0:T(8,128)(2,1)S(1)}, u32[]{:S(2)}, u32[]{:S(2)}) %collective-permute-start.15) | collective-permute-done | bytes 524320 | tf_op jit(solution)/shard_map/ppermute | solution.py:534
  73.5 1.0 copy-done.31
  74.5 3.1 %mlp.1 = (bf16[1024,256]{1,0:T(8,128)(2,1)}, bf16[1024,256]{1,0:T(8,128)(2,1)S(1)}, bf16[1024,256]{1,0:T(8,128)(2,1)S(1)}, bf16[1024,256]{1,0:T(8,128)(2,1)S(1)}...) custom-call(s32[1]{0:T(128)} %bitcast.here.refs_0_, ...), custom_call_target="tpu_custom_call" | custom-call | flops 1048576 | bytes 65536 | tf_op jit(solution)/shard_map/mlp/pallas_call | solution.py:226
  77.7 1.7 %collective-permute-start.18 = (bf16[1024,256]{1,0:T(8,128)(2,1)S(1)}, bf16[1024,256]{1,0:T(8,128)(2,1)S(1)}, u32[]{:S(2)}, u32[]{:S(2)}) collective-permute-start(bf16[1024,256]{1,0:T(8,128)(2,1)S(1)} %get-tuple-element.36.refs_0_), channel_id=1, source_target_pairs={{0,1},{1,0},{2,3},{3,2},{4,5},{5,4},{6,7},{7,6},{8,9},{9,8},{10,11... | collective-permute-start | bytes 1572872 | tf_op jit(solution)/shard_map/ppermute | solution.py:534
  79.4 10.1 %collective-permute-done.18.refs_0_.refs_1_ = bf16[1024,256]{1,0:T(8,128)(2,1)S(1)} collective-permute-done((bf16[1024,256]{1,0:T(8,128)(2,1)S(1)}, bf16[1024,256]{1,0:T(8,128)(2,1)S(1)}, u32[]{:S(2)}, u32[]{:S(2)}) %collective-permute-start.18) | collective-permute-done | bytes 524320 | tf_op jit(solution)/shard_map/ppermute | solution.py:534
  89.6 1.5 weight_grads.1
  91.2 0.6 collective-permute-start.23
  91.7 4.1 %collective-permute-start.20 = (bf16[1024,256]{1,0:T(8,128)(2,1)S(1)}, bf16[1024,256]{1,0:T(8,128)(2,1)S(1)}, u32[]{:S(2)}, u32[]{:S(2)}) collective-permute-start(bf16[1024,256]{1,0:T(8,128)(2,1)S(1)} %collective-permute-done.19.refs_1_.refs_2_), channel_id=1, source_target_pairs={{0,1},{1,0},{2,3},{3,2},{4,5},{5,4},{6,7},{7,6},{8,9},{9,8},{10,11... | collective-permute-start | bytes 1572872 | tf_op jit(solution)/shard_map/ppermute | solution.py:534
  95.8 8.9 %collective-permute-start.22 = (bf16[1024,256]{1,0:T(8,128)(2,1)S(1)}, bf16[1024,256]{1,0:T(8,128)(2,1)S(1)}, u32[]{:S(2)}, u32[]{:S(2)}) collective-permute-start(bf16[1024,256]{1,0:T(8,128)(2,1)S(1)} %collective-permute-done.21.refs_17_.refs_4_), channel_id=1, source_target_pairs={{0,1},{1,0},{2,3},{3,2},{4,5},{5,4},{6,7},{7,6},{8,9},{9,8},{10,11... | collective-permute-start | bytes 1572872 | tf_op jit(solution)/shard_map/ppermute | solution.py:534
  104.7 1.6 %collective-permute-start.24 = (f32[112,256]{1,0:T(8,128)S(1)}, f32[112,256]{1,0:T(8,128)S(1)}, u32[]{:S(2)}, u32[]{:S(2)}) collective-permute-start(f32[112,256]{1,0:T(8,128)S(1)} %sum_terms.18), channel_id=1, source_target_pairs={{0,16},{4,20},{8,24},{12,28},{16,0},{20,4},{24,8},{28,12},{1,17},{... | collective-permute-start | bytes 344072 | tf_op jit(solution)/shard_map/ppermute | solution.py:530
  106.3 1.6 %collective-permute-start.25 = (f32[112,256]{1,0:T(8,128)S(1)}, f32[112,256]{1,0:T(8,128)S(1)}, u32[]{:S(2)}, u32[]{:S(2)}) collective-permute-start(f32[112,256]{1,0:T(8,128)S(1)} %sum_terms.19), channel_id=1, source_target_pairs={{0,8},{4,12},{8,0},{12,4},{16,24},{20,28},{24,16},{28,20},{1,9},{5... | collective-permute-start | bytes 344072 | tf_op jit(solution)/shard_map/ppermute | solution.py:530
  108.0 0.5 collective-permute-start.26
  108.7 5.0 %tile_grads.2 = (bf16[128,128,128]{2,1,0:T(8,128)(2,1)}, f32[8,128]{1,0:T(8,128)S(1)}) custom-call(s32[1]{0:T(128)} %bitcast.here.refs_0_, s32[4,32]{1,0:T(4,128)S(1)} %bitcast.20, s32[32]{0:T(128)S(1)} %bitcast.26, bf16[1024,256]{1,0:T(8,128)(2,1)S(1)} %get-tuple-element.36.refs_0_, bf16[1024,256]{1,0:T(8,128)(2,1)S(1)} %collective-permute-done.18.refs_0_.refs_1_, ...), custom_call_target="tpu_custom_call" | custom-call | flops 1048576 | bytes 65536 | tf_op jit(solution)/shard_map/tile_grads/pallas_call | solution.py:502
  113.7 5.8 %collective-permute-done.22.refs_5_ = bf16[1024,256]{1,0:T(8,128)(2,1)S(1)} collective-permute-done((bf16[1024,256]{1,0:T(8,128)(2,1)S(1)}, bf16[1024,256]{1,0:T(8,128)(2,1)S(1)}, u32[]{:S(2)}, u32[]{:S(2)}) %collective-permute-start.22) | collective-permute-done | bytes 524320 | tf_op jit(solution)/shard_map/ppermute | solution.py:534
  119.5 6.2 %back_terms.1 = (bf16[2048,256]{1,0:T(8,128)(2,1)S(1)}, bf16[2048,256]{1,0:T(8,128)(2,1)S(1)}, bf16[4096,256]{1,0:T(8,128)(2,1)S(1)}) custom-call(s32[1]{0:T(128)} %bitcast.here.refs_0_, s32[4,32]{1,0:T(4,128)S(1)} %bitcast.21, s32[32]{0:T(128)S(1)} %bitcast.27, bf16[1024,256]{1,0:T(8,128)(2,1)S(1)} %get-tuple-element.36.refs_0_, ...), custom_call_target="tpu_custom_call" | custom-call | flops 1048576 | bytes 65536 | tf_op jit(solution)/shard_map/back_terms/pallas_call | solution.py:402
  125.7 0.8 collective-permute-start.28
  126.6 2.2 %collective-permute-done.28.refs_2_ = bf16[2048,256]{1,0:T(8,128)(2,1)S(1)} collective-permute-done((bf16[2048,256]{1,0:T(8,128)(2,1)S(1)}, bf16[2048,256]{1,0:T(8,128)(2,1)S(1)}, u32[]{:S(2)}, u32[]{:S(2)}) %collective-permute-start.28) | collective-permute-done | bytes 1048608 | tf_op jit(solution)/shard_map/ppermute | solution.py:530
  128.8 0.2 sum_terms.23.refs_22_
  129.0 0.2 sum_terms.22.refs_21_
  129.2 2.0 %collective-permute-start.29 = (bf16[1024,256]{1,0:T(8,128)(2,1)S(1)}, bf16[1024,256]{1,0:T(8,128)(2,1)S(1)}, u32[]{:S(2)}, u32[]{:S(2)}) collective-permute-start(bf16[1024,256]{1,0:T(8,128)(2,1)S(1)} %sum_terms.22.refs_21_), channel_id=1, source_target_pairs={{0,8},{4,12},{8,0},{12,4},{16,24},{20,28},{24,16},{28,20},{1,9},{5... | collective-permute-start | bytes 1572872 | tf_op jit(solution)/shard_map/ppermute | solution.py:530
  131.3 3.6 %collective-permute-start.33 = (bf16[112,256]{1,0:T(8,128)(2,1)S(1)}, bf16[112,256]{1,0:T(8,128)(2,1)S(1)}, u32[]{:S(2)}, u32[]{:S(2)}) collective-permute-start(bf16[112,256]{1,0:T(8,128)(2,1)S(1)} %sum_terms.21.refs_7_.refs_1_), channel_id=1, source_target_pairs={{0,1},{1,2},{2,3},{3,0},{4,5},{5,6},{6,7},{7,4},{8,9},{9,10},{10,1... | collective-permute-start | bytes 172040 | tf_op jit(solution)/shard_map/ppermute | solution.py:538
  134.9 0.7 collective-permute-start.34
  135.6 1.7 %collective-permute-done.33.refs_2_ = bf16[112,256]{1,0:T(8,128)(2,1)S(1)} collective-permute-done((bf16[112,256]{1,0:T(8,128)(2,1)S(1)}, bf16[112,256]{1,0:T(8,128)(2,1)S(1)}, u32[]{:S(2)}, u32[]{:S(2)}) %collective-permute-start.33) | collective-permute-done | bytes 57376 | tf_op jit(solution)/shard_map/ppermute | solution.py:538
  137.3 2.4 %collective-permute-start.35 = (bf16[112,256]{1,0:T(8,128)(2,1)S(1)}, bf16[112,256]{1,0:T(8,128)(2,1)S(1)}, u32[]{:S(2)}, u32[]{:S(2)}) collective-permute-start(bf16[112,256]{1,0:T(8,128)(2,1)S(1)} %sum_terms.21.refs_7_.refs_1_), channel_id=1, source_target_pairs={{0,3},{1,0},{2,1},{3,2},{4,7},{5,4},{6,5},{7,6},{8,11},{9,8},{10,9... | collective-permute-start | bytes 172040 | tf_op jit(solution)/shard_map/ppermute | solution.py:538
  139.6 4.7 %tile_grads.3 = (bf16[128,128,128]{2,1,0:T(8,128)(2,1)}, f32[8,128]{1,0:T(8,128)S(1)}) custom-call(s32[1]{0:T(128)} %bitcast.here.refs_0_, s32[4,32]{1,0:T(4,128)S(1)} %bitcast.22, s32[32]{0:T(128)S(1)} %bitcast.28, bf16[1024,256]{1,0:T(8,128)(2,1)S(1)} %get-tuple-element.36.refs_0_, ...), custom_call_target="tpu_custom_call", output_to_operand_aliasing={{0}: (23, {})} | custom-call | flops 1048576 | bytes 65536 | tf_op jit(solution)/shard_map/tile_grads/pallas_call | solution.py:502
  144.4 1.0 collective-permute-start.38
  145.4 1.0 collective-permute-start.37
  146.4 1.6 %collective-permute-start.36 = (bf16[112,256]{1,0:T(8,128)(2,1)S(1)}, bf16[112,256]{1,0:T(8,128)(2,1)S(1)}, u32[]{:S(2)}, u32[]{:S(2)}) collective-permute-start(bf16[112,256]{1,0:T(8,128)(2,1)S(1)} %sum_terms.27), channel_id=1, source_target_pairs={{0,8},{4,12},{8,0},{12,4},{16,24},{20,28},{24,16},{28,20},{1,9},{5... | collective-permute-start | bytes 172040 | tf_op jit(solution)/shard_map/ppermute | solution.py:530
  148.0 0.1 sum_terms.24
  148.1 0.5 collective-permute-start.31
  148.8 1.1 collective-permute-start.32
  149.8 0.3 collective-permute-done.38
  150.1 0.3 collective-permute-done.37
  150.5 0.8 collective-permute-done.36
  151.3 1.5 collective-permute-done.39.odd
  152.8 1.0 weight_unpack.1
  153.8 1.1 collective-permute-done.31.refs_5_
  154.9 0.9 collective-permute-done.32.refs_6_
  155.8 1.6 %sum_terms.26 = bf16[1024,256]{1,0:T(8,128)(2,1)} custom-call(s32[1]{0:T(128)} %bitcast.here.refs_0_, f32[1024,256]{1,0:T(8,128)S(1)} %get-tuple-element.37.refs_1_, bf16[4096,256]{1,0:T(8,128)(2,1)S(1)} %get-tuple-element.41.refs_1_.refs_2_, bf16[2048,256]{1,0:T(8,128)(2,1)S(1)} %collective-permute-done.27.refs_2_.refs_3_, ...), custom_call_target="tpu_custom_call" | custom-call | flops 1048576 | bytes 65536 | tf_op jit(solution)/shard_map/sum_terms/pallas_call | solution.py:610
  (117 shorter events, 1.2 us)
Async XLA Ops:
  0.6 18.9 %collective-permute-start = (bf16[1024,256]{1,0:T(8,128)(2,1)}, bf16[1024,256]{1,0:T(8,128)(2,1)S(1)}, u32[]{:S(2)}, u32[]{:S(2)}) collective-permute-start(bf16[1024,256]{1,0:T(8,128)(2,1)} %refs_6_.1), channel_id=1, source_target_pairs={{0,4},{4,0},{8,12},{12,8},{16,20},{20,16},{24,28},{28,24},{1,5},{5... | collective-permute-start | bytes 1572872 | tf_op jit(solution)/shard_map/ppermute | solution.py:530
  2.2 9.7 %collective-permute-start.1 = (bf16[512,256]{1,0:T(8,128)(2,1)S(1)}, bf16[512,256]{1,0:T(8,128)(2,1)S(1)}, u32[]{:S(2)}, u32[]{:S(2)}) collective-permute-start(bf16[512,256]{1,0:T(8,128)(2,1)S(1)} %get-tuple-element.57), channel_id=1, source_target_pairs={{0,8},{4,12},{8,0},{12,4},{16,24},{20,28},{24,16},{28,20},{1,9},{5... | collective-permute-start | bytes 786440 | tf_op jit(solution)/shard_map/ppermute | solution.py:530
  4.8 9.1 %collective-permute-start.5 = (bf16[512,256]{1,0:T(8,128)(2,1)S(1)}, bf16[512,256]{1,0:T(8,128)(2,1)S(1)}, u32[]{:S(2)}, u32[]{:S(2)}) collective-permute-start(bf16[512,256]{1,0:T(8,128)(2,1)S(1)} %get-tuple-element.57), channel_id=1, source_target_pairs={{0,16},{4,20},{8,24},{12,28},{16,0},{20,4},{24,8},{28,12},{1,17},{... | collective-permute-start | bytes 786440 | tf_op jit(solution)/shard_map/ppermute | solution.py:530
  6.3 11.3 %collective-permute-start.2 = (bf16[512,256]{1,0:T(8,128)(2,1)S(1)}, bf16[512,256]{1,0:T(8,128)(2,1)S(1)}, u32[]{:S(2)}, u32[]{:S(2)}) collective-permute-start(bf16[512,256]{1,0:T(8,128)(2,1)S(1)} %get-tuple-element.56), channel_id=1, source_target_pairs={{0,8},{4,12},{8,0},{12,4},{16,24},{20,28},{24,16},{28,20},{1,9},{5... | collective-permute-start | bytes 786440 | tf_op jit(solution)/shard_map/ppermute | solution.py:530
  6.8 12.7 %collective-permute-start.6 = (bf16[512,256]{1,0:T(8,128)(2,1)S(1)}, bf16[512,256]{1,0:T(8,128)(2,1)S(1)}, u32[]{:S(2)}, u32[]{:S(2)}) collective-permute-start(bf16[512,256]{1,0:T(8,128)(2,1)S(1)} %get-tuple-element.56), channel_id=1, source_target_pairs={{0,16},{4,20},{8,24},{12,28},{16,0},{20,4},{24,8},{28,12},{1,17},{... | collective-permute-start | bytes 786440 | tf_op jit(solution)/shard_map/ppermute | solution.py:530
  11.9 15.2 %copy-start.4 = (bf16[512,256]{1,0:T(8,128)(2,1)}, bf16[512,256]{1,0:T(8,128)(2,1)S(1)}, u32[]{:S(2)}) copy-start(bf16[512,256]{1,0:T(8,128)(2,1)S(1)} %collective-permute-done.1.refs_2_.refs_4_.refs_8_) | copy-start | bytes 786436
  11.9 8.1 %collective-permute-start.3 = (bf16[512,256]{1,0:T(8,128)(2,1)S(1)}, bf16[512,256]{1,0:T(8,128)(2,1)S(1)}, u32[]{:S(2)}, u32[]{:S(2)}) collective-permute-start(bf16[512,256]{1,0:T(8,128)(2,1)S(1)} %collective-permute-done.1.refs_2_.refs_4_.refs_8_), channel_id=1, source_target_pairs={{0,4},{4,0},{8,12},{12,8},{16,20},{20,16},{24,28},{28,24},{1,5},{5... | collective-permute-start | bytes 786440 | tf_op jit(solution)/shard_map/ppermute | solution.py:530
  13.9 13.2 %copy-start.6 = (bf16[512,256]{1,0:T(8,128)(2,1)}, bf16[512,256]{1,0:T(8,128)(2,1)S(1)}, u32[]{:S(2)}) copy-start(bf16[512,256]{1,0:T(8,128)(2,1)S(1)} %collective-permute-done.5.refs_6_.refs_8_.refs_12_) | copy-start | bytes 786436
  13.9 9.1 %collective-permute-start.9 = (bf16[512,256]{1,0:T(8,128)(2,1)S(1)}, bf16[512,256]{1,0:T(8,128)(2,1)S(1)}, u32[]{:S(2)}, u32[]{:S(2)}) collective-permute-start(bf16[512,256]{1,0:T(8,128)(2,1)S(1)} %collective-permute-done.5.refs_6_.refs_8_.refs_12_), channel_id=1, source_target_pairs={{0,8},{4,12},{8,0},{12,4},{16,24},{20,28},{24,16},{28,20},{1,9},{5... | collective-permute-start | bytes 786440 | tf_op jit(solution)/shard_map/ppermute | solution.py:530
  17.6 7.9 %collective-permute-start.10 = (bf16[512,256]{1,0:T(8,128)(2,1)S(1)}, bf16[512,256]{1,0:T(8,128)(2,1)S(1)}, u32[]{:S(2)}, u32[]{:S(2)}) collective-permute-start(bf16[512,256]{1,0:T(8,128)(2,1)S(1)} %collective-permute-done.2.refs_3_.refs_5_.refs_9_), channel_id=1, source_target_pairs={{0,16},{4,20},{8,24},{12,28},{16,0},{20,4},{24,8},{28,12},{1,17},{... | collective-permute-start | bytes 786440 | tf_op jit(solution)/shard_map/ppermute | solution.py:530
  19.5 6.0 %collective-permute-start.4 = (bf16[512,256]{1,0:T(8,128)(2,1)S(1)}, bf16[512,256]{1,0:T(8,128)(2,1)S(1)}, u32[]{:S(2)}, u32[]{:S(2)}) collective-permute-start(bf16[512,256]{1,0:T(8,128)(2,1)S(1)} %collective-permute-done.2.refs_3_.refs_5_.refs_9_), channel_id=1, source_target_pairs={{0,4},{4,0},{8,12},{12,8},{16,20},{20,16},{24,28},{28,24},{1,5},{5... | collective-permute-start | bytes 786440 | tf_op jit(solution)/shard_map/ppermute | solution.py:530
  19.6 5.9 %collective-permute-start.7 = (bf16[512,256]{1,0:T(8,128)(2,1)S(1)}, bf16[512,256]{1,0:T(8,128)(2,1)S(1)}, u32[]{:S(2)}, u32[]{:S(2)}) collective-permute-start(bf16[512,256]{1,0:T(8,128)(2,1)S(1)} %collective-permute-done.5.refs_6_.refs_8_.refs_12_), channel_id=1, source_target_pairs={{0,4},{4,0},{8,12},{12,8},{16,20},{20,16},{24,28},{28,24},{1,5},{5... | collective-permute-start | bytes 786440 | tf_op jit(solution)/shard_map/ppermute | solution.py:530
  20.1 5.5 %collective-permute-start.8 = (bf16[512,256]{1,0:T(8,128)(2,1)S(1)}, bf16[512,256]{1,0:T(8,128)(2,1)S(1)}, u32[]{:S(2)}, u32[]{:S(2)}) collective-permute-start(bf16[512,256]{1,0:T(8,128)(2,1)S(1)} %collective-permute-done.6.refs_7_.refs_9_.refs_13_), channel_id=1, source_target_pairs={{0,4},{4,0},{8,12},{12,8},{16,20},{20,16},{24,28},{28,24},{1,5},{5... | collective-permute-start | bytes 786440 | tf_op jit(solution)/shard_map/ppermute | solution.py:530
  23.0 2.6 %collective-permute-start.11 = (bf16[512,256]{1,0:T(8,128)(2,1)S(1)}, bf16[512,256]{1,0:T(8,128)(2,1)S(1)}, u32[]{:S(2)}, u32[]{:S(2)}) collective-permute-start(bf16[512,256]{1,0:T(8,128)(2,1)S(1)} %collective-permute-done.9.refs_10_.refs_12_.refs_16_), channel_id=1, source_target_pairs={{0,4},{4,0},{8,12},{12,8},{16,20},{20,16},{24,28},{28,24},{1,5},{5... | collective-permute-start | bytes 786440 | tf_op jit(solution)/shard_map/ppermute | solution.py:530
  25.5 1.7 %collective-permute-start.12 = (bf16[512,256]{1,0:T(8,128)(2,1)S(1)}, bf16[512,256]{1,0:T(8,128)(2,1)}, u32[]{:S(2)}, u32[]{:S(2)}) collective-permute-start(bf16[512,256]{1,0:T(8,128)(2,1)S(1)} %collective-permute-done.10.refs_11_.refs_13_.refs_17_), channel_id=1, source_target_pairs={{0,4},{4,0},{8,12},{12,8},{16,20},{20,16},{24,28},{28,24},{1,5},{5... | collective-permute-start | bytes 786440 | tf_op jit(solution)/shard_map/ppermute | solution.py:530
  32.0 15.1 %copy-start.28 = (bf16[1024,256]{1,0:T(8,128)(2,1)S(1)}, bf16[1024,256]{1,0:T(8,128)(2,1)}, u32[]{:S(2)}) copy-start(bf16[1024,256]{1,0:T(8,128)(2,1)} %partial_messages.4.refs_1_) | copy-start | bytes 1572868
  32.0 15.0 %collective-permute-start.13 = (bf16[1024,256]{1,0:T(8,128)(2,1)}, bf16[1024,256]{1,0:T(8,128)(2,1)S(1)}, u32[]{:S(2)}, u32[]{:S(2)}) collective-permute-start(bf16[1024,256]{1,0:T(8,128)(2,1)} %partial_messages.4.refs_1_), channel_id=1, source_target_pairs={{0,1},{1,0},{2,3},{3,2},{4,5},{5,4},{6,7},{7,6},{8,9},{9,8},{10,11... | collective-permute-start | bytes 1572872 | tf_op jit(solution)/shard_map/ppermute | solution.py:534
  38.5 19.0 %collective-permute-start.16 = (bf16[1024,256]{1,0:T(8,128)(2,1)}, bf16[1024,256]{1,0:T(8,128)(2,1)S(1)}, u32[]{:S(2)}, u32[]{:S(2)}) collective-permute-start(bf16[1024,256]{1,0:T(8,128)(2,1)} %partial_messages.5.refs_1_), channel_id=1, source_target_pairs={{0,1},{1,0},{2,3},{3,2},{4,5},{5,4},{6,7},{7,6},{8,9},{9,8},{10,11... | collective-permute-start | bytes 1572872 | tf_op jit(solution)/shard_map/ppermute | solution.py:534
  47.3 26.2 %copy-start.1 = (bf16[1024,256]{1,0:T(8,128)(2,1)S(1)}, bf16[1024,256]{1,0:T(8,128)(2,1)}, u32[]{:S(2)}) copy-start(bf16[1024,256]{1,0:T(8,128)(2,1)} %refs_6_.1) | copy-start | bytes 1572868
  47.3 26.2 %copy-start.26 = (bf16[1024,256]{1,0:T(8,128)(2,1)S(1)}, bf16[1024,256]{1,0:T(8,128)(2,1)}, u32[]{:S(2)}) copy-start(bf16[1024,256]{1,0:T(8,128)(2,1)} %cot.3) | copy-start | bytes 1572868
  47.3 26.1 %copy-start.29 = (bf16[512,256]{1,0:T(8,128)(2,1)S(1)}, bf16[512,256]{1,0:T(8,128)(2,1)}, u32[]{:S(2)}) copy-start(bf16[512,256]{1,0:T(8,128)(2,1)} %w_in.1) | copy-start | bytes 786436
  47.3 26.1 %copy-start.32 = (bf16[256,256]{1,0:T(8,128)(2,1)S(1)}, bf16[256,256]{1,0:T(8,128)(2,1)}, u32[]{:S(2)}) copy-start(bf16[256,256]{1,0:T(8,128)(2,1)} %refs_5_.1) | copy-start | bytes 393220
  47.3 26.1 %copy-start.35 = (f32[256]{0:T(256)S(1)}, f32[256]{0:T(256)}, u32[]{:S(2)}) copy-start(f32[256]{0:T(256)} %param.15) | copy-start | bytes 3076
  47.3 26.1 %copy-start.36 = (f32[256]{0:T(256)S(1)}, f32[256]{0:T(256)}, u32[]{:S(2)}) copy-start(f32[256]{0:T(256)} %param.17) | copy-start | bytes 3076
  47.4 26.1 %copy-start.37 = (f32[256]{0:T(256)S(1)}, f32[256]{0:T(256)}, u32[]{:S(2)}) copy-start(f32[256]{0:T(256)} %param.18) | copy-start | bytes 3076
  47.4 10.4 %collective-permute-start.14 = (bf16[1024,256]{1,0:T(8,128)(2,1)S(1)}, bf16[1024,256]{1,0:T(8,128)(2,1)S(1)}, u32[]{:S(2)}, u32[]{:S(2)}) collective-permute-start(bf16[1024,256]{1,0:T(8,128)(2,1)S(1)} %sum_terms.14), channel_id=1, source_target_pairs={{0,4},{1,2},{2,1},{3,7},{4,0},{5,6},{6,5},{7,3},{8,12},{9,10},{10,... | collective-permute-start | bytes 1572872 | tf_op jit(solution)/shard_map/ppermute | solution.py:547
  57.7 5.0 %collective-permute-start.17 = (bf16[1024,256]{1,0:T(8,128)(2,1)S(1)}, bf16[1024,256]{1,0:T(8,128)(2,1)S(1)}, u32[]{:S(2)}, u32[]{:S(2)}) collective-permute-start(bf16[1024,256]{1,0:T(8,128)(2,1)S(1)} %sum_terms.16), channel_id=1, source_target_pairs={{0,4},{1,2},{2,1},{3,7},{4,0},{5,6},{6,5},{7,3},{8,12},{9,10},{10,... | collective-permute-start | bytes 1572872 | tf_op jit(solution)/shard_map/ppermute | solution.py:547
  59.1 14.4 %collective-permute-start.15 = (bf16[1024,256]{1,0:T(8,128)(2,1)S(1)}, bf16[1024,256]{1,0:T(8,128)(2,1)S(1)}, u32[]{:S(2)}, u32[]{:S(2)}) collective-permute-start(bf16[1024,256]{1,0:T(8,128)(2,1)S(1)} %sum_terms.15), channel_id=1, source_target_pairs={{0,1},{1,0},{2,3},{3,2},{4,5},{5,4},{6,7},{7,6},{8,9},{9,8},{10,11... | collective-permute-start | bytes 1572872 | tf_op jit(solution)/shard_map/ppermute | solution.py:534
  77.7 11.8 %collective-permute-start.18 = (bf16[1024,256]{1,0:T(8,128)(2,1)S(1)}, bf16[1024,256]{1,0:T(8,128)(2,1)S(1)}, u32[]{:S(2)}, u32[]{:S(2)}) collective-permute-start(bf16[1024,256]{1,0:T(8,128)(2,1)S(1)} %get-tuple-element.36.refs_0_), channel_id=1, source_target_pairs={{0,1},{1,0},{2,3},{3,2},{4,5},{5,4},{6,7},{7,6},{8,9},{9,8},{10,11... | collective-permute-start | bytes 1572872 | tf_op jit(solution)/shard_map/ppermute | solution.py:534
  79.4 10.1 %collective-permute-start.19 = (bf16[1024,256]{1,0:T(8,128)(2,1)S(1)}, bf16[1024,256]{1,0:T(8,128)(2,1)S(1)}, u32[]{:S(2)}, u32[]{:S(2)}) collective-permute-start(bf16[1024,256]{1,0:T(8,128)(2,1)S(1)} %get-tuple-element.36.refs_0_), channel_id=1, source_target_pairs={{0,4},{1,2},{2,1},{3,7},{4,0},{5,6},{6,5},{7,3},{8,12},{9,10},{10,... | collective-permute-start | bytes 1572872 | tf_op jit(solution)/shard_map/ppermute | solution.py:547
  89.5 6.3 %collective-permute-start.21 = (bf16[1024,256]{1,0:T(8,128)(2,1)S(1)}, bf16[1024,256]{1,0:T(8,128)(2,1)S(1)}, u32[]{:S(2)}, u32[]{:S(2)}) collective-permute-start(bf16[1024,256]{1,0:T(8,128)(2,1)S(1)} %collective-permute-done.18.refs_0_.refs_1_), channel_id=1, source_target_pairs={{0,4},{1,2},{2,1},{3,7},{4,0},{5,6},{6,5},{7,3},{8,12},{9,10},{10,... | collective-permute-start | bytes 1572872 | tf_op jit(solution)/shard_map/ppermute | solution.py:547
  89.5 19.1 %copy-start.3 = (bf16[1024,256]{1,0:T(8,128)(2,1)S(1)}, bf16[1024,256]{1,0:T(8,128)(2,1)}, u32[]{:S(2)}) copy-start(bf16[1024,256]{1,0:T(8,128)(2,1)} %copy-done.2) | copy-start | bytes 1572868
  89.5 19.1 %copy-start.5 = (bf16[512,256]{1,0:T(8,128)(2,1)S(1)}, bf16[512,256]{1,0:T(8,128)(2,1)}, u32[]{:S(2)}) copy-start(bf16[512,256]{1,0:T(8,128)(2,1)} %copy-done.4) | copy-start | bytes 786436
  89.5 19.1 %copy-start.7 = (bf16[512,256]{1,0:T(8,128)(2,1)S(1)}, bf16[512,256]{1,0:T(8,128)(2,1)}, u32[]{:S(2)}) copy-start(bf16[512,256]{1,0:T(8,128)(2,1)} %copy-done.6) | copy-start | bytes 786436
  89.5 19.1 %copy-start.9 = (bf16[512,256]{1,0:T(8,128)(2,1)S(1)}, bf16[512,256]{1,0:T(8,128)(2,1)}, u32[]{:S(2)}) copy-start(bf16[512,256]{1,0:T(8,128)(2,1)} %copy-done.8) | copy-start | bytes 786436
  89.5 19.1 %copy-start.11 = (bf16[512,256]{1,0:T(8,128)(2,1)S(1)}, bf16[512,256]{1,0:T(8,128)(2,1)}, u32[]{:S(2)}) copy-start(bf16[512,256]{1,0:T(8,128)(2,1)} %copy-done.10) | copy-start | bytes 786436
  89.5 19.1 %copy-start.13 = (bf16[512,256]{1,0:T(8,128)(2,1)S(1)}, bf16[512,256]{1,0:T(8,128)(2,1)}, u32[]{:S(2)}) copy-start(bf16[512,256]{1,0:T(8,128)(2,1)} %copy-done.12) | copy-start | bytes 786436
  89.5 19.1 %copy-start.15 = (bf16[512,256]{1,0:T(8,128)(2,1)S(1)}, bf16[512,256]{1,0:T(8,128)(2,1)}, u32[]{:S(2)}) copy-start(bf16[512,256]{1,0:T(8,128)(2,1)} %copy-done.14) | copy-start | bytes 786436
  89.6 19.1 %copy-start.17 = (bf16[512,256]{1,0:T(8,128)(2,1)S(1)}, bf16[512,256]{1,0:T(8,128)(2,1)}, u32[]{:S(2)}) copy-start(bf16[512,256]{1,0:T(8,128)(2,1)} %copy-done.16) | copy-start | bytes 786436
  89.6 19.1 %copy-start.19 = (bf16[512,256]{1,0:T(8,128)(2,1)S(1)}, bf16[512,256]{1,0:T(8,128)(2,1)}, u32[]{:S(2)}) copy-start(bf16[512,256]{1,0:T(8,128)(2,1)} %copy-done.18) | copy-start | bytes 786436
  89.6 19.1 %copy-start.21 = (bf16[512,256]{1,0:T(8,128)(2,1)S(1)}, bf16[512,256]{1,0:T(8,128)(2,1)}, u32[]{:S(2)}) copy-start(bf16[512,256]{1,0:T(8,128)(2,1)} %copy-done.20) | copy-start | bytes 786436
  89.6 19.1 %copy-start.23 = (bf16[512,256]{1,0:T(8,128)(2,1)S(1)}, bf16[512,256]{1,0:T(8,128)(2,1)}, u32[]{:S(2)}) copy-start(bf16[512,256]{1,0:T(8,128)(2,1)} %copy-done.22) | copy-start | bytes 786436
  89.6 19.1 %copy-start.25 = (bf16[512,256]{1,0:T(8,128)(2,1)S(1)}, bf16[512,256]{1,0:T(8,128)(2,1)}, u32[]{:S(2)}) copy-start(bf16[512,256]{1,0:T(8,128)(2,1)} %copy-done.24) | copy-start | bytes 786436
  89.6 19.1 %copy-start.33 = (s32[32,1,4]{0,2,1:T(4,128)S(1)}, s32[32,1,4]{0,2,1:T(4,128)}, u32[]{:S(2)}) copy-start(s32[32,1,4]{0,2,1:T(4,128)} %param.12) | copy-start | bytes 1540
  89.6 19.1 %copy-start.34 = (s32[32,1]{0,1:T(1,128)S(1)}, s32[32,1]{0,1:T(1,128)}, u32[]{:S(2)}) copy-start(s32[32,1]{0,1:T(1,128)} %param.13) | copy-start | bytes 388
  91.2 13.5 %collective-permute-start.23 = (f32[448,256]{1,0:T(8,128)S(1)}, f32[448,256]{1,0:T(8,128)S(1)}, u32[]{:S(2)}, u32[]{:S(2)}) collective-permute-start(f32[448,256]{1,0:T(8,128)S(1)} %get-tuple-element.39), channel_id=1, source_target_pairs={{0,4},{4,0},{8,12},{12,8},{16,20},{20,16},{24,28},{28,24},{1,5},{5... | collective-permute-start | bytes 1376264 | tf_op jit(solution)/shard_map/ppermute | solution.py:530
  91.7 16.8 %collective-permute-start.20 = (bf16[1024,256]{1,0:T(8,128)(2,1)S(1)}, bf16[1024,256]{1,0:T(8,128)(2,1)S(1)}, u32[]{:S(2)}, u32[]{:S(2)}) collective-permute-start(bf16[1024,256]{1,0:T(8,128)(2,1)S(1)} %collective-permute-done.19.refs_1_.refs_2_), channel_id=1, source_target_pairs={{0,1},{1,0},{2,3},{3,2},{4,5},{5,4},{6,7},{7,6},{8,9},{9,8},{10,11... | collective-permute-start | bytes 1572872 | tf_op jit(solution)/shard_map/ppermute | solution.py:534
  95.8 23.7 %collective-permute-start.22 = (bf16[1024,256]{1,0:T(8,128)(2,1)S(1)}, bf16[1024,256]{1,0:T(8,128)(2,1)S(1)}, u32[]{:S(2)}, u32[]{:S(2)}) collective-permute-start(bf16[1024,256]{1,0:T(8,128)(2,1)S(1)} %collective-permute-done.21.refs_17_.refs_4_), channel_id=1, source_target_pairs={{0,1},{1,0},{2,3},{3,2},{4,5},{5,4},{6,7},{7,6},{8,9},{9,8},{10,11... | collective-permute-start | bytes 1572872 | tf_op jit(solution)/shard_map/ppermute | solution.py:534
  104.7 8.9 %collective-permute-start.24 = (f32[112,256]{1,0:T(8,128)S(1)}, f32[112,256]{1,0:T(8,128)S(1)}, u32[]{:S(2)}, u32[]{:S(2)}) collective-permute-start(f32[112,256]{1,0:T(8,128)S(1)} %sum_terms.18), channel_id=1, source_target_pairs={{0,16},{4,20},{8,24},{12,28},{16,0},{20,4},{24,8},{28,12},{1,17},{... | collective-permute-start | bytes 344072 | tf_op jit(solution)/shard_map/ppermute | solution.py:530
  106.3 7.3 %collective-permute-start.25 = (f32[112,256]{1,0:T(8,128)S(1)}, f32[112,256]{1,0:T(8,128)S(1)}, u32[]{:S(2)}, u32[]{:S(2)}) collective-permute-start(f32[112,256]{1,0:T(8,128)S(1)} %sum_terms.19), channel_id=1, source_target_pairs={{0,8},{4,12},{8,0},{12,4},{16,24},{20,28},{24,16},{28,20},{1,9},{5... | collective-permute-start | bytes 344072 | tf_op jit(solution)/shard_map/ppermute | solution.py:530
  108.0 5.8 %collective-permute-start.26 = (f32[112,256]{1,0:T(8,128)S(1)}, f32[112,256]{1,0:T(8,128)S(1)}, u32[]{:S(2)}, u32[]{:S(2)}) collective-permute-start(f32[112,256]{1,0:T(8,128)S(1)} %sum_terms.20), channel_id=1, source_target_pairs={{0,24},{4,28},{8,16},{12,20},{16,8},{20,12},{24,0},{28,4},{1,25},{... | collective-permute-start | bytes 344072 | tf_op jit(solution)/shard_map/ppermute | solution.py:530
  125.7 3.1 %collective-permute-start.28 = (bf16[2048,256]{1,0:T(8,128)(2,1)S(1)}, bf16[2048,256]{1,0:T(8,128)(2,1)S(1)}, u32[]{:S(2)}, u32[]{:S(2)}) collective-permute-start(bf16[2048,256]{1,0:T(8,128)(2,1)S(1)} %get-tuple-element.43), channel_id=1, source_target_pairs={{0,4},{4,0},{8,12},{12,8},{16,20},{20,16},{24,28},{28,24},{1,5},{5... | collective-permute-start | bytes 3145736 | tf_op jit(solution)/shard_map/ppermute | solution.py:530
  126.5 19.9 %collective-permute-start.27 = (bf16[2048,256]{1,0:T(8,128)(2,1)S(1)}, bf16[2048,256]{1,0:T(8,128)(2,1)S(1)}, u32[]{:S(2)}, u32[]{:S(2)}) collective-permute-start(bf16[2048,256]{1,0:T(8,128)(2,1)S(1)} %get-tuple-element.42), channel_id=1, source_target_pairs={{0,4},{4,0},{8,12},{12,8},{16,20},{20,16},{24,28},{28,24},{1,5},{5... | collective-permute-start | bytes 3145736 | tf_op jit(solution)/shard_map/ppermute | solution.py:530
  129.0 19.0 %collective-permute-start.30 = (bf16[1024,256]{1,0:T(8,128)(2,1)S(1)}, bf16[1024,256]{1,0:T(8,128)(2,1)S(1)}, u32[]{:S(2)}, u32[]{:S(2)}) collective-permute-start(bf16[1024,256]{1,0:T(8,128)(2,1)S(1)} %sum_terms.23.refs_22_), channel_id=1, source_target_pairs={{0,16},{4,20},{8,24},{12,28},{16,0},{20,4},{24,8},{28,12},{1,17},{... | collective-permute-start | bytes 1572872 | tf_op jit(solution)/shard_map/ppermute | solution.py:530
  129.2 19.4 %collective-permute-start.29 = (bf16[1024,256]{1,0:T(8,128)(2,1)S(1)}, bf16[1024,256]{1,0:T(8,128)(2,1)S(1)}, u32[]{:S(2)}, u32[]{:S(2)}) collective-permute-start(bf16[1024,256]{1,0:T(8,128)(2,1)S(1)} %sum_terms.22.refs_21_), channel_id=1, source_target_pairs={{0,8},{4,12},{8,0},{12,4},{16,24},{20,28},{24,16},{28,20},{1,9},{5... | collective-permute-start | bytes 1572872 | tf_op jit(solution)/shard_map/ppermute | solution.py:530
  131.3 6.0 %collective-permute-start.33 = (bf16[112,256]{1,0:T(8,128)(2,1)S(1)}, bf16[112,256]{1,0:T(8,128)(2,1)S(1)}, u32[]{:S(2)}, u32[]{:S(2)}) collective-permute-start(bf16[112,256]{1,0:T(8,128)(2,1)S(1)} %sum_terms.21.refs_7_.refs_1_), channel_id=1, source_target_pairs={{0,1},{1,2},{2,3},{3,0},{4,5},{5,6},{6,7},{7,4},{8,9},{9,10},{10,1... | collective-permute-start | bytes 172040 | tf_op jit(solution)/shard_map/ppermute | solution.py:538
  134.9 9.5 %collective-permute-start.34 = (bf16[112,256]{1,0:T(8,128)(2,1)S(1)}, bf16[112,256]{1,0:T(8,128)(2,1)S(1)}, u32[]{:S(2)}, u32[]{:S(2)}) collective-permute-start(bf16[112,256]{1,0:T(8,128)(2,1)S(1)} %sum_terms.21.refs_7_.refs_1_), channel_id=1, source_target_pairs={{0,2},{1,3},{2,0},{3,1},{4,6},{5,7},{6,4},{7,5},{8,10},{9,11},{10,... | collective-permute-start | bytes 172040 | tf_op jit(solution)/shard_map/ppermute | solution.py:538
  137.3 7.1 %collective-permute-start.35 = (bf16[112,256]{1,0:T(8,128)(2,1)S(1)}, bf16[112,256]{1,0:T(8,128)(2,1)S(1)}, u32[]{:S(2)}, u32[]{:S(2)}) collective-permute-start(bf16[112,256]{1,0:T(8,128)(2,1)S(1)} %sum_terms.21.refs_7_.refs_1_), channel_id=1, source_target_pairs={{0,3},{1,0},{2,1},{3,2},{4,7},{5,4},{6,5},{7,6},{8,11},{9,8},{10,9... | collective-permute-start | bytes 172040 | tf_op jit(solution)/shard_map/ppermute | solution.py:538
  144.4 5.7 %collective-permute-start.38 = (bf16[112,256]{1,0:T(8,128)(2,1)S(1)}, bf16[112,256]{1,0:T(8,128)(2,1)S(1)}, u32[]{:S(2)}, u32[]{:S(2)}) collective-permute-start(bf16[112,256]{1,0:T(8,128)(2,1)S(1)} %sum_terms.27), channel_id=1, source_target_pairs={{0,24},{4,28},{8,16},{12,20},{16,8},{20,12},{24,0},{28,4},{1,25},{... | collective-permute-start | bytes 172040 | tf_op jit(solution)/shard_map/ppermute | solution.py:530
  145.4 5.1 %collective-permute-start.37 = (bf16[112,256]{1,0:T(8,128)(2,1)S(1)}, bf16[112,256]{1,0:T(8,128)(2,1)S(1)}, u32[]{:S(2)}, u32[]{:S(2)}) collective-permute-start(bf16[112,256]{1,0:T(8,128)(2,1)S(1)} %sum_terms.27), channel_id=1, source_target_pairs={{0,16},{4,20},{8,24},{12,28},{16,0},{20,4},{24,8},{28,12},{1,17},{... | collective-permute-start | bytes 172040 | tf_op jit(solution)/shard_map/ppermute | solution.py:530
  146.4 4.8 %collective-permute-start.36 = (bf16[112,256]{1,0:T(8,128)(2,1)S(1)}, bf16[112,256]{1,0:T(8,128)(2,1)S(1)}, u32[]{:S(2)}, u32[]{:S(2)}) collective-permute-start(bf16[112,256]{1,0:T(8,128)(2,1)S(1)} %sum_terms.27), channel_id=1, source_target_pairs={{0,8},{4,12},{8,0},{12,4},{16,24},{20,28},{24,16},{28,20},{1,9},{5... | collective-permute-start | bytes 172040 | tf_op jit(solution)/shard_map/ppermute | solution.py:530
  148.1 6.8 %collective-permute-start.31 = (bf16[512,256]{1,0:T(8,128)(2,1)S(1)}, bf16[512,256]{1,0:T(8,128)(2,1)S(1)}, u32[]{:S(2)}, u32[]{:S(2)}) collective-permute-start(bf16[512,256]{1,0:T(8,128)(2,1)S(1)} %sum_terms.24), channel_id=1, source_target_pairs={{0,8},{4,12},{8,0},{12,4},{16,24},{20,28},{24,16},{28,20},{1,9},{5... | collective-permute-start | bytes 786440 | tf_op jit(solution)/shard_map/ppermute | solution.py:530
  148.8 7.0 %collective-permute-start.32 = (bf16[512,256]{1,0:T(8,128)(2,1)S(1)}, bf16[512,256]{1,0:T(8,128)(2,1)S(1)}, u32[]{:S(2)}, u32[]{:S(2)}) collective-permute-start(bf16[512,256]{1,0:T(8,128)(2,1)S(1)} %sum_terms.25), channel_id=1, source_target_pairs={{0,16},{4,20},{8,24},{12,28},{16,0},{20,4},{24,8},{28,12},{1,17},{... | collective-permute-start | bytes 786440 | tf_op jit(solution)/shard_map/ppermute | solution.py:530
  151.2 1.6 collective-permute-start.39
  (14 other events, 70.3 us)

commit v12 on v11

--- a/solution.py
+++ b/solution.py
@@ -140,7 +140,7 @@
             pltpu.SemaphoreType.DMA((len(pieces),)),
             pltpu.SemaphoreType.DMA((n_picks,)),
         ],
-        compiler_params=params(60),
+        compiler_params=params(48),
         cost_estimate=SMALL,
         name="partial_messages",
     )(here, cols, counts, *pieces, tiles)
@@ -698,6 +698,7 @@
         grad_tiles, token = tile_grad_call(
             *known, grads, pieces, tile_local.shape, rows, (1, 0), near_grads, first
         )
+        row_weights = sum_call(here, row_weights.shape[0], [(row_weights, 0)], after=(rest, *first))
         all_weights = level_weights(here, row_weights, (token,))
         joint = jnp.concatenate([all_weights] + [swap(all_weights, bits) for bits in (2, 4, 6)], axis=0)
         weights = unpack_call(here, joint, swap(joint, 1), width)

time: 158 us -> 154 us (0.975)
  Pallas kernels: 39.4 us -> 34.6 us
  waiting for transfers between devices: 65.7 us -> 67.5 us
    pallas_call x3, Pallas kernels: 15 us -> 9.41 us  [forward_call(): pl.pallas_call(functools.partial(forward_kernel, outputs, len(pieces), pa...]
    ppermute x6, waiting for transfers between devices: 39.3 us -> 42.8 us  [outer_swap(): return lax.ppermute(value, 'col', [(0, 1), (1, 0), (2, 3), (3, 2)])]
    ppermute x3, waiting for transfers between devices: 1.71 us -> 0.01 us  [turn(): return lax.ppermute(value, 'col', [(i, (i + by) % 4) for i in range(4)])]
  transfers between devices with their start and end apart: 40 -> 40, of which waited for: 20 -> 17; matrix products, arithmetic and copies ran while one was open for 1% -> 1% of each run, Pallas kernels for 15% -> 13%
where the time goes in v12:
time: 154 us
  waiting for transfers between devices  67.5 us (44%)
  starting transfers between devices  47.5 us (31%)
  Pallas kernels  34.6 us (22%)
  local copies, waits for them, and re-layouts  3.48 us (2%)
    ppermute x6, waiting for transfers between devices, outer_swap(): return lax.ppermute(value, 'col', [(0, 1), (1, 0), (2, 3), (3, 2)])  42.8 us
    ppermute x27, waiting for transfers between devices, swap(): return lax.ppermute(value, 'row', [(i, i ^ bit) for i in range(8)])  24.7 us
    ppermute x6, starting transfers between devices, outer_swap(): return lax.ppermute(value, 'col', [(0, 1), (1, 0), (2, 3), (3, 2)])  20.6 us
    ppermute x27, starting transfers between devices, swap(): return lax.ppermute(value, 'row', [(i, i ^ bit) for i in range(8)])  19.5 us
    pallas_call x2, Pallas kernels, tile_grad_call(): pl.pallas_call(functools.partial(tile_grad_kernel, rows, slots, len(grads...  9.98 us
    pallas_call x3, Pallas kernels, forward_call(): pl.pallas_call(functools.partial(forward_kernel, outputs, len(pieces), pa...  9.41 us
    ppermute x3, starting transfers between devices, turn(): return lax.ppermute(value, 'col', [(i, (i + by) % 4) for i in range(4)])  7.2 us
    pallas_call x1, Pallas kernels, back_call(): pl.pallas_call(functools.partial(back_kernel, rows, slots, len(grads), le...  6.48 us
  transfers between devices with their start and end apart: 40, of which 17 were waited for; matrix products, arithmetic and copies ran while one was open for 1% of the time, Pallas kernels for 13%

profile of v12, /device:TPU:0, one launch (start us, length us, event | category | flops | bytes accessed | tf_op | source)
XLA Modules:
  0.0 154.0 jit_solution(10277397656966913669)
XLA Ops:
  0.6 0.5 collective-permute-start
  1.1 1.1 fusion
  2.2 2.6 %collective-permute-start.1 = (bf16[512,256]{1,0:T(8,128)(2,1)S(1)}, bf16[512,256]{1,0:T(8,128)(2,1)S(1)}, u32[]{:S(2)}, u32[]{:S(2)}) collective-permute-start(bf16[512,256]{1,0:T(8,128)(2,1)S(1)} %get-tuple-element.57), channel_id=1, source_target_pairs={{0,8},{4,12},{8,0},{12,4},{16,24},{20,28},{24,16},{28,20},{1,9},{5... | collective-permute-start | bytes 786440 | tf_op jit(solution)/shard_map/ppermute | solution.py:530
  4.8 1.5 collective-permute-start.5
  6.3 0.5 collective-permute-start.2
  6.9 5.1 %collective-permute-done.1.refs_2_.refs_4_.refs_8_ = bf16[512,256]{1,0:T(8,128)(2,1)S(1)} collective-permute-done((bf16[512,256]{1,0:T(8,128)(2,1)S(1)}, bf16[512,256]{1,0:T(8,128)(2,1)S(1)}, u32[]{:S(2)}, u32[]{:S(2)}) %collective-permute-start.1) | collective-permute-done | bytes 262176 | tf_op jit(solution)/shard_map/ppermute | solution.py:530
  11.9 2.0 %collective-permute-done.5.refs_6_.refs_8_.refs_12_ = bf16[512,256]{1,0:T(8,128)(2,1)S(1)} collective-permute-done((bf16[512,256]{1,0:T(8,128)(2,1)S(1)}, bf16[512,256]{1,0:T(8,128)(2,1)S(1)}, u32[]{:S(2)}, u32[]{:S(2)}) %collective-permute-start.5) | collective-permute-done | bytes 262176 | tf_op jit(solution)/shard_map/ppermute | solution.py:530
  14.0 3.6 %collective-permute-done.2.refs_3_.refs_5_.refs_9_ = bf16[512,256]{1,0:T(8,128)(2,1)S(1)} collective-permute-done((bf16[512,256]{1,0:T(8,128)(2,1)S(1)}, bf16[512,256]{1,0:T(8,128)(2,1)S(1)}, u32[]{:S(2)}, u32[]{:S(2)}) %collective-permute-start.2) | collective-permute-done | bytes 262176 | tf_op jit(solution)/shard_map/ppermute | solution.py:530
  17.6 2.0 %collective-permute-start.10 = (bf16[512,256]{1,0:T(8,128)(2,1)S(1)}, bf16[512,256]{1,0:T(8,128)(2,1)S(1)}, u32[]{:S(2)}, u32[]{:S(2)}) collective-permute-start(bf16[512,256]{1,0:T(8,128)(2,1)S(1)} %collective-permute-done.2.refs_3_.refs_5_.refs_9_), channel_id=1, source_target_pairs={{0,16},{4,20},{8,24},{12,28},{16,0},{20,4},{24,8},{28,12},{1,17},{... | collective-permute-start | bytes 786440 | tf_op jit(solution)/shard_map/ppermute | solution.py:530
  19.5 0.5 collective-permute-start.7
  20.1 2.9 %collective-permute-done.9.refs_10_.refs_12_.refs_16_ = bf16[512,256]{1,0:T(8,128)(2,1)S(1)} collective-permute-done((bf16[512,256]{1,0:T(8,128)(2,1)S(1)}, bf16[512,256]{1,0:T(8,128)(2,1)S(1)}, u32[]{:S(2)}, u32[]{:S(2)}) %collective-permute-start.9) | collective-permute-done | bytes 262176 | tf_op jit(solution)/shard_map/ppermute | solution.py:530
  23.0 2.5 %collective-permute-done.10.refs_11_.refs_13_.refs_17_ = bf16[512,256]{1,0:T(8,128)(2,1)S(1)} collective-permute-done((bf16[512,256]{1,0:T(8,128)(2,1)S(1)}, bf16[512,256]{1,0:T(8,128)(2,1)S(1)}, u32[]{:S(2)}, u32[]{:S(2)}) %collective-permute-start.10) | collective-permute-done | bytes 262176 | tf_op jit(solution)/shard_map/ppermute | solution.py:530
  25.5 1.6 %collective-permute-done.12.refs_13_.refs_15_.refs_19_ = bf16[512,256]{1,0:T(8,128)(2,1)} collective-permute-done((bf16[512,256]{1,0:T(8,128)(2,1)S(1)}, bf16[512,256]{1,0:T(8,128)(2,1)}, u32[]{:S(2)}, u32[]{:S(2)}) %collective-permute-start.12) | collective-permute-done | bytes 262176 | tf_op jit(solution)/shard_map/ppermute | solution.py:530
  27.2 1.0 copy-done.1
  28.2 0.7 copy-done.5
  28.9 0.7 copy-done.6
  29.5 2.9 %partial_messages.4.refs_1_ = bf16[1024,256]{1,0:T(8,128)(2,1)S(1)} custom-call(s32[1]{0:T(128)} %bitcast.here.refs_0_, s32[4,32]{1,0:T(4,128)S(1)} %bitcast.17, s32[32]{0:T(128)S(1)} %bitcast.23, bf16[1024,256]{1,0:T(8,128)(2,1)S(1)} %copy-done.1, bf16[1024,256]{1,0:T(8,128)(2,1)S(1)} %collective-permute-done.refs_1_.refs_3_.refs_7_, ...), custom_call_target="tpu_custom_call" | custom-call | flops 1048576 | bytes 65536 | tf_op jit(solution)/shard_map/partial_messages/pallas_call | solution.py:132
  32.5 1.7 %collective-permute-start.13 = (bf16[1024,256]{1,0:T(8,128)(2,1)S(1)}, bf16[1024,256]{1,0:T(8,128)(2,1)S(1)}, u32[]{:S(2)}, u32[]{:S(2)}) collective-permute-start(bf16[1024,256]{1,0:T(8,128)(2,1)S(1)} %partial_messages.4.refs_1_), channel_id=1, source_target_pairs={{0,1},{1,0},{2,3},{3,2},{4,5},{5,4},{6,7},{7,6},{8,9},{9,8},{10,11... | collective-permute-start | bytes 1572872 | tf_op jit(solution)/shard_map/ppermute | solution.py:534
  34.2 2.9 %partial_messages.5.refs_1_ = bf16[1024,256]{1,0:T(8,128)(2,1)S(1)} custom-call(s32[1]{0:T(128)} %bitcast.here.refs_0_, s32[4,32]{1,0:T(4,128)S(1)} %bitcast.18, s32[32]{0:T(128)S(1)} %bitcast.24, bf16[1024,256]{1,0:T(8,128)(2,1)S(1)} %copy-done.1, bf16[1024,256]{1,0:T(8,128)(2,1)S(1)} %collective-permute-done.refs_1_.refs_3_.refs_7_, ...), custom_call_target="tpu_custom_call" | custom-call | flops 1048576 | bytes 65536 | tf_op jit(solution)/shard_map/partial_messages/pallas_call | solution.py:132
  37.1 0.5 collective-permute-start.16
  37.6 9.7 %collective-permute-done.13.refs_2_ = bf16[1024,256]{1,0:T(8,128)(2,1)S(1)} collective-permute-done((bf16[1024,256]{1,0:T(8,128)(2,1)S(1)}, bf16[1024,256]{1,0:T(8,128)(2,1)S(1)}, u32[]{:S(2)}, u32[]{:S(2)}) %collective-permute-start.13) | collective-permute-done | bytes 524320 | tf_op jit(solution)/shard_map/ppermute | solution.py:534
  47.3 0.2 sum_terms.15
  47.6 3.5 %partial_messages.3 = (bf16[1024,256]{1,0:T(8,128)(2,1)S(1)}, bf16[1024,256]{1,0:T(8,128)(2,1)S(1)}) custom-call(s32[1]{0:T(128)} %bitcast.here.refs_0_, s32[4,32]{1,0:T(4,128)S(1)} %bitcast.19, s32[32]{0:T(128)S(1)} %bitcast.25, bf16[1024,256]{1,0:T(8,128)(2,1)S(1)} %copy-done.1, bf16[1024,256]{1,0:T(8,128)(2,1)S(1)} %collective-permute-done.refs_1_.refs_3_.refs_7_, ...), custom_call_target="tpu_custom_call" | custom-call | flops 1048576 | bytes 65536 | tf_op jit(solution)/shard_map/partial_messages/pallas_call | solution.py:132
  51.2 6.6 %collective-permute-done.16.refs_2_ = bf16[1024,256]{1,0:T(8,128)(2,1)S(1)} collective-permute-done((bf16[1024,256]{1,0:T(8,128)(2,1)S(1)}, bf16[1024,256]{1,0:T(8,128)(2,1)S(1)}, u32[]{:S(2)}, u32[]{:S(2)}) %collective-permute-start.16) | collective-permute-done | bytes 524320 | tf_op jit(solution)/shard_map/ppermute | solution.py:534
  57.7 0.2 sum_terms.17
  58.0 0.2 sum_terms.16
  58.3 3.6 %collective-permute-start.15 = (bf16[1024,256]{1,0:T(8,128)(2,1)S(1)}, bf16[1024,256]{1,0:T(8,128)(2,1)S(1)}, u32[]{:S(2)}, u32[]{:S(2)}) collective-permute-start(bf16[1024,256]{1,0:T(8,128)(2,1)S(1)} %sum_terms.16), channel_id=1, source_target_pairs={{0,1},{1,0},{2,3},{3,2},{4,5},{5,4},{6,7},{7,6},{8,9},{9,8},{10,11... | collective-permute-start | bytes 1572872 | tf_op jit(solution)/shard_map/ppermute | solution.py:534
  61.9 10.7 %collective-permute-done.15.refs_1_ = bf16[1024,256]{1,0:T(8,128)(2,1)S(1)} collective-permute-done((bf16[1024,256]{1,0:T(8,128)(2,1)S(1)}, bf16[1024,256]{1,0:T(8,128)(2,1)S(1)}, u32[]{:S(2)}, u32[]{:S(2)}) %collective-permute-start.15) | collective-permute-done | bytes 524320 | tf_op jit(solution)/shard_map/ppermute | solution.py:534
  72.7 3.2 %mlp.1 = (bf16[1024,256]{1,0:T(8,128)(2,1)}, bf16[1024,256]{1,0:T(8,128)(2,1)S(1)}, bf16[1024,256]{1,0:T(8,128)(2,1)S(1)}, bf16[1024,256]{1,0:T(8,128)(2,1)S(1)}...) custom-call(s32[1]{0:T(128)} %bitcast.here.refs_0_, ...), custom_call_target="tpu_custom_call" | custom-call | flops 1048576 | bytes 65536 | tf_op jit(solution)/shard_map/mlp/pallas_call | solution.py:226
  75.9 1.7 %collective-permute-start.18 = (bf16[1024,256]{1,0:T(8,128)(2,1)S(1)}, bf16[1024,256]{1,0:T(8,128)(2,1)S(1)}, u32[]{:S(2)}, u32[]{:S(2)}) collective-permute-start(bf16[1024,256]{1,0:T(8,128)(2,1)S(1)} %get-tuple-element.36.refs_0_), channel_id=1, source_target_pairs={{0,1},{1,0},{2,3},{3,2},{4,5},{5,4},{6,7},{7,6},{8,9},{9,8},{10,11... | collective-permute-start | bytes 1572872 | tf_op jit(solution)/shard_map/ppermute | solution.py:534
  77.6 10.1 %collective-permute-done.18.refs_0_.refs_1_ = bf16[1024,256]{1,0:T(8,128)(2,1)S(1)} collective-permute-done((bf16[1024,256]{1,0:T(8,128)(2,1)S(1)}, bf16[1024,256]{1,0:T(8,128)(2,1)S(1)}, u32[]{:S(2)}, u32[]{:S(2)}) %collective-permute-start.18) | collective-permute-done | bytes 524320 | tf_op jit(solution)/shard_map/ppermute | solution.py:534
  87.8 1.5 weight_grads.1
  89.3 0.6 collective-permute-start.23
  89.9 4.0 %collective-permute-start.20 = (bf16[1024,256]{1,0:T(8,128)(2,1)S(1)}, bf16[1024,256]{1,0:T(8,128)(2,1)S(1)}, u32[]{:S(2)}, u32[]{:S(2)}) collective-permute-start(bf16[1024,256]{1,0:T(8,128)(2,1)S(1)} %collective-permute-done.19.refs_1_.refs_2_), channel_id=1, source_target_pairs={{0,1},{1,0},{2,3},{3,2},{4,5},{5,4},{6,7},{7,6},{8,9},{9,8},{10,11... | collective-permute-start | bytes 1572872 | tf_op jit(solution)/shard_map/ppermute | solution.py:534
  93.9 9.1 %collective-permute-start.22 = (bf16[1024,256]{1,0:T(8,128)(2,1)S(1)}, bf16[1024,256]{1,0:T(8,128)(2,1)S(1)}, u32[]{:S(2)}, u32[]{:S(2)}) collective-permute-start(bf16[1024,256]{1,0:T(8,128)(2,1)S(1)} %collective-permute-done.21.refs_17_.refs_4_), channel_id=1, source_target_pairs={{0,1},{1,0},{2,3},{3,2},{4,5},{5,4},{6,7},{7,6},{8,9},{9,8},{10,11... | collective-permute-start | bytes 1572872 | tf_op jit(solution)/shard_map/ppermute | solution.py:534
  103.0 1.6 %collective-permute-start.24 = (f32[112,256]{1,0:T(8,128)S(1)}, f32[112,256]{1,0:T(8,128)S(1)}, u32[]{:S(2)}, u32[]{:S(2)}) collective-permute-start(f32[112,256]{1,0:T(8,128)S(1)} %sum_terms.19), channel_id=1, source_target_pairs={{0,16},{4,20},{8,24},{12,28},{16,0},{20,4},{24,8},{28,12},{1,17},{... | collective-permute-start | bytes 344072 | tf_op jit(solution)/shard_map/ppermute | solution.py:530
  104.6 1.6 %collective-permute-start.25 = (f32[112,256]{1,0:T(8,128)S(1)}, f32[112,256]{1,0:T(8,128)S(1)}, u32[]{:S(2)}, u32[]{:S(2)}) collective-permute-start(f32[112,256]{1,0:T(8,128)S(1)} %sum_terms.20), channel_id=1, source_target_pairs={{0,8},{4,12},{8,0},{12,4},{16,24},{20,28},{24,16},{28,20},{1,9},{5... | collective-permute-start | bytes 344072 | tf_op jit(solution)/shard_map/ppermute | solution.py:530
  106.2 0.6 collective-permute-start.26
  106.8 5.2 %tile_grads.2 = (bf16[128,128,128]{2,1,0:T(8,128)(2,1)}, f32[8,128]{1,0:T(8,128)S(1)}) custom-call(s32[1]{0:T(128)} %bitcast.here.refs_0_, s32[4,32]{1,0:T(4,128)S(1)} %bitcast.20, s32[32]{0:T(128)S(1)} %bitcast.26, bf16[1024,256]{1,0:T(8,128)(2,1)S(1)} %get-tuple-element.36.refs_0_, bf16[1024,256]{1,0:T(8,128)(2,1)S(1)} %collective-permute-done.18.refs_0_.refs_1_, ...), custom_call_target="tpu_custom_call" | custom-call | flops 1048576 | bytes 65536 | tf_op jit(solution)/shard_map/tile_grads/pallas_call | solution.py:502
  112.0 5.6 %collective-permute-done.22.refs_5_ = bf16[1024,256]{1,0:T(8,128)(2,1)S(1)} collective-permute-done((bf16[1024,256]{1,0:T(8,128)(2,1)S(1)}, bf16[1024,256]{1,0:T(8,128)(2,1)S(1)}, u32[]{:S(2)}, u32[]{:S(2)}) %collective-permute-start.22) | collective-permute-done | bytes 524320 | tf_op jit(solution)/shard_map/ppermute | solution.py:534
  117.6 6.5 %back_terms.1 = (bf16[2048,256]{1,0:T(8,128)(2,1)S(1)}, bf16[2048,256]{1,0:T(8,128)(2,1)S(1)}, bf16[4096,256]{1,0:T(8,128)(2,1)S(1)}) custom-call(s32[1]{0:T(128)} %bitcast.here.refs_0_, s32[4,32]{1,0:T(4,128)S(1)} %bitcast.21, s32[32]{0:T(128)S(1)} %bitcast.27, bf16[1024,256]{1,0:T(8,128)(2,1)S(1)} %get-tuple-element.36.refs_0_, ...), custom_call_target="tpu_custom_call" | custom-call | flops 1048576 | bytes 65536 | tf_op jit(solution)/shard_map/back_terms/pallas_call | solution.py:402
  124.1 0.1 collective-permute-start.28
  124.3 0.5 collective-permute-start.27
  124.7 2.1 %collective-permute-done.28.refs_2_ = bf16[2048,256]{1,0:T(8,128)(2,1)S(1)} collective-permute-done((bf16[2048,256]{1,0:T(8,128)(2,1)S(1)}, bf16[2048,256]{1,0:T(8,128)(2,1)S(1)}, u32[]{:S(2)}, u32[]{:S(2)}) %collective-permute-start.28) | collective-permute-done | bytes 1048608 | tf_op jit(solution)/shard_map/ppermute | solution.py:530
  126.9 0.2 sum_terms.24.refs_22_.refs_4_
  127.1 0.7 collective-permute-start.30
  127.7 0.2 sum_terms.23.refs_21_.refs_3_
  127.9 1.5 collective-permute-start.29
  129.4 2.9 %collective-permute-start.33 = (bf16[112,256]{1,0:T(8,128)(2,1)S(1)}, bf16[112,256]{1,0:T(8,128)(2,1)S(1)}, u32[]{:S(2)}, u32[]{:S(2)}) collective-permute-start(bf16[112,256]{1,0:T(8,128)(2,1)S(1)} %sum_terms.28.refs_1_), channel_id=1, source_target_pairs={{0,1},{1,2},{2,3},{3,0},{4,5},{5,6},{6,7},{7,4},{8,9},{9,10},{10,1... | collective-permute-start | bytes 172040 | tf_op jit(solution)/shard_map/ppermute | solution.py:538
  132.3 1.4 collective-permute-start.34
  133.7 2.8 %collective-permute-start.35 = (bf16[112,256]{1,0:T(8,128)(2,1)S(1)}, bf16[112,256]{1,0:T(8,128)(2,1)S(1)}, u32[]{:S(2)}, u32[]{:S(2)}) collective-permute-start(bf16[112,256]{1,0:T(8,128)(2,1)S(1)} %sum_terms.28.refs_1_), channel_id=1, source_target_pairs={{0,3},{1,0},{2,1},{3,2},{4,7},{5,4},{6,5},{7,6},{8,11},{9,8},{10,9... | collective-permute-start | bytes 172040 | tf_op jit(solution)/shard_map/ppermute | solution.py:538
  136.6 4.8 %tile_grads.3 = (bf16[128,128,128]{2,1,0:T(8,128)(2,1)}, f32[8,128]{1,0:T(8,128)S(1)}) custom-call(s32[1]{0:T(128)} %bitcast.here.refs_0_, s32[4,32]{1,0:T(4,128)S(1)} %bitcast.22, s32[32]{0:T(128)S(1)} %bitcast.28, bf16[1024,256]{1,0:T(8,128)(2,1)S(1)} %get-tuple-element.36.refs_0_, ...), custom_call_target="tpu_custom_call", output_to_operand_aliasing={{0}: (23, {})} | custom-call | flops 1048576 | bytes 65536 | tf_op jit(solution)/shard_map/tile_grads/pallas_call | solution.py:502
  141.5 0.5 collective-permute-start.38
  142.0 1.0 collective-permute-start.37
  143.0 2.0 %collective-permute-start.36 = (bf16[112,256]{1,0:T(8,128)(2,1)S(1)}, bf16[112,256]{1,0:T(8,128)(2,1)S(1)}, u32[]{:S(2)}, u32[]{:S(2)}) collective-permute-start(bf16[112,256]{1,0:T(8,128)(2,1)S(1)} %sum_terms.29), channel_id=1, source_target_pairs={{0,8},{4,12},{8,0},{12,4},{16,24},{20,28},{24,16},{28,20},{1,9},{5... | collective-permute-start | bytes 172040 | tf_op jit(solution)/shard_map/ppermute | solution.py:530
  145.0 0.1 sum_terms.25
  145.3 0.1 sum_terms.26
  145.4 1.0 collective-permute-start.32
  146.5 0.8 collective-permute-done.38
  147.2 0.5 collective-permute-done.36
  147.8 1.5 collective-permute-done.39.odd
  149.3 1.0 weight_unpack.1
  150.3 2.1 %collective-permute-done.31.refs_5_ = bf16[512,256]{1,0:T(8,128)(2,1)S(1)} collective-permute-done((bf16[512,256]{1,0:T(8,128)(2,1)S(1)}, bf16[512,256]{1,0:T(8,128)(2,1)S(1)}, u32[]{:S(2)}, u32[]{:S(2)}) %collective-permute-start.31) | collective-permute-done | bytes 262176 | tf_op jit(solution)/shard_map/ppermute | solution.py:530
  152.4 1.6 %sum_terms.27 = bf16[1024,256]{1,0:T(8,128)(2,1)} custom-call(s32[1]{0:T(128)} %bitcast.here.refs_0_, f32[1024,256]{1,0:T(8,128)S(1)} %get-tuple-element.37.refs_1_, bf16[4096,256]{1,0:T(8,128)(2,1)S(1)} %get-tuple-element.41.refs_1_.refs_2_, bf16[2048,256]{1,0:T(8,128)(2,1)S(1)} %collective-permute-done.27.refs_2_.refs_3_, ...), custom_call_target="tpu_custom_call" | custom-call | flops 1048576 | bytes 65536 | tf_op jit(solution)/shard_map/sum_terms/pallas_call | solution.py:610
  (62 shorter events, 0.8 us)
Async XLA Ops:
  0.6 18.9 %collective-permute-start = (bf16[1024,256]{1,0:T(8,128)(2,1)}, bf16[1024,256]{1,0:T(8,128)(2,1)S(1)}, u32[]{:S(2)}, u32[]{:S(2)}) collective-permute-start(bf16[1024,256]{1,0:T(8,128)(2,1)} %refs_6_.1), channel_id=1, source_target_pairs={{0,4},{4,0},{8,12},{12,8},{16,20},{20,16},{24,28},{28,24},{1,5},{5... | collective-permute-start | bytes 1572872 | tf_op jit(solution)/shard_map/ppermute | solution.py:530
  2.2 9.7 %collective-permute-start.1 = (bf16[512,256]{1,0:T(8,128)(2,1)S(1)}, bf16[512,256]{1,0:T(8,128)(2,1)S(1)}, u32[]{:S(2)}, u32[]{:S(2)}) collective-permute-start(bf16[512,256]{1,0:T(8,128)(2,1)S(1)} %get-tuple-element.57), channel_id=1, source_target_pairs={{0,8},{4,12},{8,0},{12,4},{16,24},{20,28},{24,16},{28,20},{1,9},{5... | collective-permute-start | bytes 786440 | tf_op jit(solution)/shard_map/ppermute | solution.py:530
  4.8 9.1 %collective-permute-start.5 = (bf16[512,256]{1,0:T(8,128)(2,1)S(1)}, bf16[512,256]{1,0:T(8,128)(2,1)S(1)}, u32[]{:S(2)}, u32[]{:S(2)}) collective-permute-start(bf16[512,256]{1,0:T(8,128)(2,1)S(1)} %get-tuple-element.57), channel_id=1, source_target_pairs={{0,16},{4,20},{8,24},{12,28},{16,0},{20,4},{24,8},{28,12},{1,17},{... | collective-permute-start | bytes 786440 | tf_op jit(solution)/shard_map/ppermute | solution.py:530
  6.3 11.3 %collective-permute-start.2 = (bf16[512,256]{1,0:T(8,128)(2,1)S(1)}, bf16[512,256]{1,0:T(8,128)(2,1)S(1)}, u32[]{:S(2)}, u32[]{:S(2)}) collective-permute-start(bf16[512,256]{1,0:T(8,128)(2,1)S(1)} %get-tuple-element.56), channel_id=1, source_target_pairs={{0,8},{4,12},{8,0},{12,4},{16,24},{20,28},{24,16},{28,20},{1,9},{5... | collective-permute-start | bytes 786440 | tf_op jit(solution)/shard_map/ppermute | solution.py:530
  6.8 12.7 %collective-permute-start.6 = (bf16[512,256]{1,0:T(8,128)(2,1)S(1)}, bf16[512,256]{1,0:T(8,128)(2,1)S(1)}, u32[]{:S(2)}, u32[]{:S(2)}) collective-permute-start(bf16[512,256]{1,0:T(8,128)(2,1)S(1)} %get-tuple-element.56), channel_id=1, source_target_pairs={{0,16},{4,20},{8,24},{12,28},{16,0},{20,4},{24,8},{28,12},{1,17},{... | collective-permute-start | bytes 786440 | tf_op jit(solution)/shard_map/ppermute | solution.py:530
  11.9 8.1 %collective-permute-start.3 = (bf16[512,256]{1,0:T(8,128)(2,1)S(1)}, bf16[512,256]{1,0:T(8,128)(2,1)S(1)}, u32[]{:S(2)}, u32[]{:S(2)}) collective-permute-start(bf16[512,256]{1,0:T(8,128)(2,1)S(1)} %collective-permute-done.1.refs_2_.refs_4_.refs_8_), channel_id=1, source_target_pairs={{0,4},{4,0},{8,12},{12,8},{16,20},{20,16},{24,28},{28,24},{1,5},{5... | collective-permute-start | bytes 786440 | tf_op jit(solution)/shard_map/ppermute | solution.py:530
  13.9 9.1 %collective-permute-start.9 = (bf16[512,256]{1,0:T(8,128)(2,1)S(1)}, bf16[512,256]{1,0:T(8,128)(2,1)S(1)}, u32[]{:S(2)}, u32[]{:S(2)}) collective-permute-start(bf16[512,256]{1,0:T(8,128)(2,1)S(1)} %collective-permute-done.5.refs_6_.refs_8_.refs_12_), channel_id=1, source_target_pairs={{0,8},{4,12},{8,0},{12,4},{16,24},{20,28},{24,16},{28,20},{1,9},{5... | collective-permute-start | bytes 786440 | tf_op jit(solution)/shard_map/ppermute | solution.py:530
  17.6 7.9 %collective-permute-start.10 = (bf16[512,256]{1,0:T(8,128)(2,1)S(1)}, bf16[512,256]{1,0:T(8,128)(2,1)S(1)}, u32[]{:S(2)}, u32[]{:S(2)}) collective-permute-start(bf16[512,256]{1,0:T(8,128)(2,1)S(1)} %collective-permute-done.2.refs_3_.refs_5_.refs_9_), channel_id=1, source_target_pairs={{0,16},{4,20},{8,24},{12,28},{16,0},{20,4},{24,8},{28,12},{1,17},{... | collective-permute-start | bytes 786440 | tf_op jit(solution)/shard_map/ppermute | solution.py:530
  19.5 6.0 %collective-permute-start.4 = (bf16[512,256]{1,0:T(8,128)(2,1)S(1)}, bf16[512,256]{1,0:T(8,128)(2,1)S(1)}, u32[]{:S(2)}, u32[]{:S(2)}) collective-permute-start(bf16[512,256]{1,0:T(8,128)(2,1)S(1)} %collective-permute-done.2.refs_3_.refs_5_.refs_9_), channel_id=1, source_target_pairs={{0,4},{4,0},{8,12},{12,8},{16,20},{20,16},{24,28},{28,24},{1,5},{5... | collective-permute-start | bytes 786440 | tf_op jit(solution)/shard_map/ppermute | solution.py:530
  19.5 6.0 %collective-permute-start.7 = (bf16[512,256]{1,0:T(8,128)(2,1)S(1)}, bf16[512,256]{1,0:T(8,128)(2,1)S(1)}, u32[]{:S(2)}, u32[]{:S(2)}) collective-permute-start(bf16[512,256]{1,0:T(8,128)(2,1)S(1)} %collective-permute-done.5.refs_6_.refs_8_.refs_12_), channel_id=1, source_target_pairs={{0,4},{4,0},{8,12},{12,8},{16,20},{20,16},{24,28},{28,24},{1,5},{5... | collective-permute-start | bytes 786440 | tf_op jit(solution)/shard_map/ppermute | solution.py:530
  20.1 5.4 %collective-permute-start.8 = (bf16[512,256]{1,0:T(8,128)(2,1)S(1)}, bf16[512,256]{1,0:T(8,128)(2,1)S(1)}, u32[]{:S(2)}, u32[]{:S(2)}) collective-permute-start(bf16[512,256]{1,0:T(8,128)(2,1)S(1)} %collective-permute-done.6.refs_7_.refs_9_.refs_13_), channel_id=1, source_target_pairs={{0,4},{4,0},{8,12},{12,8},{16,20},{20,16},{24,28},{28,24},{1,5},{5... | collective-permute-start | bytes 786440 | tf_op jit(solution)/shard_map/ppermute | solution.py:530
  23.0 2.5 %collective-permute-start.11 = (bf16[512,256]{1,0:T(8,128)(2,1)S(1)}, bf16[512,256]{1,0:T(8,128)(2,1)S(1)}, u32[]{:S(2)}, u32[]{:S(2)}) collective-permute-start(bf16[512,256]{1,0:T(8,128)(2,1)S(1)} %collective-permute-done.9.refs_10_.refs_12_.refs_16_), channel_id=1, source_target_pairs={{0,4},{4,0},{8,12},{12,8},{16,20},{20,16},{24,28},{28,24},{1,5},{5... | collective-permute-start | bytes 786440 | tf_op jit(solution)/shard_map/ppermute | solution.py:530
  25.5 1.7 %collective-permute-start.12 = (bf16[512,256]{1,0:T(8,128)(2,1)S(1)}, bf16[512,256]{1,0:T(8,128)(2,1)}, u32[]{:S(2)}, u32[]{:S(2)}) collective-permute-start(bf16[512,256]{1,0:T(8,128)(2,1)S(1)} %collective-permute-done.10.refs_11_.refs_13_.refs_17_), channel_id=1, source_target_pairs={{0,4},{4,0},{8,12},{12,8},{16,20},{20,16},{24,28},{28,24},{1,5},{5... | collective-permute-start | bytes 786440 | tf_op jit(solution)/shard_map/ppermute | solution.py:530
  27.2 1.0 copy-start.1
  28.2 0.7 copy-start.5
  28.9 0.7 copy-start.6
  32.5 14.8 %collective-permute-start.13 = (bf16[1024,256]{1,0:T(8,128)(2,1)S(1)}, bf16[1024,256]{1,0:T(8,128)(2,1)S(1)}, u32[]{:S(2)}, u32[]{:S(2)}) collective-permute-start(bf16[1024,256]{1,0:T(8,128)(2,1)S(1)} %partial_messages.4.refs_1_), channel_id=1, source_target_pairs={{0,1},{1,0},{2,3},{3,2},{4,5},{5,4},{6,7},{7,6},{8,9},{9,8},{10,11... | collective-permute-start | bytes 1572872 | tf_op jit(solution)/shard_map/ppermute | solution.py:534
  37.1 20.6 %collective-permute-start.16 = (bf16[1024,256]{1,0:T(8,128)(2,1)S(1)}, bf16[1024,256]{1,0:T(8,128)(2,1)S(1)}, u32[]{:S(2)}, u32[]{:S(2)}) collective-permute-start(bf16[1024,256]{1,0:T(8,128)(2,1)S(1)} %partial_messages.5.refs_1_), channel_id=1, source_target_pairs={{0,1},{1,0},{2,3},{3,2},{4,5},{5,4},{6,7},{7,6},{8,9},{9,8},{10,11... | collective-permute-start | bytes 1572872 | tf_op jit(solution)/shard_map/ppermute | solution.py:534
  47.5 25.1 %copy-start.2 = (bf16[1024,256]{1,0:T(8,128)(2,1)S(1)}, bf16[1024,256]{1,0:T(8,128)(2,1)}, u32[]{:S(2)}) copy-start(bf16[1024,256]{1,0:T(8,128)(2,1)} %cot.3) | copy-start | bytes 1572868
  47.5 25.1 %copy-start.3 = (bf16[512,256]{1,0:T(8,128)(2,1)S(1)}, bf16[512,256]{1,0:T(8,128)(2,1)}, u32[]{:S(2)}) copy-start(bf16[512,256]{1,0:T(8,128)(2,1)} %w_in.1) | copy-start | bytes 786436
  47.5 25.1 %copy-start.4 = (bf16[256,256]{1,0:T(8,128)(2,1)S(1)}, bf16[256,256]{1,0:T(8,128)(2,1)}, u32[]{:S(2)}) copy-start(bf16[256,256]{1,0:T(8,128)(2,1)} %refs_5_.1) | copy-start | bytes 393220
  47.5 25.1 %copy-start.7 = (f32[256]{0:T(256)S(1)}, f32[256]{0:T(256)}, u32[]{:S(2)}) copy-start(f32[256]{0:T(256)} %param.15) | copy-start | bytes 3076
  47.5 25.1 %copy-start.8 = (f32[256]{0:T(256)S(1)}, f32[256]{0:T(256)}, u32[]{:S(2)}) copy-start(f32[256]{0:T(256)} %param.17) | copy-start | bytes 3076
  47.6 25.1 %copy-start.9 = (f32[256]{0:T(256)S(1)}, f32[256]{0:T(256)}, u32[]{:S(2)}) copy-start(f32[256]{0:T(256)} %param.18) | copy-start | bytes 3076
  47.6 10.4 %collective-permute-start.14 = (bf16[1024,256]{1,0:T(8,128)(2,1)S(1)}, bf16[1024,256]{1,0:T(8,128)(2,1)S(1)}, u32[]{:S(2)}, u32[]{:S(2)}) collective-permute-start(bf16[1024,256]{1,0:T(8,128)(2,1)S(1)} %sum_terms.15), channel_id=1, source_target_pairs={{0,4},{1,2},{2,1},{3,7},{4,0},{5,6},{6,5},{7,3},{8,12},{9,10},{10,... | collective-permute-start | bytes 1572872 | tf_op jit(solution)/shard_map/ppermute | solution.py:547
  57.9 4.0 %collective-permute-start.17 = (bf16[1024,256]{1,0:T(8,128)(2,1)S(1)}, bf16[1024,256]{1,0:T(8,128)(2,1)S(1)}, u32[]{:S(2)}, u32[]{:S(2)}) collective-permute-start(bf16[1024,256]{1,0:T(8,128)(2,1)S(1)} %sum_terms.17), channel_id=1, source_target_pairs={{0,4},{1,2},{2,1},{3,7},{4,0},{5,6},{6,5},{7,3},{8,12},{9,10},{10,... | collective-permute-start | bytes 1572872 | tf_op jit(solution)/shard_map/ppermute | solution.py:547
  58.3 14.4 %collective-permute-start.15 = (bf16[1024,256]{1,0:T(8,128)(2,1)S(1)}, bf16[1024,256]{1,0:T(8,128)(2,1)S(1)}, u32[]{:S(2)}, u32[]{:S(2)}) collective-permute-start(bf16[1024,256]{1,0:T(8,128)(2,1)S(1)} %sum_terms.16), channel_id=1, source_target_pairs={{0,1},{1,0},{2,3},{3,2},{4,5},{5,4},{6,7},{7,6},{8,9},{9,8},{10,11... | collective-permute-start | bytes 1572872 | tf_op jit(solution)/shard_map/ppermute | solution.py:534
  75.9 11.8 %collective-permute-start.18 = (bf16[1024,256]{1,0:T(8,128)(2,1)S(1)}, bf16[1024,256]{1,0:T(8,128)(2,1)S(1)}, u32[]{:S(2)}, u32[]{:S(2)}) collective-permute-start(bf16[1024,256]{1,0:T(8,128)(2,1)S(1)} %get-tuple-element.36.refs_0_), channel_id=1, source_target_pairs={{0,1},{1,0},{2,3},{3,2},{4,5},{5,4},{6,7},{7,6},{8,9},{9,8},{10,11... | collective-permute-start | bytes 1572872 | tf_op jit(solution)/shard_map/ppermute | solution.py:534
  77.6 10.1 %collective-permute-start.19 = (bf16[1024,256]{1,0:T(8,128)(2,1)S(1)}, bf16[1024,256]{1,0:T(8,128)(2,1)S(1)}, u32[]{:S(2)}, u32[]{:S(2)}) collective-permute-start(bf16[1024,256]{1,0:T(8,128)(2,1)S(1)} %get-tuple-element.36.refs_0_), channel_id=1, source_target_pairs={{0,4},{1,2},{2,1},{3,7},{4,0},{5,6},{6,5},{7,3},{8,12},{9,10},{10,... | collective-permute-start | bytes 1572872 | tf_op jit(solution)/shard_map/ppermute | solution.py:547
  87.8 6.1 %collective-permute-start.21 = (bf16[1024,256]{1,0:T(8,128)(2,1)S(1)}, bf16[1024,256]{1,0:T(8,128)(2,1)S(1)}, u32[]{:S(2)}, u32[]{:S(2)}) collective-permute-start(bf16[1024,256]{1,0:T(8,128)(2,1)S(1)} %collective-permute-done.18.refs_0_.refs_1_), channel_id=1, source_target_pairs={{0,4},{1,2},{2,1},{3,7},{4,0},{5,6},{6,5},{7,3},{8,12},{9,10},{10,... | collective-permute-start | bytes 1572872 | tf_op jit(solution)/shard_map/ppermute | solution.py:547
  89.3 13.7 %collective-permute-start.23 = (f32[448,256]{1,0:T(8,128)S(1)}, f32[448,256]{1,0:T(8,128)S(1)}, u32[]{:S(2)}, u32[]{:S(2)}) collective-permute-start(f32[448,256]{1,0:T(8,128)S(1)} %get-tuple-element.39), channel_id=1, source_target_pairs={{0,4},{4,0},{8,12},{12,8},{16,20},{20,16},{24,28},{28,24},{1,5},{5... | collective-permute-start | bytes 1376264 | tf_op jit(solution)/shard_map/ppermute | solution.py:530
  89.9 16.9 %collective-permute-start.20 = (bf16[1024,256]{1,0:T(8,128)(2,1)S(1)}, bf16[1024,256]{1,0:T(8,128)(2,1)S(1)}, u32[]{:S(2)}, u32[]{:S(2)}) collective-permute-start(bf16[1024,256]{1,0:T(8,128)(2,1)S(1)} %collective-permute-done.19.refs_1_.refs_2_), channel_id=1, source_target_pairs={{0,1},{1,0},{2,3},{3,2},{4,5},{5,4},{6,7},{7,6},{8,9},{9,8},{10,11... | collective-permute-start | bytes 1572872 | tf_op jit(solution)/shard_map/ppermute | solution.py:534
  93.9 23.7 %collective-permute-start.22 = (bf16[1024,256]{1,0:T(8,128)(2,1)S(1)}, bf16[1024,256]{1,0:T(8,128)(2,1)S(1)}, u32[]{:S(2)}, u32[]{:S(2)}) collective-permute-start(bf16[1024,256]{1,0:T(8,128)(2,1)S(1)} %collective-permute-done.21.refs_17_.refs_4_), channel_id=1, source_target_pairs={{0,1},{1,0},{2,3},{3,2},{4,5},{5,4},{6,7},{7,6},{8,9},{9,8},{10,11... | collective-permute-start | bytes 1572872 | tf_op jit(solution)/shard_map/ppermute | solution.py:534
  103.0 8.9 %collective-permute-start.24 = (f32[112,256]{1,0:T(8,128)S(1)}, f32[112,256]{1,0:T(8,128)S(1)}, u32[]{:S(2)}, u32[]{:S(2)}) collective-permute-start(f32[112,256]{1,0:T(8,128)S(1)} %sum_terms.19), channel_id=1, source_target_pairs={{0,16},{4,20},{8,24},{12,28},{16,0},{20,4},{24,8},{28,12},{1,17},{... | collective-permute-start | bytes 344072 | tf_op jit(solution)/shard_map/ppermute | solution.py:530
  104.6 13.0 %copy-start = (bf16[32,1,4,128,128]{4,3,2,1,0:T(8,128)(2,1)S(1)}, bf16[32,1,4,128,128]{4,3,2,1,0:T(8,128)(2,1)}, u32[]{:S(2)}) copy-start(bf16[32,1,4,128,128]{4,3,2,1,0:T(8,128)(2,1)} %param.11) | copy-start | bytes 12582916
  104.6 7.3 %collective-permute-start.25 = (f32[112,256]{1,0:T(8,128)S(1)}, f32[112,256]{1,0:T(8,128)S(1)}, u32[]{:S(2)}, u32[]{:S(2)}) collective-permute-start(f32[112,256]{1,0:T(8,128)S(1)} %sum_terms.20), channel_id=1, source_target_pairs={{0,8},{4,12},{8,0},{12,4},{16,24},{20,28},{24,16},{28,20},{1,9},{5... | collective-permute-start | bytes 344072 | tf_op jit(solution)/shard_map/ppermute | solution.py:530
  106.2 5.8 %collective-permute-start.26 = (f32[112,256]{1,0:T(8,128)S(1)}, f32[112,256]{1,0:T(8,128)S(1)}, u32[]{:S(2)}, u32[]{:S(2)}) collective-permute-start(f32[112,256]{1,0:T(8,128)S(1)} %sum_terms.21), channel_id=1, source_target_pairs={{0,24},{4,28},{8,16},{12,20},{16,8},{20,12},{24,0},{28,4},{1,25},{... | collective-permute-start | bytes 344072 | tf_op jit(solution)/shard_map/ppermute | solution.py:530
  124.1 2.7 %collective-permute-start.28 = (bf16[2048,256]{1,0:T(8,128)(2,1)S(1)}, bf16[2048,256]{1,0:T(8,128)(2,1)S(1)}, u32[]{:S(2)}, u32[]{:S(2)}) collective-permute-start(bf16[2048,256]{1,0:T(8,128)(2,1)S(1)} %get-tuple-element.43), channel_id=1, source_target_pairs={{0,4},{4,0},{8,12},{12,8},{16,20},{20,16},{24,28},{28,24},{1,5},{5... | collective-permute-start | bytes 3145736 | tf_op jit(solution)/shard_map/ppermute | solution.py:530
  124.3 5.1 %collective-permute-start.27 = (bf16[2048,256]{1,0:T(8,128)(2,1)S(1)}, bf16[2048,256]{1,0:T(8,128)(2,1)S(1)}, u32[]{:S(2)}, u32[]{:S(2)}) collective-permute-start(bf16[2048,256]{1,0:T(8,128)(2,1)S(1)} %get-tuple-element.42), channel_id=1, source_target_pairs={{0,4},{4,0},{8,12},{12,8},{16,20},{20,16},{24,28},{28,24},{1,5},{5... | collective-permute-start | bytes 3145736 | tf_op jit(solution)/shard_map/ppermute | solution.py:530
  127.1 18.0 %collective-permute-start.30 = (bf16[1024,256]{1,0:T(8,128)(2,1)S(1)}, bf16[1024,256]{1,0:T(8,128)(2,1)S(1)}, u32[]{:S(2)}, u32[]{:S(2)}) collective-permute-start(bf16[1024,256]{1,0:T(8,128)(2,1)S(1)} %sum_terms.24.refs_22_.refs_4_), channel_id=1, source_target_pairs={{0,16},{4,20},{8,24},{12,28},{16,0},{20,4},{24,8},{28,12},{1,17},{... | collective-permute-start | bytes 1572872 | tf_op jit(solution)/shard_map/ppermute | solution.py:530
  127.9 17.4 %collective-permute-start.29 = (bf16[1024,256]{1,0:T(8,128)(2,1)S(1)}, bf16[1024,256]{1,0:T(8,128)(2,1)S(1)}, u32[]{:S(2)}, u32[]{:S(2)}) collective-permute-start(bf16[1024,256]{1,0:T(8,128)(2,1)S(1)} %sum_terms.23.refs_21_.refs_3_), channel_id=1, source_target_pairs={{0,8},{4,12},{8,0},{12,4},{16,24},{20,28},{24,16},{28,20},{1,9},{5... | collective-permute-start | bytes 1572872 | tf_op jit(solution)/shard_map/ppermute | solution.py:530
  129.4 12.0 %collective-permute-start.33 = (bf16[112,256]{1,0:T(8,128)(2,1)S(1)}, bf16[112,256]{1,0:T(8,128)(2,1)S(1)}, u32[]{:S(2)}, u32[]{:S(2)}) collective-permute-start(bf16[112,256]{1,0:T(8,128)(2,1)S(1)} %sum_terms.28.refs_1_), channel_id=1, source_target_pairs={{0,1},{1,2},{2,3},{3,0},{4,5},{5,6},{6,7},{7,4},{8,9},{9,10},{10,1... | collective-permute-start | bytes 172040 | tf_op jit(solution)/shard_map/ppermute | solution.py:538
  132.3 9.1 %collective-permute-start.34 = (bf16[112,256]{1,0:T(8,128)(2,1)S(1)}, bf16[112,256]{1,0:T(8,128)(2,1)S(1)}, u32[]{:S(2)}, u32[]{:S(2)}) collective-permute-start(bf16[112,256]{1,0:T(8,128)(2,1)S(1)} %sum_terms.28.refs_1_), channel_id=1, source_target_pairs={{0,2},{1,3},{2,0},{3,1},{4,6},{5,7},{6,4},{7,5},{8,10},{9,11},{10,... | collective-permute-start | bytes 172040 | tf_op jit(solution)/shard_map/ppermute | solution.py:538
  133.7 7.7 %collective-permute-start.35 = (bf16[112,256]{1,0:T(8,128)(2,1)S(1)}, bf16[112,256]{1,0:T(8,128)(2,1)S(1)}, u32[]{:S(2)}, u32[]{:S(2)}) collective-permute-start(bf16[112,256]{1,0:T(8,128)(2,1)S(1)} %sum_terms.28.refs_1_), channel_id=1, source_target_pairs={{0,3},{1,0},{2,1},{3,2},{4,7},{5,4},{6,5},{7,6},{8,11},{9,8},{10,9... | collective-permute-start | bytes 172040 | tf_op jit(solution)/shard_map/ppermute | solution.py:538
  141.5 5.8 %collective-permute-start.38 = (bf16[112,256]{1,0:T(8,128)(2,1)S(1)}, bf16[112,256]{1,0:T(8,128)(2,1)S(1)}, u32[]{:S(2)}, u32[]{:S(2)}) collective-permute-start(bf16[112,256]{1,0:T(8,128)(2,1)S(1)} %sum_terms.29), channel_id=1, source_target_pairs={{0,24},{4,28},{8,16},{12,20},{16,8},{20,12},{24,0},{28,4},{1,25},{... | collective-permute-start | bytes 172040 | tf_op jit(solution)/shard_map/ppermute | solution.py:530
  142.0 5.2 %collective-permute-start.37 = (bf16[112,256]{1,0:T(8,128)(2,1)S(1)}, bf16[112,256]{1,0:T(8,128)(2,1)S(1)}, u32[]{:S(2)}, u32[]{:S(2)}) collective-permute-start(bf16[112,256]{1,0:T(8,128)(2,1)S(1)} %sum_terms.29), channel_id=1, source_target_pairs={{0,16},{4,20},{8,24},{12,28},{16,0},{20,4},{24,8},{28,12},{1,17},{... | collective-permute-start | bytes 172040 | tf_op jit(solution)/shard_map/ppermute | solution.py:530
  143.0 4.7 %collective-permute-start.36 = (bf16[112,256]{1,0:T(8,128)(2,1)S(1)}, bf16[112,256]{1,0:T(8,128)(2,1)S(1)}, u32[]{:S(2)}, u32[]{:S(2)}) collective-permute-start(bf16[112,256]{1,0:T(8,128)(2,1)S(1)} %sum_terms.29), channel_id=1, source_target_pairs={{0,8},{4,12},{8,0},{12,4},{16,24},{20,28},{24,16},{28,20},{1,9},{5... | collective-permute-start | bytes 172040 | tf_op jit(solution)/shard_map/ppermute | solution.py:530
  145.2 7.2 %collective-permute-start.31 = (bf16[512,256]{1,0:T(8,128)(2,1)S(1)}, bf16[512,256]{1,0:T(8,128)(2,1)S(1)}, u32[]{:S(2)}, u32[]{:S(2)}) collective-permute-start(bf16[512,256]{1,0:T(8,128)(2,1)S(1)} %sum_terms.25), channel_id=1, source_target_pairs={{0,8},{4,12},{8,0},{12,4},{16,24},{20,28},{24,16},{28,20},{1,9},{5... | collective-permute-start | bytes 786440 | tf_op jit(solution)/shard_map/ppermute | solution.py:530
  145.4 7.0 %collective-permute-start.32 = (bf16[512,256]{1,0:T(8,128)(2,1)S(1)}, bf16[512,256]{1,0:T(8,128)(2,1)S(1)}, u32[]{:S(2)}, u32[]{:S(2)}) collective-permute-start(bf16[512,256]{1,0:T(8,128)(2,1)S(1)} %sum_terms.26), channel_id=1, source_target_pairs={{0,16},{4,20},{8,24},{12,28},{16,0},{20,4},{24,8},{28,12},{1,17},{... | collective-permute-start | bytes 786440 | tf_op jit(solution)/shard_map/ppermute | solution.py:530
  147.8 1.6 %collective-permute-start.39 = (bf16[448,256]{1,0:T(8,128)(2,1)S(1)}, bf16[448,256]{1,0:T(8,128)(2,1)S(1)}, u32[]{:S(2)}, u32[]{:S(2)}) collective-permute-start(bf16[448,256]{1,0:T(8,128)(2,1)S(1)} %pad_maximum_fusion.even), channel_id=1, source_target_pairs={{0,4},{4,0},{8,12},{12,8},{16,20},{20,16},{24,28},{28,24},{1,5},{5... | collective-permute-start | bytes 688136 | tf_op jit(solution)/shard_map/ppermute | solution.py:530

commit v13 on v12

--- a/solution.py
+++ b/solution.py
@@ -77,7 +77,7 @@
     return jnp.where(live, tile, jnp.zeros_like(tile))
 
 
-def forward_kernel(outputs, n_pieces, paired, here, cols, counts, *refs):
+def forward_kernel(outputs, n_pieces, paired, here, cols, *refs):
     pieces, tiles = refs[:n_pieces], refs[n_pieces]
     outs = refs[n_pieces + 1 : n_pieces + 1 + len(outputs)]
     nodes_v, tiles_v, sem, tile_sem = refs[n_pieces + 1 + len(outputs) :]
@@ -104,7 +104,7 @@
 
         def step(i, carry, first=first, out=out, index=index, place=place):
             row = first + i
-            count = counts[row]
+            count = cols[slots, row]
             parts = []
             for pair in range(slots // 2):
                 both = (2 * pair, 2 * pair + 1)
@@ -124,7 +124,7 @@
         lax.fori_loop(0, blocks, step, 0, unroll=4)
 
 
-def forward_call(paired, here, cols, counts, pieces, tiles, outputs, rows):
+def forward_call(paired, here, cols, pieces, tiles, outputs, rows):
     width = pieces[0].shape[1]
     gathered = sum(piece.shape[0] for piece in pieces)
     slots, block = tiles.shape[1], tiles.shape[2]
@@ -132,7 +132,7 @@
     return pl.pallas_call(
         functools.partial(forward_kernel, outputs, len(pieces), paired),
         out_shape=[jax.ShapeDtypeStruct((len(picks) * rows, width), BF16) for picks in outputs],
-        in_specs=[SMEM] * 3 + [ANY] * len(pieces) + [HBM],
+        in_specs=[SMEM] * 2 + [ANY] * len(pieces) + [HBM],
         out_specs=[VMEM] * len(outputs),
         scratch_shapes=[
             pltpu.VMEM((gathered, width), BF16),
@@ -143,7 +143,7 @@
         compiler_params=params(48),
         cost_estimate=SMALL,
         name="partial_messages",
-    )(here, cols, counts, *pieces, tiles)
+    )(here, cols, *pieces, tiles)
 
 
 def mlp_kernel(kinds, here, nodes, cot, *refs):
@@ -357,7 +357,47 @@
     lax.fori_loop(full * LIVE_STEP, found, one, 0)
 
 
-def back_kernel(rows, slots, n_grads, n_after, out_pieces, paired, here, cols, counts, *refs):
+def turn_kernel(slots, cols, tiles, out, tiles_v, live, sem):
+    copy = pltpu.make_async_copy(tiles, tiles_v, sem.at[0])
+    copy.start()
+
+    def collect(row, found):
+        count = cols[slots, row]
+        for slot in range(slots):
+            live[found] = row * slots + slot
+            found = found + (slot < count).astype(jnp.int32)
+        return found
+
+    found = lax.fori_loop(0, tiles.shape[0] // slots, collect, jnp.int32(0))
+    copy.wait()
+
+    def entry(place):
+        tile_index = live[place]
+        out[tile_index] = tiles_v[tile_index].T
+
+    for_live(found, entry)
+
+
+def turn_call(cols, tiles):
+    row_blocks, slots, block = tiles.shape[:3]
+    shape = (row_blocks * slots, block, block)
+    return pl.pallas_call(
+        functools.partial(turn_kernel, slots),
+        out_shape=jax.ShapeDtypeStruct(shape, BF16),
+        in_specs=[SMEM, HBM],
+        out_specs=VMEM,
+        scratch_shapes=[
+            pltpu.VMEM(shape, BF16),
+            pltpu.SMEM((row_blocks * slots + 8,), jnp.int32),
+            pltpu.SemaphoreType.DMA((1,)),
+        ],
+        compiler_params=params(16 if row_blocks <= 32 else 32),
+        cost_estimate=SMALL,
+        name="turned_tiles",
+    )(cols, tiles.reshape(shape))
+
+
+def back_kernel(rows, slots, n_grads, n_after, out_pieces, paired, here, cols, *refs):
     grads, tiles = refs[:n_grads], refs[n_grads]
     refs = refs[n_grads + 1 + n_after :]
     outs = refs[: len(out_pieces)]
@@ -371,7 +411,7 @@
     acc[...] = jnp.zeros_like(acc)
 
     def collect(row, found):
-        count = counts[row]
+        count = cols[slots, row]
         for slot in range(slots):
             live[found] = row * slots + slot
             source[found] = here.source(cols[slot, row])
@@ -384,7 +424,7 @@
 
     def entry(place):
         tile_index = live[place]
-        part = mm(tiles_v[tile_index], grad_v[block_at(tile_index // slots, block)], TN)
+        part = mm(tiles_v[tile_index], grad_v[block_at(tile_index // slots, block)])
         acc[block_at(source[place], block)] += part
 
     for_live(found, entry)
@@ -394,33 +434,34 @@
             out[pl.ds(index * piece, piece)] = acc[pl.ds(member * piece, piece)].astype(BF16)
 
 
-def back_call(paired, here, cols, counts, grads, tiles, total, gathered, out_pieces, after=()):
+def back_call(paired, here, cols, grads, tiles, total, gathered, out_pieces, after=()):
     rows, width = grads[0].shape
     rows = total if len(grads) == 1 else rows
-    row_blocks, slots, block = tiles.shape[:3]
+    n_tiles, block = tiles.shape[:2]
+    slots = cols.shape[0] - 1
     piece = gathered // sum(len(members) for members in out_pieces)
     return pl.pallas_call(
         functools.partial(back_kernel, rows, slots, len(grads), len(after), out_pieces, paired),
         out_shape=[jax.ShapeDtypeStruct((len(m) * piece, width), BF16) for m in out_pieces],
-        in_specs=[SMEM] * 3 + [ANY] * len(grads) + [HBM] + [ANY] * len(after),
+        in_specs=[SMEM] * 2 + [ANY] * len(grads) + [HBM] + [ANY] * len(after),
         out_specs=[VMEM] * len(out_pieces),
         scratch_shapes=[
             pltpu.VMEM((total, width), BF16),
-            pltpu.VMEM((row_blocks * slots, block, block), BF16),
+            pltpu.VMEM((n_tiles, block, block), BF16),
             pltpu.VMEM((gathered, width), F32),
-            pltpu.SMEM((row_blocks * slots + 8,), jnp.int32),
-            pltpu.SMEM((row_blocks * slots + 8,), jnp.int32),
+            pltpu.SMEM((n_tiles + 8,), jnp.int32),
+            pltpu.SMEM((n_tiles + 8,), jnp.int32),
             pltpu.SemaphoreType.DMA((len(grads),)),
             pltpu.SemaphoreType.DMA((1,)),
         ],
         compiler_params=params(28 if gathered <= 8192 else 56),
         cost_estimate=SMALL,
         name="back_terms",
-    )(here, cols, counts, *grads, tiles.reshape(row_blocks * slots, block, block), *after)
+    )(here, cols, *grads, tiles, *after)
 
 
 def tile_grad_kernel(
-    rows, slots, n_grads, n_pieces, n_chunks, n_after, groups, paired, here, cols, counts, *refs
+    rows, slots, n_grads, n_pieces, n_chunks, n_after, groups, paired, here, cols, *refs
 ):
     grads = refs[: n_grads * n_chunks]
     refs = refs[n_grads * n_chunks :]
@@ -458,7 +499,7 @@
 
         def collect(i, found, first=first, index=index):
             row = first + i
-            count = counts[row]
+            count = cols[slots, row]
             for slot in range(slots):
                 live[found] = (index * blocks + i) * slots + slot
                 source[found] = here.source(cols[slot, row])
@@ -491,7 +532,7 @@
         copy.wait()
 
 
-def tile_grad_call(paired, here, cols, counts, grads, pieces, shape, rows, groups, base=None, after=()):
+def tile_grad_call(paired, here, cols, grads, pieces, shape, rows, groups, base=None, after=()):
     row_blocks, slots, block = shape[:3]
     chunks = len(grads)
     width = grads[0][0].shape[1] * chunks
@@ -507,9 +548,9 @@
             jax.ShapeDtypeStruct((row_blocks * slots, block, block), BF16),
             jax.ShapeDtypeStruct((8, 128), F32),
         ],
-        in_specs=[SMEM] * 3 + [ANY] * (len(flat) + len(after)),
+        in_specs=[SMEM] * 2 + [ANY] * (len(flat) + len(after)),
         out_specs=[ANY, VMEM],
-        input_output_aliases={} if base is None else {3 + len(flat): 0},
+        input_output_aliases={} if base is None else {2 + len(flat): 0},
         scratch_shapes=[
             pltpu.VMEM((len(groups) * rows, width), BF16),
             pltpu.VMEM((gathered, width), BF16),
@@ -523,7 +564,7 @@
         compiler_params=params(16 if gathered <= 8192 else 40),
         cost_estimate=SMALL,
         name="tile_grads",
-    )(here, cols, counts, *flat, *after)
+    )(here, cols, *flat, *after)
 
 
 def swap(value, bit):
@@ -553,7 +594,7 @@
     y_lower, x_upper = swap(lower, 4), swap(upper, 2)
     x_lower, y_upper = swap(lower, 2), swap(upper, 4)
     d_lower, d_upper = swap(y_lower, 2), swap(x_upper, 4)
-    pieces = [nodes, swap(nodes, 1)]
+    pieces = [lower, upper, swap(nodes, 1)]
     for pair in ((x_lower, x_upper), (y_lower, y_upper), (d_lower, d_upper)):
         pieces += [*pair, *(swap(piece, 1) for piece in pair)]
     return pieces
@@ -637,9 +678,9 @@
     return sum_call(here, value.shape[0], [(term, 0) for term in terms], after=after)
 
 
-def reduce_line(here, far, near, pair, own):
+def reduce_line(here, far, near, pair, own, after):
     rows = own.shape[0]
-    far_sum = inner_swap(sum_call(here, rows, [(far, 0), (outer_swap(far), 0)]))
+    far_sum = inner_swap(sum_call(here, rows, [(far, 0), (outer_swap(far), 0)], after=after))
     near_sum = inner_swap(sum_call(here, rows, [(near, 0), (outer_swap(near), 0)]))
     pair_in = outer_swap(sum_call(here, rows, [(pair, 0)], [(far_sum, 0)]))
     return own, pair_in, near_sum
@@ -658,18 +699,18 @@
     rows, width = nodes.shape
     row_blocks, _, slots, block = tiles.shape[:4]
     tile_local = tiles.reshape(row_blocks, slots, block, block)
-    cols = tile_col.reshape(row_blocks, slots).T
-    counts = tile_count.reshape(row_blocks)
+    table = jnp.concatenate([tile_col.reshape(row_blocks, slots).T, tile_count.reshape(1, row_blocks)], axis=0)
     gathered, total = n_row * rows, n_col * rows
     paired = n_row == 8 and n_col == 4
     here = lax.axis_index(("row", "col")).astype(jnp.int32).reshape(1)
-    known = (paired, here, cols, counts)
+    known = (paired, here, table)
+    turned = turn_call(table, tile_local)
     if paired:
         pieces = [gather_square(nodes)]
         (far,) = forward_call(*known, pieces[0], tile_local, ((0,),), rows)
         (near,) = forward_call(*known, pieces[0], tile_local, ((1,),), rows)
         pair, own = forward_call(*known, pieces[0], tile_local, ((2,), (3,)), rows)
-        parts = [reduce_line(here, far, near, pair, own)]
+        parts = [reduce_line(here, far, near, pair, own, (turned,))]
         kinds = [("all", "all", "inner")]
     else:
         pieces = [[lax.all_gather(nodes, "row", axis=0, tiled=True)]]
@@ -691,7 +732,7 @@
         )
         row_weights = scatter_weights(here, kept, sent, (token,))
         urgent, rest, even = back_call(
-            *known, grads[0], tile_local, total, gathered, halves, (row_weights,)
+            *known, grads[0], turned, total, gathered, halves, (row_weights,)
         )
         urgent, rest = swap(urgent, 1), swap(rest, 1)
         arrived, first = reduce_square(here, even, urgent, rest, rows)
@@ -712,7 +753,7 @@
             weight_sums[2 * width : 3 * width],
             weight_sums[3 * width : 3 * width + 3],
         )
-        (terms,) = back_call(*known, grads[0], tile_local, total, gathered, (tuple(range(n_row)),))
+        (terms,) = back_call(*known, grads[0], turned, total, gathered, (tuple(range(n_row)),))
         back = lax.psum_scatter(terms, "row", scatter_dimension=0, tiled=True)
         grad_nodes = sum_call(here, rows, [(direct, 0), (back, 0)])
         grad_tiles, _ = tile_grad_call(

time: 154 us -> 153 us (level)
  Pallas kernels: 34.6 us -> 39.7 us
  waiting for transfers between devices: 67.5 us -> 63.4 us
  local copies, waits for them, and re-layouts: 3.48 us -> 1.12 us
    ppermute x6, waiting for transfers between devices: 42.8 us -> 39.1 us  [outer_swap(): return lax.ppermute(value, 'col', [(0, 1), (1, 0), (2, 3), (3, 2)])]
    pallas_call x0 -> x1, Pallas kernels: none -> 2.9 us  [turn_call(): pl.pallas_call(functools.partial(turn_kernel, slots), out_shape=jax.Shape...]
    unnamed x20, local copies, waits for them, and re-layouts: 2.42 us -> 0.06 us
  transfers between devices with their start and end apart: 40 -> 40, of which waited for: 17 -> 17; matrix products, arithmetic and copies ran while one was open for 1% -> 1% of each run, Pallas kernels for 13% -> 16%
where the time goes in v13:
time: 153 us; the launch traced here: 152 us
  waiting for transfers between devices  63.4 us (41%)
  starting transfers between devices  46.1 us (30%)
  Pallas kernels  39.7 us (26%)
    ppermute x6, waiting for transfers between devices, outer_swap(): return lax.ppermute(value, 'col', [(0, 1), (1, 0), (2, 3), (3, 2)])  39.1 us
    ppermute x27, waiting for transfers between devices, swap(): return lax.ppermute(value, 'row', [(i, i ^ bit) for i in range(8)])  24.3 us
    ppermute x6, starting transfers between devices, outer_swap(): return lax.ppermute(value, 'col', [(0, 1), (1, 0), (2, 3), (3, 2)])  20.4 us
    ppermute x27, starting transfers between devices, swap(): return lax.ppermute(value, 'row', [(i, i ^ bit) for i in range(8)])  18.9 us
    pallas_call x2, Pallas kernels, tile_grad_call(): pl.pallas_call(functools.partial(tile_grad_kernel, rows, slots, len(grads...  11 us
    pallas_call x3, Pallas kernels, forward_call(): pl.pallas_call(functools.partial(forward_kernel, outputs, len(pieces), pa...  10.4 us
    pallas_call x1, Pallas kernels, back_call(): pl.pallas_call(functools.partial(back_kernel, rows, slots, len(grads), le...  6.7 us
    ppermute x3, starting transfers between devices, turn(): return lax.ppermute(value, 'col', [(i, (i + by) % 4) for i in range(4)])  6.69 us
  transfers between devices with their start and end apart: 40, of which 17 were waited for; matrix products, arithmetic and copies ran while one was open for 1% of the time, Pallas kernels for 16%

profile of v13, /device:TPU:0, one launch (start us, length us, event | category | flops | bytes accessed | tf_op | source)
XLA Modules:
  0.0 152.1 jit_solution(14158463330909552603)
XLA Ops:
  0.6 0.5 collective-permute-start
  1.1 1.1 fusion
  2.2 2.6 %collective-permute-start.1 = (bf16[512,256]{1,0:T(8,128)(2,1)S(1)}, bf16[512,256]{1,0:T(8,128)(2,1)S(1)}, u32[]{:S(2)}, u32[]{:S(2)}) collective-permute-start(bf16[512,256]{1,0:T(8,128)(2,1)S(1)} %get-tuple-element.57.refs_0_.refs_2_.refs_6_), channel_id=1, source_target_pairs={{0,8},{4,12},{8,0},{12,4},{16,24},{20,28},{24,16},{28,20},{1,9},{5... | collective-permute-start | bytes 786440 | tf_op jit(solution)/shard_map/ppermute | solution.py:571
  4.8 1.5 collective-permute-start.5
  6.3 0.5 collective-permute-start.2
  6.9 5.1 %collective-permute-done.1.refs_3_.refs_5_.refs_9_ = bf16[512,256]{1,0:T(8,128)(2,1)S(1)} collective-permute-done((bf16[512,256]{1,0:T(8,128)(2,1)S(1)}, bf16[512,256]{1,0:T(8,128)(2,1)S(1)}, u32[]{:S(2)}, u32[]{:S(2)}) %collective-permute-start.1) | collective-permute-done | bytes 262176 | tf_op jit(solution)/shard_map/ppermute | solution.py:571
  11.9 2.0 %collective-permute-done.5.refs_7_.refs_9_.refs_13_ = bf16[512,256]{1,0:T(8,128)(2,1)S(1)} collective-permute-done((bf16[512,256]{1,0:T(8,128)(2,1)S(1)}, bf16[512,256]{1,0:T(8,128)(2,1)S(1)}, u32[]{:S(2)}, u32[]{:S(2)}) %collective-permute-start.5) | collective-permute-done | bytes 262176 | tf_op jit(solution)/shard_map/ppermute | solution.py:571
  14.0 3.6 %collective-permute-done.2.refs_4_.refs_6_.refs_10_ = bf16[512,256]{1,0:T(8,128)(2,1)S(1)} collective-permute-done((bf16[512,256]{1,0:T(8,128)(2,1)S(1)}, bf16[512,256]{1,0:T(8,128)(2,1)S(1)}, u32[]{:S(2)}, u32[]{:S(2)}) %collective-permute-start.2) | collective-permute-done | bytes 262176 | tf_op jit(solution)/shard_map/ppermute | solution.py:571
  17.6 2.0 %collective-permute-start.10 = (bf16[512,256]{1,0:T(8,128)(2,1)S(1)}, bf16[512,256]{1,0:T(8,128)(2,1)S(1)}, u32[]{:S(2)}, u32[]{:S(2)}) collective-permute-start(bf16[512,256]{1,0:T(8,128)(2,1)S(1)} %collective-permute-done.2.refs_4_.refs_6_.refs_10_), channel_id=1, source_target_pairs={{0,16},{4,20},{8,24},{12,28},{16,0},{20,4},{24,8},{28,12},{1,17},{... | collective-permute-start | bytes 786440 | tf_op jit(solution)/shard_map/ppermute | solution.py:571
  19.5 0.5 collective-permute-start.7
  20.1 2.9 %collective-permute-done.9.refs_11_.refs_13_.refs_17_ = bf16[512,256]{1,0:T(8,128)(2,1)S(1)} collective-permute-done((bf16[512,256]{1,0:T(8,128)(2,1)S(1)}, bf16[512,256]{1,0:T(8,128)(2,1)S(1)}, u32[]{:S(2)}, u32[]{:S(2)}) %collective-permute-start.9) | collective-permute-done | bytes 262176 | tf_op jit(solution)/shard_map/ppermute | solution.py:571
  23.0 2.5 %collective-permute-done.10.refs_12_.refs_14_.refs_18_ = bf16[512,256]{1,0:T(8,128)(2,1)S(1)} collective-permute-done((bf16[512,256]{1,0:T(8,128)(2,1)S(1)}, bf16[512,256]{1,0:T(8,128)(2,1)S(1)}, u32[]{:S(2)}, u32[]{:S(2)}) %collective-permute-start.10) | collective-permute-done | bytes 262176 | tf_op jit(solution)/shard_map/ppermute | solution.py:571
  25.5 0.7 pad_add_fusion.cols
  26.2 0.9 collective-permute-done.12.refs_14_.refs_16_.refs_20_
  27.2 3.5 %partial_messages.4.refs_1_ = bf16[1024,256]{1,0:T(8,128)(2,1)S(1)} custom-call(s32[1]{0:T(128)} %bitcast.here.refs_0_, s32[5,32]{1,0:T(8,128)S(1)} %pad_add_fusion.cols, bf16[512,256]{1,0:T(8,128)(2,1)S(1)} %get-tuple-element.57.refs_0_.refs_2_.refs_6_, bf16[512,256]{1,0:T(8,128)(2,1)S(1)} %get-tuple-element.56.refs_1_.refs_3_.refs_7_, ...), custom_call_target="tpu_custom_call" | custom-call | flops 1048576 | bytes 65536 | tf_op jit(solution)/shard_map/partial_messages/pallas_call | solution.py:132
  30.7 1.7 %collective-permute-start.13 = (bf16[1024,256]{1,0:T(8,128)(2,1)S(1)}, bf16[1024,256]{1,0:T(8,128)(2,1)S(1)}, u32[]{:S(2)}, u32[]{:S(2)}) collective-permute-start(bf16[1024,256]{1,0:T(8,128)(2,1)S(1)} %partial_messages.4.refs_1_), channel_id=1, source_target_pairs={{0,1},{1,0},{2,3},{3,2},{4,5},{5,4},{6,7},{7,6},{8,9},{9,8},{10,11... | collective-permute-start | bytes 1572872 | tf_op jit(solution)/shard_map/ppermute | solution.py:575
  32.4 2.9 %turned_tiles.1.refs_3_.refs_6_ = bf16[128,128,128]{2,1,0:T(8,128)(2,1)S(1)} custom-call(s32[5,32]{1,0:T(8,128)S(1)} %pad_add_fusion.cols, bf16[128,128,128]{2,1,0:T(8,128)(2,1)S(1)} %bitcast.16), custom_call_target="tpu_custom_call" | custom-call | flops 1048576 | bytes 65536 | tf_op jit(solution)/shard_map/turned_tiles/pallas_call | solution.py:384
  35.3 3.1 %partial_messages.5.refs_1_ = bf16[1024,256]{1,0:T(8,128)(2,1)S(1)} custom-call(s32[1]{0:T(128)} %bitcast.here.refs_0_, s32[5,32]{1,0:T(8,128)S(1)} %pad_add_fusion.cols, bf16[512,256]{1,0:T(8,128)(2,1)S(1)} %get-tuple-element.57.refs_0_.refs_2_.refs_6_, bf16[512,256]{1,0:T(8,128)(2,1)S(1)} %get-tuple-element.56.refs_1_.refs_3_.refs_7_, ...), custom_call_target="tpu_custom_call" | custom-call | flops 1048576 | bytes 65536 | tf_op jit(solution)/shard_map/partial_messages/pallas_call | solution.py:132
  38.4 0.2 collective-permute-start.16
  38.6 6.9 %collective-permute-done.13.refs_2_ = bf16[1024,256]{1,0:T(8,128)(2,1)S(1)} collective-permute-done((bf16[1024,256]{1,0:T(8,128)(2,1)S(1)}, bf16[1024,256]{1,0:T(8,128)(2,1)S(1)}, u32[]{:S(2)}, u32[]{:S(2)}) %collective-permute-start.13) | collective-permute-done | bytes 524320 | tf_op jit(solution)/shard_map/ppermute | solution.py:575
  45.5 0.2 sum_terms.15
  45.8 3.7 %partial_messages.3 = (bf16[1024,256]{1,0:T(8,128)(2,1)S(1)}, bf16[1024,256]{1,0:T(8,128)(2,1)S(1)}) custom-call(s32[1]{0:T(128)} %bitcast.here.refs_0_, s32[5,32]{1,0:T(8,128)S(1)} %pad_add_fusion.cols, bf16[512,256]{1,0:T(8,128)(2,1)S(1)} %get-tuple-element.57.refs_0_.refs_2_.refs_6_, bf16[512,256]{1,0:T(8,128)(2,1)S(1)} %get-tuple-element.56.refs_1_.refs_3_.refs_7_, ...), custom_call_target="tpu_custom_call" | custom-call | flops 1048576 | bytes 65536 | tf_op jit(solution)/shard_map/partial_messages/pallas_call | solution.py:132
  49.6 6.3 %collective-permute-done.16.refs_2_ = bf16[1024,256]{1,0:T(8,128)(2,1)S(1)} collective-permute-done((bf16[1024,256]{1,0:T(8,128)(2,1)S(1)}, bf16[1024,256]{1,0:T(8,128)(2,1)S(1)}, u32[]{:S(2)}, u32[]{:S(2)}) %collective-permute-start.16) | collective-permute-done | bytes 524320 | tf_op jit(solution)/shard_map/ppermute | solution.py:575
  55.9 0.2 sum_terms.17
  56.2 0.2 sum_terms.16
  56.5 3.6 %collective-permute-start.15 = (bf16[1024,256]{1,0:T(8,128)(2,1)S(1)}, bf16[1024,256]{1,0:T(8,128)(2,1)S(1)}, u32[]{:S(2)}, u32[]{:S(2)}) collective-permute-start(bf16[1024,256]{1,0:T(8,128)(2,1)S(1)} %sum_terms.16), channel_id=1, source_target_pairs={{0,1},{1,0},{2,3},{3,2},{4,5},{5,4},{6,7},{7,6},{8,9},{9,8},{10,11... | collective-permute-start | bytes 1572872 | tf_op jit(solution)/shard_map/ppermute | solution.py:575
  60.1 10.7 %collective-permute-done.15.refs_1_ = bf16[1024,256]{1,0:T(8,128)(2,1)S(1)} collective-permute-done((bf16[1024,256]{1,0:T(8,128)(2,1)S(1)}, bf16[1024,256]{1,0:T(8,128)(2,1)S(1)}, u32[]{:S(2)}, u32[]{:S(2)}) %collective-permute-start.15) | collective-permute-done | bytes 524320 | tf_op jit(solution)/shard_map/ppermute | solution.py:575
  70.9 3.2 %mlp.1 = (bf16[1024,256]{1,0:T(8,128)(2,1)}, bf16[1024,256]{1,0:T(8,128)(2,1)S(1)}, bf16[1024,256]{1,0:T(8,128)(2,1)S(1)}, bf16[1024,256]{1,0:T(8,128)(2,1)S(1)}...) custom-call(s32[1]{0:T(128)} %bitcast.here.refs_0_, ...), custom_call_target="tpu_custom_call" | custom-call | flops 1048576 | bytes 65536 | tf_op jit(solution)/shard_map/mlp/pallas_call | solution.py:226
  74.1 1.7 %collective-permute-start.18 = (bf16[1024,256]{1,0:T(8,128)(2,1)S(1)}, bf16[1024,256]{1,0:T(8,128)(2,1)S(1)}, u32[]{:S(2)}, u32[]{:S(2)}) collective-permute-start(bf16[1024,256]{1,0:T(8,128)(2,1)S(1)} %get-tuple-element.36.refs_0_), channel_id=1, source_target_pairs={{0,1},{1,0},{2,3},{3,2},{4,5},{5,4},{6,7},{7,6},{8,9},{9,8},{10,11... | collective-permute-start | bytes 1572872 | tf_op jit(solution)/shard_map/ppermute | solution.py:575
  75.8 10.1 %collective-permute-done.18.refs_0_.refs_1_ = bf16[1024,256]{1,0:T(8,128)(2,1)S(1)} collective-permute-done((bf16[1024,256]{1,0:T(8,128)(2,1)S(1)}, bf16[1024,256]{1,0:T(8,128)(2,1)S(1)}, u32[]{:S(2)}, u32[]{:S(2)}) %collective-permute-start.18) | collective-permute-done | bytes 524320 | tf_op jit(solution)/shard_map/ppermute | solution.py:575
  85.9 1.5 %weight_grads.1 = (f32[448,256]{1,0:T(8,128)S(1)}, f32[448,256]{1,0:T(8,128)S(1)}, f32[1024,256]{1,0:T(8,128)S(1)}) custom-call(s32[1]{0:T(128)} %bitcast.here.refs_0_, bf16[1024,256]{1,0:T(8,128)(2,1)S(1)} %copy-done.3, bf16[1024,256]{1,0:T(8,128)(2,1)S(1)} %get-tuple-element.31.msg, bf16[1024,256]{1,0:T(8,128)(2,1)S(1)} %get-tuple-element.32.act, ...), custom_call_target="tpu_custom_call" | custom-call | flops 1048576 | bytes 65536 | tf_op jit(solution)/shard_map/weight_grads/pallas_call | solution.py:279
  87.5 0.6 collective-permute-start.23
  88.0 4.1 %collective-permute-start.20 = (bf16[1024,256]{1,0:T(8,128)(2,1)S(1)}, bf16[1024,256]{1,0:T(8,128)(2,1)S(1)}, u32[]{:S(2)}, u32[]{:S(2)}) collective-permute-start(bf16[1024,256]{1,0:T(8,128)(2,1)S(1)} %collective-permute-done.19.refs_1_.refs_2_), channel_id=1, source_target_pairs={{0,1},{1,0},{2,3},{3,2},{4,5},{5,4},{6,7},{7,6},{8,9},{9,8},{10,11... | collective-permute-start | bytes 1572872 | tf_op jit(solution)/shard_map/ppermute | solution.py:575
  92.1 9.0 %collective-permute-start.22 = (bf16[1024,256]{1,0:T(8,128)(2,1)S(1)}, bf16[1024,256]{1,0:T(8,128)(2,1)S(1)}, u32[]{:S(2)}, u32[]{:S(2)}) collective-permute-start(bf16[1024,256]{1,0:T(8,128)(2,1)S(1)} %collective-permute-done.21.refs_18_.refs_4_), channel_id=1, source_target_pairs={{0,1},{1,0},{2,3},{3,2},{4,5},{5,4},{6,7},{7,6},{8,9},{9,8},{10,11... | collective-permute-start | bytes 1572872 | tf_op jit(solution)/shard_map/ppermute | solution.py:575
  101.2 1.6 %collective-permute-start.24 = (f32[112,256]{1,0:T(8,128)S(1)}, f32[112,256]{1,0:T(8,128)S(1)}, u32[]{:S(2)}, u32[]{:S(2)}) collective-permute-start(f32[112,256]{1,0:T(8,128)S(1)} %sum_terms.19), channel_id=1, source_target_pairs={{0,16},{4,20},{8,24},{12,28},{16,0},{20,4},{24,8},{28,12},{1,17},{... | collective-permute-start | bytes 344072 | tf_op jit(solution)/shard_map/ppermute | solution.py:571
  102.8 1.6 %collective-permute-start.25 = (f32[112,256]{1,0:T(8,128)S(1)}, f32[112,256]{1,0:T(8,128)S(1)}, u32[]{:S(2)}, u32[]{:S(2)}) collective-permute-start(f32[112,256]{1,0:T(8,128)S(1)} %sum_terms.20), channel_id=1, source_target_pairs={{0,8},{4,12},{8,0},{12,4},{16,24},{20,28},{24,16},{28,20},{1,9},{5... | collective-permute-start | bytes 344072 | tf_op jit(solution)/shard_map/ppermute | solution.py:571
  104.4 0.5 collective-permute-start.26
  104.9 5.8 %tile_grads.2 = (bf16[128,128,128]{2,1,0:T(8,128)(2,1)}, f32[8,128]{1,0:T(8,128)S(1)}) custom-call(s32[1]{0:T(128)} %bitcast.here.refs_0_, s32[5,32]{1,0:T(8,128)S(1)} %pad_add_fusion.cols, bf16[1024,256]{1,0:T(8,128)(2,1)S(1)} %get-tuple-element.36.refs_0_, bf16[1024,256]{1,0:T(8,128)(2,1)S(1)} %collective-permute-done.18.refs_0_.refs_1_, ...), custom_call_target="tpu_custom_call" | custom-call | flops 1048576 | bytes 65536 | tf_op jit(solution)/shard_map/tile_grads/pallas_call | solution.py:543
  110.8 5.1 %collective-permute-done.22.refs_5_ = bf16[1024,256]{1,0:T(8,128)(2,1)S(1)} collective-permute-done((bf16[1024,256]{1,0:T(8,128)(2,1)S(1)}, bf16[1024,256]{1,0:T(8,128)(2,1)S(1)}, u32[]{:S(2)}, u32[]{:S(2)}) %collective-permute-start.22) | collective-permute-done | bytes 524320 | tf_op jit(solution)/shard_map/ppermute | solution.py:575
  115.9 6.7 %back_terms.1 = (bf16[2048,256]{1,0:T(8,128)(2,1)S(1)}, bf16[2048,256]{1,0:T(8,128)(2,1)S(1)}, bf16[4096,256]{1,0:T(8,128)(2,1)S(1)}) custom-call(s32[1]{0:T(128)} %bitcast.here.refs_0_, s32[5,32]{1,0:T(8,128)S(1)} %pad_add_fusion.cols, bf16[1024,256]{1,0:T(8,128)(2,1)S(1)} %get-tuple-element.36.refs_0_, ...), custom_call_target="tpu_custom_call" | custom-call | flops 1048576 | bytes 65536 | tf_op jit(solution)/shard_map/back_terms/pallas_call | solution.py:443
  122.6 0.5 collective-permute-start.27
  123.1 2.1 %collective-permute-done.28.refs_2_ = bf16[2048,256]{1,0:T(8,128)(2,1)S(1)} collective-permute-done((bf16[2048,256]{1,0:T(8,128)(2,1)S(1)}, bf16[2048,256]{1,0:T(8,128)(2,1)S(1)}, u32[]{:S(2)}, u32[]{:S(2)}) %collective-permute-start.28) | collective-permute-done | bytes 1048608 | tf_op jit(solution)/shard_map/ppermute | solution.py:571
  125.3 0.2 sum_terms.24.refs_23_.refs_4_
  125.5 0.5 collective-permute-start.30
  126.0 0.2 sum_terms.23.refs_22_.refs_3_
  126.2 0.8 collective-permute-start.29
  127.0 2.0 %collective-permute-start.33 = (bf16[112,256]{1,0:T(8,128)(2,1)S(1)}, bf16[112,256]{1,0:T(8,128)(2,1)S(1)}, u32[]{:S(2)}, u32[]{:S(2)}) collective-permute-start(bf16[112,256]{1,0:T(8,128)(2,1)S(1)} %sum_terms.28.refs_1_), channel_id=1, source_target_pairs={{0,1},{1,2},{2,3},{3,0},{4,5},{5,6},{6,7},{7,4},{8,9},{9,10},{10,1... | collective-permute-start | bytes 172040 | tf_op jit(solution)/shard_map/ppermute | solution.py:579
  128.9 1.9 %collective-permute-start.34 = (bf16[112,256]{1,0:T(8,128)(2,1)S(1)}, bf16[112,256]{1,0:T(8,128)(2,1)S(1)}, u32[]{:S(2)}, u32[]{:S(2)}) collective-permute-start(bf16[112,256]{1,0:T(8,128)(2,1)S(1)} %sum_terms.28.refs_1_), channel_id=1, source_target_pairs={{0,2},{1,3},{2,0},{3,1},{4,6},{5,7},{6,4},{7,5},{8,10},{9,11},{10,... | collective-permute-start | bytes 172040 | tf_op jit(solution)/shard_map/ppermute | solution.py:579
  130.8 2.8 %collective-permute-start.35 = (bf16[112,256]{1,0:T(8,128)(2,1)S(1)}, bf16[112,256]{1,0:T(8,128)(2,1)S(1)}, u32[]{:S(2)}, u32[]{:S(2)}) collective-permute-start(bf16[112,256]{1,0:T(8,128)(2,1)S(1)} %sum_terms.28.refs_1_), channel_id=1, source_target_pairs={{0,3},{1,0},{2,1},{3,2},{4,7},{5,4},{6,5},{7,6},{8,11},{9,8},{10,9... | collective-permute-start | bytes 172040 | tf_op jit(solution)/shard_map/ppermute | solution.py:579
  133.7 5.2 %tile_grads.3 = (bf16[128,128,128]{2,1,0:T(8,128)(2,1)}, f32[8,128]{1,0:T(8,128)S(1)}) custom-call(s32[1]{0:T(128)} %bitcast.here.refs_0_, s32[5,32]{1,0:T(8,128)S(1)} %pad_add_fusion.cols, bf16[1024,256]{1,0:T(8,128)(2,1)S(1)} %get-tuple-element.36.refs_0_, ...), custom_call_target="tpu_custom_call", output_to_operand_aliasing={{0}: (23, {})} | custom-call | flops 1048576 | bytes 65536 | tf_op jit(solution)/shard_map/tile_grads/pallas_call | solution.py:543
  139.0 0.6 collective-permute-start.38
  139.6 2.1 %collective-permute-start.37 = (bf16[112,256]{1,0:T(8,128)(2,1)S(1)}, bf16[112,256]{1,0:T(8,128)(2,1)S(1)}, u32[]{:S(2)}, u32[]{:S(2)}) collective-permute-start(bf16[112,256]{1,0:T(8,128)(2,1)S(1)} %sum_terms.29), channel_id=1, source_target_pairs={{0,16},{4,20},{8,24},{12,28},{16,0},{20,4},{24,8},{28,12},{1,17},{... | collective-permute-start | bytes 172040 | tf_op jit(solution)/shard_map/ppermute | solution.py:571
  141.7 0.9 collective-permute-start.36
  142.5 0.1 sum_terms.25
  142.7 1.2 collective-permute-start.31
  143.9 0.1 sum_terms.26
  144.0 0.2 collective-permute-start.32
  144.2 0.5 collective-permute-done.38
  144.7 1.8 %collective-permute-done.36 = bf16[112,256]{1,0:T(8,128)(2,1)S(1)} collective-permute-done((bf16[112,256]{1,0:T(8,128)(2,1)S(1)}, bf16[112,256]{1,0:T(8,128)(2,1)S(1)}, u32[]{:S(2)}, u32[]{:S(2)}) %collective-permute-start.36) | collective-permute-done | bytes 57376 | tf_op jit(solution)/shard_map/ppermute | solution.py:571
  146.6 1.5 collective-permute-done.39.odd
  148.1 1.0 weight_unpack.1
  149.0 1.1 collective-permute-done.31.refs_5_
  150.1 0.4 collective-permute-done.32.refs_6_
  150.5 1.6 %sum_terms.27 = bf16[1024,256]{1,0:T(8,128)(2,1)} custom-call(s32[1]{0:T(128)} %bitcast.here.refs_0_, f32[1024,256]{1,0:T(8,128)S(1)} %get-tuple-element.37.refs_1_, bf16[4096,256]{1,0:T(8,128)(2,1)S(1)} %get-tuple-element.41.refs_1_.refs_2_, bf16[2048,256]{1,0:T(8,128)(2,1)S(1)} %collective-permute-done.27.refs_2_.refs_3_, ...), custom_call_target="tpu_custom_call" | custom-call | flops 1048576 | bytes 65536 | tf_op jit(solution)/shard_map/sum_terms/pallas_call | solution.py:651
  (64 shorter events, 0.7 us)
Async XLA Ops:
  0.6 18.9 %collective-permute-start = (bf16[1024,256]{1,0:T(8,128)(2,1)}, bf16[1024,256]{1,0:T(8,128)(2,1)S(1)}, u32[]{:S(2)}, u32[]{:S(2)}) collective-permute-start(bf16[1024,256]{1,0:T(8,128)(2,1)} %nodes.3), channel_id=1, source_target_pairs={{0,4},{4,0},{8,12},{12,8},{16,20},{20,16},{24,28},{28,24},{1,5},{5... | collective-permute-start | bytes 1572872 | tf_op jit(solution)/shard_map/ppermute | solution.py:571
  2.2 9.7 %collective-permute-start.1 = (bf16[512,256]{1,0:T(8,128)(2,1)S(1)}, bf16[512,256]{1,0:T(8,128)(2,1)S(1)}, u32[]{:S(2)}, u32[]{:S(2)}) collective-permute-start(bf16[512,256]{1,0:T(8,128)(2,1)S(1)} %get-tuple-element.57.refs_0_.refs_2_.refs_6_), channel_id=1, source_target_pairs={{0,8},{4,12},{8,0},{12,4},{16,24},{20,28},{24,16},{28,20},{1,9},{5... | collective-permute-start | bytes 786440 | tf_op jit(solution)/shard_map/ppermute | solution.py:571
  4.8 9.1 %collective-permute-start.5 = (bf16[512,256]{1,0:T(8,128)(2,1)S(1)}, bf16[512,256]{1,0:T(8,128)(2,1)S(1)}, u32[]{:S(2)}, u32[]{:S(2)}) collective-permute-start(bf16[512,256]{1,0:T(8,128)(2,1)S(1)} %get-tuple-element.57.refs_0_.refs_2_.refs_6_), channel_id=1, source_target_pairs={{0,16},{4,20},{8,24},{12,28},{16,0},{20,4},{24,8},{28,12},{1,17},{... | collective-permute-start | bytes 786440 | tf_op jit(solution)/shard_map/ppermute | solution.py:571
  6.3 11.3 %collective-permute-start.2 = (bf16[512,256]{1,0:T(8,128)(2,1)S(1)}, bf16[512,256]{1,0:T(8,128)(2,1)S(1)}, u32[]{:S(2)}, u32[]{:S(2)}) collective-permute-start(bf16[512,256]{1,0:T(8,128)(2,1)S(1)} %get-tuple-element.56.refs_1_.refs_3_.refs_7_), channel_id=1, source_target_pairs={{0,8},{4,12},{8,0},{12,4},{16,24},{20,28},{24,16},{28,20},{1,9},{5... | collective-permute-start | bytes 786440 | tf_op jit(solution)/shard_map/ppermute | solution.py:571
  6.8 12.7 %collective-permute-start.6 = (bf16[512,256]{1,0:T(8,128)(2,1)S(1)}, bf16[512,256]{1,0:T(8,128)(2,1)S(1)}, u32[]{:S(2)}, u32[]{:S(2)}) collective-permute-start(bf16[512,256]{1,0:T(8,128)(2,1)S(1)} %get-tuple-element.56.refs_1_.refs_3_.refs_7_), channel_id=1, source_target_pairs={{0,16},{4,20},{8,24},{12,28},{16,0},{20,4},{24,8},{28,12},{1,17},{... | collective-permute-start | bytes 786440 | tf_op jit(solution)/shard_map/ppermute | solution.py:571
  11.9 8.1 %collective-permute-start.3 = (bf16[512,256]{1,0:T(8,128)(2,1)S(1)}, bf16[512,256]{1,0:T(8,128)(2,1)S(1)}, u32[]{:S(2)}, u32[]{:S(2)}) collective-permute-start(bf16[512,256]{1,0:T(8,128)(2,1)S(1)} %collective-permute-done.1.refs_3_.refs_5_.refs_9_), channel_id=1, source_target_pairs={{0,4},{4,0},{8,12},{12,8},{16,20},{20,16},{24,28},{28,24},{1,5},{5... | collective-permute-start | bytes 786440 | tf_op jit(solution)/shard_map/ppermute | solution.py:571
  13.9 9.1 %collective-permute-start.9 = (bf16[512,256]{1,0:T(8,128)(2,1)S(1)}, bf16[512,256]{1,0:T(8,128)(2,1)S(1)}, u32[]{:S(2)}, u32[]{:S(2)}) collective-permute-start(bf16[512,256]{1,0:T(8,128)(2,1)S(1)} %collective-permute-done.5.refs_7_.refs_9_.refs_13_), channel_id=1, source_target_pairs={{0,8},{4,12},{8,0},{12,4},{16,24},{20,28},{24,16},{28,20},{1,9},{5... | collective-permute-start | bytes 786440 | tf_op jit(solution)/shard_map/ppermute | solution.py:571
  17.6 7.9 %collective-permute-start.10 = (bf16[512,256]{1,0:T(8,128)(2,1)S(1)}, bf16[512,256]{1,0:T(8,128)(2,1)S(1)}, u32[]{:S(2)}, u32[]{:S(2)}) collective-permute-start(bf16[512,256]{1,0:T(8,128)(2,1)S(1)} %collective-permute-done.2.refs_4_.refs_6_.refs_10_), channel_id=1, source_target_pairs={{0,16},{4,20},{8,24},{12,28},{16,0},{20,4},{24,8},{28,12},{1,17},{... | collective-permute-start | bytes 786440 | tf_op jit(solution)/shard_map/ppermute | solution.py:571
  19.5 6.7 %collective-permute-start.4 = (bf16[512,256]{1,0:T(8,128)(2,1)S(1)}, bf16[512,256]{1,0:T(8,128)(2,1)S(1)}, u32[]{:S(2)}, u32[]{:S(2)}) collective-permute-start(bf16[512,256]{1,0:T(8,128)(2,1)S(1)} %collective-permute-done.2.refs_4_.refs_6_.refs_10_), channel_id=1, source_target_pairs={{0,4},{4,0},{8,12},{12,8},{16,20},{20,16},{24,28},{28,24},{1,5},{5... | collective-permute-start | bytes 786440 | tf_op jit(solution)/shard_map/ppermute | solution.py:571
  19.5 6.7 %collective-permute-start.7 = (bf16[512,256]{1,0:T(8,128)(2,1)S(1)}, bf16[512,256]{1,0:T(8,128)(2,1)}, u32[]{:S(2)}, u32[]{:S(2)}) collective-permute-start(bf16[512,256]{1,0:T(8,128)(2,1)S(1)} %collective-permute-done.5.refs_7_.refs_9_.refs_13_), channel_id=1, source_target_pairs={{0,4},{4,0},{8,12},{12,8},{16,20},{20,16},{24,28},{28,24},{1,5},{5... | collective-permute-start | bytes 786440 | tf_op jit(solution)/shard_map/ppermute | solution.py:571
  20.1 6.2 %collective-permute-start.8 = (bf16[512,256]{1,0:T(8,128)(2,1)S(1)}, bf16[512,256]{1,0:T(8,128)(2,1)}, u32[]{:S(2)}, u32[]{:S(2)}) collective-permute-start(bf16[512,256]{1,0:T(8,128)(2,1)S(1)} %collective-permute-done.6.refs_8_.refs_10_.refs_14_), channel_id=1, source_target_pairs={{0,4},{4,0},{8,12},{12,8},{16,20},{20,16},{24,28},{28,24},{1,5},{5... | collective-permute-start | bytes 786440 | tf_op jit(solution)/shard_map/ppermute | solution.py:571
  23.0 3.3 %collective-permute-start.11 = (bf16[512,256]{1,0:T(8,128)(2,1)S(1)}, bf16[512,256]{1,0:T(8,128)(2,1)}, u32[]{:S(2)}, u32[]{:S(2)}) collective-permute-start(bf16[512,256]{1,0:T(8,128)(2,1)S(1)} %collective-permute-done.9.refs_11_.refs_13_.refs_17_), channel_id=1, source_target_pairs={{0,4},{4,0},{8,12},{12,8},{16,20},{20,16},{24,28},{28,24},{1,5},{5... | collective-permute-start | bytes 786440 | tf_op jit(solution)/shard_map/ppermute | solution.py:571
  25.5 1.7 %collective-permute-start.12 = (bf16[512,256]{1,0:T(8,128)(2,1)S(1)}, bf16[512,256]{1,0:T(8,128)(2,1)}, u32[]{:S(2)}, u32[]{:S(2)}) collective-permute-start(bf16[512,256]{1,0:T(8,128)(2,1)S(1)} %collective-permute-done.10.refs_12_.refs_14_.refs_18_), channel_id=1, source_target_pairs={{0,4},{4,0},{8,12},{12,8},{16,20},{20,16},{24,28},{28,24},{1,5},{5... | collective-permute-start | bytes 786440 | tf_op jit(solution)/shard_map/ppermute | solution.py:571
  26.2 4.5 %copy-start.1 = (bf16[512,256]{1,0:T(8,128)(2,1)}, bf16[512,256]{1,0:T(8,128)(2,1)S(1)}, u32[]{:S(2)}) copy-start(bf16[512,256]{1,0:T(8,128)(2,1)S(1)} %collective-permute-done.4.refs_6_.refs_8_.refs_12_) | copy-start | bytes 786436
  27.2 5.2 %copy-start = (bf16[32,1,4,128,128]{4,3,2,1,0:T(8,128)(2,1)S(1)}, bf16[32,1,4,128,128]{4,3,2,1,0:T(8,128)(2,1)}, u32[]{:S(2)}) copy-start(bf16[32,1,4,128,128]{4,3,2,1,0:T(8,128)(2,1)} %param.11) | copy-start | bytes 12582916
  30.7 14.8 %collective-permute-start.13 = (bf16[1024,256]{1,0:T(8,128)(2,1)S(1)}, bf16[1024,256]{1,0:T(8,128)(2,1)S(1)}, u32[]{:S(2)}, u32[]{:S(2)}) collective-permute-start(bf16[1024,256]{1,0:T(8,128)(2,1)S(1)} %partial_messages.4.refs_1_), channel_id=1, source_target_pairs={{0,1},{1,0},{2,3},{3,2},{4,5},{5,4},{6,7},{7,6},{8,9},{9,8},{10,11... | collective-permute-start | bytes 1572872 | tf_op jit(solution)/shard_map/ppermute | solution.py:575
  32.4 2.9 %copy-start.2 = (bf16[512,256]{1,0:T(8,128)(2,1)S(1)}, bf16[512,256]{1,0:T(8,128)(2,1)}, u32[]{:S(2)}) copy-start(bf16[512,256]{1,0:T(8,128)(2,1)} %copy-done.1) | copy-start | bytes 786436
  38.4 17.5 %collective-permute-start.16 = (bf16[1024,256]{1,0:T(8,128)(2,1)S(1)}, bf16[1024,256]{1,0:T(8,128)(2,1)S(1)}, u32[]{:S(2)}, u32[]{:S(2)}) collective-permute-start(bf16[1024,256]{1,0:T(8,128)(2,1)S(1)} %partial_messages.5.refs_1_), channel_id=1, source_target_pairs={{0,1},{1,0},{2,3},{3,2},{4,5},{5,4},{6,7},{7,6},{8,9},{9,8},{10,11... | collective-permute-start | bytes 1572872 | tf_op jit(solution)/shard_map/ppermute | solution.py:575
  45.7 25.1 %copy-start.3 = (bf16[1024,256]{1,0:T(8,128)(2,1)S(1)}, bf16[1024,256]{1,0:T(8,128)(2,1)}, u32[]{:S(2)}) copy-start(bf16[1024,256]{1,0:T(8,128)(2,1)} %nodes.3) | copy-start | bytes 1572868
  45.7 25.1 %copy-start.4 = (bf16[1024,256]{1,0:T(8,128)(2,1)S(1)}, bf16[1024,256]{1,0:T(8,128)(2,1)}, u32[]{:S(2)}) copy-start(bf16[1024,256]{1,0:T(8,128)(2,1)} %cot.3) | copy-start | bytes 1572868
  45.7 25.1 %copy-start.5 = (bf16[512,256]{1,0:T(8,128)(2,1)S(1)}, bf16[512,256]{1,0:T(8,128)(2,1)}, u32[]{:S(2)}) copy-start(bf16[512,256]{1,0:T(8,128)(2,1)} %w_in.1) | copy-start | bytes 786436
  45.7 25.1 %copy-start.6 = (bf16[256,256]{1,0:T(8,128)(2,1)S(1)}, bf16[256,256]{1,0:T(8,128)(2,1)}, u32[]{:S(2)}) copy-start(bf16[256,256]{1,0:T(8,128)(2,1)} %refs_5_.1) | copy-start | bytes 393220
  45.7 25.1 %copy-start.7 = (f32[256]{0:T(256)S(1)}, f32[256]{0:T(256)}, u32[]{:S(2)}) copy-start(f32[256]{0:T(256)} %param.15) | copy-start | bytes 3076
  45.7 25.1 %copy-start.8 = (f32[256]{0:T(256)S(1)}, f32[256]{0:T(256)}, u32[]{:S(2)}) copy-start(f32[256]{0:T(256)} %param.17) | copy-start | bytes 3076
  45.8 25.1 %copy-start.9 = (f32[256]{0:T(256)S(1)}, f32[256]{0:T(256)}, u32[]{:S(2)}) copy-start(f32[256]{0:T(256)} %param.18) | copy-start | bytes 3076
  45.8 10.4 %collective-permute-start.14 = (bf16[1024,256]{1,0:T(8,128)(2,1)S(1)}, bf16[1024,256]{1,0:T(8,128)(2,1)S(1)}, u32[]{:S(2)}, u32[]{:S(2)}) collective-permute-start(bf16[1024,256]{1,0:T(8,128)(2,1)S(1)} %sum_terms.15), channel_id=1, source_target_pairs={{0,4},{1,2},{2,1},{3,7},{4,0},{5,6},{6,5},{7,3},{8,12},{9,10},{10,... | collective-permute-start | bytes 1572872 | tf_op jit(solution)/shard_map/ppermute | solution.py:588
  56.1 4.0 %collective-permute-start.17 = (bf16[1024,256]{1,0:T(8,128)(2,1)S(1)}, bf16[1024,256]{1,0:T(8,128)(2,1)S(1)}, u32[]{:S(2)}, u32[]{:S(2)}) collective-permute-start(bf16[1024,256]{1,0:T(8,128)(2,1)S(1)} %sum_terms.17), channel_id=1, source_target_pairs={{0,4},{1,2},{2,1},{3,7},{4,0},{5,6},{6,5},{7,3},{8,12},{9,10},{10,... | collective-permute-start | bytes 1572872 | tf_op jit(solution)/shard_map/ppermute | solution.py:588
  56.5 14.4 %collective-permute-start.15 = (bf16[1024,256]{1,0:T(8,128)(2,1)S(1)}, bf16[1024,256]{1,0:T(8,128)(2,1)S(1)}, u32[]{:S(2)}, u32[]{:S(2)}) collective-permute-start(bf16[1024,256]{1,0:T(8,128)(2,1)S(1)} %sum_terms.16), channel_id=1, source_target_pairs={{0,1},{1,0},{2,3},{3,2},{4,5},{5,4},{6,7},{7,6},{8,9},{9,8},{10,11... | collective-permute-start | bytes 1572872 | tf_op jit(solution)/shard_map/ppermute | solution.py:575
  74.1 11.8 %collective-permute-start.18 = (bf16[1024,256]{1,0:T(8,128)(2,1)S(1)}, bf16[1024,256]{1,0:T(8,128)(2,1)S(1)}, u32[]{:S(2)}, u32[]{:S(2)}) collective-permute-start(bf16[1024,256]{1,0:T(8,128)(2,1)S(1)} %get-tuple-element.36.refs_0_), channel_id=1, source_target_pairs={{0,1},{1,0},{2,3},{3,2},{4,5},{5,4},{6,7},{7,6},{8,9},{9,8},{10,11... | collective-permute-start | bytes 1572872 | tf_op jit(solution)/shard_map/ppermute | solution.py:575
  75.8 10.1 %collective-permute-start.19 = (bf16[1024,256]{1,0:T(8,128)(2,1)S(1)}, bf16[1024,256]{1,0:T(8,128)(2,1)S(1)}, u32[]{:S(2)}, u32[]{:S(2)}) collective-permute-start(bf16[1024,256]{1,0:T(8,128)(2,1)S(1)} %get-tuple-element.36.refs_0_), channel_id=1, source_target_pairs={{0,4},{1,2},{2,1},{3,7},{4,0},{5,6},{6,5},{7,3},{8,12},{9,10},{10,... | collective-permute-start | bytes 1572872 | tf_op jit(solution)/shard_map/ppermute | solution.py:588
  85.9 6.2 %collective-permute-start.21 = (bf16[1024,256]{1,0:T(8,128)(2,1)S(1)}, bf16[1024,256]{1,0:T(8,128)(2,1)S(1)}, u32[]{:S(2)}, u32[]{:S(2)}) collective-permute-start(bf16[1024,256]{1,0:T(8,128)(2,1)S(1)} %collective-permute-done.18.refs_0_.refs_1_), channel_id=1, source_target_pairs={{0,4},{1,2},{2,1},{3,7},{4,0},{5,6},{6,5},{7,3},{8,12},{9,10},{10,... | collective-permute-start | bytes 1572872 | tf_op jit(solution)/shard_map/ppermute | solution.py:588
  87.5 13.7 %collective-permute-start.23 = (f32[448,256]{1,0:T(8,128)S(1)}, f32[448,256]{1,0:T(8,128)S(1)}, u32[]{:S(2)}, u32[]{:S(2)}) collective-permute-start(f32[448,256]{1,0:T(8,128)S(1)} %get-tuple-element.39), channel_id=1, source_target_pairs={{0,4},{4,0},{8,12},{12,8},{16,20},{20,16},{24,28},{28,24},{1,5},{5... | collective-permute-start | bytes 1376264 | tf_op jit(solution)/shard_map/ppermute | solution.py:571
  88.0 16.9 %collective-permute-start.20 = (bf16[1024,256]{1,0:T(8,128)(2,1)S(1)}, bf16[1024,256]{1,0:T(8,128)(2,1)S(1)}, u32[]{:S(2)}, u32[]{:S(2)}) collective-permute-start(bf16[1024,256]{1,0:T(8,128)(2,1)S(1)} %collective-permute-done.19.refs_1_.refs_2_), channel_id=1, source_target_pairs={{0,1},{1,0},{2,3},{3,2},{4,5},{5,4},{6,7},{7,6},{8,9},{9,8},{10,11... | collective-permute-start | bytes 1572872 | tf_op jit(solution)/shard_map/ppermute | solution.py:575
  92.1 23.7 %collective-permute-start.22 = (bf16[1024,256]{1,0:T(8,128)(2,1)S(1)}, bf16[1024,256]{1,0:T(8,128)(2,1)S(1)}, u32[]{:S(2)}, u32[]{:S(2)}) collective-permute-start(bf16[1024,256]{1,0:T(8,128)(2,1)S(1)} %collective-permute-done.21.refs_18_.refs_4_), channel_id=1, source_target_pairs={{0,1},{1,0},{2,3},{3,2},{4,5},{5,4},{6,7},{7,6},{8,9},{9,8},{10,11... | collective-permute-start | bytes 1572872 | tf_op jit(solution)/shard_map/ppermute | solution.py:575
  101.2 9.5 %collective-permute-start.24 = (f32[112,256]{1,0:T(8,128)S(1)}, f32[112,256]{1,0:T(8,128)S(1)}, u32[]{:S(2)}, u32[]{:S(2)}) collective-permute-start(f32[112,256]{1,0:T(8,128)S(1)} %sum_terms.19), channel_id=1, source_target_pairs={{0,16},{4,20},{8,24},{12,28},{16,0},{20,4},{24,8},{28,12},{1,17},{... | collective-permute-start | bytes 344072 | tf_op jit(solution)/shard_map/ppermute | solution.py:571
  102.8 7.9 %collective-permute-start.25 = (f32[112,256]{1,0:T(8,128)S(1)}, f32[112,256]{1,0:T(8,128)S(1)}, u32[]{:S(2)}, u32[]{:S(2)}) collective-permute-start(f32[112,256]{1,0:T(8,128)S(1)} %sum_terms.20), channel_id=1, source_target_pairs={{0,8},{4,12},{8,0},{12,4},{16,24},{20,28},{24,16},{28,20},{1,9},{5... | collective-permute-start | bytes 344072 | tf_op jit(solution)/shard_map/ppermute | solution.py:571
  104.4 6.3 %collective-permute-start.26 = (f32[112,256]{1,0:T(8,128)S(1)}, f32[112,256]{1,0:T(8,128)S(1)}, u32[]{:S(2)}, u32[]{:S(2)}) collective-permute-start(f32[112,256]{1,0:T(8,128)S(1)} %sum_terms.21), channel_id=1, source_target_pairs={{0,24},{4,28},{8,16},{12,20},{16,8},{20,12},{24,0},{28,4},{1,25},{... | collective-permute-start | bytes 344072 | tf_op jit(solution)/shard_map/ppermute | solution.py:571
  122.6 2.7 %collective-permute-start.28 = (bf16[2048,256]{1,0:T(8,128)(2,1)S(1)}, bf16[2048,256]{1,0:T(8,128)(2,1)S(1)}, u32[]{:S(2)}, u32[]{:S(2)}) collective-permute-start(bf16[2048,256]{1,0:T(8,128)(2,1)S(1)} %get-tuple-element.43), channel_id=1, source_target_pairs={{0,4},{4,0},{8,12},{12,8},{16,20},{20,16},{24,28},{28,24},{1,5},{5... | collective-permute-start | bytes 3145736 | tf_op jit(solution)/shard_map/ppermute | solution.py:571
  122.6 4.3 %collective-permute-start.27 = (bf16[2048,256]{1,0:T(8,128)(2,1)S(1)}, bf16[2048,256]{1,0:T(8,128)(2,1)S(1)}, u32[]{:S(2)}, u32[]{:S(2)}) collective-permute-start(bf16[2048,256]{1,0:T(8,128)(2,1)S(1)} %get-tuple-element.42), channel_id=1, source_target_pairs={{0,4},{4,0},{8,12},{12,8},{16,20},{20,16},{24,28},{28,24},{1,5},{5... | collective-permute-start | bytes 3145736 | tf_op jit(solution)/shard_map/ppermute | solution.py:571
  125.5 17.1 %collective-permute-start.30 = (bf16[1024,256]{1,0:T(8,128)(2,1)S(1)}, bf16[1024,256]{1,0:T(8,128)(2,1)S(1)}, u32[]{:S(2)}, u32[]{:S(2)}) collective-permute-start(bf16[1024,256]{1,0:T(8,128)(2,1)S(1)} %sum_terms.24.refs_23_.refs_4_), channel_id=1, source_target_pairs={{0,16},{4,20},{8,24},{12,28},{16,0},{20,4},{24,8},{28,12},{1,17},{... | collective-permute-start | bytes 1572872 | tf_op jit(solution)/shard_map/ppermute | solution.py:571
  126.2 17.7 %collective-permute-start.29 = (bf16[1024,256]{1,0:T(8,128)(2,1)S(1)}, bf16[1024,256]{1,0:T(8,128)(2,1)S(1)}, u32[]{:S(2)}, u32[]{:S(2)}) collective-permute-start(bf16[1024,256]{1,0:T(8,128)(2,1)S(1)} %sum_terms.23.refs_22_.refs_3_), channel_id=1, source_target_pairs={{0,8},{4,12},{8,0},{12,4},{16,24},{20,28},{24,16},{28,20},{1,9},{5... | collective-permute-start | bytes 1572872 | tf_op jit(solution)/shard_map/ppermute | solution.py:571
  127.0 11.9 %collective-permute-start.33 = (bf16[112,256]{1,0:T(8,128)(2,1)S(1)}, bf16[112,256]{1,0:T(8,128)(2,1)S(1)}, u32[]{:S(2)}, u32[]{:S(2)}) collective-permute-start(bf16[112,256]{1,0:T(8,128)(2,1)S(1)} %sum_terms.28.refs_1_), channel_id=1, source_target_pairs={{0,1},{1,2},{2,3},{3,0},{4,5},{5,6},{6,7},{7,4},{8,9},{9,10},{10,1... | collective-permute-start | bytes 172040 | tf_op jit(solution)/shard_map/ppermute | solution.py:579
  128.9 10.0 %collective-permute-start.34 = (bf16[112,256]{1,0:T(8,128)(2,1)S(1)}, bf16[112,256]{1,0:T(8,128)(2,1)S(1)}, u32[]{:S(2)}, u32[]{:S(2)}) collective-permute-start(bf16[112,256]{1,0:T(8,128)(2,1)S(1)} %sum_terms.28.refs_1_), channel_id=1, source_target_pairs={{0,2},{1,3},{2,0},{3,1},{4,6},{5,7},{6,4},{7,5},{8,10},{9,11},{10,... | collective-permute-start | bytes 172040 | tf_op jit(solution)/shard_map/ppermute | solution.py:579
  130.8 8.1 %collective-permute-start.35 = (bf16[112,256]{1,0:T(8,128)(2,1)S(1)}, bf16[112,256]{1,0:T(8,128)(2,1)S(1)}, u32[]{:S(2)}, u32[]{:S(2)}) collective-permute-start(bf16[112,256]{1,0:T(8,128)(2,1)S(1)} %sum_terms.28.refs_1_), channel_id=1, source_target_pairs={{0,3},{1,0},{2,1},{3,2},{4,7},{5,4},{6,5},{7,6},{8,11},{9,8},{10,9... | collective-permute-start | bytes 172040 | tf_op jit(solution)/shard_map/ppermute | solution.py:579
  139.0 5.8 %collective-permute-start.38 = (bf16[112,256]{1,0:T(8,128)(2,1)S(1)}, bf16[112,256]{1,0:T(8,128)(2,1)S(1)}, u32[]{:S(2)}, u32[]{:S(2)}) collective-permute-start(bf16[112,256]{1,0:T(8,128)(2,1)S(1)} %sum_terms.29), channel_id=1, source_target_pairs={{0,24},{4,28},{8,16},{12,20},{16,8},{20,12},{24,0},{28,4},{1,25},{... | collective-permute-start | bytes 172040 | tf_op jit(solution)/shard_map/ppermute | solution.py:571
  139.6 5.1 %collective-permute-start.37 = (bf16[112,256]{1,0:T(8,128)(2,1)S(1)}, bf16[112,256]{1,0:T(8,128)(2,1)S(1)}, u32[]{:S(2)}, u32[]{:S(2)}) collective-permute-start(bf16[112,256]{1,0:T(8,128)(2,1)S(1)} %sum_terms.29), channel_id=1, source_target_pairs={{0,16},{4,20},{8,24},{12,28},{16,0},{20,4},{24,8},{28,12},{1,17},{... | collective-permute-start | bytes 172040 | tf_op jit(solution)/shard_map/ppermute | solution.py:571
  141.7 4.9 %collective-permute-start.36 = (bf16[112,256]{1,0:T(8,128)(2,1)S(1)}, bf16[112,256]{1,0:T(8,128)(2,1)S(1)}, u32[]{:S(2)}, u32[]{:S(2)}) collective-permute-start(bf16[112,256]{1,0:T(8,128)(2,1)S(1)} %sum_terms.29), channel_id=1, source_target_pairs={{0,8},{4,12},{8,0},{12,4},{16,24},{20,28},{24,16},{28,20},{1,9},{5... | collective-permute-start | bytes 172040 | tf_op jit(solution)/shard_map/ppermute | solution.py:571
  142.7 7.4 %collective-permute-start.31 = (bf16[512,256]{1,0:T(8,128)(2,1)S(1)}, bf16[512,256]{1,0:T(8,128)(2,1)S(1)}, u32[]{:S(2)}, u32[]{:S(2)}) collective-permute-start(bf16[512,256]{1,0:T(8,128)(2,1)S(1)} %sum_terms.25), channel_id=1, source_target_pairs={{0,8},{4,12},{8,0},{12,4},{16,24},{20,28},{24,16},{28,20},{1,9},{5... | collective-permute-start | bytes 786440 | tf_op jit(solution)/shard_map/ppermute | solution.py:571
  144.0 6.4 %collective-permute-start.32 = (bf16[512,256]{1,0:T(8,128)(2,1)S(1)}, bf16[512,256]{1,0:T(8,128)(2,1)S(1)}, u32[]{:S(2)}, u32[]{:S(2)}) collective-permute-start(bf16[512,256]{1,0:T(8,128)(2,1)S(1)} %sum_terms.26), channel_id=1, source_target_pairs={{0,16},{4,20},{8,24},{12,28},{16,0},{20,4},{24,8},{28,12},{1,17},{... | collective-permute-start | bytes 786440 | tf_op jit(solution)/shard_map/ppermute | solution.py:571
  146.5 1.6 %collective-permute-start.39 = (bf16[448,256]{1,0:T(8,128)(2,1)S(1)}, bf16[448,256]{1,0:T(8,128)(2,1)S(1)}, u32[]{:S(2)}, u32[]{:S(2)}) collective-permute-start(bf16[448,256]{1,0:T(8,128)(2,1)S(1)} %pad_maximum_fusion.even), channel_id=1, source_target_pairs={{0,4},{4,0},{8,12},{12,8},{16,20},{20,16},{24,28},{28,24},{1,5},{5... | collective-permute-start | bytes 688136 | tf_op jit(solution)/shard_map/ppermute | solution.py:571

commit v14 on v13

--- a/solution.py
+++ b/solution.py
@@ -20,6 +20,7 @@
 
 
 LIVE_STEP = 4
+TILE_PARTS = 4
 GRAD_PLAN = ((3, 0, None), (2, 1, None), (1, 2, "inner"), (1, 3, "outer"), (0, 4, "inner"), (0, 5, "outer"))
 SWAP_ORDER = (0, 4, 2, 6, 1, 5, 3, 7)
 
@@ -342,19 +343,19 @@
             pl.when(condition)(getattr(copy, verb))
 
 
-def for_live(found, entry):
+def for_live(first, last, entry):
     def several(i, carry):
         for index in range(LIVE_STEP):
-            entry(i * LIVE_STEP + index)
+            entry(first + i * LIVE_STEP + index)
         return carry
 
     def one(i, carry):
         entry(i)
         return carry
 
-    full = found // LIVE_STEP
+    full = jnp.maximum(last - first, 0) // LIVE_STEP
     lax.fori_loop(0, full, several, 0)
-    lax.fori_loop(full * LIVE_STEP, found, one, 0)
+    lax.fori_loop(first + full * LIVE_STEP, last, one, 0)
 
 
 def turn_kernel(slots, cols, tiles, out, tiles_v, live, sem):
@@ -372,10 +373,9 @@
     copy.wait()
 
     def entry(place):
-        tile_index = live[place]
-        out[tile_index] = tiles_v[tile_index].T
-
-    for_live(found, entry)
+        out[place] = tiles_v[live[place]].T
+
+    for_live(0, found, entry)
 
 
 def turn_call(cols, tiles):
@@ -401,37 +401,56 @@
     grads, tiles = refs[:n_grads], refs[n_grads]
     refs = refs[n_grads + 1 + n_after :]
     outs = refs[: len(out_pieces)]
-    grad_v, tiles_v, acc, live, source, sem, tile_sem = refs[len(out_pieces) :]
+    grad_v, tiles_v, acc, stage, live, source, sem, tile_sem, out_sem = refs[len(out_pieces) :]
     n_tiles, block = tiles.shape[:2]
     here = Place(here, paired, rows // block)
     jobs = grad_jobs(rows, grads, grad_v, sem, here)
     run_jobs(jobs, "start")
-    tile_copy = pltpu.make_async_copy(tiles, tiles_v, tile_sem.at[0])
-    tile_copy.start()
-    acc[...] = jnp.zeros_like(acc)
+    part = n_tiles // TILE_PARTS
+    tile_copies = [
+        pltpu.make_async_copy(
+            tiles.at[pl.ds(index * part, part)], tiles_v.at[pl.ds(index * part, part)], tile_sem.at[index]
+        )
+        for index in range(TILE_PARTS)
+    ]
+    tile_copies[0].start()
 
     def collect(row, found):
         count = cols[slots, row]
         for slot in range(slots):
-            live[found] = row * slots + slot
+            live[found] = row
             source[found] = here.source(cols[slot, row])
             found = found + (slot < count).astype(jnp.int32)
         return found
 
     found = lax.fori_loop(0, n_tiles // slots, collect, jnp.int32(0))
+    for index in range(1, TILE_PARTS):
+        pl.when(index * part < found)(tile_copies[index].start)
+    acc[...] = jnp.zeros_like(acc)
     run_jobs(jobs, "wait")
-    tile_copy.wait()
 
     def entry(place):
-        tile_index = live[place]
-        part = mm(tiles_v[tile_index], grad_v[block_at(tile_index // slots, block)])
-        acc[block_at(source[place], block)] += part
-
-    for_live(found, entry)
+        term = mm(tiles_v[place], grad_v[block_at(live[place], block)])
+        acc[block_at(source[place], block)] += term
+
+    tile_copies[0].wait()
+    for index in range(TILE_PARTS):
+        if index:
+            pl.when(index * part < found)(tile_copies[index].wait)
+        for_live(index * part, jnp.minimum(found, (index + 1) * part), entry)
     piece = acc.shape[0] // sum(len(members) for members in out_pieces)
+    copies = []
     for out, members in zip(outs, out_pieces):
         for index, member in enumerate(members):
-            out[pl.ds(index * piece, piece)] = acc[pl.ds(member * piece, piece)].astype(BF16)
+            where = pl.ds(member * piece, piece)
+            stage[where] = acc[where].astype(BF16)
+            copy = pltpu.make_async_copy(
+                stage.at[where], out.at[pl.ds(index * piece, piece)], out_sem.at[len(copies)]
+            )
+            copy.start()
+            copies.append(copy)
+    for copy in copies:
+        copy.wait()
 
 
 def back_call(paired, here, cols, grads, tiles, total, gathered, out_pieces, after=()):
@@ -444,15 +463,17 @@
         functools.partial(back_kernel, rows, slots, len(grads), len(after), out_pieces, paired),
         out_shape=[jax.ShapeDtypeStruct((len(m) * piece, width), BF16) for m in out_pieces],
         in_specs=[SMEM] * 2 + [ANY] * len(grads) + [HBM] + [ANY] * len(after),
-        out_specs=[VMEM] * len(out_pieces),
+        out_specs=[ANY] * len(out_pieces),
         scratch_shapes=[
             pltpu.VMEM((total, width), BF16),
             pltpu.VMEM((n_tiles, block, block), BF16),
             pltpu.VMEM((gathered, width), F32),
+            pltpu.VMEM((gathered, width), BF16),
             pltpu.SMEM((n_tiles + 8,), jnp.int32),
             pltpu.SMEM((n_tiles + 8,), jnp.int32),
             pltpu.SemaphoreType.DMA((len(grads),)),
-            pltpu.SemaphoreType.DMA((1,)),
+            pltpu.SemaphoreType.DMA((TILE_PARTS,)),
+            pltpu.SemaphoreType.DMA((sum(len(members) for members in out_pieces),)),
         ],
         compiler_params=params(28 if gathered <= 8192 else 56),
         cost_estimate=SMALL,
@@ -517,7 +538,7 @@
         node = nodes_v[block_at(source[place], block)]
         tiles_v[tile_index] = (mm(grad, node, NT) * scale).astype(BF16)
 
-    for_live(found, entry)
+    for_live(0, found, entry)
     size = blocks * slots
     copies = []
     for index, group in enumerate(groups):
@@ -630,7 +651,7 @@
 def sum_call(here, rows, terms, gated=(), split=(), dtype=BF16, after=()):
     both = [*terms, *gated]
     width = both[0][0].shape[1]
-    step = min(rows, 256)
+    step = min(rows, 512)
     steps = rows // step
     half = steps // 2
 
@@ -657,7 +678,7 @@
         + [spec_of(piece) for pair in split for spec_of, (_, piece) in zip((early, late), pair)]
         + [ANY] * len(after),
         out_specs=pl.BlockSpec((step, width), lambda i: (i, 0)),
-        compiler_params=params(8),
+        compiler_params=params(16),
         cost_estimate=SMALL,
         name="sum_terms",
     )(here, *(array for array, _ in both), *(array for pair in split for array, _ in pair), *after)

time: 153 us -> 152 us (level)
  Pallas kernels: 39.7 us -> 38 us
  transfers between devices with their start and end apart: 40 -> 40, of which waited for: 17 -> 18; matrix products, arithmetic and copies ran while one was open for 1% -> 1% of each run, Pallas kernels for 16% -> 16%
where the time goes in v14:
time: 152 us
  waiting for transfers between devices  64.4 us (42%)
  starting transfers between devices  46.4 us (31%)
  Pallas kernels  38 us (25%)
    ppermute x6, waiting for transfers between devices, outer_swap(): return lax.ppermute(value, 'col', [(0, 1), (1, 0), (2, 3), (3, 2)])  40.1 us
    ppermute x27, waiting for transfers between devices, swap(): return lax.ppermute(value, 'row', [(i, i ^ bit) for i in range(8)])  24.3 us
    ppermute x6, starting transfers between devices, outer_swap(): return lax.ppermute(value, 'col', [(0, 1), (1, 0), (2, 3), (3, 2)])  20.2 us
    ppermute x27, starting transfers between devices, swap(): return lax.ppermute(value, 'row', [(i, i ^ bit) for i in range(8)])  19.8 us
    pallas_call x2, Pallas kernels, tile_grad_call(): pl.pallas_call(functools.partial(tile_grad_kernel, rows, slots, len(grads...  10.4 us
    pallas_call x3, Pallas kernels, forward_call(): pl.pallas_call(functools.partial(forward_kernel, outputs, len(pieces), pa...  10.4 us
    pallas_call x1, Pallas kernels, back_call(): pl.pallas_call(functools.partial(back_kernel, rows, slots, len(grads), le...  6.5 us
    ppermute x3, starting transfers between devices, turn(): return lax.ppermute(value, 'col', [(i, (i + by) % 4) for i in range(4)])  6.15 us
  transfers between devices with their start and end apart: 40, of which 18 were waited for; matrix products, arithmetic and copies ran while one was open for 1% of the time, Pallas kernels for 16%

profile of v14, /device:TPU:0, one launch (start us, length us, event | category | flops | bytes accessed | tf_op | source)
XLA Modules:
  0.0 151.6 jit_solution(3839842782679131437)
XLA Ops:
  0.6 0.5 collective-permute-start
  1.1 1.1 fusion
  2.2 2.6 %collective-permute-start.1 = (bf16[512,256]{1,0:T(8,128)(2,1)S(1)}, bf16[512,256]{1,0:T(8,128)(2,1)S(1)}, u32[]{:S(2)}, u32[]{:S(2)}) collective-permute-start(bf16[512,256]{1,0:T(8,128)(2,1)S(1)} %get-tuple-element.57.refs_0_.refs_2_.refs_6_), channel_id=1, source_target_pairs={{0,8},{4,12},{8,0},{12,4},{16,24},{20,28},{24,16},{28,20},{1,9},{5... | collective-permute-start | bytes 786440 | tf_op jit(solution)/shard_map/ppermute | solution.py:592
  4.8 1.5 %collective-permute-start.5 = (bf16[512,256]{1,0:T(8,128)(2,1)S(1)}, bf16[512,256]{1,0:T(8,128)(2,1)S(1)}, u32[]{:S(2)}, u32[]{:S(2)}) collective-permute-start(bf16[512,256]{1,0:T(8,128)(2,1)S(1)} %get-tuple-element.57.refs_0_.refs_2_.refs_6_), channel_id=1, source_target_pairs={{0,16},{4,20},{8,24},{12,28},{16,0},{20,4},{24,8},{28,12},{1,17},{... | collective-permute-start | bytes 786440 | tf_op jit(solution)/shard_map/ppermute | solution.py:592
  6.3 0.5 collective-permute-start.2
  6.9 5.1 %collective-permute-done.1.refs_3_.refs_5_.refs_9_ = bf16[512,256]{1,0:T(8,128)(2,1)S(1)} collective-permute-done((bf16[512,256]{1,0:T(8,128)(2,1)S(1)}, bf16[512,256]{1,0:T(8,128)(2,1)S(1)}, u32[]{:S(2)}, u32[]{:S(2)}) %collective-permute-start.1) | collective-permute-done | bytes 262176 | tf_op jit(solution)/shard_map/ppermute | solution.py:592
  11.9 2.0 %collective-permute-done.5.refs_7_.refs_9_.refs_13_ = bf16[512,256]{1,0:T(8,128)(2,1)S(1)} collective-permute-done((bf16[512,256]{1,0:T(8,128)(2,1)S(1)}, bf16[512,256]{1,0:T(8,128)(2,1)S(1)}, u32[]{:S(2)}, u32[]{:S(2)}) %collective-permute-start.5) | collective-permute-done | bytes 262176 | tf_op jit(solution)/shard_map/ppermute | solution.py:592
  14.0 3.6 %collective-permute-done.2.refs_4_.refs_6_.refs_10_ = bf16[512,256]{1,0:T(8,128)(2,1)S(1)} collective-permute-done((bf16[512,256]{1,0:T(8,128)(2,1)S(1)}, bf16[512,256]{1,0:T(8,128)(2,1)S(1)}, u32[]{:S(2)}, u32[]{:S(2)}) %collective-permute-start.2) | collective-permute-done | bytes 262176 | tf_op jit(solution)/shard_map/ppermute | solution.py:592
  17.6 2.0 %collective-permute-start.10 = (bf16[512,256]{1,0:T(8,128)(2,1)S(1)}, bf16[512,256]{1,0:T(8,128)(2,1)S(1)}, u32[]{:S(2)}, u32[]{:S(2)}) collective-permute-start(bf16[512,256]{1,0:T(8,128)(2,1)S(1)} %collective-permute-done.2.refs_4_.refs_6_.refs_10_), channel_id=1, source_target_pairs={{0,16},{4,20},{8,24},{12,28},{16,0},{20,4},{24,8},{28,12},{1,17},{... | collective-permute-start | bytes 786440 | tf_op jit(solution)/shard_map/ppermute | solution.py:592
  19.5 0.5 collective-permute-start.7
  20.1 2.9 %collective-permute-done.9.refs_11_.refs_13_.refs_17_ = bf16[512,256]{1,0:T(8,128)(2,1)S(1)} collective-permute-done((bf16[512,256]{1,0:T(8,128)(2,1)S(1)}, bf16[512,256]{1,0:T(8,128)(2,1)S(1)}, u32[]{:S(2)}, u32[]{:S(2)}) %collective-permute-start.9) | collective-permute-done | bytes 262176 | tf_op jit(solution)/shard_map/ppermute | solution.py:592
  23.0 2.5 %collective-permute-done.10.refs_12_.refs_14_.refs_18_ = bf16[512,256]{1,0:T(8,128)(2,1)S(1)} collective-permute-done((bf16[512,256]{1,0:T(8,128)(2,1)S(1)}, bf16[512,256]{1,0:T(8,128)(2,1)S(1)}, u32[]{:S(2)}, u32[]{:S(2)}) %collective-permute-start.10) | collective-permute-done | bytes 262176 | tf_op jit(solution)/shard_map/ppermute | solution.py:592
  25.5 0.7 pad_add_fusion.cols
  26.2 0.9 collective-permute-done.12.refs_14_.refs_16_.refs_20_
  27.2 3.5 %partial_messages.4.refs_1_ = bf16[1024,256]{1,0:T(8,128)(2,1)S(1)} custom-call(s32[1]{0:T(128)} %bitcast.here.refs_0_, s32[5,32]{1,0:T(8,128)S(1)} %pad_add_fusion.cols, bf16[512,256]{1,0:T(8,128)(2,1)S(1)} %get-tuple-element.57.refs_0_.refs_2_.refs_6_, bf16[512,256]{1,0:T(8,128)(2,1)S(1)} %get-tuple-element.56.refs_1_.refs_3_.refs_7_, ...), custom_call_target="tpu_custom_call" | custom-call | flops 1048576 | bytes 65536 | tf_op jit(solution)/shard_map/partial_messages/pallas_call | solution.py:133
  30.7 1.7 %collective-permute-start.13 = (bf16[1024,256]{1,0:T(8,128)(2,1)S(1)}, bf16[1024,256]{1,0:T(8,128)(2,1)S(1)}, u32[]{:S(2)}, u32[]{:S(2)}) collective-permute-start(bf16[1024,256]{1,0:T(8,128)(2,1)S(1)} %partial_messages.4.refs_1_), channel_id=1, source_target_pairs={{0,1},{1,0},{2,3},{3,2},{4,5},{5,4},{6,7},{7,6},{8,9},{9,8},{10,11... | collective-permute-start | bytes 1572872 | tf_op jit(solution)/shard_map/ppermute | solution.py:596
  32.4 2.6 %turned_tiles.1.refs_3_.refs_6_ = bf16[128,128,128]{2,1,0:T(8,128)(2,1)S(1)} custom-call(s32[5,32]{1,0:T(8,128)S(1)} %pad_add_fusion.cols, bf16[128,128,128]{2,1,0:T(8,128)(2,1)S(1)} %bitcast.16), custom_call_target="tpu_custom_call" | custom-call | flops 1048576 | bytes 65536 | tf_op jit(solution)/shard_map/turned_tiles/pallas_call | solution.py:384
  35.0 3.1 %partial_messages.5.refs_1_ = bf16[1024,256]{1,0:T(8,128)(2,1)S(1)} custom-call(s32[1]{0:T(128)} %bitcast.here.refs_0_, s32[5,32]{1,0:T(8,128)S(1)} %pad_add_fusion.cols, bf16[512,256]{1,0:T(8,128)(2,1)S(1)} %get-tuple-element.57.refs_0_.refs_2_.refs_6_, bf16[512,256]{1,0:T(8,128)(2,1)S(1)} %get-tuple-element.56.refs_1_.refs_3_.refs_7_, ...), custom_call_target="tpu_custom_call" | custom-call | flops 1048576 | bytes 65536 | tf_op jit(solution)/shard_map/partial_messages/pallas_call | solution.py:133
  38.1 0.1 collective-permute-start.16
  38.2 7.3 %collective-permute-done.13.refs_2_ = bf16[1024,256]{1,0:T(8,128)(2,1)S(1)} collective-permute-done((bf16[1024,256]{1,0:T(8,128)(2,1)S(1)}, bf16[1024,256]{1,0:T(8,128)(2,1)S(1)}, u32[]{:S(2)}, u32[]{:S(2)}) %collective-permute-start.13) | collective-permute-done | bytes 524320 | tf_op jit(solution)/shard_map/ppermute | solution.py:596
  45.5 0.1 sum_terms.15
  45.7 0.1 collective-permute-start.14
  45.8 3.7 %partial_messages.3 = (bf16[1024,256]{1,0:T(8,128)(2,1)S(1)}, bf16[1024,256]{1,0:T(8,128)(2,1)S(1)}) custom-call(s32[1]{0:T(128)} %bitcast.here.refs_0_, s32[5,32]{1,0:T(8,128)S(1)} %pad_add_fusion.cols, bf16[512,256]{1,0:T(8,128)(2,1)S(1)} %get-tuple-element.57.refs_0_.refs_2_.refs_6_, bf16[512,256]{1,0:T(8,128)(2,1)S(1)} %get-tuple-element.56.refs_1_.refs_3_.refs_7_, ...), custom_call_target="tpu_custom_call" | custom-call | flops 1048576 | bytes 65536 | tf_op jit(solution)/shard_map/partial_messages/pallas_call | solution.py:133
  49.6 6.4 %collective-permute-done.16.refs_2_ = bf16[1024,256]{1,0:T(8,128)(2,1)S(1)} collective-permute-done((bf16[1024,256]{1,0:T(8,128)(2,1)S(1)}, bf16[1024,256]{1,0:T(8,128)(2,1)S(1)}, u32[]{:S(2)}, u32[]{:S(2)}) %collective-permute-start.16) | collective-permute-done | bytes 524320 | tf_op jit(solution)/shard_map/ppermute | solution.py:596
  55.9 0.1 sum_terms.17
  56.2 0.2 sum_terms.16
  56.4 3.6 %collective-permute-start.15 = (bf16[1024,256]{1,0:T(8,128)(2,1)S(1)}, bf16[1024,256]{1,0:T(8,128)(2,1)S(1)}, u32[]{:S(2)}, u32[]{:S(2)}) collective-permute-start(bf16[1024,256]{1,0:T(8,128)(2,1)S(1)} %sum_terms.16), channel_id=1, source_target_pairs={{0,1},{1,0},{2,3},{3,2},{4,5},{5,4},{6,7},{7,6},{8,9},{9,8},{10,11... | collective-permute-start | bytes 1572872 | tf_op jit(solution)/shard_map/ppermute | solution.py:596
  60.0 10.7 %collective-permute-done.15.refs_1_ = bf16[1024,256]{1,0:T(8,128)(2,1)S(1)} collective-permute-done((bf16[1024,256]{1,0:T(8,128)(2,1)S(1)}, bf16[1024,256]{1,0:T(8,128)(2,1)S(1)}, u32[]{:S(2)}, u32[]{:S(2)}) %collective-permute-start.15) | collective-permute-done | bytes 524320 | tf_op jit(solution)/shard_map/ppermute | solution.py:596
  70.8 3.2 %mlp.1 = (bf16[1024,256]{1,0:T(8,128)(2,1)}, bf16[1024,256]{1,0:T(8,128)(2,1)S(1)}, bf16[1024,256]{1,0:T(8,128)(2,1)S(1)}, bf16[1024,256]{1,0:T(8,128)(2,1)S(1)}...) custom-call(s32[1]{0:T(128)} %bitcast.here.refs_0_, ...), custom_call_target="tpu_custom_call" | custom-call | flops 1048576 | bytes 65536 | tf_op jit(solution)/shard_map/mlp/pallas_call | solution.py:227
  74.0 1.7 %collective-permute-start.18 = (bf16[1024,256]{1,0:T(8,128)(2,1)S(1)}, bf16[1024,256]{1,0:T(8,128)(2,1)S(1)}, u32[]{:S(2)}, u32[]{:S(2)}) collective-permute-start(bf16[1024,256]{1,0:T(8,128)(2,1)S(1)} %get-tuple-element.36.refs_0_), channel_id=1, source_target_pairs={{0,1},{1,0},{2,3},{3,2},{4,5},{5,4},{6,7},{7,6},{8,9},{9,8},{10,11... | collective-permute-start | bytes 1572872 | tf_op jit(solution)/shard_map/ppermute | solution.py:596
  75.8 10.1 %collective-permute-done.18.refs_0_.refs_1_ = bf16[1024,256]{1,0:T(8,128)(2,1)S(1)} collective-permute-done((bf16[1024,256]{1,0:T(8,128)(2,1)S(1)}, bf16[1024,256]{1,0:T(8,128)(2,1)S(1)}, u32[]{:S(2)}, u32[]{:S(2)}) %collective-permute-start.18) | collective-permute-done | bytes 524320 | tf_op jit(solution)/shard_map/ppermute | solution.py:596
  85.9 1.5 %weight_grads.1 = (f32[448,256]{1,0:T(8,128)S(1)}, f32[448,256]{1,0:T(8,128)S(1)}, f32[1024,256]{1,0:T(8,128)S(1)}) custom-call(s32[1]{0:T(128)} %bitcast.here.refs_0_, bf16[1024,256]{1,0:T(8,128)(2,1)S(1)} %copy-done.3, bf16[1024,256]{1,0:T(8,128)(2,1)S(1)} %get-tuple-element.31.msg, bf16[1024,256]{1,0:T(8,128)(2,1)S(1)} %get-tuple-element.32.act, ...), custom_call_target="tpu_custom_call" | custom-call | flops 1048576 | bytes 65536 | tf_op jit(solution)/shard_map/weight_grads/pallas_call | solution.py:280
  87.4 0.6 collective-permute-start.23
  88.0 4.1 %collective-permute-start.20 = (bf16[1024,256]{1,0:T(8,128)(2,1)S(1)}, bf16[1024,256]{1,0:T(8,128)(2,1)S(1)}, u32[]{:S(2)}, u32[]{:S(2)}) collective-permute-start(bf16[1024,256]{1,0:T(8,128)(2,1)S(1)} %collective-permute-done.19.refs_1_.refs_2_), channel_id=1, source_target_pairs={{0,1},{1,0},{2,3},{3,2},{4,5},{5,4},{6,7},{7,6},{8,9},{9,8},{10,11... | collective-permute-start | bytes 1572872 | tf_op jit(solution)/shard_map/ppermute | solution.py:596
  92.0 9.1 %collective-permute-start.22 = (bf16[1024,256]{1,0:T(8,128)(2,1)S(1)}, bf16[1024,256]{1,0:T(8,128)(2,1)S(1)}, u32[]{:S(2)}, u32[]{:S(2)}) collective-permute-start(bf16[1024,256]{1,0:T(8,128)(2,1)S(1)} %collective-permute-done.21.refs_18_.refs_4_), channel_id=1, source_target_pairs={{0,1},{1,0},{2,3},{3,2},{4,5},{5,4},{6,7},{7,6},{8,9},{9,8},{10,11... | collective-permute-start | bytes 1572872 | tf_op jit(solution)/shard_map/ppermute | solution.py:596
  101.1 1.6 %collective-permute-start.24 = (f32[112,256]{1,0:T(8,128)S(1)}, f32[112,256]{1,0:T(8,128)S(1)}, u32[]{:S(2)}, u32[]{:S(2)}) collective-permute-start(f32[112,256]{1,0:T(8,128)S(1)} %sum_terms.19), channel_id=1, source_target_pairs={{0,16},{4,20},{8,24},{12,28},{16,0},{20,4},{24,8},{28,12},{1,17},{... | collective-permute-start | bytes 344072 | tf_op jit(solution)/shard_map/ppermute | solution.py:592
  102.7 1.6 %collective-permute-start.25 = (f32[112,256]{1,0:T(8,128)S(1)}, f32[112,256]{1,0:T(8,128)S(1)}, u32[]{:S(2)}, u32[]{:S(2)}) collective-permute-start(f32[112,256]{1,0:T(8,128)S(1)} %sum_terms.20), channel_id=1, source_target_pairs={{0,8},{4,12},{8,0},{12,4},{16,24},{20,28},{24,16},{28,20},{1,9},{5... | collective-permute-start | bytes 344072 | tf_op jit(solution)/shard_map/ppermute | solution.py:592
  104.3 0.5 collective-permute-start.26
  104.9 5.1 %tile_grads.2 = (bf16[128,128,128]{2,1,0:T(8,128)(2,1)}, f32[8,128]{1,0:T(8,128)S(1)}) custom-call(s32[1]{0:T(128)} %bitcast.here.refs_0_, s32[5,32]{1,0:T(8,128)S(1)} %pad_add_fusion.cols, bf16[1024,256]{1,0:T(8,128)(2,1)S(1)} %get-tuple-element.36.refs_0_, bf16[1024,256]{1,0:T(8,128)(2,1)S(1)} %collective-permute-done.18.refs_0_.refs_1_, ...), custom_call_target="tpu_custom_call" | custom-call | flops 1048576 | bytes 65536 | tf_op jit(solution)/shard_map/tile_grads/pallas_call | solution.py:564
  110.1 5.7 %collective-permute-done.22.refs_5_ = bf16[1024,256]{1,0:T(8,128)(2,1)S(1)} collective-permute-done((bf16[1024,256]{1,0:T(8,128)(2,1)S(1)}, bf16[1024,256]{1,0:T(8,128)(2,1)S(1)}, u32[]{:S(2)}, u32[]{:S(2)}) %collective-permute-start.22) | collective-permute-done | bytes 524320 | tf_op jit(solution)/shard_map/ppermute | solution.py:596
  115.8 6.5 %back_terms.1 = (bf16[2048,256]{1,0:T(8,128)(2,1)S(1)}, bf16[2048,256]{1,0:T(8,128)(2,1)S(1)}, bf16[4096,256]{1,0:T(8,128)(2,1)S(1)}) custom-call(s32[1]{0:T(128)} %bitcast.here.refs_0_, s32[5,32]{1,0:T(8,128)S(1)} %pad_add_fusion.cols, bf16[1024,256]{1,0:T(8,128)(2,1)S(1)} %get-tuple-element.36.refs_0_, ...), custom_call_target="tpu_custom_call" | custom-call | flops 1048576 | bytes 65536 | tf_op jit(solution)/shard_map/back_terms/pallas_call | solution.py:462
  122.4 0.5 collective-permute-start.27
  122.9 2.1 %collective-permute-done.28.refs_2_ = bf16[2048,256]{1,0:T(8,128)(2,1)S(1)} collective-permute-done((bf16[2048,256]{1,0:T(8,128)(2,1)S(1)}, bf16[2048,256]{1,0:T(8,128)(2,1)S(1)}, u32[]{:S(2)}, u32[]{:S(2)}) %collective-permute-start.28) | collective-permute-done | bytes 1048608 | tf_op jit(solution)/shard_map/ppermute | solution.py:592
  125.0 0.2 sum_terms.24.refs_23_.refs_4_
  125.2 2.3 %collective-permute-start.30 = (bf16[1024,256]{1,0:T(8,128)(2,1)S(1)}, bf16[1024,256]{1,0:T(8,128)(2,1)S(1)}, u32[]{:S(2)}, u32[]{:S(2)}) collective-permute-start(bf16[1024,256]{1,0:T(8,128)(2,1)S(1)} %sum_terms.24.refs_23_.refs_4_), channel_id=1, source_target_pairs={{0,16},{4,20},{8,24},{12,28},{16,0},{20,4},{24,8},{28,12},{1,17},{... | collective-permute-start | bytes 1572872 | tf_op jit(solution)/shard_map/ppermute | solution.py:592
  127.5 0.2 sum_terms.23.refs_22_.refs_3_
  127.8 2.1 %collective-permute-start.33 = (bf16[112,256]{1,0:T(8,128)(2,1)S(1)}, bf16[112,256]{1,0:T(8,128)(2,1)S(1)}, u32[]{:S(2)}, u32[]{:S(2)}) collective-permute-start(bf16[112,256]{1,0:T(8,128)(2,1)S(1)} %sum_terms.28.refs_1_), channel_id=1, source_target_pairs={{0,1},{1,2},{2,3},{3,0},{4,5},{5,6},{6,7},{7,4},{8,9},{9,10},{10,1... | collective-permute-start | bytes 172040 | tf_op jit(solution)/shard_map/ppermute | solution.py:600
  129.9 1.3 collective-permute-start.34
  131.1 2.8 %collective-permute-start.35 = (bf16[112,256]{1,0:T(8,128)(2,1)S(1)}, bf16[112,256]{1,0:T(8,128)(2,1)S(1)}, u32[]{:S(2)}, u32[]{:S(2)}) collective-permute-start(bf16[112,256]{1,0:T(8,128)(2,1)S(1)} %sum_terms.28.refs_1_), channel_id=1, source_target_pairs={{0,3},{1,0},{2,1},{3,2},{4,7},{5,4},{6,5},{7,6},{8,11},{9,8},{10,9... | collective-permute-start | bytes 172040 | tf_op jit(solution)/shard_map/ppermute | solution.py:600
  133.9 5.3 %tile_grads.3 = (bf16[128,128,128]{2,1,0:T(8,128)(2,1)}, f32[8,128]{1,0:T(8,128)S(1)}) custom-call(s32[1]{0:T(128)} %bitcast.here.refs_0_, s32[5,32]{1,0:T(8,128)S(1)} %pad_add_fusion.cols, bf16[1024,256]{1,0:T(8,128)(2,1)S(1)} %get-tuple-element.36.refs_0_, ...), custom_call_target="tpu_custom_call", output_to_operand_aliasing={{0}: (23, {})} | custom-call | flops 1048576 | bytes 65536 | tf_op jit(solution)/shard_map/tile_grads/pallas_call | solution.py:564
  139.3 0.1 collective-permute-start.38
  139.4 2.4 %collective-permute-start.37 = (bf16[112,256]{1,0:T(8,128)(2,1)S(1)}, bf16[112,256]{1,0:T(8,128)(2,1)S(1)}, u32[]{:S(2)}, u32[]{:S(2)}) collective-permute-start(bf16[112,256]{1,0:T(8,128)(2,1)S(1)} %sum_terms.29), channel_id=1, source_target_pairs={{0,16},{4,20},{8,24},{12,28},{16,0},{20,4},{24,8},{28,12},{1,17},{... | collective-permute-start | bytes 172040 | tf_op jit(solution)/shard_map/ppermute | solution.py:592
  141.7 1.1 collective-permute-start.36
  142.9 0.1 sum_terms.25
  143.0 1.0 collective-permute-start.31
  143.9 0.1 sum_terms.26
  144.0 0.2 collective-permute-start.32
  144.3 0.3 collective-permute-done.38
  144.5 2.1 %collective-permute-done.36 = bf16[112,256]{1,0:T(8,128)(2,1)S(1)} collective-permute-done((bf16[112,256]{1,0:T(8,128)(2,1)S(1)}, bf16[112,256]{1,0:T(8,128)(2,1)S(1)}, u32[]{:S(2)}, u32[]{:S(2)}) %collective-permute-start.36) | collective-permute-done | bytes 57376 | tf_op jit(solution)/shard_map/ppermute | solution.py:592
  146.7 1.5 collective-permute-done.39.odd
  148.2 1.0 weight_unpack.1
  149.1 1.1 collective-permute-done.31.refs_5_
  150.3 0.2 collective-permute-done.32.refs_6_
  150.5 1.2 sum_terms.27
  (64 shorter events, 0.8 us)
Async XLA Ops:
  0.6 18.9 %collective-permute-start = (bf16[1024,256]{1,0:T(8,128)(2,1)}, bf16[1024,256]{1,0:T(8,128)(2,1)S(1)}, u32[]{:S(2)}, u32[]{:S(2)}) collective-permute-start(bf16[1024,256]{1,0:T(8,128)(2,1)} %nodes.3), channel_id=1, source_target_pairs={{0,4},{4,0},{8,12},{12,8},{16,20},{20,16},{24,28},{28,24},{1,5},{5... | collective-permute-start | bytes 1572872 | tf_op jit(solution)/shard_map/ppermute | solution.py:592
  2.2 9.7 %collective-permute-start.1 = (bf16[512,256]{1,0:T(8,128)(2,1)S(1)}, bf16[512,256]{1,0:T(8,128)(2,1)S(1)}, u32[]{:S(2)}, u32[]{:S(2)}) collective-permute-start(bf16[512,256]{1,0:T(8,128)(2,1)S(1)} %get-tuple-element.57.refs_0_.refs_2_.refs_6_), channel_id=1, source_target_pairs={{0,8},{4,12},{8,0},{12,4},{16,24},{20,28},{24,16},{28,20},{1,9},{5... | collective-permute-start | bytes 786440 | tf_op jit(solution)/shard_map/ppermute | solution.py:592
  4.8 9.1 %collective-permute-start.5 = (bf16[512,256]{1,0:T(8,128)(2,1)S(1)}, bf16[512,256]{1,0:T(8,128)(2,1)S(1)}, u32[]{:S(2)}, u32[]{:S(2)}) collective-permute-start(bf16[512,256]{1,0:T(8,128)(2,1)S(1)} %get-tuple-element.57.refs_0_.refs_2_.refs_6_), channel_id=1, source_target_pairs={{0,16},{4,20},{8,24},{12,28},{16,0},{20,4},{24,8},{28,12},{1,17},{... | collective-permute-start | bytes 786440 | tf_op jit(solution)/shard_map/ppermute | solution.py:592
  6.3 11.3 %collective-permute-start.2 = (bf16[512,256]{1,0:T(8,128)(2,1)S(1)}, bf16[512,256]{1,0:T(8,128)(2,1)S(1)}, u32[]{:S(2)}, u32[]{:S(2)}) collective-permute-start(bf16[512,256]{1,0:T(8,128)(2,1)S(1)} %get-tuple-element.56.refs_1_.refs_3_.refs_7_), channel_id=1, source_target_pairs={{0,8},{4,12},{8,0},{12,4},{16,24},{20,28},{24,16},{28,20},{1,9},{5... | collective-permute-start | bytes 786440 | tf_op jit(solution)/shard_map/ppermute | solution.py:592
  6.8 12.7 %collective-permute-start.6 = (bf16[512,256]{1,0:T(8,128)(2,1)S(1)}, bf16[512,256]{1,0:T(8,128)(2,1)S(1)}, u32[]{:S(2)}, u32[]{:S(2)}) collective-permute-start(bf16[512,256]{1,0:T(8,128)(2,1)S(1)} %get-tuple-element.56.refs_1_.refs_3_.refs_7_), channel_id=1, source_target_pairs={{0,16},{4,20},{8,24},{12,28},{16,0},{20,4},{24,8},{28,12},{1,17},{... | collective-permute-start | bytes 786440 | tf_op jit(solution)/shard_map/ppermute | solution.py:592
  11.9 8.1 %collective-permute-start.3 = (bf16[512,256]{1,0:T(8,128)(2,1)S(1)}, bf16[512,256]{1,0:T(8,128)(2,1)S(1)}, u32[]{:S(2)}, u32[]{:S(2)}) collective-permute-start(bf16[512,256]{1,0:T(8,128)(2,1)S(1)} %collective-permute-done.1.refs_3_.refs_5_.refs_9_), channel_id=1, source_target_pairs={{0,4},{4,0},{8,12},{12,8},{16,20},{20,16},{24,28},{28,24},{1,5},{5... | collective-permute-start | bytes 786440 | tf_op jit(solution)/shard_map/ppermute | solution.py:592
  13.9 9.1 %collective-permute-start.9 = (bf16[512,256]{1,0:T(8,128)(2,1)S(1)}, bf16[512,256]{1,0:T(8,128)(2,1)S(1)}, u32[]{:S(2)}, u32[]{:S(2)}) collective-permute-start(bf16[512,256]{1,0:T(8,128)(2,1)S(1)} %collective-permute-done.5.refs_7_.refs_9_.refs_13_), channel_id=1, source_target_pairs={{0,8},{4,12},{8,0},{12,4},{16,24},{20,28},{24,16},{28,20},{1,9},{5... | collective-permute-start | bytes 786440 | tf_op jit(solution)/shard_map/ppermute | solution.py:592
  17.6 7.9 %collective-permute-start.10 = (bf16[512,256]{1,0:T(8,128)(2,1)S(1)}, bf16[512,256]{1,0:T(8,128)(2,1)S(1)}, u32[]{:S(2)}, u32[]{:S(2)}) collective-permute-start(bf16[512,256]{1,0:T(8,128)(2,1)S(1)} %collective-permute-done.2.refs_4_.refs_6_.refs_10_), channel_id=1, source_target_pairs={{0,16},{4,20},{8,24},{12,28},{16,0},{20,4},{24,8},{28,12},{1,17},{... | collective-permute-start | bytes 786440 | tf_op jit(solution)/shard_map/ppermute | solution.py:592
  19.5 6.7 %collective-permute-start.4 = (bf16[512,256]{1,0:T(8,128)(2,1)S(1)}, bf16[512,256]{1,0:T(8,128)(2,1)S(1)}, u32[]{:S(2)}, u32[]{:S(2)}) collective-permute-start(bf16[512,256]{1,0:T(8,128)(2,1)S(1)} %collective-permute-done.2.refs_4_.refs_6_.refs_10_), channel_id=1, source_target_pairs={{0,4},{4,0},{8,12},{12,8},{16,20},{20,16},{24,28},{28,24},{1,5},{5... | collective-permute-start | bytes 786440 | tf_op jit(solution)/shard_map/ppermute | solution.py:592
  19.5 6.7 %collective-permute-start.7 = (bf16[512,256]{1,0:T(8,128)(2,1)S(1)}, bf16[512,256]{1,0:T(8,128)(2,1)}, u32[]{:S(2)}, u32[]{:S(2)}) collective-permute-start(bf16[512,256]{1,0:T(8,128)(2,1)S(1)} %collective-permute-done.5.refs_7_.refs_9_.refs_13_), channel_id=1, source_target_pairs={{0,4},{4,0},{8,12},{12,8},{16,20},{20,16},{24,28},{28,24},{1,5},{5... | collective-permute-start | bytes 786440 | tf_op jit(solution)/shard_map/ppermute | solution.py:592
  20.1 6.2 %collective-permute-start.8 = (bf16[512,256]{1,0:T(8,128)(2,1)S(1)}, bf16[512,256]{1,0:T(8,128)(2,1)}, u32[]{:S(2)}, u32[]{:S(2)}) collective-permute-start(bf16[512,256]{1,0:T(8,128)(2,1)S(1)} %collective-permute-done.6.refs_8_.refs_10_.refs_14_), channel_id=1, source_target_pairs={{0,4},{4,0},{8,12},{12,8},{16,20},{20,16},{24,28},{28,24},{1,5},{5... | collective-permute-start | bytes 786440 | tf_op jit(solution)/shard_map/ppermute | solution.py:592
  23.0 3.3 %collective-permute-start.11 = (bf16[512,256]{1,0:T(8,128)(2,1)S(1)}, bf16[512,256]{1,0:T(8,128)(2,1)}, u32[]{:S(2)}, u32[]{:S(2)}) collective-permute-start(bf16[512,256]{1,0:T(8,128)(2,1)S(1)} %collective-permute-done.9.refs_11_.refs_13_.refs_17_), channel_id=1, source_target_pairs={{0,4},{4,0},{8,12},{12,8},{16,20},{20,16},{24,28},{28,24},{1,5},{5... | collective-permute-start | bytes 786440 | tf_op jit(solution)/shard_map/ppermute | solution.py:592
  25.5 1.7 %collective-permute-start.12 = (bf16[512,256]{1,0:T(8,128)(2,1)S(1)}, bf16[512,256]{1,0:T(8,128)(2,1)}, u32[]{:S(2)}, u32[]{:S(2)}) collective-permute-start(bf16[512,256]{1,0:T(8,128)(2,1)S(1)} %collective-permute-done.10.refs_12_.refs_14_.refs_18_), channel_id=1, source_target_pairs={{0,4},{4,0},{8,12},{12,8},{16,20},{20,16},{24,28},{28,24},{1,5},{5... | collective-permute-start | bytes 786440 | tf_op jit(solution)/shard_map/ppermute | solution.py:592
  26.2 4.5 %copy-start.1 = (bf16[512,256]{1,0:T(8,128)(2,1)}, bf16[512,256]{1,0:T(8,128)(2,1)S(1)}, u32[]{:S(2)}) copy-start(bf16[512,256]{1,0:T(8,128)(2,1)S(1)} %collective-permute-done.4.refs_6_.refs_8_.refs_12_) | copy-start | bytes 786436
  27.2 5.2 %copy-start = (bf16[32,1,4,128,128]{4,3,2,1,0:T(8,128)(2,1)S(1)}, bf16[32,1,4,128,128]{4,3,2,1,0:T(8,128)(2,1)}, u32[]{:S(2)}) copy-start(bf16[32,1,4,128,128]{4,3,2,1,0:T(8,128)(2,1)} %param.11) | copy-start | bytes 12582916
  30.7 14.8 %collective-permute-start.13 = (bf16[1024,256]{1,0:T(8,128)(2,1)S(1)}, bf16[1024,256]{1,0:T(8,128)(2,1)S(1)}, u32[]{:S(2)}, u32[]{:S(2)}) collective-permute-start(bf16[1024,256]{1,0:T(8,128)(2,1)S(1)} %partial_messages.4.refs_1_), channel_id=1, source_target_pairs={{0,1},{1,0},{2,3},{3,2},{4,5},{5,4},{6,7},{7,6},{8,9},{9,8},{10,11... | collective-permute-start | bytes 1572872 | tf_op jit(solution)/shard_map/ppermute | solution.py:596
  32.4 2.6 %copy-start.2 = (bf16[512,256]{1,0:T(8,128)(2,1)S(1)}, bf16[512,256]{1,0:T(8,128)(2,1)}, u32[]{:S(2)}) copy-start(bf16[512,256]{1,0:T(8,128)(2,1)} %copy-done.1) | copy-start | bytes 786436
  38.1 17.8 %collective-permute-start.16 = (bf16[1024,256]{1,0:T(8,128)(2,1)S(1)}, bf16[1024,256]{1,0:T(8,128)(2,1)S(1)}, u32[]{:S(2)}, u32[]{:S(2)}) collective-permute-start(bf16[1024,256]{1,0:T(8,128)(2,1)S(1)} %partial_messages.5.refs_1_), channel_id=1, source_target_pairs={{0,1},{1,0},{2,3},{3,2},{4,5},{5,4},{6,7},{7,6},{8,9},{9,8},{10,11... | collective-permute-start | bytes 1572872 | tf_op jit(solution)/shard_map/ppermute | solution.py:596
  45.7 25.1 %copy-start.3 = (bf16[1024,256]{1,0:T(8,128)(2,1)S(1)}, bf16[1024,256]{1,0:T(8,128)(2,1)}, u32[]{:S(2)}) copy-start(bf16[1024,256]{1,0:T(8,128)(2,1)} %nodes.3) | copy-start | bytes 1572868
  45.7 25.1 %copy-start.4 = (bf16[1024,256]{1,0:T(8,128)(2,1)S(1)}, bf16[1024,256]{1,0:T(8,128)(2,1)}, u32[]{:S(2)}) copy-start(bf16[1024,256]{1,0:T(8,128)(2,1)} %cot.3) | copy-start | bytes 1572868
  45.7 25.1 %copy-start.5 = (bf16[512,256]{1,0:T(8,128)(2,1)S(1)}, bf16[512,256]{1,0:T(8,128)(2,1)}, u32[]{:S(2)}) copy-start(bf16[512,256]{1,0:T(8,128)(2,1)} %w_in.1) | copy-start | bytes 786436
  45.7 25.1 %copy-start.6 = (bf16[256,256]{1,0:T(8,128)(2,1)S(1)}, bf16[256,256]{1,0:T(8,128)(2,1)}, u32[]{:S(2)}) copy-start(bf16[256,256]{1,0:T(8,128)(2,1)} %refs_5_.1) | copy-start | bytes 393220
  45.7 25.1 %copy-start.7 = (f32[256]{0:T(256)S(1)}, f32[256]{0:T(256)}, u32[]{:S(2)}) copy-start(f32[256]{0:T(256)} %param.15) | copy-start | bytes 3076
  45.7 25.1 %copy-start.8 = (f32[256]{0:T(256)S(1)}, f32[256]{0:T(256)}, u32[]{:S(2)}) copy-start(f32[256]{0:T(256)} %param.17) | copy-start | bytes 3076
  45.7 25.1 %copy-start.9 = (f32[256]{0:T(256)S(1)}, f32[256]{0:T(256)}, u32[]{:S(2)}) copy-start(f32[256]{0:T(256)} %param.18) | copy-start | bytes 3076
  45.7 10.4 %collective-permute-start.14 = (bf16[1024,256]{1,0:T(8,128)(2,1)S(1)}, bf16[1024,256]{1,0:T(8,128)(2,1)S(1)}, u32[]{:S(2)}, u32[]{:S(2)}) collective-permute-start(bf16[1024,256]{1,0:T(8,128)(2,1)S(1)} %sum_terms.15), channel_id=1, source_target_pairs={{0,4},{1,2},{2,1},{3,7},{4,0},{5,6},{6,5},{7,3},{8,12},{9,10},{10,... | collective-permute-start | bytes 1572872 | tf_op jit(solution)/shard_map/ppermute | solution.py:609
  56.1 4.0 %collective-permute-start.17 = (bf16[1024,256]{1,0:T(8,128)(2,1)S(1)}, bf16[1024,256]{1,0:T(8,128)(2,1)S(1)}, u32[]{:S(2)}, u32[]{:S(2)}) collective-permute-start(bf16[1024,256]{1,0:T(8,128)(2,1)S(1)} %sum_terms.17), channel_id=1, source_target_pairs={{0,4},{1,2},{2,1},{3,7},{4,0},{5,6},{6,5},{7,3},{8,12},{9,10},{10,... | collective-permute-start | bytes 1572872 | tf_op jit(solution)/shard_map/ppermute | solution.py:609
  56.4 14.4 %collective-permute-start.15 = (bf16[1024,256]{1,0:T(8,128)(2,1)S(1)}, bf16[1024,256]{1,0:T(8,128)(2,1)S(1)}, u32[]{:S(2)}, u32[]{:S(2)}) collective-permute-start(bf16[1024,256]{1,0:T(8,128)(2,1)S(1)} %sum_terms.16), channel_id=1, source_target_pairs={{0,1},{1,0},{2,3},{3,2},{4,5},{5,4},{6,7},{7,6},{8,9},{9,8},{10,11... | collective-permute-start | bytes 1572872 | tf_op jit(solution)/shard_map/ppermute | solution.py:596
  74.0 11.8 %collective-permute-start.18 = (bf16[1024,256]{1,0:T(8,128)(2,1)S(1)}, bf16[1024,256]{1,0:T(8,128)(2,1)S(1)}, u32[]{:S(2)}, u32[]{:S(2)}) collective-permute-start(bf16[1024,256]{1,0:T(8,128)(2,1)S(1)} %get-tuple-element.36.refs_0_), channel_id=1, source_target_pairs={{0,1},{1,0},{2,3},{3,2},{4,5},{5,4},{6,7},{7,6},{8,9},{9,8},{10,11... | collective-permute-start | bytes 1572872 | tf_op jit(solution)/shard_map/ppermute | solution.py:596
  75.8 10.1 %collective-permute-start.19 = (bf16[1024,256]{1,0:T(8,128)(2,1)S(1)}, bf16[1024,256]{1,0:T(8,128)(2,1)S(1)}, u32[]{:S(2)}, u32[]{:S(2)}) collective-permute-start(bf16[1024,256]{1,0:T(8,128)(2,1)S(1)} %get-tuple-element.36.refs_0_), channel_id=1, source_target_pairs={{0,4},{1,2},{2,1},{3,7},{4,0},{5,6},{6,5},{7,3},{8,12},{9,10},{10,... | collective-permute-start | bytes 1572872 | tf_op jit(solution)/shard_map/ppermute | solution.py:609
  85.8 6.2 %collective-permute-start.21 = (bf16[1024,256]{1,0:T(8,128)(2,1)S(1)}, bf16[1024,256]{1,0:T(8,128)(2,1)S(1)}, u32[]{:S(2)}, u32[]{:S(2)}) collective-permute-start(bf16[1024,256]{1,0:T(8,128)(2,1)S(1)} %collective-permute-done.18.refs_0_.refs_1_), channel_id=1, source_target_pairs={{0,4},{1,2},{2,1},{3,7},{4,0},{5,6},{6,5},{7,3},{8,12},{9,10},{10,... | collective-permute-start | bytes 1572872 | tf_op jit(solution)/shard_map/ppermute | solution.py:609
  87.4 13.7 %collective-permute-start.23 = (f32[448,256]{1,0:T(8,128)S(1)}, f32[448,256]{1,0:T(8,128)S(1)}, u32[]{:S(2)}, u32[]{:S(2)}) collective-permute-start(f32[448,256]{1,0:T(8,128)S(1)} %get-tuple-element.39), channel_id=1, source_target_pairs={{0,4},{4,0},{8,12},{12,8},{16,20},{20,16},{24,28},{28,24},{1,5},{5... | collective-permute-start | bytes 1376264 | tf_op jit(solution)/shard_map/ppermute | solution.py:592
  88.0 16.9 %collective-permute-start.20 = (bf16[1024,256]{1,0:T(8,128)(2,1)S(1)}, bf16[1024,256]{1,0:T(8,128)(2,1)S(1)}, u32[]{:S(2)}, u32[]{:S(2)}) collective-permute-start(bf16[1024,256]{1,0:T(8,128)(2,1)S(1)} %collective-permute-done.19.refs_1_.refs_2_), channel_id=1, source_target_pairs={{0,1},{1,0},{2,3},{3,2},{4,5},{5,4},{6,7},{7,6},{8,9},{9,8},{10,11... | collective-permute-start | bytes 1572872 | tf_op jit(solution)/shard_map/ppermute | solution.py:596
  92.0 23.7 %collective-permute-start.22 = (bf16[1024,256]{1,0:T(8,128)(2,1)S(1)}, bf16[1024,256]{1,0:T(8,128)(2,1)S(1)}, u32[]{:S(2)}, u32[]{:S(2)}) collective-permute-start(bf16[1024,256]{1,0:T(8,128)(2,1)S(1)} %collective-permute-done.21.refs_18_.refs_4_), channel_id=1, source_target_pairs={{0,1},{1,0},{2,3},{3,2},{4,5},{5,4},{6,7},{7,6},{8,9},{9,8},{10,11... | collective-permute-start | bytes 1572872 | tf_op jit(solution)/shard_map/ppermute | solution.py:596
  101.1 8.9 %collective-permute-start.24 = (f32[112,256]{1,0:T(8,128)S(1)}, f32[112,256]{1,0:T(8,128)S(1)}, u32[]{:S(2)}, u32[]{:S(2)}) collective-permute-start(f32[112,256]{1,0:T(8,128)S(1)} %sum_terms.19), channel_id=1, source_target_pairs={{0,16},{4,20},{8,24},{12,28},{16,0},{20,4},{24,8},{28,12},{1,17},{... | collective-permute-start | bytes 344072 | tf_op jit(solution)/shard_map/ppermute | solution.py:592
  102.7 7.3 %collective-permute-start.25 = (f32[112,256]{1,0:T(8,128)S(1)}, f32[112,256]{1,0:T(8,128)S(1)}, u32[]{:S(2)}, u32[]{:S(2)}) collective-permute-start(f32[112,256]{1,0:T(8,128)S(1)} %sum_terms.20), channel_id=1, source_target_pairs={{0,8},{4,12},{8,0},{12,4},{16,24},{20,28},{24,16},{28,20},{1,9},{5... | collective-permute-start | bytes 344072 | tf_op jit(solution)/shard_map/ppermute | solution.py:592
  104.3 5.8 %collective-permute-start.26 = (f32[112,256]{1,0:T(8,128)S(1)}, f32[112,256]{1,0:T(8,128)S(1)}, u32[]{:S(2)}, u32[]{:S(2)}) collective-permute-start(f32[112,256]{1,0:T(8,128)S(1)} %sum_terms.21), channel_id=1, source_target_pairs={{0,24},{4,28},{8,16},{12,20},{16,8},{20,12},{24,0},{28,4},{1,25},{... | collective-permute-start | bytes 344072 | tf_op jit(solution)/shard_map/ppermute | solution.py:592
  122.3 2.7 %collective-permute-start.28 = (bf16[2048,256]{1,0:T(8,128)(2,1)S(1)}, bf16[2048,256]{1,0:T(8,128)(2,1)S(1)}, u32[]{:S(2)}, u32[]{:S(2)}) collective-permute-start(bf16[2048,256]{1,0:T(8,128)(2,1)S(1)} %get-tuple-element.43), channel_id=1, source_target_pairs={{0,4},{4,0},{8,12},{12,8},{16,20},{20,16},{24,28},{28,24},{1,5},{5... | collective-permute-start | bytes 3145736 | tf_op jit(solution)/shard_map/ppermute | solution.py:592
  122.4 5.4 %collective-permute-start.27 = (bf16[2048,256]{1,0:T(8,128)(2,1)S(1)}, bf16[2048,256]{1,0:T(8,128)(2,1)S(1)}, u32[]{:S(2)}, u32[]{:S(2)}) collective-permute-start(bf16[2048,256]{1,0:T(8,128)(2,1)S(1)} %get-tuple-element.42), channel_id=1, source_target_pairs={{0,4},{4,0},{8,12},{12,8},{16,20},{20,16},{24,28},{28,24},{1,5},{5... | collective-permute-start | bytes 3145736 | tf_op jit(solution)/shard_map/ppermute | solution.py:592
  125.2 17.7 %collective-permute-start.30 = (bf16[1024,256]{1,0:T(8,128)(2,1)S(1)}, bf16[1024,256]{1,0:T(8,128)(2,1)S(1)}, u32[]{:S(2)}, u32[]{:S(2)}) collective-permute-start(bf16[1024,256]{1,0:T(8,128)(2,1)S(1)} %sum_terms.24.refs_23_.refs_4_), channel_id=1, source_target_pairs={{0,16},{4,20},{8,24},{12,28},{16,0},{20,4},{24,8},{28,12},{1,17},{... | collective-permute-start | bytes 1572872 | tf_op jit(solution)/shard_map/ppermute | solution.py:592
  127.7 16.3 %collective-permute-start.29 = (bf16[1024,256]{1,0:T(8,128)(2,1)S(1)}, bf16[1024,256]{1,0:T(8,128)(2,1)S(1)}, u32[]{:S(2)}, u32[]{:S(2)}) collective-permute-start(bf16[1024,256]{1,0:T(8,128)(2,1)S(1)} %sum_terms.23.refs_22_.refs_3_), channel_id=1, source_target_pairs={{0,8},{4,12},{8,0},{12,4},{16,24},{20,28},{24,16},{28,20},{1,9},{5... | collective-permute-start | bytes 1572872 | tf_op jit(solution)/shard_map/ppermute | solution.py:592
  127.8 11.5 %collective-permute-start.33 = (bf16[112,256]{1,0:T(8,128)(2,1)S(1)}, bf16[112,256]{1,0:T(8,128)(2,1)S(1)}, u32[]{:S(2)}, u32[]{:S(2)}) collective-permute-start(bf16[112,256]{1,0:T(8,128)(2,1)S(1)} %sum_terms.28.refs_1_), channel_id=1, source_target_pairs={{0,1},{1,2},{2,3},{3,0},{4,5},{5,6},{6,7},{7,4},{8,9},{9,10},{10,1... | collective-permute-start | bytes 172040 | tf_op jit(solution)/shard_map/ppermute | solution.py:600
  129.9 9.4 %collective-permute-start.34 = (bf16[112,256]{1,0:T(8,128)(2,1)S(1)}, bf16[112,256]{1,0:T(8,128)(2,1)S(1)}, u32[]{:S(2)}, u32[]{:S(2)}) collective-permute-start(bf16[112,256]{1,0:T(8,128)(2,1)S(1)} %sum_terms.28.refs_1_), channel_id=1, source_target_pairs={{0,2},{1,3},{2,0},{3,1},{4,6},{5,7},{6,4},{7,5},{8,10},{9,11},{10,... | collective-permute-start | bytes 172040 | tf_op jit(solution)/shard_map/ppermute | solution.py:600
  131.1 8.1 %collective-permute-start.35 = (bf16[112,256]{1,0:T(8,128)(2,1)S(1)}, bf16[112,256]{1,0:T(8,128)(2,1)S(1)}, u32[]{:S(2)}, u32[]{:S(2)}) collective-permute-start(bf16[112,256]{1,0:T(8,128)(2,1)S(1)} %sum_terms.28.refs_1_), channel_id=1, source_target_pairs={{0,3},{1,0},{2,1},{3,2},{4,7},{5,4},{6,5},{7,6},{8,11},{9,8},{10,9... | collective-permute-start | bytes 172040 | tf_op jit(solution)/shard_map/ppermute | solution.py:600
  139.3 5.2 %collective-permute-start.38 = (bf16[112,256]{1,0:T(8,128)(2,1)S(1)}, bf16[112,256]{1,0:T(8,128)(2,1)S(1)}, u32[]{:S(2)}, u32[]{:S(2)}) collective-permute-start(bf16[112,256]{1,0:T(8,128)(2,1)S(1)} %sum_terms.29), channel_id=1, source_target_pairs={{0,24},{4,28},{8,16},{12,20},{16,8},{20,12},{24,0},{28,4},{1,25},{... | collective-permute-start | bytes 172040 | tf_op jit(solution)/shard_map/ppermute | solution.py:592
  139.4 5.2 %collective-permute-start.37 = (bf16[112,256]{1,0:T(8,128)(2,1)S(1)}, bf16[112,256]{1,0:T(8,128)(2,1)S(1)}, u32[]{:S(2)}, u32[]{:S(2)}) collective-permute-start(bf16[112,256]{1,0:T(8,128)(2,1)S(1)} %sum_terms.29), channel_id=1, source_target_pairs={{0,16},{4,20},{8,24},{12,28},{16,0},{20,4},{24,8},{28,12},{1,17},{... | collective-permute-start | bytes 172040 | tf_op jit(solution)/shard_map/ppermute | solution.py:592
  141.7 4.9 %collective-permute-start.36 = (bf16[112,256]{1,0:T(8,128)(2,1)S(1)}, bf16[112,256]{1,0:T(8,128)(2,1)S(1)}, u32[]{:S(2)}, u32[]{:S(2)}) collective-permute-start(bf16[112,256]{1,0:T(8,128)(2,1)S(1)} %sum_terms.29), channel_id=1, source_target_pairs={{0,8},{4,12},{8,0},{12,4},{16,24},{20,28},{24,16},{28,20},{1,9},{5... | collective-permute-start | bytes 172040 | tf_op jit(solution)/shard_map/ppermute | solution.py:592
  143.0 7.3 %collective-permute-start.31 = (bf16[512,256]{1,0:T(8,128)(2,1)S(1)}, bf16[512,256]{1,0:T(8,128)(2,1)S(1)}, u32[]{:S(2)}, u32[]{:S(2)}) collective-permute-start(bf16[512,256]{1,0:T(8,128)(2,1)S(1)} %sum_terms.25), channel_id=1, source_target_pairs={{0,8},{4,12},{8,0},{12,4},{16,24},{20,28},{24,16},{28,20},{1,9},{5... | collective-permute-start | bytes 786440 | tf_op jit(solution)/shard_map/ppermute | solution.py:592
  144.0 6.4 %collective-permute-start.32 = (bf16[512,256]{1,0:T(8,128)(2,1)S(1)}, bf16[512,256]{1,0:T(8,128)(2,1)S(1)}, u32[]{:S(2)}, u32[]{:S(2)}) collective-permute-start(bf16[512,256]{1,0:T(8,128)(2,1)S(1)} %sum_terms.26), channel_id=1, source_target_pairs={{0,16},{4,20},{8,24},{12,28},{16,0},{20,4},{24,8},{28,12},{1,17},{... | collective-permute-start | bytes 786440 | tf_op jit(solution)/shard_map/ppermute | solution.py:592
  146.6 1.6 %collective-permute-start.39 = (bf16[448,256]{1,0:T(8,128)(2,1)S(1)}, bf16[448,256]{1,0:T(8,128)(2,1)S(1)}, u32[]{:S(2)}, u32[]{:S(2)}) collective-permute-start(bf16[448,256]{1,0:T(8,128)(2,1)S(1)} %pad_maximum_fusion.even), channel_id=1, source_target_pairs={{0,4},{4,0},{8,12},{12,8},{16,20},{20,16},{24,28},{28,24},{1,5},{5... | collective-permute-start | bytes 688136 | tf_op jit(solution)/shard_map/ppermute | solution.py:592

commit v15 on v13

--- a/solution.py
+++ b/solution.py
@@ -146,77 +146,69 @@
     )(here, cols, *pieces, tiles)
 
 
-def mlp_kernel(kinds, here, nodes, cot, *refs):
+def mlp_kernel(kinds, step, here, nodes, cot, *refs):
     n_parts = sum(len(chunk) for chunk in kinds)
     parts = refs[:n_parts]
     w_in, bias, w_out, gain, shift, updated, gpre_o, act_o, gproj_o, msg_o, vec = refs[
         n_parts : n_parts + 11
     ]
     gmsgs = refs[n_parts + 11 :]
-    width = nodes.shape[1]
+    rows, width = nodes.shape
     inner = Place(here).inner()
-    messages = []
-    place = 0
-    for chunk in kinds:
-        total = None
-        for kind in chunk:
-            term = parts[place][...].astype(F32)
-            place += 1
-            if kind == "inner":
-                term = jnp.where(inner, term, 0.0)
-            total = term if total is None else total + term
-        messages.append(total.astype(BF16))
-    message = jnp.concatenate(messages, axis=1) if len(messages) > 1 else messages[0]
-    node = nodes[...]
-    pre = mm(node, w_in[:width]) + mm(message, w_in[width:]) + bias[...]
-    sig = 0.5 + 0.5 * jnp.tanh(0.5 * pre)
-    act = (pre * sig).astype(BF16)
-    proj = mm(act, w_out[...])
-    mean = jnp.mean(proj, axis=-1, keepdims=True)
-    var = jnp.mean((proj - mean) ** 2, axis=-1, keepdims=True)
-    rstd = 1.0 / jnp.sqrt(var + 1e-05)
-    normed = (proj - mean) * rstd
-    updated[...] = (node.astype(F32) + normed * gain[...] + shift[...]).astype(BF16)
-    grad_out = cot[...].astype(F32)
-    gscaled = grad_out * gain[...]
-    gproj = (
-        (
-            gscaled
-            - jnp.mean(gscaled, axis=-1, keepdims=True)
-            - normed * jnp.mean(gscaled * normed, axis=-1, keepdims=True)
-        )
-        * rstd
-    ).astype(BF16)
-    gact = mm(gproj, w_out[...], NT)
-    gpre = gact * sig * (1.0 + pre * (1.0 - sig))
-    gpre_b = gpre.astype(BF16)
-    gmsg = mm(gpre_b, w_in[width:], NT).astype(BF16)
-    part = width // len(gmsgs)
-    for index, out in enumerate(gmsgs):
-        out[...] = gmsg[:, index * part : (index + 1) * part]
-    gpre_o[...] = gpre_b
-    act_o[...] = act
-    gproj_o[...] = gproj
-    msg_o[...] = message
-
-    @pl.when(pl.program_id(0) == 0)
-    def _():
-        vec[...] = jnp.zeros_like(vec)
-
-    vec[0:1] += jnp.sum(gpre, axis=0, keepdims=True)
-    vec[1:2] += jnp.sum(grad_out * normed, axis=0, keepdims=True)
-    vec[2:3] += jnp.sum(grad_out, axis=0, keepdims=True)
+    vec[...] = jnp.zeros_like(vec)
+    for first in range(0, rows, step):
+        where = slice(first, first + step)
+        messages = []
+        place = 0
+        for chunk in kinds:
+            total = None
+            for kind in chunk:
+                term = parts[place][where].astype(F32)
+                place += 1
+                if kind == "inner":
+                    term = jnp.where(inner, term, 0.0)
+                total = term if total is None else total + term
+            messages.append(total.astype(BF16))
+        message = jnp.concatenate(messages, axis=1) if len(messages) > 1 else messages[0]
+        node = nodes[where]
+        pre = mm(node, w_in[:width]) + mm(message, w_in[width:]) + bias[...]
+        sig = 0.5 + 0.5 * jnp.tanh(0.5 * pre)
+        act = (pre * sig).astype(BF16)
+        proj = mm(act, w_out[...])
+        mean = jnp.mean(proj, axis=-1, keepdims=True)
+        var = jnp.mean((proj - mean) ** 2, axis=-1, keepdims=True)
+        rstd = 1.0 / jnp.sqrt(var + 1e-05)
+        normed = (proj - mean) * rstd
+        updated[where] = (node.astype(F32) + normed * gain[...] + shift[...]).astype(BF16)
+        grad_out = cot[where].astype(F32)
+        gscaled = grad_out * gain[...]
+        gproj = (
+            (
+                gscaled
+                - jnp.mean(gscaled, axis=-1, keepdims=True)
+                - normed * jnp.mean(gscaled * normed, axis=-1, keepdims=True)
+            )
+            * rstd
+        ).astype(BF16)
+        gact = mm(gproj, w_out[...], NT)
+        gpre = gact * sig * (1.0 + pre * (1.0 - sig))
+        gpre_b = gpre.astype(BF16)
+        gmsg = mm(gpre_b, w_in[width:], NT).astype(BF16)
+        part = width // len(gmsgs)
+        for index, out in enumerate(gmsgs):
+            out[where] = gmsg[:, index * part : (index + 1) * part]
+        gpre_o[where] = gpre_b
+        act_o[where] = act
+        gproj_o[where] = gproj
+        msg_o[where] = message
+        vec[0:1] += jnp.sum(gpre, axis=0, keepdims=True)
+        vec[1:2] += jnp.sum(grad_out * normed, axis=0, keepdims=True)
+        vec[2:3] += jnp.sum(grad_out, axis=0, keepdims=True)
 
 
 def mlp_call(here, nodes, cot, parts, kinds, w_in, bias, w_out, gain, shift):
     rows, width = nodes.shape
     step = min(rows, 512)
-
-    def blocked(array):
-        return pl.BlockSpec((step, array.shape[1]), lambda i: (i, 0))
-
-    def whole(array):
-        return pl.BlockSpec(array.shape, lambda i: (0, 0))
 
     flat = [term for chunk in parts for term in chunk]
     row_like = jax.ShapeDtypeStruct((rows, width), BF16)
@@ -224,11 +216,10 @@
     outs = [row_like] * 5 + [jax.ShapeDtypeStruct((8, width), F32)] + [chunk_like] * len(parts)
     weights = (w_in, bias, w_out, gain, shift)
     result = pl.pallas_call(
-        functools.partial(mlp_kernel, kinds),
-        grid=(rows // step,),
+        functools.partial(mlp_kernel, kinds, step),
         out_shape=outs,
-        in_specs=[SMEM] + [blocked(a) for a in (nodes, cot, *flat)] + [whole(a) for a in weights],
-        out_specs=[blocked(a) for a in outs[:5]] + [whole(outs[5])] + [blocked(a) for a in outs[6:]],
+        in_specs=[SMEM] + [VMEM] * (2 + len(flat) + len(weights)),
+        out_specs=[VMEM] * len(outs),
         compiler_params=params(40),
         cost_estimate=SMALL,
         name="mlp",
@@ -236,52 +227,42 @@
     return result[:6], result[6:]
 
 
-def weight_kernel(factor, pieces, n_after, here, nodes, msg, act, gpre, gproj, cot, w_in, vec, *refs):
+def weight_kernel(factor, pieces, step, n_after, here, nodes, msg, act, gpre, gproj, cot, w_in, vec, *refs):
     *outs, direct, grads = refs[n_after:]
-    width = nodes.shape[1]
-
-    @pl.when(pl.program_id(0) == 0)
-    def _():
-        grads[...] = jnp.zeros_like(grads)
-        grads[3 * width : 3 * width + 8] = vec[...] * factor
-
-    gpre_b = gpre[...]
-    grads[:width] += mm(nodes[...], gpre_b, TN) * factor
-    grads[width : 2 * width] += mm(msg[...], gpre_b, TN) * factor
-    grads[2 * width : 3 * width] += mm(act[...], gproj[...], TN) * factor
-    direct[...] = cot[...].astype(F32) + mm(gpre_b, w_in[:width], NT)
-
-    @pl.when(pl.program_id(0) == pl.num_programs(0) - 1)
-    def _():
-        if pieces == 1:
-            outs[0][...] = grads[: outs[0].shape[0]]
-        else:
-            rows = grads.shape[0] // pieces
-            for place, member in enumerate(SWAP_ORDER):
-                where = pl.ds(pl.multiple_of((Place(here).mine ^ member) * rows, 8), rows)
-                out, index = outs[2 * place // pieces], place % (pieces // 2)
-                out[index * rows : (index + 1) * rows] = grads[where]
+    rows, width = nodes.shape
+    for first in range(0, rows, step):
+        where = slice(first, first + step)
+        gpre_b = gpre[where]
+        terms = (mm(nodes[where], gpre_b, TN), mm(msg[where], gpre_b, TN), mm(act[where], gproj[where], TN))
+        for index, term in enumerate(terms):
+            own = slice(index * width, (index + 1) * width)
+            grads[own] = term if first == 0 else grads[own] + term
+        direct[where] = cot[where].astype(F32) + mm(gpre_b, w_in[:width], NT)
+    grads[3 * width : 3 * width + 8] = vec[...]
+    grads[3 * width + 8 :] = jnp.zeros((grads.shape[0] - 3 * width - 8, width), F32)
+    if pieces == 1:
+        outs[0][...] = grads[: outs[0].shape[0]] * factor
+    else:
+        rows = grads.shape[0] // pieces
+        for place, member in enumerate(SWAP_ORDER):
+            where = pl.ds(pl.multiple_of((Place(here).mine ^ member) * rows, 8), rows)
+            out, index = outs[2 * place // pieces], place % (pieces // 2)
+            out[index * rows : (index + 1) * rows] = grads[where] * factor
 
 
 def weight_call(factor, pieces, here, nodes, msg, act, gpre, gproj, cot, w_in, vec, after=()):
     rows, width = nodes.shape
     step = min(rows, 256)
-    blocked = pl.BlockSpec((step, width), lambda i: (i, 0))
-
-    def whole(shape):
-        return pl.BlockSpec(shape, lambda i: (0, 0))
-
     padded = (3 * width + width // 2, width)
     if pieces == 1:
         outs = [jax.ShapeDtypeStruct((3 * width + 8, width), F32)]
     else:
         outs = [jax.ShapeDtypeStruct((padded[0] // 2, width), F32)] * 2
     return pl.pallas_call(
-        functools.partial(weight_kernel, factor, pieces, len(after)),
-        grid=(rows // step,),
+        functools.partial(weight_kernel, factor, pieces, step, len(after)),
         out_shape=[*outs, jax.ShapeDtypeStruct((rows, width), F32)],
-        in_specs=[SMEM] + [blocked] * 6 + [whole(w_in.shape), whole(vec.shape)] + [ANY] * len(after),
-        out_specs=[whole(out.shape) for out in outs] + [blocked],
+        in_specs=[SMEM] + [VMEM] * 8 + [ANY] * len(after),
+        out_specs=[VMEM] * (len(outs) + 1),
         scratch_shapes=[pltpu.VMEM(padded, F32)],
         compiler_params=params(40),
         cost_estimate=SMALL,
@@ -342,19 +323,19 @@
             pl.when(condition)(getattr(copy, verb))
 
 
-def for_live(found, entry):
+def for_live(first, last, entry):
     def several(i, carry):
         for index in range(LIVE_STEP):
-            entry(i * LIVE_STEP + index)
+            entry(first + i * LIVE_STEP + index)
         return carry
 
     def one(i, carry):
         entry(i)
         return carry
 
-    full = found // LIVE_STEP
+    full = jnp.maximum(last - first, 0) // LIVE_STEP
     lax.fori_loop(0, full, several, 0)
-    lax.fori_loop(full * LIVE_STEP, found, one, 0)
+    lax.fori_loop(first + full * LIVE_STEP, last, one, 0)
 
 
 def turn_kernel(slots, cols, tiles, out, tiles_v, live, sem):
@@ -372,10 +353,9 @@
     copy.wait()
 
     def entry(place):
-        tile_index = live[place]
-        out[tile_index] = tiles_v[tile_index].T
-
-    for_live(found, entry)
+        out[place] = tiles_v[live[place]].T
+
+    for_live(0, found, entry)
 
 
 def turn_call(cols, tiles):
@@ -401,33 +381,29 @@
     grads, tiles = refs[:n_grads], refs[n_grads]
     refs = refs[n_grads + 1 + n_after :]
     outs = refs[: len(out_pieces)]
-    grad_v, tiles_v, acc, live, source, sem, tile_sem = refs[len(out_pieces) :]
+    grad_v, acc, live, source, sem = refs[len(out_pieces) :]
     n_tiles, block = tiles.shape[:2]
     here = Place(here, paired, rows // block)
     jobs = grad_jobs(rows, grads, grad_v, sem, here)
     run_jobs(jobs, "start")
-    tile_copy = pltpu.make_async_copy(tiles, tiles_v, tile_sem.at[0])
-    tile_copy.start()
-    acc[...] = jnp.zeros_like(acc)
 
     def collect(row, found):
         count = cols[slots, row]
         for slot in range(slots):
-            live[found] = row * slots + slot
+            live[found] = row
             source[found] = here.source(cols[slot, row])
             found = found + (slot < count).astype(jnp.int32)
         return found
 
     found = lax.fori_loop(0, n_tiles // slots, collect, jnp.int32(0))
+    acc[...] = jnp.zeros_like(acc)
     run_jobs(jobs, "wait")
-    tile_copy.wait()
 
     def entry(place):
-        tile_index = live[place]
-        part = mm(tiles_v[tile_index], grad_v[block_at(tile_index // slots, block)])
-        acc[block_at(source[place], block)] += part
-
-    for_live(found, entry)
+        term = mm(tiles[place], grad_v[block_at(live[place], block)])
+        acc[block_at(source[place], block)] += term
+
+    for_live(0, found, entry)
     piece = acc.shape[0] // sum(len(members) for members in out_pieces)
     for out, members in zip(outs, out_pieces):
         for index, member in enumerate(members):
@@ -443,16 +419,14 @@
     return pl.pallas_call(
         functools.partial(back_kernel, rows, slots, len(grads), len(after), out_pieces, paired),
         out_shape=[jax.ShapeDtypeStruct((len(m) * piece, width), BF16) for m in out_pieces],
-        in_specs=[SMEM] * 2 + [ANY] * len(grads) + [HBM] + [ANY] * len(after),
+        in_specs=[SMEM] * 2 + [ANY] * len(grads) + [VMEM] + [ANY] * len(after),
         out_specs=[VMEM] * len(out_pieces),
         scratch_shapes=[
             pltpu.VMEM((total, width), BF16),
-            pltpu.VMEM((n_tiles, block, block), BF16),
             pltpu.VMEM((gathered, width), F32),
             pltpu.SMEM((n_tiles + 8,), jnp.int32),
             pltpu.SMEM((n_tiles + 8,), jnp.int32),
             pltpu.SemaphoreType.DMA((len(grads),)),
-            pltpu.SemaphoreType.DMA((1,)),
         ],
         compiler_params=params(28 if gathered <= 8192 else 56),
         cost_estimate=SMALL,
@@ -517,7 +491,7 @@
         node = nodes_v[block_at(source[place], block)]
         tiles_v[tile_index] = (mm(grad, node, NT) * scale).astype(BF16)
 
-    for_live(found, entry)
+    for_live(0, found, entry)
     size = blocks * slots
     copies = []
     for index, group in enumerate(groups):
@@ -630,7 +604,7 @@
 def sum_call(here, rows, terms, gated=(), split=(), dtype=BF16, after=()):
     both = [*terms, *gated]
     width = both[0][0].shape[1]
-    step = min(rows, 256)
+    step = min(rows, 512)
     steps = rows // step
     half = steps // 2
 
@@ -657,7 +631,7 @@
         + [spec_of(piece) for pair in split for spec_of, (_, piece) in zip((early, late), pair)]
         + [ANY] * len(after),
         out_specs=pl.BlockSpec((step, width), lambda i: (i, 0)),
-        compiler_params=params(8),
+        compiler_params=params(16),
         cost_estimate=SMALL,
         name="sum_terms",
     )(here, *(array for array, _ in both), *(array for pair in split for array, _ in pair), *after)

time: 153 us -> 151 us (0.987)
  waiting for transfers between devices: 63.4 us -> 61.7 us
where the time goes in v15:
time: 151 us
  waiting for transfers between devices  61.7 us (41%)
  starting transfers between devices  47.2 us (31%)
  Pallas kernels  38.8 us (26%)
    ppermute x6, waiting for transfers between devices, outer_swap(): return lax.ppermute(value, 'col', [(0, 1), (1, 0), (2, 3), (3, 2)])  38.1 us
    ppermute x27, waiting for transfers between devices, swap(): return lax.ppermute(value, 'row', [(i, i ^ bit) for i in range(8)])  23.6 us
    ppermute x6, starting transfers between devices, outer_swap(): return lax.ppermute(value, 'col', [(0, 1), (1, 0), (2, 3), (3, 2)])  20.9 us
    ppermute x27, starting transfers between devices, swap(): return lax.ppermute(value, 'row', [(i, i ^ bit) for i in range(8)])  19.7 us
    pallas_call x2, Pallas kernels, tile_grad_call(): pl.pallas_call(functools.partial(tile_grad_kernel, rows, slots, len(grads...  11.8 us
    pallas_call x3, Pallas kernels, forward_call(): pl.pallas_call(functools.partial(forward_kernel, outputs, len(pieces), pa...  10.4 us
    pallas_call x1, Pallas kernels, back_call(): pl.pallas_call(functools.partial(back_kernel, rows, slots, len(grads), le...  6.65 us
    ppermute x3, starting transfers between devices, turn(): return lax.ppermute(value, 'col', [(i, (i + by) % 4) for i in range(4)])  6.37 us
  transfers between devices with their start and end apart: 40, of which 17 were waited for; matrix products, arithmetic and copies ran while one was open for 1% of the time, Pallas kernels for 16%

profile of v15, /device:TPU:0, one launch (start us, length us, event | category | flops | bytes accessed | tf_op | source)
XLA Modules:
  0.0 150.6 jit_solution(9129697265405173358)
XLA Ops:
  0.6 0.5 collective-permute-start
  1.1 1.1 fusion
  2.2 2.6 %collective-permute-start.1 = (bf16[512,256]{1,0:T(8,128)(2,1)S(1)}, bf16[512,256]{1,0:T(8,128)(2,1)S(1)}, u32[]{:S(2)}, u32[]{:S(2)}) collective-permute-start(bf16[512,256]{1,0:T(8,128)(2,1)S(1)} %get-tuple-element.57.refs_0_.refs_2_.refs_6_), channel_id=1, source_target_pairs={{0,8},{4,12},{8,0},{12,4},{16,24},{20,28},{24,16},{28,20},{1,9},{5... | collective-permute-start | bytes 786440 | tf_op jit(solution)/shard_map/ppermute | solution.py:545
  4.8 1.5 %collective-permute-start.5 = (bf16[512,256]{1,0:T(8,128)(2,1)S(1)}, bf16[512,256]{1,0:T(8,128)(2,1)S(1)}, u32[]{:S(2)}, u32[]{:S(2)}) collective-permute-start(bf16[512,256]{1,0:T(8,128)(2,1)S(1)} %get-tuple-element.57.refs_0_.refs_2_.refs_6_), channel_id=1, source_target_pairs={{0,16},{4,20},{8,24},{12,28},{16,0},{20,4},{24,8},{28,12},{1,17},{... | collective-permute-start | bytes 786440 | tf_op jit(solution)/shard_map/ppermute | solution.py:545
  6.3 0.5 collective-permute-start.2
  6.9 5.1 %collective-permute-done.1.refs_3_.refs_5_.refs_9_ = bf16[512,256]{1,0:T(8,128)(2,1)S(1)} collective-permute-done((bf16[512,256]{1,0:T(8,128)(2,1)S(1)}, bf16[512,256]{1,0:T(8,128)(2,1)S(1)}, u32[]{:S(2)}, u32[]{:S(2)}) %collective-permute-start.1) | collective-permute-done | bytes 262176 | tf_op jit(solution)/shard_map/ppermute | solution.py:545
  11.9 2.0 %collective-permute-done.5.refs_7_.refs_9_.refs_13_ = bf16[512,256]{1,0:T(8,128)(2,1)S(1)} collective-permute-done((bf16[512,256]{1,0:T(8,128)(2,1)S(1)}, bf16[512,256]{1,0:T(8,128)(2,1)S(1)}, u32[]{:S(2)}, u32[]{:S(2)}) %collective-permute-start.5) | collective-permute-done | bytes 262176 | tf_op jit(solution)/shard_map/ppermute | solution.py:545
  14.0 3.6 %collective-permute-done.2.refs_4_.refs_6_.refs_10_ = bf16[512,256]{1,0:T(8,128)(2,1)S(1)} collective-permute-done((bf16[512,256]{1,0:T(8,128)(2,1)S(1)}, bf16[512,256]{1,0:T(8,128)(2,1)S(1)}, u32[]{:S(2)}, u32[]{:S(2)}) %collective-permute-start.2) | collective-permute-done | bytes 262176 | tf_op jit(solution)/shard_map/ppermute | solution.py:545
  17.6 2.0 %collective-permute-start.10 = (bf16[512,256]{1,0:T(8,128)(2,1)S(1)}, bf16[512,256]{1,0:T(8,128)(2,1)S(1)}, u32[]{:S(2)}, u32[]{:S(2)}) collective-permute-start(bf16[512,256]{1,0:T(8,128)(2,1)S(1)} %collective-permute-done.2.refs_4_.refs_6_.refs_10_), channel_id=1, source_target_pairs={{0,16},{4,20},{8,24},{12,28},{16,0},{20,4},{24,8},{28,12},{1,17},{... | collective-permute-start | bytes 786440 | tf_op jit(solution)/shard_map/ppermute | solution.py:545
  19.5 0.5 collective-permute-start.7
  20.1 2.9 %collective-permute-done.9.refs_11_.refs_13_.refs_17_ = bf16[512,256]{1,0:T(8,128)(2,1)S(1)} collective-permute-done((bf16[512,256]{1,0:T(8,128)(2,1)S(1)}, bf16[512,256]{1,0:T(8,128)(2,1)S(1)}, u32[]{:S(2)}, u32[]{:S(2)}) %collective-permute-start.9) | collective-permute-done | bytes 262176 | tf_op jit(solution)/shard_map/ppermute | solution.py:545
  23.0 2.5 %collective-permute-done.10.refs_12_.refs_14_.refs_18_ = bf16[512,256]{1,0:T(8,128)(2,1)S(1)} collective-permute-done((bf16[512,256]{1,0:T(8,128)(2,1)S(1)}, bf16[512,256]{1,0:T(8,128)(2,1)S(1)}, u32[]{:S(2)}, u32[]{:S(2)}) %collective-permute-start.10) | collective-permute-done | bytes 262176 | tf_op jit(solution)/shard_map/ppermute | solution.py:545
  25.5 0.7 pad_add_fusion.cols
  26.2 0.9 collective-permute-done.12.refs_14_.refs_16_.refs_20_
  27.2 3.5 %partial_messages.4.refs_1_ = bf16[1024,256]{1,0:T(8,128)(2,1)S(1)} custom-call(s32[1]{0:T(128)} %bitcast.here.refs_0_, s32[5,32]{1,0:T(8,128)S(1)} %pad_add_fusion.cols, bf16[512,256]{1,0:T(8,128)(2,1)S(1)} %get-tuple-element.57.refs_0_.refs_2_.refs_6_, bf16[512,256]{1,0:T(8,128)(2,1)S(1)} %get-tuple-element.56.refs_1_.refs_3_.refs_7_, ...), custom_call_target="tpu_custom_call" | custom-call | flops 1048576 | bytes 65536 | tf_op jit(solution)/shard_map/partial_messages/pallas_call | solution.py:132
  30.7 1.7 %collective-permute-start.13 = (bf16[1024,256]{1,0:T(8,128)(2,1)S(1)}, bf16[1024,256]{1,0:T(8,128)(2,1)S(1)}, u32[]{:S(2)}, u32[]{:S(2)}) collective-permute-start(bf16[1024,256]{1,0:T(8,128)(2,1)S(1)} %partial_messages.4.refs_1_), channel_id=1, source_target_pairs={{0,1},{1,0},{2,3},{3,2},{4,5},{5,4},{6,7},{7,6},{8,9},{9,8},{10,11... | collective-permute-start | bytes 1572872 | tf_op jit(solution)/shard_map/ppermute | solution.py:549
  32.4 3.0 %turned_tiles.1.refs_3_.refs_6_ = bf16[128,128,128]{2,1,0:T(8,128)(2,1)S(1)} custom-call(s32[5,32]{1,0:T(8,128)S(1)} %pad_add_fusion.cols, bf16[128,128,128]{2,1,0:T(8,128)(2,1)S(1)} %bitcast.16), custom_call_target="tpu_custom_call" | custom-call | flops 1048576 | bytes 65536 | tf_op jit(solution)/shard_map/turned_tiles/pallas_call | solution.py:364
  35.3 3.1 %partial_messages.5.refs_1_ = bf16[1024,256]{1,0:T(8,128)(2,1)S(1)} custom-call(s32[1]{0:T(128)} %bitcast.here.refs_0_, s32[5,32]{1,0:T(8,128)S(1)} %pad_add_fusion.cols, bf16[512,256]{1,0:T(8,128)(2,1)S(1)} %get-tuple-element.57.refs_0_.refs_2_.refs_6_, bf16[512,256]{1,0:T(8,128)(2,1)S(1)} %get-tuple-element.56.refs_1_.refs_3_.refs_7_, ...), custom_call_target="tpu_custom_call" | custom-call | flops 1048576 | bytes 65536 | tf_op jit(solution)/shard_map/partial_messages/pallas_call | solution.py:132
  38.6 6.9 %collective-permute-done.13.refs_2_ = bf16[1024,256]{1,0:T(8,128)(2,1)S(1)} collective-permute-done((bf16[1024,256]{1,0:T(8,128)(2,1)S(1)}, bf16[1024,256]{1,0:T(8,128)(2,1)S(1)}, u32[]{:S(2)}, u32[]{:S(2)}) %collective-permute-start.13) | collective-permute-done | bytes 524320 | tf_op jit(solution)/shard_map/ppermute | solution.py:549
  45.5 0.1 sum_terms.15
  45.7 0.1 collective-permute-start.14
  45.8 3.7 %partial_messages.3 = (bf16[1024,256]{1,0:T(8,128)(2,1)S(1)}, bf16[1024,256]{1,0:T(8,128)(2,1)S(1)}) custom-call(s32[1]{0:T(128)} %bitcast.here.refs_0_, s32[5,32]{1,0:T(8,128)S(1)} %pad_add_fusion.cols, bf16[512,256]{1,0:T(8,128)(2,1)S(1)} %get-tuple-element.57.refs_0_.refs_2_.refs_6_, bf16[512,256]{1,0:T(8,128)(2,1)S(1)} %get-tuple-element.56.refs_1_.refs_3_.refs_7_, ...), custom_call_target="tpu_custom_call" | custom-call | flops 1048576 | bytes 65536 | tf_op jit(solution)/shard_map/partial_messages/pallas_call | solution.py:132
  49.6 6.4 %collective-permute-done.16.refs_2_ = bf16[1024,256]{1,0:T(8,128)(2,1)S(1)} collective-permute-done((bf16[1024,256]{1,0:T(8,128)(2,1)S(1)}, bf16[1024,256]{1,0:T(8,128)(2,1)S(1)}, u32[]{:S(2)}, u32[]{:S(2)}) %collective-permute-start.16) | collective-permute-done | bytes 524320 | tf_op jit(solution)/shard_map/ppermute | solution.py:549
  55.9 0.1 sum_terms.17
  56.2 0.2 sum_terms.16
  56.4 3.6 %collective-permute-start.15 = (bf16[1024,256]{1,0:T(8,128)(2,1)S(1)}, bf16[1024,256]{1,0:T(8,128)(2,1)S(1)}, u32[]{:S(2)}, u32[]{:S(2)}) collective-permute-start(bf16[1024,256]{1,0:T(8,128)(2,1)S(1)} %sum_terms.16), channel_id=1, source_target_pairs={{0,1},{1,0},{2,3},{3,2},{4,5},{5,4},{6,7},{7,6},{8,9},{9,8},{10,11... | collective-permute-start | bytes 1572872 | tf_op jit(solution)/shard_map/ppermute | solution.py:549
  60.0 10.7 %collective-permute-done.15.refs_1_ = bf16[1024,256]{1,0:T(8,128)(2,1)S(1)} collective-permute-done((bf16[1024,256]{1,0:T(8,128)(2,1)S(1)}, bf16[1024,256]{1,0:T(8,128)(2,1)S(1)}, u32[]{:S(2)}, u32[]{:S(2)}) %collective-permute-start.15) | collective-permute-done | bytes 524320 | tf_op jit(solution)/shard_map/ppermute | solution.py:549
  70.8 2.9 %mlp.1 = (bf16[1024,256]{1,0:T(8,128)(2,1)}, bf16[1024,256]{1,0:T(8,128)(2,1)S(1)}, bf16[1024,256]{1,0:T(8,128)(2,1)S(1)}, bf16[1024,256]{1,0:T(8,128)(2,1)S(1)}...) custom-call(s32[1]{0:T(128)} %bitcast.here.refs_0_, ...), custom_call_target="tpu_custom_call" | custom-call | flops 1048576 | bytes 65536 | tf_op jit(solution)/shard_map/mlp/pallas_call | solution.py:218
  73.7 1.7 %collective-permute-start.18 = (bf16[1024,256]{1,0:T(8,128)(2,1)S(1)}, bf16[1024,256]{1,0:T(8,128)(2,1)S(1)}, u32[]{:S(2)}, u32[]{:S(2)}) collective-permute-start(bf16[1024,256]{1,0:T(8,128)(2,1)S(1)} %get-tuple-element.36.refs_0_), channel_id=1, source_target_pairs={{0,1},{1,0},{2,3},{3,2},{4,5},{5,4},{6,7},{7,6},{8,9},{9,8},{10,11... | collective-permute-start | bytes 1572872 | tf_op jit(solution)/shard_map/ppermute | solution.py:549
  75.5 10.1 %collective-permute-done.18.refs_0_.refs_1_ = bf16[1024,256]{1,0:T(8,128)(2,1)S(1)} collective-permute-done((bf16[1024,256]{1,0:T(8,128)(2,1)S(1)}, bf16[1024,256]{1,0:T(8,128)(2,1)S(1)}, u32[]{:S(2)}, u32[]{:S(2)}) %collective-permute-start.18) | collective-permute-done | bytes 524320 | tf_op jit(solution)/shard_map/ppermute | solution.py:549
  85.5 0.8 weight_grads.1
  86.4 0.6 collective-permute-start.23
  87.0 4.1 %collective-permute-start.20 = (bf16[1024,256]{1,0:T(8,128)(2,1)S(1)}, bf16[1024,256]{1,0:T(8,128)(2,1)S(1)}, u32[]{:S(2)}, u32[]{:S(2)}) collective-permute-start(bf16[1024,256]{1,0:T(8,128)(2,1)S(1)} %collective-permute-done.19.refs_1_.refs_2_), channel_id=1, source_target_pairs={{0,1},{1,0},{2,3},{3,2},{4,5},{5,4},{6,7},{7,6},{8,9},{9,8},{10,11... | collective-permute-start | bytes 1572872 | tf_op jit(solution)/shard_map/ppermute | solution.py:549
  91.0 9.8 %collective-permute-start.22 = (bf16[1024,256]{1,0:T(8,128)(2,1)S(1)}, bf16[1024,256]{1,0:T(8,128)(2,1)S(1)}, u32[]{:S(2)}, u32[]{:S(2)}) collective-permute-start(bf16[1024,256]{1,0:T(8,128)(2,1)S(1)} %collective-permute-done.21.refs_18_.refs_4_), channel_id=1, source_target_pairs={{0,1},{1,0},{2,3},{3,2},{4,5},{5,4},{6,7},{7,6},{8,9},{9,8},{10,11... | collective-permute-start | bytes 1572872 | tf_op jit(solution)/shard_map/ppermute | solution.py:549
  100.8 1.6 %collective-permute-start.24 = (f32[112,256]{1,0:T(8,128)S(1)}, f32[112,256]{1,0:T(8,128)S(1)}, u32[]{:S(2)}, u32[]{:S(2)}) collective-permute-start(f32[112,256]{1,0:T(8,128)S(1)} %sum_terms.19), channel_id=1, source_target_pairs={{0,16},{4,20},{8,24},{12,28},{16,0},{20,4},{24,8},{28,12},{1,17},{... | collective-permute-start | bytes 344072 | tf_op jit(solution)/shard_map/ppermute | solution.py:545
  102.4 1.6 %collective-permute-start.25 = (f32[112,256]{1,0:T(8,128)S(1)}, f32[112,256]{1,0:T(8,128)S(1)}, u32[]{:S(2)}, u32[]{:S(2)}) collective-permute-start(f32[112,256]{1,0:T(8,128)S(1)} %sum_terms.20), channel_id=1, source_target_pairs={{0,8},{4,12},{8,0},{12,4},{16,24},{20,28},{24,16},{28,20},{1,9},{5... | collective-permute-start | bytes 344072 | tf_op jit(solution)/shard_map/ppermute | solution.py:545
  104.0 0.5 collective-permute-start.26
  104.6 6.1 %tile_grads.2 = (bf16[128,128,128]{2,1,0:T(8,128)(2,1)}, f32[8,128]{1,0:T(8,128)S(1)}) custom-call(s32[1]{0:T(128)} %bitcast.here.refs_0_, s32[5,32]{1,0:T(8,128)S(1)} %pad_add_fusion.cols, bf16[1024,256]{1,0:T(8,128)(2,1)S(1)} %get-tuple-element.36.refs_0_, bf16[1024,256]{1,0:T(8,128)(2,1)S(1)} %collective-permute-done.18.refs_0_.refs_1_, ...), custom_call_target="tpu_custom_call" | custom-call | flops 1048576 | bytes 65536 | tf_op jit(solution)/shard_map/tile_grads/pallas_call | solution.py:517
  110.7 4.1 %collective-permute-done.22.refs_5_ = bf16[1024,256]{1,0:T(8,128)(2,1)S(1)} collective-permute-done((bf16[1024,256]{1,0:T(8,128)(2,1)S(1)}, bf16[1024,256]{1,0:T(8,128)(2,1)S(1)}, u32[]{:S(2)}, u32[]{:S(2)}) %collective-permute-start.22) | collective-permute-done | bytes 524320 | tf_op jit(solution)/shard_map/ppermute | solution.py:549
  114.8 6.7 %back_terms.1 = (bf16[2048,256]{1,0:T(8,128)(2,1)S(1)}, bf16[2048,256]{1,0:T(8,128)(2,1)S(1)}, bf16[4096,256]{1,0:T(8,128)(2,1)S(1)}) custom-call(s32[1]{0:T(128)} %bitcast.here.refs_0_, s32[5,32]{1,0:T(8,128)S(1)} %pad_add_fusion.cols, bf16[1024,256]{1,0:T(8,128)(2,1)S(1)} %get-tuple-element.36.refs_0_, ...), custom_call_target="tpu_custom_call" | custom-call | flops 1048576 | bytes 65536 | tf_op jit(solution)/shard_map/back_terms/pallas_call | solution.py:419
  121.5 0.5 collective-permute-start.27
  122.0 2.1 %collective-permute-done.28.refs_2_ = bf16[2048,256]{1,0:T(8,128)(2,1)S(1)} collective-permute-done((bf16[2048,256]{1,0:T(8,128)(2,1)S(1)}, bf16[2048,256]{1,0:T(8,128)(2,1)S(1)}, u32[]{:S(2)}, u32[]{:S(2)}) %collective-permute-start.28) | collective-permute-done | bytes 1048608 | tf_op jit(solution)/shard_map/ppermute | solution.py:545
  124.2 0.2 sum_terms.24.refs_23_.refs_4_
  124.3 1.1 collective-permute-start.30
  125.4 0.2 sum_terms.23.refs_22_.refs_3_
  125.6 0.6 collective-permute-start.29
  126.1 2.0 %collective-permute-start.33 = (bf16[112,256]{1,0:T(8,128)(2,1)S(1)}, bf16[112,256]{1,0:T(8,128)(2,1)S(1)}, u32[]{:S(2)}, u32[]{:S(2)}) collective-permute-start(bf16[112,256]{1,0:T(8,128)(2,1)S(1)} %sum_terms.28.refs_1_), channel_id=1, source_target_pairs={{0,1},{1,2},{2,3},{3,0},{4,5},{5,6},{6,7},{7,4},{8,9},{9,10},{10,1... | collective-permute-start | bytes 172040 | tf_op jit(solution)/shard_map/ppermute | solution.py:553
  128.1 1.6 %collective-permute-start.34 = (bf16[112,256]{1,0:T(8,128)(2,1)S(1)}, bf16[112,256]{1,0:T(8,128)(2,1)S(1)}, u32[]{:S(2)}, u32[]{:S(2)}) collective-permute-start(bf16[112,256]{1,0:T(8,128)(2,1)S(1)} %sum_terms.28.refs_1_), channel_id=1, source_target_pairs={{0,2},{1,3},{2,0},{3,1},{4,6},{5,7},{6,4},{7,5},{8,10},{9,11},{10,... | collective-permute-start | bytes 172040 | tf_op jit(solution)/shard_map/ppermute | solution.py:553
  129.7 2.8 %collective-permute-start.35 = (bf16[112,256]{1,0:T(8,128)(2,1)S(1)}, bf16[112,256]{1,0:T(8,128)(2,1)S(1)}, u32[]{:S(2)}, u32[]{:S(2)}) collective-permute-start(bf16[112,256]{1,0:T(8,128)(2,1)S(1)} %sum_terms.28.refs_1_), channel_id=1, source_target_pairs={{0,3},{1,0},{2,1},{3,2},{4,7},{5,4},{6,5},{7,6},{8,11},{9,8},{10,9... | collective-permute-start | bytes 172040 | tf_op jit(solution)/shard_map/ppermute | solution.py:553
  132.5 5.7 %tile_grads.3 = (bf16[128,128,128]{2,1,0:T(8,128)(2,1)}, f32[8,128]{1,0:T(8,128)S(1)}) custom-call(s32[1]{0:T(128)} %bitcast.here.refs_0_, s32[5,32]{1,0:T(8,128)S(1)} %pad_add_fusion.cols, bf16[1024,256]{1,0:T(8,128)(2,1)S(1)} %get-tuple-element.36.refs_0_, ...), custom_call_target="tpu_custom_call", output_to_operand_aliasing={{0}: (23, {})} | custom-call | flops 1048576 | bytes 65536 | tf_op jit(solution)/shard_map/tile_grads/pallas_call | solution.py:517
  138.3 1.2 collective-permute-start.38
  139.5 0.6 collective-permute-start.37
  140.1 1.7 %collective-permute-start.36 = (bf16[112,256]{1,0:T(8,128)(2,1)S(1)}, bf16[112,256]{1,0:T(8,128)(2,1)S(1)}, u32[]{:S(2)}, u32[]{:S(2)}) collective-permute-start(bf16[112,256]{1,0:T(8,128)(2,1)S(1)} %sum_terms.29), channel_id=1, source_target_pairs={{0,8},{4,12},{8,0},{12,4},{16,24},{20,28},{24,16},{28,20},{1,9},{5... | collective-permute-start | bytes 172040 | tf_op jit(solution)/shard_map/ppermute | solution.py:545
  141.9 0.1 sum_terms.25
  142.0 0.4 collective-permute-start.31
  142.3 0.1 sum_terms.26
  142.4 1.5 collective-permute-start.32
  143.9 0.8 collective-permute-done.37
  144.8 0.2 collective-permute-done.36
  145.1 1.5 collective-permute-done.39.odd
  146.6 1.0 weight_unpack.1
  147.5 1.4 collective-permute-done.31.refs_5_
  149.0 0.5 collective-permute-done.32.refs_6_
  149.5 1.2 sum_terms.27
  (64 shorter events, 0.7 us)
Async XLA Ops:
  0.6 18.9 %collective-permute-start = (bf16[1024,256]{1,0:T(8,128)(2,1)}, bf16[1024,256]{1,0:T(8,128)(2,1)S(1)}, u32[]{:S(2)}, u32[]{:S(2)}) collective-permute-start(bf16[1024,256]{1,0:T(8,128)(2,1)} %nodes.3), channel_id=1, source_target_pairs={{0,4},{4,0},{8,12},{12,8},{16,20},{20,16},{24,28},{28,24},{1,5},{5... | collective-permute-start | bytes 1572872 | tf_op jit(solution)/shard_map/ppermute | solution.py:545
  2.2 9.7 %collective-permute-start.1 = (bf16[512,256]{1,0:T(8,128)(2,1)S(1)}, bf16[512,256]{1,0:T(8,128)(2,1)S(1)}, u32[]{:S(2)}, u32[]{:S(2)}) collective-permute-start(bf16[512,256]{1,0:T(8,128)(2,1)S(1)} %get-tuple-element.57.refs_0_.refs_2_.refs_6_), channel_id=1, source_target_pairs={{0,8},{4,12},{8,0},{12,4},{16,24},{20,28},{24,16},{28,20},{1,9},{5... | collective-permute-start | bytes 786440 | tf_op jit(solution)/shard_map/ppermute | solution.py:545
  4.8 9.1 %collective-permute-start.5 = (bf16[512,256]{1,0:T(8,128)(2,1)S(1)}, bf16[512,256]{1,0:T(8,128)(2,1)S(1)}, u32[]{:S(2)}, u32[]{:S(2)}) collective-permute-start(bf16[512,256]{1,0:T(8,128)(2,1)S(1)} %get-tuple-element.57.refs_0_.refs_2_.refs_6_), channel_id=1, source_target_pairs={{0,16},{4,20},{8,24},{12,28},{16,0},{20,4},{24,8},{28,12},{1,17},{... | collective-permute-start | bytes 786440 | tf_op jit(solution)/shard_map/ppermute | solution.py:545
  6.3 11.3 %collective-permute-start.2 = (bf16[512,256]{1,0:T(8,128)(2,1)S(1)}, bf16[512,256]{1,0:T(8,128)(2,1)S(1)}, u32[]{:S(2)}, u32[]{:S(2)}) collective-permute-start(bf16[512,256]{1,0:T(8,128)(2,1)S(1)} %get-tuple-element.56.refs_1_.refs_3_.refs_7_), channel_id=1, source_target_pairs={{0,8},{4,12},{8,0},{12,4},{16,24},{20,28},{24,16},{28,20},{1,9},{5... | collective-permute-start | bytes 786440 | tf_op jit(solution)/shard_map/ppermute | solution.py:545
  6.8 12.7 %collective-permute-start.6 = (bf16[512,256]{1,0:T(8,128)(2,1)S(1)}, bf16[512,256]{1,0:T(8,128)(2,1)S(1)}, u32[]{:S(2)}, u32[]{:S(2)}) collective-permute-start(bf16[512,256]{1,0:T(8,128)(2,1)S(1)} %get-tuple-element.56.refs_1_.refs_3_.refs_7_), channel_id=1, source_target_pairs={{0,16},{4,20},{8,24},{12,28},{16,0},{20,4},{24,8},{28,12},{1,17},{... | collective-permute-start | bytes 786440 | tf_op jit(solution)/shard_map/ppermute | solution.py:545
  11.9 8.1 %collective-permute-start.3 = (bf16[512,256]{1,0:T(8,128)(2,1)S(1)}, bf16[512,256]{1,0:T(8,128)(2,1)S(1)}, u32[]{:S(2)}, u32[]{:S(2)}) collective-permute-start(bf16[512,256]{1,0:T(8,128)(2,1)S(1)} %collective-permute-done.1.refs_3_.refs_5_.refs_9_), channel_id=1, source_target_pairs={{0,4},{4,0},{8,12},{12,8},{16,20},{20,16},{24,28},{28,24},{1,5},{5... | collective-permute-start | bytes 786440 | tf_op jit(solution)/shard_map/ppermute | solution.py:545
  13.9 9.1 %collective-permute-start.9 = (bf16[512,256]{1,0:T(8,128)(2,1)S(1)}, bf16[512,256]{1,0:T(8,128)(2,1)S(1)}, u32[]{:S(2)}, u32[]{:S(2)}) collective-permute-start(bf16[512,256]{1,0:T(8,128)(2,1)S(1)} %collective-permute-done.5.refs_7_.refs_9_.refs_13_), channel_id=1, source_target_pairs={{0,8},{4,12},{8,0},{12,4},{16,24},{20,28},{24,16},{28,20},{1,9},{5... | collective-permute-start | bytes 786440 | tf_op jit(solution)/shard_map/ppermute | solution.py:545
  17.6 7.9 %collective-permute-start.10 = (bf16[512,256]{1,0:T(8,128)(2,1)S(1)}, bf16[512,256]{1,0:T(8,128)(2,1)S(1)}, u32[]{:S(2)}, u32[]{:S(2)}) collective-permute-start(bf16[512,256]{1,0:T(8,128)(2,1)S(1)} %collective-permute-done.2.refs_4_.refs_6_.refs_10_), channel_id=1, source_target_pairs={{0,16},{4,20},{8,24},{12,28},{16,0},{20,4},{24,8},{28,12},{1,17},{... | collective-permute-start | bytes 786440 | tf_op jit(solution)/shard_map/ppermute | solution.py:545
  19.5 6.7 %collective-permute-start.4 = (bf16[512,256]{1,0:T(8,128)(2,1)S(1)}, bf16[512,256]{1,0:T(8,128)(2,1)S(1)}, u32[]{:S(2)}, u32[]{:S(2)}) collective-permute-start(bf16[512,256]{1,0:T(8,128)(2,1)S(1)} %collective-permute-done.2.refs_4_.refs_6_.refs_10_), channel_id=1, source_target_pairs={{0,4},{4,0},{8,12},{12,8},{16,20},{20,16},{24,28},{28,24},{1,5},{5... | collective-permute-start | bytes 786440 | tf_op jit(solution)/shard_map/ppermute | solution.py:545
  19.5 6.7 %collective-permute-start.7 = (bf16[512,256]{1,0:T(8,128)(2,1)S(1)}, bf16[512,256]{1,0:T(8,128)(2,1)}, u32[]{:S(2)}, u32[]{:S(2)}) collective-permute-start(bf16[512,256]{1,0:T(8,128)(2,1)S(1)} %collective-permute-done.5.refs_7_.refs_9_.refs_13_), channel_id=1, source_target_pairs={{0,4},{4,0},{8,12},{12,8},{16,20},{20,16},{24,28},{28,24},{1,5},{5... | collective-permute-start | bytes 786440 | tf_op jit(solution)/shard_map/ppermute | solution.py:545
  20.1 6.2 %collective-permute-start.8 = (bf16[512,256]{1,0:T(8,128)(2,1)S(1)}, bf16[512,256]{1,0:T(8,128)(2,1)}, u32[]{:S(2)}, u32[]{:S(2)}) collective-permute-start(bf16[512,256]{1,0:T(8,128)(2,1)S(1)} %collective-permute-done.6.refs_8_.refs_10_.refs_14_), channel_id=1, source_target_pairs={{0,4},{4,0},{8,12},{12,8},{16,20},{20,16},{24,28},{28,24},{1,5},{5... | collective-permute-start | bytes 786440 | tf_op jit(solution)/shard_map/ppermute | solution.py:545
  23.0 3.3 %collective-permute-start.11 = (bf16[512,256]{1,0:T(8,128)(2,1)S(1)}, bf16[512,256]{1,0:T(8,128)(2,1)}, u32[]{:S(2)}, u32[]{:S(2)}) collective-permute-start(bf16[512,256]{1,0:T(8,128)(2,1)S(1)} %collective-permute-done.9.refs_11_.refs_13_.refs_17_), channel_id=1, source_target_pairs={{0,4},{4,0},{8,12},{12,8},{16,20},{20,16},{24,28},{28,24},{1,5},{5... | collective-permute-start | bytes 786440 | tf_op jit(solution)/shard_map/ppermute | solution.py:545
  25.5 1.7 %collective-permute-start.12 = (bf16[512,256]{1,0:T(8,128)(2,1)S(1)}, bf16[512,256]{1,0:T(8,128)(2,1)}, u32[]{:S(2)}, u32[]{:S(2)}) collective-permute-start(bf16[512,256]{1,0:T(8,128)(2,1)S(1)} %collective-permute-done.10.refs_12_.refs_14_.refs_18_), channel_id=1, source_target_pairs={{0,4},{4,0},{8,12},{12,8},{16,20},{20,16},{24,28},{28,24},{1,5},{5... | collective-permute-start | bytes 786440 | tf_op jit(solution)/shard_map/ppermute | solution.py:545
  26.2 4.5 %copy-start.1 = (bf16[512,256]{1,0:T(8,128)(2,1)}, bf16[512,256]{1,0:T(8,128)(2,1)S(1)}, u32[]{:S(2)}) copy-start(bf16[512,256]{1,0:T(8,128)(2,1)S(1)} %collective-permute-done.4.refs_6_.refs_8_.refs_12_) | copy-start | bytes 786436
  27.2 5.2 %copy-start = (bf16[32,1,4,128,128]{4,3,2,1,0:T(8,128)(2,1)S(1)}, bf16[32,1,4,128,128]{4,3,2,1,0:T(8,128)(2,1)}, u32[]{:S(2)}) copy-start(bf16[32,1,4,128,128]{4,3,2,1,0:T(8,128)(2,1)} %param.11) | copy-start | bytes 12582916
  30.7 14.8 %collective-permute-start.13 = (bf16[1024,256]{1,0:T(8,128)(2,1)S(1)}, bf16[1024,256]{1,0:T(8,128)(2,1)S(1)}, u32[]{:S(2)}, u32[]{:S(2)}) collective-permute-start(bf16[1024,256]{1,0:T(8,128)(2,1)S(1)} %partial_messages.4.refs_1_), channel_id=1, source_target_pairs={{0,1},{1,0},{2,3},{3,2},{4,5},{5,4},{6,7},{7,6},{8,9},{9,8},{10,11... | collective-permute-start | bytes 1572872 | tf_op jit(solution)/shard_map/ppermute | solution.py:549
  32.4 3.0 %copy-start.2 = (bf16[512,256]{1,0:T(8,128)(2,1)S(1)}, bf16[512,256]{1,0:T(8,128)(2,1)}, u32[]{:S(2)}) copy-start(bf16[512,256]{1,0:T(8,128)(2,1)} %copy-done.1) | copy-start | bytes 786436
  38.5 17.4 %collective-permute-start.16 = (bf16[1024,256]{1,0:T(8,128)(2,1)S(1)}, bf16[1024,256]{1,0:T(8,128)(2,1)S(1)}, u32[]{:S(2)}, u32[]{:S(2)}) collective-permute-start(bf16[1024,256]{1,0:T(8,128)(2,1)S(1)} %partial_messages.5.refs_1_), channel_id=1, source_target_pairs={{0,1},{1,0},{2,3},{3,2},{4,5},{5,4},{6,7},{7,6},{8,9},{9,8},{10,11... | collective-permute-start | bytes 1572872 | tf_op jit(solution)/shard_map/ppermute | solution.py:549
  45.7 25.1 %copy-start.3 = (bf16[1024,256]{1,0:T(8,128)(2,1)S(1)}, bf16[1024,256]{1,0:T(8,128)(2,1)}, u32[]{:S(2)}) copy-start(bf16[1024,256]{1,0:T(8,128)(2,1)} %nodes.3) | copy-start | bytes 1572868
  45.7 25.1 %copy-start.4 = (bf16[1024,256]{1,0:T(8,128)(2,1)S(1)}, bf16[1024,256]{1,0:T(8,128)(2,1)}, u32[]{:S(2)}) copy-start(bf16[1024,256]{1,0:T(8,128)(2,1)} %cot.3) | copy-start | bytes 1572868
  45.7 25.1 %copy-start.5 = (bf16[512,256]{1,0:T(8,128)(2,1)S(1)}, bf16[512,256]{1,0:T(8,128)(2,1)}, u32[]{:S(2)}) copy-start(bf16[512,256]{1,0:T(8,128)(2,1)} %w_in.1) | copy-start | bytes 786436
  45.7 25.1 %copy-start.6 = (bf16[256,256]{1,0:T(8,128)(2,1)S(1)}, bf16[256,256]{1,0:T(8,128)(2,1)}, u32[]{:S(2)}) copy-start(bf16[256,256]{1,0:T(8,128)(2,1)} %refs_5_.1) | copy-start | bytes 393220
  45.7 25.1 %copy-start.7 = (f32[256]{0:T(256)S(1)}, f32[256]{0:T(256)}, u32[]{:S(2)}) copy-start(f32[256]{0:T(256)} %param.15) | copy-start | bytes 3076
  45.7 25.1 %copy-start.8 = (f32[256]{0:T(256)S(1)}, f32[256]{0:T(256)}, u32[]{:S(2)}) copy-start(f32[256]{0:T(256)} %param.17) | copy-start | bytes 3076
  45.7 25.1 %copy-start.9 = (f32[256]{0:T(256)S(1)}, f32[256]{0:T(256)}, u32[]{:S(2)}) copy-start(f32[256]{0:T(256)} %param.18) | copy-start | bytes 3076
  45.7 10.4 %collective-permute-start.14 = (bf16[1024,256]{1,0:T(8,128)(2,1)S(1)}, bf16[1024,256]{1,0:T(8,128)(2,1)S(1)}, u32[]{:S(2)}, u32[]{:S(2)}) collective-permute-start(bf16[1024,256]{1,0:T(8,128)(2,1)S(1)} %sum_terms.15), channel_id=1, source_target_pairs={{0,4},{1,2},{2,1},{3,7},{4,0},{5,6},{6,5},{7,3},{8,12},{9,10},{10,... | collective-permute-start | bytes 1572872 | tf_op jit(solution)/shard_map/ppermute | solution.py:562
  56.1 4.0 %collective-permute-start.17 = (bf16[1024,256]{1,0:T(8,128)(2,1)S(1)}, bf16[1024,256]{1,0:T(8,128)(2,1)S(1)}, u32[]{:S(2)}, u32[]{:S(2)}) collective-permute-start(bf16[1024,256]{1,0:T(8,128)(2,1)S(1)} %sum_terms.17), channel_id=1, source_target_pairs={{0,4},{1,2},{2,1},{3,7},{4,0},{5,6},{6,5},{7,3},{8,12},{9,10},{10,... | collective-permute-start | bytes 1572872 | tf_op jit(solution)/shard_map/ppermute | solution.py:562
  56.4 14.4 %collective-permute-start.15 = (bf16[1024,256]{1,0:T(8,128)(2,1)S(1)}, bf16[1024,256]{1,0:T(8,128)(2,1)S(1)}, u32[]{:S(2)}, u32[]{:S(2)}) collective-permute-start(bf16[1024,256]{1,0:T(8,128)(2,1)S(1)} %sum_terms.16), channel_id=1, source_target_pairs={{0,1},{1,0},{2,3},{3,2},{4,5},{5,4},{6,7},{7,6},{8,9},{9,8},{10,11... | collective-permute-start | bytes 1572872 | tf_op jit(solution)/shard_map/ppermute | solution.py:549
  73.7 11.8 %collective-permute-start.18 = (bf16[1024,256]{1,0:T(8,128)(2,1)S(1)}, bf16[1024,256]{1,0:T(8,128)(2,1)S(1)}, u32[]{:S(2)}, u32[]{:S(2)}) collective-permute-start(bf16[1024,256]{1,0:T(8,128)(2,1)S(1)} %get-tuple-element.36.refs_0_), channel_id=1, source_target_pairs={{0,1},{1,0},{2,3},{3,2},{4,5},{5,4},{6,7},{7,6},{8,9},{9,8},{10,11... | collective-permute-start | bytes 1572872 | tf_op jit(solution)/shard_map/ppermute | solution.py:549
  75.5 10.1 %collective-permute-start.19 = (bf16[1024,256]{1,0:T(8,128)(2,1)S(1)}, bf16[1024,256]{1,0:T(8,128)(2,1)S(1)}, u32[]{:S(2)}, u32[]{:S(2)}) collective-permute-start(bf16[1024,256]{1,0:T(8,128)(2,1)S(1)} %get-tuple-element.36.refs_0_), channel_id=1, source_target_pairs={{0,4},{1,2},{2,1},{3,7},{4,0},{5,6},{6,5},{7,3},{8,12},{9,10},{10,... | collective-permute-start | bytes 1572872 | tf_op jit(solution)/shard_map/ppermute | solution.py:562
  85.5 5.5 %collective-permute-start.21 = (bf16[1024,256]{1,0:T(8,128)(2,1)S(1)}, bf16[1024,256]{1,0:T(8,128)(2,1)S(1)}, u32[]{:S(2)}, u32[]{:S(2)}) collective-permute-start(bf16[1024,256]{1,0:T(8,128)(2,1)S(1)} %collective-permute-done.18.refs_0_.refs_1_), channel_id=1, source_target_pairs={{0,4},{1,2},{2,1},{3,7},{4,0},{5,6},{6,5},{7,3},{8,12},{9,10},{10,... | collective-permute-start | bytes 1572872 | tf_op jit(solution)/shard_map/ppermute | solution.py:562
  86.4 14.4 %collective-permute-start.23 = (f32[448,256]{1,0:T(8,128)S(1)}, f32[448,256]{1,0:T(8,128)S(1)}, u32[]{:S(2)}, u32[]{:S(2)}) collective-permute-start(f32[448,256]{1,0:T(8,128)S(1)} %get-tuple-element.39), channel_id=1, source_target_pairs={{0,4},{4,0},{8,12},{12,8},{16,20},{20,16},{24,28},{28,24},{1,5},{5... | collective-permute-start | bytes 1376264 | tf_op jit(solution)/shard_map/ppermute | solution.py:545
  87.0 17.6 %collective-permute-start.20 = (bf16[1024,256]{1,0:T(8,128)(2,1)S(1)}, bf16[1024,256]{1,0:T(8,128)(2,1)S(1)}, u32[]{:S(2)}, u32[]{:S(2)}) collective-permute-start(bf16[1024,256]{1,0:T(8,128)(2,1)S(1)} %collective-permute-done.19.refs_1_.refs_2_), channel_id=1, source_target_pairs={{0,1},{1,0},{2,3},{3,2},{4,5},{5,4},{6,7},{7,6},{8,9},{9,8},{10,11... | collective-permute-start | bytes 1572872 | tf_op jit(solution)/shard_map/ppermute | solution.py:549
  91.0 23.7 %collective-permute-start.22 = (bf16[1024,256]{1,0:T(8,128)(2,1)S(1)}, bf16[1024,256]{1,0:T(8,128)(2,1)S(1)}, u32[]{:S(2)}, u32[]{:S(2)}) collective-permute-start(bf16[1024,256]{1,0:T(8,128)(2,1)S(1)} %collective-permute-done.21.refs_18_.refs_4_), channel_id=1, source_target_pairs={{0,1},{1,0},{2,3},{3,2},{4,5},{5,4},{6,7},{7,6},{8,9},{9,8},{10,11... | collective-permute-start | bytes 1572872 | tf_op jit(solution)/shard_map/ppermute | solution.py:549
  100.8 9.9 %collective-permute-start.24 = (f32[112,256]{1,0:T(8,128)S(1)}, f32[112,256]{1,0:T(8,128)S(1)}, u32[]{:S(2)}, u32[]{:S(2)}) collective-permute-start(f32[112,256]{1,0:T(8,128)S(1)} %sum_terms.19), channel_id=1, source_target_pairs={{0,16},{4,20},{8,24},{12,28},{16,0},{20,4},{24,8},{28,12},{1,17},{... | collective-permute-start | bytes 344072 | tf_op jit(solution)/shard_map/ppermute | solution.py:545
  102.4 8.2 %collective-permute-start.25 = (f32[112,256]{1,0:T(8,128)S(1)}, f32[112,256]{1,0:T(8,128)S(1)}, u32[]{:S(2)}, u32[]{:S(2)}) collective-permute-start(f32[112,256]{1,0:T(8,128)S(1)} %sum_terms.20), channel_id=1, source_target_pairs={{0,8},{4,12},{8,0},{12,4},{16,24},{20,28},{24,16},{28,20},{1,9},{5... | collective-permute-start | bytes 344072 | tf_op jit(solution)/shard_map/ppermute | solution.py:545
  104.0 6.7 %collective-permute-start.26 = (f32[112,256]{1,0:T(8,128)S(1)}, f32[112,256]{1,0:T(8,128)S(1)}, u32[]{:S(2)}, u32[]{:S(2)}) collective-permute-start(f32[112,256]{1,0:T(8,128)S(1)} %sum_terms.21), channel_id=1, source_target_pairs={{0,24},{4,28},{8,16},{12,20},{16,8},{20,12},{24,0},{28,4},{1,25},{... | collective-permute-start | bytes 344072 | tf_op jit(solution)/shard_map/ppermute | solution.py:545
  121.4 2.7 %collective-permute-start.28 = (bf16[2048,256]{1,0:T(8,128)(2,1)S(1)}, bf16[2048,256]{1,0:T(8,128)(2,1)S(1)}, u32[]{:S(2)}, u32[]{:S(2)}) collective-permute-start(bf16[2048,256]{1,0:T(8,128)(2,1)S(1)} %get-tuple-element.43), channel_id=1, source_target_pairs={{0,4},{4,0},{8,12},{12,8},{16,20},{20,16},{24,28},{28,24},{1,5},{5... | collective-permute-start | bytes 3145736 | tf_op jit(solution)/shard_map/ppermute | solution.py:545
  121.5 4.6 %collective-permute-start.27 = (bf16[2048,256]{1,0:T(8,128)(2,1)S(1)}, bf16[2048,256]{1,0:T(8,128)(2,1)S(1)}, u32[]{:S(2)}, u32[]{:S(2)}) collective-permute-start(bf16[2048,256]{1,0:T(8,128)(2,1)S(1)} %get-tuple-element.42), channel_id=1, source_target_pairs={{0,4},{4,0},{8,12},{12,8},{16,20},{20,16},{24,28},{28,24},{1,5},{5... | collective-permute-start | bytes 3145736 | tf_op jit(solution)/shard_map/ppermute | solution.py:545
  124.3 17.5 %collective-permute-start.30 = (bf16[1024,256]{1,0:T(8,128)(2,1)S(1)}, bf16[1024,256]{1,0:T(8,128)(2,1)S(1)}, u32[]{:S(2)}, u32[]{:S(2)}) collective-permute-start(bf16[1024,256]{1,0:T(8,128)(2,1)S(1)} %sum_terms.24.refs_23_.refs_4_), channel_id=1, source_target_pairs={{0,16},{4,20},{8,24},{12,28},{16,0},{20,4},{24,8},{28,12},{1,17},{... | collective-permute-start | bytes 1572872 | tf_op jit(solution)/shard_map/ppermute | solution.py:545
  125.6 16.8 %collective-permute-start.29 = (bf16[1024,256]{1,0:T(8,128)(2,1)S(1)}, bf16[1024,256]{1,0:T(8,128)(2,1)S(1)}, u32[]{:S(2)}, u32[]{:S(2)}) collective-permute-start(bf16[1024,256]{1,0:T(8,128)(2,1)S(1)} %sum_terms.23.refs_22_.refs_3_), channel_id=1, source_target_pairs={{0,8},{4,12},{8,0},{12,4},{16,24},{20,28},{24,16},{28,20},{1,9},{5... | collective-permute-start | bytes 1572872 | tf_op jit(solution)/shard_map/ppermute | solution.py:545
  126.1 12.1 %collective-permute-start.33 = (bf16[112,256]{1,0:T(8,128)(2,1)S(1)}, bf16[112,256]{1,0:T(8,128)(2,1)S(1)}, u32[]{:S(2)}, u32[]{:S(2)}) collective-permute-start(bf16[112,256]{1,0:T(8,128)(2,1)S(1)} %sum_terms.28.refs_1_), channel_id=1, source_target_pairs={{0,1},{1,2},{2,3},{3,0},{4,5},{5,6},{6,7},{7,4},{8,9},{9,10},{10,1... | collective-permute-start | bytes 172040 | tf_op jit(solution)/shard_map/ppermute | solution.py:553
  128.1 10.1 %collective-permute-start.34 = (bf16[112,256]{1,0:T(8,128)(2,1)S(1)}, bf16[112,256]{1,0:T(8,128)(2,1)S(1)}, u32[]{:S(2)}, u32[]{:S(2)}) collective-permute-start(bf16[112,256]{1,0:T(8,128)(2,1)S(1)} %sum_terms.28.refs_1_), channel_id=1, source_target_pairs={{0,2},{1,3},{2,0},{3,1},{4,6},{5,7},{6,4},{7,5},{8,10},{9,11},{10,... | collective-permute-start | bytes 172040 | tf_op jit(solution)/shard_map/ppermute | solution.py:553
  129.7 8.6 %collective-permute-start.35 = (bf16[112,256]{1,0:T(8,128)(2,1)S(1)}, bf16[112,256]{1,0:T(8,128)(2,1)S(1)}, u32[]{:S(2)}, u32[]{:S(2)}) collective-permute-start(bf16[112,256]{1,0:T(8,128)(2,1)S(1)} %sum_terms.28.refs_1_), channel_id=1, source_target_pairs={{0,3},{1,0},{2,1},{3,2},{4,7},{5,4},{6,5},{7,6},{8,11},{9,8},{10,9... | collective-permute-start | bytes 172040 | tf_op jit(solution)/shard_map/ppermute | solution.py:553
  138.3 5.6 %collective-permute-start.38 = (bf16[112,256]{1,0:T(8,128)(2,1)S(1)}, bf16[112,256]{1,0:T(8,128)(2,1)S(1)}, u32[]{:S(2)}, u32[]{:S(2)}) collective-permute-start(bf16[112,256]{1,0:T(8,128)(2,1)S(1)} %sum_terms.29), channel_id=1, source_target_pairs={{0,24},{4,28},{8,16},{12,20},{16,8},{20,12},{24,0},{28,4},{1,25},{... | collective-permute-start | bytes 172040 | tf_op jit(solution)/shard_map/ppermute | solution.py:545
  139.5 5.2 %collective-permute-start.37 = (bf16[112,256]{1,0:T(8,128)(2,1)S(1)}, bf16[112,256]{1,0:T(8,128)(2,1)S(1)}, u32[]{:S(2)}, u32[]{:S(2)}) collective-permute-start(bf16[112,256]{1,0:T(8,128)(2,1)S(1)} %sum_terms.29), channel_id=1, source_target_pairs={{0,16},{4,20},{8,24},{12,28},{16,0},{20,4},{24,8},{28,12},{1,17},{... | collective-permute-start | bytes 172040 | tf_op jit(solution)/shard_map/ppermute | solution.py:545
  140.1 4.9 %collective-permute-start.36 = (bf16[112,256]{1,0:T(8,128)(2,1)S(1)}, bf16[112,256]{1,0:T(8,128)(2,1)S(1)}, u32[]{:S(2)}, u32[]{:S(2)}) collective-permute-start(bf16[112,256]{1,0:T(8,128)(2,1)S(1)} %sum_terms.29), channel_id=1, source_target_pairs={{0,8},{4,12},{8,0},{12,4},{16,24},{20,28},{24,16},{28,20},{1,9},{5... | collective-permute-start | bytes 172040 | tf_op jit(solution)/shard_map/ppermute | solution.py:545
  142.0 7.0 %collective-permute-start.31 = (bf16[512,256]{1,0:T(8,128)(2,1)S(1)}, bf16[512,256]{1,0:T(8,128)(2,1)S(1)}, u32[]{:S(2)}, u32[]{:S(2)}) collective-permute-start(bf16[512,256]{1,0:T(8,128)(2,1)S(1)} %sum_terms.25), channel_id=1, source_target_pairs={{0,8},{4,12},{8,0},{12,4},{16,24},{20,28},{24,16},{28,20},{1,9},{5... | collective-permute-start | bytes 786440 | tf_op jit(solution)/shard_map/ppermute | solution.py:545
  142.4 7.1 %collective-permute-start.32 = (bf16[512,256]{1,0:T(8,128)(2,1)S(1)}, bf16[512,256]{1,0:T(8,128)(2,1)S(1)}, u32[]{:S(2)}, u32[]{:S(2)}) collective-permute-start(bf16[512,256]{1,0:T(8,128)(2,1)S(1)} %sum_terms.26), channel_id=1, source_target_pairs={{0,16},{4,20},{8,24},{12,28},{16,0},{20,4},{24,8},{28,12},{1,17},{... | collective-permute-start | bytes 786440 | tf_op jit(solution)/shard_map/ppermute | solution.py:545
  145.0 1.6 %collective-permute-start.39 = (bf16[448,256]{1,0:T(8,128)(2,1)S(1)}, bf16[448,256]{1,0:T(8,128)(2,1)S(1)}, u32[]{:S(2)}, u32[]{:S(2)}) collective-permute-start(bf16[448,256]{1,0:T(8,128)(2,1)S(1)} %pad_maximum_fusion.even), channel_id=1, source_target_pairs={{0,4},{4,0},{8,12},{12,8},{16,20},{20,16},{24,28},{28,24},{1,5},{5... | collective-permute-start | bytes 688136 | tf_op jit(solution)/shard_map/ppermute | solution.py:545

commit v16 on v15

--- a/solution.py
+++ b/solution.py
@@ -702,7 +702,7 @@
         grads = [gather_line(gmsgs[0])]
         kept, sent, direct = weight_call(factor, n_row, *weight_args, (grads[0][1], grads[0][2]))
         near_grads, token = tile_grad_call(
-            *known, [grads[0][:2]], pieces, tile_local.shape, rows, (3, 2), after=(grads[0][3], grads[0][4])
+            *known, [grads[0][:4]], pieces, tile_local.shape, rows, (3, 2, 1), after=(grads[0][4],)
         )
         row_weights = scatter_weights(here, kept, sent, (token,))
         urgent, rest, even = back_call(
@@ -711,7 +711,7 @@
         urgent, rest = swap(urgent, 1), swap(rest, 1)
         arrived, first = reduce_square(here, even, urgent, rest, rows)
         grad_tiles, token = tile_grad_call(
-            *known, grads, pieces, tile_local.shape, rows, (1, 0), near_grads, first
+            *known, grads, pieces, tile_local.shape, rows, (0,), near_grads, first
         )
         row_weights = sum_call(here, row_weights.shape[0], [(row_weights, 0)], after=(rest, *first))
         all_weights = level_weights(here, row_weights, (token,))

time: 151 us -> 149 us (0.987)
  Pallas kernels: 38.8 us -> 36.8 us
  transfers between devices with their start and end apart: 40 -> 40, of which waited for: 17 -> 16; matrix products, arithmetic and copies ran while one was open for 1% -> 1% of each run, Pallas kernels for 16% -> 16%
where the time goes in v16:
time: 149 us; the launch traced here: 148 us
  waiting for transfers between devices  61.8 us (41%)
  starting transfers between devices  46.7 us (31%)
  Pallas kernels  36.8 us (25%)
    ppermute x6, waiting for transfers between devices, outer_swap(): return lax.ppermute(value, 'col', [(0, 1), (1, 0), (2, 3), (3, 2)])  37.6 us
    ppermute x27, waiting for transfers between devices, swap(): return lax.ppermute(value, 'row', [(i, i ^ bit) for i in range(8)])  24.2 us
    ppermute x6, starting transfers between devices, outer_swap(): return lax.ppermute(value, 'col', [(0, 1), (1, 0), (2, 3), (3, 2)])  20.9 us
    ppermute x27, starting transfers between devices, swap(): return lax.ppermute(value, 'row', [(i, i ^ bit) for i in range(8)])  20 us
    pallas_call x2, Pallas kernels, tile_grad_call(): pl.pallas_call(functools.partial(tile_grad_kernel, rows, slots, len(grads...  11 us
    pallas_call x3, Pallas kernels, forward_call(): pl.pallas_call(functools.partial(forward_kernel, outputs, len(pieces), pa...  10.4 us
    pallas_call x1, Pallas kernels, back_call(): pl.pallas_call(functools.partial(back_kernel, rows, slots, len(grads), le...  5.81 us
    ppermute x3, starting transfers between devices, turn(): return lax.ppermute(value, 'col', [(i, (i + by) % 4) for i in range(4)])  5.61 us
  transfers between devices with their start and end apart: 40, of which 16 were waited for; matrix products, arithmetic and copies ran while one was open for 1% of the time, Pallas kernels for 16%

profile of v16, /device:TPU:0, one launch (start us, length us, event | category | flops | bytes accessed | tf_op | source)
XLA Modules:
  0.0 148.2 jit_solution(17837952939825424688)
XLA Ops:
  0.6 0.5 collective-permute-start
  1.1 1.1 fusion
  2.2 2.6 %collective-permute-start.1 = (bf16[512,256]{1,0:T(8,128)(2,1)S(1)}, bf16[512,256]{1,0:T(8,128)(2,1)S(1)}, u32[]{:S(2)}, u32[]{:S(2)}) collective-permute-start(bf16[512,256]{1,0:T(8,128)(2,1)S(1)} %get-tuple-element.57.refs_0_.refs_4_.refs_6_), channel_id=1, source_target_pairs={{0,8},{4,12},{8,0},{12,4},{16,24},{20,28},{24,16},{28,20},{1,9},{5... | collective-permute-start | bytes 786440 | tf_op jit(solution)/shard_map/ppermute | solution.py:545
  4.8 1.5 %collective-permute-start.5 = (bf16[512,256]{1,0:T(8,128)(2,1)S(1)}, bf16[512,256]{1,0:T(8,128)(2,1)S(1)}, u32[]{:S(2)}, u32[]{:S(2)}) collective-permute-start(bf16[512,256]{1,0:T(8,128)(2,1)S(1)} %get-tuple-element.57.refs_0_.refs_4_.refs_6_), channel_id=1, source_target_pairs={{0,16},{4,20},{8,24},{12,28},{16,0},{20,4},{24,8},{28,12},{1,17},{... | collective-permute-start | bytes 786440 | tf_op jit(solution)/shard_map/ppermute | solution.py:545
  6.3 0.5 collective-permute-start.2
  6.9 5.1 %collective-permute-done.1.refs_3_.refs_7_.refs_9_ = bf16[512,256]{1,0:T(8,128)(2,1)S(1)} collective-permute-done((bf16[512,256]{1,0:T(8,128)(2,1)S(1)}, bf16[512,256]{1,0:T(8,128)(2,1)S(1)}, u32[]{:S(2)}, u32[]{:S(2)}) %collective-permute-start.1) | collective-permute-done | bytes 262176 | tf_op jit(solution)/shard_map/ppermute | solution.py:545
  11.9 2.0 %collective-permute-done.5.refs_7_.refs_11_.refs_13_ = bf16[512,256]{1,0:T(8,128)(2,1)S(1)} collective-permute-done((bf16[512,256]{1,0:T(8,128)(2,1)S(1)}, bf16[512,256]{1,0:T(8,128)(2,1)S(1)}, u32[]{:S(2)}, u32[]{:S(2)}) %collective-permute-start.5) | collective-permute-done | bytes 262176 | tf_op jit(solution)/shard_map/ppermute | solution.py:545
  14.0 3.6 %collective-permute-done.2.refs_4_.refs_8_.refs_10_ = bf16[512,256]{1,0:T(8,128)(2,1)S(1)} collective-permute-done((bf16[512,256]{1,0:T(8,128)(2,1)S(1)}, bf16[512,256]{1,0:T(8,128)(2,1)S(1)}, u32[]{:S(2)}, u32[]{:S(2)}) %collective-permute-start.2) | collective-permute-done | bytes 262176 | tf_op jit(solution)/shard_map/ppermute | solution.py:545
  17.6 2.0 %collective-permute-start.10 = (bf16[512,256]{1,0:T(8,128)(2,1)S(1)}, bf16[512,256]{1,0:T(8,128)(2,1)S(1)}, u32[]{:S(2)}, u32[]{:S(2)}) collective-permute-start(bf16[512,256]{1,0:T(8,128)(2,1)S(1)} %collective-permute-done.2.refs_4_.refs_8_.refs_10_), channel_id=1, source_target_pairs={{0,16},{4,20},{8,24},{12,28},{16,0},{20,4},{24,8},{28,12},{1,17},{... | collective-permute-start | bytes 786440 | tf_op jit(solution)/shard_map/ppermute | solution.py:545
  19.5 0.5 collective-permute-start.7
  20.1 2.9 %collective-permute-done.9.refs_11_.refs_15_.refs_17_ = bf16[512,256]{1,0:T(8,128)(2,1)S(1)} collective-permute-done((bf16[512,256]{1,0:T(8,128)(2,1)S(1)}, bf16[512,256]{1,0:T(8,128)(2,1)S(1)}, u32[]{:S(2)}, u32[]{:S(2)}) %collective-permute-start.9) | collective-permute-done | bytes 262176 | tf_op jit(solution)/shard_map/ppermute | solution.py:545
  23.0 2.5 %collective-permute-done.10.refs_12_.refs_16_.refs_18_ = bf16[512,256]{1,0:T(8,128)(2,1)S(1)} collective-permute-done((bf16[512,256]{1,0:T(8,128)(2,1)S(1)}, bf16[512,256]{1,0:T(8,128)(2,1)S(1)}, u32[]{:S(2)}, u32[]{:S(2)}) %collective-permute-start.10) | collective-permute-done | bytes 262176 | tf_op jit(solution)/shard_map/ppermute | solution.py:545
  25.5 0.7 pad_add_fusion.cols
  26.2 0.9 collective-permute-done.12.refs_14_.refs_18_.refs_20_
  27.2 3.5 %partial_messages.4.refs_1_ = bf16[1024,256]{1,0:T(8,128)(2,1)S(1)} custom-call(s32[1]{0:T(128)} %bitcast.here.refs_0_, s32[5,32]{1,0:T(8,128)S(1)} %pad_add_fusion.cols, bf16[512,256]{1,0:T(8,128)(2,1)S(1)} %get-tuple-element.57.refs_0_.refs_4_.refs_6_, bf16[512,256]{1,0:T(8,128)(2,1)S(1)} %get-tuple-element.56.refs_1_.refs_5_.refs_7_, ...), custom_call_target="tpu_custom_call" | custom-call | flops 1048576 | bytes 65536 | tf_op jit(solution)/shard_map/partial_messages/pallas_call | solution.py:132
  30.7 1.7 %collective-permute-start.13 = (bf16[1024,256]{1,0:T(8,128)(2,1)S(1)}, bf16[1024,256]{1,0:T(8,128)(2,1)S(1)}, u32[]{:S(2)}, u32[]{:S(2)}) collective-permute-start(bf16[1024,256]{1,0:T(8,128)(2,1)S(1)} %partial_messages.4.refs_1_), channel_id=1, source_target_pairs={{0,1},{1,0},{2,3},{3,2},{4,5},{5,4},{6,7},{7,6},{8,9},{9,8},{10,11... | collective-permute-start | bytes 1572872 | tf_op jit(solution)/shard_map/ppermute | solution.py:549
  32.4 2.6 %turned_tiles.1.refs_3_.refs_6_ = bf16[128,128,128]{2,1,0:T(8,128)(2,1)S(1)} custom-call(s32[5,32]{1,0:T(8,128)S(1)} %pad_add_fusion.cols, bf16[128,128,128]{2,1,0:T(8,128)(2,1)S(1)} %bitcast.16), custom_call_target="tpu_custom_call" | custom-call | flops 1048576 | bytes 65536 | tf_op jit(solution)/shard_map/turned_tiles/pallas_call | solution.py:364
  35.0 3.1 %partial_messages.5.refs_1_ = bf16[1024,256]{1,0:T(8,128)(2,1)S(1)} custom-call(s32[1]{0:T(128)} %bitcast.here.refs_0_, s32[5,32]{1,0:T(8,128)S(1)} %pad_add_fusion.cols, bf16[512,256]{1,0:T(8,128)(2,1)S(1)} %get-tuple-element.57.refs_0_.refs_4_.refs_6_, bf16[512,256]{1,0:T(8,128)(2,1)S(1)} %get-tuple-element.56.refs_1_.refs_5_.refs_7_, ...), custom_call_target="tpu_custom_call" | custom-call | flops 1048576 | bytes 65536 | tf_op jit(solution)/shard_map/partial_messages/pallas_call | solution.py:132
  38.2 0.1 collective-permute-start.16
  38.2 7.3 %collective-permute-done.13.refs_2_ = bf16[1024,256]{1,0:T(8,128)(2,1)S(1)} collective-permute-done((bf16[1024,256]{1,0:T(8,128)(2,1)S(1)}, bf16[1024,256]{1,0:T(8,128)(2,1)S(1)}, u32[]{:S(2)}, u32[]{:S(2)}) %collective-permute-start.13) | collective-permute-done | bytes 524320 | tf_op jit(solution)/shard_map/ppermute | solution.py:549
  45.5 0.1 sum_terms.15
  45.7 0.1 collective-permute-start.14
  45.8 3.7 %partial_messages.3 = (bf16[1024,256]{1,0:T(8,128)(2,1)S(1)}, bf16[1024,256]{1,0:T(8,128)(2,1)S(1)}) custom-call(s32[1]{0:T(128)} %bitcast.here.refs_0_, s32[5,32]{1,0:T(8,128)S(1)} %pad_add_fusion.cols, bf16[512,256]{1,0:T(8,128)(2,1)S(1)} %get-tuple-element.57.refs_0_.refs_4_.refs_6_, bf16[512,256]{1,0:T(8,128)(2,1)S(1)} %get-tuple-element.56.refs_1_.refs_5_.refs_7_, ...), custom_call_target="tpu_custom_call" | custom-call | flops 1048576 | bytes 65536 | tf_op jit(solution)/shard_map/partial_messages/pallas_call | solution.py:132
  49.6 6.4 %collective-permute-done.16.refs_2_ = bf16[1024,256]{1,0:T(8,128)(2,1)S(1)} collective-permute-done((bf16[1024,256]{1,0:T(8,128)(2,1)S(1)}, bf16[1024,256]{1,0:T(8,128)(2,1)S(1)}, u32[]{:S(2)}, u32[]{:S(2)}) %collective-permute-start.16) | collective-permute-done | bytes 524320 | tf_op jit(solution)/shard_map/ppermute | solution.py:549
  55.9 0.1 sum_terms.17
  56.2 0.2 sum_terms.16
  56.4 3.6 %collective-permute-start.15 = (bf16[1024,256]{1,0:T(8,128)(2,1)S(1)}, bf16[1024,256]{1,0:T(8,128)(2,1)S(1)}, u32[]{:S(2)}, u32[]{:S(2)}) collective-permute-start(bf16[1024,256]{1,0:T(8,128)(2,1)S(1)} %sum_terms.16), channel_id=1, source_target_pairs={{0,1},{1,0},{2,3},{3,2},{4,5},{5,4},{6,7},{7,6},{8,9},{9,8},{10,11... | collective-permute-start | bytes 1572872 | tf_op jit(solution)/shard_map/ppermute | solution.py:549
  60.0 10.7 %collective-permute-done.15.refs_1_ = bf16[1024,256]{1,0:T(8,128)(2,1)S(1)} collective-permute-done((bf16[1024,256]{1,0:T(8,128)(2,1)S(1)}, bf16[1024,256]{1,0:T(8,128)(2,1)S(1)}, u32[]{:S(2)}, u32[]{:S(2)}) %collective-permute-start.15) | collective-permute-done | bytes 524320 | tf_op jit(solution)/shard_map/ppermute | solution.py:549
  70.8 2.9 %mlp.1 = (bf16[1024,256]{1,0:T(8,128)(2,1)}, bf16[1024,256]{1,0:T(8,128)(2,1)S(1)}, bf16[1024,256]{1,0:T(8,128)(2,1)S(1)}, bf16[1024,256]{1,0:T(8,128)(2,1)S(1)}...) custom-call(s32[1]{0:T(128)} %bitcast.here.refs_0_, ...), custom_call_target="tpu_custom_call" | custom-call | flops 1048576 | bytes 65536 | tf_op jit(solution)/shard_map/mlp/pallas_call | solution.py:218
  73.7 1.7 %collective-permute-start.18 = (bf16[1024,256]{1,0:T(8,128)(2,1)S(1)}, bf16[1024,256]{1,0:T(8,128)(2,1)S(1)}, u32[]{:S(2)}, u32[]{:S(2)}) collective-permute-start(bf16[1024,256]{1,0:T(8,128)(2,1)S(1)} %get-tuple-element.36.refs_0_), channel_id=1, source_target_pairs={{0,1},{1,0},{2,3},{3,2},{4,5},{5,4},{6,7},{7,6},{8,9},{9,8},{10,11... | collective-permute-start | bytes 1572872 | tf_op jit(solution)/shard_map/ppermute | solution.py:549
  75.5 10.1 %collective-permute-done.18.refs_0_.refs_1_ = bf16[1024,256]{1,0:T(8,128)(2,1)S(1)} collective-permute-done((bf16[1024,256]{1,0:T(8,128)(2,1)S(1)}, bf16[1024,256]{1,0:T(8,128)(2,1)S(1)}, u32[]{:S(2)}, u32[]{:S(2)}) %collective-permute-start.18) | collective-permute-done | bytes 524320 | tf_op jit(solution)/shard_map/ppermute | solution.py:549
  85.5 0.8 weight_grads.1
  86.4 0.6 collective-permute-start.23
  87.0 4.1 %collective-permute-start.20 = (bf16[1024,256]{1,0:T(8,128)(2,1)S(1)}, bf16[1024,256]{1,0:T(8,128)(2,1)S(1)}, u32[]{:S(2)}, u32[]{:S(2)}) collective-permute-start(bf16[1024,256]{1,0:T(8,128)(2,1)S(1)} %collective-permute-done.19.refs_1_.refs_2_), channel_id=1, source_target_pairs={{0,1},{1,0},{2,3},{3,2},{4,5},{5,4},{6,7},{7,6},{8,9},{9,8},{10,11... | collective-permute-start | bytes 1572872 | tf_op jit(solution)/shard_map/ppermute | solution.py:549
  91.0 9.8 %collective-permute-start.22 = (bf16[1024,256]{1,0:T(8,128)(2,1)S(1)}, bf16[1024,256]{1,0:T(8,128)(2,1)S(1)}, u32[]{:S(2)}, u32[]{:S(2)}) collective-permute-start(bf16[1024,256]{1,0:T(8,128)(2,1)S(1)} %collective-permute-done.21.refs_19_.refs_4_), channel_id=1, source_target_pairs={{0,1},{1,0},{2,3},{3,2},{4,5},{5,4},{6,7},{7,6},{8,9},{9,8},{10,11... | collective-permute-start | bytes 1572872 | tf_op jit(solution)/shard_map/ppermute | solution.py:549
  100.8 1.6 %collective-permute-start.24 = (f32[112,256]{1,0:T(8,128)S(1)}, f32[112,256]{1,0:T(8,128)S(1)}, u32[]{:S(2)}, u32[]{:S(2)}) collective-permute-start(f32[112,256]{1,0:T(8,128)S(1)} %sum_terms.19), channel_id=1, source_target_pairs={{0,16},{4,20},{8,24},{12,28},{16,0},{20,4},{24,8},{28,12},{1,17},{... | collective-permute-start | bytes 344072 | tf_op jit(solution)/shard_map/ppermute | solution.py:545
  102.4 1.6 %collective-permute-start.25 = (f32[112,256]{1,0:T(8,128)S(1)}, f32[112,256]{1,0:T(8,128)S(1)}, u32[]{:S(2)}, u32[]{:S(2)}) collective-permute-start(f32[112,256]{1,0:T(8,128)S(1)} %sum_terms.20), channel_id=1, source_target_pairs={{0,8},{4,12},{8,0},{12,4},{16,24},{20,28},{24,16},{28,20},{1,9},{5... | collective-permute-start | bytes 344072 | tf_op jit(solution)/shard_map/ppermute | solution.py:545
  104.0 0.5 collective-permute-start.26
  104.6 6.9 %tile_grads.2 = (bf16[128,128,128]{2,1,0:T(8,128)(2,1)}, f32[8,128]{1,0:T(8,128)S(1)}) custom-call(s32[1]{0:T(128)} %bitcast.here.refs_0_, s32[5,32]{1,0:T(8,128)S(1)} %pad_add_fusion.cols, bf16[1024,256]{1,0:T(8,128)(2,1)S(1)} %get-tuple-element.36.refs_0_, bf16[1024,256]{1,0:T(8,128)(2,1)S(1)} %collective-permute-done.18.refs_0_.refs_1_, ...), custom_call_target="tpu_custom_call" | custom-call | flops 1048576 | bytes 65536 | tf_op jit(solution)/shard_map/tile_grads/pallas_call | solution.py:517
  111.6 3.2 %collective-permute-done.22.refs_5_ = bf16[1024,256]{1,0:T(8,128)(2,1)S(1)} collective-permute-done((bf16[1024,256]{1,0:T(8,128)(2,1)S(1)}, bf16[1024,256]{1,0:T(8,128)(2,1)S(1)}, u32[]{:S(2)}, u32[]{:S(2)}) %collective-permute-start.22) | collective-permute-done | bytes 524320 | tf_op jit(solution)/shard_map/ppermute | solution.py:549
  114.8 5.8 %back_terms.1 = (bf16[2048,256]{1,0:T(8,128)(2,1)S(1)}, bf16[2048,256]{1,0:T(8,128)(2,1)S(1)}, bf16[4096,256]{1,0:T(8,128)(2,1)S(1)}) custom-call(s32[1]{0:T(128)} %bitcast.here.refs_0_, s32[5,32]{1,0:T(8,128)S(1)} %pad_add_fusion.cols, bf16[1024,256]{1,0:T(8,128)(2,1)S(1)} %get-tuple-element.36.refs_0_, ...), custom_call_target="tpu_custom_call" | custom-call | flops 1048576 | bytes 65536 | tf_op jit(solution)/shard_map/back_terms/pallas_call | solution.py:419
  120.6 0.1 collective-permute-start.28
  120.7 0.5 collective-permute-start.27
  121.2 2.1 %collective-permute-done.28.refs_2_ = bf16[2048,256]{1,0:T(8,128)(2,1)S(1)} collective-permute-done((bf16[2048,256]{1,0:T(8,128)(2,1)S(1)}, bf16[2048,256]{1,0:T(8,128)(2,1)S(1)}, u32[]{:S(2)}, u32[]{:S(2)}) %collective-permute-start.28) | collective-permute-done | bytes 1048608 | tf_op jit(solution)/shard_map/ppermute | solution.py:545
  123.3 0.2 sum_terms.24.refs_23_.refs_4_
  123.5 1.3 collective-permute-start.30
  124.8 0.2 sum_terms.23.refs_22_.refs_3_
  125.0 1.2 collective-permute-start.29
  126.2 3.2 %collective-permute-start.33 = (bf16[112,256]{1,0:T(8,128)(2,1)S(1)}, bf16[112,256]{1,0:T(8,128)(2,1)S(1)}, u32[]{:S(2)}, u32[]{:S(2)}) collective-permute-start(bf16[112,256]{1,0:T(8,128)(2,1)S(1)} %sum_terms.28.refs_1_), channel_id=1, source_target_pairs={{0,1},{1,2},{2,3},{3,0},{4,5},{5,6},{6,7},{7,4},{8,9},{9,10},{10,1... | collective-permute-start | bytes 172040 | tf_op jit(solution)/shard_map/ppermute | solution.py:553
  129.4 2.4 %collective-permute-start.35 = (bf16[112,256]{1,0:T(8,128)(2,1)S(1)}, bf16[112,256]{1,0:T(8,128)(2,1)S(1)}, u32[]{:S(2)}, u32[]{:S(2)}) collective-permute-start(bf16[112,256]{1,0:T(8,128)(2,1)S(1)} %sum_terms.28.refs_1_), channel_id=1, source_target_pairs={{0,3},{1,0},{2,1},{3,2},{4,7},{5,4},{6,5},{7,6},{8,11},{9,8},{10,9... | collective-permute-start | bytes 172040 | tf_op jit(solution)/shard_map/ppermute | solution.py:553
  131.8 4.0 %tile_grads.3 = (bf16[128,128,128]{2,1,0:T(8,128)(2,1)}, f32[8,128]{1,0:T(8,128)S(1)}) custom-call(s32[1]{0:T(128)} %bitcast.here.refs_0_, s32[5,32]{1,0:T(8,128)S(1)} %pad_add_fusion.cols, bf16[1024,256]{1,0:T(8,128)(2,1)S(1)} %get-tuple-element.36.refs_0_, ...), custom_call_target="tpu_custom_call", output_to_operand_aliasing={{0}: (23, {})} | custom-call | flops 1048576 | bytes 65536 | tf_op jit(solution)/shard_map/tile_grads/pallas_call | solution.py:517
  135.9 0.6 collective-permute-start.38
  136.5 1.2 collective-permute-start.37
  137.6 1.8 %collective-permute-start.36 = (bf16[112,256]{1,0:T(8,128)(2,1)S(1)}, bf16[112,256]{1,0:T(8,128)(2,1)S(1)}, u32[]{:S(2)}, u32[]{:S(2)}) collective-permute-start(bf16[112,256]{1,0:T(8,128)(2,1)S(1)} %sum_terms.29), channel_id=1, source_target_pairs={{0,8},{4,12},{8,0},{12,4},{16,24},{20,28},{24,16},{28,20},{1,9},{5... | collective-permute-start | bytes 172040 | tf_op jit(solution)/shard_map/ppermute | solution.py:545
  139.5 0.1 sum_terms.25
  139.6 0.3 collective-permute-start.31
  139.9 0.1 sum_terms.26
  140.0 0.9 collective-permute-start.32
  140.9 0.5 collective-permute-done.38
  141.4 1.0 collective-permute-done.36
  142.5 1.5 collective-permute-done.39.odd
  144.0 1.0 weight_unpack.1
  144.9 2.1 %collective-permute-done.31.refs_5_ = bf16[512,256]{1,0:T(8,128)(2,1)S(1)} collective-permute-done((bf16[512,256]{1,0:T(8,128)(2,1)S(1)}, bf16[512,256]{1,0:T(8,128)(2,1)S(1)}, u32[]{:S(2)}, u32[]{:S(2)}) %collective-permute-start.31) | collective-permute-done | bytes 262176 | tf_op jit(solution)/shard_map/ppermute | solution.py:545
  147.0 1.2 sum_terms.27
  (64 shorter events, 0.6 us)
Async XLA Ops:
  0.6 18.9 %collective-permute-start = (bf16[1024,256]{1,0:T(8,128)(2,1)}, bf16[1024,256]{1,0:T(8,128)(2,1)S(1)}, u32[]{:S(2)}, u32[]{:S(2)}) collective-permute-start(bf16[1024,256]{1,0:T(8,128)(2,1)} %nodes.3), channel_id=1, source_target_pairs={{0,4},{4,0},{8,12},{12,8},{16,20},{20,16},{24,28},{28,24},{1,5},{5... | collective-permute-start | bytes 1572872 | tf_op jit(solution)/shard_map/ppermute | solution.py:545
  2.2 9.7 %collective-permute-start.1 = (bf16[512,256]{1,0:T(8,128)(2,1)S(1)}, bf16[512,256]{1,0:T(8,128)(2,1)S(1)}, u32[]{:S(2)}, u32[]{:S(2)}) collective-permute-start(bf16[512,256]{1,0:T(8,128)(2,1)S(1)} %get-tuple-element.57.refs_0_.refs_4_.refs_6_), channel_id=1, source_target_pairs={{0,8},{4,12},{8,0},{12,4},{16,24},{20,28},{24,16},{28,20},{1,9},{5... | collective-permute-start | bytes 786440 | tf_op jit(solution)/shard_map/ppermute | solution.py:545
  4.8 9.1 %collective-permute-start.5 = (bf16[512,256]{1,0:T(8,128)(2,1)S(1)}, bf16[512,256]{1,0:T(8,128)(2,1)S(1)}, u32[]{:S(2)}, u32[]{:S(2)}) collective-permute-start(bf16[512,256]{1,0:T(8,128)(2,1)S(1)} %get-tuple-element.57.refs_0_.refs_4_.refs_6_), channel_id=1, source_target_pairs={{0,16},{4,20},{8,24},{12,28},{16,0},{20,4},{24,8},{28,12},{1,17},{... | collective-permute-start | bytes 786440 | tf_op jit(solution)/shard_map/ppermute | solution.py:545
  6.3 11.3 %collective-permute-start.2 = (bf16[512,256]{1,0:T(8,128)(2,1)S(1)}, bf16[512,256]{1,0:T(8,128)(2,1)S(1)}, u32[]{:S(2)}, u32[]{:S(2)}) collective-permute-start(bf16[512,256]{1,0:T(8,128)(2,1)S(1)} %get-tuple-element.56.refs_1_.refs_5_.refs_7_), channel_id=1, source_target_pairs={{0,8},{4,12},{8,0},{12,4},{16,24},{20,28},{24,16},{28,20},{1,9},{5... | collective-permute-start | bytes 786440 | tf_op jit(solution)/shard_map/ppermute | solution.py:545
  6.8 12.7 %collective-permute-start.6 = (bf16[512,256]{1,0:T(8,128)(2,1)S(1)}, bf16[512,256]{1,0:T(8,128)(2,1)S(1)}, u32[]{:S(2)}, u32[]{:S(2)}) collective-permute-start(bf16[512,256]{1,0:T(8,128)(2,1)S(1)} %get-tuple-element.56.refs_1_.refs_5_.refs_7_), channel_id=1, source_target_pairs={{0,16},{4,20},{8,24},{12,28},{16,0},{20,4},{24,8},{28,12},{1,17},{... | collective-permute-start | bytes 786440 | tf_op jit(solution)/shard_map/ppermute | solution.py:545
  11.9 8.1 %collective-permute-start.3 = (bf16[512,256]{1,0:T(8,128)(2,1)S(1)}, bf16[512,256]{1,0:T(8,128)(2,1)S(1)}, u32[]{:S(2)}, u32[]{:S(2)}) collective-permute-start(bf16[512,256]{1,0:T(8,128)(2,1)S(1)} %collective-permute-done.1.refs_3_.refs_7_.refs_9_), channel_id=1, source_target_pairs={{0,4},{4,0},{8,12},{12,8},{16,20},{20,16},{24,28},{28,24},{1,5},{5... | collective-permute-start | bytes 786440 | tf_op jit(solution)/shard_map/ppermute | solution.py:545
  13.9 9.1 %collective-permute-start.9 = (bf16[512,256]{1,0:T(8,128)(2,1)S(1)}, bf16[512,256]{1,0:T(8,128)(2,1)S(1)}, u32[]{:S(2)}, u32[]{:S(2)}) collective-permute-start(bf16[512,256]{1,0:T(8,128)(2,1)S(1)} %collective-permute-done.5.refs_7_.refs_11_.refs_13_), channel_id=1, source_target_pairs={{0,8},{4,12},{8,0},{12,4},{16,24},{20,28},{24,16},{28,20},{1,9},{5... | collective-permute-start | bytes 786440 | tf_op jit(solution)/shard_map/ppermute | solution.py:545
  17.6 7.9 %collective-permute-start.10 = (bf16[512,256]{1,0:T(8,128)(2,1)S(1)}, bf16[512,256]{1,0:T(8,128)(2,1)S(1)}, u32[]{:S(2)}, u32[]{:S(2)}) collective-permute-start(bf16[512,256]{1,0:T(8,128)(2,1)S(1)} %collective-permute-done.2.refs_4_.refs_8_.refs_10_), channel_id=1, source_target_pairs={{0,16},{4,20},{8,24},{12,28},{16,0},{20,4},{24,8},{28,12},{1,17},{... | collective-permute-start | bytes 786440 | tf_op jit(solution)/shard_map/ppermute | solution.py:545
  19.5 6.7 %collective-permute-start.4 = (bf16[512,256]{1,0:T(8,128)(2,1)S(1)}, bf16[512,256]{1,0:T(8,128)(2,1)S(1)}, u32[]{:S(2)}, u32[]{:S(2)}) collective-permute-start(bf16[512,256]{1,0:T(8,128)(2,1)S(1)} %collective-permute-done.2.refs_4_.refs_8_.refs_10_), channel_id=1, source_target_pairs={{0,4},{4,0},{8,12},{12,8},{16,20},{20,16},{24,28},{28,24},{1,5},{5... | collective-permute-start | bytes 786440 | tf_op jit(solution)/shard_map/ppermute | solution.py:545
  19.5 6.7 %collective-permute-start.7 = (bf16[512,256]{1,0:T(8,128)(2,1)S(1)}, bf16[512,256]{1,0:T(8,128)(2,1)}, u32[]{:S(2)}, u32[]{:S(2)}) collective-permute-start(bf16[512,256]{1,0:T(8,128)(2,1)S(1)} %collective-permute-done.5.refs_7_.refs_11_.refs_13_), channel_id=1, source_target_pairs={{0,4},{4,0},{8,12},{12,8},{16,20},{20,16},{24,28},{28,24},{1,5},{5... | collective-permute-start | bytes 786440 | tf_op jit(solution)/shard_map/ppermute | solution.py:545
  20.1 6.2 %collective-permute-start.8 = (bf16[512,256]{1,0:T(8,128)(2,1)S(1)}, bf16[512,256]{1,0:T(8,128)(2,1)}, u32[]{:S(2)}, u32[]{:S(2)}) collective-permute-start(bf16[512,256]{1,0:T(8,128)(2,1)S(1)} %collective-permute-done.6.refs_8_.refs_12_.refs_14_), channel_id=1, source_target_pairs={{0,4},{4,0},{8,12},{12,8},{16,20},{20,16},{24,28},{28,24},{1,5},{5... | collective-permute-start | bytes 786440 | tf_op jit(solution)/shard_map/ppermute | solution.py:545
  23.0 3.3 %collective-permute-start.11 = (bf16[512,256]{1,0:T(8,128)(2,1)S(1)}, bf16[512,256]{1,0:T(8,128)(2,1)}, u32[]{:S(2)}, u32[]{:S(2)}) collective-permute-start(bf16[512,256]{1,0:T(8,128)(2,1)S(1)} %collective-permute-done.9.refs_11_.refs_15_.refs_17_), channel_id=1, source_target_pairs={{0,4},{4,0},{8,12},{12,8},{16,20},{20,16},{24,28},{28,24},{1,5},{5... | collective-permute-start | bytes 786440 | tf_op jit(solution)/shard_map/ppermute | solution.py:545
  25.5 1.7 %collective-permute-start.12 = (bf16[512,256]{1,0:T(8,128)(2,1)S(1)}, bf16[512,256]{1,0:T(8,128)(2,1)}, u32[]{:S(2)}, u32[]{:S(2)}) collective-permute-start(bf16[512,256]{1,0:T(8,128)(2,1)S(1)} %collective-permute-done.10.refs_12_.refs_16_.refs_18_), channel_id=1, source_target_pairs={{0,4},{4,0},{8,12},{12,8},{16,20},{20,16},{24,28},{28,24},{1,5},{5... | collective-permute-start | bytes 786440 | tf_op jit(solution)/shard_map/ppermute | solution.py:545
  26.2 4.5 %copy-start.1 = (bf16[512,256]{1,0:T(8,128)(2,1)}, bf16[512,256]{1,0:T(8,128)(2,1)S(1)}, u32[]{:S(2)}) copy-start(bf16[512,256]{1,0:T(8,128)(2,1)S(1)} %collective-permute-done.4.refs_6_.refs_10_.refs_12_) | copy-start | bytes 786436
  27.2 5.2 %copy-start = (bf16[32,1,4,128,128]{4,3,2,1,0:T(8,128)(2,1)S(1)}, bf16[32,1,4,128,128]{4,3,2,1,0:T(8,128)(2,1)}, u32[]{:S(2)}) copy-start(bf16[32,1,4,128,128]{4,3,2,1,0:T(8,128)(2,1)} %param.11) | copy-start | bytes 12582916
  30.7 14.8 %collective-permute-start.13 = (bf16[1024,256]{1,0:T(8,128)(2,1)S(1)}, bf16[1024,256]{1,0:T(8,128)(2,1)S(1)}, u32[]{:S(2)}, u32[]{:S(2)}) collective-permute-start(bf16[1024,256]{1,0:T(8,128)(2,1)S(1)} %partial_messages.4.refs_1_), channel_id=1, source_target_pairs={{0,1},{1,0},{2,3},{3,2},{4,5},{5,4},{6,7},{7,6},{8,9},{9,8},{10,11... | collective-permute-start | bytes 1572872 | tf_op jit(solution)/shard_map/ppermute | solution.py:549
  32.4 2.6 %copy-start.2 = (bf16[512,256]{1,0:T(8,128)(2,1)S(1)}, bf16[512,256]{1,0:T(8,128)(2,1)}, u32[]{:S(2)}) copy-start(bf16[512,256]{1,0:T(8,128)(2,1)} %copy-done.1) | copy-start | bytes 786436
  38.2 17.8 %collective-permute-start.16 = (bf16[1024,256]{1,0:T(8,128)(2,1)S(1)}, bf16[1024,256]{1,0:T(8,128)(2,1)S(1)}, u32[]{:S(2)}, u32[]{:S(2)}) collective-permute-start(bf16[1024,256]{1,0:T(8,128)(2,1)S(1)} %partial_messages.5.refs_1_), channel_id=1, source_target_pairs={{0,1},{1,0},{2,3},{3,2},{4,5},{5,4},{6,7},{7,6},{8,9},{9,8},{10,11... | collective-permute-start | bytes 1572872 | tf_op jit(solution)/shard_map/ppermute | solution.py:549
  45.7 25.1 %copy-start.3 = (bf16[1024,256]{1,0:T(8,128)(2,1)S(1)}, bf16[1024,256]{1,0:T(8,128)(2,1)}, u32[]{:S(2)}) copy-start(bf16[1024,256]{1,0:T(8,128)(2,1)} %nodes.3) | copy-start | bytes 1572868
  45.7 25.1 %copy-start.4 = (bf16[1024,256]{1,0:T(8,128)(2,1)S(1)}, bf16[1024,256]{1,0:T(8,128)(2,1)}, u32[]{:S(2)}) copy-start(bf16[1024,256]{1,0:T(8,128)(2,1)} %cot.3) | copy-start | bytes 1572868
  45.7 25.1 %copy-start.5 = (bf16[512,256]{1,0:T(8,128)(2,1)S(1)}, bf16[512,256]{1,0:T(8,128)(2,1)}, u32[]{:S(2)}) copy-start(bf16[512,256]{1,0:T(8,128)(2,1)} %w_in.1) | copy-start | bytes 786436
  45.7 25.1 %copy-start.6 = (bf16[256,256]{1,0:T(8,128)(2,1)S(1)}, bf16[256,256]{1,0:T(8,128)(2,1)}, u32[]{:S(2)}) copy-start(bf16[256,256]{1,0:T(8,128)(2,1)} %refs_5_.1) | copy-start | bytes 393220
  45.7 25.1 %copy-start.7 = (f32[256]{0:T(256)S(1)}, f32[256]{0:T(256)}, u32[]{:S(2)}) copy-start(f32[256]{0:T(256)} %param.15) | copy-start | bytes 3076
  45.7 25.1 %copy-start.8 = (f32[256]{0:T(256)S(1)}, f32[256]{0:T(256)}, u32[]{:S(2)}) copy-start(f32[256]{0:T(256)} %param.17) | copy-start | bytes 3076
  45.7 25.1 %copy-start.9 = (f32[256]{0:T(256)S(1)}, f32[256]{0:T(256)}, u32[]{:S(2)}) copy-start(f32[256]{0:T(256)} %param.18) | copy-start | bytes 3076
  45.7 10.4 %collective-permute-start.14 = (bf16[1024,256]{1,0:T(8,128)(2,1)S(1)}, bf16[1024,256]{1,0:T(8,128)(2,1)S(1)}, u32[]{:S(2)}, u32[]{:S(2)}) collective-permute-start(bf16[1024,256]{1,0:T(8,128)(2,1)S(1)} %sum_terms.15), channel_id=1, source_target_pairs={{0,4},{1,2},{2,1},{3,7},{4,0},{5,6},{6,5},{7,3},{8,12},{9,10},{10,... | collective-permute-start | bytes 1572872 | tf_op jit(solution)/shard_map/ppermute | solution.py:562
  56.1 4.0 %collective-permute-start.17 = (bf16[1024,256]{1,0:T(8,128)(2,1)S(1)}, bf16[1024,256]{1,0:T(8,128)(2,1)S(1)}, u32[]{:S(2)}, u32[]{:S(2)}) collective-permute-start(bf16[1024,256]{1,0:T(8,128)(2,1)S(1)} %sum_terms.17), channel_id=1, source_target_pairs={{0,4},{1,2},{2,1},{3,7},{4,0},{5,6},{6,5},{7,3},{8,12},{9,10},{10,... | collective-permute-start | bytes 1572872 | tf_op jit(solution)/shard_map/ppermute | solution.py:562
  56.4 14.4 %collective-permute-start.15 = (bf16[1024,256]{1,0:T(8,128)(2,1)S(1)}, bf16[1024,256]{1,0:T(8,128)(2,1)S(1)}, u32[]{:S(2)}, u32[]{:S(2)}) collective-permute-start(bf16[1024,256]{1,0:T(8,128)(2,1)S(1)} %sum_terms.16), channel_id=1, source_target_pairs={{0,1},{1,0},{2,3},{3,2},{4,5},{5,4},{6,7},{7,6},{8,9},{9,8},{10,11... | collective-permute-start | bytes 1572872 | tf_op jit(solution)/shard_map/ppermute | solution.py:549
  73.7 11.8 %collective-permute-start.18 = (bf16[1024,256]{1,0:T(8,128)(2,1)S(1)}, bf16[1024,256]{1,0:T(8,128)(2,1)S(1)}, u32[]{:S(2)}, u32[]{:S(2)}) collective-permute-start(bf16[1024,256]{1,0:T(8,128)(2,1)S(1)} %get-tuple-element.36.refs_0_), channel_id=1, source_target_pairs={{0,1},{1,0},{2,3},{3,2},{4,5},{5,4},{6,7},{7,6},{8,9},{9,8},{10,11... | collective-permute-start | bytes 1572872 | tf_op jit(solution)/shard_map/ppermute | solution.py:549
  75.5 10.1 %collective-permute-start.19 = (bf16[1024,256]{1,0:T(8,128)(2,1)S(1)}, bf16[1024,256]{1,0:T(8,128)(2,1)S(1)}, u32[]{:S(2)}, u32[]{:S(2)}) collective-permute-start(bf16[1024,256]{1,0:T(8,128)(2,1)S(1)} %get-tuple-element.36.refs_0_), channel_id=1, source_target_pairs={{0,4},{1,2},{2,1},{3,7},{4,0},{5,6},{6,5},{7,3},{8,12},{9,10},{10,... | collective-permute-start | bytes 1572872 | tf_op jit(solution)/shard_map/ppermute | solution.py:562
  85.5 5.5 %collective-permute-start.21 = (bf16[1024,256]{1,0:T(8,128)(2,1)S(1)}, bf16[1024,256]{1,0:T(8,128)(2,1)S(1)}, u32[]{:S(2)}, u32[]{:S(2)}) collective-permute-start(bf16[1024,256]{1,0:T(8,128)(2,1)S(1)} %collective-permute-done.18.refs_0_.refs_1_), channel_id=1, source_target_pairs={{0,4},{1,2},{2,1},{3,7},{4,0},{5,6},{6,5},{7,3},{8,12},{9,10},{10,... | collective-permute-start | bytes 1572872 | tf_op jit(solution)/shard_map/ppermute | solution.py:562
  86.4 14.4 %collective-permute-start.23 = (f32[448,256]{1,0:T(8,128)S(1)}, f32[448,256]{1,0:T(8,128)S(1)}, u32[]{:S(2)}, u32[]{:S(2)}) collective-permute-start(f32[448,256]{1,0:T(8,128)S(1)} %get-tuple-element.39), channel_id=1, source_target_pairs={{0,4},{4,0},{8,12},{12,8},{16,20},{20,16},{24,28},{28,24},{1,5},{5... | collective-permute-start | bytes 1376264 | tf_op jit(solution)/shard_map/ppermute | solution.py:545
  87.0 17.6 %collective-permute-start.20 = (bf16[1024,256]{1,0:T(8,128)(2,1)S(1)}, bf16[1024,256]{1,0:T(8,128)(2,1)S(1)}, u32[]{:S(2)}, u32[]{:S(2)}) collective-permute-start(bf16[1024,256]{1,0:T(8,128)(2,1)S(1)} %collective-permute-done.19.refs_1_.refs_2_), channel_id=1, source_target_pairs={{0,1},{1,0},{2,3},{3,2},{4,5},{5,4},{6,7},{7,6},{8,9},{9,8},{10,11... | collective-permute-start | bytes 1572872 | tf_op jit(solution)/shard_map/ppermute | solution.py:549
  91.0 23.7 %collective-permute-start.22 = (bf16[1024,256]{1,0:T(8,128)(2,1)S(1)}, bf16[1024,256]{1,0:T(8,128)(2,1)S(1)}, u32[]{:S(2)}, u32[]{:S(2)}) collective-permute-start(bf16[1024,256]{1,0:T(8,128)(2,1)S(1)} %collective-permute-done.21.refs_19_.refs_4_), channel_id=1, source_target_pairs={{0,1},{1,0},{2,3},{3,2},{4,5},{5,4},{6,7},{7,6},{8,9},{9,8},{10,11... | collective-permute-start | bytes 1572872 | tf_op jit(solution)/shard_map/ppermute | solution.py:549
  100.8 10.7 %collective-permute-start.24 = (f32[112,256]{1,0:T(8,128)S(1)}, f32[112,256]{1,0:T(8,128)S(1)}, u32[]{:S(2)}, u32[]{:S(2)}) collective-permute-start(f32[112,256]{1,0:T(8,128)S(1)} %sum_terms.19), channel_id=1, source_target_pairs={{0,16},{4,20},{8,24},{12,28},{16,0},{20,4},{24,8},{28,12},{1,17},{... | collective-permute-start | bytes 344072 | tf_op jit(solution)/shard_map/ppermute | solution.py:545
  102.4 9.1 %collective-permute-start.25 = (f32[112,256]{1,0:T(8,128)S(1)}, f32[112,256]{1,0:T(8,128)S(1)}, u32[]{:S(2)}, u32[]{:S(2)}) collective-permute-start(f32[112,256]{1,0:T(8,128)S(1)} %sum_terms.20), channel_id=1, source_target_pairs={{0,8},{4,12},{8,0},{12,4},{16,24},{20,28},{24,16},{28,20},{1,9},{5... | collective-permute-start | bytes 344072 | tf_op jit(solution)/shard_map/ppermute | solution.py:545
  104.0 7.5 %collective-permute-start.26 = (f32[112,256]{1,0:T(8,128)S(1)}, f32[112,256]{1,0:T(8,128)S(1)}, u32[]{:S(2)}, u32[]{:S(2)}) collective-permute-start(f32[112,256]{1,0:T(8,128)S(1)} %sum_terms.21), channel_id=1, source_target_pairs={{0,24},{4,28},{8,16},{12,20},{16,8},{20,12},{24,0},{28,4},{1,25},{... | collective-permute-start | bytes 344072 | tf_op jit(solution)/shard_map/ppermute | solution.py:545
  120.6 2.7 %collective-permute-start.28 = (bf16[2048,256]{1,0:T(8,128)(2,1)S(1)}, bf16[2048,256]{1,0:T(8,128)(2,1)S(1)}, u32[]{:S(2)}, u32[]{:S(2)}) collective-permute-start(bf16[2048,256]{1,0:T(8,128)(2,1)S(1)} %get-tuple-element.43), channel_id=1, source_target_pairs={{0,4},{4,0},{8,12},{12,8},{16,20},{20,16},{24,28},{28,24},{1,5},{5... | collective-permute-start | bytes 3145736 | tf_op jit(solution)/shard_map/ppermute | solution.py:545
  120.7 5.5 %collective-permute-start.27 = (bf16[2048,256]{1,0:T(8,128)(2,1)S(1)}, bf16[2048,256]{1,0:T(8,128)(2,1)S(1)}, u32[]{:S(2)}, u32[]{:S(2)}) collective-permute-start(bf16[2048,256]{1,0:T(8,128)(2,1)S(1)} %get-tuple-element.42), channel_id=1, source_target_pairs={{0,4},{4,0},{8,12},{12,8},{16,20},{20,16},{24,28},{28,24},{1,5},{5... | collective-permute-start | bytes 3145736 | tf_op jit(solution)/shard_map/ppermute | solution.py:545
  123.5 16.0 %collective-permute-start.30 = (bf16[1024,256]{1,0:T(8,128)(2,1)S(1)}, bf16[1024,256]{1,0:T(8,128)(2,1)S(1)}, u32[]{:S(2)}, u32[]{:S(2)}) collective-permute-start(bf16[1024,256]{1,0:T(8,128)(2,1)S(1)} %sum_terms.24.refs_23_.refs_4_), channel_id=1, source_target_pairs={{0,16},{4,20},{8,24},{12,28},{16,0},{20,4},{24,8},{28,12},{1,17},{... | collective-permute-start | bytes 1572872 | tf_op jit(solution)/shard_map/ppermute | solution.py:545
  125.0 14.9 %collective-permute-start.29 = (bf16[1024,256]{1,0:T(8,128)(2,1)S(1)}, bf16[1024,256]{1,0:T(8,128)(2,1)S(1)}, u32[]{:S(2)}, u32[]{:S(2)}) collective-permute-start(bf16[1024,256]{1,0:T(8,128)(2,1)S(1)} %sum_terms.23.refs_22_.refs_3_), channel_id=1, source_target_pairs={{0,8},{4,12},{8,0},{12,4},{16,24},{20,28},{24,16},{28,20},{1,9},{5... | collective-permute-start | bytes 1572872 | tf_op jit(solution)/shard_map/ppermute | solution.py:545
  126.2 9.6 %collective-permute-start.33 = (bf16[112,256]{1,0:T(8,128)(2,1)S(1)}, bf16[112,256]{1,0:T(8,128)(2,1)S(1)}, u32[]{:S(2)}, u32[]{:S(2)}) collective-permute-start(bf16[112,256]{1,0:T(8,128)(2,1)S(1)} %sum_terms.28.refs_1_), channel_id=1, source_target_pairs={{0,1},{1,2},{2,3},{3,0},{4,5},{5,6},{6,7},{7,4},{8,9},{9,10},{10,1... | collective-permute-start | bytes 172040 | tf_op jit(solution)/shard_map/ppermute | solution.py:553
  129.4 6.5 %collective-permute-start.34 = (bf16[112,256]{1,0:T(8,128)(2,1)S(1)}, bf16[112,256]{1,0:T(8,128)(2,1)S(1)}, u32[]{:S(2)}, u32[]{:S(2)}) collective-permute-start(bf16[112,256]{1,0:T(8,128)(2,1)S(1)} %sum_terms.28.refs_1_), channel_id=1, source_target_pairs={{0,2},{1,3},{2,0},{3,1},{4,6},{5,7},{6,4},{7,5},{8,10},{9,11},{10,... | collective-permute-start | bytes 172040 | tf_op jit(solution)/shard_map/ppermute | solution.py:553
  129.4 6.5 %collective-permute-start.35 = (bf16[112,256]{1,0:T(8,128)(2,1)S(1)}, bf16[112,256]{1,0:T(8,128)(2,1)S(1)}, u32[]{:S(2)}, u32[]{:S(2)}) collective-permute-start(bf16[112,256]{1,0:T(8,128)(2,1)S(1)} %sum_terms.28.refs_1_), channel_id=1, source_target_pairs={{0,3},{1,0},{2,1},{3,2},{4,7},{5,4},{6,5},{7,6},{8,11},{9,8},{10,9... | collective-permute-start | bytes 172040 | tf_op jit(solution)/shard_map/ppermute | solution.py:553
  135.9 5.5 %collective-permute-start.38 = (bf16[112,256]{1,0:T(8,128)(2,1)S(1)}, bf16[112,256]{1,0:T(8,128)(2,1)S(1)}, u32[]{:S(2)}, u32[]{:S(2)}) collective-permute-start(bf16[112,256]{1,0:T(8,128)(2,1)S(1)} %sum_terms.29), channel_id=1, source_target_pairs={{0,24},{4,28},{8,16},{12,20},{16,8},{20,12},{24,0},{28,4},{1,25},{... | collective-permute-start | bytes 172040 | tf_op jit(solution)/shard_map/ppermute | solution.py:545
  136.5 4.9 %collective-permute-start.37 = (bf16[112,256]{1,0:T(8,128)(2,1)S(1)}, bf16[112,256]{1,0:T(8,128)(2,1)S(1)}, u32[]{:S(2)}, u32[]{:S(2)}) collective-permute-start(bf16[112,256]{1,0:T(8,128)(2,1)S(1)} %sum_terms.29), channel_id=1, source_target_pairs={{0,16},{4,20},{8,24},{12,28},{16,0},{20,4},{24,8},{28,12},{1,17},{... | collective-permute-start | bytes 172040 | tf_op jit(solution)/shard_map/ppermute | solution.py:545
  137.6 4.8 %collective-permute-start.36 = (bf16[112,256]{1,0:T(8,128)(2,1)S(1)}, bf16[112,256]{1,0:T(8,128)(2,1)S(1)}, u32[]{:S(2)}, u32[]{:S(2)}) collective-permute-start(bf16[112,256]{1,0:T(8,128)(2,1)S(1)} %sum_terms.29), channel_id=1, source_target_pairs={{0,8},{4,12},{8,0},{12,4},{16,24},{20,28},{24,16},{28,20},{1,9},{5... | collective-permute-start | bytes 172040 | tf_op jit(solution)/shard_map/ppermute | solution.py:545
  139.6 7.4 %collective-permute-start.31 = (bf16[512,256]{1,0:T(8,128)(2,1)S(1)}, bf16[512,256]{1,0:T(8,128)(2,1)S(1)}, u32[]{:S(2)}, u32[]{:S(2)}) collective-permute-start(bf16[512,256]{1,0:T(8,128)(2,1)S(1)} %sum_terms.25), channel_id=1, source_target_pairs={{0,8},{4,12},{8,0},{12,4},{16,24},{20,28},{24,16},{28,20},{1,9},{5... | collective-permute-start | bytes 786440 | tf_op jit(solution)/shard_map/ppermute | solution.py:545
  140.0 7.0 %collective-permute-start.32 = (bf16[512,256]{1,0:T(8,128)(2,1)S(1)}, bf16[512,256]{1,0:T(8,128)(2,1)S(1)}, u32[]{:S(2)}, u32[]{:S(2)}) collective-permute-start(bf16[512,256]{1,0:T(8,128)(2,1)S(1)} %sum_terms.26), channel_id=1, source_target_pairs={{0,16},{4,20},{8,24},{12,28},{16,0},{20,4},{24,8},{28,12},{1,17},{... | collective-permute-start | bytes 786440 | tf_op jit(solution)/shard_map/ppermute | solution.py:545
  142.4 1.6 %collective-permute-start.39 = (bf16[448,256]{1,0:T(8,128)(2,1)S(1)}, bf16[448,256]{1,0:T(8,128)(2,1)S(1)}, u32[]{:S(2)}, u32[]{:S(2)}) collective-permute-start(bf16[448,256]{1,0:T(8,128)(2,1)S(1)} %pad_maximum_fusion.even), channel_id=1, source_target_pairs={{0,4},{4,0},{8,12},{12,8},{16,20},{20,16},{24,28},{28,24},{1,5},{5... | collective-permute-start | bytes 688136 | tf_op jit(solution)/shard_map/ppermute | solution.py:545

commit v17 on v16

--- a/solution.py
+++ b/solution.py
@@ -710,11 +710,11 @@
         )
         urgent, rest = swap(urgent, 1), swap(rest, 1)
         arrived, first = reduce_square(here, even, urgent, rest, rows)
-        grad_tiles, token = tile_grad_call(
+        grad_tiles, _ = tile_grad_call(
             *known, grads, pieces, tile_local.shape, rows, (0,), near_grads, first
         )
         row_weights = sum_call(here, row_weights.shape[0], [(row_weights, 0)], after=(rest, *first))
-        all_weights = level_weights(here, row_weights, (token,))
+        all_weights = level_weights(here, row_weights, first)
         joint = jnp.concatenate([all_weights] + [swap(all_weights, bits) for bits in (2, 4, 6)], axis=0)
         weights = unpack_call(here, joint, swap(joint, 1), width)
         grad_nodes = sum_call(here, rows, [(direct, 0), (even, 0), (rest, 0)], split=arrived)

time: 149 us -> 150 us (level)
  starting transfers between devices: 46.7 us -> 49.8 us
  waiting for transfers between devices: 61.8 us -> 60 us
    ppermute x27, waiting for transfers between devices: 24.2 us -> 20.4 us  [swap(): return lax.ppermute(value, 'row', [(i, i ^ bit) for i in range(8)])]
    ppermute x27, starting transfers between devices: 20 us -> 22 us  [swap(): return lax.ppermute(value, 'row', [(i, i ^ bit) for i in range(8)])]
    ppermute x3, waiting for transfers between devices: 0.01 us -> 1.83 us  [turn(): return lax.ppermute(value, 'col', [(i, (i + by) % 4) for i in range(4)])]
where the time goes in v17:
time: 150 us
  waiting for transfers between devices  60 us (40%)
  starting transfers between devices  49.8 us (33%)
  Pallas kernels  37.1 us (25%)
    ppermute x6, waiting for transfers between devices, outer_swap(): return lax.ppermute(value, 'col', [(0, 1), (1, 0), (2, 3), (3, 2)])  37.8 us
    ppermute x27, starting transfers between devices, swap(): return lax.ppermute(value, 'row', [(i, i ^ bit) for i in range(8)])  22 us
    ppermute x6, starting transfers between devices, outer_swap(): return lax.ppermute(value, 'col', [(0, 1), (1, 0), (2, 3), (3, 2)])  21.3 us
    ppermute x27, waiting for transfers between devices, swap(): return lax.ppermute(value, 'row', [(i, i ^ bit) for i in range(8)])  20.4 us
    pallas_call x2, Pallas kernels, tile_grad_call(): pl.pallas_call(functools.partial(tile_grad_kernel, rows, slots, len(grads...  11.4 us
    pallas_call x3, Pallas kernels, forward_call(): pl.pallas_call(functools.partial(forward_kernel, outputs, len(pieces), pa...  10.4 us
    ppermute x3, starting transfers between devices, turn(): return lax.ppermute(value, 'col', [(i, (i + by) % 4) for i in range(4)])  6.28 us
    pallas_call x1, Pallas kernels, back_call(): pl.pallas_call(functools.partial(back_kernel, rows, slots, len(grads), le...  5.66 us
  transfers between devices with their start and end apart: 40, of which 16 were waited for; matrix products, arithmetic and copies ran while one was open for 1% of the time, Pallas kernels for 16%

profile of v17, /device:TPU:0, one launch (start us, length us, event | category | flops | bytes accessed | tf_op | source)
XLA Modules:
  0.0 149.7 jit_solution(17517930090924997845)
XLA Ops:
  0.6 0.5 collective-permute-start
  1.1 1.1 fusion
  2.2 2.6 %collective-permute-start.1 = (bf16[512,256]{1,0:T(8,128)(2,1)S(1)}, bf16[512,256]{1,0:T(8,128)(2,1)S(1)}, u32[]{:S(2)}, u32[]{:S(2)}) collective-permute-start(bf16[512,256]{1,0:T(8,128)(2,1)S(1)} %get-tuple-element.55.refs_0_.refs_4_.refs_6_), channel_id=1, source_target_pairs={{0,8},{4,12},{8,0},{12,4},{16,24},{20,28},{24,16},{28,20},{1,9},{5... | collective-permute-start | bytes 786440 | tf_op jit(solution)/shard_map/ppermute | solution.py:545
  4.8 1.5 %collective-permute-start.5 = (bf16[512,256]{1,0:T(8,128)(2,1)S(1)}, bf16[512,256]{1,0:T(8,128)(2,1)S(1)}, u32[]{:S(2)}, u32[]{:S(2)}) collective-permute-start(bf16[512,256]{1,0:T(8,128)(2,1)S(1)} %get-tuple-element.55.refs_0_.refs_4_.refs_6_), channel_id=1, source_target_pairs={{0,16},{4,20},{8,24},{12,28},{16,0},{20,4},{24,8},{28,12},{1,17},{... | collective-permute-start | bytes 786440 | tf_op jit(solution)/shard_map/ppermute | solution.py:545
  6.3 0.5 collective-permute-start.2
  6.9 5.1 %collective-permute-done.1.refs_3_.refs_7_.refs_9_ = bf16[512,256]{1,0:T(8,128)(2,1)S(1)} collective-permute-done((bf16[512,256]{1,0:T(8,128)(2,1)S(1)}, bf16[512,256]{1,0:T(8,128)(2,1)S(1)}, u32[]{:S(2)}, u32[]{:S(2)}) %collective-permute-start.1) | collective-permute-done | bytes 262176 | tf_op jit(solution)/shard_map/ppermute | solution.py:545
  11.9 2.0 %collective-permute-done.5.refs_7_.refs_11_.refs_13_ = bf16[512,256]{1,0:T(8,128)(2,1)S(1)} collective-permute-done((bf16[512,256]{1,0:T(8,128)(2,1)S(1)}, bf16[512,256]{1,0:T(8,128)(2,1)S(1)}, u32[]{:S(2)}, u32[]{:S(2)}) %collective-permute-start.5) | collective-permute-done | bytes 262176 | tf_op jit(solution)/shard_map/ppermute | solution.py:545
  14.0 3.6 %collective-permute-done.2.refs_4_.refs_8_.refs_10_ = bf16[512,256]{1,0:T(8,128)(2,1)S(1)} collective-permute-done((bf16[512,256]{1,0:T(8,128)(2,1)S(1)}, bf16[512,256]{1,0:T(8,128)(2,1)S(1)}, u32[]{:S(2)}, u32[]{:S(2)}) %collective-permute-start.2) | collective-permute-done | bytes 262176 | tf_op jit(solution)/shard_map/ppermute | solution.py:545
  17.6 2.0 %collective-permute-start.10 = (bf16[512,256]{1,0:T(8,128)(2,1)S(1)}, bf16[512,256]{1,0:T(8,128)(2,1)S(1)}, u32[]{:S(2)}, u32[]{:S(2)}) collective-permute-start(bf16[512,256]{1,0:T(8,128)(2,1)S(1)} %collective-permute-done.2.refs_4_.refs_8_.refs_10_), channel_id=1, source_target_pairs={{0,16},{4,20},{8,24},{12,28},{16,0},{20,4},{24,8},{28,12},{1,17},{... | collective-permute-start | bytes 786440 | tf_op jit(solution)/shard_map/ppermute | solution.py:545
  19.5 0.5 collective-permute-start.7
  20.1 2.9 %collective-permute-done.9.refs_11_.refs_15_.refs_17_ = bf16[512,256]{1,0:T(8,128)(2,1)S(1)} collective-permute-done((bf16[512,256]{1,0:T(8,128)(2,1)S(1)}, bf16[512,256]{1,0:T(8,128)(2,1)S(1)}, u32[]{:S(2)}, u32[]{:S(2)}) %collective-permute-start.9) | collective-permute-done | bytes 262176 | tf_op jit(solution)/shard_map/ppermute | solution.py:545
  23.0 2.5 %collective-permute-done.10.refs_12_.refs_16_.refs_18_ = bf16[512,256]{1,0:T(8,128)(2,1)S(1)} collective-permute-done((bf16[512,256]{1,0:T(8,128)(2,1)S(1)}, bf16[512,256]{1,0:T(8,128)(2,1)S(1)}, u32[]{:S(2)}, u32[]{:S(2)}) %collective-permute-start.10) | collective-permute-done | bytes 262176 | tf_op jit(solution)/shard_map/ppermute | solution.py:545
  25.5 0.7 pad_add_fusion.cols
  26.2 0.9 collective-permute-done.12.refs_14_.refs_18_.refs_20_
  27.2 3.5 %partial_messages.4.refs_1_ = bf16[1024,256]{1,0:T(8,128)(2,1)S(1)} custom-call(s32[1]{0:T(128)} %bitcast.here.refs_0_, s32[5,32]{1,0:T(8,128)S(1)} %pad_add_fusion.cols, bf16[512,256]{1,0:T(8,128)(2,1)S(1)} %get-tuple-element.55.refs_0_.refs_4_.refs_6_, bf16[512,256]{1,0:T(8,128)(2,1)S(1)} %get-tuple-element.54.refs_1_.refs_5_.refs_7_, ...), custom_call_target="tpu_custom_call" | custom-call | flops 1048576 | bytes 65536 | tf_op jit(solution)/shard_map/partial_messages/pallas_call | solution.py:132
  30.7 1.7 %collective-permute-start.13 = (bf16[1024,256]{1,0:T(8,128)(2,1)S(1)}, bf16[1024,256]{1,0:T(8,128)(2,1)S(1)}, u32[]{:S(2)}, u32[]{:S(2)}) collective-permute-start(bf16[1024,256]{1,0:T(8,128)(2,1)S(1)} %partial_messages.4.refs_1_), channel_id=1, source_target_pairs={{0,1},{1,0},{2,3},{3,2},{4,5},{5,4},{6,7},{7,6},{8,9},{9,8},{10,11... | collective-permute-start | bytes 1572872 | tf_op jit(solution)/shard_map/ppermute | solution.py:549
  32.4 2.6 %turned_tiles.1.refs_3_.refs_6_ = bf16[128,128,128]{2,1,0:T(8,128)(2,1)S(1)} custom-call(s32[5,32]{1,0:T(8,128)S(1)} %pad_add_fusion.cols, bf16[128,128,128]{2,1,0:T(8,128)(2,1)S(1)} %bitcast.16), custom_call_target="tpu_custom_call" | custom-call | flops 1048576 | bytes 65536 | tf_op jit(solution)/shard_map/turned_tiles/pallas_call | solution.py:364
  35.0 3.1 %partial_messages.5.refs_1_ = bf16[1024,256]{1,0:T(8,128)(2,1)S(1)} custom-call(s32[1]{0:T(128)} %bitcast.here.refs_0_, s32[5,32]{1,0:T(8,128)S(1)} %pad_add_fusion.cols, bf16[512,256]{1,0:T(8,128)(2,1)S(1)} %get-tuple-element.55.refs_0_.refs_4_.refs_6_, bf16[512,256]{1,0:T(8,128)(2,1)S(1)} %get-tuple-element.54.refs_1_.refs_5_.refs_7_, ...), custom_call_target="tpu_custom_call" | custom-call | flops 1048576 | bytes 65536 | tf_op jit(solution)/shard_map/partial_messages/pallas_call | solution.py:132
  38.1 0.5 collective-permute-start.16
  38.6 6.9 %collective-permute-done.13.refs_2_ = bf16[1024,256]{1,0:T(8,128)(2,1)S(1)} collective-permute-done((bf16[1024,256]{1,0:T(8,128)(2,1)S(1)}, bf16[1024,256]{1,0:T(8,128)(2,1)S(1)}, u32[]{:S(2)}, u32[]{:S(2)}) %collective-permute-start.13) | collective-permute-done | bytes 524320 | tf_op jit(solution)/shard_map/ppermute | solution.py:549
  45.5 0.1 sum_terms.15
  45.8 3.7 %partial_messages.3 = (bf16[1024,256]{1,0:T(8,128)(2,1)S(1)}, bf16[1024,256]{1,0:T(8,128)(2,1)S(1)}) custom-call(s32[1]{0:T(128)} %bitcast.here.refs_0_, s32[5,32]{1,0:T(8,128)S(1)} %pad_add_fusion.cols, bf16[512,256]{1,0:T(8,128)(2,1)S(1)} %get-tuple-element.55.refs_0_.refs_4_.refs_6_, bf16[512,256]{1,0:T(8,128)(2,1)S(1)} %get-tuple-element.54.refs_1_.refs_5_.refs_7_, ...), custom_call_target="tpu_custom_call" | custom-call | flops 1048576 | bytes 65536 | tf_op jit(solution)/shard_map/partial_messages/pallas_call | solution.py:132
  49.6 6.4 %collective-permute-done.16.refs_2_ = bf16[1024,256]{1,0:T(8,128)(2,1)S(1)} collective-permute-done((bf16[1024,256]{1,0:T(8,128)(2,1)S(1)}, bf16[1024,256]{1,0:T(8,128)(2,1)S(1)}, u32[]{:S(2)}, u32[]{:S(2)}) %collective-permute-start.16) | collective-permute-done | bytes 524320 | tf_op jit(solution)/shard_map/ppermute | solution.py:549
  55.9 0.1 sum_terms.17
  56.2 0.2 sum_terms.16
  56.4 3.6 %collective-permute-start.15 = (bf16[1024,256]{1,0:T(8,128)(2,1)S(1)}, bf16[1024,256]{1,0:T(8,128)(2,1)S(1)}, u32[]{:S(2)}, u32[]{:S(2)}) collective-permute-start(bf16[1024,256]{1,0:T(8,128)(2,1)S(1)} %sum_terms.16), channel_id=1, source_target_pairs={{0,1},{1,0},{2,3},{3,2},{4,5},{5,4},{6,7},{7,6},{8,9},{9,8},{10,11... | collective-permute-start | bytes 1572872 | tf_op jit(solution)/shard_map/ppermute | solution.py:549
  60.0 10.7 %collective-permute-done.15.refs_1_ = bf16[1024,256]{1,0:T(8,128)(2,1)S(1)} collective-permute-done((bf16[1024,256]{1,0:T(8,128)(2,1)S(1)}, bf16[1024,256]{1,0:T(8,128)(2,1)S(1)}, u32[]{:S(2)}, u32[]{:S(2)}) %collective-permute-start.15) | collective-permute-done | bytes 524320 | tf_op jit(solution)/shard_map/ppermute | solution.py:549
  70.8 2.9 %mlp.1 = (bf16[1024,256]{1,0:T(8,128)(2,1)}, bf16[1024,256]{1,0:T(8,128)(2,1)S(1)}, bf16[1024,256]{1,0:T(8,128)(2,1)S(1)}, bf16[1024,256]{1,0:T(8,128)(2,1)S(1)}...) custom-call(s32[1]{0:T(128)} %bitcast.here.refs_0_, ...), custom_call_target="tpu_custom_call" | custom-call | flops 1048576 | bytes 65536 | tf_op jit(solution)/shard_map/mlp/pallas_call | solution.py:218
  73.7 1.7 %collective-permute-start.18 = (bf16[1024,256]{1,0:T(8,128)(2,1)S(1)}, bf16[1024,256]{1,0:T(8,128)(2,1)S(1)}, u32[]{:S(2)}, u32[]{:S(2)}) collective-permute-start(bf16[1024,256]{1,0:T(8,128)(2,1)S(1)} %get-tuple-element.35.refs_0_), channel_id=1, source_target_pairs={{0,1},{1,0},{2,3},{3,2},{4,5},{5,4},{6,7},{7,6},{8,9},{9,8},{10,11... | collective-permute-start | bytes 1572872 | tf_op jit(solution)/shard_map/ppermute | solution.py:549
  75.5 10.1 %collective-permute-done.18.refs_0_.refs_1_ = bf16[1024,256]{1,0:T(8,128)(2,1)S(1)} collective-permute-done((bf16[1024,256]{1,0:T(8,128)(2,1)S(1)}, bf16[1024,256]{1,0:T(8,128)(2,1)S(1)}, u32[]{:S(2)}, u32[]{:S(2)}) %collective-permute-start.18) | collective-permute-done | bytes 524320 | tf_op jit(solution)/shard_map/ppermute | solution.py:549
  85.5 0.8 weight_grads.1
  86.4 0.6 collective-permute-start.23
  87.0 4.1 %collective-permute-start.20 = (bf16[1024,256]{1,0:T(8,128)(2,1)S(1)}, bf16[1024,256]{1,0:T(8,128)(2,1)S(1)}, u32[]{:S(2)}, u32[]{:S(2)}) collective-permute-start(bf16[1024,256]{1,0:T(8,128)(2,1)S(1)} %collective-permute-done.19.refs_1_.refs_2_), channel_id=1, source_target_pairs={{0,1},{1,0},{2,3},{3,2},{4,5},{5,4},{6,7},{7,6},{8,9},{9,8},{10,11... | collective-permute-start | bytes 1572872 | tf_op jit(solution)/shard_map/ppermute | solution.py:549
  91.0 9.8 %collective-permute-start.22 = (bf16[1024,256]{1,0:T(8,128)(2,1)S(1)}, bf16[1024,256]{1,0:T(8,128)(2,1)S(1)}, u32[]{:S(2)}, u32[]{:S(2)}) collective-permute-start(bf16[1024,256]{1,0:T(8,128)(2,1)S(1)} %collective-permute-done.21.refs_19_.refs_4_), channel_id=1, source_target_pairs={{0,1},{1,0},{2,3},{3,2},{4,5},{5,4},{6,7},{7,6},{8,9},{9,8},{10,11... | collective-permute-start | bytes 1572872 | tf_op jit(solution)/shard_map/ppermute | solution.py:549
  100.8 1.6 %collective-permute-start.24 = (f32[112,256]{1,0:T(8,128)S(1)}, f32[112,256]{1,0:T(8,128)S(1)}, u32[]{:S(2)}, u32[]{:S(2)}) collective-permute-start(f32[112,256]{1,0:T(8,128)S(1)} %sum_terms.19), channel_id=1, source_target_pairs={{0,16},{4,20},{8,24},{12,28},{16,0},{20,4},{24,8},{28,12},{1,17},{... | collective-permute-start | bytes 344072 | tf_op jit(solution)/shard_map/ppermute | solution.py:545
  102.4 1.6 %collective-permute-start.25 = (f32[112,256]{1,0:T(8,128)S(1)}, f32[112,256]{1,0:T(8,128)S(1)}, u32[]{:S(2)}, u32[]{:S(2)}) collective-permute-start(f32[112,256]{1,0:T(8,128)S(1)} %sum_terms.20), channel_id=1, source_target_pairs={{0,8},{4,12},{8,0},{12,4},{16,24},{20,28},{24,16},{28,20},{1,9},{5... | collective-permute-start | bytes 344072 | tf_op jit(solution)/shard_map/ppermute | solution.py:545
  104.0 0.5 collective-permute-start.26
  104.6 6.5 %tile_grads.2 = (bf16[128,128,128]{2,1,0:T(8,128)(2,1)}, f32[8,128]{1,0:T(8,128)S(1)}) custom-call(s32[1]{0:T(128)} %bitcast.here.refs_0_, s32[5,32]{1,0:T(8,128)S(1)} %pad_add_fusion.cols, bf16[1024,256]{1,0:T(8,128)(2,1)S(1)} %get-tuple-element.35.refs_0_, bf16[1024,256]{1,0:T(8,128)(2,1)S(1)} %collective-permute-done.18.refs_0_.refs_1_, ...), custom_call_target="tpu_custom_call" | custom-call | flops 1048576 | bytes 65536 | tf_op jit(solution)/shard_map/tile_grads/pallas_call | solution.py:517
  111.1 3.7 %collective-permute-done.22.refs_5_ = bf16[1024,256]{1,0:T(8,128)(2,1)S(1)} collective-permute-done((bf16[1024,256]{1,0:T(8,128)(2,1)S(1)}, bf16[1024,256]{1,0:T(8,128)(2,1)S(1)}, u32[]{:S(2)}, u32[]{:S(2)}) %collective-permute-start.22) | collective-permute-done | bytes 524320 | tf_op jit(solution)/shard_map/ppermute | solution.py:549
  114.8 5.7 %back_terms.1 = (bf16[2048,256]{1,0:T(8,128)(2,1)S(1)}, bf16[2048,256]{1,0:T(8,128)(2,1)S(1)}, bf16[4096,256]{1,0:T(8,128)(2,1)S(1)}) custom-call(s32[1]{0:T(128)} %bitcast.here.refs_0_, s32[5,32]{1,0:T(8,128)S(1)} %pad_add_fusion.cols, bf16[1024,256]{1,0:T(8,128)(2,1)S(1)} %get-tuple-element.35.refs_0_, ...), custom_call_target="tpu_custom_call" | custom-call | flops 1048576 | bytes 65536 | tf_op jit(solution)/shard_map/back_terms/pallas_call | solution.py:419
  120.4 0.4 collective-permute-start.28
  120.8 0.2 collective-permute-start.27
  121.0 2.1 %collective-permute-done.28.refs_2_ = bf16[2048,256]{1,0:T(8,128)(2,1)S(1)} collective-permute-done((bf16[2048,256]{1,0:T(8,128)(2,1)S(1)}, bf16[2048,256]{1,0:T(8,128)(2,1)S(1)}, u32[]{:S(2)}, u32[]{:S(2)}) %collective-permute-start.28) | collective-permute-done | bytes 1048608 | tf_op jit(solution)/shard_map/ppermute | solution.py:545
  123.2 0.2 sum_terms.24.refs_23_.refs_4_.refs_6_
  123.3 1.7 %collective-permute-start.30 = (bf16[1024,256]{1,0:T(8,128)(2,1)S(1)}, bf16[1024,256]{1,0:T(8,128)(2,1)S(1)}, u32[]{:S(2)}, u32[]{:S(2)}) collective-permute-start(bf16[1024,256]{1,0:T(8,128)(2,1)S(1)} %sum_terms.24.refs_23_.refs_4_.refs_6_), channel_id=1, source_target_pairs={{0,16},{4,20},{8,24},{12,28},{16,0},{20,4},{24,8},{28,12},{1,17},{... | collective-permute-start | bytes 1572872 | tf_op jit(solution)/shard_map/ppermute | solution.py:545
  125.0 0.1 sum_terms.23.refs_22_.refs_3_.refs_5_
  125.2 1.5 collective-permute-start.29
  126.7 0.7 collective-permute-start.33
  127.4 2.7 %collective-permute-start.34 = (bf16[112,256]{1,0:T(8,128)(2,1)S(1)}, bf16[112,256]{1,0:T(8,128)(2,1)S(1)}, u32[]{:S(2)}, u32[]{:S(2)}) collective-permute-start(bf16[112,256]{1,0:T(8,128)(2,1)S(1)} %sum_terms.28.refs_1_), channel_id=1, source_target_pairs={{0,2},{1,3},{2,0},{3,1},{4,6},{5,7},{6,4},{7,5},{8,10},{9,11},{10,... | collective-permute-start | bytes 172040 | tf_op jit(solution)/shard_map/ppermute | solution.py:553
  130.1 2.8 %collective-permute-start.35 = (bf16[112,256]{1,0:T(8,128)(2,1)S(1)}, bf16[112,256]{1,0:T(8,128)(2,1)S(1)}, u32[]{:S(2)}, u32[]{:S(2)}) collective-permute-start(bf16[112,256]{1,0:T(8,128)(2,1)S(1)} %sum_terms.28.refs_1_), channel_id=1, source_target_pairs={{0,3},{1,0},{2,1},{3,2},{4,7},{5,4},{6,5},{7,6},{8,11},{9,8},{10,9... | collective-permute-start | bytes 172040 | tf_op jit(solution)/shard_map/ppermute | solution.py:553
  132.9 1.1 collective-permute-done.34.refs_3_
  134.0 0.7 collective-permute-done.35.refs_4_
  134.8 1.5 %collective-permute-start.38 = (bf16[112,256]{1,0:T(8,128)(2,1)S(1)}, bf16[112,256]{1,0:T(8,128)(2,1)S(1)}, u32[]{:S(2)}, u32[]{:S(2)}) collective-permute-start(bf16[112,256]{1,0:T(8,128)(2,1)S(1)} %sum_terms.29), channel_id=1, source_target_pairs={{0,24},{4,28},{8,16},{12,20},{16,8},{20,12},{24,0},{28,4},{1,25},{... | collective-permute-start | bytes 172040 | tf_op jit(solution)/shard_map/ppermute | solution.py:545
  136.3 1.0 collective-permute-start.37
  137.3 1.0 collective-permute-start.36
  138.4 0.1 sum_terms.25
  138.5 1.1 collective-permute-start.31
  139.5 0.5 collective-permute-done.29.refs_3_.refs_4_
  140.0 0.1 sum_terms.26
  140.1 1.5 %collective-permute-start.32 = (bf16[512,256]{1,0:T(8,128)(2,1)S(1)}, bf16[512,256]{1,0:T(8,128)(2,1)S(1)}, u32[]{:S(2)}, u32[]{:S(2)}) collective-permute-start(bf16[512,256]{1,0:T(8,128)(2,1)S(1)} %sum_terms.26), channel_id=1, source_target_pairs={{0,16},{4,20},{8,24},{12,28},{16,0},{20,4},{24,8},{28,12},{1,17},{... | collective-permute-start | bytes 786440 | tf_op jit(solution)/shard_map/ppermute | solution.py:545
  141.7 0.8 collective-permute-done.36
  142.6 5.0 %tile_grads.3 = (bf16[128,128,128]{2,1,0:T(8,128)(2,1)}, f32[8,128]{1,0:T(8,128)}) custom-call(s32[1]{0:T(128)} %bitcast.here.refs_0_, s32[5,32]{1,0:T(8,128)S(1)} %pad_add_fusion.cols, bf16[1024,256]{1,0:T(8,128)(2,1)S(1)} %get-tuple-element.35.refs_0_, ...), custom_call_target="tpu_custom_call", output_to_operand_aliasing={{0}: (23, {})} | custom-call | flops 1048576 | bytes 65536 | tf_op jit(solution)/shard_map/tile_grads/pallas_call | solution.py:517
  147.6 1.0 weight_unpack.1
  148.5 1.2 sum_terms.27
  (64 shorter events, 0.7 us)
Async XLA Ops:
  0.6 18.9 %collective-permute-start = (bf16[1024,256]{1,0:T(8,128)(2,1)}, bf16[1024,256]{1,0:T(8,128)(2,1)S(1)}, u32[]{:S(2)}, u32[]{:S(2)}) collective-permute-start(bf16[1024,256]{1,0:T(8,128)(2,1)} %nodes.3), channel_id=1, source_target_pairs={{0,4},{4,0},{8,12},{12,8},{16,20},{20,16},{24,28},{28,24},{1,5},{5... | collective-permute-start | bytes 1572872 | tf_op jit(solution)/shard_map/ppermute | solution.py:545
  2.2 9.7 %collective-permute-start.1 = (bf16[512,256]{1,0:T(8,128)(2,1)S(1)}, bf16[512,256]{1,0:T(8,128)(2,1)S(1)}, u32[]{:S(2)}, u32[]{:S(2)}) collective-permute-start(bf16[512,256]{1,0:T(8,128)(2,1)S(1)} %get-tuple-element.55.refs_0_.refs_4_.refs_6_), channel_id=1, source_target_pairs={{0,8},{4,12},{8,0},{12,4},{16,24},{20,28},{24,16},{28,20},{1,9},{5... | collective-permute-start | bytes 786440 | tf_op jit(solution)/shard_map/ppermute | solution.py:545
  4.8 9.1 %collective-permute-start.5 = (bf16[512,256]{1,0:T(8,128)(2,1)S(1)}, bf16[512,256]{1,0:T(8,128)(2,1)S(1)}, u32[]{:S(2)}, u32[]{:S(2)}) collective-permute-start(bf16[512,256]{1,0:T(8,128)(2,1)S(1)} %get-tuple-element.55.refs_0_.refs_4_.refs_6_), channel_id=1, source_target_pairs={{0,16},{4,20},{8,24},{12,28},{16,0},{20,4},{24,8},{28,12},{1,17},{... | collective-permute-start | bytes 786440 | tf_op jit(solution)/shard_map/ppermute | solution.py:545
  6.3 11.3 %collective-permute-start.2 = (bf16[512,256]{1,0:T(8,128)(2,1)S(1)}, bf16[512,256]{1,0:T(8,128)(2,1)S(1)}, u32[]{:S(2)}, u32[]{:S(2)}) collective-permute-start(bf16[512,256]{1,0:T(8,128)(2,1)S(1)} %get-tuple-element.54.refs_1_.refs_5_.refs_7_), channel_id=1, source_target_pairs={{0,8},{4,12},{8,0},{12,4},{16,24},{20,28},{24,16},{28,20},{1,9},{5... | collective-permute-start | bytes 786440 | tf_op jit(solution)/shard_map/ppermute | solution.py:545
  6.8 12.7 %collective-permute-start.6 = (bf16[512,256]{1,0:T(8,128)(2,1)S(1)}, bf16[512,256]{1,0:T(8,128)(2,1)S(1)}, u32[]{:S(2)}, u32[]{:S(2)}) collective-permute-start(bf16[512,256]{1,0:T(8,128)(2,1)S(1)} %get-tuple-element.54.refs_1_.refs_5_.refs_7_), channel_id=1, source_target_pairs={{0,16},{4,20},{8,24},{12,28},{16,0},{20,4},{24,8},{28,12},{1,17},{... | collective-permute-start | bytes 786440 | tf_op jit(solution)/shard_map/ppermute | solution.py:545
  11.9 8.1 %collective-permute-start.3 = (bf16[512,256]{1,0:T(8,128)(2,1)S(1)}, bf16[512,256]{1,0:T(8,128)(2,1)S(1)}, u32[]{:S(2)}, u32[]{:S(2)}) collective-permute-start(bf16[512,256]{1,0:T(8,128)(2,1)S(1)} %collective-permute-done.1.refs_3_.refs_7_.refs_9_), channel_id=1, source_target_pairs={{0,4},{4,0},{8,12},{12,8},{16,20},{20,16},{24,28},{28,24},{1,5},{5... | collective-permute-start | bytes 786440 | tf_op jit(solution)/shard_map/ppermute | solution.py:545
  13.9 9.1 %collective-permute-start.9 = (bf16[512,256]{1,0:T(8,128)(2,1)S(1)}, bf16[512,256]{1,0:T(8,128)(2,1)S(1)}, u32[]{:S(2)}, u32[]{:S(2)}) collective-permute-start(bf16[512,256]{1,0:T(8,128)(2,1)S(1)} %collective-permute-done.5.refs_7_.refs_11_.refs_13_), channel_id=1, source_target_pairs={{0,8},{4,12},{8,0},{12,4},{16,24},{20,28},{24,16},{28,20},{1,9},{5... | collective-permute-start | bytes 786440 | tf_op jit(solution)/shard_map/ppermute | solution.py:545
  17.6 7.9 %collective-permute-start.10 = (bf16[512,256]{1,0:T(8,128)(2,1)S(1)}, bf16[512,256]{1,0:T(8,128)(2,1)S(1)}, u32[]{:S(2)}, u32[]{:S(2)}) collective-permute-start(bf16[512,256]{1,0:T(8,128)(2,1)S(1)} %collective-permute-done.2.refs_4_.refs_8_.refs_10_), channel_id=1, source_target_pairs={{0,16},{4,20},{8,24},{12,28},{16,0},{20,4},{24,8},{28,12},{1,17},{... | collective-permute-start | bytes 786440 | tf_op jit(solution)/shard_map/ppermute | solution.py:545
  19.5 6.7 %collective-permute-start.4 = (bf16[512,256]{1,0:T(8,128)(2,1)S(1)}, bf16[512,256]{1,0:T(8,128)(2,1)S(1)}, u32[]{:S(2)}, u32[]{:S(2)}) collective-permute-start(bf16[512,256]{1,0:T(8,128)(2,1)S(1)} %collective-permute-done.2.refs_4_.refs_8_.refs_10_), channel_id=1, source_target_pairs={{0,4},{4,0},{8,12},{12,8},{16,20},{20,16},{24,28},{28,24},{1,5},{5... | collective-permute-start | bytes 786440 | tf_op jit(solution)/shard_map/ppermute | solution.py:545
  19.5 6.7 %collective-permute-start.7 = (bf16[512,256]{1,0:T(8,128)(2,1)S(1)}, bf16[512,256]{1,0:T(8,128)(2,1)}, u32[]{:S(2)}, u32[]{:S(2)}) collective-permute-start(bf16[512,256]{1,0:T(8,128)(2,1)S(1)} %collective-permute-done.5.refs_7_.refs_11_.refs_13_), channel_id=1, source_target_pairs={{0,4},{4,0},{8,12},{12,8},{16,20},{20,16},{24,28},{28,24},{1,5},{5... | collective-permute-start | bytes 786440 | tf_op jit(solution)/shard_map/ppermute | solution.py:545
  20.1 6.2 %collective-permute-start.8 = (bf16[512,256]{1,0:T(8,128)(2,1)S(1)}, bf16[512,256]{1,0:T(8,128)(2,1)}, u32[]{:S(2)}, u32[]{:S(2)}) collective-permute-start(bf16[512,256]{1,0:T(8,128)(2,1)S(1)} %collective-permute-done.6.refs_8_.refs_12_.refs_14_), channel_id=1, source_target_pairs={{0,4},{4,0},{8,12},{12,8},{16,20},{20,16},{24,28},{28,24},{1,5},{5... | collective-permute-start | bytes 786440 | tf_op jit(solution)/shard_map/ppermute | solution.py:545
  23.0 3.3 %collective-permute-start.11 = (bf16[512,256]{1,0:T(8,128)(2,1)S(1)}, bf16[512,256]{1,0:T(8,128)(2,1)}, u32[]{:S(2)}, u32[]{:S(2)}) collective-permute-start(bf16[512,256]{1,0:T(8,128)(2,1)S(1)} %collective-permute-done.9.refs_11_.refs_15_.refs_17_), channel_id=1, source_target_pairs={{0,4},{4,0},{8,12},{12,8},{16,20},{20,16},{24,28},{28,24},{1,5},{5... | collective-permute-start | bytes 786440 | tf_op jit(solution)/shard_map/ppermute | solution.py:545
  25.5 1.7 %collective-permute-start.12 = (bf16[512,256]{1,0:T(8,128)(2,1)S(1)}, bf16[512,256]{1,0:T(8,128)(2,1)}, u32[]{:S(2)}, u32[]{:S(2)}) collective-permute-start(bf16[512,256]{1,0:T(8,128)(2,1)S(1)} %collective-permute-done.10.refs_12_.refs_16_.refs_18_), channel_id=1, source_target_pairs={{0,4},{4,0},{8,12},{12,8},{16,20},{20,16},{24,28},{28,24},{1,5},{5... | collective-permute-start | bytes 786440 | tf_op jit(solution)/shard_map/ppermute | solution.py:545
  26.2 4.5 %copy-start.1 = (bf16[512,256]{1,0:T(8,128)(2,1)}, bf16[512,256]{1,0:T(8,128)(2,1)S(1)}, u32[]{:S(2)}) copy-start(bf16[512,256]{1,0:T(8,128)(2,1)S(1)} %collective-permute-done.4.refs_6_.refs_10_.refs_12_) | copy-start | bytes 786436
  27.2 5.2 %copy-start = (bf16[32,1,4,128,128]{4,3,2,1,0:T(8,128)(2,1)S(1)}, bf16[32,1,4,128,128]{4,3,2,1,0:T(8,128)(2,1)}, u32[]{:S(2)}) copy-start(bf16[32,1,4,128,128]{4,3,2,1,0:T(8,128)(2,1)} %param.11) | copy-start | bytes 12582916
  30.7 14.8 %collective-permute-start.13 = (bf16[1024,256]{1,0:T(8,128)(2,1)S(1)}, bf16[1024,256]{1,0:T(8,128)(2,1)S(1)}, u32[]{:S(2)}, u32[]{:S(2)}) collective-permute-start(bf16[1024,256]{1,0:T(8,128)(2,1)S(1)} %partial_messages.4.refs_1_), channel_id=1, source_target_pairs={{0,1},{1,0},{2,3},{3,2},{4,5},{5,4},{6,7},{7,6},{8,9},{9,8},{10,11... | collective-permute-start | bytes 1572872 | tf_op jit(solution)/shard_map/ppermute | solution.py:549
  32.4 2.6 %copy-start.2 = (bf16[512,256]{1,0:T(8,128)(2,1)S(1)}, bf16[512,256]{1,0:T(8,128)(2,1)}, u32[]{:S(2)}) copy-start(bf16[512,256]{1,0:T(8,128)(2,1)} %copy-done.1) | copy-start | bytes 786436
  38.1 17.8 %collective-permute-start.16 = (bf16[1024,256]{1,0:T(8,128)(2,1)S(1)}, bf16[1024,256]{1,0:T(8,128)(2,1)S(1)}, u32[]{:S(2)}, u32[]{:S(2)}) collective-permute-start(bf16[1024,256]{1,0:T(8,128)(2,1)S(1)} %partial_messages.5.refs_1_), channel_id=1, source_target_pairs={{0,1},{1,0},{2,3},{3,2},{4,5},{5,4},{6,7},{7,6},{8,9},{9,8},{10,11... | collective-permute-start | bytes 1572872 | tf_op jit(solution)/shard_map/ppermute | solution.py:549
  45.7 25.1 %copy-start.3 = (bf16[1024,256]{1,0:T(8,128)(2,1)S(1)}, bf16[1024,256]{1,0:T(8,128)(2,1)}, u32[]{:S(2)}) copy-start(bf16[1024,256]{1,0:T(8,128)(2,1)} %nodes.3) | copy-start | bytes 1572868
  45.7 25.1 %copy-start.4 = (bf16[1024,256]{1,0:T(8,128)(2,1)S(1)}, bf16[1024,256]{1,0:T(8,128)(2,1)}, u32[]{:S(2)}) copy-start(bf16[1024,256]{1,0:T(8,128)(2,1)} %cot.3) | copy-start | bytes 1572868
  45.7 25.1 %copy-start.5 = (bf16[512,256]{1,0:T(8,128)(2,1)S(1)}, bf16[512,256]{1,0:T(8,128)(2,1)}, u32[]{:S(2)}) copy-start(bf16[512,256]{1,0:T(8,128)(2,1)} %w_in.1) | copy-start | bytes 786436
  45.7 25.1 %copy-start.6 = (bf16[256,256]{1,0:T(8,128)(2,1)S(1)}, bf16[256,256]{1,0:T(8,128)(2,1)}, u32[]{:S(2)}) copy-start(bf16[256,256]{1,0:T(8,128)(2,1)} %refs_5_.1) | copy-start | bytes 393220
  45.7 25.1 %copy-start.7 = (f32[256]{0:T(256)S(1)}, f32[256]{0:T(256)}, u32[]{:S(2)}) copy-start(f32[256]{0:T(256)} %param.15) | copy-start | bytes 3076
  45.7 25.1 %copy-start.8 = (f32[256]{0:T(256)S(1)}, f32[256]{0:T(256)}, u32[]{:S(2)}) copy-start(f32[256]{0:T(256)} %param.17) | copy-start | bytes 3076
  45.7 25.1 %copy-start.9 = (f32[256]{0:T(256)S(1)}, f32[256]{0:T(256)}, u32[]{:S(2)}) copy-start(f32[256]{0:T(256)} %param.18) | copy-start | bytes 3076
  45.7 10.4 %collective-permute-start.14 = (bf16[1024,256]{1,0:T(8,128)(2,1)S(1)}, bf16[1024,256]{1,0:T(8,128)(2,1)S(1)}, u32[]{:S(2)}, u32[]{:S(2)}) collective-permute-start(bf16[1024,256]{1,0:T(8,128)(2,1)S(1)} %sum_terms.15), channel_id=1, source_target_pairs={{0,4},{1,2},{2,1},{3,7},{4,0},{5,6},{6,5},{7,3},{8,12},{9,10},{10,... | collective-permute-start | bytes 1572872 | tf_op jit(solution)/shard_map/ppermute | solution.py:562
  56.1 4.0 %collective-permute-start.17 = (bf16[1024,256]{1,0:T(8,128)(2,1)S(1)}, bf16[1024,256]{1,0:T(8,128)(2,1)S(1)}, u32[]{:S(2)}, u32[]{:S(2)}) collective-permute-start(bf16[1024,256]{1,0:T(8,128)(2,1)S(1)} %sum_terms.17), channel_id=1, source_target_pairs={{0,4},{1,2},{2,1},{3,7},{4,0},{5,6},{6,5},{7,3},{8,12},{9,10},{10,... | collective-permute-start | bytes 1572872 | tf_op jit(solution)/shard_map/ppermute | solution.py:562
  56.4 14.4 %collective-permute-start.15 = (bf16[1024,256]{1,0:T(8,128)(2,1)S(1)}, bf16[1024,256]{1,0:T(8,128)(2,1)S(1)}, u32[]{:S(2)}, u32[]{:S(2)}) collective-permute-start(bf16[1024,256]{1,0:T(8,128)(2,1)S(1)} %sum_terms.16), channel_id=1, source_target_pairs={{0,1},{1,0},{2,3},{3,2},{4,5},{5,4},{6,7},{7,6},{8,9},{9,8},{10,11... | collective-permute-start | bytes 1572872 | tf_op jit(solution)/shard_map/ppermute | solution.py:549
  73.7 11.8 %collective-permute-start.18 = (bf16[1024,256]{1,0:T(8,128)(2,1)S(1)}, bf16[1024,256]{1,0:T(8,128)(2,1)S(1)}, u32[]{:S(2)}, u32[]{:S(2)}) collective-permute-start(bf16[1024,256]{1,0:T(8,128)(2,1)S(1)} %get-tuple-element.35.refs_0_), channel_id=1, source_target_pairs={{0,1},{1,0},{2,3},{3,2},{4,5},{5,4},{6,7},{7,6},{8,9},{9,8},{10,11... | collective-permute-start | bytes 1572872 | tf_op jit(solution)/shard_map/ppermute | solution.py:549
  75.5 10.1 %collective-permute-start.19 = (bf16[1024,256]{1,0:T(8,128)(2,1)S(1)}, bf16[1024,256]{1,0:T(8,128)(2,1)S(1)}, u32[]{:S(2)}, u32[]{:S(2)}) collective-permute-start(bf16[1024,256]{1,0:T(8,128)(2,1)S(1)} %get-tuple-element.35.refs_0_), channel_id=1, source_target_pairs={{0,4},{1,2},{2,1},{3,7},{4,0},{5,6},{6,5},{7,3},{8,12},{9,10},{10,... | collective-permute-start | bytes 1572872 | tf_op jit(solution)/shard_map/ppermute | solution.py:562
  85.5 5.5 %collective-permute-start.21 = (bf16[1024,256]{1,0:T(8,128)(2,1)S(1)}, bf16[1024,256]{1,0:T(8,128)(2,1)S(1)}, u32[]{:S(2)}, u32[]{:S(2)}) collective-permute-start(bf16[1024,256]{1,0:T(8,128)(2,1)S(1)} %collective-permute-done.18.refs_0_.refs_1_), channel_id=1, source_target_pairs={{0,4},{1,2},{2,1},{3,7},{4,0},{5,6},{6,5},{7,3},{8,12},{9,10},{10,... | collective-permute-start | bytes 1572872 | tf_op jit(solution)/shard_map/ppermute | solution.py:562
  86.4 14.4 %collective-permute-start.23 = (f32[448,256]{1,0:T(8,128)S(1)}, f32[448,256]{1,0:T(8,128)S(1)}, u32[]{:S(2)}, u32[]{:S(2)}) collective-permute-start(f32[448,256]{1,0:T(8,128)S(1)} %get-tuple-element.38), channel_id=1, source_target_pairs={{0,4},{4,0},{8,12},{12,8},{16,20},{20,16},{24,28},{28,24},{1,5},{5... | collective-permute-start | bytes 1376264 | tf_op jit(solution)/shard_map/ppermute | solution.py:545
  87.0 17.6 %collective-permute-start.20 = (bf16[1024,256]{1,0:T(8,128)(2,1)S(1)}, bf16[1024,256]{1,0:T(8,128)(2,1)S(1)}, u32[]{:S(2)}, u32[]{:S(2)}) collective-permute-start(bf16[1024,256]{1,0:T(8,128)(2,1)S(1)} %collective-permute-done.19.refs_1_.refs_2_), channel_id=1, source_target_pairs={{0,1},{1,0},{2,3},{3,2},{4,5},{5,4},{6,7},{7,6},{8,9},{9,8},{10,11... | collective-permute-start | bytes 1572872 | tf_op jit(solution)/shard_map/ppermute | solution.py:549
  91.0 23.7 %collective-permute-start.22 = (bf16[1024,256]{1,0:T(8,128)(2,1)S(1)}, bf16[1024,256]{1,0:T(8,128)(2,1)S(1)}, u32[]{:S(2)}, u32[]{:S(2)}) collective-permute-start(bf16[1024,256]{1,0:T(8,128)(2,1)S(1)} %collective-permute-done.21.refs_19_.refs_4_), channel_id=1, source_target_pairs={{0,1},{1,0},{2,3},{3,2},{4,5},{5,4},{6,7},{7,6},{8,9},{9,8},{10,11... | collective-permute-start | bytes 1572872 | tf_op jit(solution)/shard_map/ppermute | solution.py:549
  100.8 10.2 %collective-permute-start.24 = (f32[112,256]{1,0:T(8,128)S(1)}, f32[112,256]{1,0:T(8,128)S(1)}, u32[]{:S(2)}, u32[]{:S(2)}) collective-permute-start(f32[112,256]{1,0:T(8,128)S(1)} %sum_terms.19), channel_id=1, source_target_pairs={{0,16},{4,20},{8,24},{12,28},{16,0},{20,4},{24,8},{28,12},{1,17},{... | collective-permute-start | bytes 344072 | tf_op jit(solution)/shard_map/ppermute | solution.py:545
  102.4 8.6 %collective-permute-start.25 = (f32[112,256]{1,0:T(8,128)S(1)}, f32[112,256]{1,0:T(8,128)S(1)}, u32[]{:S(2)}, u32[]{:S(2)}) collective-permute-start(f32[112,256]{1,0:T(8,128)S(1)} %sum_terms.20), channel_id=1, source_target_pairs={{0,8},{4,12},{8,0},{12,4},{16,24},{20,28},{24,16},{28,20},{1,9},{5... | collective-permute-start | bytes 344072 | tf_op jit(solution)/shard_map/ppermute | solution.py:545
  104.0 7.1 %collective-permute-start.26 = (f32[112,256]{1,0:T(8,128)S(1)}, f32[112,256]{1,0:T(8,128)S(1)}, u32[]{:S(2)}, u32[]{:S(2)}) collective-permute-start(f32[112,256]{1,0:T(8,128)S(1)} %sum_terms.21), channel_id=1, source_target_pairs={{0,24},{4,28},{8,16},{12,20},{16,8},{20,12},{24,0},{28,4},{1,25},{... | collective-permute-start | bytes 344072 | tf_op jit(solution)/shard_map/ppermute | solution.py:545
  120.4 2.7 %collective-permute-start.28 = (bf16[2048,256]{1,0:T(8,128)(2,1)S(1)}, bf16[2048,256]{1,0:T(8,128)(2,1)S(1)}, u32[]{:S(2)}, u32[]{:S(2)}) collective-permute-start(bf16[2048,256]{1,0:T(8,128)(2,1)S(1)} %get-tuple-element.42), channel_id=1, source_target_pairs={{0,4},{4,0},{8,12},{12,8},{16,20},{20,16},{24,28},{28,24},{1,5},{5... | collective-permute-start | bytes 3145736 | tf_op jit(solution)/shard_map/ppermute | solution.py:545
  120.8 5.8 %collective-permute-start.27 = (bf16[2048,256]{1,0:T(8,128)(2,1)S(1)}, bf16[2048,256]{1,0:T(8,128)(2,1)S(1)}, u32[]{:S(2)}, u32[]{:S(2)}) collective-permute-start(bf16[2048,256]{1,0:T(8,128)(2,1)S(1)} %get-tuple-element.41), channel_id=1, source_target_pairs={{0,4},{4,0},{8,12},{12,8},{16,20},{20,16},{24,28},{28,24},{1,5},{5... | collective-permute-start | bytes 3145736 | tf_op jit(solution)/shard_map/ppermute | solution.py:545
  123.3 15.0 %collective-permute-start.30 = (bf16[1024,256]{1,0:T(8,128)(2,1)S(1)}, bf16[1024,256]{1,0:T(8,128)(2,1)S(1)}, u32[]{:S(2)}, u32[]{:S(2)}) collective-permute-start(bf16[1024,256]{1,0:T(8,128)(2,1)S(1)} %sum_terms.24.refs_23_.refs_4_.refs_6_), channel_id=1, source_target_pairs={{0,16},{4,20},{8,24},{12,28},{16,0},{20,4},{24,8},{28,12},{1,17},{... | collective-permute-start | bytes 1572872 | tf_op jit(solution)/shard_map/ppermute | solution.py:545
  125.2 14.9 %collective-permute-start.29 = (bf16[1024,256]{1,0:T(8,128)(2,1)S(1)}, bf16[1024,256]{1,0:T(8,128)(2,1)S(1)}, u32[]{:S(2)}, u32[]{:S(2)}) collective-permute-start(bf16[1024,256]{1,0:T(8,128)(2,1)S(1)} %sum_terms.23.refs_22_.refs_3_.refs_5_), channel_id=1, source_target_pairs={{0,8},{4,12},{8,0},{12,4},{16,24},{20,28},{24,16},{28,20},{1,9},{5... | collective-permute-start | bytes 1572872 | tf_op jit(solution)/shard_map/ppermute | solution.py:545
  126.7 6.3 %collective-permute-start.33 = (bf16[112,256]{1,0:T(8,128)(2,1)S(1)}, bf16[112,256]{1,0:T(8,128)(2,1)S(1)}, u32[]{:S(2)}, u32[]{:S(2)}) collective-permute-start(bf16[112,256]{1,0:T(8,128)(2,1)S(1)} %sum_terms.28.refs_1_), channel_id=1, source_target_pairs={{0,1},{1,2},{2,3},{3,0},{4,5},{5,6},{6,7},{7,4},{8,9},{9,10},{10,1... | collective-permute-start | bytes 172040 | tf_op jit(solution)/shard_map/ppermute | solution.py:553
  127.4 6.6 %collective-permute-start.34 = (bf16[112,256]{1,0:T(8,128)(2,1)S(1)}, bf16[112,256]{1,0:T(8,128)(2,1)S(1)}, u32[]{:S(2)}, u32[]{:S(2)}) collective-permute-start(bf16[112,256]{1,0:T(8,128)(2,1)S(1)} %sum_terms.28.refs_1_), channel_id=1, source_target_pairs={{0,2},{1,3},{2,0},{3,1},{4,6},{5,7},{6,4},{7,5},{8,10},{9,11},{10,... | collective-permute-start | bytes 172040 | tf_op jit(solution)/shard_map/ppermute | solution.py:553
  130.1 4.7 %collective-permute-start.35 = (bf16[112,256]{1,0:T(8,128)(2,1)S(1)}, bf16[112,256]{1,0:T(8,128)(2,1)S(1)}, u32[]{:S(2)}, u32[]{:S(2)}) collective-permute-start(bf16[112,256]{1,0:T(8,128)(2,1)S(1)} %sum_terms.28.refs_1_), channel_id=1, source_target_pairs={{0,3},{1,0},{2,1},{3,2},{4,7},{5,4},{6,5},{7,6},{8,11},{9,8},{10,9... | collective-permute-start | bytes 172040 | tf_op jit(solution)/shard_map/ppermute | solution.py:553
  134.8 6.9 %collective-permute-start.38 = (bf16[112,256]{1,0:T(8,128)(2,1)S(1)}, bf16[112,256]{1,0:T(8,128)(2,1)S(1)}, u32[]{:S(2)}, u32[]{:S(2)}) collective-permute-start(bf16[112,256]{1,0:T(8,128)(2,1)S(1)} %sum_terms.29), channel_id=1, source_target_pairs={{0,24},{4,28},{8,16},{12,20},{16,8},{20,12},{24,0},{28,4},{1,25},{... | collective-permute-start | bytes 172040 | tf_op jit(solution)/shard_map/ppermute | solution.py:545
  136.3 5.3 %collective-permute-start.37 = (bf16[112,256]{1,0:T(8,128)(2,1)S(1)}, bf16[112,256]{1,0:T(8,128)(2,1)S(1)}, u32[]{:S(2)}, u32[]{:S(2)}) collective-permute-start(bf16[112,256]{1,0:T(8,128)(2,1)S(1)} %sum_terms.29), channel_id=1, source_target_pairs={{0,16},{4,20},{8,24},{12,28},{16,0},{20,4},{24,8},{28,12},{1,17},{... | collective-permute-start | bytes 172040 | tf_op jit(solution)/shard_map/ppermute | solution.py:545
  137.3 5.2 %collective-permute-start.36 = (bf16[112,256]{1,0:T(8,128)(2,1)S(1)}, bf16[112,256]{1,0:T(8,128)(2,1)S(1)}, u32[]{:S(2)}, u32[]{:S(2)}) collective-permute-start(bf16[112,256]{1,0:T(8,128)(2,1)S(1)} %sum_terms.29), channel_id=1, source_target_pairs={{0,8},{4,12},{8,0},{12,4},{16,24},{20,28},{24,16},{28,20},{1,9},{5... | collective-permute-start | bytes 172040 | tf_op jit(solution)/shard_map/ppermute | solution.py:545
  138.5 10.1 %collective-permute-start.31 = (bf16[512,256]{1,0:T(8,128)(2,1)S(1)}, bf16[512,256]{1,0:T(8,128)(2,1)S(1)}, u32[]{:S(2)}, u32[]{:S(2)}) collective-permute-start(bf16[512,256]{1,0:T(8,128)(2,1)S(1)} %sum_terms.25), channel_id=1, source_target_pairs={{0,8},{4,12},{8,0},{12,4},{16,24},{20,28},{24,16},{28,20},{1,9},{5... | collective-permute-start | bytes 786440 | tf_op jit(solution)/shard_map/ppermute | solution.py:545
  140.1 8.4 %collective-permute-start.32 = (bf16[512,256]{1,0:T(8,128)(2,1)S(1)}, bf16[512,256]{1,0:T(8,128)(2,1)S(1)}, u32[]{:S(2)}, u32[]{:S(2)}) collective-permute-start(bf16[512,256]{1,0:T(8,128)(2,1)S(1)} %sum_terms.26), channel_id=1, source_target_pairs={{0,16},{4,20},{8,24},{12,28},{16,0},{20,4},{24,8},{28,12},{1,17},{... | collective-permute-start | bytes 786440 | tf_op jit(solution)/shard_map/ppermute | solution.py:545
  142.5 5.1 %collective-permute-start.39 = (bf16[448,256]{1,0:T(8,128)(2,1)S(1)}, bf16[448,256]{1,0:T(8,128)(2,1)S(1)}, u32[]{:S(2)}, u32[]{:S(2)}) collective-permute-start(bf16[448,256]{1,0:T(8,128)(2,1)S(1)} %pad_maximum_fusion.even), channel_id=1, source_target_pairs={{0,4},{4,0},{8,12},{12,8},{16,20},{20,16},{24,28},{28,24},{1,5},{5... | collective-permute-start | bytes 688136 | tf_op jit(solution)/shard_map/ppermute | solution.py:545

commit v18 on v16

--- a/solution.py
+++ b/solution.py
@@ -19,7 +19,7 @@
 SMALL = pl.CostEstimate(flops=1 << 20, bytes_accessed=1 << 16, transcendentals=0)
 
 
-LIVE_STEP = 4
+LIVE_STEPS = (8, 2, 1)
 GRAD_PLAN = ((3, 0, None), (2, 1, None), (1, 2, "inner"), (1, 3, "outer"), (0, 4, "inner"), (0, 5, "outer"))
 SWAP_ORDER = (0, 4, 2, 6, 1, 5, 3, 7)
 
@@ -324,18 +324,18 @@
 
 
 def for_live(first, last, entry):
-    def several(i, carry):
-        for index in range(LIVE_STEP):
-            entry(first + i * LIVE_STEP + index)
-        return carry
-
-    def one(i, carry):
-        entry(i)
-        return carry
-
-    full = jnp.maximum(last - first, 0) // LIVE_STEP
-    lax.fori_loop(0, full, several, 0)
-    lax.fori_loop(first + full * LIVE_STEP, last, one, 0)
+    def several(many, start):
+        def run(i, carry):
+            for index in range(many):
+                entry(start + i * many + index)
+            return carry
+
+        return run
+
+    for many in LIVE_STEPS:
+        times = jnp.maximum(last - first, 0) // many
+        lax.fori_loop(0, times, several(many, first), 0)
+        first = first + times * many
 
 
 def turn_kernel(slots, cols, tiles, out, tiles_v, live, sem):

time: 149 us -> 148 us (level)
  Pallas kernels: 36.8 us -> 34.5 us
  transfers between devices with their start and end apart: 40 -> 40, of which waited for: 16 -> 17; matrix products, arithmetic and copies ran while one was open for 1% -> 1% of each run, Pallas kernels for 16% -> 15%
where the time goes in v18:
time: 148 us
  waiting for transfers between devices  63 us (43%)
  starting transfers between devices  47.2 us (32%)
  Pallas kernels  34.5 us (23%)
    ppermute x6, waiting for transfers between devices, outer_swap(): return lax.ppermute(value, 'col', [(0, 1), (1, 0), (2, 3), (3, 2)])  39 us
    ppermute x27, waiting for transfers between devices, swap(): return lax.ppermute(value, 'row', [(i, i ^ bit) for i in range(8)])  24 us
    ppermute x6, starting transfers between devices, outer_swap(): return lax.ppermute(value, 'col', [(0, 1), (1, 0), (2, 3), (3, 2)])  21 us
    ppermute x27, starting transfers between devices, swap(): return lax.ppermute(value, 'row', [(i, i ^ bit) for i in range(8)])  20.8 us
    pallas_call x3, Pallas kernels, forward_call(): pl.pallas_call(functools.partial(forward_kernel, outputs, len(pieces), pa...  10.4 us
    pallas_call x2, Pallas kernels, tile_grad_call(): pl.pallas_call(functools.partial(tile_grad_kernel, rows, slots, len(grads...  9.78 us
    ppermute x3, starting transfers between devices, turn(): return lax.ppermute(value, 'col', [(i, (i + by) % 4) for i in range(4)])  5.29 us
    pallas_call x1, Pallas kernels, back_call(): pl.pallas_call(functools.partial(back_kernel, rows, slots, len(grads), le...  4.99 us
  transfers between devices with their start and end apart: 40, of which 17 were waited for; matrix products, arithmetic and copies ran while one was open for 1% of the time, Pallas kernels for 15%

profile of v18, /device:TPU:0, one launch (start us, length us, event | category | flops | bytes accessed | tf_op | source)
XLA Modules:
  0.0 147.7 jit_solution(13400332481689673732)
XLA Ops:
  0.6 0.5 collective-permute-start
  1.1 1.1 fusion
  2.2 2.6 %collective-permute-start.1 = (bf16[512,256]{1,0:T(8,128)(2,1)S(1)}, bf16[512,256]{1,0:T(8,128)(2,1)S(1)}, u32[]{:S(2)}, u32[]{:S(2)}) collective-permute-start(bf16[512,256]{1,0:T(8,128)(2,1)S(1)} %get-tuple-element.57.refs_0_.refs_4_.refs_6_), channel_id=1, source_target_pairs={{0,8},{4,12},{8,0},{12,4},{16,24},{20,28},{24,16},{28,20},{1,9},{5... | collective-permute-start | bytes 786440 | tf_op jit(solution)/shard_map/ppermute | solution.py:545
  4.8 1.5 %collective-permute-start.5 = (bf16[512,256]{1,0:T(8,128)(2,1)S(1)}, bf16[512,256]{1,0:T(8,128)(2,1)S(1)}, u32[]{:S(2)}, u32[]{:S(2)}) collective-permute-start(bf16[512,256]{1,0:T(8,128)(2,1)S(1)} %get-tuple-element.57.refs_0_.refs_4_.refs_6_), channel_id=1, source_target_pairs={{0,16},{4,20},{8,24},{12,28},{16,0},{20,4},{24,8},{28,12},{1,17},{... | collective-permute-start | bytes 786440 | tf_op jit(solution)/shard_map/ppermute | solution.py:545
  6.3 0.5 collective-permute-start.2
  6.9 5.1 %collective-permute-done.1.refs_3_.refs_7_.refs_9_ = bf16[512,256]{1,0:T(8,128)(2,1)S(1)} collective-permute-done((bf16[512,256]{1,0:T(8,128)(2,1)S(1)}, bf16[512,256]{1,0:T(8,128)(2,1)S(1)}, u32[]{:S(2)}, u32[]{:S(2)}) %collective-permute-start.1) | collective-permute-done | bytes 262176 | tf_op jit(solution)/shard_map/ppermute | solution.py:545
  11.9 2.0 %collective-permute-done.5.refs_7_.refs_11_.refs_13_ = bf16[512,256]{1,0:T(8,128)(2,1)S(1)} collective-permute-done((bf16[512,256]{1,0:T(8,128)(2,1)S(1)}, bf16[512,256]{1,0:T(8,128)(2,1)S(1)}, u32[]{:S(2)}, u32[]{:S(2)}) %collective-permute-start.5) | collective-permute-done | bytes 262176 | tf_op jit(solution)/shard_map/ppermute | solution.py:545
  14.0 3.6 %collective-permute-done.2.refs_4_.refs_8_.refs_10_ = bf16[512,256]{1,0:T(8,128)(2,1)S(1)} collective-permute-done((bf16[512,256]{1,0:T(8,128)(2,1)S(1)}, bf16[512,256]{1,0:T(8,128)(2,1)S(1)}, u32[]{:S(2)}, u32[]{:S(2)}) %collective-permute-start.2) | collective-permute-done | bytes 262176 | tf_op jit(solution)/shard_map/ppermute | solution.py:545
  17.6 2.0 %collective-permute-start.10 = (bf16[512,256]{1,0:T(8,128)(2,1)S(1)}, bf16[512,256]{1,0:T(8,128)(2,1)S(1)}, u32[]{:S(2)}, u32[]{:S(2)}) collective-permute-start(bf16[512,256]{1,0:T(8,128)(2,1)S(1)} %collective-permute-done.2.refs_4_.refs_8_.refs_10_), channel_id=1, source_target_pairs={{0,16},{4,20},{8,24},{12,28},{16,0},{20,4},{24,8},{28,12},{1,17},{... | collective-permute-start | bytes 786440 | tf_op jit(solution)/shard_map/ppermute | solution.py:545
  19.5 0.5 collective-permute-start.7
  20.1 2.9 %collective-permute-done.9.refs_11_.refs_15_.refs_17_ = bf16[512,256]{1,0:T(8,128)(2,1)S(1)} collective-permute-done((bf16[512,256]{1,0:T(8,128)(2,1)S(1)}, bf16[512,256]{1,0:T(8,128)(2,1)S(1)}, u32[]{:S(2)}, u32[]{:S(2)}) %collective-permute-start.9) | collective-permute-done | bytes 262176 | tf_op jit(solution)/shard_map/ppermute | solution.py:545
  23.0 2.5 %collective-permute-done.10.refs_12_.refs_16_.refs_18_ = bf16[512,256]{1,0:T(8,128)(2,1)S(1)} collective-permute-done((bf16[512,256]{1,0:T(8,128)(2,1)S(1)}, bf16[512,256]{1,0:T(8,128)(2,1)S(1)}, u32[]{:S(2)}, u32[]{:S(2)}) %collective-permute-start.10) | collective-permute-done | bytes 262176 | tf_op jit(solution)/shard_map/ppermute | solution.py:545
  25.5 0.7 pad_add_fusion.cols
  26.2 0.9 collective-permute-done.12.refs_14_.refs_18_.refs_20_
  27.2 3.5 %partial_messages.4.refs_1_ = bf16[1024,256]{1,0:T(8,128)(2,1)S(1)} custom-call(s32[1]{0:T(128)} %bitcast.here.refs_0_, s32[5,32]{1,0:T(8,128)S(1)} %pad_add_fusion.cols, bf16[512,256]{1,0:T(8,128)(2,1)S(1)} %get-tuple-element.57.refs_0_.refs_4_.refs_6_, bf16[512,256]{1,0:T(8,128)(2,1)S(1)} %get-tuple-element.56.refs_1_.refs_5_.refs_7_, ...), custom_call_target="tpu_custom_call" | custom-call | flops 1048576 | bytes 65536 | tf_op jit(solution)/shard_map/partial_messages/pallas_call | solution.py:132
  30.7 1.7 %collective-permute-start.13 = (bf16[1024,256]{1,0:T(8,128)(2,1)S(1)}, bf16[1024,256]{1,0:T(8,128)(2,1)S(1)}, u32[]{:S(2)}, u32[]{:S(2)}) collective-permute-start(bf16[1024,256]{1,0:T(8,128)(2,1)S(1)} %partial_messages.4.refs_1_), channel_id=1, source_target_pairs={{0,1},{1,0},{2,3},{3,2},{4,5},{5,4},{6,7},{7,6},{8,9},{9,8},{10,11... | collective-permute-start | bytes 1572872 | tf_op jit(solution)/shard_map/ppermute | solution.py:549
  32.4 2.4 %turned_tiles.1.refs_3_.refs_6_ = bf16[128,128,128]{2,1,0:T(8,128)(2,1)S(1)} custom-call(s32[5,32]{1,0:T(8,128)S(1)} %pad_add_fusion.cols, bf16[128,128,128]{2,1,0:T(8,128)(2,1)S(1)} %bitcast.16), custom_call_target="tpu_custom_call" | custom-call | flops 1048576 | bytes 65536 | tf_op jit(solution)/shard_map/turned_tiles/pallas_call | solution.py:364
  34.7 3.1 %partial_messages.5.refs_1_ = bf16[1024,256]{1,0:T(8,128)(2,1)S(1)} custom-call(s32[1]{0:T(128)} %bitcast.here.refs_0_, s32[5,32]{1,0:T(8,128)S(1)} %pad_add_fusion.cols, bf16[512,256]{1,0:T(8,128)(2,1)S(1)} %get-tuple-element.57.refs_0_.refs_4_.refs_6_, bf16[512,256]{1,0:T(8,128)(2,1)S(1)} %get-tuple-element.56.refs_1_.refs_5_.refs_7_, ...), custom_call_target="tpu_custom_call" | custom-call | flops 1048576 | bytes 65536 | tf_op jit(solution)/shard_map/partial_messages/pallas_call | solution.py:132
  37.9 0.1 collective-permute-start.16
  38.0 7.5 %collective-permute-done.13.refs_2_ = bf16[1024,256]{1,0:T(8,128)(2,1)S(1)} collective-permute-done((bf16[1024,256]{1,0:T(8,128)(2,1)S(1)}, bf16[1024,256]{1,0:T(8,128)(2,1)S(1)}, u32[]{:S(2)}, u32[]{:S(2)}) %collective-permute-start.13) | collective-permute-done | bytes 524320 | tf_op jit(solution)/shard_map/ppermute | solution.py:549
  45.5 0.1 sum_terms.15
  45.8 3.7 %partial_messages.3 = (bf16[1024,256]{1,0:T(8,128)(2,1)S(1)}, bf16[1024,256]{1,0:T(8,128)(2,1)S(1)}) custom-call(s32[1]{0:T(128)} %bitcast.here.refs_0_, s32[5,32]{1,0:T(8,128)S(1)} %pad_add_fusion.cols, bf16[512,256]{1,0:T(8,128)(2,1)S(1)} %get-tuple-element.57.refs_0_.refs_4_.refs_6_, bf16[512,256]{1,0:T(8,128)(2,1)S(1)} %get-tuple-element.56.refs_1_.refs_5_.refs_7_, ...), custom_call_target="tpu_custom_call" | custom-call | flops 1048576 | bytes 65536 | tf_op jit(solution)/shard_map/partial_messages/pallas_call | solution.py:132
  49.6 6.4 %collective-permute-done.16.refs_2_ = bf16[1024,256]{1,0:T(8,128)(2,1)S(1)} collective-permute-done((bf16[1024,256]{1,0:T(8,128)(2,1)S(1)}, bf16[1024,256]{1,0:T(8,128)(2,1)S(1)}, u32[]{:S(2)}, u32[]{:S(2)}) %collective-permute-start.16) | collective-permute-done | bytes 524320 | tf_op jit(solution)/shard_map/ppermute | solution.py:549
  55.9 0.1 sum_terms.17
  56.2 0.2 sum_terms.16
  56.4 3.6 %collective-permute-start.15 = (bf16[1024,256]{1,0:T(8,128)(2,1)S(1)}, bf16[1024,256]{1,0:T(8,128)(2,1)S(1)}, u32[]{:S(2)}, u32[]{:S(2)}) collective-permute-start(bf16[1024,256]{1,0:T(8,128)(2,1)S(1)} %sum_terms.16), channel_id=1, source_target_pairs={{0,1},{1,0},{2,3},{3,2},{4,5},{5,4},{6,7},{7,6},{8,9},{9,8},{10,11... | collective-permute-start | bytes 1572872 | tf_op jit(solution)/shard_map/ppermute | solution.py:549
  60.0 10.7 %collective-permute-done.15.refs_1_ = bf16[1024,256]{1,0:T(8,128)(2,1)S(1)} collective-permute-done((bf16[1024,256]{1,0:T(8,128)(2,1)S(1)}, bf16[1024,256]{1,0:T(8,128)(2,1)S(1)}, u32[]{:S(2)}, u32[]{:S(2)}) %collective-permute-start.15) | collective-permute-done | bytes 524320 | tf_op jit(solution)/shard_map/ppermute | solution.py:549
  70.8 2.9 %mlp.1 = (bf16[1024,256]{1,0:T(8,128)(2,1)}, bf16[1024,256]{1,0:T(8,128)(2,1)S(1)}, bf16[1024,256]{1,0:T(8,128)(2,1)S(1)}, bf16[1024,256]{1,0:T(8,128)(2,1)S(1)}...) custom-call(s32[1]{0:T(128)} %bitcast.here.refs_0_, ...), custom_call_target="tpu_custom_call" | custom-call | flops 1048576 | bytes 65536 | tf_op jit(solution)/shard_map/mlp/pallas_call | solution.py:218
  73.7 1.7 %collective-permute-start.18 = (bf16[1024,256]{1,0:T(8,128)(2,1)S(1)}, bf16[1024,256]{1,0:T(8,128)(2,1)S(1)}, u32[]{:S(2)}, u32[]{:S(2)}) collective-permute-start(bf16[1024,256]{1,0:T(8,128)(2,1)S(1)} %get-tuple-element.36.refs_0_), channel_id=1, source_target_pairs={{0,1},{1,0},{2,3},{3,2},{4,5},{5,4},{6,7},{7,6},{8,9},{9,8},{10,11... | collective-permute-start | bytes 1572872 | tf_op jit(solution)/shard_map/ppermute | solution.py:549
  75.5 10.1 %collective-permute-done.18.refs_0_.refs_1_ = bf16[1024,256]{1,0:T(8,128)(2,1)S(1)} collective-permute-done((bf16[1024,256]{1,0:T(8,128)(2,1)S(1)}, bf16[1024,256]{1,0:T(8,128)(2,1)S(1)}, u32[]{:S(2)}, u32[]{:S(2)}) %collective-permute-start.18) | collective-permute-done | bytes 524320 | tf_op jit(solution)/shard_map/ppermute | solution.py:549
  85.5 0.8 weight_grads.1
  86.4 0.6 collective-permute-start.23
  87.0 4.1 %collective-permute-start.20 = (bf16[1024,256]{1,0:T(8,128)(2,1)S(1)}, bf16[1024,256]{1,0:T(8,128)(2,1)S(1)}, u32[]{:S(2)}, u32[]{:S(2)}) collective-permute-start(bf16[1024,256]{1,0:T(8,128)(2,1)S(1)} %collective-permute-done.19.refs_1_.refs_2_), channel_id=1, source_target_pairs={{0,1},{1,0},{2,3},{3,2},{4,5},{5,4},{6,7},{7,6},{8,9},{9,8},{10,11... | collective-permute-start | bytes 1572872 | tf_op jit(solution)/shard_map/ppermute | solution.py:549
  91.0 9.8 %collective-permute-start.22 = (bf16[1024,256]{1,0:T(8,128)(2,1)S(1)}, bf16[1024,256]{1,0:T(8,128)(2,1)S(1)}, u32[]{:S(2)}, u32[]{:S(2)}) collective-permute-start(bf16[1024,256]{1,0:T(8,128)(2,1)S(1)} %collective-permute-done.21.refs_19_.refs_4_), channel_id=1, source_target_pairs={{0,1},{1,0},{2,3},{3,2},{4,5},{5,4},{6,7},{7,6},{8,9},{9,8},{10,11... | collective-permute-start | bytes 1572872 | tf_op jit(solution)/shard_map/ppermute | solution.py:549
  100.8 1.6 %collective-permute-start.24 = (f32[112,256]{1,0:T(8,128)S(1)}, f32[112,256]{1,0:T(8,128)S(1)}, u32[]{:S(2)}, u32[]{:S(2)}) collective-permute-start(f32[112,256]{1,0:T(8,128)S(1)} %sum_terms.19), channel_id=1, source_target_pairs={{0,16},{4,20},{8,24},{12,28},{16,0},{20,4},{24,8},{28,12},{1,17},{... | collective-permute-start | bytes 344072 | tf_op jit(solution)/shard_map/ppermute | solution.py:545
  102.4 1.6 %collective-permute-start.25 = (f32[112,256]{1,0:T(8,128)S(1)}, f32[112,256]{1,0:T(8,128)S(1)}, u32[]{:S(2)}, u32[]{:S(2)}) collective-permute-start(f32[112,256]{1,0:T(8,128)S(1)} %sum_terms.20), channel_id=1, source_target_pairs={{0,8},{4,12},{8,0},{12,4},{16,24},{20,28},{24,16},{28,20},{1,9},{5... | collective-permute-start | bytes 344072 | tf_op jit(solution)/shard_map/ppermute | solution.py:545
  104.0 0.5 collective-permute-start.26
  104.6 5.9 %tile_grads.2 = (bf16[128,128,128]{2,1,0:T(8,128)(2,1)}, f32[8,128]{1,0:T(8,128)S(1)}) custom-call(s32[1]{0:T(128)} %bitcast.here.refs_0_, s32[5,32]{1,0:T(8,128)S(1)} %pad_add_fusion.cols, bf16[1024,256]{1,0:T(8,128)(2,1)S(1)} %get-tuple-element.36.refs_0_, bf16[1024,256]{1,0:T(8,128)(2,1)S(1)} %collective-permute-done.18.refs_0_.refs_1_, ...), custom_call_target="tpu_custom_call" | custom-call | flops 1048576 | bytes 65536 | tf_op jit(solution)/shard_map/tile_grads/pallas_call | solution.py:517
  110.5 4.3 %collective-permute-done.22.refs_5_ = bf16[1024,256]{1,0:T(8,128)(2,1)S(1)} collective-permute-done((bf16[1024,256]{1,0:T(8,128)(2,1)S(1)}, bf16[1024,256]{1,0:T(8,128)(2,1)S(1)}, u32[]{:S(2)}, u32[]{:S(2)}) %collective-permute-start.22) | collective-permute-done | bytes 524320 | tf_op jit(solution)/shard_map/ppermute | solution.py:549
  114.8 5.0 %back_terms.1 = (bf16[2048,256]{1,0:T(8,128)(2,1)S(1)}, bf16[2048,256]{1,0:T(8,128)(2,1)S(1)}, bf16[4096,256]{1,0:T(8,128)(2,1)S(1)}) custom-call(s32[1]{0:T(128)} %bitcast.here.refs_0_, s32[5,32]{1,0:T(8,128)S(1)} %pad_add_fusion.cols, bf16[1024,256]{1,0:T(8,128)(2,1)S(1)} %get-tuple-element.36.refs_0_, ...), custom_call_target="tpu_custom_call" | custom-call | flops 1048576 | bytes 65536 | tf_op jit(solution)/shard_map/back_terms/pallas_call | solution.py:419
  119.9 0.5 collective-permute-start.27
  120.4 2.1 %collective-permute-done.28.refs_2_ = bf16[2048,256]{1,0:T(8,128)(2,1)S(1)} collective-permute-done((bf16[2048,256]{1,0:T(8,128)(2,1)S(1)}, bf16[2048,256]{1,0:T(8,128)(2,1)S(1)}, u32[]{:S(2)}, u32[]{:S(2)}) %collective-permute-start.28) | collective-permute-done | bytes 1048608 | tf_op jit(solution)/shard_map/ppermute | solution.py:545
  122.5 0.2 sum_terms.24.refs_23_.refs_4_
  122.7 1.2 collective-permute-start.30
  123.8 0.2 sum_terms.23.refs_22_.refs_3_
  124.0 2.1 %collective-permute-start.29 = (bf16[1024,256]{1,0:T(8,128)(2,1)S(1)}, bf16[1024,256]{1,0:T(8,128)(2,1)S(1)}, u32[]{:S(2)}, u32[]{:S(2)}) collective-permute-start(bf16[1024,256]{1,0:T(8,128)(2,1)S(1)} %sum_terms.23.refs_22_.refs_3_), channel_id=1, source_target_pairs={{0,8},{4,12},{8,0},{12,4},{16,24},{20,28},{24,16},{28,20},{1,9},{5... | collective-permute-start | bytes 1572872 | tf_op jit(solution)/shard_map/ppermute | solution.py:545
  126.1 1.6 %collective-permute-start.33 = (bf16[112,256]{1,0:T(8,128)(2,1)S(1)}, bf16[112,256]{1,0:T(8,128)(2,1)S(1)}, u32[]{:S(2)}, u32[]{:S(2)}) collective-permute-start(bf16[112,256]{1,0:T(8,128)(2,1)S(1)} %sum_terms.28.refs_1_), channel_id=1, source_target_pairs={{0,1},{1,2},{2,3},{3,0},{4,5},{5,6},{6,7},{7,4},{8,9},{9,10},{10,1... | collective-permute-start | bytes 172040 | tf_op jit(solution)/shard_map/ppermute | solution.py:553
  127.7 1.8 %collective-permute-start.34 = (bf16[112,256]{1,0:T(8,128)(2,1)S(1)}, bf16[112,256]{1,0:T(8,128)(2,1)S(1)}, u32[]{:S(2)}, u32[]{:S(2)}) collective-permute-start(bf16[112,256]{1,0:T(8,128)(2,1)S(1)} %sum_terms.28.refs_1_), channel_id=1, source_target_pairs={{0,2},{1,3},{2,0},{3,1},{4,6},{5,7},{6,4},{7,5},{8,10},{9,11},{10,... | collective-permute-start | bytes 172040 | tf_op jit(solution)/shard_map/ppermute | solution.py:553
  129.5 1.9 %collective-permute-start.35 = (bf16[112,256]{1,0:T(8,128)(2,1)S(1)}, bf16[112,256]{1,0:T(8,128)(2,1)S(1)}, u32[]{:S(2)}, u32[]{:S(2)}) collective-permute-start(bf16[112,256]{1,0:T(8,128)(2,1)S(1)} %sum_terms.28.refs_1_), channel_id=1, source_target_pairs={{0,3},{1,0},{2,1},{3,2},{4,7},{5,4},{6,5},{7,6},{8,11},{9,8},{10,9... | collective-permute-start | bytes 172040 | tf_op jit(solution)/shard_map/ppermute | solution.py:553
  131.4 3.9 %tile_grads.3 = (bf16[128,128,128]{2,1,0:T(8,128)(2,1)}, f32[8,128]{1,0:T(8,128)S(1)}) custom-call(s32[1]{0:T(128)} %bitcast.here.refs_0_, s32[5,32]{1,0:T(8,128)S(1)} %pad_add_fusion.cols, bf16[1024,256]{1,0:T(8,128)(2,1)S(1)} %get-tuple-element.36.refs_0_, ...), custom_call_target="tpu_custom_call", output_to_operand_aliasing={{0}: (23, {})} | custom-call | flops 1048576 | bytes 65536 | tf_op jit(solution)/shard_map/tile_grads/pallas_call | solution.py:517
  135.4 0.7 collective-permute-start.38
  136.1 1.6 %collective-permute-start.37 = (bf16[112,256]{1,0:T(8,128)(2,1)S(1)}, bf16[112,256]{1,0:T(8,128)(2,1)S(1)}, u32[]{:S(2)}, u32[]{:S(2)}) collective-permute-start(bf16[112,256]{1,0:T(8,128)(2,1)S(1)} %sum_terms.29), channel_id=1, source_target_pairs={{0,16},{4,20},{8,24},{12,28},{16,0},{20,4},{24,8},{28,12},{1,17},{... | collective-permute-start | bytes 172040 | tf_op jit(solution)/shard_map/ppermute | solution.py:545
  137.7 1.3 collective-permute-start.36
  139.0 0.1 sum_terms.25
  139.1 0.8 collective-permute-start.31
  139.9 0.1 sum_terms.26
  140.0 0.5 collective-permute-start.32
  140.5 0.7 collective-permute-done.38
  141.2 1.4 collective-permute-done.36
  142.6 1.5 collective-permute-done.39.odd
  144.1 1.0 weight_unpack.1
  145.1 1.0 collective-permute-done.31.refs_5_
  146.1 0.4 collective-permute-done.32.refs_6_
  146.5 1.2 sum_terms.27
  (64 shorter events, 0.7 us)
Async XLA Ops:
  0.6 18.9 %collective-permute-start = (bf16[1024,256]{1,0:T(8,128)(2,1)}, bf16[1024,256]{1,0:T(8,128)(2,1)S(1)}, u32[]{:S(2)}, u32[]{:S(2)}) collective-permute-start(bf16[1024,256]{1,0:T(8,128)(2,1)} %nodes.3), channel_id=1, source_target_pairs={{0,4},{4,0},{8,12},{12,8},{16,20},{20,16},{24,28},{28,24},{1,5},{5... | collective-permute-start | bytes 1572872 | tf_op jit(solution)/shard_map/ppermute | solution.py:545
  2.2 9.7 %collective-permute-start.1 = (bf16[512,256]{1,0:T(8,128)(2,1)S(1)}, bf16[512,256]{1,0:T(8,128)(2,1)S(1)}, u32[]{:S(2)}, u32[]{:S(2)}) collective-permute-start(bf16[512,256]{1,0:T(8,128)(2,1)S(1)} %get-tuple-element.57.refs_0_.refs_4_.refs_6_), channel_id=1, source_target_pairs={{0,8},{4,12},{8,0},{12,4},{16,24},{20,28},{24,16},{28,20},{1,9},{5... | collective-permute-start | bytes 786440 | tf_op jit(solution)/shard_map/ppermute | solution.py:545
  4.8 9.1 %collective-permute-start.5 = (bf16[512,256]{1,0:T(8,128)(2,1)S(1)}, bf16[512,256]{1,0:T(8,128)(2,1)S(1)}, u32[]{:S(2)}, u32[]{:S(2)}) collective-permute-start(bf16[512,256]{1,0:T(8,128)(2,1)S(1)} %get-tuple-element.57.refs_0_.refs_4_.refs_6_), channel_id=1, source_target_pairs={{0,16},{4,20},{8,24},{12,28},{16,0},{20,4},{24,8},{28,12},{1,17},{... | collective-permute-start | bytes 786440 | tf_op jit(solution)/shard_map/ppermute | solution.py:545
  6.3 11.3 %collective-permute-start.2 = (bf16[512,256]{1,0:T(8,128)(2,1)S(1)}, bf16[512,256]{1,0:T(8,128)(2,1)S(1)}, u32[]{:S(2)}, u32[]{:S(2)}) collective-permute-start(bf16[512,256]{1,0:T(8,128)(2,1)S(1)} %get-tuple-element.56.refs_1_.refs_5_.refs_7_), channel_id=1, source_target_pairs={{0,8},{4,12},{8,0},{12,4},{16,24},{20,28},{24,16},{28,20},{1,9},{5... | collective-permute-start | bytes 786440 | tf_op jit(solution)/shard_map/ppermute | solution.py:545
  6.8 12.7 %collective-permute-start.6 = (bf16[512,256]{1,0:T(8,128)(2,1)S(1)}, bf16[512,256]{1,0:T(8,128)(2,1)S(1)}, u32[]{:S(2)}, u32[]{:S(2)}) collective-permute-start(bf16[512,256]{1,0:T(8,128)(2,1)S(1)} %get-tuple-element.56.refs_1_.refs_5_.refs_7_), channel_id=1, source_target_pairs={{0,16},{4,20},{8,24},{12,28},{16,0},{20,4},{24,8},{28,12},{1,17},{... | collective-permute-start | bytes 786440 | tf_op jit(solution)/shard_map/ppermute | solution.py:545
  11.9 8.1 %collective-permute-start.3 = (bf16[512,256]{1,0:T(8,128)(2,1)S(1)}, bf16[512,256]{1,0:T(8,128)(2,1)S(1)}, u32[]{:S(2)}, u32[]{:S(2)}) collective-permute-start(bf16[512,256]{1,0:T(8,128)(2,1)S(1)} %collective-permute-done.1.refs_3_.refs_7_.refs_9_), channel_id=1, source_target_pairs={{0,4},{4,0},{8,12},{12,8},{16,20},{20,16},{24,28},{28,24},{1,5},{5... | collective-permute-start | bytes 786440 | tf_op jit(solution)/shard_map/ppermute | solution.py:545
  13.9 9.1 %collective-permute-start.9 = (bf16[512,256]{1,0:T(8,128)(2,1)S(1)}, bf16[512,256]{1,0:T(8,128)(2,1)S(1)}, u32[]{:S(2)}, u32[]{:S(2)}) collective-permute-start(bf16[512,256]{1,0:T(8,128)(2,1)S(1)} %collective-permute-done.5.refs_7_.refs_11_.refs_13_), channel_id=1, source_target_pairs={{0,8},{4,12},{8,0},{12,4},{16,24},{20,28},{24,16},{28,20},{1,9},{5... | collective-permute-start | bytes 786440 | tf_op jit(solution)/shard_map/ppermute | solution.py:545
  17.6 7.9 %collective-permute-start.10 = (bf16[512,256]{1,0:T(8,128)(2,1)S(1)}, bf16[512,256]{1,0:T(8,128)(2,1)S(1)}, u32[]{:S(2)}, u32[]{:S(2)}) collective-permute-start(bf16[512,256]{1,0:T(8,128)(2,1)S(1)} %collective-permute-done.2.refs_4_.refs_8_.refs_10_), channel_id=1, source_target_pairs={{0,16},{4,20},{8,24},{12,28},{16,0},{20,4},{24,8},{28,12},{1,17},{... | collective-permute-start | bytes 786440 | tf_op jit(solution)/shard_map/ppermute | solution.py:545
  19.5 6.7 %collective-permute-start.4 = (bf16[512,256]{1,0:T(8,128)(2,1)S(1)}, bf16[512,256]{1,0:T(8,128)(2,1)S(1)}, u32[]{:S(2)}, u32[]{:S(2)}) collective-permute-start(bf16[512,256]{1,0:T(8,128)(2,1)S(1)} %collective-permute-done.2.refs_4_.refs_8_.refs_10_), channel_id=1, source_target_pairs={{0,4},{4,0},{8,12},{12,8},{16,20},{20,16},{24,28},{28,24},{1,5},{5... | collective-permute-start | bytes 786440 | tf_op jit(solution)/shard_map/ppermute | solution.py:545
  19.5 6.7 %collective-permute-start.7 = (bf16[512,256]{1,0:T(8,128)(2,1)S(1)}, bf16[512,256]{1,0:T(8,128)(2,1)}, u32[]{:S(2)}, u32[]{:S(2)}) collective-permute-start(bf16[512,256]{1,0:T(8,128)(2,1)S(1)} %collective-permute-done.5.refs_7_.refs_11_.refs_13_), channel_id=1, source_target_pairs={{0,4},{4,0},{8,12},{12,8},{16,20},{20,16},{24,28},{28,24},{1,5},{5... | collective-permute-start | bytes 786440 | tf_op jit(solution)/shard_map/ppermute | solution.py:545
  20.1 6.2 %collective-permute-start.8 = (bf16[512,256]{1,0:T(8,128)(2,1)S(1)}, bf16[512,256]{1,0:T(8,128)(2,1)}, u32[]{:S(2)}, u32[]{:S(2)}) collective-permute-start(bf16[512,256]{1,0:T(8,128)(2,1)S(1)} %collective-permute-done.6.refs_8_.refs_12_.refs_14_), channel_id=1, source_target_pairs={{0,4},{4,0},{8,12},{12,8},{16,20},{20,16},{24,28},{28,24},{1,5},{5... | collective-permute-start | bytes 786440 | tf_op jit(solution)/shard_map/ppermute | solution.py:545
  23.0 3.3 %collective-permute-start.11 = (bf16[512,256]{1,0:T(8,128)(2,1)S(1)}, bf16[512,256]{1,0:T(8,128)(2,1)}, u32[]{:S(2)}, u32[]{:S(2)}) collective-permute-start(bf16[512,256]{1,0:T(8,128)(2,1)S(1)} %collective-permute-done.9.refs_11_.refs_15_.refs_17_), channel_id=1, source_target_pairs={{0,4},{4,0},{8,12},{12,8},{16,20},{20,16},{24,28},{28,24},{1,5},{5... | collective-permute-start | bytes 786440 | tf_op jit(solution)/shard_map/ppermute | solution.py:545
  25.5 1.7 %collective-permute-start.12 = (bf16[512,256]{1,0:T(8,128)(2,1)S(1)}, bf16[512,256]{1,0:T(8,128)(2,1)}, u32[]{:S(2)}, u32[]{:S(2)}) collective-permute-start(bf16[512,256]{1,0:T(8,128)(2,1)S(1)} %collective-permute-done.10.refs_12_.refs_16_.refs_18_), channel_id=1, source_target_pairs={{0,4},{4,0},{8,12},{12,8},{16,20},{20,16},{24,28},{28,24},{1,5},{5... | collective-permute-start | bytes 786440 | tf_op jit(solution)/shard_map/ppermute | solution.py:545
  26.2 4.5 %copy-start.1 = (bf16[512,256]{1,0:T(8,128)(2,1)}, bf16[512,256]{1,0:T(8,128)(2,1)S(1)}, u32[]{:S(2)}) copy-start(bf16[512,256]{1,0:T(8,128)(2,1)S(1)} %collective-permute-done.4.refs_6_.refs_10_.refs_12_) | copy-start | bytes 786436
  27.2 5.2 %copy-start = (bf16[32,1,4,128,128]{4,3,2,1,0:T(8,128)(2,1)S(1)}, bf16[32,1,4,128,128]{4,3,2,1,0:T(8,128)(2,1)}, u32[]{:S(2)}) copy-start(bf16[32,1,4,128,128]{4,3,2,1,0:T(8,128)(2,1)} %param.11) | copy-start | bytes 12582916
  30.7 14.8 %collective-permute-start.13 = (bf16[1024,256]{1,0:T(8,128)(2,1)S(1)}, bf16[1024,256]{1,0:T(8,128)(2,1)S(1)}, u32[]{:S(2)}, u32[]{:S(2)}) collective-permute-start(bf16[1024,256]{1,0:T(8,128)(2,1)S(1)} %partial_messages.4.refs_1_), channel_id=1, source_target_pairs={{0,1},{1,0},{2,3},{3,2},{4,5},{5,4},{6,7},{7,6},{8,9},{9,8},{10,11... | collective-permute-start | bytes 1572872 | tf_op jit(solution)/shard_map/ppermute | solution.py:549
  32.4 2.4 %copy-start.2 = (bf16[512,256]{1,0:T(8,128)(2,1)S(1)}, bf16[512,256]{1,0:T(8,128)(2,1)}, u32[]{:S(2)}) copy-start(bf16[512,256]{1,0:T(8,128)(2,1)} %copy-done.1) | copy-start | bytes 786436
  37.9 18.0 %collective-permute-start.16 = (bf16[1024,256]{1,0:T(8,128)(2,1)S(1)}, bf16[1024,256]{1,0:T(8,128)(2,1)S(1)}, u32[]{:S(2)}, u32[]{:S(2)}) collective-permute-start(bf16[1024,256]{1,0:T(8,128)(2,1)S(1)} %partial_messages.5.refs_1_), channel_id=1, source_target_pairs={{0,1},{1,0},{2,3},{3,2},{4,5},{5,4},{6,7},{7,6},{8,9},{9,8},{10,11... | collective-permute-start | bytes 1572872 | tf_op jit(solution)/shard_map/ppermute | solution.py:549
  45.7 25.1 %copy-start.3 = (bf16[1024,256]{1,0:T(8,128)(2,1)S(1)}, bf16[1024,256]{1,0:T(8,128)(2,1)}, u32[]{:S(2)}) copy-start(bf16[1024,256]{1,0:T(8,128)(2,1)} %nodes.3) | copy-start | bytes 1572868
  45.7 25.1 %copy-start.4 = (bf16[1024,256]{1,0:T(8,128)(2,1)S(1)}, bf16[1024,256]{1,0:T(8,128)(2,1)}, u32[]{:S(2)}) copy-start(bf16[1024,256]{1,0:T(8,128)(2,1)} %cot.3) | copy-start | bytes 1572868
  45.7 25.1 %copy-start.5 = (bf16[512,256]{1,0:T(8,128)(2,1)S(1)}, bf16[512,256]{1,0:T(8,128)(2,1)}, u32[]{:S(2)}) copy-start(bf16[512,256]{1,0:T(8,128)(2,1)} %w_in.1) | copy-start | bytes 786436
  45.7 25.1 %copy-start.6 = (bf16[256,256]{1,0:T(8,128)(2,1)S(1)}, bf16[256,256]{1,0:T(8,128)(2,1)}, u32[]{:S(2)}) copy-start(bf16[256,256]{1,0:T(8,128)(2,1)} %refs_5_.1) | copy-start | bytes 393220
  45.7 25.1 %copy-start.7 = (f32[256]{0:T(256)S(1)}, f32[256]{0:T(256)}, u32[]{:S(2)}) copy-start(f32[256]{0:T(256)} %param.15) | copy-start | bytes 3076
  45.7 25.1 %copy-start.8 = (f32[256]{0:T(256)S(1)}, f32[256]{0:T(256)}, u32[]{:S(2)}) copy-start(f32[256]{0:T(256)} %param.17) | copy-start | bytes 3076
  45.7 25.1 %copy-start.9 = (f32[256]{0:T(256)S(1)}, f32[256]{0:T(256)}, u32[]{:S(2)}) copy-start(f32[256]{0:T(256)} %param.18) | copy-start | bytes 3076
  45.7 10.4 %collective-permute-start.14 = (bf16[1024,256]{1,0:T(8,128)(2,1)S(1)}, bf16[1024,256]{1,0:T(8,128)(2,1)S(1)}, u32[]{:S(2)}, u32[]{:S(2)}) collective-permute-start(bf16[1024,256]{1,0:T(8,128)(2,1)S(1)} %sum_terms.15), channel_id=1, source_target_pairs={{0,4},{1,2},{2,1},{3,7},{4,0},{5,6},{6,5},{7,3},{8,12},{9,10},{10,... | collective-permute-start | bytes 1572872 | tf_op jit(solution)/shard_map/ppermute | solution.py:562
  56.1 4.0 %collective-permute-start.17 = (bf16[1024,256]{1,0:T(8,128)(2,1)S(1)}, bf16[1024,256]{1,0:T(8,128)(2,1)S(1)}, u32[]{:S(2)}, u32[]{:S(2)}) collective-permute-start(bf16[1024,256]{1,0:T(8,128)(2,1)S(1)} %sum_terms.17), channel_id=1, source_target_pairs={{0,4},{1,2},{2,1},{3,7},{4,0},{5,6},{6,5},{7,3},{8,12},{9,10},{10,... | collective-permute-start | bytes 1572872 | tf_op jit(solution)/shard_map/ppermute | solution.py:562
  56.4 14.4 %collective-permute-start.15 = (bf16[1024,256]{1,0:T(8,128)(2,1)S(1)}, bf16[1024,256]{1,0:T(8,128)(2,1)S(1)}, u32[]{:S(2)}, u32[]{:S(2)}) collective-permute-start(bf16[1024,256]{1,0:T(8,128)(2,1)S(1)} %sum_terms.16), channel_id=1, source_target_pairs={{0,1},{1,0},{2,3},{3,2},{4,5},{5,4},{6,7},{7,6},{8,9},{9,8},{10,11... | collective-permute-start | bytes 1572872 | tf_op jit(solution)/shard_map/ppermute | solution.py:549
  73.7 11.8 %collective-permute-start.18 = (bf16[1024,256]{1,0:T(8,128)(2,1)S(1)}, bf16[1024,256]{1,0:T(8,128)(2,1)S(1)}, u32[]{:S(2)}, u32[]{:S(2)}) collective-permute-start(bf16[1024,256]{1,0:T(8,128)(2,1)S(1)} %get-tuple-element.36.refs_0_), channel_id=1, source_target_pairs={{0,1},{1,0},{2,3},{3,2},{4,5},{5,4},{6,7},{7,6},{8,9},{9,8},{10,11... | collective-permute-start | bytes 1572872 | tf_op jit(solution)/shard_map/ppermute | solution.py:549
  75.5 10.1 %collective-permute-start.19 = (bf16[1024,256]{1,0:T(8,128)(2,1)S(1)}, bf16[1024,256]{1,0:T(8,128)(2,1)S(1)}, u32[]{:S(2)}, u32[]{:S(2)}) collective-permute-start(bf16[1024,256]{1,0:T(8,128)(2,1)S(1)} %get-tuple-element.36.refs_0_), channel_id=1, source_target_pairs={{0,4},{1,2},{2,1},{3,7},{4,0},{5,6},{6,5},{7,3},{8,12},{9,10},{10,... | collective-permute-start | bytes 1572872 | tf_op jit(solution)/shard_map/ppermute | solution.py:562
  85.5 5.5 %collective-permute-start.21 = (bf16[1024,256]{1,0:T(8,128)(2,1)S(1)}, bf16[1024,256]{1,0:T(8,128)(2,1)S(1)}, u32[]{:S(2)}, u32[]{:S(2)}) collective-permute-start(bf16[1024,256]{1,0:T(8,128)(2,1)S(1)} %collective-permute-done.18.refs_0_.refs_1_), channel_id=1, source_target_pairs={{0,4},{1,2},{2,1},{3,7},{4,0},{5,6},{6,5},{7,3},{8,12},{9,10},{10,... | collective-permute-start | bytes 1572872 | tf_op jit(solution)/shard_map/ppermute | solution.py:562
  86.4 14.4 %collective-permute-start.23 = (f32[448,256]{1,0:T(8,128)S(1)}, f32[448,256]{1,0:T(8,128)S(1)}, u32[]{:S(2)}, u32[]{:S(2)}) collective-permute-start(f32[448,256]{1,0:T(8,128)S(1)} %get-tuple-element.39), channel_id=1, source_target_pairs={{0,4},{4,0},{8,12},{12,8},{16,20},{20,16},{24,28},{28,24},{1,5},{5... | collective-permute-start | bytes 1376264 | tf_op jit(solution)/shard_map/ppermute | solution.py:545
  87.0 17.6 %collective-permute-start.20 = (bf16[1024,256]{1,0:T(8,128)(2,1)S(1)}, bf16[1024,256]{1,0:T(8,128)(2,1)S(1)}, u32[]{:S(2)}, u32[]{:S(2)}) collective-permute-start(bf16[1024,256]{1,0:T(8,128)(2,1)S(1)} %collective-permute-done.19.refs_1_.refs_2_), channel_id=1, source_target_pairs={{0,1},{1,0},{2,3},{3,2},{4,5},{5,4},{6,7},{7,6},{8,9},{9,8},{10,11... | collective-permute-start | bytes 1572872 | tf_op jit(solution)/shard_map/ppermute | solution.py:549
  91.0 23.7 %collective-permute-start.22 = (bf16[1024,256]{1,0:T(8,128)(2,1)S(1)}, bf16[1024,256]{1,0:T(8,128)(2,1)S(1)}, u32[]{:S(2)}, u32[]{:S(2)}) collective-permute-start(bf16[1024,256]{1,0:T(8,128)(2,1)S(1)} %collective-permute-done.21.refs_19_.refs_4_), channel_id=1, source_target_pairs={{0,1},{1,0},{2,3},{3,2},{4,5},{5,4},{6,7},{7,6},{8,9},{9,8},{10,11... | collective-permute-start | bytes 1572872 | tf_op jit(solution)/shard_map/ppermute | solution.py:549
  100.8 9.6 %collective-permute-start.24 = (f32[112,256]{1,0:T(8,128)S(1)}, f32[112,256]{1,0:T(8,128)S(1)}, u32[]{:S(2)}, u32[]{:S(2)}) collective-permute-start(f32[112,256]{1,0:T(8,128)S(1)} %sum_terms.19), channel_id=1, source_target_pairs={{0,16},{4,20},{8,24},{12,28},{16,0},{20,4},{24,8},{28,12},{1,17},{... | collective-permute-start | bytes 344072 | tf_op jit(solution)/shard_map/ppermute | solution.py:545
  102.4 8.0 %collective-permute-start.25 = (f32[112,256]{1,0:T(8,128)S(1)}, f32[112,256]{1,0:T(8,128)S(1)}, u32[]{:S(2)}, u32[]{:S(2)}) collective-permute-start(f32[112,256]{1,0:T(8,128)S(1)} %sum_terms.20), channel_id=1, source_target_pairs={{0,8},{4,12},{8,0},{12,4},{16,24},{20,28},{24,16},{28,20},{1,9},{5... | collective-permute-start | bytes 344072 | tf_op jit(solution)/shard_map/ppermute | solution.py:545
  104.0 6.4 %collective-permute-start.26 = (f32[112,256]{1,0:T(8,128)S(1)}, f32[112,256]{1,0:T(8,128)S(1)}, u32[]{:S(2)}, u32[]{:S(2)}) collective-permute-start(f32[112,256]{1,0:T(8,128)S(1)} %sum_terms.21), channel_id=1, source_target_pairs={{0,24},{4,28},{8,16},{12,20},{16,8},{20,12},{24,0},{28,4},{1,25},{... | collective-permute-start | bytes 344072 | tf_op jit(solution)/shard_map/ppermute | solution.py:545
  119.8 2.7 %collective-permute-start.28 = (bf16[2048,256]{1,0:T(8,128)(2,1)S(1)}, bf16[2048,256]{1,0:T(8,128)(2,1)S(1)}, u32[]{:S(2)}, u32[]{:S(2)}) collective-permute-start(bf16[2048,256]{1,0:T(8,128)(2,1)S(1)} %get-tuple-element.43), channel_id=1, source_target_pairs={{0,4},{4,0},{8,12},{12,8},{16,20},{20,16},{24,28},{28,24},{1,5},{5... | collective-permute-start | bytes 3145736 | tf_op jit(solution)/shard_map/ppermute | solution.py:545
  119.9 6.3 %collective-permute-start.27 = (bf16[2048,256]{1,0:T(8,128)(2,1)S(1)}, bf16[2048,256]{1,0:T(8,128)(2,1)S(1)}, u32[]{:S(2)}, u32[]{:S(2)}) collective-permute-start(bf16[2048,256]{1,0:T(8,128)(2,1)S(1)} %get-tuple-element.42), channel_id=1, source_target_pairs={{0,4},{4,0},{8,12},{12,8},{16,20},{20,16},{24,28},{28,24},{1,5},{5... | collective-permute-start | bytes 3145736 | tf_op jit(solution)/shard_map/ppermute | solution.py:545
  122.7 16.3 %collective-permute-start.30 = (bf16[1024,256]{1,0:T(8,128)(2,1)S(1)}, bf16[1024,256]{1,0:T(8,128)(2,1)S(1)}, u32[]{:S(2)}, u32[]{:S(2)}) collective-permute-start(bf16[1024,256]{1,0:T(8,128)(2,1)S(1)} %sum_terms.24.refs_23_.refs_4_), channel_id=1, source_target_pairs={{0,16},{4,20},{8,24},{12,28},{16,0},{20,4},{24,8},{28,12},{1,17},{... | collective-permute-start | bytes 1572872 | tf_op jit(solution)/shard_map/ppermute | solution.py:545
  124.0 15.9 %collective-permute-start.29 = (bf16[1024,256]{1,0:T(8,128)(2,1)S(1)}, bf16[1024,256]{1,0:T(8,128)(2,1)S(1)}, u32[]{:S(2)}, u32[]{:S(2)}) collective-permute-start(bf16[1024,256]{1,0:T(8,128)(2,1)S(1)} %sum_terms.23.refs_22_.refs_3_), channel_id=1, source_target_pairs={{0,8},{4,12},{8,0},{12,4},{16,24},{20,28},{24,16},{28,20},{1,9},{5... | collective-permute-start | bytes 1572872 | tf_op jit(solution)/shard_map/ppermute | solution.py:545
  126.1 9.2 %collective-permute-start.33 = (bf16[112,256]{1,0:T(8,128)(2,1)S(1)}, bf16[112,256]{1,0:T(8,128)(2,1)S(1)}, u32[]{:S(2)}, u32[]{:S(2)}) collective-permute-start(bf16[112,256]{1,0:T(8,128)(2,1)S(1)} %sum_terms.28.refs_1_), channel_id=1, source_target_pairs={{0,1},{1,2},{2,3},{3,0},{4,5},{5,6},{6,7},{7,4},{8,9},{9,10},{10,1... | collective-permute-start | bytes 172040 | tf_op jit(solution)/shard_map/ppermute | solution.py:553
  127.7 7.6 %collective-permute-start.34 = (bf16[112,256]{1,0:T(8,128)(2,1)S(1)}, bf16[112,256]{1,0:T(8,128)(2,1)S(1)}, u32[]{:S(2)}, u32[]{:S(2)}) collective-permute-start(bf16[112,256]{1,0:T(8,128)(2,1)S(1)} %sum_terms.28.refs_1_), channel_id=1, source_target_pairs={{0,2},{1,3},{2,0},{3,1},{4,6},{5,7},{6,4},{7,5},{8,10},{9,11},{10,... | collective-permute-start | bytes 172040 | tf_op jit(solution)/shard_map/ppermute | solution.py:553
  129.5 5.8 %collective-permute-start.35 = (bf16[112,256]{1,0:T(8,128)(2,1)S(1)}, bf16[112,256]{1,0:T(8,128)(2,1)S(1)}, u32[]{:S(2)}, u32[]{:S(2)}) collective-permute-start(bf16[112,256]{1,0:T(8,128)(2,1)S(1)} %sum_terms.28.refs_1_), channel_id=1, source_target_pairs={{0,3},{1,0},{2,1},{3,2},{4,7},{5,4},{6,5},{7,6},{8,11},{9,8},{10,9... | collective-permute-start | bytes 172040 | tf_op jit(solution)/shard_map/ppermute | solution.py:553
  135.4 5.8 %collective-permute-start.38 = (bf16[112,256]{1,0:T(8,128)(2,1)S(1)}, bf16[112,256]{1,0:T(8,128)(2,1)S(1)}, u32[]{:S(2)}, u32[]{:S(2)}) collective-permute-start(bf16[112,256]{1,0:T(8,128)(2,1)S(1)} %sum_terms.29), channel_id=1, source_target_pairs={{0,24},{4,28},{8,16},{12,20},{16,8},{20,12},{24,0},{28,4},{1,25},{... | collective-permute-start | bytes 172040 | tf_op jit(solution)/shard_map/ppermute | solution.py:545
  136.1 5.1 %collective-permute-start.37 = (bf16[112,256]{1,0:T(8,128)(2,1)S(1)}, bf16[112,256]{1,0:T(8,128)(2,1)S(1)}, u32[]{:S(2)}, u32[]{:S(2)}) collective-permute-start(bf16[112,256]{1,0:T(8,128)(2,1)S(1)} %sum_terms.29), channel_id=1, source_target_pairs={{0,16},{4,20},{8,24},{12,28},{16,0},{20,4},{24,8},{28,12},{1,17},{... | collective-permute-start | bytes 172040 | tf_op jit(solution)/shard_map/ppermute | solution.py:545
  137.7 4.9 %collective-permute-start.36 = (bf16[112,256]{1,0:T(8,128)(2,1)S(1)}, bf16[112,256]{1,0:T(8,128)(2,1)S(1)}, u32[]{:S(2)}, u32[]{:S(2)}) collective-permute-start(bf16[112,256]{1,0:T(8,128)(2,1)S(1)} %sum_terms.29), channel_id=1, source_target_pairs={{0,8},{4,12},{8,0},{12,4},{16,24},{20,28},{24,16},{28,20},{1,9},{5... | collective-permute-start | bytes 172040 | tf_op jit(solution)/shard_map/ppermute | solution.py:545
  139.1 7.0 %collective-permute-start.31 = (bf16[512,256]{1,0:T(8,128)(2,1)S(1)}, bf16[512,256]{1,0:T(8,128)(2,1)S(1)}, u32[]{:S(2)}, u32[]{:S(2)}) collective-permute-start(bf16[512,256]{1,0:T(8,128)(2,1)S(1)} %sum_terms.25), channel_id=1, source_target_pairs={{0,8},{4,12},{8,0},{12,4},{16,24},{20,28},{24,16},{28,20},{1,9},{5... | collective-permute-start | bytes 786440 | tf_op jit(solution)/shard_map/ppermute | solution.py:545
  140.0 6.5 %collective-permute-start.32 = (bf16[512,256]{1,0:T(8,128)(2,1)S(1)}, bf16[512,256]{1,0:T(8,128)(2,1)S(1)}, u32[]{:S(2)}, u32[]{:S(2)}) collective-permute-start(bf16[512,256]{1,0:T(8,128)(2,1)S(1)} %sum_terms.26), channel_id=1, source_target_pairs={{0,16},{4,20},{8,24},{12,28},{16,0},{20,4},{24,8},{28,12},{1,17},{... | collective-permute-start | bytes 786440 | tf_op jit(solution)/shard_map/ppermute | solution.py:545
  142.6 1.6 %collective-permute-start.39 = (bf16[448,256]{1,0:T(8,128)(2,1)S(1)}, bf16[448,256]{1,0:T(8,128)(2,1)S(1)}, u32[]{:S(2)}, u32[]{:S(2)}) collective-permute-start(bf16[448,256]{1,0:T(8,128)(2,1)S(1)} %pad_maximum_fusion.even), channel_id=1, source_target_pairs={{0,4},{4,0},{8,12},{12,8},{16,20},{20,16},{24,28},{28,24},{1,5},{5... | collective-permute-start | bytes 688136 | tf_op jit(solution)/shard_map/ppermute | solution.py:545
